TPU v7x, 32 devices: a whole 2x2x4 slice. The times are simulated.
32 devices in a mesh: grp: 2 (over core), dev: 16 (over z, y, x).
Axes of the slice: x: 2, y: 2, z: 4, core: 2. Of those that a mesh axis runs over, the one named last changes fastest.
Arguments:
- images: bfloat16 [4096, 512], P(('grp', 'dev')), may hold values from -128 to 128
- texts: bfloat16 [4096, 512], P(('grp', 'dev')), may hold values from -128 to 128
- logit_scale: float32 [1], replicated, may hold values from 20 to 50
- logit_bias: float32 [1], replicated, may hold values from -12 to -6
Outputs:
- image_grad: float32 [4096, 512], P(('grp', 'dev'))
- text_grad: float32 [4096, 512], P(('grp', 'dev'))
All inputs are finite; a program needn't handle non-finite values.
Results may differ from a plain program's by a relative error of at most 0.0047.
Values may be sent and summed in bfloat16 or wider, within the bound.
No kernel may reach another device: no remote copies, remote signals or barrier semaphores. Data moves between devices by JAX's collectives and lax.ppermute only.
A program may use at most 64 MiB of HBM per device.

v0:
```python
import jax
import jax.numpy as jnp
from jax import lax
from jax.sharding import PartitionSpec as P


def normalized(raw_rows):
    widened = raw_rows.astype(jnp.float32)
    factor = lax.rsqrt(jnp.sum(widened * widened, axis=-1, keepdims=True) + 1e-06)
    return (widened * factor, factor)


def unnormalize(grad_unit, unit_rows, factor):
    along = jnp.sum(unit_rows * grad_unit, axis=-1, keepdims=True)
    return factor * (grad_unit - unit_rows * along)


def collect_groups(own_rows):
    gathered = lax.all_gather(own_rows, "grp", axis=0, tiled=True)
    return gathered


def return_groups(partials):
    owned = lax.psum_scatter(partials, "grp", scatter_dimension=0, tiled=True)
    return owned


def pair_tiles(image_rows, text_rows, temper, offset):
    row_count = image_rows.shape[0]
    dev_count = lax.axis_size("dev")
    grp_count = lax.axis_size("grp")
    group_at = lax.axis_index("grp")
    device_at = lax.axis_index("dev")
    column = collect_groups(text_rows)
    position = jnp.arange(grp_count * row_count, dtype=jnp.int32)
    column_ids = (position // row_count * dev_count + device_at) * row_count + position % row_count
    group_base = group_at * dev_count * row_count
    piece_rows = lax.all_gather(image_rows, "dev", axis=0, tiled=True)
    piece_count = piece_rows.shape[0]
    row_ids = group_base + jnp.arange(piece_count, dtype=jnp.int32)
    logits = (
        temper
        * lax.dot_general(
            piece_rows, column, (((1,), (1,)), ((), ())), preferred_element_type=jnp.float32
        )
        + offset
    )
    same_pair = (row_ids[:, None] == column_ids[None, :]).astype(jnp.float32)
    coefficient = (temper * (jax.nn.sigmoid(logits) - same_pair)).astype(jnp.bfloat16)
    partial_value = jnp.dot(coefficient, column, preferred_element_type=jnp.float32)
    dev_total = partial_value
    grp_total = lax.dot_general(
        coefficient, piece_rows, (((0,), (0,)), ((), ())), preferred_element_type=jnp.float32
    )
    dev_total, grp_total = (dev_total, grp_total)
    image_total = lax.psum_scatter(dev_total, "dev", scatter_dimension=0, tiled=True)
    text_total = return_groups(grp_total)
    return (image_total, text_total)


def on_device(images, texts, logit_scale, logit_bias):
    img_unit, img_factor = normalized(images)
    txt_unit, txt_factor = normalized(texts)
    img_send = img_unit.astype(jnp.bfloat16)
    txt_send = txt_unit.astype(jnp.bfloat16)
    temper = logit_scale[0]
    offset = logit_bias[0]
    image_side, text_side = pair_tiles(img_send, txt_send, temper, offset)
    return (
        unnormalize(image_side, img_unit, img_factor),
        unnormalize(text_side, txt_unit, txt_factor),
    )


def solution(mesh):
    in_specs = (P(("grp", "dev"), None), P(("grp", "dev"), None), P(), P())
    out_specs = (P(("grp", "dev"), None), P(("grp", "dev"), None))
    return jax.shard_map(
        on_device, mesh=mesh, in_specs=in_specs, out_specs=out_specs, check_vma=False
    )
```

profile of v0, /device:TPU:0, one launch (start us, length us, event | category | flops | bytes accessed | tf_op | source)
XLA Modules:
  0.0 194.0 jit_solution(9836755277054095336)
XLA Ops:
  7.2 0.0 all-gather.2.cloned.1.call-start
  7.2 1.0 fusion.17
  8.2 1.7 fusion.13
  9.9 0.0 all-gather.2.cloned.1.call-update
  9.9 0.0 reduce-scatter.5.cloned.1.call-start
  11.3 1.0 fusion.21
  12.3 1.0 fusion.10
  13.3 2.1 %all_gather.7 = bf16[256,512]{1,0:T(8,128)(2,1)S(1)} all-gather(bf16[128,512]{1,0:T(8,128)(2,1)S(1)} %fusion.10), channel_id=1, replica_groups=mesh['grp'=2,'dev'=16] {'grp'}, dimensions={0}, use_global_device_ids=true | all-gather | bytes 393216 | tf_op jit(solution)/shard_map/all_gather | solution.py:19
  15.4 59.4 %all-gather.2.cloned.1.call-done = bf16[2048,512]{1,0:T(8,128)(2,1)} async-done(((bf16[128,512]{1,0:T(8,128)(2,1)}), bf16[2048,512]{1,0:T(8,128)(2,1)}) %all-gather.2.cloned.1.call-update) | async-done | bytes 2097168 | tf_op jit(solution)/shard_map/all_gather | solution.py:38
  74.8 2.7 %fusion.7 = bf16[2048,256]{1,0:T(8,128)(2,1)S(1)} fusion(bf16[2048,512]{1,0:T(8,128)(2,1)} %all-gather.2.cloned.1.call-done, bf16[256,512]{1,0:T(8,128)(2,1)S(1)} %all_gather.7, s32[256]{0:T(256)S(1)} %fusion.24, f32[]{:T(128)} %bitcast.9, f32[]{:T(128)} %bitcast.8, s32[2048]{0:T(1024)S(1)} %iota_add_fusion), kind=kOutput, calls=%fused_computation.8 | convolution fusion | flops 542113792 | bytes 3417096 | tf_op jit(solution)/shard_map/dot_general | solution.py:43
  77.5 0.0 copy-done.2
  77.5 1.5 fusion.29
  79.0 0.0 reduce-scatter.5.cloned.1.call-update
  79.1 0.0 reduce-scatter.3.cloned.1.call-start
  79.1 2.6 %fusion.28 = f32[2048,512]{1,0:T(8,128)} fusion(bf16[2048,256]{1,0:T(8,128)(2,1)S(1)} %fusion.7, bf16[256,512]{1,0:T(8,128)(2,1)S(1)} %all_gather.7), kind=kOutput, calls=%fused_computation.41 | convolution fusion | flops 536870912 | bytes 5505024 | tf_op jit(solution)/shard_map/dot_general | solution.py:50
  81.8 0.0 reduce-scatter.3.cloned.1.call-update
  81.8 4.0 %reduce-scatter.5.cloned.1.call-done = f32[128,512]{1,0:T(8,128)} async-done(((f32[256,512]{1,0:T(8,128)}), f32[128,512]{1,0:T(8,128)}) %reduce-scatter.5.cloned.1.call-update) | async-done | bytes 262160 | tf_op jit(solution)/shard_map/reduce_scatter | solution.py:24
  85.8 0.0 copy-done
  85.8 1.1 fusion.18
  87.0 1.8 fusion.20
  88.7 95.8 %reduce-scatter.3.cloned.1.call-done = f32[128,512]{1,0:T(8,128)} async-done(((f32[2048,512]{1,0:T(8,128)}), f32[128,512]{1,0:T(8,128)}) %reduce-scatter.3.cloned.1.call-update) | async-done | bytes 262160 | tf_op jit(solution)/shard_map/reduce_scatter | solution.py:56
  184.5 0.0 copy-done.1
  184.5 1.1 fusion.14
  185.6 1.8 fusion.16
  (7 shorter events, 0.0 us)
Async XLA Ops:
  7.2 67.6 %all-gather.2.cloned.1.call-start = ((), (), s32[]{:S(2)}) async-start(), calls=%async_computation.2 | async-start | bytes 2228224 | tf_op jit(solution)/shard_map/all_gather | solution.py:38
  9.9 75.9 %reduce-scatter.5.cloned.1.call-start = ((), (), s32[]{:S(2)}) async-start(), calls=%async_computation.4 | async-start | bytes 786432 | tf_op jit(solution)/shard_map/reduce_scatter | solution.py:24
  74.8 2.7 %copy-start.2 = (bf16[2048,512]{1,0:T(8,128)(2,1)S(1)}, bf16[2048,512]{1,0:T(8,128)(2,1)}, u32[]{:S(2)}) copy-start(bf16[2048,512]{1,0:T(8,128)(2,1)} %all-gather.2.cloned.1.call-done) | copy-start | bytes 6291460
  79.1 105.5 %reduce-scatter.3.cloned.1.call-start = ((), (), s32[]{:S(2)}) async-start(), calls=%async_computation.3 | async-start | bytes 4456448 | tf_op jit(solution)/shard_map/reduce_scatter | solution.py:56
  81.7 4.1 %copy-start = (bf16[128,512]{1,0:T(8,128)(2,1)S(1)}, bf16[128,512]{1,0:T(8,128)(2,1)}, u32[]{:S(2)}) copy-start(bf16[128,512]{1,0:T(8,128)(2,1)} %param.5) | copy-start | bytes 393220
  81.7 102.8 %copy-start.1 = (bf16[128,512]{1,0:T(8,128)(2,1)S(1)}, bf16[128,512]{1,0:T(8,128)(2,1)}, u32[]{:S(2)}) copy-start(bf16[128,512]{1,0:T(8,128)(2,1)} %param.4) | copy-start | bytes 393220
Sparse Core Ops, SparseCore 0:
  11.3 63.3 all-gather.1
  79.2 6.5 reduce-scatter.4
  88.2 96.2 reduce-scatter.2
where the time goes:
time: 194 us
  waiting for transfers between devices  159 us (82%)
  between operations  15.1 us (8%)
  other arithmetic  10.5 us (5%)
  matrix products  6.87 us (4%)
  blocking collectives  2.09 us (1%)
    reduce_scatter x1, waiting for transfers between devices, pair_tiles(): lax.psum_scatter(dev_total, 'dev', scatter_dimension=0, tiled=True)  95.8 us
    all_gather x1, waiting for transfers between devices, pair_tiles(): piece_rows = lax.all_gather(image_rows, 'dev', axis=0, tiled=True)  59.4 us
    reduce_scatter x1, waiting for transfers between devices, return_groups(): owned = lax.psum_scatter(partials, 'grp', scatter_dimension=0, tiled=True)  4.04 us
  transfers between devices with their start and end apart: 3, of which 3 were waited for; matrix products, arithmetic and copies ran while one was open for 4% of the time, Pallas kernels for 0%

commit v1 on v0

v1 whole, which is shorter than its diff:
```python
import functools
import math

import jax
import jax.numpy as jnp
from jax import lax
from jax.experimental import pallas as pl
from jax.experimental.pallas import tpu as pltpu
from jax.sharding import PartitionSpec as P

AXES = ("grp", "dev")
VMEM_LIMIT = 50 * 1024 * 1024


def unit_rows(raw):
    wide = raw.astype(jnp.float32)
    factor = lax.rsqrt(jnp.sum(wide * wide, axis=-1, keepdims=True) + 1e-06)
    return wide * factor, factor


def pairs_kernel(image_count, text_count, rows, span, *refs):
    scale_ref, bias_ref = refs[:2]
    image_refs = refs[2:2 + image_count]
    text_refs = refs[2 + image_count:2 + image_count + text_count]
    outs = refs[2 + image_count + text_count:]
    image_out = outs[:image_count]
    text_out = outs[image_count:image_count + text_count]
    v_images, image_acc = outs[image_count + text_count:]
    temper = scale_ref[0]
    offset = bias_ref[0]
    for a, ref in enumerate(image_refs):
        unit, _ = unit_rows(ref[...])
        v_images[a * rows:(a + 1) * rows, :] = unit.astype(jnp.bfloat16)
    vi = v_images[...]
    for first in range(0, text_count, span):
        here = range(first, min(first + span, text_count))
        vt = jnp.concatenate(
            [unit_rows(text_refs[c][...])[0].astype(jnp.bfloat16) for c in here], axis=0
        )
        logits = temper * lax.dot_general(
            vi, vt, (((1,), (1,)), ((), ())), preferred_element_type=jnp.float32
        ) + offset
        chance = 1.0 / (1.0 + jnp.exp(-logits))
        if first == 0:
            row = lax.broadcasted_iota(jnp.int32, chance.shape, 0)
            column = lax.broadcasted_iota(jnp.int32, chance.shape, 1)
            same = (row == column) & (row < rows)
            chance = chance - same.astype(jnp.float32)
        coefficient = (temper * chance).astype(jnp.bfloat16)
        image_part = jnp.dot(coefficient, vt, preferred_element_type=jnp.float32)
        text_part = lax.dot_general(
            coefficient, vi, (((0,), (0,)), ((), ())), preferred_element_type=jnp.float32
        )
        for at, c in enumerate(here):
            text_out[c][...] = text_part[at * rows:(at + 1) * rows, :].astype(text_out[c].dtype)
        if first == 0:
            image_acc[...] = image_part
        else:
            image_acc[...] += image_part
    for a, ref in enumerate(image_out):
        ref[...] = image_acc[a * rows:(a + 1) * rows, :].astype(ref.dtype)


def pair_terms(images, texts, scale, bias):
    rows, width = images[0].shape
    image_count, text_count = len(images), len(texts)
    own = jax.ShapeDtypeStruct((rows, width), jnp.float32)
    sent = jax.ShapeDtypeStruct((rows, width), jnp.bfloat16)
    out_shape = [own] + [sent] * (image_count - 1) + [own] + [sent] * (text_count - 1)
    smem = pl.BlockSpec(memory_space=pltpu.SMEM)
    vmem = pl.BlockSpec(memory_space=pltpu.VMEM)
    pairs = image_count * text_count * rows * rows
    outs = pl.pallas_call(
        functools.partial(pairs_kernel, image_count, text_count, rows, 2),
        out_shape=out_shape,
        in_specs=[smem, smem] + [vmem] * (image_count + text_count),
        out_specs=[vmem] * len(out_shape),
        scratch_shapes=[
            pltpu.VMEM((image_count * rows, width), jnp.bfloat16),
            pltpu.VMEM((image_count * rows, width), jnp.float32),
        ],
        compiler_params=pltpu.CompilerParams(vmem_limit_bytes=VMEM_LIMIT),
        cost_estimate=pl.CostEstimate(
            flops=6 * pairs * width,
            bytes_accessed=4 * (image_count + text_count) * rows * width,
            transcendentals=2 * pairs,
        ),
        name="pair_terms",
    )(scale, bias, *images, *texts)
    return outs[:image_count], outs[image_count:]


def finish_kernel(image_count, text_count, image_ref, text_ref, *refs):
    image_parts = refs[:image_count]
    text_parts = refs[image_count:image_count + text_count]
    outs = refs[image_count + text_count:]
    for raw, parts, out in ((image_ref, image_parts, outs[0]), (text_ref, text_parts, outs[1])):
        unit, factor = unit_rows(raw[...])
        total = parts[0][...].astype(jnp.float32)
        for part in parts[1:]:
            total = total + part[...].astype(jnp.float32)
        along = jnp.sum(unit * total, axis=-1, keepdims=True)
        out[...] = factor * (total - unit * along)


def finish(images, texts, image_parts, text_parts):
    out = jax.ShapeDtypeStruct(images.shape, jnp.float32)
    vmem = pl.BlockSpec(memory_space=pltpu.VMEM)
    count = len(image_parts) + len(text_parts)
    return pl.pallas_call(
        functools.partial(finish_kernel, len(image_parts), len(text_parts)),
        out_shape=(out, out),
        in_specs=[vmem] * (2 + count),
        out_specs=(vmem, vmem),
        compiler_params=pltpu.CompilerParams(vmem_limit_bytes=VMEM_LIMIT),
        cost_estimate=pl.CostEstimate(
            flops=10 * count * images.size, bytes_accessed=3 * count * images.size,
            transcendentals=0,
        ),
        name="finish",
    )(images, texts, *image_parts, *text_parts)


def plan(grp_count, dev_count):
    options = [n for n in range(1, dev_count + 1) if dev_count % n == 0]
    near = min(options, key=lambda n: (dev_count // n + grp_count * n, -n))
    return dev_count // near, near


def shift(value, grp_count, far_count, near_count, by_grp, by_far, by_near):
    perm = []
    for g in range(grp_count):
        for f in range(far_count):
            for n in range(near_count):
                source = (g * far_count + f) * near_count + n
                g2 = (g + by_grp) % grp_count
                f2 = (f + by_far) % far_count
                n2 = (n + by_near) % near_count
                perm.append((source, (g2 * far_count + f2) * near_count + n2))
    return lax.ppermute(value, AXES, perm)


def solution(mesh):
    grp_count, dev_count = mesh.shape["grp"], mesh.shape["dev"]
    far_count, near_count = plan(grp_count, dev_count)
    move = functools.partial(
        shift, grp_count=grp_count, far_count=far_count, near_count=near_count
    )
    image_steps = [dict(by_grp=0, by_far=f, by_near=0) for f in range(far_count)]
    text_steps = [
        dict(by_grp=g, by_far=0, by_near=n) for n in range(near_count) for g in range(grp_count)
    ]

    def back(step):
        return {name: -by for name, by in step.items()}

    def on_device(images, texts, logit_scale, logit_bias):
        image_rows = [images] + [move(images, **step) for step in image_steps[1:]]
        text_rows = [texts] + [move(texts, **step) for step in text_steps[1:]]
        image_parts, text_parts = pair_terms(image_rows, text_rows, logit_scale, logit_bias)
        image_parts = [image_parts[0]] + [
            move(part, **back(step)) for part, step in zip(image_parts[1:], image_steps[1:])
        ]
        text_parts = [text_parts[0]] + [
            move(part, **back(step)) for part, step in zip(text_parts[1:], text_steps[1:])
        ]
        return finish(images, texts, image_parts, text_parts)

    in_specs = (P(AXES, None), P(AXES, None), P(), P())
    out_specs = (P(AXES, None), P(AXES, None))
    return jax.shard_map(
        on_device, mesh=mesh, in_specs=in_specs, out_specs=out_specs, check_vma=False
    )
```

time: 194 us -> 60.4 us (0.31)
  waiting for transfers between devices: 159 us -> 32.2 us
  starting transfers between devices: 0.12 us -> 19.7 us
  between operations: 15.1 us -> 1.98 us
  other arithmetic: 10.5 us -> 0 us
  matrix products: 6.87 us -> 0 us
  Pallas kernels: 0 us -> 3.97 us
  blocking collectives: 2.09 us -> 0 us
    reduce_scatter x2 -> x0, waiting for transfers between devices: 99.8 us -> none  [the longest x1 95.8 us: pair_tiles(): lax.psum_scatter(dev_total, 'dev', scatter_dimension=0, tiled=True)]
    all_gather x1 -> x0, waiting for transfers between devices: 59.4 us -> none  [pair_tiles(): piece_rows = lax.all_gather(image_rows, 'dev', axis=0, tiled=True)]
    ppermute x0 -> x20, waiting for transfers between devices: none -> 32.2 us  [shift(): return lax.ppermute(value, AXES, perm)]
    ppermute x0 -> x20, starting transfers between devices: none -> 19.7 us  [shift(): return lax.ppermute(value, AXES, perm)]
    dot_general x3 -> x0, matrix products: 6.87 us -> none  [the longest x1 2.72 us: pair_tiles(): lax.dot_general(piece_rows, column, (((1,), (1,)), ((), ())), preferred_e...]
    reduce_sum x4 -> x0, other arithmetic: 4.28 us -> none  [the longest x2 2.25 us: unnormalize(): along = jnp.sum(unit_rows * grad_unit, axis=-1, keepdims=True)]
    pallas_call x0 -> x2, Pallas kernels: none -> 3.97 us  [the longest x1 2.88 us: pair_terms(): pl.pallas_call(functools.partial(pairs_kernel, image_count, text_count, r...]
    mul x2 -> x0, other arithmetic: 3.58 us -> none  [unnormalize(): return factor * (grad_unit - unit_rows * along)]
  transfers between devices with their start and end apart: 3 -> 20, of which waited for: 3 -> 7; matrix products, arithmetic and copies ran while one was open for 4% -> 0% of each run, Pallas kernels for 0% -> 0%
where the time goes in v1:
time: 60.4 us; the launch traced here: 59.6 us
  waiting for transfers between devices  32.2 us (53%)
  starting transfers between devices  19.7 us (33%)
  Pallas kernels  3.97 us (7%)
  between operations  1.98 us (3%)
  local copies, waits for them, and re-layouts  1.8 us (3%)
    ppermute x20, waiting for transfers between devices, shift(): return lax.ppermute(value, AXES, perm)  32.2 us
    ppermute x20, starting transfers between devices, shift(): return lax.ppermute(value, AXES, perm)  19.7 us
    pallas_call x1, Pallas kernels, pair_terms(): pl.pallas_call(functools.partial(pairs_kernel, image_count, text_count, r...  2.88 us
    unnamed x4, local copies, waits for them, and re-layouts  1.8 us
  transfers between devices with their start and end apart: 20, of which 7 were waited for; matrix products, arithmetic and copies ran while one was open for 0% of the time, Pallas kernels for 0%

profile of v1, /device:TPU:0, one launch (start us, length us, event | category | flops | bytes accessed | tf_op | source)
XLA Modules:
  0.0 59.6 jit_solution(9425333606569768188)
XLA Ops:
  0.6 5.1 %collective-permute-start.2 = (bf16[128,512]{1,0:T(8,128)(2,1)}, bf16[128,512]{1,0:T(8,128)(2,1)S(1)}, u32[]{:S(2)}, u32[]{:S(2)}) collective-permute-start(bf16[128,512]{1,0:T(8,128)(2,1)} %image_ref.1), channel_id=1, source_target_pairs={{0,12},{1,13},{2,14},{3,15},{4,0},{5,1},{6,2},{7,3},{8,4},{9,5},{1... | collective-permute-start | bytes 393224 | tf_op jit(solution)/shard_map/ppermute | solution.py:140
  5.7 1.0 %collective-permute-start = (bf16[128,512]{1,0:T(8,128)(2,1)}, bf16[128,512]{1,0:T(8,128)(2,1)S(1)}, u32[]{:S(2)}, u32[]{:S(2)}) collective-permute-start(bf16[128,512]{1,0:T(8,128)(2,1)} %image_ref.1), channel_id=1, source_target_pairs={{0,4},{1,5},{2,6},{3,7},{4,8},{5,9},{6,10},{7,11},{8,12},{9,13},{1... | collective-permute-start | bytes 393224 | tf_op jit(solution)/shard_map/ppermute | solution.py:140
  6.7 1.0 %collective-permute-start.9 = (bf16[128,512]{1,0:T(8,128)(2,1)}, bf16[128,512]{1,0:T(8,128)(2,1)S(1)}, u32[]{:S(2)}, u32[]{:S(2)}) collective-permute-start(bf16[128,512]{1,0:T(8,128)(2,1)} %text_ref.1), channel_id=1, source_target_pairs={{0,19},{1,16},{2,17},{3,18},{4,23},{5,20},{6,21},{7,22},{8,27},{9,... | collective-permute-start | bytes 393224 | tf_op jit(solution)/shard_map/ppermute | solution.py:140
  7.8 1.4 %collective-permute-start.8 = (bf16[128,512]{1,0:T(8,128)(2,1)}, bf16[128,512]{1,0:T(8,128)(2,1)S(1)}, u32[]{:S(2)}, u32[]{:S(2)}) collective-permute-start(bf16[128,512]{1,0:T(8,128)(2,1)} %text_ref.1), channel_id=1, source_target_pairs={{0,3},{1,0},{2,1},{3,2},{4,7},{5,4},{6,5},{7,6},{8,11},{9,8},{10,9... | collective-permute-start | bytes 393224 | tf_op jit(solution)/shard_map/ppermute | solution.py:140
  9.2 0.7 %collective-permute-done.2.refs_5_ = bf16[128,512]{1,0:T(8,128)(2,1)S(1)} collective-permute-done((bf16[128,512]{1,0:T(8,128)(2,1)}, bf16[128,512]{1,0:T(8,128)(2,1)S(1)}, u32[]{:S(2)}, u32[]{:S(2)}) %collective-permute-start.2) | collective-permute-done | bytes 131104 | tf_op jit(solution)/shard_map/ppermute | solution.py:140
  10.0 7.2 %collective-permute-done.1.refs_4_ = bf16[128,512]{1,0:T(8,128)(2,1)S(1)} collective-permute-done((bf16[128,512]{1,0:T(8,128)(2,1)}, bf16[128,512]{1,0:T(8,128)(2,1)S(1)}, u32[]{:S(2)}, u32[]{:S(2)}) %collective-permute-start.1) | collective-permute-done | bytes 131104 | tf_op jit(solution)/shard_map/ppermute | solution.py:140
  17.1 1.5 %collective-permute-start.6 = (bf16[128,512]{1,0:T(8,128)(2,1)}, bf16[128,512]{1,0:T(8,128)(2,1)S(1)}, u32[]{:S(2)}, u32[]{:S(2)}) collective-permute-start(bf16[128,512]{1,0:T(8,128)(2,1)} %text_ref.1), channel_id=1, source_target_pairs={{0,2},{1,3},{2,0},{3,1},{4,6},{5,7},{6,4},{7,5},{8,10},{9,11},{10,... | collective-permute-start | bytes 393224 | tf_op jit(solution)/shard_map/ppermute | solution.py:140
  18.8 1.4 %collective-permute-start.4 = (bf16[128,512]{1,0:T(8,128)(2,1)}, bf16[128,512]{1,0:T(8,128)(2,1)S(1)}, u32[]{:S(2)}, u32[]{:S(2)}) collective-permute-start(bf16[128,512]{1,0:T(8,128)(2,1)} %text_ref.1), channel_id=1, source_target_pairs={{0,1},{1,2},{2,3},{3,0},{4,5},{5,6},{6,7},{7,4},{8,9},{9,10},{10,1... | collective-permute-start | bytes 393224 | tf_op jit(solution)/shard_map/ppermute | solution.py:140
  20.2 0.3 collective-permute-start.3
  21.8 6.2 %collective-permute-done.6.refs_10_ = bf16[128,512]{1,0:T(8,128)(2,1)S(1)} collective-permute-done((bf16[128,512]{1,0:T(8,128)(2,1)}, bf16[128,512]{1,0:T(8,128)(2,1)S(1)}, u32[]{:S(2)}, u32[]{:S(2)}) %collective-permute-start.6) | collective-permute-done | bytes 131104 | tf_op jit(solution)/shard_map/ppermute | solution.py:140
  28.0 0.9 %copy-done = bf16[128,512]{1,0:T(8,128)(2,1)S(1)} copy-done((bf16[128,512]{1,0:T(8,128)(2,1)S(1)}, bf16[128,512]{1,0:T(8,128)(2,1)}, u32[]{:S(2)}) %copy-start) | copy-done | bytes 131096
  28.9 0.9 %copy-done.1 = bf16[128,512]{1,0:T(8,128)(2,1)S(1)} copy-done((bf16[128,512]{1,0:T(8,128)(2,1)S(1)}, bf16[128,512]{1,0:T(8,128)(2,1)}, u32[]{:S(2)}) %copy-start.1) | copy-done | bytes 131096
  29.8 2.9 %pair_terms.1 = (f32[128,512]{1,0:T(8,128)S(1)}, bf16[128,512]{1,0:T(8,128)(2,1)S(1)}, bf16[128,512]{1,0:T(8,128)(2,1)S(1)}, bf16[128,512]{1,0:T(8,128)(2,1)S(1)...) custom-call(f32[1]{0:T(128)S(6)} %copy.6.refs_0_, ...), custom_call_target="tpu_custom_call" | custom-call | flops 1610612736 | bytes 3145728 | tf_op jit(solution)/shard_map/pair_terms/pallas_call | solution.py:73
  32.7 1.6 %collective-permute-start.10 = (bf16[128,512]{1,0:T(8,128)(2,1)S(1)}, bf16[128,512]{1,0:T(8,128)(2,1)S(1)}, u32[]{:S(2)}, u32[]{:S(2)}) collective-permute-start(bf16[128,512]{1,0:T(8,128)(2,1)S(1)} %get-tuple-element.15), channel_id=1, source_target_pairs={{0,12},{1,13},{2,14},{3,15},{4,0},{5,1},{6,2},{7,3},{8,4},{9,5},{1... | collective-permute-start | bytes 393224 | tf_op jit(solution)/shard_map/ppermute | solution.py:140
  34.3 1.9 %collective-permute-start.12 = (bf16[128,512]{1,0:T(8,128)(2,1)S(1)}, bf16[128,512]{1,0:T(8,128)(2,1)S(1)}, u32[]{:S(2)}, u32[]{:S(2)}) collective-permute-start(bf16[128,512]{1,0:T(8,128)(2,1)S(1)} %get-tuple-element.17), channel_id=1, source_target_pairs={{0,4},{1,5},{2,6},{3,7},{4,8},{5,9},{6,10},{7,11},{8,12},{9,13},{1... | collective-permute-start | bytes 393224 | tf_op jit(solution)/shard_map/ppermute | solution.py:140
  36.3 0.4 collective-permute-start.14
  36.7 1.6 %collective-permute-done.10.refs_1_ = bf16[128,512]{1,0:T(8,128)(2,1)S(1)} collective-permute-done((bf16[128,512]{1,0:T(8,128)(2,1)S(1)}, bf16[128,512]{1,0:T(8,128)(2,1)S(1)}, u32[]{:S(2)}, u32[]{:S(2)}) %collective-permute-start.10) | collective-permute-done | bytes 131104 | tf_op jit(solution)/shard_map/ppermute | solution.py:140
  38.3 8.0 %collective-permute-done.11.refs_2_ = bf16[128,512]{1,0:T(8,128)(2,1)S(1)} collective-permute-done((bf16[128,512]{1,0:T(8,128)(2,1)S(1)}, bf16[128,512]{1,0:T(8,128)(2,1)S(1)}, u32[]{:S(2)}, u32[]{:S(2)}) %collective-permute-start.11) | collective-permute-done | bytes 131104 | tf_op jit(solution)/shard_map/ppermute | solution.py:140
  46.3 0.7 %collective-permute-start.16 = (bf16[128,512]{1,0:T(8,128)(2,1)S(1)}, bf16[128,512]{1,0:T(8,128)(2,1)S(1)}, u32[]{:S(2)}, u32[]{:S(2)}) collective-permute-start(bf16[128,512]{1,0:T(8,128)(2,1)S(1)} %get-tuple-element.22), channel_id=1, source_target_pairs={{0,2},{1,3},{2,0},{3,1},{4,6},{5,7},{6,4},{7,5},{8,10},{9,11},{10,... | collective-permute-start | bytes 393224 | tf_op jit(solution)/shard_map/ppermute | solution.py:140
  47.2 0.6 collective-permute-start.18
  47.7 2.3 %collective-permute-start.19 = (bf16[128,512]{1,0:T(8,128)(2,1)S(1)}, bf16[128,512]{1,0:T(8,128)(2,1)S(1)}, u32[]{:S(2)}, u32[]{:S(2)}) collective-permute-start(bf16[128,512]{1,0:T(8,128)(2,1)S(1)} %get-tuple-element.25), channel_id=1, source_target_pairs={{0,17},{1,18},{2,19},{3,16},{4,21},{5,22},{6,23},{7,20},{8,25},{9,... | collective-permute-start | bytes 393224 | tf_op jit(solution)/shard_map/ppermute | solution.py:140
  50.0 8.1 %collective-permute-done.16.refs_8_ = bf16[128,512]{1,0:T(8,128)(2,1)S(1)} collective-permute-done((bf16[128,512]{1,0:T(8,128)(2,1)S(1)}, bf16[128,512]{1,0:T(8,128)(2,1)S(1)}, u32[]{:S(2)}, u32[]{:S(2)}) %collective-permute-start.16) | collective-permute-done | bytes 131104 | tf_op jit(solution)/shard_map/ppermute | solution.py:140
  58.2 0.3 collective-permute-done.17.refs_9_
  58.5 1.1 %finish.1 = (f32[128,512]{1,0:T(8,128)}, f32[128,512]{1,0:T(8,128)}) custom-call(bf16[128,512]{1,0:T(8,128)(2,1)S(1)} %copy-done, bf16[128,512]{1,0:T(8,128)(2,1)S(1)} %copy-done.1, f32[128,512]{1,0:T(8,128)S(1)} %get-tuple-element.14.refs_0_, bf16[128,512]{1,0:T(8,128)(2,1)S(1)} %collective-permute-done.10.refs_1_, ...), custom_call_target="tpu_custom_call" | custom-call | flops 7864320 | bytes 2359296 | tf_op jit(solution)/shard_map/finish/pallas_call | solution.py:110
  (22 shorter events, 0.3 us)
Async XLA Ops:
  0.6 9.3 %collective-permute-start.2 = (bf16[128,512]{1,0:T(8,128)(2,1)}, bf16[128,512]{1,0:T(8,128)(2,1)S(1)}, u32[]{:S(2)}, u32[]{:S(2)}) collective-permute-start(bf16[128,512]{1,0:T(8,128)(2,1)} %image_ref.1), channel_id=1, source_target_pairs={{0,12},{1,13},{2,14},{3,15},{4,0},{5,1},{6,2},{7,3},{8,4},{9,5},{1... | collective-permute-start | bytes 393224 | tf_op jit(solution)/shard_map/ppermute | solution.py:140
  5.7 11.4 %collective-permute-start.1 = (bf16[128,512]{1,0:T(8,128)(2,1)}, bf16[128,512]{1,0:T(8,128)(2,1)S(1)}, u32[]{:S(2)}, u32[]{:S(2)}) collective-permute-start(bf16[128,512]{1,0:T(8,128)(2,1)} %image_ref.1), channel_id=1, source_target_pairs={{0,8},{1,9},{2,10},{3,11},{4,12},{5,13},{6,14},{7,15},{8,0},{9,1},... | collective-permute-start | bytes 393224 | tf_op jit(solution)/shard_map/ppermute | solution.py:140
  5.7 12.9 %collective-permute-start = (bf16[128,512]{1,0:T(8,128)(2,1)}, bf16[128,512]{1,0:T(8,128)(2,1)S(1)}, u32[]{:S(2)}, u32[]{:S(2)}) collective-permute-start(bf16[128,512]{1,0:T(8,128)(2,1)} %image_ref.1), channel_id=1, source_target_pairs={{0,4},{1,5},{2,6},{3,7},{4,8},{5,9},{6,10},{7,11},{8,12},{9,13},{1... | collective-permute-start | bytes 393224 | tf_op jit(solution)/shard_map/ppermute | solution.py:140
  6.7 12.1 %collective-permute-start.9 = (bf16[128,512]{1,0:T(8,128)(2,1)}, bf16[128,512]{1,0:T(8,128)(2,1)S(1)}, u32[]{:S(2)}, u32[]{:S(2)}) collective-permute-start(bf16[128,512]{1,0:T(8,128)(2,1)} %text_ref.1), channel_id=1, source_target_pairs={{0,19},{1,16},{2,17},{3,18},{4,23},{5,20},{6,21},{7,22},{8,27},{9,... | collective-permute-start | bytes 393224 | tf_op jit(solution)/shard_map/ppermute | solution.py:140
  7.8 12.4 %collective-permute-start.8 = (bf16[128,512]{1,0:T(8,128)(2,1)}, bf16[128,512]{1,0:T(8,128)(2,1)S(1)}, u32[]{:S(2)}, u32[]{:S(2)}) collective-permute-start(bf16[128,512]{1,0:T(8,128)(2,1)} %text_ref.1), channel_id=1, source_target_pairs={{0,3},{1,0},{2,1},{3,2},{4,7},{5,4},{6,5},{7,6},{8,11},{9,8},{10,9... | collective-permute-start | bytes 393224 | tf_op jit(solution)/shard_map/ppermute | solution.py:140
  10.0 11.8 %collective-permute-start.7 = (bf16[128,512]{1,0:T(8,128)(2,1)}, bf16[128,512]{1,0:T(8,128)(2,1)S(1)}, u32[]{:S(2)}, u32[]{:S(2)}) collective-permute-start(bf16[128,512]{1,0:T(8,128)(2,1)} %text_ref.1), channel_id=1, source_target_pairs={{0,18},{1,19},{2,16},{3,17},{4,22},{5,23},{6,20},{7,21},{8,26},{9,... | collective-permute-start | bytes 393224 | tf_op jit(solution)/shard_map/ppermute | solution.py:140
  17.1 10.8 %collective-permute-start.6 = (bf16[128,512]{1,0:T(8,128)(2,1)}, bf16[128,512]{1,0:T(8,128)(2,1)S(1)}, u32[]{:S(2)}, u32[]{:S(2)}) collective-permute-start(bf16[128,512]{1,0:T(8,128)(2,1)} %text_ref.1), channel_id=1, source_target_pairs={{0,2},{1,3},{2,0},{3,1},{4,6},{5,7},{6,4},{7,5},{8,10},{9,11},{10,... | collective-permute-start | bytes 393224 | tf_op jit(solution)/shard_map/ppermute | solution.py:140
  18.7 9.3 %collective-permute-start.5 = (bf16[128,512]{1,0:T(8,128)(2,1)}, bf16[128,512]{1,0:T(8,128)(2,1)S(1)}, u32[]{:S(2)}, u32[]{:S(2)}) collective-permute-start(bf16[128,512]{1,0:T(8,128)(2,1)} %text_ref.1), channel_id=1, source_target_pairs={{0,17},{1,18},{2,19},{3,16},{4,21},{5,22},{6,23},{7,20},{8,25},{9,... | collective-permute-start | bytes 393224 | tf_op jit(solution)/shard_map/ppermute | solution.py:140
  18.8 9.1 %collective-permute-start.4 = (bf16[128,512]{1,0:T(8,128)(2,1)}, bf16[128,512]{1,0:T(8,128)(2,1)S(1)}, u32[]{:S(2)}, u32[]{:S(2)}) collective-permute-start(bf16[128,512]{1,0:T(8,128)(2,1)} %text_ref.1), channel_id=1, source_target_pairs={{0,1},{1,2},{2,3},{3,0},{4,5},{5,6},{6,7},{7,4},{8,9},{9,10},{10,1... | collective-permute-start | bytes 393224 | tf_op jit(solution)/shard_map/ppermute | solution.py:140
  20.2 7.7 %collective-permute-start.3 = (bf16[128,512]{1,0:T(8,128)(2,1)}, bf16[128,512]{1,0:T(8,128)(2,1)S(1)}, u32[]{:S(2)}, u32[]{:S(2)}) collective-permute-start(bf16[128,512]{1,0:T(8,128)(2,1)} %text_ref.1), channel_id=1, source_target_pairs={{0,16},{1,17},{2,18},{3,19},{4,20},{5,21},{6,22},{7,23},{8,24},{9,... | collective-permute-start | bytes 393224 | tf_op jit(solution)/shard_map/ppermute | solution.py:140
  28.0 0.9 %copy-start = (bf16[128,512]{1,0:T(8,128)(2,1)S(1)}, bf16[128,512]{1,0:T(8,128)(2,1)}, u32[]{:S(2)}) copy-start(bf16[128,512]{1,0:T(8,128)(2,1)} %image_ref.1) | copy-start | bytes 393220
  28.9 0.9 %copy-start.1 = (bf16[128,512]{1,0:T(8,128)(2,1)S(1)}, bf16[128,512]{1,0:T(8,128)(2,1)}, u32[]{:S(2)}) copy-start(bf16[128,512]{1,0:T(8,128)(2,1)} %text_ref.1) | copy-start | bytes 393220
  32.7 5.6 %collective-permute-start.10 = (bf16[128,512]{1,0:T(8,128)(2,1)S(1)}, bf16[128,512]{1,0:T(8,128)(2,1)S(1)}, u32[]{:S(2)}, u32[]{:S(2)}) collective-permute-start(bf16[128,512]{1,0:T(8,128)(2,1)S(1)} %get-tuple-element.15), channel_id=1, source_target_pairs={{0,12},{1,13},{2,14},{3,15},{4,0},{5,1},{6,2},{7,3},{8,4},{9,5},{1... | collective-permute-start | bytes 393224 | tf_op jit(solution)/shard_map/ppermute | solution.py:140
  34.3 12.0 %collective-permute-start.11 = (bf16[128,512]{1,0:T(8,128)(2,1)S(1)}, bf16[128,512]{1,0:T(8,128)(2,1)S(1)}, u32[]{:S(2)}, u32[]{:S(2)}) collective-permute-start(bf16[128,512]{1,0:T(8,128)(2,1)S(1)} %get-tuple-element.16), channel_id=1, source_target_pairs={{0,8},{1,9},{2,10},{3,11},{4,12},{5,13},{6,14},{7,15},{8,0},{9,1},... | collective-permute-start | bytes 393224 | tf_op jit(solution)/shard_map/ppermute | solution.py:140
  34.3 12.8 %collective-permute-start.12 = (bf16[128,512]{1,0:T(8,128)(2,1)S(1)}, bf16[128,512]{1,0:T(8,128)(2,1)S(1)}, u32[]{:S(2)}, u32[]{:S(2)}) collective-permute-start(bf16[128,512]{1,0:T(8,128)(2,1)S(1)} %get-tuple-element.17), channel_id=1, source_target_pairs={{0,4},{1,5},{2,6},{3,7},{4,8},{5,9},{6,10},{7,11},{8,12},{9,13},{1... | collective-permute-start | bytes 393224 | tf_op jit(solution)/shard_map/ppermute | solution.py:140
  36.3 10.9 %collective-permute-start.13 = (bf16[128,512]{1,0:T(8,128)(2,1)S(1)}, bf16[128,512]{1,0:T(8,128)(2,1)S(1)}, u32[]{:S(2)}, u32[]{:S(2)}) collective-permute-start(bf16[128,512]{1,0:T(8,128)(2,1)S(1)} %get-tuple-element.19), channel_id=1, source_target_pairs={{0,16},{1,17},{2,18},{3,19},{4,20},{5,21},{6,22},{7,23},{8,24},{9,... | collective-permute-start | bytes 393224 | tf_op jit(solution)/shard_map/ppermute | solution.py:140
  36.3 11.5 %collective-permute-start.14 = (bf16[128,512]{1,0:T(8,128)(2,1)S(1)}, bf16[128,512]{1,0:T(8,128)(2,1)S(1)}, u32[]{:S(2)}, u32[]{:S(2)}) collective-permute-start(bf16[128,512]{1,0:T(8,128)(2,1)S(1)} %get-tuple-element.20), channel_id=1, source_target_pairs={{0,3},{1,0},{2,1},{3,2},{4,7},{5,4},{6,5},{7,6},{8,11},{9,8},{10,9... | collective-permute-start | bytes 393224 | tf_op jit(solution)/shard_map/ppermute | solution.py:140
  38.3 11.7 %collective-permute-start.15 = (bf16[128,512]{1,0:T(8,128)(2,1)S(1)}, bf16[128,512]{1,0:T(8,128)(2,1)S(1)}, u32[]{:S(2)}, u32[]{:S(2)}) collective-permute-start(bf16[128,512]{1,0:T(8,128)(2,1)S(1)} %get-tuple-element.21), channel_id=1, source_target_pairs={{0,19},{1,16},{2,17},{3,18},{4,23},{5,20},{6,21},{7,22},{8,27},{9,... | collective-permute-start | bytes 393224 | tf_op jit(solution)/shard_map/ppermute | solution.py:140
  46.3 11.8 %collective-permute-start.16 = (bf16[128,512]{1,0:T(8,128)(2,1)S(1)}, bf16[128,512]{1,0:T(8,128)(2,1)S(1)}, u32[]{:S(2)}, u32[]{:S(2)}) collective-permute-start(bf16[128,512]{1,0:T(8,128)(2,1)S(1)} %get-tuple-element.22), channel_id=1, source_target_pairs={{0,2},{1,3},{2,0},{3,1},{4,6},{5,7},{6,4},{7,5},{8,10},{9,11},{10,... | collective-permute-start | bytes 393224 | tf_op jit(solution)/shard_map/ppermute | solution.py:140
  47.1 11.4 %collective-permute-start.17 = (bf16[128,512]{1,0:T(8,128)(2,1)S(1)}, bf16[128,512]{1,0:T(8,128)(2,1)S(1)}, u32[]{:S(2)}, u32[]{:S(2)}) collective-permute-start(bf16[128,512]{1,0:T(8,128)(2,1)S(1)} %get-tuple-element.23), channel_id=1, source_target_pairs={{0,18},{1,19},{2,16},{3,17},{4,22},{5,23},{6,20},{7,21},{8,26},{9,... | collective-permute-start | bytes 393224 | tf_op jit(solution)/shard_map/ppermute | solution.py:140
  47.2 11.3 %collective-permute-start.18 = (bf16[128,512]{1,0:T(8,128)(2,1)S(1)}, bf16[128,512]{1,0:T(8,128)(2,1)S(1)}, u32[]{:S(2)}, u32[]{:S(2)}) collective-permute-start(bf16[128,512]{1,0:T(8,128)(2,1)S(1)} %get-tuple-element.24), channel_id=1, source_target_pairs={{0,1},{1,2},{2,3},{3,0},{4,5},{5,6},{6,7},{7,4},{8,9},{9,10},{10,1... | collective-permute-start | bytes 393224 | tf_op jit(solution)/shard_map/ppermute | solution.py:140
  47.7 10.8 %collective-permute-start.19 = (bf16[128,512]{1,0:T(8,128)(2,1)S(1)}, bf16[128,512]{1,0:T(8,128)(2,1)S(1)}, u32[]{:S(2)}, u32[]{:S(2)}) collective-permute-start(bf16[128,512]{1,0:T(8,128)(2,1)S(1)} %get-tuple-element.25), channel_id=1, source_target_pairs={{0,17},{1,18},{2,19},{3,16},{4,21},{5,22},{6,23},{7,20},{8,25},{9,... | collective-permute-start | bytes 393224 | tf_op jit(solution)/shard_map/ppermute | solution.py:140

commit v2 on v1

v2 whole, which is shorter than its diff:
```python
import functools
import math

import jax
import jax.numpy as jnp
from jax import lax
from jax.experimental import pallas as pl
from jax.experimental.pallas import tpu as pltpu
from jax.sharding import PartitionSpec as P

AXES = ("grp", "dev")
VMEM_LIMIT = 50 * 1024 * 1024


def unit_rows(raw):
    wide = raw.astype(jnp.float32)
    factor = lax.rsqrt(jnp.sum(wide * wide, axis=-1, keepdims=True) + 1e-06)
    return wide * factor, factor


def pairs_kernel(image_count, text_count, rows, span, *refs):
    scale_ref, bias_ref = refs[:2]
    image_refs = [refs[2].at[a] for a in range(image_count)]
    text_refs = [refs[3].at[c] for c in range(text_count)]
    at_ref = refs[4]
    image_out = [refs[5].at[a] for a in range(image_count)]
    text_out = [refs[6].at[c] for c in range(text_count)]
    v_images, image_acc = refs[7:]
    image_at, text_at = at_ref[0], at_ref[1]
    temper = scale_ref[0]
    offset = bias_ref[0]
    for a, ref in enumerate(image_refs):
        unit, _ = unit_rows(ref[...])
        v_images[a * rows:(a + 1) * rows, :] = unit.astype(jnp.bfloat16)
    vi = v_images[...]
    for first in range(0, text_count, span):
        here = range(first, min(first + span, text_count))
        vt = jnp.concatenate(
            [unit_rows(text_refs[c][...])[0].astype(jnp.bfloat16) for c in here], axis=0
        )
        logits = temper * lax.dot_general(
            vi, vt, (((1,), (1,)), ((), ())), preferred_element_type=jnp.float32
        ) + offset
        chance = 1.0 / (1.0 + jnp.exp(-logits))
        row = lax.broadcasted_iota(jnp.int32, chance.shape, 0) - image_at * rows
        column = lax.broadcasted_iota(jnp.int32, chance.shape, 1) - (text_at - first) * rows
        same = (row == column) & (row >= 0) & (row < rows)
        chance = chance - same.astype(jnp.float32)
        coefficient = (temper * chance).astype(jnp.bfloat16)
        image_part = jnp.dot(coefficient, vt, preferred_element_type=jnp.float32)
        text_part = lax.dot_general(
            coefficient, vi, (((0,), (0,)), ((), ())), preferred_element_type=jnp.float32
        )
        for at, c in enumerate(here):
            text_out[c][...] = text_part[at * rows:(at + 1) * rows, :].astype(text_out[c].dtype)
        if first == 0:
            image_acc[...] = image_part
        else:
            image_acc[...] += image_part
    for a, ref in enumerate(image_out):
        ref[...] = image_acc[a * rows:(a + 1) * rows, :].astype(ref.dtype)


def pair_terms(images, texts, scale, bias, image_at, text_at):
    image_count, rows, width = images.shape
    text_count = texts.shape[0]
    out_shape = [
        jax.ShapeDtypeStruct(images.shape, jnp.bfloat16),
        jax.ShapeDtypeStruct(texts.shape, jnp.bfloat16),
    ]
    smem = pl.BlockSpec(memory_space=pltpu.SMEM)
    vmem = pl.BlockSpec(memory_space=pltpu.VMEM)
    pairs = image_count * text_count * rows * rows
    return pl.pallas_call(
        functools.partial(pairs_kernel, image_count, text_count, rows, 2),
        out_shape=out_shape,
        in_specs=[smem, smem, vmem, vmem, smem],
        out_specs=[vmem] * len(out_shape),
        scratch_shapes=[
            pltpu.VMEM((image_count * rows, width), jnp.bfloat16),
            pltpu.VMEM((image_count * rows, width), jnp.float32),
        ],
        compiler_params=pltpu.CompilerParams(vmem_limit_bytes=VMEM_LIMIT),
        cost_estimate=pl.CostEstimate(
            flops=6 * pairs * width,
            bytes_accessed=4 * (image_count + text_count) * rows * width,
            transcendentals=2 * pairs,
        ),
        name="pair_terms",
    )(scale, bias, images, texts, jnp.stack([image_at, text_at]))


def finish_kernel(image_count, text_count, image_ref, text_ref, *refs):
    image_parts = [refs[0].at[a] for a in range(image_count)]
    text_parts = [refs[1].at[c] for c in range(text_count)]
    outs = refs[2:]
    for raw, parts, out in ((image_ref, image_parts, outs[0]), (text_ref, text_parts, outs[1])):
        unit, factor = unit_rows(raw[...])
        total = parts[0][...].astype(jnp.float32)
        for part in parts[1:]:
            total = total + part[...].astype(jnp.float32)
        along = jnp.sum(unit * total, axis=-1, keepdims=True)
        out[...] = factor * (total - unit * along)


def finish(images, texts, image_parts, text_parts):
    out = jax.ShapeDtypeStruct(images.shape, jnp.float32)
    vmem = pl.BlockSpec(memory_space=pltpu.VMEM)
    count = image_parts.shape[0] + text_parts.shape[0]
    return pl.pallas_call(
        functools.partial(finish_kernel, image_parts.shape[0], text_parts.shape[0]),
        out_shape=(out, out),
        in_specs=[vmem] * 4,
        out_specs=(vmem, vmem),
        compiler_params=pltpu.CompilerParams(vmem_limit_bytes=VMEM_LIMIT),
        cost_estimate=pl.CostEstimate(
            flops=10 * count * images.size, bytes_accessed=3 * count * images.size,
            transcendentals=0,
        ),
        name="finish",
    )(images, texts, image_parts, text_parts)


def plan(grp_count, dev_count):
    options = [n for n in range(1, dev_count + 1) if dev_count % n == 0]
    near = min(options, key=lambda n: (dev_count // n + grp_count * n, -n))
    return dev_count // near, near


def solution(mesh):
    grp_count, dev_count = mesh.shape["grp"], mesh.shape["dev"]
    far_count, near_count = plan(grp_count, dev_count)
    image_groups = [
        [(g * far_count + f) * near_count + n for f in range(far_count)]
        for g in range(grp_count) for n in range(near_count)
    ]
    text_groups = [
        [(g * far_count + f) * near_count + n for g in range(grp_count) for n in range(near_count)]
        for f in range(far_count)
    ]

    def swap(value, groups):
        return lax.all_to_all(value, AXES, 0, 0, axis_index_groups=groups, tiled=True)

    def on_device(images, texts, logit_scale, logit_bias):
        group_at, dev_at = lax.axis_index("grp"), lax.axis_index("dev")
        image_at = dev_at // near_count
        text_at = group_at * near_count + dev_at % near_count
        image_rows = swap(jnp.broadcast_to(images, (far_count,) + images.shape), image_groups)
        text_rows = swap(
            jnp.broadcast_to(texts, (grp_count * near_count,) + texts.shape), text_groups
        )
        image_parts, text_parts = pair_terms(
            image_rows, text_rows, logit_scale, logit_bias, image_at, text_at
        )
        return finish(
            images, texts, swap(image_parts, image_groups), swap(text_parts, text_groups)
        )

    in_specs = (P(AXES, None), P(AXES, None), P(), P())
    out_specs = (P(AXES, None), P(AXES, None))
    return jax.shard_map(
        on_device, mesh=mesh, in_specs=in_specs, out_specs=out_specs, check_vma=False
    )
```

time: 60.4 us -> 82.3 us (1.36)
  blocking collectives: 0 us -> 55.9 us
  waiting for transfers between devices: 32.2 us -> 13.5 us
  starting transfers between devices: 19.7 us -> 3.72 us
    all_to_all x0 -> x3, blocking collectives: none -> 55.9 us  [swap(): lax.all_to_all(value, AXES, 0, 0, axis_index_groups=groups, tiled=True)]
    ppermute x20 -> x0, waiting for transfers between devices: 32.2 us -> none  [shift(): return lax.ppermute(value, AXES, perm)]
    ppermute x20 -> x0, starting transfers between devices: 19.7 us -> none  [shift(): return lax.ppermute(value, AXES, perm)]
    all_to_all x0 -> x1, waiting for transfers between devices: none -> 13.5 us  [swap(): lax.all_to_all(value, AXES, 0, 0, axis_index_groups=groups, tiled=True)]
    all_to_all x0 -> x1, starting transfers between devices: none -> 3.72 us  [swap(): lax.all_to_all(value, AXES, 0, 0, axis_index_groups=groups, tiled=True)]
    broadcast_in_dim x0 -> x2, local copies, waits for them, and re-layouts: none -> 2 us  [the longest x1 1.05 us: on_device(): jnp.broadcast_to(texts, (grp_count * near_count,) + texts.shape)]
    unnamed x4, local copies, waits for them, and re-layouts: 1.8 us -> 0.01 us
  transfers between devices with their start and end apart: 20 -> 1, of which waited for: 7 -> 1; matrix products, arithmetic and copies ran while one was open for 0% -> 0% of each run, Pallas kernels for 0% -> 0%
where the time goes in v2:
time: 82.3 us; the launch traced here: 81.9 us
  blocking collectives  55.9 us (68%)
  waiting for transfers between devices  13.5 us (16%)
  Pallas kernels  4.76 us (6%)
  starting transfers between devices  3.72 us (5%)
  local copies, waits for them, and re-layouts  2.01 us (2%)
  between operations  1.96 us (2%)
    all_to_all x3, blocking collectives, swap(): lax.all_to_all(value, AXES, 0, 0, axis_index_groups=groups, tiled=True)  55.9 us
    all_to_all x1, waiting for transfers between devices, swap(): lax.all_to_all(value, AXES, 0, 0, axis_index_groups=groups, tiled=True)  13.5 us
    all_to_all x1, starting transfers between devices, swap(): lax.all_to_all(value, AXES, 0, 0, axis_index_groups=groups, tiled=True)  3.72 us
    pallas_call x1, Pallas kernels, pair_terms(): pl.pallas_call(functools.partial(pairs_kernel, image_count, text_count, r...  3.65 us
  transfers between devices with their start and end apart: 1, of which 1 were waited for; matrix products, arithmetic and copies ran while one was open for 0% of the time, Pallas kernels for 0%

profile of v2, /device:TPU:0, one launch (start us, length us, event | category | flops | bytes accessed | tf_op | source)
XLA Modules:
  0.0 81.9 jit_solution(1799388527875730838)
XLA Ops:
  0.6 0.9 %broadcast_in_dim.6 = bf16[4,128,512]{2,1,0:T(8,128)(2,1)S(1)} broadcast(bf16[128,512]{1,0:T(8,128)(2,1)} %image_ref.1), dimensions={1,2} | broadcast | bytes 655360 | tf_op jit(solution)/shard_map/broadcast_in_dim | solution.py:149
  1.6 0.0 copy-start.1
  1.6 20.7 %all_to_all.20.refs_2_ = bf16[4,128,512]{2,1,0:T(8,128)(2,1)S(1)} all-to-all(bf16[4,128,512]{2,1,0:T(8,128)(2,1)S(1)} %broadcast_in_dim.6), channel_id=1, replica_groups={{0,4,8,12},{1,5,9,13},{2,6,10,14},{3,7,11,15},{16,20,24,28},{17,21,25,2..., dimensions={0} | all-to-all | bytes 1048576 | tf_op jit(solution)/shard_map/all_to_all | solution.py:143
  22.3 0.0 copy-done.1
  22.3 1.1 %broadcast_in_dim.7 = bf16[8,128,512]{2,1,0:T(8,128)(2,1)} broadcast(bf16[128,512]{1,0:T(8,128)(2,1)S(1)} %copy-done.1), dimensions={1,2} | broadcast | bytes 1179648 | tf_op jit(solution)/shard_map/broadcast_in_dim | solution.py:151
  23.4 3.7 %all-to-all-start.1 = ((bf16[8,128,512]{2,1,0:T(8,128)(2,1)}), bf16[8,128,512]{2,1,0:T(8,128)(2,1)S(1)}, u32[]{:S(2)}, u32[]{:S(2)}) async-start(bf16[8,128,512]{2,1,0:T(8,128)(2,1)} %broadcast_in_dim.7), calls=%async_computation.1 | async-start | bytes 2097152 | tf_op jit(solution)/shard_map/all_to_all | solution.py:143
  28.4 0.1 pad_add_fusion.refs_4_
  28.5 13.5 %all-to-all-done.1.refs_3_ = bf16[8,128,512]{2,1,0:T(8,128)(2,1)S(1)} async-done(((bf16[8,128,512]{2,1,0:T(8,128)(2,1)}), bf16[8,128,512]{2,1,0:T(8,128)(2,1)S(1)}, u32[]{:S(2)}, u32[]{:S(2)}) %all-to-all-start.1) | async-done | bytes 1048608 | tf_op jit(solution)/shard_map/all_to_all | solution.py:143
  42.0 3.6 %pair_terms.1 = (bf16[4,128,512]{2,1,0:T(8,128)(2,1)S(1)}, bf16[8,128,512]{2,1,0:T(8,128)(2,1)S(1)}) custom-call(f32[1]{0:T(128)S(6)} %copy.6.refs_0_, f32[1]{0:T(128)S(6)} %copy.7.refs_1_, bf16[4,128,512]{2,1,0:T(8,128)(2,1)S(1)} %all_to_all.20.refs_2_, bf16[8,128,512]{2,1,0:T(8,128)(2,1)S(1)} %all-to-all-done.1.refs_3_, s32[2]{0:T(128)S(1)} %pad_add_fusion.refs_4_), custom_call_target="tpu_custom_call" | custom-call | flops 1610612736 | bytes 3145728 | tf_op jit(solution)/shard_map/pair_terms/pallas_call | solution.py:74
  45.6 17.6 %all_to_all.21.refs_0_ = bf16[4,128,512]{2,1,0:T(8,128)(2,1)S(1)} all-to-all(bf16[4,128,512]{2,1,0:T(8,128)(2,1)S(1)} %get-tuple-element.4), channel_id=1, replica_groups={{0,4,8,12},{1,5,9,13},{2,6,10,14},{3,7,11,15},{16,20,24,28},{17,21,25,2..., dimensions={0} | all-to-all | bytes 1048576 | tf_op jit(solution)/shard_map/all_to_all | solution.py:143
  63.3 0.0 copy-start
  63.3 17.5 %all_to_all.22.refs_1_ = bf16[8,128,512]{2,1,0:T(8,128)(2,1)S(1)} all-to-all(bf16[8,128,512]{2,1,0:T(8,128)(2,1)S(1)} %get-tuple-element.5), channel_id=1, replica_groups={{0,1,2,3,16,17,18,19},{4,5,6,7,20,21,22,23},{8,9,10,11,24,25,26,27},{12..., dimensions={0} | all-to-all | bytes 2097152 | tf_op jit(solution)/shard_map/all_to_all | solution.py:143
  80.8 0.0 copy-done
  80.8 1.1 %finish.1 = (f32[128,512]{1,0:T(8,128)}, f32[128,512]{1,0:T(8,128)}) custom-call(bf16[128,512]{1,0:T(8,128)(2,1)S(1)} %copy-done, bf16[128,512]{1,0:T(8,128)(2,1)S(1)} %copy-done.1, bf16[4,128,512]{2,1,0:T(8,128)(2,1)S(1)} %all_to_all.21.refs_0_, bf16[8,128,512]{2,1,0:T(8,128)(2,1)S(1)} %all_to_all.22.refs_1_), custom_call_target="tpu_custom_call" | custom-call | flops 7864320 | bytes 2359296 | tf_op jit(solution)/shard_map/finish/pallas_call | solution.py:110
Async XLA Ops:
  1.6 20.8 %copy-start.1 = (bf16[128,512]{1,0:T(8,128)(2,1)S(1)}, bf16[128,512]{1,0:T(8,128)(2,1)}, u32[]{:S(2)}) copy-start(bf16[128,512]{1,0:T(8,128)(2,1)} %text_ref.1) | copy-start | bytes 393220
  23.4 18.6 %all-to-all-start.1 = ((bf16[8,128,512]{2,1,0:T(8,128)(2,1)}), bf16[8,128,512]{2,1,0:T(8,128)(2,1)S(1)}, u32[]{:S(2)}, u32[]{:S(2)}) async-start(bf16[8,128,512]{2,1,0:T(8,128)(2,1)} %broadcast_in_dim.7), calls=%async_computation.1 | async-start | bytes 2097152 | tf_op jit(solution)/shard_map/all_to_all | solution.py:143
  63.3 17.5 %copy-start = (bf16[128,512]{1,0:T(8,128)(2,1)S(1)}, bf16[128,512]{1,0:T(8,128)(2,1)}, u32[]{:S(2)}) copy-start(bf16[128,512]{1,0:T(8,128)(2,1)} %image_ref.1) | copy-start | bytes 393220

commit v3 on v1

v3 whole, which is shorter than its diff:
```python
import functools

import jax
import jax.numpy as jnp
from jax import lax
from jax.experimental import pallas as pl
from jax.experimental.pallas import tpu as pltpu
from jax.sharding import PartitionSpec as P

AXES = ("grp", "dev")
VMEM_LIMIT = 50 * 1024 * 1024
SPAN = 256
EARLY = 10
VMEM = pl.BlockSpec(memory_space=pltpu.VMEM)


def unit_rows(raw):
    wide = raw.astype(jnp.float32)
    factor = lax.rsqrt(jnp.sum(wide * wide, axis=-1, keepdims=True) + 1e-06)
    return wide * factor, factor


def call(kernel, out_shape, operands, scratch=(), flops=0, transcendentals=0, name=None):
    touched = sum(x.size * x.dtype.itemsize for x in list(operands) + list(out_shape))
    outs = pl.pallas_call(
        kernel,
        out_shape=out_shape,
        in_specs=[VMEM] * len(operands),
        out_specs=[VMEM] * len(out_shape),
        scratch_shapes=scratch,
        compiler_params=pltpu.CompilerParams(vmem_limit_bytes=VMEM_LIMIT),
        cost_estimate=pl.CostEstimate(
            flops=flops, bytes_accessed=touched, transcendentals=transcendentals
        ),
        name=name,
    )(*operands)
    return tuple(outs)


def stack_units_kernel(*refs):
    out = refs[-1]
    rows = refs[0].shape[0]
    for at, ref in enumerate(refs[:-1]):
        out[at * rows:(at + 1) * rows, :] = unit_rows(ref[...])[0].astype(out.dtype)


def stack_units(blocks):
    rows, width = blocks[0].shape
    out = jax.ShapeDtypeStruct((len(blocks) * rows, width), jnp.bfloat16)
    return call(stack_units_kernel, [out], blocks, flops=4 * out.size, name="stack_units")[0]


def pairs(vi, temper, offset, text_ref, text_out, own):
    held = text_ref.shape[0]
    total = None
    for first in range(0, held, SPAN):
        last = min(first + SPAN, held)
        vt = text_ref[first:last, :]
        logits = temper * lax.dot_general(
            vi, vt, (((1,), (1,)), ((), ())), preferred_element_type=jnp.float32
        ) + offset
        chance = 1.0 / (1.0 + jnp.exp(-logits))
        if own and first == 0:
            row = lax.broadcasted_iota(jnp.int32, chance.shape, 0)
            column = lax.broadcasted_iota(jnp.int32, chance.shape, 1)
            same = (row == column) & (row < own)
            chance = chance - same.astype(jnp.float32)
        coefficient = (temper * chance).astype(jnp.bfloat16)
        text_out[first:last, :] = lax.dot_general(
            coefficient, vi, (((0,), (0,)), ((), ())), preferred_element_type=jnp.float32
        ).astype(text_out.dtype)
        part = jnp.dot(coefficient, vt, preferred_element_type=jnp.float32)
        total = part if total is None else total + part
    return total


def own_pairs_kernel(params_ref, text_ref, *refs):
    image_refs, (text_out, units_out, total_out) = refs[:-3], refs[-3:]
    rows = image_refs[0].shape[0]
    for a, ref in enumerate(image_refs):
        units_out[a * rows:(a + 1) * rows, :] = unit_rows(ref[...])[0].astype(jnp.bfloat16)
    temper, offset = params_ref[0:1, 0:1], params_ref[1:2, 0:1]
    total_out[...] = pairs(units_out[...], temper, offset, text_ref, text_out, rows)


def other_pairs_kernel(text_count, params_ref, units_ref, total_ref, *refs):
    text_refs, outs = refs[:text_count], refs[text_count:]
    text_out, image_out = outs[:text_count], outs[text_count:]
    rows = image_out[0].shape[0]
    vi = units_ref[...]
    temper, offset = params_ref[0:1, 0:1], params_ref[1:2, 0:1]
    total = total_ref[...]
    for t in range(text_count):
        total = total + pairs(vi, temper, offset, text_refs[t], text_out[t], 0)
    for a, ref in enumerate(image_out):
        ref[...] = total[a * rows:(a + 1) * rows, :].astype(ref.dtype)


def pair_terms(params, images, texts):
    rows, width = images[0].shape
    image_rows = rows * len(images)

    def cost(text_rows):
        return dict(
            flops=6 * image_rows * text_rows * width, transcendentals=2 * image_rows * text_rows
        )

    own_out, units, total = call(
        own_pairs_kernel,
        [
            jax.ShapeDtypeStruct(texts[0].shape, jnp.float32),
            jax.ShapeDtypeStruct((image_rows, width), jnp.bfloat16),
            jax.ShapeDtypeStruct((image_rows, width), jnp.float32),
        ],
        [params, texts[0], *images],
        name="own_pairs",
        **cost(EARLY * texts[0].shape[0]),
    )
    others = texts[1:]
    outs = call(
        functools.partial(other_pairs_kernel, len(others)),
        [jax.ShapeDtypeStruct(t.shape, jnp.bfloat16) for t in others]
        + [jax.ShapeDtypeStruct((rows, width), jnp.float32)]
        + [jax.ShapeDtypeStruct((rows, width), jnp.bfloat16)] * (len(images) - 1),
        [params, units, total, *others],
        name="other_pairs",
        **cost(sum(t.shape[0] for t in others)),
    )
    return outs[len(others):], (own_out,) + outs[:len(others)]


def add_stacks_kernel(part_count, *refs):
    parts, outs = refs[:part_count], refs[part_count:]
    rows = outs[0].shape[0]
    for at, out in enumerate(outs):
        total = parts[0][at * rows:(at + 1) * rows, :]
        for part in parts[1:]:
            total = total + part[at * rows:(at + 1) * rows, :].astype(jnp.float32)
        out[...] = total.astype(out.dtype)


def add_stacks(parts, count):
    shape = (parts[0].shape[0] // count, parts[0].shape[1])
    types = [jnp.float32] + [jnp.bfloat16] * (count - 1)
    return call(
        functools.partial(add_stacks_kernel, len(parts)),
        [jax.ShapeDtypeStruct(shape, t) for t in types],
        parts,
        flops=len(parts) * parts[0].size,
        name="add_stacks",
    )


def finish_kernel(image_count, text_count, image_ref, text_ref, *refs):
    image_parts = refs[:image_count]
    text_parts = refs[image_count:image_count + text_count]
    outs = refs[image_count + text_count:]
    for raw, parts, out in ((image_ref, image_parts, outs[0]), (text_ref, text_parts, outs[1])):
        unit, factor = unit_rows(raw[...])
        total = parts[0][...].astype(jnp.float32)
        for part in parts[1:]:
            total = total + part[...].astype(jnp.float32)
        along = jnp.sum(unit * total, axis=-1, keepdims=True)
        out[...] = factor * (total - unit * along)


def finish(images, texts, image_parts, text_parts):
    out = jax.ShapeDtypeStruct(images.shape, jnp.float32)
    count = len(image_parts) + len(text_parts)
    return call(
        functools.partial(finish_kernel, len(image_parts), len(text_parts)),
        [out, out],
        [images, texts, *image_parts, *text_parts],
        flops=10 * count * images.size,
        name="finish",
    )


def plan(grp_count, dev_count):
    options = [n for n in range(1, dev_count + 1) if dev_count % n == 0]
    near = min(options, key=lambda n: (dev_count // n + grp_count * n, -n))
    return dev_count // near, near


def step_to(at, by, count):
    if count & (count - 1) == 0:
        return at ^ abs(by)
    return (at + by) % count


def solution(mesh):
    grp_count, dev_count = mesh.shape["grp"], mesh.shape["dev"]
    far_count, near_count = plan(grp_count, dev_count)

    def move(value, by_grp=0, by_far=0, by_near=0):
        perm = []
        for g in range(grp_count):
            for f in range(far_count):
                for n in range(near_count):
                    g2 = step_to(g, by_grp, grp_count)
                    f2 = step_to(f, by_far, far_count)
                    n2 = step_to(n, by_near, near_count)
                    source = (g * far_count + f) * near_count + n
                    perm.append((source, (g2 * far_count + f2) * near_count + n2))
        return lax.ppermute(value, AXES, perm)

    def on_device(images, texts, logit_scale, logit_bias):
        params = jnp.concatenate(
            [jnp.broadcast_to(logit_scale, (1, 128)), jnp.broadcast_to(logit_bias, (1, 128))]
        )
        image_rows = [images] + [move(images, by_far=f) for f in range(1, far_count)]
        near_rows = [texts] + [move(texts, by_near=n) for n in range(1, near_count)]
        own_stack = stack_units(near_rows)
        stacks = [own_stack] + [move(own_stack, by_grp=g) for g in range(1, grp_count)]
        image_parts, text_parts = pair_terms(params, image_rows, stacks)
        image_parts = [image_parts[0]] + [
            move(part, by_far=-f) for f, part in enumerate(image_parts) if f
        ]
        text_parts = [text_parts[0]] + [
            move(part, by_grp=-g) for g, part in enumerate(text_parts) if g
        ]
        near_parts = add_stacks(text_parts, near_count)
        near_parts = [near_parts[0]] + [
            move(part, by_near=-n) for n, part in enumerate(near_parts) if n
        ]
        return finish(images, texts, image_parts, near_parts)

    in_specs = (P(AXES, None), P(AXES, None), P(), P())
    out_specs = (P(AXES, None), P(AXES, None))
    return jax.shard_map(
        on_device, mesh=mesh, in_specs=in_specs, out_specs=out_specs, check_vma=False
    )
```

time: 60.4 us -> 38.9 us (0.64); the launches traced: 59.6 us -> 38.8 us
  waiting for transfers between devices: 32.2 us -> 11 us
  Pallas kernels: 3.97 us -> 4.88 us
  local copies, waits for them, and re-layouts: 1.8 us -> 0.98 us
    ppermute x20 -> x14, waiting for transfers between devices: 32.2 us -> 11 us  [move(): return lax.ppermute(value, AXES, perm)]
    pallas_call x2 -> x5, Pallas kernels: 3.97 us -> 4.88 us  [call(): pl.pallas_call(kernel, out_shape=out_shape, in_specs=[VMEM] * len(operand...]
    unnamed x4 -> x6, local copies, waits for them, and re-layouts: 1.8 us -> 0.91 us
    ppermute x20 -> x14, starting transfers between devices: 19.7 us -> 19.9 us  [move(): return lax.ppermute(value, AXES, perm)]
  transfers between devices with their start and end apart: 20 -> 14, of which waited for: 7 -> 5; matrix products, arithmetic and copies ran while one was open for 0% -> 0% of each run, Pallas kernels for 0% -> 5%
where the time goes in v3:
time: 38.9 us; the launch traced here: 38.8 us
  starting transfers between devices  19.9 us (51%)
  waiting for transfers between devices  11 us (28%)
  Pallas kernels  4.88 us (13%)
  between operations  2.02 us (5%)
  local copies, waits for them, and re-layouts  0.98 us (3%)
    ppermute x14, starting transfers between devices, move(): return lax.ppermute(value, AXES, perm)  19.9 us
    ppermute x14, waiting for transfers between devices, move(): return lax.ppermute(value, AXES, perm)  11 us
    pallas_call x5, Pallas kernels, call(): pl.pallas_call(kernel, out_shape=out_shape, in_specs=[VMEM] * len(operand...  4.88 us
    unnamed x6, local copies, waits for them, and re-layouts  0.91 us
  transfers between devices with their start and end apart: 14, of which 5 were waited for; matrix products, arithmetic and copies ran while one was open for 0% of the time, Pallas kernels for 5%

profile of v3, /device:TPU:0, one launch (start us, length us, event | category | flops | bytes accessed | tf_op | source)
XLA Modules:
  0.0 38.8 jit_solution(15902464891525071104)
XLA Ops:
  0.6 4.0 %collective-permute-start.2 = (bf16[128,512]{1,0:T(8,128)(2,1)}, bf16[128,512]{1,0:T(8,128)(2,1)S(1)}, u32[]{:S(2)}, u32[]{:S(2)}) collective-permute-start(bf16[128,512]{1,0:T(8,128)(2,1)} %text_ref.1), channel_id=1, source_target_pairs={{0,3},{1,2},{2,1},{3,0},{4,7},{5,6},{6,5},{7,4},{8,11},{9,10},{10,... | collective-permute-start | bytes 393224 | tf_op jit(solution)/shard_map/ppermute | solution.py:205
  4.6 0.5 %collective-permute-start.1 = (bf16[128,512]{1,0:T(8,128)(2,1)}, bf16[128,512]{1,0:T(8,128)(2,1)S(1)}, u32[]{:S(2)}, u32[]{:S(2)}) collective-permute-start(bf16[128,512]{1,0:T(8,128)(2,1)} %text_ref.1), channel_id=1, source_target_pairs={{0,2},{1,3},{2,0},{3,1},{4,6},{5,7},{6,4},{7,5},{8,10},{9,11},{10,... | collective-permute-start | bytes 393224 | tf_op jit(solution)/shard_map/ppermute | solution.py:205
  5.1 0.1 collective-permute-start
  5.2 4.0 %collective-permute-start.5 = (bf16[128,512]{1,0:T(8,128)(2,1)}, bf16[128,512]{1,0:T(8,128)(2,1)S(1)}, u32[]{:S(2)}, u32[]{:S(2)}) collective-permute-start(bf16[128,512]{1,0:T(8,128)(2,1)} %image_ref.1), channel_id=1, source_target_pairs={{0,12},{1,13},{2,14},{3,15},{4,8},{5,9},{6,10},{7,11},{8,4},{9,5},... | collective-permute-start | bytes 393224 | tf_op jit(solution)/shard_map/ppermute | solution.py:205
  9.2 1.1 %collective-permute-start.3 = (bf16[128,512]{1,0:T(8,128)(2,1)}, bf16[128,512]{1,0:T(8,128)(2,1)S(1)}, u32[]{:S(2)}, u32[]{:S(2)}) collective-permute-start(bf16[128,512]{1,0:T(8,128)(2,1)} %image_ref.1), channel_id=1, source_target_pairs={{0,4},{1,5},{2,6},{3,7},{4,0},{5,1},{6,2},{7,3},{8,12},{9,13},{10,... | collective-permute-start | bytes 393224 | tf_op jit(solution)/shard_map/ppermute | solution.py:205
  11.7 0.9 %copy-done = bf16[128,512]{1,0:T(8,128)(2,1)S(1)} copy-done((bf16[128,512]{1,0:T(8,128)(2,1)S(1)}, bf16[128,512]{1,0:T(8,128)(2,1)}, u32[]{:S(2)}) %copy-start) | copy-done | bytes 131096
  12.6 0.2 stack_units.1.text_ref
  12.8 0.1 collective-permute-start.6
  12.9 1.0 %collective-permute-done.5.refs_3_ = bf16[128,512]{1,0:T(8,128)(2,1)S(1)} collective-permute-done((bf16[128,512]{1,0:T(8,128)(2,1)}, bf16[128,512]{1,0:T(8,128)(2,1)S(1)}, u32[]{:S(2)}, u32[]{:S(2)}) %collective-permute-start.5) | collective-permute-done | bytes 131104 | tf_op jit(solution)/shard_map/ppermute | solution.py:205
  13.9 5.8 %collective-permute-done.4.refs_2_ = bf16[128,512]{1,0:T(8,128)(2,1)S(1)} collective-permute-done((bf16[128,512]{1,0:T(8,128)(2,1)}, bf16[128,512]{1,0:T(8,128)(2,1)S(1)}, u32[]{:S(2)}, u32[]{:S(2)}) %collective-permute-start.4) | collective-permute-done | bytes 131104 | tf_op jit(solution)/shard_map/ppermute | solution.py:205
  19.8 1.8 %own_pairs.1 = (f32[512,512]{1,0:T(8,128)S(1)}, bf16[512,512]{1,0:T(8,128)(2,1)S(1)}, f32[512,512]{1,0:T(8,128)S(1)}) custom-call(f32[2,128]{1,0:T(2,128)S(1)} %concatenate.6.params_ref, bf16[512,512]{1,0:T(8,128)(2,1)S(1)} %stack_units.1.text_ref, bf16[128,512]{1,0:T(8,128)(2,1)S(1)} %copy-done.2, bf16[128,512]{1,0:T(8,128)(2,1)S(1)} %collective-permute-done.3.refs_1_, ...), custom_call_target="tpu_custom_call" | custom-call | flops 8053063680 | bytes 3671040 | tf_op jit(solution)/shard_map/own_pairs/pallas_call | solution.py:25
  21.6 1.8 %other_pairs.1 = (bf16[512,512]{1,0:T(8,128)(2,1)S(1)}, f32[128,512]{1,0:T(8,128)S(1)}, bf16[128,512]{1,0:T(8,128)(2,1)S(1)}, bf16[128,512]{1,0:T(8,128)(2,1)S(1)}, bf16[128,512]{1,0:T(8,128)(2,1)S(1)}) custom-call(f32[2,128]{1,0:T(2,128)S(1)} %concatenate.6.params_ref, bf16[512,512]{1,0:T(8,128)(2,1)S(1)} %get-tuple-element.14.units_ref, ...), custom_call_target="tpu_custom_call" | custom-call | flops 805306368 | bytes 3277824 | tf_op jit(solution)/shard_map/other_pairs/pallas_call | solution.py:25
  23.3 0.1 collective-permute-start.10
  23.4 0.1 collective-permute-start.7
  23.5 3.0 %collective-permute-start.8 = (bf16[128,512]{1,0:T(8,128)(2,1)S(1)}, bf16[128,512]{1,0:T(8,128)(2,1)S(1)}, u32[]{:S(2)}, u32[]{:S(2)}) collective-permute-start(bf16[128,512]{1,0:T(8,128)(2,1)S(1)} %get-tuple-element.18), channel_id=1, source_target_pairs={{0,8},{1,9},{2,10},{3,11},{4,12},{5,13},{6,14},{7,15},{8,0},{9,1},... | collective-permute-start | bytes 393224 | tf_op jit(solution)/shard_map/ppermute | solution.py:205
  26.5 1.3 %collective-permute-start.9 = (bf16[128,512]{1,0:T(8,128)(2,1)S(1)}, bf16[128,512]{1,0:T(8,128)(2,1)S(1)}, u32[]{:S(2)}, u32[]{:S(2)}) collective-permute-start(bf16[128,512]{1,0:T(8,128)(2,1)S(1)} %get-tuple-element.19), channel_id=1, source_target_pairs={{0,12},{1,13},{2,14},{3,15},{4,8},{5,9},{6,10},{7,11},{8,4},{9,5},... | collective-permute-start | bytes 393224 | tf_op jit(solution)/shard_map/ppermute | solution.py:205
  27.9 0.1 add_stacks.1
  28.0 1.6 %collective-permute-start.11 = (bf16[128,512]{1,0:T(8,128)(2,1)S(1)}, bf16[128,512]{1,0:T(8,128)(2,1)S(1)}, u32[]{:S(2)}, u32[]{:S(2)}) collective-permute-start(bf16[128,512]{1,0:T(8,128)(2,1)S(1)} %get-tuple-element.23), channel_id=1, source_target_pairs={{0,1},{1,0},{2,3},{3,2},{4,5},{5,4},{6,7},{7,6},{8,9},{9,8},{10,11... | collective-permute-start | bytes 393224 | tf_op jit(solution)/shard_map/ppermute | solution.py:205
  29.5 1.5 %collective-permute-start.12 = (bf16[128,512]{1,0:T(8,128)(2,1)S(1)}, bf16[128,512]{1,0:T(8,128)(2,1)S(1)}, u32[]{:S(2)}, u32[]{:S(2)}) collective-permute-start(bf16[128,512]{1,0:T(8,128)(2,1)S(1)} %get-tuple-element.24), channel_id=1, source_target_pairs={{0,2},{1,3},{2,0},{3,1},{4,6},{5,7},{6,4},{7,5},{8,10},{9,11},{10,... | collective-permute-start | bytes 393224 | tf_op jit(solution)/shard_map/ppermute | solution.py:205
  31.1 0.7 %collective-permute-done.7.refs_1_ = bf16[128,512]{1,0:T(8,128)(2,1)S(1)} collective-permute-done((bf16[128,512]{1,0:T(8,128)(2,1)S(1)}, bf16[128,512]{1,0:T(8,128)(2,1)S(1)}, u32[]{:S(2)}, u32[]{:S(2)}) %collective-permute-start.7) | collective-permute-done | bytes 131104 | tf_op jit(solution)/shard_map/ppermute | solution.py:205
  31.8 2.4 %collective-permute-start.13 = (bf16[128,512]{1,0:T(8,128)(2,1)S(1)}, bf16[128,512]{1,0:T(8,128)(2,1)S(1)}, u32[]{:S(2)}, u32[]{:S(2)}) collective-permute-start(bf16[128,512]{1,0:T(8,128)(2,1)S(1)} %get-tuple-element.25), channel_id=1, source_target_pairs={{0,3},{1,2},{2,1},{3,0},{4,7},{5,6},{6,5},{7,4},{8,11},{9,10},{10,... | collective-permute-start | bytes 393224 | tf_op jit(solution)/shard_map/ppermute | solution.py:205
  34.2 2.2 %collective-permute-done.8.refs_2_ = bf16[128,512]{1,0:T(8,128)(2,1)S(1)} collective-permute-done((bf16[128,512]{1,0:T(8,128)(2,1)S(1)}, bf16[128,512]{1,0:T(8,128)(2,1)S(1)}, u32[]{:S(2)}, u32[]{:S(2)}) %collective-permute-start.8) | collective-permute-done | bytes 131104 | tf_op jit(solution)/shard_map/ppermute | solution.py:205
  36.5 1.3 %collective-permute-done.13.refs_7_ = bf16[128,512]{1,0:T(8,128)(2,1)S(1)} collective-permute-done((bf16[128,512]{1,0:T(8,128)(2,1)S(1)}, bf16[128,512]{1,0:T(8,128)(2,1)S(1)}, u32[]{:S(2)}, u32[]{:S(2)}) %collective-permute-start.13) | collective-permute-done | bytes 131104 | tf_op jit(solution)/shard_map/ppermute | solution.py:205
  37.7 1.0 %finish.1 = (f32[128,512]{1,0:T(8,128)}, f32[128,512]{1,0:T(8,128)}) custom-call(bf16[128,512]{1,0:T(8,128)(2,1)S(1)} %copy-done.2, bf16[128,512]{1,0:T(8,128)(2,1)S(1)} %copy-done.1, f32[128,512]{1,0:T(8,128)S(1)} %get-tuple-element.16.refs_0_, bf16[128,512]{1,0:T(8,128)(2,1)S(1)} %collective-permute-done.7.refs_1_, ...), custom_call_target="tpu_custom_call" | custom-call | flops 5242880 | bytes 2097152 | tf_op jit(solution)/shard_map/finish/pallas_call | solution.py:25
  (17 shorter events, 0.1 us)
Async XLA Ops:
  0.6 8.6 %collective-permute-start.2 = (bf16[128,512]{1,0:T(8,128)(2,1)}, bf16[128,512]{1,0:T(8,128)(2,1)S(1)}, u32[]{:S(2)}, u32[]{:S(2)}) collective-permute-start(bf16[128,512]{1,0:T(8,128)(2,1)} %text_ref.1), channel_id=1, source_target_pairs={{0,3},{1,2},{2,1},{3,0},{4,7},{5,6},{6,5},{7,4},{8,11},{9,10},{10,... | collective-permute-start | bytes 393224 | tf_op jit(solution)/shard_map/ppermute | solution.py:205
  4.6 7.1 %collective-permute-start.1 = (bf16[128,512]{1,0:T(8,128)(2,1)}, bf16[128,512]{1,0:T(8,128)(2,1)S(1)}, u32[]{:S(2)}, u32[]{:S(2)}) collective-permute-start(bf16[128,512]{1,0:T(8,128)(2,1)} %text_ref.1), channel_id=1, source_target_pairs={{0,2},{1,3},{2,0},{3,1},{4,6},{5,7},{6,4},{7,5},{8,10},{9,11},{10,... | collective-permute-start | bytes 393224 | tf_op jit(solution)/shard_map/ppermute | solution.py:205
  5.1 6.6 %collective-permute-start = (bf16[128,512]{1,0:T(8,128)(2,1)}, bf16[128,512]{1,0:T(8,128)(2,1)S(1)}, u32[]{:S(2)}, u32[]{:S(2)}) collective-permute-start(bf16[128,512]{1,0:T(8,128)(2,1)} %text_ref.1), channel_id=1, source_target_pairs={{0,1},{1,0},{2,3},{3,2},{4,5},{5,4},{6,7},{7,6},{8,9},{9,8},{10,11... | collective-permute-start | bytes 393224 | tf_op jit(solution)/shard_map/ppermute | solution.py:205
  5.2 8.6 %collective-permute-start.5 = (bf16[128,512]{1,0:T(8,128)(2,1)}, bf16[128,512]{1,0:T(8,128)(2,1)S(1)}, u32[]{:S(2)}, u32[]{:S(2)}) collective-permute-start(bf16[128,512]{1,0:T(8,128)(2,1)} %image_ref.1), channel_id=1, source_target_pairs={{0,12},{1,13},{2,14},{3,15},{4,8},{5,9},{6,10},{7,11},{8,4},{9,5},... | collective-permute-start | bytes 393224 | tf_op jit(solution)/shard_map/ppermute | solution.py:205
  9.2 10.4 %collective-permute-start.4 = (bf16[128,512]{1,0:T(8,128)(2,1)}, bf16[128,512]{1,0:T(8,128)(2,1)S(1)}, u32[]{:S(2)}, u32[]{:S(2)}) collective-permute-start(bf16[128,512]{1,0:T(8,128)(2,1)} %image_ref.1), channel_id=1, source_target_pairs={{0,8},{1,9},{2,10},{3,11},{4,12},{5,13},{6,14},{7,15},{8,0},{9,1},... | collective-permute-start | bytes 393224 | tf_op jit(solution)/shard_map/ppermute | solution.py:205
  9.2 10.4 %collective-permute-start.3 = (bf16[128,512]{1,0:T(8,128)(2,1)}, bf16[128,512]{1,0:T(8,128)(2,1)S(1)}, u32[]{:S(2)}, u32[]{:S(2)}) collective-permute-start(bf16[128,512]{1,0:T(8,128)(2,1)} %image_ref.1), channel_id=1, source_target_pairs={{0,4},{1,5},{2,6},{3,7},{4,0},{5,1},{6,2},{7,3},{8,12},{9,13},{10,... | collective-permute-start | bytes 393224 | tf_op jit(solution)/shard_map/ppermute | solution.py:205
  11.7 0.9 %copy-start = (bf16[128,512]{1,0:T(8,128)(2,1)S(1)}, bf16[128,512]{1,0:T(8,128)(2,1)}, u32[]{:S(2)}) copy-start(bf16[128,512]{1,0:T(8,128)(2,1)} %text_ref.1) | copy-start | bytes 393220
  12.6 7.1 %copy-start.2 = (bf16[128,512]{1,0:T(8,128)(2,1)S(1)}, bf16[128,512]{1,0:T(8,128)(2,1)}, u32[]{:S(2)}) copy-start(bf16[128,512]{1,0:T(8,128)(2,1)} %image_ref.1) | copy-start | bytes 393220
  12.8 8.7 %collective-permute-start.6 = (bf16[512,512]{1,0:T(8,128)(2,1)S(1)}, bf16[512,512]{1,0:T(8,128)(2,1)S(1)}, u32[]{:S(2)}, u32[]{:S(2)}) collective-permute-start(bf16[512,512]{1,0:T(8,128)(2,1)S(1)} %stack_units.1.text_ref), channel_id=1, source_target_pairs={{0,16},{1,17},{2,18},{3,19},{4,20},{5,21},{6,22},{7,23},{8,24},{9,... | collective-permute-start | bytes 1572872 | tf_op jit(solution)/shard_map/ppermute | solution.py:205
  23.3 4.5 %collective-permute-start.10 = (bf16[512,512]{1,0:T(8,128)(2,1)S(1)}, bf16[512,512]{1,0:T(8,128)(2,1)S(1)}, u32[]{:S(2)}, u32[]{:S(2)}) collective-permute-start(bf16[512,512]{1,0:T(8,128)(2,1)S(1)} %get-tuple-element.21), channel_id=1, source_target_pairs={{0,16},{1,17},{2,18},{3,19},{4,20},{5,21},{6,22},{7,23},{8,24},{9,... | collective-permute-start | bytes 1572872 | tf_op jit(solution)/shard_map/ppermute | solution.py:205
  23.4 8.4 %collective-permute-start.7 = (bf16[128,512]{1,0:T(8,128)(2,1)S(1)}, bf16[128,512]{1,0:T(8,128)(2,1)S(1)}, u32[]{:S(2)}, u32[]{:S(2)}) collective-permute-start(bf16[128,512]{1,0:T(8,128)(2,1)S(1)} %get-tuple-element.17), channel_id=1, source_target_pairs={{0,4},{1,5},{2,6},{3,7},{4,0},{5,1},{6,2},{7,3},{8,12},{9,13},{10,... | collective-permute-start | bytes 393224 | tf_op jit(solution)/shard_map/ppermute | solution.py:205
  23.5 13.0 %collective-permute-start.8 = (bf16[128,512]{1,0:T(8,128)(2,1)S(1)}, bf16[128,512]{1,0:T(8,128)(2,1)S(1)}, u32[]{:S(2)}, u32[]{:S(2)}) collective-permute-start(bf16[128,512]{1,0:T(8,128)(2,1)S(1)} %get-tuple-element.18), channel_id=1, source_target_pairs={{0,8},{1,9},{2,10},{3,11},{4,12},{5,13},{6,14},{7,15},{8,0},{9,1},... | collective-permute-start | bytes 393224 | tf_op jit(solution)/shard_map/ppermute | solution.py:205
  26.5 9.9 %collective-permute-start.9 = (bf16[128,512]{1,0:T(8,128)(2,1)S(1)}, bf16[128,512]{1,0:T(8,128)(2,1)S(1)}, u32[]{:S(2)}, u32[]{:S(2)}) collective-permute-start(bf16[128,512]{1,0:T(8,128)(2,1)S(1)} %get-tuple-element.19), channel_id=1, source_target_pairs={{0,12},{1,13},{2,14},{3,15},{4,8},{5,9},{6,10},{7,11},{8,4},{9,5},... | collective-permute-start | bytes 393224 | tf_op jit(solution)/shard_map/ppermute | solution.py:205
  27.9 9.9 %copy-start.1 = (bf16[128,512]{1,0:T(8,128)(2,1)S(1)}, bf16[128,512]{1,0:T(8,128)(2,1)}, u32[]{:S(2)}) copy-start(bf16[128,512]{1,0:T(8,128)(2,1)} %text_ref.1) | copy-start | bytes 393220
  28.0 8.5 %collective-permute-start.11 = (bf16[128,512]{1,0:T(8,128)(2,1)S(1)}, bf16[128,512]{1,0:T(8,128)(2,1)S(1)}, u32[]{:S(2)}, u32[]{:S(2)}) collective-permute-start(bf16[128,512]{1,0:T(8,128)(2,1)S(1)} %get-tuple-element.23), channel_id=1, source_target_pairs={{0,1},{1,0},{2,3},{3,2},{4,5},{5,4},{6,7},{7,6},{8,9},{9,8},{10,11... | collective-permute-start | bytes 393224 | tf_op jit(solution)/shard_map/ppermute | solution.py:205
  29.5 6.9 %collective-permute-start.12 = (bf16[128,512]{1,0:T(8,128)(2,1)S(1)}, bf16[128,512]{1,0:T(8,128)(2,1)S(1)}, u32[]{:S(2)}, u32[]{:S(2)}) collective-permute-start(bf16[128,512]{1,0:T(8,128)(2,1)S(1)} %get-tuple-element.24), channel_id=1, source_target_pairs={{0,2},{1,3},{2,0},{3,1},{4,6},{5,7},{6,4},{7,5},{8,10},{9,11},{10,... | collective-permute-start | bytes 393224 | tf_op jit(solution)/shard_map/ppermute | solution.py:205
  31.8 6.0 %collective-permute-start.13 = (bf16[128,512]{1,0:T(8,128)(2,1)S(1)}, bf16[128,512]{1,0:T(8,128)(2,1)S(1)}, u32[]{:S(2)}, u32[]{:S(2)}) collective-permute-start(bf16[128,512]{1,0:T(8,128)(2,1)S(1)} %get-tuple-element.25), channel_id=1, source_target_pairs={{0,3},{1,2},{2,1},{3,0},{4,7},{5,6},{6,5},{7,4},{8,11},{9,10},{10,... | collective-permute-start | bytes 393224 | tf_op jit(solution)/shard_map/ppermute | solution.py:205

commit v4 on v3

--- a/solution.py
+++ b/solution.py
@@ -37,10 +37,20 @@
     return tuple(outs)
 
 
+def own_units_kernel(ref, out):
+    out[...] = unit_rows(ref[...])[0].astype(out.dtype)
+
+
+def own_units(raw):
+    out = jax.ShapeDtypeStruct(raw.shape, jnp.bfloat16)
+    return call(own_units_kernel, [out], [raw], flops=4 * raw.size, name="own_units")[0]
+
+
 def stack_units_kernel(*refs):
     out = refs[-1]
     rows = refs[0].shape[0]
-    for at, ref in enumerate(refs[:-1]):
+    out[:rows, :] = refs[0][...]
+    for at, ref in enumerate(refs[1:-1], 1):
         out[at * rows:(at + 1) * rows, :] = unit_rows(ref[...])[0].astype(out.dtype)
 
 
@@ -191,37 +201,53 @@
 def solution(mesh):
     grp_count, dev_count = mesh.shape["grp"], mesh.shape["dev"]
     far_count, near_count = plan(grp_count, dev_count)
-
-    def move(value, by_grp=0, by_far=0, by_near=0):
+    low_count = 2 if far_count % 2 == 0 else 1
+    high_count = far_count // low_count
+
+    def move(value, grp=0, high=0, low=0, near=0):
         perm = []
         for g in range(grp_count):
-            for f in range(far_count):
-                for n in range(near_count):
-                    g2 = step_to(g, by_grp, grp_count)
-                    f2 = step_to(f, by_far, far_count)
-                    n2 = step_to(n, by_near, near_count)
-                    source = (g * far_count + f) * near_count + n
-                    perm.append((source, (g2 * far_count + f2) * near_count + n2))
+            for h in range(high_count):
+                for w in range(low_count):
+                    for n in range(near_count):
+                        source = ((g * high_count + h) * low_count + w) * near_count + n
+                        g2 = step_to(g, grp, grp_count)
+                        h2 = step_to(h, high, high_count)
+                        w2 = step_to(w, low, low_count)
+                        n2 = step_to(n, near, near_count)
+                        target = ((g2 * high_count + h2) * low_count + w2) * near_count + n2
+                        perm.append((source, target))
         return lax.ppermute(value, AXES, perm)
+
+    far_steps = [(h, w) for h in range(high_count) for w in range(low_count)]
+
+    def gather_far(rows):
+        held = {(0, 0): rows}
+        for h in range(1, high_count):
+            held[h, 0] = move(rows, high=h)
+        for h in range(high_count):
+            for w in range(1, low_count):
+                held[h, w] = move(held[h, 0], low=w)
+        return [held[step] for step in far_steps]
 
     def on_device(images, texts, logit_scale, logit_bias):
         params = jnp.concatenate(
             [jnp.broadcast_to(logit_scale, (1, 128)), jnp.broadcast_to(logit_bias, (1, 128))]
         )
-        image_rows = [images] + [move(images, by_far=f) for f in range(1, far_count)]
-        near_rows = [texts] + [move(texts, by_near=n) for n in range(1, near_count)]
+        image_rows = gather_far(images)
+        near_rows = [own_units(texts)] + [move(texts, near=n) for n in range(1, near_count)]
         own_stack = stack_units(near_rows)
-        stacks = [own_stack] + [move(own_stack, by_grp=g) for g in range(1, grp_count)]
+        stacks = [own_stack] + [move(own_stack, grp=g) for g in range(1, grp_count)]
         image_parts, text_parts = pair_terms(params, image_rows, stacks)
         image_parts = [image_parts[0]] + [
-            move(part, by_far=-f) for f, part in enumerate(image_parts) if f
+            move(part, high=-h, low=-w) for (h, w), part in zip(far_steps, image_parts) if h or w
         ]
         text_parts = [text_parts[0]] + [
-            move(part, by_grp=-g) for g, part in enumerate(text_parts) if g
+            move(part, grp=-g) for g, part in enumerate(text_parts) if g
         ]
         near_parts = add_stacks(text_parts, near_count)
         near_parts = [near_parts[0]] + [
-            move(part, by_near=-n) for n, part in enumerate(near_parts) if n
+            move(part, near=-n) for n, part in enumerate(near_parts) if n
         ]
         return finish(images, texts, image_parts, near_parts)
 

time: 38.9 us -> 36 us (0.925)
  waiting for transfers between devices: 11 us -> 7.75 us
    ppermute x14, waiting for transfers between devices: 11 us -> 7.75 us  [move(): return lax.ppermute(value, AXES, perm)]
    pallas_call x5 -> x6, Pallas kernels: 4.88 us -> 4.97 us  [call(): pl.pallas_call(kernel, out_shape=out_shape, in_specs=[VMEM] * len(operand...]
  transfers between devices with their start and end apart: 14 -> 14, of which waited for: 5 -> 6; matrix products, arithmetic and copies ran while one was open for 0% -> 0% of each run, Pallas kernels for 5% -> 6%
where the time goes in v4:
time: 36 us; the launch traced here: 35.9 us
  starting transfers between devices  20.1 us (56%)
  waiting for transfers between devices  7.75 us (22%)
  Pallas kernels  4.97 us (14%)
  between operations  2.02 us (6%)
  local copies, waits for them, and re-layouts  0.99 us (3%)
    ppermute x14, starting transfers between devices, move(): return lax.ppermute(value, AXES, perm)  20.1 us
    ppermute x14, waiting for transfers between devices, move(): return lax.ppermute(value, AXES, perm)  7.75 us
    pallas_call x6, Pallas kernels, call(): pl.pallas_call(kernel, out_shape=out_shape, in_specs=[VMEM] * len(operand...  4.97 us
    unnamed x6, local copies, waits for them, and re-layouts  0.91 us
  transfers between devices with their start and end apart: 14, of which 6 were waited for; matrix products, arithmetic and copies ran while one was open for 0% of the time, Pallas kernels for 6%

profile of v4, /device:TPU:0, one launch (start us, length us, event | category | flops | bytes accessed | tf_op | source)
XLA Modules:
  0.0 35.9 jit_solution(9983320677228173385)
XLA Ops:
  0.6 4.1 %collective-permute-start.4 = (bf16[128,512]{1,0:T(8,128)(2,1)}, bf16[128,512]{1,0:T(8,128)(2,1)S(1)}, u32[]{:S(2)}, u32[]{:S(2)}) collective-permute-start(bf16[128,512]{1,0:T(8,128)(2,1)} %image_ref.1), channel_id=1, source_target_pairs={{0,8},{1,9},{2,10},{3,11},{4,12},{5,13},{6,14},{7,15},{8,0},{9,1},... | collective-permute-start | bytes 393224 | tf_op jit(solution)/shard_map/ppermute | solution.py:220
  4.7 1.5 %collective-permute-start.1 = (bf16[128,512]{1,0:T(8,128)(2,1)}, bf16[128,512]{1,0:T(8,128)(2,1)S(1)}, u32[]{:S(2)}, u32[]{:S(2)}) collective-permute-start(bf16[128,512]{1,0:T(8,128)(2,1)} %text_ref.1), channel_id=1, source_target_pairs={{0,2},{1,3},{2,0},{3,1},{4,6},{5,7},{6,4},{7,5},{8,10},{9,11},{10,... | collective-permute-start | bytes 393224 | tf_op jit(solution)/shard_map/ppermute | solution.py:220
  6.3 1.5 %collective-permute-start = (bf16[128,512]{1,0:T(8,128)(2,1)}, bf16[128,512]{1,0:T(8,128)(2,1)S(1)}, u32[]{:S(2)}, u32[]{:S(2)}) collective-permute-start(bf16[128,512]{1,0:T(8,128)(2,1)} %text_ref.1), channel_id=1, source_target_pairs={{0,1},{1,0},{2,3},{3,2},{4,5},{5,4},{6,7},{7,6},{8,9},{9,8},{10,11... | collective-permute-start | bytes 393224 | tf_op jit(solution)/shard_map/ppermute | solution.py:220
  7.7 0.5 %collective-permute-start.2 = (bf16[128,512]{1,0:T(8,128)(2,1)}, bf16[128,512]{1,0:T(8,128)(2,1)S(1)}, u32[]{:S(2)}, u32[]{:S(2)}) collective-permute-start(bf16[128,512]{1,0:T(8,128)(2,1)} %text_ref.1), channel_id=1, source_target_pairs={{0,3},{1,2},{2,1},{3,0},{4,7},{5,6},{6,5},{7,4},{8,11},{9,10},{10,... | collective-permute-start | bytes 393224 | tf_op jit(solution)/shard_map/ppermute | solution.py:220
  8.2 1.6 %collective-permute-start.3 = (bf16[128,512]{1,0:T(8,128)(2,1)}, bf16[128,512]{1,0:T(8,128)(2,1)S(1)}, u32[]{:S(2)}, u32[]{:S(2)}) collective-permute-start(bf16[128,512]{1,0:T(8,128)(2,1)} %image_ref.1), channel_id=1, source_target_pairs={{0,4},{1,5},{2,6},{3,7},{4,0},{5,1},{6,2},{7,3},{8,12},{9,13},{10,... | collective-permute-start | bytes 393224 | tf_op jit(solution)/shard_map/ppermute | solution.py:220
  9.8 1.6 %collective-permute-done.4.refs_2_ = bf16[128,512]{1,0:T(8,128)(2,1)S(1)} collective-permute-done((bf16[128,512]{1,0:T(8,128)(2,1)}, bf16[128,512]{1,0:T(8,128)(2,1)S(1)}, u32[]{:S(2)}, u32[]{:S(2)}) %collective-permute-start.4) | collective-permute-done | bytes 131104 | tf_op jit(solution)/shard_map/ppermute | solution.py:220
  11.4 0.8 %collective-permute-start.5 = (bf16[128,512]{1,0:T(8,128)(2,1)S(1)}, bf16[128,512]{1,0:T(8,128)(2,1)S(1)}, u32[]{:S(2)}, u32[]{:S(2)}) collective-permute-start(bf16[128,512]{1,0:T(8,128)(2,1)S(1)} %collective-permute-done.4.refs_2_), channel_id=1, source_target_pairs={{0,4},{1,5},{2,6},{3,7},{4,0},{5,1},{6,2},{7,3},{8,12},{9,13},{10,... | collective-permute-start | bytes 393224 | tf_op jit(solution)/shard_map/ppermute | solution.py:220
  12.1 0.9 %copy-done = bf16[128,512]{1,0:T(8,128)(2,1)S(1)} copy-done((bf16[128,512]{1,0:T(8,128)(2,1)S(1)}, bf16[128,512]{1,0:T(8,128)(2,1)}, u32[]{:S(2)}) %copy-start) | copy-done | bytes 131096
  14.5 0.2 stack_units.1.text_ref
  14.7 0.1 collective-permute-done.3.refs_1_
  14.9 2.0 %collective-permute-done.5.refs_3_ = bf16[128,512]{1,0:T(8,128)(2,1)S(1)} collective-permute-done((bf16[128,512]{1,0:T(8,128)(2,1)S(1)}, bf16[128,512]{1,0:T(8,128)(2,1)S(1)}, u32[]{:S(2)}, u32[]{:S(2)}) %collective-permute-start.5) | collective-permute-done | bytes 131104 | tf_op jit(solution)/shard_map/ppermute | solution.py:220
  16.9 1.8 %own_pairs.1 = (f32[512,512]{1,0:T(8,128)S(1)}, bf16[512,512]{1,0:T(8,128)(2,1)S(1)}, f32[512,512]{1,0:T(8,128)S(1)}) custom-call(f32[2,128]{1,0:T(2,128)S(1)} %concatenate.6.params_ref, bf16[512,512]{1,0:T(8,128)(2,1)S(1)} %stack_units.1.text_ref, bf16[128,512]{1,0:T(8,128)(2,1)S(1)} %copy-done.2, bf16[128,512]{1,0:T(8,128)(2,1)S(1)} %collective-permute-done.3.refs_1_, ...), custom_call_target="tpu_custom_call" | custom-call | flops 8053063680 | bytes 3671040 | tf_op jit(solution)/shard_map/own_pairs/pallas_call | solution.py:25
  18.7 1.8 %other_pairs.1 = (bf16[512,512]{1,0:T(8,128)(2,1)S(1)}, f32[128,512]{1,0:T(8,128)S(1)}, bf16[128,512]{1,0:T(8,128)(2,1)S(1)}, bf16[128,512]{1,0:T(8,128)(2,1)S(1)}, bf16[128,512]{1,0:T(8,128)(2,1)S(1)}) custom-call(f32[2,128]{1,0:T(2,128)S(1)} %concatenate.6.params_ref, bf16[512,512]{1,0:T(8,128)(2,1)S(1)} %get-tuple-element.14.units_ref, ...), custom_call_target="tpu_custom_call" | custom-call | flops 805306368 | bytes 3277824 | tf_op jit(solution)/shard_map/other_pairs/pallas_call | solution.py:25
  20.6 1.0 %collective-permute-start.7 = (bf16[128,512]{1,0:T(8,128)(2,1)S(1)}, bf16[128,512]{1,0:T(8,128)(2,1)S(1)}, u32[]{:S(2)}, u32[]{:S(2)}) collective-permute-start(bf16[128,512]{1,0:T(8,128)(2,1)S(1)} %get-tuple-element.17), channel_id=1, source_target_pairs={{0,4},{1,5},{2,6},{3,7},{4,0},{5,1},{6,2},{7,3},{8,12},{9,13},{10,... | collective-permute-start | bytes 393224 | tf_op jit(solution)/shard_map/ppermute | solution.py:220
  21.6 3.0 %collective-permute-start.8 = (bf16[128,512]{1,0:T(8,128)(2,1)S(1)}, bf16[128,512]{1,0:T(8,128)(2,1)S(1)}, u32[]{:S(2)}, u32[]{:S(2)}) collective-permute-start(bf16[128,512]{1,0:T(8,128)(2,1)S(1)} %get-tuple-element.18), channel_id=1, source_target_pairs={{0,8},{1,9},{2,10},{3,11},{4,12},{5,13},{6,14},{7,15},{8,0},{9,1},... | collective-permute-start | bytes 393224 | tf_op jit(solution)/shard_map/ppermute | solution.py:220
  24.6 0.4 %collective-permute-start.9 = (bf16[128,512]{1,0:T(8,128)(2,1)S(1)}, bf16[128,512]{1,0:T(8,128)(2,1)S(1)}, u32[]{:S(2)}, u32[]{:S(2)}) collective-permute-start(bf16[128,512]{1,0:T(8,128)(2,1)S(1)} %get-tuple-element.19), channel_id=1, source_target_pairs={{0,12},{1,13},{2,14},{3,15},{4,8},{5,9},{6,10},{7,11},{8,4},{9,5},... | collective-permute-start | bytes 393224 | tf_op jit(solution)/shard_map/ppermute | solution.py:220
  25.1 0.1 add_stacks.1
  25.2 1.6 %collective-permute-start.11 = (bf16[128,512]{1,0:T(8,128)(2,1)S(1)}, bf16[128,512]{1,0:T(8,128)(2,1)S(1)}, u32[]{:S(2)}, u32[]{:S(2)}) collective-permute-start(bf16[128,512]{1,0:T(8,128)(2,1)S(1)} %get-tuple-element.23), channel_id=1, source_target_pairs={{0,1},{1,0},{2,3},{3,2},{4,5},{5,4},{6,7},{7,6},{8,9},{9,8},{10,11... | collective-permute-start | bytes 393224 | tf_op jit(solution)/shard_map/ppermute | solution.py:220
  26.8 1.5 %collective-permute-start.12 = (bf16[128,512]{1,0:T(8,128)(2,1)S(1)}, bf16[128,512]{1,0:T(8,128)(2,1)S(1)}, u32[]{:S(2)}, u32[]{:S(2)}) collective-permute-start(bf16[128,512]{1,0:T(8,128)(2,1)S(1)} %get-tuple-element.24), channel_id=1, source_target_pairs={{0,2},{1,3},{2,0},{3,1},{4,6},{5,7},{6,4},{7,5},{8,10},{9,11},{10,... | collective-permute-start | bytes 393224 | tf_op jit(solution)/shard_map/ppermute | solution.py:220
  28.3 0.7 %collective-permute-done.7.refs_1_ = bf16[128,512]{1,0:T(8,128)(2,1)S(1)} collective-permute-done((bf16[128,512]{1,0:T(8,128)(2,1)S(1)}, bf16[128,512]{1,0:T(8,128)(2,1)S(1)}, u32[]{:S(2)}, u32[]{:S(2)}) %collective-permute-start.7) | collective-permute-done | bytes 131104 | tf_op jit(solution)/shard_map/ppermute | solution.py:220
  29.0 2.5 %collective-permute-start.13 = (bf16[128,512]{1,0:T(8,128)(2,1)S(1)}, bf16[128,512]{1,0:T(8,128)(2,1)S(1)}, u32[]{:S(2)}, u32[]{:S(2)}) collective-permute-start(bf16[128,512]{1,0:T(8,128)(2,1)S(1)} %get-tuple-element.25), channel_id=1, source_target_pairs={{0,3},{1,2},{2,1},{3,0},{4,7},{5,6},{6,5},{7,4},{8,11},{9,10},{10,... | collective-permute-start | bytes 393224 | tf_op jit(solution)/shard_map/ppermute | solution.py:220
  31.5 3.1 %collective-permute-done.8.refs_2_ = bf16[128,512]{1,0:T(8,128)(2,1)S(1)} collective-permute-done((bf16[128,512]{1,0:T(8,128)(2,1)S(1)}, bf16[128,512]{1,0:T(8,128)(2,1)S(1)}, u32[]{:S(2)}, u32[]{:S(2)}) %collective-permute-start.8) | collective-permute-done | bytes 131104 | tf_op jit(solution)/shard_map/ppermute | solution.py:220
  34.6 0.3 collective-permute-done.13.refs_7_
  34.8 1.0 %finish.1 = (f32[128,512]{1,0:T(8,128)}, f32[128,512]{1,0:T(8,128)}) custom-call(bf16[128,512]{1,0:T(8,128)(2,1)S(1)} %copy-done.2, bf16[128,512]{1,0:T(8,128)(2,1)S(1)} %copy-done.1, f32[128,512]{1,0:T(8,128)S(1)} %get-tuple-element.16.refs_0_, bf16[128,512]{1,0:T(8,128)(2,1)S(1)} %collective-permute-done.7.refs_1_, ...), custom_call_target="tpu_custom_call" | custom-call | flops 5242880 | bytes 2097152 | tf_op jit(solution)/shard_map/finish/pallas_call | solution.py:25
  (18 shorter events, 0.4 us)
Async XLA Ops:
  0.6 10.7 %collective-permute-start.4 = (bf16[128,512]{1,0:T(8,128)(2,1)}, bf16[128,512]{1,0:T(8,128)(2,1)S(1)}, u32[]{:S(2)}, u32[]{:S(2)}) collective-permute-start(bf16[128,512]{1,0:T(8,128)(2,1)} %image_ref.1), channel_id=1, source_target_pairs={{0,8},{1,9},{2,10},{3,11},{4,12},{5,13},{6,14},{7,15},{8,0},{9,1},... | collective-permute-start | bytes 393224 | tf_op jit(solution)/shard_map/ppermute | solution.py:220
  4.7 9.7 %collective-permute-start.1 = (bf16[128,512]{1,0:T(8,128)(2,1)}, bf16[128,512]{1,0:T(8,128)(2,1)S(1)}, u32[]{:S(2)}, u32[]{:S(2)}) collective-permute-start(bf16[128,512]{1,0:T(8,128)(2,1)} %text_ref.1), channel_id=1, source_target_pairs={{0,2},{1,3},{2,0},{3,1},{4,6},{5,7},{6,4},{7,5},{8,10},{9,11},{10,... | collective-permute-start | bytes 393224 | tf_op jit(solution)/shard_map/ppermute | solution.py:220
  6.3 8.2 %collective-permute-start = (bf16[128,512]{1,0:T(8,128)(2,1)}, bf16[128,512]{1,0:T(8,128)(2,1)S(1)}, u32[]{:S(2)}, u32[]{:S(2)}) collective-permute-start(bf16[128,512]{1,0:T(8,128)(2,1)} %text_ref.1), channel_id=1, source_target_pairs={{0,1},{1,0},{2,3},{3,2},{4,5},{5,4},{6,7},{7,6},{8,9},{9,8},{10,11... | collective-permute-start | bytes 393224 | tf_op jit(solution)/shard_map/ppermute | solution.py:220
  7.7 6.7 %collective-permute-start.2 = (bf16[128,512]{1,0:T(8,128)(2,1)}, bf16[128,512]{1,0:T(8,128)(2,1)S(1)}, u32[]{:S(2)}, u32[]{:S(2)}) collective-permute-start(bf16[128,512]{1,0:T(8,128)(2,1)} %text_ref.1), channel_id=1, source_target_pairs={{0,3},{1,2},{2,1},{3,0},{4,7},{5,6},{6,5},{7,4},{8,11},{9,10},{10,... | collective-permute-start | bytes 393224 | tf_op jit(solution)/shard_map/ppermute | solution.py:220
  8.2 6.6 %collective-permute-start.3 = (bf16[128,512]{1,0:T(8,128)(2,1)}, bf16[128,512]{1,0:T(8,128)(2,1)S(1)}, u32[]{:S(2)}, u32[]{:S(2)}) collective-permute-start(bf16[128,512]{1,0:T(8,128)(2,1)} %image_ref.1), channel_id=1, source_target_pairs={{0,4},{1,5},{2,6},{3,7},{4,0},{5,1},{6,2},{7,3},{8,12},{9,13},{10,... | collective-permute-start | bytes 393224 | tf_op jit(solution)/shard_map/ppermute | solution.py:220
  11.4 5.5 %collective-permute-start.5 = (bf16[128,512]{1,0:T(8,128)(2,1)S(1)}, bf16[128,512]{1,0:T(8,128)(2,1)S(1)}, u32[]{:S(2)}, u32[]{:S(2)}) collective-permute-start(bf16[128,512]{1,0:T(8,128)(2,1)S(1)} %collective-permute-done.4.refs_2_), channel_id=1, source_target_pairs={{0,4},{1,5},{2,6},{3,7},{4,0},{5,1},{6,2},{7,3},{8,12},{9,13},{10,... | collective-permute-start | bytes 393224 | tf_op jit(solution)/shard_map/ppermute | solution.py:220
  12.1 0.9 %copy-start = (bf16[128,512]{1,0:T(8,128)(2,1)S(1)}, bf16[128,512]{1,0:T(8,128)(2,1)}, u32[]{:S(2)}) copy-start(bf16[128,512]{1,0:T(8,128)(2,1)} %text_ref.1) | copy-start | bytes 393220
  14.4 2.5 %copy-start.2 = (bf16[128,512]{1,0:T(8,128)(2,1)S(1)}, bf16[128,512]{1,0:T(8,128)(2,1)}, u32[]{:S(2)}) copy-start(bf16[128,512]{1,0:T(8,128)(2,1)} %image_ref.1) | copy-start | bytes 393220
  14.7 4.1 %collective-permute-start.6 = (bf16[512,512]{1,0:T(8,128)(2,1)S(1)}, bf16[512,512]{1,0:T(8,128)(2,1)S(1)}, u32[]{:S(2)}, u32[]{:S(2)}) collective-permute-start(bf16[512,512]{1,0:T(8,128)(2,1)S(1)} %stack_units.1.text_ref), channel_id=1, source_target_pairs={{0,16},{1,17},{2,18},{3,19},{4,20},{5,21},{6,22},{7,23},{8,24},{9,... | collective-permute-start | bytes 1572872 | tf_op jit(solution)/shard_map/ppermute | solution.py:220
  20.5 4.5 %collective-permute-start.10 = (bf16[512,512]{1,0:T(8,128)(2,1)S(1)}, bf16[512,512]{1,0:T(8,128)(2,1)S(1)}, u32[]{:S(2)}, u32[]{:S(2)}) collective-permute-start(bf16[512,512]{1,0:T(8,128)(2,1)S(1)} %get-tuple-element.21), channel_id=1, source_target_pairs={{0,16},{1,17},{2,18},{3,19},{4,20},{5,21},{6,22},{7,23},{8,24},{9,... | collective-permute-start | bytes 1572872 | tf_op jit(solution)/shard_map/ppermute | solution.py:220
  20.6 8.4 %collective-permute-start.7 = (bf16[128,512]{1,0:T(8,128)(2,1)S(1)}, bf16[128,512]{1,0:T(8,128)(2,1)S(1)}, u32[]{:S(2)}, u32[]{:S(2)}) collective-permute-start(bf16[128,512]{1,0:T(8,128)(2,1)S(1)} %get-tuple-element.17), channel_id=1, source_target_pairs={{0,4},{1,5},{2,6},{3,7},{4,0},{5,1},{6,2},{7,3},{8,12},{9,13},{10,... | collective-permute-start | bytes 393224 | tf_op jit(solution)/shard_map/ppermute | solution.py:220
  21.6 13.0 %collective-permute-start.8 = (bf16[128,512]{1,0:T(8,128)(2,1)S(1)}, bf16[128,512]{1,0:T(8,128)(2,1)S(1)}, u32[]{:S(2)}, u32[]{:S(2)}) collective-permute-start(bf16[128,512]{1,0:T(8,128)(2,1)S(1)} %get-tuple-element.18), channel_id=1, source_target_pairs={{0,8},{1,9},{2,10},{3,11},{4,12},{5,13},{6,14},{7,15},{8,0},{9,1},... | collective-permute-start | bytes 393224 | tf_op jit(solution)/shard_map/ppermute | solution.py:220
  24.6 9.9 %collective-permute-start.9 = (bf16[128,512]{1,0:T(8,128)(2,1)S(1)}, bf16[128,512]{1,0:T(8,128)(2,1)S(1)}, u32[]{:S(2)}, u32[]{:S(2)}) collective-permute-start(bf16[128,512]{1,0:T(8,128)(2,1)S(1)} %get-tuple-element.19), channel_id=1, source_target_pairs={{0,12},{1,13},{2,14},{3,15},{4,8},{5,9},{6,10},{7,11},{8,4},{9,5},... | collective-permute-start | bytes 393224 | tf_op jit(solution)/shard_map/ppermute | solution.py:220
  25.1 9.8 %copy-start.1 = (bf16[128,512]{1,0:T(8,128)(2,1)S(1)}, bf16[128,512]{1,0:T(8,128)(2,1)}, u32[]{:S(2)}) copy-start(bf16[128,512]{1,0:T(8,128)(2,1)} %text_ref.1) | copy-start | bytes 393220
  25.2 9.4 %collective-permute-start.11 = (bf16[128,512]{1,0:T(8,128)(2,1)S(1)}, bf16[128,512]{1,0:T(8,128)(2,1)S(1)}, u32[]{:S(2)}, u32[]{:S(2)}) collective-permute-start(bf16[128,512]{1,0:T(8,128)(2,1)S(1)} %get-tuple-element.23), channel_id=1, source_target_pairs={{0,1},{1,0},{2,3},{3,2},{4,5},{5,4},{6,7},{7,6},{8,9},{9,8},{10,11... | collective-permute-start | bytes 393224 | tf_op jit(solution)/shard_map/ppermute | solution.py:220
  26.8 7.8 %collective-permute-start.12 = (bf16[128,512]{1,0:T(8,128)(2,1)S(1)}, bf16[128,512]{1,0:T(8,128)(2,1)S(1)}, u32[]{:S(2)}, u32[]{:S(2)}) collective-permute-start(bf16[128,512]{1,0:T(8,128)(2,1)S(1)} %get-tuple-element.24), channel_id=1, source_target_pairs={{0,2},{1,3},{2,0},{3,1},{4,6},{5,7},{6,4},{7,5},{8,10},{9,11},{10,... | collective-permute-start | bytes 393224 | tf_op jit(solution)/shard_map/ppermute | solution.py:220
  29.0 5.9 %collective-permute-start.13 = (bf16[128,512]{1,0:T(8,128)(2,1)S(1)}, bf16[128,512]{1,0:T(8,128)(2,1)S(1)}, u32[]{:S(2)}, u32[]{:S(2)}) collective-permute-start(bf16[128,512]{1,0:T(8,128)(2,1)S(1)} %get-tuple-element.25), channel_id=1, source_target_pairs={{0,3},{1,2},{2,1},{3,0},{4,7},{5,6},{6,5},{7,4},{8,11},{9,10},{10,... | collective-permute-start | bytes 393224 | tf_op jit(solution)/shard_map/ppermute | solution.py:220

commit v5 on v4

--- a/solution.py
+++ b/solution.py
@@ -37,13 +37,41 @@
     return tuple(outs)
 
 
-def own_units_kernel(ref, out):
-    out[...] = unit_rows(ref[...])[0].astype(out.dtype)
-
-
-def own_units(raw):
-    out = jax.ShapeDtypeStruct(raw.shape, jnp.bfloat16)
-    return call(own_units_kernel, [out], [raw], flops=4 * raw.size, name="own_units")[0]
+def prepare_kernel(text_ref, scale_ref, bias_ref, units, params, raw, scalars, sems):
+    copies = [
+        pltpu.make_async_copy(text_ref, raw, sems.at[0]),
+        pltpu.make_async_copy(scale_ref, scalars.at[0], sems.at[1]),
+        pltpu.make_async_copy(bias_ref, scalars.at[1], sems.at[2]),
+    ]
+    for copy in copies:
+        copy.start()
+    for copy in copies:
+        copy.wait()
+    units[...] = unit_rows(raw[...])[0].astype(units.dtype)
+    params[0:1, :] = jnp.full((1, 128), scalars[0, 0], jnp.float32)
+    params[1:2, :] = jnp.full((1, 128), scalars[1, 0], jnp.float32)
+
+
+def prepare(texts, scale, bias):
+    return pl.pallas_call(
+        prepare_kernel,
+        out_shape=(
+            jax.ShapeDtypeStruct(texts.shape, jnp.bfloat16),
+            jax.ShapeDtypeStruct((2, 128), jnp.float32),
+        ),
+        in_specs=[pl.BlockSpec(memory_space=pltpu.HBM)] * 3,
+        out_specs=(VMEM, VMEM),
+        scratch_shapes=[
+            pltpu.VMEM(texts.shape, texts.dtype),
+            pltpu.SMEM((2, 1), jnp.float32),
+            pltpu.SemaphoreType.DMA((3,)),
+        ],
+        compiler_params=pltpu.CompilerParams(vmem_limit_bytes=VMEM_LIMIT),
+        cost_estimate=pl.CostEstimate(
+            flops=4 * texts.size, bytes_accessed=4 * texts.size, transcendentals=0
+        ),
+        name="prepare",
+    )(texts, scale, bias)
 
 
 def stack_units_kernel(*refs):
@@ -106,7 +134,7 @@
         ref[...] = total[a * rows:(a + 1) * rows, :].astype(ref.dtype)
 
 
-def pair_terms(params, images, texts):
+def pair_terms(params, images, texts, image_types):
     rows, width = images[0].shape
     image_rows = rows * len(images)
 
@@ -130,8 +158,7 @@
     outs = call(
         functools.partial(other_pairs_kernel, len(others)),
         [jax.ShapeDtypeStruct(t.shape, jnp.bfloat16) for t in others]
-        + [jax.ShapeDtypeStruct((rows, width), jnp.float32)]
-        + [jax.ShapeDtypeStruct((rows, width), jnp.bfloat16)] * (len(images) - 1),
+        + [jax.ShapeDtypeStruct((rows, width), t) for t in image_types],
         [params, units, total, *others],
         name="other_pairs",
         **cost(sum(t.shape[0] for t in others)),
@@ -159,6 +186,20 @@
         flops=len(parts) * parts[0].size,
         name="add_stacks",
     )
+
+
+def add_parts_kernel(*refs):
+    total = refs[0][...].astype(jnp.float32)
+    for part in refs[1:-1]:
+        total = total + part[...].astype(jnp.float32)
+    refs[-1][...] = total.astype(refs[-1].dtype)
+
+
+def add_parts(parts):
+    out = jax.ShapeDtypeStruct(parts[0].shape, jnp.bfloat16)
+    return call(
+        add_parts_kernel, [out], parts, flops=len(parts) * out.size, name="add_parts"
+    )[0]
 
 
 def finish_kernel(image_count, text_count, image_ref, text_ref, *refs):
@@ -225,26 +266,37 @@
         held = {(0, 0): rows}
         for h in range(1, high_count):
             held[h, 0] = move(rows, high=h)
-        for h in range(high_count):
+        for w in range(1, low_count):
+            held[0, w] = move(rows, low=w)
+        for h in range(1, high_count):
             for w in range(1, low_count):
-                held[h, w] = move(held[h, 0], low=w)
+                block, held[0, w] = lax.optimization_barrier((held[h, 0], held[0, w]))
+                held[h, w] = move(block, low=w)
         return [held[step] for step in far_steps]
 
+    def return_far(parts):
+        came = {
+            (h, w): move(parts[h, w], low=-w)
+            for h in reversed(range(high_count)) for w in range(1, low_count)
+        }
+        owned = [parts[0, 0]] + [came[0, w] for w in range(1, low_count)]
+        for h in range(1, high_count):
+            both = add_parts([parts[h, 0]] + [came[h, w] for w in range(1, low_count)])
+            owned.append(move(both, high=-h))
+        return owned
+
     def on_device(images, texts, logit_scale, logit_bias):
-        params = jnp.concatenate(
-            [jnp.broadcast_to(logit_scale, (1, 128)), jnp.broadcast_to(logit_bias, (1, 128))]
-        )
+        own_texts, params = prepare(texts, logit_scale, logit_bias)
         image_rows = gather_far(images)
-        near_rows = [own_units(texts)] + [move(texts, near=n) for n in range(1, near_count)]
+        near_rows = [own_texts] + [move(texts, near=n) for n in range(1, near_count)]
         own_stack = stack_units(near_rows)
         stacks = [own_stack] + [move(own_stack, grp=g) for g in range(1, grp_count)]
-        image_parts, text_parts = pair_terms(params, image_rows, stacks)
-        image_parts = [image_parts[0]] + [
-            move(part, high=-h, low=-w) for (h, w), part in zip(far_steps, image_parts) if h or w
-        ]
+        image_types = [jnp.bfloat16 if w else jnp.float32 for _, w in far_steps]
+        image_parts, text_parts = pair_terms(params, image_rows, stacks, image_types)
         text_parts = [text_parts[0]] + [
             move(part, grp=-g) for g, part in enumerate(text_parts) if g
         ]
+        image_parts = return_far(dict(zip(far_steps, image_parts)))
         near_parts = add_stacks(text_parts, near_count)
         near_parts = [near_parts[0]] + [
             move(part, near=-n) for n, part in enumerate(near_parts) if n

time: 36 us -> 40.3 us (1.12)
  waiting for transfers between devices: 7.75 us -> 14 us
  starting transfers between devices: 20.1 us -> 17.5 us
  Pallas kernels: 4.97 us -> 5.7 us
    ppermute x14, waiting for transfers between devices: 7.75 us -> 14 us  [move(): return lax.ppermute(value, AXES, perm)]
    ppermute x14, starting transfers between devices: 20.1 us -> 17.5 us  [move(): return lax.ppermute(value, AXES, perm)]
    pallas_call x0 -> x1, Pallas kernels: none -> 0.82 us  [prepare(): pl.pallas_call(prepare_kernel, out_shape=(jax.ShapeDtypeStruct(texts.shap...]
  transfers between devices with their start and end apart: 14 -> 14, of which waited for: 6 -> 5; matrix products, arithmetic and copies ran while one was open for 0% -> 0% of each run, Pallas kernels for 6% -> 7%
where the time goes in v5:
time: 40.3 us; the launch traced here: 40.1 us
  starting transfers between devices  17.5 us (43%)
  waiting for transfers between devices  14 us (35%)
  Pallas kernels  5.7 us (14%)
  between operations  2.03 us (5%)
  local copies, waits for them, and re-layouts  0.91 us (2%)
    ppermute x14, starting transfers between devices, move(): return lax.ppermute(value, AXES, perm)  17.5 us
    ppermute x14, waiting for transfers between devices, move(): return lax.ppermute(value, AXES, perm)  14 us
    pallas_call x6, Pallas kernels, call(): pl.pallas_call(kernel, out_shape=out_shape, in_specs=[VMEM] * len(operand...  4.88 us
    unnamed x6, local copies, waits for them, and re-layouts  0.91 us
    pallas_call x1, Pallas kernels, prepare(): pl.pallas_call(prepare_kernel, out_shape=(jax.ShapeDtypeStruct(texts.shap...  0.82 us
  transfers between devices with their start and end apart: 14, of which 5 were waited for; matrix products, arithmetic and copies ran while one was open for 0% of the time, Pallas kernels for 7%

profile of v5, /device:TPU:0, one launch (start us, length us, event | category | flops | bytes accessed | tf_op | source)
XLA Modules:
  0.0 40.1 jit_solution(1967284504430140358)
XLA Ops:
  0.6 3.1 %collective-permute-start.4 = (bf16[128,512]{1,0:T(8,128)(2,1)}, bf16[128,512]{1,0:T(8,128)(2,1)S(1)}, u32[]{:S(2)}, u32[]{:S(2)}) collective-permute-start(bf16[128,512]{1,0:T(8,128)(2,1)} %image_ref.1), channel_id=1, source_target_pairs={{0,4},{1,5},{2,6},{3,7},{4,0},{5,1},{6,2},{7,3},{8,12},{9,13},{10,... | collective-permute-start | bytes 393224 | tf_op jit(solution)/shard_map/ppermute | solution.py:261
  3.7 2.6 %collective-permute-start.3 = (bf16[128,512]{1,0:T(8,128)(2,1)}, bf16[128,512]{1,0:T(8,128)(2,1)S(1)}, u32[]{:S(2)}, u32[]{:S(2)}) collective-permute-start(bf16[128,512]{1,0:T(8,128)(2,1)} %image_ref.1), channel_id=1, source_target_pairs={{0,8},{1,9},{2,10},{3,11},{4,12},{5,13},{6,14},{7,15},{8,0},{9,1},... | collective-permute-start | bytes 393224 | tf_op jit(solution)/shard_map/ppermute | solution.py:261
  6.3 1.5 %collective-permute-start.1 = (bf16[128,512]{1,0:T(8,128)(2,1)}, bf16[128,512]{1,0:T(8,128)(2,1)S(1)}, u32[]{:S(2)}, u32[]{:S(2)}) collective-permute-start(bf16[128,512]{1,0:T(8,128)(2,1)} %text_ref.3), channel_id=1, source_target_pairs={{0,2},{1,3},{2,0},{3,1},{4,6},{5,7},{6,4},{7,5},{8,10},{9,11},{10,... | collective-permute-start | bytes 393224 | tf_op jit(solution)/shard_map/ppermute | solution.py:261
  7.8 1.5 %collective-permute-start = (bf16[128,512]{1,0:T(8,128)(2,1)}, bf16[128,512]{1,0:T(8,128)(2,1)S(1)}, u32[]{:S(2)}, u32[]{:S(2)}) collective-permute-start(bf16[128,512]{1,0:T(8,128)(2,1)} %text_ref.3), channel_id=1, source_target_pairs={{0,1},{1,0},{2,3},{3,2},{4,5},{5,4},{6,7},{7,6},{8,9},{9,8},{10,11... | collective-permute-start | bytes 393224 | tf_op jit(solution)/shard_map/ppermute | solution.py:261
  9.3 0.5 %collective-permute-start.2 = (bf16[128,512]{1,0:T(8,128)(2,1)}, bf16[128,512]{1,0:T(8,128)(2,1)S(1)}, u32[]{:S(2)}, u32[]{:S(2)}) collective-permute-start(bf16[128,512]{1,0:T(8,128)(2,1)} %text_ref.3), channel_id=1, source_target_pairs={{0,3},{1,2},{2,1},{3,0},{4,7},{5,6},{6,5},{7,4},{8,11},{9,10},{10,... | collective-permute-start | bytes 393224 | tf_op jit(solution)/shard_map/ppermute | solution.py:261
  9.8 2.9 %collective-permute-done.3.refs_2_ = bf16[128,512]{1,0:T(8,128)(2,1)S(1)} collective-permute-done((bf16[128,512]{1,0:T(8,128)(2,1)}, bf16[128,512]{1,0:T(8,128)(2,1)S(1)}, u32[]{:S(2)}, u32[]{:S(2)}) %collective-permute-start.3) | collective-permute-done | bytes 131104 | tf_op jit(solution)/shard_map/ppermute | solution.py:261
  12.7 0.4 %collective-permute-start.5 = (bf16[128,512]{1,0:T(8,128)(2,1)S(1)}, bf16[128,512]{1,0:T(8,128)(2,1)S(1)}, u32[]{:S(2)}, u32[]{:S(2)}) collective-permute-start(bf16[128,512]{1,0:T(8,128)(2,1)S(1)} %collective-permute-done.3.refs_2_), channel_id=1, source_target_pairs={{0,4},{1,5},{2,6},{3,7},{4,0},{5,1},{6,2},{7,3},{8,12},{9,13},{10,... | collective-permute-start | bytes 393224 | tf_op jit(solution)/shard_map/ppermute | solution.py:261
  14.4 0.9 %copy-done = bf16[128,512]{1,0:T(8,128)(2,1)S(1)} copy-done((bf16[128,512]{1,0:T(8,128)(2,1)S(1)}, bf16[128,512]{1,0:T(8,128)(2,1)}, u32[]{:S(2)}) %copy-start) | copy-done | bytes 131096
  15.3 0.8 %prepare.1 = (bf16[128,512]{1,0:T(8,128)(2,1)S(1)}, f32[2,128]{1,0:T(2,128)S(1)}) custom-call(bf16[128,512]{1,0:T(8,128)(2,1)S(1)} %copy-done, f32[1]{0:T(128)S(6)} %copy.6.scale_ref, f32[1]{0:T(128)S(6)} %copy.7.bias_ref), custom_call_target="tpu_custom_call" | custom-call | flops 262144 | bytes 262144 | tf_op jit(solution)/shard_map/prepare/pallas_call | solution.py:56
  16.2 0.2 stack_units.1.text_ref
  16.4 1.2 %collective-permute-done.5.refs_3_ = bf16[128,512]{1,0:T(8,128)(2,1)S(1)} collective-permute-done((bf16[128,512]{1,0:T(8,128)(2,1)S(1)}, bf16[128,512]{1,0:T(8,128)(2,1)S(1)}, u32[]{:S(2)}, u32[]{:S(2)}) %collective-permute-start.5) | collective-permute-done | bytes 131104 | tf_op jit(solution)/shard_map/ppermute | solution.py:261
  17.6 1.8 %own_pairs.1 = (f32[512,512]{1,0:T(8,128)S(1)}, bf16[512,512]{1,0:T(8,128)(2,1)S(1)}, f32[512,512]{1,0:T(8,128)S(1)}) custom-call(f32[2,128]{1,0:T(2,128)S(1)} %get-tuple-element.18.params_ref, bf16[512,512]{1,0:T(8,128)(2,1)S(1)} %stack_units.1.text_ref, bf16[128,512]{1,0:T(8,128)(2,1)S(1)} %copy-done.2, ...), custom_call_target="tpu_custom_call" | custom-call | flops 8053063680 | bytes 3671040 | tf_op jit(solution)/shard_map/own_pairs/pallas_call | solution.py:25
  19.4 1.8 %other_pairs.1 = (bf16[512,512]{1,0:T(8,128)(2,1)S(1)}, f32[128,512]{1,0:T(8,128)S(1)}, bf16[128,512]{1,0:T(8,128)(2,1)S(1)}, f32[128,512]{1,0:T(8,128)S(1)}, bf16[128,512]{1,0:T(8,128)(2,1)S(1)}) custom-call(f32[2,128]{1,0:T(2,128)S(1)} %get-tuple-element.18.params_ref, bf16[512,512]{1,0:T(8,128)(2,1)S(1)} %get-tuple-element.22.units_ref, ...), custom_call_target="tpu_custom_call" | custom-call | flops 805306368 | bytes 3408896 | tf_op jit(solution)/shard_map/other_pairs/pallas_call | solution.py:25
  21.3 1.1 %collective-permute-start.8 = (bf16[128,512]{1,0:T(8,128)(2,1)S(1)}, bf16[128,512]{1,0:T(8,128)(2,1)S(1)}, u32[]{:S(2)}, u32[]{:S(2)}) collective-permute-start(bf16[128,512]{1,0:T(8,128)(2,1)S(1)} %get-tuple-element.27), channel_id=1, source_target_pairs={{0,4},{1,5},{2,6},{3,7},{4,0},{5,1},{6,2},{7,3},{8,12},{9,13},{10,... | collective-permute-start | bytes 393224 | tf_op jit(solution)/shard_map/ppermute | solution.py:261
  22.4 1.0 %collective-permute-start.7 = (bf16[128,512]{1,0:T(8,128)(2,1)S(1)}, bf16[128,512]{1,0:T(8,128)(2,1)S(1)}, u32[]{:S(2)}, u32[]{:S(2)}) collective-permute-start(bf16[128,512]{1,0:T(8,128)(2,1)S(1)} %get-tuple-element.25), channel_id=1, source_target_pairs={{0,4},{1,5},{2,6},{3,7},{4,0},{5,1},{6,2},{7,3},{8,12},{9,13},{10,... | collective-permute-start | bytes 393224 | tf_op jit(solution)/shard_map/ppermute | solution.py:261
  23.4 4.3 %collective-permute-done.8.refs_1_ = bf16[128,512]{1,0:T(8,128)(2,1)S(1)} collective-permute-done((bf16[128,512]{1,0:T(8,128)(2,1)S(1)}, bf16[128,512]{1,0:T(8,128)(2,1)S(1)}, u32[]{:S(2)}, u32[]{:S(2)}) %collective-permute-start.8) | collective-permute-done | bytes 131104 | tf_op jit(solution)/shard_map/ppermute | solution.py:261
  27.7 2.1 %collective-permute-start.9 = (bf16[128,512]{1,0:T(8,128)(2,1)S(1)}, bf16[128,512]{1,0:T(8,128)(2,1)S(1)}, u32[]{:S(2)}, u32[]{:S(2)}) collective-permute-start(bf16[128,512]{1,0:T(8,128)(2,1)S(1)} %add_parts.1), channel_id=1, source_target_pairs={{0,8},{1,9},{2,10},{3,11},{4,12},{5,13},{6,14},{7,15},{8,0},{9,1},... | collective-permute-start | bytes 393224 | tf_op jit(solution)/shard_map/ppermute | solution.py:261
  29.8 0.1 add_stacks.1
  29.9 1.6 %collective-permute-start.11 = (bf16[128,512]{1,0:T(8,128)(2,1)S(1)}, bf16[128,512]{1,0:T(8,128)(2,1)S(1)}, u32[]{:S(2)}, u32[]{:S(2)}) collective-permute-start(bf16[128,512]{1,0:T(8,128)(2,1)S(1)} %get-tuple-element.31), channel_id=1, source_target_pairs={{0,1},{1,0},{2,3},{3,2},{4,5},{5,4},{6,7},{7,6},{8,9},{9,8},{10,11... | collective-permute-start | bytes 393224 | tf_op jit(solution)/shard_map/ppermute | solution.py:261
  31.4 1.5 %collective-permute-start.12 = (bf16[128,512]{1,0:T(8,128)(2,1)S(1)}, bf16[128,512]{1,0:T(8,128)(2,1)S(1)}, u32[]{:S(2)}, u32[]{:S(2)}) collective-permute-start(bf16[128,512]{1,0:T(8,128)(2,1)S(1)} %get-tuple-element.32), channel_id=1, source_target_pairs={{0,2},{1,3},{2,0},{3,1},{4,6},{5,7},{6,4},{7,5},{8,10},{9,11},{10,... | collective-permute-start | bytes 393224 | tf_op jit(solution)/shard_map/ppermute | solution.py:261
  33.0 0.5 %collective-permute-start.13 = (bf16[128,512]{1,0:T(8,128)(2,1)S(1)}, bf16[128,512]{1,0:T(8,128)(2,1)S(1)}, u32[]{:S(2)}, u32[]{:S(2)}) collective-permute-start(bf16[128,512]{1,0:T(8,128)(2,1)S(1)} %get-tuple-element.33), channel_id=1, source_target_pairs={{0,3},{1,2},{2,1},{3,0},{4,7},{5,6},{6,5},{7,4},{8,11},{9,10},{10,... | collective-permute-start | bytes 393224 | tf_op jit(solution)/shard_map/ppermute | solution.py:261
  33.4 2.6 %collective-permute-done.9.refs_2_ = bf16[128,512]{1,0:T(8,128)(2,1)S(1)} collective-permute-done((bf16[128,512]{1,0:T(8,128)(2,1)S(1)}, bf16[128,512]{1,0:T(8,128)(2,1)S(1)}, u32[]{:S(2)}, u32[]{:S(2)}) %collective-permute-start.9) | collective-permute-done | bytes 131104 | tf_op jit(solution)/shard_map/ppermute | solution.py:261
  36.1 3.0 %collective-permute-done.12.refs_5_ = bf16[128,512]{1,0:T(8,128)(2,1)S(1)} collective-permute-done((bf16[128,512]{1,0:T(8,128)(2,1)S(1)}, bf16[128,512]{1,0:T(8,128)(2,1)S(1)}, u32[]{:S(2)}, u32[]{:S(2)}) %collective-permute-start.12) | collective-permute-done | bytes 131104 | tf_op jit(solution)/shard_map/ppermute | solution.py:261
  39.1 1.0 %finish.1 = (f32[128,512]{1,0:T(8,128)}, f32[128,512]{1,0:T(8,128)}) custom-call(bf16[128,512]{1,0:T(8,128)(2,1)S(1)} %copy-done.2, bf16[128,512]{1,0:T(8,128)(2,1)S(1)} %copy-done.1, f32[128,512]{1,0:T(8,128)S(1)} %get-tuple-element.24.refs_0_, bf16[128,512]{1,0:T(8,128)(2,1)S(1)} %collective-permute-done.7.refs_1_, ...), custom_call_target="tpu_custom_call" | custom-call | flops 4587520 | bytes 1966080 | tf_op jit(solution)/shard_map/finish/pallas_call | solution.py:25
  (17 shorter events, 0.2 us)
Async XLA Ops:
  0.6 9.2 %collective-permute-start.4 = (bf16[128,512]{1,0:T(8,128)(2,1)}, bf16[128,512]{1,0:T(8,128)(2,1)S(1)}, u32[]{:S(2)}, u32[]{:S(2)}) collective-permute-start(bf16[128,512]{1,0:T(8,128)(2,1)} %image_ref.1), channel_id=1, source_target_pairs={{0,4},{1,5},{2,6},{3,7},{4,0},{5,1},{6,2},{7,3},{8,12},{9,13},{10,... | collective-permute-start | bytes 393224 | tf_op jit(solution)/shard_map/ppermute | solution.py:261
  3.7 8.9 %collective-permute-start.3 = (bf16[128,512]{1,0:T(8,128)(2,1)}, bf16[128,512]{1,0:T(8,128)(2,1)S(1)}, u32[]{:S(2)}, u32[]{:S(2)}) collective-permute-start(bf16[128,512]{1,0:T(8,128)(2,1)} %image_ref.1), channel_id=1, source_target_pairs={{0,8},{1,9},{2,10},{3,11},{4,12},{5,13},{6,14},{7,15},{8,0},{9,1},... | collective-permute-start | bytes 393224 | tf_op jit(solution)/shard_map/ppermute | solution.py:261
  6.3 9.8 %collective-permute-start.1 = (bf16[128,512]{1,0:T(8,128)(2,1)}, bf16[128,512]{1,0:T(8,128)(2,1)S(1)}, u32[]{:S(2)}, u32[]{:S(2)}) collective-permute-start(bf16[128,512]{1,0:T(8,128)(2,1)} %text_ref.3), channel_id=1, source_target_pairs={{0,2},{1,3},{2,0},{3,1},{4,6},{5,7},{6,4},{7,5},{8,10},{9,11},{10,... | collective-permute-start | bytes 393224 | tf_op jit(solution)/shard_map/ppermute | solution.py:261
  7.8 8.3 %collective-permute-start = (bf16[128,512]{1,0:T(8,128)(2,1)}, bf16[128,512]{1,0:T(8,128)(2,1)S(1)}, u32[]{:S(2)}, u32[]{:S(2)}) collective-permute-start(bf16[128,512]{1,0:T(8,128)(2,1)} %text_ref.3), channel_id=1, source_target_pairs={{0,1},{1,0},{2,3},{3,2},{4,5},{5,4},{6,7},{7,6},{8,9},{9,8},{10,11... | collective-permute-start | bytes 393224 | tf_op jit(solution)/shard_map/ppermute | solution.py:261
  9.3 6.8 %collective-permute-start.2 = (bf16[128,512]{1,0:T(8,128)(2,1)}, bf16[128,512]{1,0:T(8,128)(2,1)S(1)}, u32[]{:S(2)}, u32[]{:S(2)}) collective-permute-start(bf16[128,512]{1,0:T(8,128)(2,1)} %text_ref.3), channel_id=1, source_target_pairs={{0,3},{1,2},{2,1},{3,0},{4,7},{5,6},{6,5},{7,4},{8,11},{9,10},{10,... | collective-permute-start | bytes 393224 | tf_op jit(solution)/shard_map/ppermute | solution.py:261
  12.7 5.0 %collective-permute-start.5 = (bf16[128,512]{1,0:T(8,128)(2,1)S(1)}, bf16[128,512]{1,0:T(8,128)(2,1)S(1)}, u32[]{:S(2)}, u32[]{:S(2)}) collective-permute-start(bf16[128,512]{1,0:T(8,128)(2,1)S(1)} %collective-permute-done.3.refs_2_), channel_id=1, source_target_pairs={{0,4},{1,5},{2,6},{3,7},{4,0},{5,1},{6,2},{7,3},{8,12},{9,13},{10,... | collective-permute-start | bytes 393224 | tf_op jit(solution)/shard_map/ppermute | solution.py:261
  14.4 0.9 %copy-start = (bf16[128,512]{1,0:T(8,128)(2,1)S(1)}, bf16[128,512]{1,0:T(8,128)(2,1)}, u32[]{:S(2)}) copy-start(bf16[128,512]{1,0:T(8,128)(2,1)} %text_ref.3) | copy-start | bytes 393220
  16.2 1.5 %copy-start.2 = (bf16[128,512]{1,0:T(8,128)(2,1)S(1)}, bf16[128,512]{1,0:T(8,128)(2,1)}, u32[]{:S(2)}) copy-start(bf16[128,512]{1,0:T(8,128)(2,1)} %image_ref.1) | copy-start | bytes 393220
  16.3 3.1 %collective-permute-start.6 = (bf16[512,512]{1,0:T(8,128)(2,1)S(1)}, bf16[512,512]{1,0:T(8,128)(2,1)S(1)}, u32[]{:S(2)}, u32[]{:S(2)}) collective-permute-start(bf16[512,512]{1,0:T(8,128)(2,1)S(1)} %stack_units.1.text_ref), channel_id=1, source_target_pairs={{0,16},{1,17},{2,18},{3,19},{4,20},{5,21},{6,22},{7,23},{8,24},{9,... | collective-permute-start | bytes 1572872 | tf_op jit(solution)/shard_map/ppermute | solution.py:261
  21.2 8.6 %collective-permute-start.10 = (bf16[512,512]{1,0:T(8,128)(2,1)S(1)}, bf16[512,512]{1,0:T(8,128)(2,1)S(1)}, u32[]{:S(2)}, u32[]{:S(2)}) collective-permute-start(bf16[512,512]{1,0:T(8,128)(2,1)S(1)} %get-tuple-element.29), channel_id=1, source_target_pairs={{0,16},{1,17},{2,18},{3,19},{4,20},{5,21},{6,22},{7,23},{8,24},{9,... | collective-permute-start | bytes 1572872 | tf_op jit(solution)/shard_map/ppermute | solution.py:261
  21.3 6.4 %collective-permute-start.8 = (bf16[128,512]{1,0:T(8,128)(2,1)S(1)}, bf16[128,512]{1,0:T(8,128)(2,1)S(1)}, u32[]{:S(2)}, u32[]{:S(2)}) collective-permute-start(bf16[128,512]{1,0:T(8,128)(2,1)S(1)} %get-tuple-element.27), channel_id=1, source_target_pairs={{0,4},{1,5},{2,6},{3,7},{4,0},{5,1},{6,2},{7,3},{8,12},{9,13},{10,... | collective-permute-start | bytes 393224 | tf_op jit(solution)/shard_map/ppermute | solution.py:261
  22.4 11.1 %collective-permute-start.7 = (bf16[128,512]{1,0:T(8,128)(2,1)S(1)}, bf16[128,512]{1,0:T(8,128)(2,1)S(1)}, u32[]{:S(2)}, u32[]{:S(2)}) collective-permute-start(bf16[128,512]{1,0:T(8,128)(2,1)S(1)} %get-tuple-element.25), channel_id=1, source_target_pairs={{0,4},{1,5},{2,6},{3,7},{4,0},{5,1},{6,2},{7,3},{8,12},{9,13},{10,... | collective-permute-start | bytes 393224 | tf_op jit(solution)/shard_map/ppermute | solution.py:261
  27.7 8.4 %collective-permute-start.9 = (bf16[128,512]{1,0:T(8,128)(2,1)S(1)}, bf16[128,512]{1,0:T(8,128)(2,1)S(1)}, u32[]{:S(2)}, u32[]{:S(2)}) collective-permute-start(bf16[128,512]{1,0:T(8,128)(2,1)S(1)} %add_parts.1), channel_id=1, source_target_pairs={{0,8},{1,9},{2,10},{3,11},{4,12},{5,13},{6,14},{7,15},{8,0},{9,1},... | collective-permute-start | bytes 393224 | tf_op jit(solution)/shard_map/ppermute | solution.py:261
  29.8 9.3 %copy-start.1 = (bf16[128,512]{1,0:T(8,128)(2,1)S(1)}, bf16[128,512]{1,0:T(8,128)(2,1)}, u32[]{:S(2)}) copy-start(bf16[128,512]{1,0:T(8,128)(2,1)} %text_ref.3) | copy-start | bytes 393220
  29.9 6.2 %collective-permute-start.11 = (bf16[128,512]{1,0:T(8,128)(2,1)S(1)}, bf16[128,512]{1,0:T(8,128)(2,1)S(1)}, u32[]{:S(2)}, u32[]{:S(2)}) collective-permute-start(bf16[128,512]{1,0:T(8,128)(2,1)S(1)} %get-tuple-element.31), channel_id=1, source_target_pairs={{0,1},{1,0},{2,3},{3,2},{4,5},{5,4},{6,7},{7,6},{8,9},{9,8},{10,11... | collective-permute-start | bytes 393224 | tf_op jit(solution)/shard_map/ppermute | solution.py:261
  31.4 7.6 %collective-permute-start.12 = (bf16[128,512]{1,0:T(8,128)(2,1)S(1)}, bf16[128,512]{1,0:T(8,128)(2,1)S(1)}, u32[]{:S(2)}, u32[]{:S(2)}) collective-permute-start(bf16[128,512]{1,0:T(8,128)(2,1)S(1)} %get-tuple-element.32), channel_id=1, source_target_pairs={{0,2},{1,3},{2,0},{3,1},{4,6},{5,7},{6,4},{7,5},{8,10},{9,11},{10,... | collective-permute-start | bytes 393224 | tf_op jit(solution)/shard_map/ppermute | solution.py:261
  33.0 6.1 %collective-permute-start.13 = (bf16[128,512]{1,0:T(8,128)(2,1)S(1)}, bf16[128,512]{1,0:T(8,128)(2,1)S(1)}, u32[]{:S(2)}, u32[]{:S(2)}) collective-permute-start(bf16[128,512]{1,0:T(8,128)(2,1)S(1)} %get-tuple-element.33), channel_id=1, source_target_pairs={{0,3},{1,2},{2,1},{3,0},{4,7},{5,6},{6,5},{7,4},{8,11},{9,10},{10,... | collective-permute-start | bytes 393224 | tf_op jit(solution)/shard_map/ppermute | solution.py:261

commit v6 on v5

--- a/solution.py
+++ b/solution.py
@@ -10,7 +10,7 @@
 AXES = ("grp", "dev")
 VMEM_LIMIT = 50 * 1024 * 1024
 SPAN = 256
-EARLY = 10
+LATE = 40
 VMEM = pl.BlockSpec(memory_space=pltpu.VMEM)
 
 
@@ -112,65 +112,75 @@
     return total
 
 
-def own_pairs_kernel(params_ref, text_ref, *refs):
+def own_pairs_kernel(has_own, params_ref, text_ref, *refs):
     image_refs, (text_out, units_out, total_out) = refs[:-3], refs[-3:]
     rows = image_refs[0].shape[0]
     for a, ref in enumerate(image_refs):
         units_out[a * rows:(a + 1) * rows, :] = unit_rows(ref[...])[0].astype(jnp.bfloat16)
     temper, offset = params_ref[0:1, 0:1], params_ref[1:2, 0:1]
-    total_out[...] = pairs(units_out[...], temper, offset, text_ref, text_out, rows)
-
-
-def other_pairs_kernel(text_count, params_ref, units_ref, total_ref, *refs):
-    text_refs, outs = refs[:text_count], refs[text_count:]
+    own = rows if has_own else 0
+    total_out[...] = pairs(units_out[...], temper, offset, text_ref, text_out, own)
+
+
+def own_pairs(params, text, images, has_own, weight, name):
+    rows, width = images[0].shape
+    image_rows = rows * len(images)
+    return call(
+        functools.partial(own_pairs_kernel, has_own),
+        [
+            jax.ShapeDtypeStruct(text.shape, jnp.float32),
+            jax.ShapeDtypeStruct((image_rows, width), jnp.bfloat16),
+            jax.ShapeDtypeStruct((image_rows, width), jnp.float32),
+        ],
+        [params, text, *images],
+        flops=6 * weight * image_rows * text.shape[0] * width,
+        transcendentals=2 * weight * image_rows * text.shape[0],
+        name=name,
+    )
+
+
+def other_pairs_kernel(part_count, text_count, params_ref, *refs):
+    units_refs, total_refs = refs[:part_count], refs[part_count:2 * part_count]
+    text_refs = refs[2 * part_count:2 * part_count + text_count]
+    outs = refs[2 * part_count + text_count:]
     text_out, image_out = outs[:text_count], outs[text_count:]
     rows = image_out[0].shape[0]
-    vi = units_ref[...]
+    vi = jnp.concatenate([ref[...] for ref in units_refs], axis=0)
     temper, offset = params_ref[0:1, 0:1], params_ref[1:2, 0:1]
-    total = total_ref[...]
+    total = jnp.concatenate([ref[...] for ref in total_refs], axis=0)
     for t in range(text_count):
         total = total + pairs(vi, temper, offset, text_refs[t], text_out[t], 0)
     for a, ref in enumerate(image_out):
         ref[...] = total[a * rows:(a + 1) * rows, :].astype(ref.dtype)
 
 
-def pair_terms(params, images, texts, image_types):
-    rows, width = images[0].shape
-    image_rows = rows * len(images)
-
-    def cost(text_rows):
-        return dict(
-            flops=6 * image_rows * text_rows * width, transcendentals=2 * image_rows * text_rows
-        )
-
-    own_out, units, total = call(
-        own_pairs_kernel,
-        [
-            jax.ShapeDtypeStruct(texts[0].shape, jnp.float32),
-            jax.ShapeDtypeStruct((image_rows, width), jnp.bfloat16),
-            jax.ShapeDtypeStruct((image_rows, width), jnp.float32),
-        ],
-        [params, texts[0], *images],
-        name="own_pairs",
-        **cost(EARLY * texts[0].shape[0]),
-    )
+def pair_terms(params, early, late, texts):
+    rows, width = early[0].shape
+    held = []
+    for images, weight, name in ((early, 1, "early_pairs"), (late, LATE, "late_pairs")):
+        if images:
+            held.append(own_pairs(params, texts[0], images, images is early, weight, name))
+    count = len(early) + len(late)
     others = texts[1:]
+    text_rows = sum(t.shape[0] for t in others)
     outs = call(
-        functools.partial(other_pairs_kernel, len(others)),
+        functools.partial(other_pairs_kernel, len(held), len(others)),
         [jax.ShapeDtypeStruct(t.shape, jnp.bfloat16) for t in others]
-        + [jax.ShapeDtypeStruct((rows, width), t) for t in image_types],
-        [params, units, total, *others],
+        + [jax.ShapeDtypeStruct((rows, width), jnp.float32)]
+        + [jax.ShapeDtypeStruct((rows, width), jnp.bfloat16)] * (count - 1),
+        [params, *[h[1] for h in held], *[h[2] for h in held], *others],
+        flops=6 * count * rows * text_rows * width,
+        transcendentals=2 * count * rows * text_rows,
         name="other_pairs",
-        **cost(sum(t.shape[0] for t in others)),
-    )
-    return outs[len(others):], (own_out,) + outs[:len(others)]
+    )
+    return outs[len(others):], [h[0] for h in held], outs[:len(others)]
 
 
 def add_stacks_kernel(part_count, *refs):
     parts, outs = refs[:part_count], refs[part_count:]
     rows = outs[0].shape[0]
     for at, out in enumerate(outs):
-        total = parts[0][at * rows:(at + 1) * rows, :]
+        total = parts[0][at * rows:(at + 1) * rows, :].astype(jnp.float32)
         for part in parts[1:]:
             total = total + part[at * rows:(at + 1) * rows, :].astype(jnp.float32)
         out[...] = total.astype(out.dtype)
@@ -188,41 +198,22 @@
     )
 
 
-def add_parts_kernel(*refs):
-    total = refs[0][...].astype(jnp.float32)
-    for part in refs[1:-1]:
-        total = total + part[...].astype(jnp.float32)
-    refs[-1][...] = total.astype(refs[-1].dtype)
-
-
-def add_parts(parts):
-    out = jax.ShapeDtypeStruct(parts[0].shape, jnp.bfloat16)
-    return call(
-        add_parts_kernel, [out], parts, flops=len(parts) * out.size, name="add_parts"
-    )[0]
-
-
-def finish_kernel(image_count, text_count, image_ref, text_ref, *refs):
-    image_parts = refs[:image_count]
-    text_parts = refs[image_count:image_count + text_count]
-    outs = refs[image_count + text_count:]
-    for raw, parts, out in ((image_ref, image_parts, outs[0]), (text_ref, text_parts, outs[1])):
+def finish_kernel(sides, image_ref, text_ref, *refs):
+    outs = refs[len(sides):]
+    for side, (raw, out) in enumerate(zip((image_ref, text_ref), outs)):
         unit, factor = unit_rows(raw[...])
-        total = parts[0][...].astype(jnp.float32)
-        for part in parts[1:]:
-            total = total + part[...].astype(jnp.float32)
+        total = sum(ref[...].astype(jnp.float32) for at, ref in zip(sides, refs) if at == side)
         along = jnp.sum(unit * total, axis=-1, keepdims=True)
         out[...] = factor * (total - unit * along)
 
 
-def finish(images, texts, image_parts, text_parts):
+def finish(images, texts, parts):
     out = jax.ShapeDtypeStruct(images.shape, jnp.float32)
-    count = len(image_parts) + len(text_parts)
     return call(
-        functools.partial(finish_kernel, len(image_parts), len(text_parts)),
+        functools.partial(finish_kernel, [side for side, _ in parts]),
         [out, out],
-        [images, texts, *image_parts, *text_parts],
-        flops=10 * count * images.size,
+        [images, texts, *[part for _, part in parts]],
+        flops=10 * len(parts) * images.size,
         name="finish",
     )
 
@@ -260,48 +251,38 @@
                         perm.append((source, target))
         return lax.ppermute(value, AXES, perm)
 
-    far_steps = [(h, w) for h in range(high_count) for w in range(low_count)]
-
-    def gather_far(rows):
-        held = {(0, 0): rows}
-        for h in range(1, high_count):
-            held[h, 0] = move(rows, high=h)
-        for w in range(1, low_count):
-            held[0, w] = move(rows, low=w)
-        for h in range(1, high_count):
-            for w in range(1, low_count):
-                block, held[0, w] = lax.optimization_barrier((held[h, 0], held[0, w]))
-                held[h, w] = move(block, low=w)
-        return [held[step] for step in far_steps]
-
-    def return_far(parts):
-        came = {
-            (h, w): move(parts[h, w], low=-w)
-            for h in reversed(range(high_count)) for w in range(1, low_count)
-        }
-        owned = [parts[0, 0]] + [came[0, w] for w in range(1, low_count)]
-        for h in range(1, high_count):
-            both = add_parts([parts[h, 0]] + [came[h, w] for w in range(1, low_count)])
-            owned.append(move(both, high=-h))
-        return owned
-
     def on_device(images, texts, logit_scale, logit_bias):
         own_texts, params = prepare(texts, logit_scale, logit_bias)
-        image_rows = gather_far(images)
+        early = {(0, 0): images}
+        for h in range(1, high_count):
+            early[h, 0] = move(images, high=h)
+        for w in range(1, low_count):
+            early[0, w] = move(images, low=w)
+        late = {}
+        for h in range(1, high_count):
+            block, own_texts, params = lax.optimization_barrier((early[h, 0], own_texts, params))
+            for w in range(1, low_count):
+                late[h, w] = move(block, low=w)
         near_rows = [own_texts] + [move(texts, near=n) for n in range(1, near_count)]
         own_stack = stack_units(near_rows)
         stacks = [own_stack] + [move(own_stack, grp=g) for g in range(1, grp_count)]
-        image_types = [jnp.bfloat16 if w else jnp.float32 for _, w in far_steps]
-        image_parts, text_parts = pair_terms(params, image_rows, stacks, image_types)
-        text_parts = [text_parts[0]] + [
-            move(part, grp=-g) for g, part in enumerate(text_parts) if g
-        ]
-        image_parts = return_far(dict(zip(far_steps, image_parts)))
-        near_parts = add_stacks(text_parts, near_count)
+        image_parts, own_parts, other_parts = pair_terms(
+            params, list(early.values()), list(late.values()), stacks
+        )
+        far_parts = dict(zip([*early, *late], image_parts))
+        came = [move(part, grp=-g) for g, part in enumerate(other_parts, 1)]
+        low_parts = [move(p, low=-w) for (h, w), p in far_parts.items() if w and not h]
+        high_parts = [move(p, high=-h, low=-w) for (h, w), p in far_parts.items() if h]
+        near_parts = add_stacks([*own_parts, *came], near_count)
         near_parts = [near_parts[0]] + [
             move(part, near=-n) for n, part in enumerate(near_parts) if n
         ]
-        return finish(images, texts, image_parts, near_parts)
+        return finish(
+            images,
+            texts,
+            [(0, part) for part in [far_parts[0, 0]] + low_parts + high_parts]
+            + [(1, part) for part in near_parts],
+        )
 
     in_specs = (P(AXES, None), P(AXES, None), P(), P())
     out_specs = (P(AXES, None), P(AXES, None))

time: 40.3 us -> 36.1 us (0.90)
  waiting for transfers between devices: 14 us -> 7.18 us
  starting transfers between devices: 17.5 us -> 19.8 us
    ppermute x14, waiting for transfers between devices: 14 us -> 7.18 us  [move(): return lax.ppermute(value, AXES, perm)]
    ppermute x14, starting transfers between devices: 17.5 us -> 19.8 us  [move(): return lax.ppermute(value, AXES, perm)]
  transfers between devices with their start and end apart: 14 -> 14, of which waited for: 5 -> 5; matrix products, arithmetic and copies ran while one was open for 0% -> 0% of each run, Pallas kernels for 7% -> 9%
where the time goes in v6:
time: 36.1 us; the launch traced here: 35.9 us
  starting transfers between devices  19.8 us (55%)
  waiting for transfers between devices  7.18 us (20%)
  Pallas kernels  5.98 us (17%)
  between operations  2.03 us (6%)
  local copies, waits for them, and re-layouts  0.91 us (3%)
    ppermute x14, starting transfers between devices, move(): return lax.ppermute(value, AXES, perm)  19.8 us
    ppermute x14, waiting for transfers between devices, move(): return lax.ppermute(value, AXES, perm)  7.18 us
    pallas_call x6, Pallas kernels, call(): pl.pallas_call(kernel, out_shape=out_shape, in_specs=[VMEM] * len(operand...  5.16 us
    unnamed x6, local copies, waits for them, and re-layouts  0.91 us
    pallas_call x1, Pallas kernels, prepare(): pl.pallas_call(prepare_kernel, out_shape=(jax.ShapeDtypeStruct(texts.shap...  0.82 us
  transfers between devices with their start and end apart: 14, of which 5 were waited for; matrix products, arithmetic and copies ran while one was open for 0% of the time, Pallas kernels for 9%

profile of v6, /device:TPU:0, one launch (start us, length us, event | category | flops | bytes accessed | tf_op | source)
XLA Modules:
  0.0 35.9 jit_solution(17034566573625381852)
XLA Ops:
  0.6 4.1 %collective-permute-start = (bf16[128,512]{1,0:T(8,128)(2,1)}, bf16[128,512]{1,0:T(8,128)(2,1)S(1)}, u32[]{:S(2)}, u32[]{:S(2)}) collective-permute-start(bf16[128,512]{1,0:T(8,128)(2,1)} %image_ref.1), channel_id=1, source_target_pairs={{0,8},{1,9},{2,10},{3,11},{4,12},{5,13},{6,14},{7,15},{8,0},{9,1},... | collective-permute-start | bytes 393224 | tf_op jit(solution)/shard_map/ppermute | solution.py:252
  4.7 1.5 %collective-permute-start.2 = (bf16[128,512]{1,0:T(8,128)(2,1)}, bf16[128,512]{1,0:T(8,128)(2,1)S(1)}, u32[]{:S(2)}, u32[]{:S(2)}) collective-permute-start(bf16[128,512]{1,0:T(8,128)(2,1)} %text_ref.3), channel_id=1, source_target_pairs={{0,2},{1,3},{2,0},{3,1},{4,6},{5,7},{6,4},{7,5},{8,10},{9,11},{10,... | collective-permute-start | bytes 393224 | tf_op jit(solution)/shard_map/ppermute | solution.py:252
  6.3 1.5 %collective-permute-start.1 = (bf16[128,512]{1,0:T(8,128)(2,1)}, bf16[128,512]{1,0:T(8,128)(2,1)S(1)}, u32[]{:S(2)}, u32[]{:S(2)}) collective-permute-start(bf16[128,512]{1,0:T(8,128)(2,1)} %text_ref.3), channel_id=1, source_target_pairs={{0,1},{1,0},{2,3},{3,2},{4,5},{5,4},{6,7},{7,6},{8,9},{9,8},{10,11... | collective-permute-start | bytes 393224 | tf_op jit(solution)/shard_map/ppermute | solution.py:252
  7.7 0.5 %collective-permute-start.3 = (bf16[128,512]{1,0:T(8,128)(2,1)}, bf16[128,512]{1,0:T(8,128)(2,1)S(1)}, u32[]{:S(2)}, u32[]{:S(2)}) collective-permute-start(bf16[128,512]{1,0:T(8,128)(2,1)} %text_ref.3), channel_id=1, source_target_pairs={{0,3},{1,2},{2,1},{3,0},{4,7},{5,6},{6,5},{7,4},{8,11},{9,10},{10,... | collective-permute-start | bytes 393224 | tf_op jit(solution)/shard_map/ppermute | solution.py:252
  8.2 1.6 %collective-permute-start.4 = (bf16[128,512]{1,0:T(8,128)(2,1)}, bf16[128,512]{1,0:T(8,128)(2,1)S(1)}, u32[]{:S(2)}, u32[]{:S(2)}) collective-permute-start(bf16[128,512]{1,0:T(8,128)(2,1)} %image_ref.1), channel_id=1, source_target_pairs={{0,4},{1,5},{2,6},{3,7},{4,0},{5,1},{6,2},{7,3},{8,12},{9,13},{10,... | collective-permute-start | bytes 393224 | tf_op jit(solution)/shard_map/ppermute | solution.py:252
  11.1 0.9 %copy-done = bf16[128,512]{1,0:T(8,128)(2,1)S(1)} copy-done((bf16[128,512]{1,0:T(8,128)(2,1)S(1)}, bf16[128,512]{1,0:T(8,128)(2,1)}, u32[]{:S(2)}) %copy-start) | copy-done | bytes 131096
  12.0 0.8 %prepare.1 = (bf16[128,512]{1,0:T(8,128)(2,1)S(1)}, f32[2,128]{1,0:T(2,128)S(1)}) custom-call(bf16[128,512]{1,0:T(8,128)(2,1)S(1)} %copy-done, f32[1]{0:T(128)S(6)} %copy.6.scale_ref, f32[1]{0:T(128)S(6)} %copy.7.bias_ref), custom_call_target="tpu_custom_call" | custom-call | flops 262144 | bytes 262144 | tf_op jit(solution)/shard_map/prepare/pallas_call | solution.py:56
  12.9 0.5 %collective-permute-start.5 = (bf16[128,512]{1,0:T(8,128)(2,1)S(1)}, bf16[128,512]{1,0:T(8,128)(2,1)S(1)}, u32[]{:S(2)}, u32[]{:S(2)}) collective-permute-start(bf16[128,512]{1,0:T(8,128)(2,1)S(1)} %collective-permute-done.refs_1_), channel_id=1, source_target_pairs={{0,4},{1,5},{2,6},{3,7},{4,0},{5,1},{6,2},{7,3},{8,12},{9,13},{10,... | collective-permute-start | bytes 393224 | tf_op jit(solution)/shard_map/ppermute | solution.py:252
  13.4 0.8 %collective-permute-done.3.refs_3_ = bf16[128,512]{1,0:T(8,128)(2,1)S(1)} collective-permute-done((bf16[128,512]{1,0:T(8,128)(2,1)}, bf16[128,512]{1,0:T(8,128)(2,1)S(1)}, u32[]{:S(2)}, u32[]{:S(2)}) %collective-permute-start.3) | collective-permute-done | bytes 131104 | tf_op jit(solution)/shard_map/ppermute | solution.py:252
  14.2 0.2 stack_units.1.text_ref
  14.4 1.0 %early_pairs.1 = (f32[512,512]{1,0:T(8,128)S(1)}, bf16[384,512]{1,0:T(8,128)(2,1)S(1)}, f32[384,512]{1,0:T(8,128)S(1)}) custom-call(f32[2,128]{1,0:T(2,128)S(1)} %get-tuple-element.24.params_ref, bf16[512,512]{1,0:T(8,128)(2,1)S(1)} %stack_units.1.text_ref, bf16[128,512]{1,0:T(8,128)(2,1)S(1)} %copy-done.2, ...), custom_call_target="tpu_custom_call" | custom-call | flops 603979776 | bytes 3146752 | tf_op jit(solution)/shard_map/early_pairs/pallas_call | solution.py:25
  15.5 2.4 %collective-permute-done.5.refs_0_ = bf16[128,512]{1,0:T(8,128)(2,1)S(1)} collective-permute-done((bf16[128,512]{1,0:T(8,128)(2,1)S(1)}, bf16[128,512]{1,0:T(8,128)(2,1)S(1)}, u32[]{:S(2)}, u32[]{:S(2)}) %collective-permute-start.5) | collective-permute-done | bytes 131104 | tf_op jit(solution)/shard_map/ppermute | solution.py:252
  17.9 1.0 %late_pairs.1 = (f32[512,512]{1,0:T(8,128)S(1)}, bf16[128,512]{1,0:T(8,128)(2,1)S(1)}, f32[128,512]{1,0:T(8,128)S(1)}) custom-call(f32[2,128]{1,0:T(2,128)S(1)} %get-tuple-element.24.params_ref, bf16[512,512]{1,0:T(8,128)(2,1)S(1)} %stack_units.1.text_ref, bf16[128,512]{1,0:T(8,128)(2,1)S(1)} %collective-permute-done.5.refs_0_), custom_call_target="tpu_custom_call" | custom-call | flops 8053063680 | bytes 2098176 | tf_op jit(solution)/shard_map/late_pairs/pallas_call | solution.py:25
  18.9 1.8 %other_pairs.1 = (bf16[512,512]{1,0:T(8,128)(2,1)S(1)}, f32[128,512]{1,0:T(8,128)S(1)}, bf16[128,512]{1,0:T(8,128)(2,1)S(1)}, bf16[128,512]{1,0:T(8,128)(2,1)S(1)}, bf16[128,512]{1,0:T(8,128)(2,1)S(1)}) custom-call(f32[2,128]{1,0:T(2,128)S(1)} %get-tuple-element.24.params_ref, bf16[384,512]{1,0:T(8,128)(2,1)S(1)} %get-tuple-element.26.refs_0_, ...), custom_call_target="tpu_custom_call" | custom-call | flops 805306368 | bytes 3277824 | tf_op jit(solution)/shard_map/other_pairs/pallas_call | solution.py:25
  20.8 0.5 %collective-permute-start.7 = (bf16[128,512]{1,0:T(8,128)(2,1)S(1)}, bf16[128,512]{1,0:T(8,128)(2,1)S(1)}, u32[]{:S(2)}, u32[]{:S(2)}) collective-permute-start(bf16[128,512]{1,0:T(8,128)(2,1)S(1)} %get-tuple-element.32), channel_id=1, source_target_pairs={{0,4},{1,5},{2,6},{3,7},{4,0},{5,1},{6,2},{7,3},{8,12},{9,13},{10,... | collective-permute-start | bytes 393224 | tf_op jit(solution)/shard_map/ppermute | solution.py:252
  21.3 2.5 %collective-permute-start.8 = (bf16[128,512]{1,0:T(8,128)(2,1)S(1)}, bf16[128,512]{1,0:T(8,128)(2,1)S(1)}, u32[]{:S(2)}, u32[]{:S(2)}) collective-permute-start(bf16[128,512]{1,0:T(8,128)(2,1)S(1)} %get-tuple-element.33), channel_id=1, source_target_pairs={{0,8},{1,9},{2,10},{3,11},{4,12},{5,13},{6,14},{7,15},{8,0},{9,1},... | collective-permute-start | bytes 393224 | tf_op jit(solution)/shard_map/ppermute | solution.py:252
  23.8 1.5 %collective-permute-start.9 = (bf16[128,512]{1,0:T(8,128)(2,1)S(1)}, bf16[128,512]{1,0:T(8,128)(2,1)S(1)}, u32[]{:S(2)}, u32[]{:S(2)}) collective-permute-start(bf16[128,512]{1,0:T(8,128)(2,1)S(1)} %get-tuple-element.34), channel_id=1, source_target_pairs={{0,12},{1,13},{2,14},{3,15},{4,8},{5,9},{6,10},{7,11},{8,4},{9,5},... | collective-permute-start | bytes 393224 | tf_op jit(solution)/shard_map/ppermute | solution.py:252
  25.4 1.6 %collective-permute-start.11 = (bf16[128,512]{1,0:T(8,128)(2,1)S(1)}, bf16[128,512]{1,0:T(8,128)(2,1)S(1)}, u32[]{:S(2)}, u32[]{:S(2)}) collective-permute-start(bf16[128,512]{1,0:T(8,128)(2,1)S(1)} %get-tuple-element.39), channel_id=1, source_target_pairs={{0,1},{1,0},{2,3},{3,2},{4,5},{5,4},{6,7},{7,6},{8,9},{9,8},{10,11... | collective-permute-start | bytes 393224 | tf_op jit(solution)/shard_map/ppermute | solution.py:252
  26.9 1.5 %collective-permute-start.12 = (bf16[128,512]{1,0:T(8,128)(2,1)S(1)}, bf16[128,512]{1,0:T(8,128)(2,1)S(1)}, u32[]{:S(2)}, u32[]{:S(2)}) collective-permute-start(bf16[128,512]{1,0:T(8,128)(2,1)S(1)} %get-tuple-element.40), channel_id=1, source_target_pairs={{0,2},{1,3},{2,0},{3,1},{4,6},{5,7},{6,4},{7,5},{8,10},{9,11},{10,... | collective-permute-start | bytes 393224 | tf_op jit(solution)/shard_map/ppermute | solution.py:252
  28.5 0.5 %collective-permute-done.7.refs_1_ = bf16[128,512]{1,0:T(8,128)(2,1)S(1)} collective-permute-done((bf16[128,512]{1,0:T(8,128)(2,1)S(1)}, bf16[128,512]{1,0:T(8,128)(2,1)S(1)}, u32[]{:S(2)}, u32[]{:S(2)}) %collective-permute-start.7) | collective-permute-done | bytes 131104 | tf_op jit(solution)/shard_map/ppermute | solution.py:252
  28.9 2.4 %collective-permute-start.13 = (bf16[128,512]{1,0:T(8,128)(2,1)S(1)}, bf16[128,512]{1,0:T(8,128)(2,1)S(1)}, u32[]{:S(2)}, u32[]{:S(2)}) collective-permute-start(bf16[128,512]{1,0:T(8,128)(2,1)S(1)} %get-tuple-element.41), channel_id=1, source_target_pairs={{0,3},{1,2},{2,1},{3,0},{4,7},{5,6},{6,5},{7,4},{8,11},{9,10},{10,... | collective-permute-start | bytes 393224 | tf_op jit(solution)/shard_map/ppermute | solution.py:252
  31.4 2.8 %collective-permute-done.8.refs_2_ = bf16[128,512]{1,0:T(8,128)(2,1)S(1)} collective-permute-done((bf16[128,512]{1,0:T(8,128)(2,1)S(1)}, bf16[128,512]{1,0:T(8,128)(2,1)S(1)}, u32[]{:S(2)}, u32[]{:S(2)}) %collective-permute-start.8) | collective-permute-done | bytes 131104 | tf_op jit(solution)/shard_map/ppermute | solution.py:252
  34.2 0.7 %collective-permute-done.13.refs_7_ = bf16[128,512]{1,0:T(8,128)(2,1)S(1)} collective-permute-done((bf16[128,512]{1,0:T(8,128)(2,1)S(1)}, bf16[128,512]{1,0:T(8,128)(2,1)S(1)}, u32[]{:S(2)}, u32[]{:S(2)}) %collective-permute-start.13) | collective-permute-done | bytes 131104 | tf_op jit(solution)/shard_map/ppermute | solution.py:252
  34.9 1.0 %finish.1 = (f32[128,512]{1,0:T(8,128)}, f32[128,512]{1,0:T(8,128)}) custom-call(bf16[128,512]{1,0:T(8,128)(2,1)S(1)} %copy-done.2, bf16[128,512]{1,0:T(8,128)(2,1)S(1)} %copy-done.1, f32[128,512]{1,0:T(8,128)S(1)} %get-tuple-element.31.refs_0_, bf16[128,512]{1,0:T(8,128)(2,1)S(1)} %collective-permute-done.7.refs_1_, ...), custom_call_target="tpu_custom_call" | custom-call | flops 5242880 | bytes 2097152 | tf_op jit(solution)/shard_map/finish/pallas_call | solution.py:25
  (17 shorter events, 0.3 us)
Async XLA Ops:
  0.6 12.2 %collective-permute-start = (bf16[128,512]{1,0:T(8,128)(2,1)}, bf16[128,512]{1,0:T(8,128)(2,1)S(1)}, u32[]{:S(2)}, u32[]{:S(2)}) collective-permute-start(bf16[128,512]{1,0:T(8,128)(2,1)} %image_ref.1), channel_id=1, source_target_pairs={{0,8},{1,9},{2,10},{3,11},{4,12},{5,13},{6,14},{7,15},{8,0},{9,1},... | collective-permute-start | bytes 393224 | tf_op jit(solution)/shard_map/ppermute | solution.py:252
  4.7 8.6 %collective-permute-start.2 = (bf16[128,512]{1,0:T(8,128)(2,1)}, bf16[128,512]{1,0:T(8,128)(2,1)S(1)}, u32[]{:S(2)}, u32[]{:S(2)}) collective-permute-start(bf16[128,512]{1,0:T(8,128)(2,1)} %text_ref.3), channel_id=1, source_target_pairs={{0,2},{1,3},{2,0},{3,1},{4,6},{5,7},{6,4},{7,5},{8,10},{9,11},{10,... | collective-permute-start | bytes 393224 | tf_op jit(solution)/shard_map/ppermute | solution.py:252
  6.3 7.1 %collective-permute-start.1 = (bf16[128,512]{1,0:T(8,128)(2,1)}, bf16[128,512]{1,0:T(8,128)(2,1)S(1)}, u32[]{:S(2)}, u32[]{:S(2)}) collective-permute-start(bf16[128,512]{1,0:T(8,128)(2,1)} %text_ref.3), channel_id=1, source_target_pairs={{0,1},{1,0},{2,3},{3,2},{4,5},{5,4},{6,7},{7,6},{8,9},{9,8},{10,11... | collective-permute-start | bytes 393224 | tf_op jit(solution)/shard_map/ppermute | solution.py:252
  7.7 6.4 %collective-permute-start.3 = (bf16[128,512]{1,0:T(8,128)(2,1)}, bf16[128,512]{1,0:T(8,128)(2,1)S(1)}, u32[]{:S(2)}, u32[]{:S(2)}) collective-permute-start(bf16[128,512]{1,0:T(8,128)(2,1)} %text_ref.3), channel_id=1, source_target_pairs={{0,3},{1,2},{2,1},{3,0},{4,7},{5,6},{6,5},{7,4},{8,11},{9,10},{10,... | collective-permute-start | bytes 393224 | tf_op jit(solution)/shard_map/ppermute | solution.py:252
  8.2 6.2 %collective-permute-start.4 = (bf16[128,512]{1,0:T(8,128)(2,1)}, bf16[128,512]{1,0:T(8,128)(2,1)S(1)}, u32[]{:S(2)}, u32[]{:S(2)}) collective-permute-start(bf16[128,512]{1,0:T(8,128)(2,1)} %image_ref.1), channel_id=1, source_target_pairs={{0,4},{1,5},{2,6},{3,7},{4,0},{5,1},{6,2},{7,3},{8,12},{9,13},{10,... | collective-permute-start | bytes 393224 | tf_op jit(solution)/shard_map/ppermute | solution.py:252
  11.1 0.9 %copy-start = (bf16[128,512]{1,0:T(8,128)(2,1)S(1)}, bf16[128,512]{1,0:T(8,128)(2,1)}, u32[]{:S(2)}) copy-start(bf16[128,512]{1,0:T(8,128)(2,1)} %text_ref.3) | copy-start | bytes 393220
  12.8 1.6 %copy-start.2 = (bf16[128,512]{1,0:T(8,128)(2,1)S(1)}, bf16[128,512]{1,0:T(8,128)(2,1)}, u32[]{:S(2)}) copy-start(bf16[128,512]{1,0:T(8,128)(2,1)} %image_ref.1) | copy-start | bytes 393220
  12.9 5.0 %collective-permute-start.5 = (bf16[128,512]{1,0:T(8,128)(2,1)S(1)}, bf16[128,512]{1,0:T(8,128)(2,1)S(1)}, u32[]{:S(2)}, u32[]{:S(2)}) collective-permute-start(bf16[128,512]{1,0:T(8,128)(2,1)S(1)} %collective-permute-done.refs_1_), channel_id=1, source_target_pairs={{0,4},{1,5},{2,6},{3,7},{4,0},{5,1},{6,2},{7,3},{8,12},{9,13},{10,... | collective-permute-start | bytes 393224 | tf_op jit(solution)/shard_map/ppermute | solution.py:252
  14.3 4.6 %collective-permute-start.6 = (bf16[512,512]{1,0:T(8,128)(2,1)S(1)}, bf16[512,512]{1,0:T(8,128)(2,1)S(1)}, u32[]{:S(2)}, u32[]{:S(2)}) collective-permute-start(bf16[512,512]{1,0:T(8,128)(2,1)S(1)} %stack_units.1.text_ref), channel_id=1, source_target_pairs={{0,16},{1,17},{2,18},{3,19},{4,20},{5,21},{6,22},{7,23},{8,24},{9,... | collective-permute-start | bytes 1572872 | tf_op jit(solution)/shard_map/ppermute | solution.py:252
  20.7 4.5 %collective-permute-start.10 = (bf16[512,512]{1,0:T(8,128)(2,1)S(1)}, bf16[512,512]{1,0:T(8,128)(2,1)S(1)}, u32[]{:S(2)}, u32[]{:S(2)}) collective-permute-start(bf16[512,512]{1,0:T(8,128)(2,1)S(1)} %get-tuple-element.37), channel_id=1, source_target_pairs={{0,16},{1,17},{2,18},{3,19},{4,20},{5,21},{6,22},{7,23},{8,24},{9,... | collective-permute-start | bytes 1572872 | tf_op jit(solution)/shard_map/ppermute | solution.py:252
  20.8 8.1 %collective-permute-start.7 = (bf16[128,512]{1,0:T(8,128)(2,1)S(1)}, bf16[128,512]{1,0:T(8,128)(2,1)S(1)}, u32[]{:S(2)}, u32[]{:S(2)}) collective-permute-start(bf16[128,512]{1,0:T(8,128)(2,1)S(1)} %get-tuple-element.32), channel_id=1, source_target_pairs={{0,4},{1,5},{2,6},{3,7},{4,0},{5,1},{6,2},{7,3},{8,12},{9,13},{10,... | collective-permute-start | bytes 393224 | tf_op jit(solution)/shard_map/ppermute | solution.py:252
  21.3 12.9 %collective-permute-start.8 = (bf16[128,512]{1,0:T(8,128)(2,1)S(1)}, bf16[128,512]{1,0:T(8,128)(2,1)S(1)}, u32[]{:S(2)}, u32[]{:S(2)}) collective-permute-start(bf16[128,512]{1,0:T(8,128)(2,1)S(1)} %get-tuple-element.33), channel_id=1, source_target_pairs={{0,8},{1,9},{2,10},{3,11},{4,12},{5,13},{6,14},{7,15},{8,0},{9,1},... | collective-permute-start | bytes 393224 | tf_op jit(solution)/shard_map/ppermute | solution.py:252
  23.8 10.4 %collective-permute-start.9 = (bf16[128,512]{1,0:T(8,128)(2,1)S(1)}, bf16[128,512]{1,0:T(8,128)(2,1)S(1)}, u32[]{:S(2)}, u32[]{:S(2)}) collective-permute-start(bf16[128,512]{1,0:T(8,128)(2,1)S(1)} %get-tuple-element.34), channel_id=1, source_target_pairs={{0,12},{1,13},{2,14},{3,15},{4,8},{5,9},{6,10},{7,11},{8,4},{9,5},... | collective-permute-start | bytes 393224 | tf_op jit(solution)/shard_map/ppermute | solution.py:252
  25.2 9.6 %copy-start.1 = (bf16[128,512]{1,0:T(8,128)(2,1)S(1)}, bf16[128,512]{1,0:T(8,128)(2,1)}, u32[]{:S(2)}) copy-start(bf16[128,512]{1,0:T(8,128)(2,1)} %text_ref.3) | copy-start | bytes 393220
  25.4 8.8 %collective-permute-start.11 = (bf16[128,512]{1,0:T(8,128)(2,1)S(1)}, bf16[128,512]{1,0:T(8,128)(2,1)S(1)}, u32[]{:S(2)}, u32[]{:S(2)}) collective-permute-start(bf16[128,512]{1,0:T(8,128)(2,1)S(1)} %get-tuple-element.39), channel_id=1, source_target_pairs={{0,1},{1,0},{2,3},{3,2},{4,5},{5,4},{6,7},{7,6},{8,9},{9,8},{10,11... | collective-permute-start | bytes 393224 | tf_op jit(solution)/shard_map/ppermute | solution.py:252
  26.9 7.3 %collective-permute-start.12 = (bf16[128,512]{1,0:T(8,128)(2,1)S(1)}, bf16[128,512]{1,0:T(8,128)(2,1)S(1)}, u32[]{:S(2)}, u32[]{:S(2)}) collective-permute-start(bf16[128,512]{1,0:T(8,128)(2,1)S(1)} %get-tuple-element.40), channel_id=1, source_target_pairs={{0,2},{1,3},{2,0},{3,1},{4,6},{5,7},{6,4},{7,5},{8,10},{9,11},{10,... | collective-permute-start | bytes 393224 | tf_op jit(solution)/shard_map/ppermute | solution.py:252
  28.9 6.0 %collective-permute-start.13 = (bf16[128,512]{1,0:T(8,128)(2,1)S(1)}, bf16[128,512]{1,0:T(8,128)(2,1)S(1)}, u32[]{:S(2)}, u32[]{:S(2)}) collective-permute-start(bf16[128,512]{1,0:T(8,128)(2,1)S(1)} %get-tuple-element.41), channel_id=1, source_target_pairs={{0,3},{1,2},{2,1},{3,0},{4,7},{5,6},{6,5},{7,4},{8,11},{9,10},{10,... | collective-permute-start | bytes 393224 | tf_op jit(solution)/shard_map/ppermute | solution.py:252

commit v7 on v6

v7 whole, which is shorter than its diff:
```python
import functools
import math

import jax
import jax.numpy as jnp
from jax import lax
from jax.experimental import pallas as pl
from jax.experimental.pallas import tpu as pltpu
from jax.sharding import PartitionSpec as P

AXES = ("grp", "dev")
VMEM_LIMIT = 32 * 1024 * 1024
SPAN = 256
LATE = 30000
LOG2_E = math.log2(math.e)
VMEM = pl.BlockSpec(memory_space=pltpu.VMEM)


def unit_rows(raw):
    wide = raw.astype(jnp.float32)
    factor = lax.rsqrt(jnp.sum(wide * wide, axis=-1, keepdims=True) + 1e-06)
    return wide * factor, factor


def call(kernel, out_shape, operands, scratch=(), flops=0, transcendentals=0, name=None):
    touched = sum(x.size * x.dtype.itemsize for x in list(operands) + list(out_shape))
    outs = pl.pallas_call(
        kernel,
        out_shape=out_shape,
        in_specs=[VMEM] * len(operands),
        out_specs=[VMEM] * len(out_shape),
        scratch_shapes=scratch,
        compiler_params=pltpu.CompilerParams(vmem_limit_bytes=VMEM_LIMIT),
        cost_estimate=pl.CostEstimate(
            flops=flops, bytes_accessed=touched, transcendentals=transcendentals
        ),
        name=name,
    )(*operands)
    return tuple(outs)


def units_kernel(*refs):
    rows = refs[0].shape[0]
    for at, ref in enumerate(refs[:-1]):
        refs[-1][at * rows:(at + 1) * rows, :] = unit_rows(ref[...])[0].astype(refs[-1].dtype)


def units(blocks, name, weight=1):
    rows, width = blocks[0].shape
    out = jax.ShapeDtypeStruct((len(blocks) * rows, width), jnp.bfloat16)
    return call(units_kernel, [out], blocks, flops=4 * weight * out.size, name=name)[0]


def stack_units_kernel(*refs):
    out = refs[-1]
    rows = refs[0].shape[0]
    out[:rows, :] = refs[0][...]
    for at, ref in enumerate(refs[1:-1], 1):
        out[at * rows:(at + 1) * rows, :] = unit_rows(ref[...])[0].astype(out.dtype)


def stack_units(blocks):
    rows, width = blocks[0].shape
    out = jax.ShapeDtypeStruct((len(blocks) * rows, width), jnp.bfloat16)
    return call(stack_units_kernel, [out], blocks, flops=4 * out.size, name="stack_units")[0]


def pairs(vi, params_ref, text_ref, text_out, own=0, text_add=None):
    slope, shift, temper = (params_ref[0:1, at:at + 1] for at in range(3))
    held = text_ref.shape[0]
    total = None
    for first in range(0, held, SPAN):
        last = min(first + SPAN, held)
        vt = text_ref[first:last, :]
        dots = lax.dot_general(
            vi, vt, (((1,), (1,)), ((), ())), preferred_element_type=jnp.float32
        )
        e = jnp.exp2(slope * dots + shift)
        chance = pl.reciprocal(1.0 + e, approx=True)
        if own and first == 0:
            row = lax.broadcasted_iota(jnp.int32, chance.shape, 0)
            column = lax.broadcasted_iota(jnp.int32, chance.shape, 1)
            same = (row == column) & (row < own)
            chance = jnp.where(same, -e * chance, chance)
        coefficient = (temper * chance).astype(jnp.bfloat16)
        text_part = lax.dot_general(
            coefficient, vi, (((0,), (0,)), ((), ())), preferred_element_type=jnp.float32
        )
        if text_add is not None:
            text_part = text_add[first:last, :] + text_part
        text_out[first:last, :] = text_part.astype(text_out.dtype)
        part = jnp.dot(coefficient, vt, preferred_element_type=jnp.float32)
        total = part if total is None else total + part
    return total


def early_pairs_kernel(params_ref, text_ref, *refs):
    image_refs, (text_out, units_out, total_out) = refs[:-3], refs[-3:]
    rows = image_refs[0].shape[0]
    for a, ref in enumerate(image_refs):
        units_out[a * rows:(a + 1) * rows, :] = unit_rows(ref[...])[0].astype(jnp.bfloat16)
    total_out[...] = pairs(units_out[...], params_ref, text_ref, text_out, own=rows)


def rest_pairs_kernel(
    count, params_ref, early_ref, total_ref, own_text_ref, own_add_ref, late_ref, *refs
):
    text_refs, own_out = refs[:count], refs[count]
    other_out, image_out = refs[count + 1:2 * count + 1], refs[2 * count + 1:]
    rows = image_out[0].shape[0]
    early, late = early_ref[...], late_ref[...]
    total = jnp.concatenate(
        [
            total_ref[...],
            pairs(late, params_ref, own_text_ref, own_out, text_add=own_add_ref),
        ],
        axis=0,
    )
    vi = jnp.concatenate([early, late], axis=0)
    for text_ref, out in zip(text_refs, other_out):
        total = total + pairs(vi, params_ref, text_ref, out)
    for a, ref in enumerate(image_out):
        ref[...] = total[a * rows:(a + 1) * rows, :].astype(ref.dtype)


def pair_terms(params, early, late, texts):
    rows, width = early[0].shape
    early_rows, late_rows = rows * len(early), rows * len(late)
    own, others = texts[0], texts[1:]
    other_rows = sum(t.shape[0] for t in others)

    def cost(pair_count):
        return dict(flops=6 * pair_count * width, transcendentals=2 * pair_count)

    own_add, early_units, total = call(
        early_pairs_kernel,
        [
            jax.ShapeDtypeStruct(own.shape, jnp.float32),
            jax.ShapeDtypeStruct((early_rows, width), jnp.bfloat16),
            jax.ShapeDtypeStruct((early_rows, width), jnp.float32),
        ],
        [params, own, *early],
        name="early_pairs",
        **cost(early_rows * own.shape[0]),
    )
    late_units = units(late, "late_units", LATE)
    outs = call(
        functools.partial(rest_pairs_kernel, len(others)),
        [jax.ShapeDtypeStruct(own.shape, jnp.float32)]
        + [jax.ShapeDtypeStruct(t.shape, jnp.bfloat16) for t in others]
        + [jax.ShapeDtypeStruct((rows, width), jnp.float32)]
        + [jax.ShapeDtypeStruct((rows, width), jnp.bfloat16)] * (len(early) + len(late) - 1),
        [params, early_units, total, own, own_add, late_units, *others],
        name="rest_pairs",
        **cost(late_rows * own.shape[0] + (early_rows + late_rows) * other_rows),
    )
    count = 1 + len(others)
    return outs[count:], outs[:count]


def add_stacks_kernel(part_count, *refs):
    parts, outs = refs[:part_count], refs[part_count:]
    rows = outs[0].shape[0]
    for at, out in enumerate(outs):
        total = parts[0][at * rows:(at + 1) * rows, :].astype(jnp.float32)
        for part in parts[1:]:
            total = total + part[at * rows:(at + 1) * rows, :].astype(jnp.float32)
        out[...] = total.astype(out.dtype)


def add_stacks(parts, count):
    shape = (parts[0].shape[0] // count, parts[0].shape[1])
    types = [jnp.float32] + [jnp.bfloat16] * (count - 1)
    return call(
        functools.partial(add_stacks_kernel, len(parts)),
        [jax.ShapeDtypeStruct(shape, t) for t in types],
        parts,
        flops=len(parts) * parts[0].size,
        name="add_stacks",
    )


def finish_kernel(sides, image_ref, text_ref, *refs):
    parts, outs = refs[:len(sides)], refs[len(sides):len(sides) + 2]
    staged, sems = refs[len(sides) + 2:]
    copies = []
    for side, raw in enumerate((image_ref, text_ref)):
        unit, factor = unit_rows(raw[...])
        total = sum(ref[...].astype(jnp.float32) for at, ref in zip(sides, parts) if at == side)
        along = jnp.sum(unit * total, axis=-1, keepdims=True)
        staged[side] = factor * (total - unit * along)
        copies.append(pltpu.make_async_copy(staged.at[side], outs[side], sems.at[side]))
        copies[-1].start()
    for copy in copies:
        copy.wait()


def finish(images, texts, parts):
    out = jax.ShapeDtypeStruct(images.shape, jnp.float32)
    return pl.pallas_call(
        functools.partial(finish_kernel, [side for side, _ in parts]),
        out_shape=(out, out),
        in_specs=[VMEM] * (2 + len(parts)),
        out_specs=[pl.BlockSpec(memory_space=pl.ANY)] * 2,
        scratch_shapes=[
            pltpu.VMEM((2,) + images.shape, jnp.float32),
            pltpu.SemaphoreType.DMA((2,)),
        ],
        compiler_params=pltpu.CompilerParams(vmem_limit_bytes=VMEM_LIMIT),
        cost_estimate=pl.CostEstimate(
            flops=10 * len(parts) * images.size,
            bytes_accessed=3 * len(parts) * images.size,
            transcendentals=0,
        ),
        name="finish",
    )(images, texts, *[part for _, part in parts])


def plan(grp_count, dev_count):
    options = [n for n in range(1, dev_count + 1) if dev_count % n == 0]
    near = min(options, key=lambda n: (dev_count // n + grp_count * n, -n))
    return dev_count // near, near


def step_to(at, by, count):
    if count & (count - 1) == 0:
        return at ^ abs(by)
    return (at + by) % count


def solution(mesh):
    grp_count, dev_count = mesh.shape["grp"], mesh.shape["dev"]
    far_count, near_count = plan(grp_count, dev_count)
    low_count = 2 if far_count % 2 == 0 else 1
    high_count = far_count // low_count

    def move(value, grp=0, high=0, low=0, near=0):
        perm = []
        for g in range(grp_count):
            for h in range(high_count):
                for w in range(low_count):
                    for n in range(near_count):
                        source = ((g * high_count + h) * low_count + w) * near_count + n
                        g2 = step_to(g, grp, grp_count)
                        h2 = step_to(h, high, high_count)
                        w2 = step_to(w, low, low_count)
                        n2 = step_to(n, near, near_count)
                        target = ((g2 * high_count + h2) * low_count + w2) * near_count + n2
                        perm.append((source, target))
        return lax.ppermute(value, AXES, perm)

    def on_device(images, texts, logit_scale, logit_bias):
        params = jnp.concatenate(
            [logit_scale * -LOG2_E, logit_bias * -LOG2_E, logit_scale]
        ).reshape(1, 3)
        early = {(0, 0): images}
        for h in range(1, high_count):
            early[h, 0] = move(images, high=h)
        for w in range(1, low_count):
            early[0, w] = move(images, low=w)
        late = {}
        for h in range(1, high_count):
            block, params = lax.optimization_barrier((early[h, 0], params))
            for w in range(1, low_count):
                late[h, w] = move(block, low=w)
        near_rows = [units([texts], "own_units")] + [move(texts, near=n) for n in range(1, near_count)]
        own_stack = stack_units(near_rows)
        stacks = [own_stack] + [move(own_stack, grp=g) for g in range(1, grp_count)]
        image_parts, text_parts = pair_terms(
            params, list(early.values()), list(late.values()), stacks
        )
        far_parts = dict(zip([*early, *late], image_parts))
        came = [move(part, grp=-g) for g, part in enumerate(text_parts) if g]
        low_parts = [move(p, low=-w) for (h, w), p in far_parts.items() if w and not h]
        high_parts = [move(p, high=-h, low=-w) for (h, w), p in far_parts.items() if h]
        near_parts = add_stacks([text_parts[0], *came], near_count)
        near_parts = [near_parts[0]] + [
            move(part, near=-n) for n, part in enumerate(near_parts) if n
        ]
        return finish(
            images,
            texts,
            [(0, part) for part in [far_parts[0, 0]] + low_parts + high_parts]
            + [(1, part) for part in near_parts],
        )

    in_specs = (P(AXES, None), P(AXES, None), P(), P())
    out_specs = (P(AXES, None), P(AXES, None))
    return jax.shard_map(
        on_device, mesh=mesh, in_specs=in_specs, out_specs=out_specs, check_vma=False
    )
```

time: 36.1 us -> 35.4 us (0.981)
  Pallas kernels: 5.98 us -> 4.8 us
  waiting for transfers between devices: 7.18 us -> 8.21 us
  starting transfers between devices: 19.8 us -> 19.2 us
    pallas_call x6, Pallas kernels: 5.16 us -> 3.76 us  [call(): pl.pallas_call(kernel, out_shape=out_shape, in_specs=[VMEM] * len(operand...]
    ppermute x14, waiting for transfers between devices: 7.18 us -> 8.21 us  [move(): return lax.ppermute(value, AXES, perm)]
    ppermute x14, starting transfers between devices: 19.8 us -> 19.2 us  [move(): return lax.ppermute(value, AXES, perm)]
  transfers between devices with their start and end apart: 14 -> 14, of which waited for: 5 -> 7; matrix products, arithmetic and copies ran while one was open for 0% -> 0% of each run, Pallas kernels for 9% -> 4%
where the time goes in v7:
time: 35.4 us; the launch traced here: 35.2 us
  starting transfers between devices  19.2 us (54%)
  waiting for transfers between devices  8.21 us (23%)
  Pallas kernels  4.8 us (14%)
  between operations  2.01 us (6%)
  local copies, waits for them, and re-layouts  0.91 us (3%)
    ppermute x14, starting transfers between devices, move(): return lax.ppermute(value, AXES, perm)  19.2 us
    ppermute x14, waiting for transfers between devices, move(): return lax.ppermute(value, AXES, perm)  8.21 us
    pallas_call x6, Pallas kernels, call(): pl.pallas_call(kernel, out_shape=out_shape, in_specs=[VMEM] * len(operand...  3.76 us
    pallas_call x1, Pallas kernels, finish(): pl.pallas_call(functools.partial(finish_kernel, [side for side, _ in part...  1.04 us
    unnamed x6, local copies, waits for them, and re-layouts  0.91 us
  transfers between devices with their start and end apart: 14, of which 7 were waited for; matrix products, arithmetic and copies ran while one was open for 0% of the time, Pallas kernels for 4%

profile of v7, /device:TPU:0, one launch (start us, length us, event | category | flops | bytes accessed | tf_op | source)
XLA Modules:
  0.0 35.2 jit_solution(5076211506999447591)
XLA Ops:
  0.6 4.1 %collective-permute-start = (bf16[128,512]{1,0:T(8,128)(2,1)}, bf16[128,512]{1,0:T(8,128)(2,1)S(1)}, u32[]{:S(2)}, u32[]{:S(2)}) collective-permute-start(bf16[128,512]{1,0:T(8,128)(2,1)} %image_ref.1), channel_id=1, source_target_pairs={{0,8},{1,9},{2,10},{3,11},{4,12},{5,13},{6,14},{7,15},{8,0},{9,1},... | collective-permute-start | bytes 393224 | tf_op jit(solution)/shard_map/ppermute | solution.py:250
  4.7 1.6 %collective-permute-start.4 = (bf16[128,512]{1,0:T(8,128)(2,1)}, bf16[128,512]{1,0:T(8,128)(2,1)S(1)}, u32[]{:S(2)}, u32[]{:S(2)}) collective-permute-start(bf16[128,512]{1,0:T(8,128)(2,1)} %image_ref.1), channel_id=1, source_target_pairs={{0,4},{1,5},{2,6},{3,7},{4,0},{5,1},{6,2},{7,3},{8,12},{9,13},{10,... | collective-permute-start | bytes 393224 | tf_op jit(solution)/shard_map/ppermute | solution.py:250
  6.3 1.5 %collective-permute-start.2 = (bf16[128,512]{1,0:T(8,128)(2,1)}, bf16[128,512]{1,0:T(8,128)(2,1)S(1)}, u32[]{:S(2)}, u32[]{:S(2)}) collective-permute-start(bf16[128,512]{1,0:T(8,128)(2,1)} %text_ref.1), channel_id=1, source_target_pairs={{0,2},{1,3},{2,0},{3,1},{4,6},{5,7},{6,4},{7,5},{8,10},{9,11},{10,... | collective-permute-start | bytes 393224 | tf_op jit(solution)/shard_map/ppermute | solution.py:250
  7.8 1.5 %collective-permute-start.1 = (bf16[128,512]{1,0:T(8,128)(2,1)}, bf16[128,512]{1,0:T(8,128)(2,1)S(1)}, u32[]{:S(2)}, u32[]{:S(2)}) collective-permute-start(bf16[128,512]{1,0:T(8,128)(2,1)} %text_ref.1), channel_id=1, source_target_pairs={{0,1},{1,0},{2,3},{3,2},{4,5},{5,4},{6,7},{7,6},{8,9},{9,8},{10,11... | collective-permute-start | bytes 393224 | tf_op jit(solution)/shard_map/ppermute | solution.py:250
  9.3 0.5 %collective-permute-start.3 = (bf16[128,512]{1,0:T(8,128)(2,1)}, bf16[128,512]{1,0:T(8,128)(2,1)S(1)}, u32[]{:S(2)}, u32[]{:S(2)}) collective-permute-start(bf16[128,512]{1,0:T(8,128)(2,1)} %text_ref.1), channel_id=1, source_target_pairs={{0,3},{1,2},{2,1},{3,0},{4,7},{5,6},{6,5},{7,4},{8,11},{9,10},{10,... | collective-permute-start | bytes 393224 | tf_op jit(solution)/shard_map/ppermute | solution.py:250
  11.2 0.2 collective-permute-done.refs_1_
  11.4 0.7 %collective-permute-start.5 = (bf16[128,512]{1,0:T(8,128)(2,1)S(1)}, bf16[128,512]{1,0:T(8,128)(2,1)S(1)}, u32[]{:S(2)}, u32[]{:S(2)}) collective-permute-start(bf16[128,512]{1,0:T(8,128)(2,1)S(1)} %collective-permute-done.refs_1_), channel_id=1, source_target_pairs={{0,4},{1,5},{2,6},{3,7},{4,0},{5,1},{6,2},{7,3},{8,12},{9,13},{10,... | collective-permute-start | bytes 393224 | tf_op jit(solution)/shard_map/ppermute | solution.py:250
  12.1 0.9 %copy-done = bf16[128,512]{1,0:T(8,128)(2,1)S(1)} copy-done((bf16[128,512]{1,0:T(8,128)(2,1)S(1)}, bf16[128,512]{1,0:T(8,128)(2,1)}, u32[]{:S(2)}) %copy-start) | copy-done | bytes 131096
  13.1 0.7 %collective-permute-done.1.refs_1_ = bf16[128,512]{1,0:T(8,128)(2,1)S(1)} collective-permute-done((bf16[128,512]{1,0:T(8,128)(2,1)}, bf16[128,512]{1,0:T(8,128)(2,1)S(1)}, u32[]{:S(2)}, u32[]{:S(2)}) %collective-permute-start.1) | collective-permute-done | bytes 131104 | tf_op jit(solution)/shard_map/ppermute | solution.py:250
  13.8 1.9 %collective-permute-done.3.refs_3_ = bf16[128,512]{1,0:T(8,128)(2,1)S(1)} collective-permute-done((bf16[128,512]{1,0:T(8,128)(2,1)}, bf16[128,512]{1,0:T(8,128)(2,1)S(1)}, u32[]{:S(2)}, u32[]{:S(2)}) %collective-permute-start.3) | collective-permute-done | bytes 131104 | tf_op jit(solution)/shard_map/ppermute | solution.py:250
  16.0 1.1 %early_pairs.1 = (f32[512,512]{1,0:T(8,128)S(1)}, bf16[384,512]{1,0:T(8,128)(2,1)S(1)}, f32[384,512]{1,0:T(8,128)S(1)}) custom-call(f32[1,3]{1,0:T(1,128)S(1)} %maximum_bitcast_fusion.params_ref, bf16[512,512]{1,0:T(8,128)(2,1)S(1)} %stack_units.1.text_ref.own_text_ref, bf16[128,512]{1,0:T(8,128)(2,1)S(1)} %copy-done.2, ...), custom_call_target="tpu_custom_call" | custom-call | flops 603979776 | bytes 3145740 | tf_op jit(solution)/shard_map/early_pairs/pallas_call | solution.py:27
  17.2 0.7 %collective-permute-done.6.refs_0_ = bf16[512,512]{1,0:T(8,128)(2,1)S(1)} collective-permute-done((bf16[512,512]{1,0:T(8,128)(2,1)S(1)}, bf16[512,512]{1,0:T(8,128)(2,1)S(1)}, u32[]{:S(2)}, u32[]{:S(2)}) %collective-permute-start.6) | collective-permute-done | bytes 524320 | tf_op jit(solution)/shard_map/ppermute | solution.py:250
  17.9 2.2 %rest_pairs.1 = (f32[512,512]{1,0:T(8,128)S(1)}, bf16[512,512]{1,0:T(8,128)(2,1)S(1)}, f32[128,512]{1,0:T(8,128)S(1)}, bf16[128,512]{1,0:T(8,128)(2,1)S(1)}, bf1...) custom-call(f32[1,3]{1,0:T(1,128)S(1)} %maximum_bitcast_fusion.params_ref, ...), custom_call_target="tpu_custom_call" | custom-call | flops 1006632960 | bytes 5636108 | tf_op jit(solution)/shard_map/rest_pairs/pallas_call | solution.py:27
  20.1 0.2 collective-permute-start.10
  20.3 0.5 %collective-permute-start.7 = (bf16[128,512]{1,0:T(8,128)(2,1)S(1)}, bf16[128,512]{1,0:T(8,128)(2,1)S(1)}, u32[]{:S(2)}, u32[]{:S(2)}) collective-permute-start(bf16[128,512]{1,0:T(8,128)(2,1)S(1)} %get-tuple-element.23), channel_id=1, source_target_pairs={{0,4},{1,5},{2,6},{3,7},{4,0},{5,1},{6,2},{7,3},{8,12},{9,13},{10,... | collective-permute-start | bytes 393224 | tf_op jit(solution)/shard_map/ppermute | solution.py:250
  20.8 2.5 %collective-permute-start.8 = (bf16[128,512]{1,0:T(8,128)(2,1)S(1)}, bf16[128,512]{1,0:T(8,128)(2,1)S(1)}, u32[]{:S(2)}, u32[]{:S(2)}) collective-permute-start(bf16[128,512]{1,0:T(8,128)(2,1)S(1)} %get-tuple-element.24), channel_id=1, source_target_pairs={{0,8},{1,9},{2,10},{3,11},{4,12},{5,13},{6,14},{7,15},{8,0},{9,1},... | collective-permute-start | bytes 393224 | tf_op jit(solution)/shard_map/ppermute | solution.py:250
  23.2 1.5 %collective-permute-start.9 = (bf16[128,512]{1,0:T(8,128)(2,1)S(1)}, bf16[128,512]{1,0:T(8,128)(2,1)S(1)}, u32[]{:S(2)}, u32[]{:S(2)}) collective-permute-start(bf16[128,512]{1,0:T(8,128)(2,1)S(1)} %get-tuple-element.25), channel_id=1, source_target_pairs={{0,12},{1,13},{2,14},{3,15},{4,8},{5,9},{6,10},{7,11},{8,4},{9,5},... | collective-permute-start | bytes 393224 | tf_op jit(solution)/shard_map/ppermute | solution.py:250
  24.8 1.0 %collective-permute-start.11 = (bf16[128,512]{1,0:T(8,128)(2,1)S(1)}, bf16[128,512]{1,0:T(8,128)(2,1)S(1)}, u32[]{:S(2)}, u32[]{:S(2)}) collective-permute-start(bf16[128,512]{1,0:T(8,128)(2,1)S(1)} %get-tuple-element.29), channel_id=1, source_target_pairs={{0,1},{1,0},{2,3},{3,2},{4,5},{5,4},{6,7},{7,6},{8,9},{9,8},{10,11... | collective-permute-start | bytes 393224 | tf_op jit(solution)/shard_map/ppermute | solution.py:250
  25.8 1.5 %collective-permute-start.12 = (bf16[128,512]{1,0:T(8,128)(2,1)S(1)}, bf16[128,512]{1,0:T(8,128)(2,1)S(1)}, u32[]{:S(2)}, u32[]{:S(2)}) collective-permute-start(bf16[128,512]{1,0:T(8,128)(2,1)S(1)} %get-tuple-element.30), channel_id=1, source_target_pairs={{0,2},{1,3},{2,0},{3,1},{4,6},{5,7},{6,4},{7,5},{8,10},{9,11},{10,... | collective-permute-start | bytes 393224 | tf_op jit(solution)/shard_map/ppermute | solution.py:250
  27.3 1.0 %collective-permute-done.7.refs_1_ = bf16[128,512]{1,0:T(8,128)(2,1)S(1)} collective-permute-done((bf16[128,512]{1,0:T(8,128)(2,1)S(1)}, bf16[128,512]{1,0:T(8,128)(2,1)S(1)}, u32[]{:S(2)}, u32[]{:S(2)}) %collective-permute-start.7) | collective-permute-done | bytes 131104 | tf_op jit(solution)/shard_map/ppermute | solution.py:250
  28.3 2.1 %collective-permute-start.13 = (bf16[128,512]{1,0:T(8,128)(2,1)S(1)}, bf16[128,512]{1,0:T(8,128)(2,1)S(1)}, u32[]{:S(2)}, u32[]{:S(2)}) collective-permute-start(bf16[128,512]{1,0:T(8,128)(2,1)S(1)} %get-tuple-element.31), channel_id=1, source_target_pairs={{0,3},{1,2},{2,1},{3,0},{4,7},{5,6},{6,5},{7,4},{8,11},{9,10},{10,... | collective-permute-start | bytes 393224 | tf_op jit(solution)/shard_map/ppermute | solution.py:250
  30.4 3.3 %collective-permute-done.8.refs_2_ = bf16[128,512]{1,0:T(8,128)(2,1)S(1)} collective-permute-done((bf16[128,512]{1,0:T(8,128)(2,1)S(1)}, bf16[128,512]{1,0:T(8,128)(2,1)S(1)}, u32[]{:S(2)}, u32[]{:S(2)}) %collective-permute-start.8) | collective-permute-done | bytes 131104 | tf_op jit(solution)/shard_map/ppermute | solution.py:250
  33.7 0.5 %collective-permute-done.13.refs_7_ = bf16[128,512]{1,0:T(8,128)(2,1)S(1)} collective-permute-done((bf16[128,512]{1,0:T(8,128)(2,1)S(1)}, bf16[128,512]{1,0:T(8,128)(2,1)S(1)}, u32[]{:S(2)}, u32[]{:S(2)}) %collective-permute-start.13) | collective-permute-done | bytes 131104 | tf_op jit(solution)/shard_map/ppermute | solution.py:250
  34.2 1.0 %finish.1 = (f32[128,512]{1,0:T(8,128)}, f32[128,512]{1,0:T(8,128)}) custom-call(bf16[128,512]{1,0:T(8,128)(2,1)S(1)} %copy-done.2, bf16[128,512]{1,0:T(8,128)(2,1)S(1)} %copy-done.1, f32[128,512]{1,0:T(8,128)S(1)} %get-tuple-element.22.refs_0_, bf16[128,512]{1,0:T(8,128)(2,1)S(1)} %collective-permute-done.7.refs_1_, ...), custom_call_target="tpu_custom_call" | custom-call | flops 5242880 | bytes 1572864 | tf_op jit(solution)/shard_map/finish/pallas_call | solution.py:200
  (18 shorter events, 0.7 us)
Async XLA Ops:
  0.6 10.7 %collective-permute-start = (bf16[128,512]{1,0:T(8,128)(2,1)}, bf16[128,512]{1,0:T(8,128)(2,1)S(1)}, u32[]{:S(2)}, u32[]{:S(2)}) collective-permute-start(bf16[128,512]{1,0:T(8,128)(2,1)} %image_ref.1), channel_id=1, source_target_pairs={{0,8},{1,9},{2,10},{3,11},{4,12},{5,13},{6,14},{7,15},{8,0},{9,1},... | collective-permute-start | bytes 393224 | tf_op jit(solution)/shard_map/ppermute | solution.py:250
  4.7 11.3 %collective-permute-start.4 = (bf16[128,512]{1,0:T(8,128)(2,1)}, bf16[128,512]{1,0:T(8,128)(2,1)S(1)}, u32[]{:S(2)}, u32[]{:S(2)}) collective-permute-start(bf16[128,512]{1,0:T(8,128)(2,1)} %image_ref.1), channel_id=1, source_target_pairs={{0,4},{1,5},{2,6},{3,7},{4,0},{5,1},{6,2},{7,3},{8,12},{9,13},{10,... | collective-permute-start | bytes 393224 | tf_op jit(solution)/shard_map/ppermute | solution.py:250
  6.3 6.8 %collective-permute-start.2 = (bf16[128,512]{1,0:T(8,128)(2,1)}, bf16[128,512]{1,0:T(8,128)(2,1)S(1)}, u32[]{:S(2)}, u32[]{:S(2)}) collective-permute-start(bf16[128,512]{1,0:T(8,128)(2,1)} %text_ref.1), channel_id=1, source_target_pairs={{0,2},{1,3},{2,0},{3,1},{4,6},{5,7},{6,4},{7,5},{8,10},{9,11},{10,... | collective-permute-start | bytes 393224 | tf_op jit(solution)/shard_map/ppermute | solution.py:250
  7.8 6.0 %collective-permute-start.1 = (bf16[128,512]{1,0:T(8,128)(2,1)}, bf16[128,512]{1,0:T(8,128)(2,1)S(1)}, u32[]{:S(2)}, u32[]{:S(2)}) collective-permute-start(bf16[128,512]{1,0:T(8,128)(2,1)} %text_ref.1), channel_id=1, source_target_pairs={{0,1},{1,0},{2,3},{3,2},{4,5},{5,4},{6,7},{7,6},{8,9},{9,8},{10,11... | collective-permute-start | bytes 393224 | tf_op jit(solution)/shard_map/ppermute | solution.py:250
  9.3 6.4 %collective-permute-start.3 = (bf16[128,512]{1,0:T(8,128)(2,1)}, bf16[128,512]{1,0:T(8,128)(2,1)S(1)}, u32[]{:S(2)}, u32[]{:S(2)}) collective-permute-start(bf16[128,512]{1,0:T(8,128)(2,1)} %text_ref.1), channel_id=1, source_target_pairs={{0,3},{1,2},{2,1},{3,0},{4,7},{5,6},{6,5},{7,4},{8,11},{9,10},{10,... | collective-permute-start | bytes 393224 | tf_op jit(solution)/shard_map/ppermute | solution.py:250
  11.4 5.7 %collective-permute-start.5 = (bf16[128,512]{1,0:T(8,128)(2,1)S(1)}, bf16[128,512]{1,0:T(8,128)(2,1)S(1)}, u32[]{:S(2)}, u32[]{:S(2)}) collective-permute-start(bf16[128,512]{1,0:T(8,128)(2,1)S(1)} %collective-permute-done.refs_1_), channel_id=1, source_target_pairs={{0,4},{1,5},{2,6},{3,7},{4,0},{5,1},{6,2},{7,3},{8,12},{9,13},{10,... | collective-permute-start | bytes 393224 | tf_op jit(solution)/shard_map/ppermute | solution.py:250
  12.1 0.9 %copy-start = (bf16[128,512]{1,0:T(8,128)(2,1)S(1)}, bf16[128,512]{1,0:T(8,128)(2,1)}, u32[]{:S(2)}) copy-start(bf16[128,512]{1,0:T(8,128)(2,1)} %text_ref.1) | copy-start | bytes 393220
  13.1 2.9 %copy-start.2 = (bf16[128,512]{1,0:T(8,128)(2,1)S(1)}, bf16[128,512]{1,0:T(8,128)(2,1)}, u32[]{:S(2)}) copy-start(bf16[128,512]{1,0:T(8,128)(2,1)} %image_ref.1) | copy-start | bytes 393220
  15.9 2.0 %collective-permute-start.6 = (bf16[512,512]{1,0:T(8,128)(2,1)S(1)}, bf16[512,512]{1,0:T(8,128)(2,1)S(1)}, u32[]{:S(2)}, u32[]{:S(2)}) collective-permute-start(bf16[512,512]{1,0:T(8,128)(2,1)S(1)} %stack_units.1.text_ref.own_text_ref), channel_id=1, source_target_pairs={{0,16},{1,17},{2,18},{3,19},{4,20},{5,21},{6,22},{7,23},{8,24},{9,... | collective-permute-start | bytes 1572872 | tf_op jit(solution)/shard_map/ppermute | solution.py:250
  20.1 4.6 %collective-permute-start.10 = (bf16[512,512]{1,0:T(8,128)(2,1)S(1)}, bf16[512,512]{1,0:T(8,128)(2,1)S(1)}, u32[]{:S(2)}, u32[]{:S(2)}) collective-permute-start(bf16[512,512]{1,0:T(8,128)(2,1)S(1)} %get-tuple-element.27), channel_id=1, source_target_pairs={{0,16},{1,17},{2,18},{3,19},{4,20},{5,21},{6,22},{7,23},{8,24},{9,... | collective-permute-start | bytes 1572872 | tf_op jit(solution)/shard_map/ppermute | solution.py:250
  20.3 8.0 %collective-permute-start.7 = (bf16[128,512]{1,0:T(8,128)(2,1)S(1)}, bf16[128,512]{1,0:T(8,128)(2,1)S(1)}, u32[]{:S(2)}, u32[]{:S(2)}) collective-permute-start(bf16[128,512]{1,0:T(8,128)(2,1)S(1)} %get-tuple-element.23), channel_id=1, source_target_pairs={{0,4},{1,5},{2,6},{3,7},{4,0},{5,1},{6,2},{7,3},{8,12},{9,13},{10,... | collective-permute-start | bytes 393224 | tf_op jit(solution)/shard_map/ppermute | solution.py:250
  20.8 12.9 %collective-permute-start.8 = (bf16[128,512]{1,0:T(8,128)(2,1)S(1)}, bf16[128,512]{1,0:T(8,128)(2,1)S(1)}, u32[]{:S(2)}, u32[]{:S(2)}) collective-permute-start(bf16[128,512]{1,0:T(8,128)(2,1)S(1)} %get-tuple-element.24), channel_id=1, source_target_pairs={{0,8},{1,9},{2,10},{3,11},{4,12},{5,13},{6,14},{7,15},{8,0},{9,1},... | collective-permute-start | bytes 393224 | tf_op jit(solution)/shard_map/ppermute | solution.py:250
  23.2 10.4 %collective-permute-start.9 = (bf16[128,512]{1,0:T(8,128)(2,1)S(1)}, bf16[128,512]{1,0:T(8,128)(2,1)S(1)}, u32[]{:S(2)}, u32[]{:S(2)}) collective-permute-start(bf16[128,512]{1,0:T(8,128)(2,1)S(1)} %get-tuple-element.25), channel_id=1, source_target_pairs={{0,12},{1,13},{2,14},{3,15},{4,8},{5,9},{6,10},{7,11},{8,4},{9,5},... | collective-permute-start | bytes 393224 | tf_op jit(solution)/shard_map/ppermute | solution.py:250
  24.7 9.5 %copy-start.1 = (bf16[128,512]{1,0:T(8,128)(2,1)S(1)}, bf16[128,512]{1,0:T(8,128)(2,1)}, u32[]{:S(2)}) copy-start(bf16[128,512]{1,0:T(8,128)(2,1)} %text_ref.1) | copy-start | bytes 393220
  24.8 8.9 %collective-permute-start.11 = (bf16[128,512]{1,0:T(8,128)(2,1)S(1)}, bf16[128,512]{1,0:T(8,128)(2,1)S(1)}, u32[]{:S(2)}, u32[]{:S(2)}) collective-permute-start(bf16[128,512]{1,0:T(8,128)(2,1)S(1)} %get-tuple-element.29), channel_id=1, source_target_pairs={{0,1},{1,0},{2,3},{3,2},{4,5},{5,4},{6,7},{7,6},{8,9},{9,8},{10,11... | collective-permute-start | bytes 393224 | tf_op jit(solution)/shard_map/ppermute | solution.py:250
  25.8 7.9 %collective-permute-start.12 = (bf16[128,512]{1,0:T(8,128)(2,1)S(1)}, bf16[128,512]{1,0:T(8,128)(2,1)S(1)}, u32[]{:S(2)}, u32[]{:S(2)}) collective-permute-start(bf16[128,512]{1,0:T(8,128)(2,1)S(1)} %get-tuple-element.30), channel_id=1, source_target_pairs={{0,2},{1,3},{2,0},{3,1},{4,6},{5,7},{6,4},{7,5},{8,10},{9,11},{10,... | collective-permute-start | bytes 393224 | tf_op jit(solution)/shard_map/ppermute | solution.py:250
  28.3 5.9 %collective-permute-start.13 = (bf16[128,512]{1,0:T(8,128)(2,1)S(1)}, bf16[128,512]{1,0:T(8,128)(2,1)S(1)}, u32[]{:S(2)}, u32[]{:S(2)}) collective-permute-start(bf16[128,512]{1,0:T(8,128)(2,1)S(1)} %get-tuple-element.31), channel_id=1, source_target_pairs={{0,3},{1,2},{2,1},{3,0},{4,7},{5,6},{6,5},{7,4},{8,11},{9,10},{10,... | collective-permute-start | bytes 393224 | tf_op jit(solution)/shard_map/ppermute | solution.py:250

commit v8 on v7

--- a/solution.py
+++ b/solution.py
@@ -11,6 +11,7 @@
 AXES = ("grp", "dev")
 VMEM_LIMIT = 32 * 1024 * 1024
 SPAN = 256
+PIECE = 32
 LATE = 30000
 LOG2_E = math.log2(math.e)
 VMEM = pl.BlockSpec(memory_space=pltpu.VMEM)
@@ -69,12 +70,20 @@
     slope, shift, temper = (params_ref[0:1, at:at + 1] for at in range(3))
     held = text_ref.shape[0]
     total = None
+
+    def dots_of(first):
+        return lax.dot_general(
+            vi,
+            text_ref[first:min(first + SPAN, held), :],
+            (((1,), (1,)), ((), ())),
+            preferred_element_type=jnp.float32,
+        )
+
+    coming = dots_of(0)
     for first in range(0, held, SPAN):
         last = min(first + SPAN, held)
+        dots, coming = coming, dots_of(last) if last < held else None
         vt = text_ref[first:last, :]
-        dots = lax.dot_general(
-            vi, vt, (((1,), (1,)), ((), ())), preferred_element_type=jnp.float32
-        )
         e = jnp.exp2(slope * dots + shift)
         chance = pl.reciprocal(1.0 + e, approx=True)
         if own and first == 0:
@@ -183,14 +192,24 @@
 def finish_kernel(sides, image_ref, text_ref, *refs):
     parts, outs = refs[:len(sides)], refs[len(sides):len(sides) + 2]
     staged, sems = refs[len(sides) + 2:]
+    rows = image_ref.shape[0]
+    piece = math.gcd(rows, PIECE)
     copies = []
     for side, raw in enumerate((image_ref, text_ref)):
-        unit, factor = unit_rows(raw[...])
-        total = sum(ref[...].astype(jnp.float32) for at, ref in zip(sides, parts) if at == side)
-        along = jnp.sum(unit * total, axis=-1, keepdims=True)
-        staged[side] = factor * (total - unit * along)
-        copies.append(pltpu.make_async_copy(staged.at[side], outs[side], sems.at[side]))
-        copies[-1].start()
+        for first in range(0, rows, piece):
+            here = pl.ds(first, piece)
+            unit, factor = unit_rows(raw[here, :])
+            total = sum(
+                ref[here, :].astype(jnp.float32) for at, ref in zip(sides, parts) if at == side
+            )
+            along = jnp.sum(unit * total, axis=-1, keepdims=True)
+            staged[side, here, :] = factor * (total - unit * along)
+            copies.append(
+                pltpu.make_async_copy(
+                    staged.at[side, here, :], outs[side].at[here, :], sems.at[len(copies)]
+                )
+            )
+            copies[-1].start()
     for copy in copies:
         copy.wait()
 
@@ -204,7 +223,7 @@
         out_specs=[pl.BlockSpec(memory_space=pl.ANY)] * 2,
         scratch_shapes=[
             pltpu.VMEM((2,) + images.shape, jnp.float32),
-            pltpu.SemaphoreType.DMA((2,)),
+            pltpu.SemaphoreType.DMA((2 * (images.shape[0] // math.gcd(images.shape[0], PIECE)),)),
         ],
         compiler_params=pltpu.CompilerParams(vmem_limit_bytes=VMEM_LIMIT),
         cost_estimate=pl.CostEstimate(
@@ -271,8 +290,8 @@
         )
         far_parts = dict(zip([*early, *late], image_parts))
         came = [move(part, grp=-g) for g, part in enumerate(text_parts) if g]
-        low_parts = [move(p, low=-w) for (h, w), p in far_parts.items() if w and not h]
-        high_parts = [move(p, high=-h, low=-w) for (h, w), p in far_parts.items() if h]
+        far_order = [step for step in early if step[0]] + [step for step in early if step[1]] + list(late)
+        far_came = [move(far_parts[h, w], high=-h, low=-w) for h, w in far_order]
         near_parts = add_stacks([text_parts[0], *came], near_count)
         near_parts = [near_parts[0]] + [
             move(part, near=-n) for n, part in enumerate(near_parts) if n
@@ -280,7 +299,7 @@
         return finish(
             images,
             texts,
-            [(0, part) for part in [far_parts[0, 0]] + low_parts + high_parts]
+            [(0, part) for part in [far_parts[0, 0]] + far_came]
             + [(1, part) for part in near_parts],
         )
 

time: 35.4 us -> 37.5 us (1.059)
  waiting for transfers between devices: 8.21 us -> 10.6 us
    ppermute x14, waiting for transfers between devices: 8.21 us -> 10.6 us  [move(): return lax.ppermute(value, AXES, perm)]
where the time goes in v8:
time: 37.5 us; the launch traced here: 37.3 us
  starting transfers between devices  19.1 us (51%)
  waiting for transfers between devices  10.6 us (28%)
  Pallas kernels  4.59 us (12%)
  between operations  2.02 us (5%)
  local copies, waits for them, and re-layouts  0.91 us (2%)
    ppermute x14, starting transfers between devices, move(): return lax.ppermute(value, AXES, perm)  19.1 us
    ppermute x14, waiting for transfers between devices, move(): return lax.ppermute(value, AXES, perm)  10.6 us
    pallas_call x6, Pallas kernels, call(): pl.pallas_call(kernel, out_shape=out_shape, in_specs=[VMEM] * len(operand...  3.53 us
    pallas_call x1, Pallas kernels, finish(): pl.pallas_call(functools.partial(finish_kernel, [side for side, _ in part...  1.07 us
    unnamed x6, local copies, waits for them, and re-layouts  0.91 us
  transfers between devices with their start and end apart: 14, of which 7 were waited for; matrix products, arithmetic and copies ran while one was open for 0% of the time, Pallas kernels for 4%

profile of v8, /device:TPU:0, one launch (start us, length us, event | category | flops | bytes accessed | tf_op | source)
XLA Modules:
  0.0 37.3 jit_solution(12287659183195463752)
XLA Ops:
  0.6 4.1 %collective-permute-start = (bf16[128,512]{1,0:T(8,128)(2,1)}, bf16[128,512]{1,0:T(8,128)(2,1)S(1)}, u32[]{:S(2)}, u32[]{:S(2)}) collective-permute-start(bf16[128,512]{1,0:T(8,128)(2,1)} %image_ref.1), channel_id=1, source_target_pairs={{0,8},{1,9},{2,10},{3,11},{4,12},{5,13},{6,14},{7,15},{8,0},{9,1},... | collective-permute-start | bytes 393224 | tf_op jit(solution)/shard_map/ppermute | solution.py:269
  4.7 1.6 %collective-permute-start.4 = (bf16[128,512]{1,0:T(8,128)(2,1)}, bf16[128,512]{1,0:T(8,128)(2,1)S(1)}, u32[]{:S(2)}, u32[]{:S(2)}) collective-permute-start(bf16[128,512]{1,0:T(8,128)(2,1)} %image_ref.1), channel_id=1, source_target_pairs={{0,4},{1,5},{2,6},{3,7},{4,0},{5,1},{6,2},{7,3},{8,12},{9,13},{10,... | collective-permute-start | bytes 393224 | tf_op jit(solution)/shard_map/ppermute | solution.py:269
  6.3 1.5 %collective-permute-start.2 = (bf16[128,512]{1,0:T(8,128)(2,1)}, bf16[128,512]{1,0:T(8,128)(2,1)S(1)}, u32[]{:S(2)}, u32[]{:S(2)}) collective-permute-start(bf16[128,512]{1,0:T(8,128)(2,1)} %text_ref.1), channel_id=1, source_target_pairs={{0,2},{1,3},{2,0},{3,1},{4,6},{5,7},{6,4},{7,5},{8,10},{9,11},{10,... | collective-permute-start | bytes 393224 | tf_op jit(solution)/shard_map/ppermute | solution.py:269
  7.8 1.5 %collective-permute-start.1 = (bf16[128,512]{1,0:T(8,128)(2,1)}, bf16[128,512]{1,0:T(8,128)(2,1)S(1)}, u32[]{:S(2)}, u32[]{:S(2)}) collective-permute-start(bf16[128,512]{1,0:T(8,128)(2,1)} %text_ref.1), channel_id=1, source_target_pairs={{0,1},{1,0},{2,3},{3,2},{4,5},{5,4},{6,7},{7,6},{8,9},{9,8},{10,11... | collective-permute-start | bytes 393224 | tf_op jit(solution)/shard_map/ppermute | solution.py:269
  9.3 0.5 %collective-permute-start.3 = (bf16[128,512]{1,0:T(8,128)(2,1)}, bf16[128,512]{1,0:T(8,128)(2,1)S(1)}, u32[]{:S(2)}, u32[]{:S(2)}) collective-permute-start(bf16[128,512]{1,0:T(8,128)(2,1)} %text_ref.1), channel_id=1, source_target_pairs={{0,3},{1,2},{2,1},{3,0},{4,7},{5,6},{6,5},{7,4},{8,11},{9,10},{10,... | collective-permute-start | bytes 393224 | tf_op jit(solution)/shard_map/ppermute | solution.py:269
  11.2 0.2 collective-permute-done.refs_1_
  11.4 0.7 %collective-permute-start.5 = (bf16[128,512]{1,0:T(8,128)(2,1)S(1)}, bf16[128,512]{1,0:T(8,128)(2,1)S(1)}, u32[]{:S(2)}, u32[]{:S(2)}) collective-permute-start(bf16[128,512]{1,0:T(8,128)(2,1)S(1)} %collective-permute-done.refs_1_), channel_id=1, source_target_pairs={{0,4},{1,5},{2,6},{3,7},{4,0},{5,1},{6,2},{7,3},{8,12},{9,13},{10,... | collective-permute-start | bytes 393224 | tf_op jit(solution)/shard_map/ppermute | solution.py:269
  12.1 0.9 %copy-done = bf16[128,512]{1,0:T(8,128)(2,1)S(1)} copy-done((bf16[128,512]{1,0:T(8,128)(2,1)S(1)}, bf16[128,512]{1,0:T(8,128)(2,1)}, u32[]{:S(2)}) %copy-start) | copy-done | bytes 131096
  13.1 0.7 %collective-permute-done.1.refs_1_ = bf16[128,512]{1,0:T(8,128)(2,1)S(1)} collective-permute-done((bf16[128,512]{1,0:T(8,128)(2,1)}, bf16[128,512]{1,0:T(8,128)(2,1)S(1)}, u32[]{:S(2)}, u32[]{:S(2)}) %collective-permute-start.1) | collective-permute-done | bytes 131104 | tf_op jit(solution)/shard_map/ppermute | solution.py:269
  13.8 1.9 %collective-permute-done.3.refs_3_ = bf16[128,512]{1,0:T(8,128)(2,1)S(1)} collective-permute-done((bf16[128,512]{1,0:T(8,128)(2,1)}, bf16[128,512]{1,0:T(8,128)(2,1)S(1)}, u32[]{:S(2)}, u32[]{:S(2)}) %collective-permute-start.3) | collective-permute-done | bytes 131104 | tf_op jit(solution)/shard_map/ppermute | solution.py:269
  16.0 1.1 %early_pairs.1 = (f32[512,512]{1,0:T(8,128)S(1)}, bf16[384,512]{1,0:T(8,128)(2,1)S(1)}, f32[384,512]{1,0:T(8,128)S(1)}) custom-call(f32[1,3]{1,0:T(1,128)S(1)} %maximum_bitcast_fusion.params_ref, bf16[512,512]{1,0:T(8,128)(2,1)S(1)} %stack_units.1.text_ref.own_text_ref, bf16[128,512]{1,0:T(8,128)(2,1)S(1)} %copy-done.2, ...), custom_call_target="tpu_custom_call" | custom-call | flops 603979776 | bytes 3145740 | tf_op jit(solution)/shard_map/early_pairs/pallas_call | solution.py:28
  17.3 0.6 %collective-permute-done.6.refs_0_ = bf16[512,512]{1,0:T(8,128)(2,1)S(1)} collective-permute-done((bf16[512,512]{1,0:T(8,128)(2,1)S(1)}, bf16[512,512]{1,0:T(8,128)(2,1)S(1)}, u32[]{:S(2)}, u32[]{:S(2)}) %collective-permute-start.6) | collective-permute-done | bytes 524320 | tf_op jit(solution)/shard_map/ppermute | solution.py:269
  17.9 1.9 %rest_pairs.1 = (f32[512,512]{1,0:T(8,128)S(1)}, bf16[512,512]{1,0:T(8,128)(2,1)S(1)}, f32[128,512]{1,0:T(8,128)S(1)}, bf16[128,512]{1,0:T(8,128)(2,1)S(1)}, bf1...) custom-call(f32[1,3]{1,0:T(1,128)S(1)} %maximum_bitcast_fusion.params_ref, ...), custom_call_target="tpu_custom_call" | custom-call | flops 1006632960 | bytes 5636108 | tf_op jit(solution)/shard_map/rest_pairs/pallas_call | solution.py:28
  19.8 0.2 collective-permute-start.10
  20.0 1.2 %collective-permute-start.7 = (bf16[128,512]{1,0:T(8,128)(2,1)S(1)}, bf16[128,512]{1,0:T(8,128)(2,1)S(1)}, u32[]{:S(2)}, u32[]{:S(2)}) collective-permute-start(bf16[128,512]{1,0:T(8,128)(2,1)S(1)} %get-tuple-element.23), channel_id=1, source_target_pairs={{0,8},{1,9},{2,10},{3,11},{4,12},{5,13},{6,14},{7,15},{8,0},{9,1},... | collective-permute-start | bytes 393224 | tf_op jit(solution)/shard_map/ppermute | solution.py:269
  21.2 1.7 %collective-permute-start.8 = (bf16[128,512]{1,0:T(8,128)(2,1)S(1)}, bf16[128,512]{1,0:T(8,128)(2,1)S(1)}, u32[]{:S(2)}, u32[]{:S(2)}) collective-permute-start(bf16[128,512]{1,0:T(8,128)(2,1)S(1)} %get-tuple-element.24), channel_id=1, source_target_pairs={{0,4},{1,5},{2,6},{3,7},{4,0},{5,1},{6,2},{7,3},{8,12},{9,13},{10,... | collective-permute-start | bytes 393224 | tf_op jit(solution)/shard_map/ppermute | solution.py:269
  22.9 1.5 %collective-permute-start.9 = (bf16[128,512]{1,0:T(8,128)(2,1)S(1)}, bf16[128,512]{1,0:T(8,128)(2,1)S(1)}, u32[]{:S(2)}, u32[]{:S(2)}) collective-permute-start(bf16[128,512]{1,0:T(8,128)(2,1)S(1)} %get-tuple-element.25), channel_id=1, source_target_pairs={{0,12},{1,13},{2,14},{3,15},{4,8},{5,9},{6,10},{7,11},{8,4},{9,5},... | collective-permute-start | bytes 393224 | tf_op jit(solution)/shard_map/ppermute | solution.py:269
  24.5 1.0 %collective-permute-start.11 = (bf16[128,512]{1,0:T(8,128)(2,1)S(1)}, bf16[128,512]{1,0:T(8,128)(2,1)S(1)}, u32[]{:S(2)}, u32[]{:S(2)}) collective-permute-start(bf16[128,512]{1,0:T(8,128)(2,1)S(1)} %get-tuple-element.29), channel_id=1, source_target_pairs={{0,1},{1,0},{2,3},{3,2},{4,5},{5,4},{6,7},{7,6},{8,9},{9,8},{10,11... | collective-permute-start | bytes 393224 | tf_op jit(solution)/shard_map/ppermute | solution.py:269
  25.5 1.5 %collective-permute-start.12 = (bf16[128,512]{1,0:T(8,128)(2,1)S(1)}, bf16[128,512]{1,0:T(8,128)(2,1)S(1)}, u32[]{:S(2)}, u32[]{:S(2)}) collective-permute-start(bf16[128,512]{1,0:T(8,128)(2,1)S(1)} %get-tuple-element.30), channel_id=1, source_target_pairs={{0,2},{1,3},{2,0},{3,1},{4,6},{5,7},{6,4},{7,5},{8,10},{9,11},{10,... | collective-permute-start | bytes 393224 | tf_op jit(solution)/shard_map/ppermute | solution.py:269
  27.0 3.0 %collective-permute-done.7.refs_1_ = bf16[128,512]{1,0:T(8,128)(2,1)S(1)} collective-permute-done((bf16[128,512]{1,0:T(8,128)(2,1)S(1)}, bf16[128,512]{1,0:T(8,128)(2,1)S(1)}, u32[]{:S(2)}, u32[]{:S(2)}) %collective-permute-start.7) | collective-permute-done | bytes 131104 | tf_op jit(solution)/shard_map/ppermute | solution.py:269
  30.0 2.0 %collective-permute-start.13 = (bf16[128,512]{1,0:T(8,128)(2,1)S(1)}, bf16[128,512]{1,0:T(8,128)(2,1)S(1)}, u32[]{:S(2)}, u32[]{:S(2)}) collective-permute-start(bf16[128,512]{1,0:T(8,128)(2,1)S(1)} %get-tuple-element.31), channel_id=1, source_target_pairs={{0,3},{1,2},{2,1},{3,0},{4,7},{5,6},{6,5},{7,4},{8,11},{9,10},{10,... | collective-permute-start | bytes 393224 | tf_op jit(solution)/shard_map/ppermute | solution.py:269
  32.1 0.3 collective-permute-done.8.refs_2_
  32.4 3.9 %collective-permute-done.13.refs_7_ = bf16[128,512]{1,0:T(8,128)(2,1)S(1)} collective-permute-done((bf16[128,512]{1,0:T(8,128)(2,1)S(1)}, bf16[128,512]{1,0:T(8,128)(2,1)S(1)}, u32[]{:S(2)}, u32[]{:S(2)}) %collective-permute-start.13) | collective-permute-done | bytes 131104 | tf_op jit(solution)/shard_map/ppermute | solution.py:269
  36.3 1.1 %finish.1 = (f32[128,512]{1,0:T(8,128)}, f32[128,512]{1,0:T(8,128)}) custom-call(bf16[128,512]{1,0:T(8,128)(2,1)S(1)} %copy-done.2, bf16[128,512]{1,0:T(8,128)(2,1)S(1)} %copy-done.1, f32[128,512]{1,0:T(8,128)S(1)} %get-tuple-element.22.refs_0_, bf16[128,512]{1,0:T(8,128)(2,1)S(1)} %collective-permute-done.7.refs_1_, ...), custom_call_target="tpu_custom_call" | custom-call | flops 5242880 | bytes 1572864 | tf_op jit(solution)/shard_map/finish/pallas_call | solution.py:219
  (18 shorter events, 0.7 us)
Async XLA Ops:
  0.6 10.7 %collective-permute-start = (bf16[128,512]{1,0:T(8,128)(2,1)}, bf16[128,512]{1,0:T(8,128)(2,1)S(1)}, u32[]{:S(2)}, u32[]{:S(2)}) collective-permute-start(bf16[128,512]{1,0:T(8,128)(2,1)} %image_ref.1), channel_id=1, source_target_pairs={{0,8},{1,9},{2,10},{3,11},{4,12},{5,13},{6,14},{7,15},{8,0},{9,1},... | collective-permute-start | bytes 393224 | tf_op jit(solution)/shard_map/ppermute | solution.py:269
  4.7 11.3 %collective-permute-start.4 = (bf16[128,512]{1,0:T(8,128)(2,1)}, bf16[128,512]{1,0:T(8,128)(2,1)S(1)}, u32[]{:S(2)}, u32[]{:S(2)}) collective-permute-start(bf16[128,512]{1,0:T(8,128)(2,1)} %image_ref.1), channel_id=1, source_target_pairs={{0,4},{1,5},{2,6},{3,7},{4,0},{5,1},{6,2},{7,3},{8,12},{9,13},{10,... | collective-permute-start | bytes 393224 | tf_op jit(solution)/shard_map/ppermute | solution.py:269
  6.3 6.8 %collective-permute-start.2 = (bf16[128,512]{1,0:T(8,128)(2,1)}, bf16[128,512]{1,0:T(8,128)(2,1)S(1)}, u32[]{:S(2)}, u32[]{:S(2)}) collective-permute-start(bf16[128,512]{1,0:T(8,128)(2,1)} %text_ref.1), channel_id=1, source_target_pairs={{0,2},{1,3},{2,0},{3,1},{4,6},{5,7},{6,4},{7,5},{8,10},{9,11},{10,... | collective-permute-start | bytes 393224 | tf_op jit(solution)/shard_map/ppermute | solution.py:269
  7.8 6.0 %collective-permute-start.1 = (bf16[128,512]{1,0:T(8,128)(2,1)}, bf16[128,512]{1,0:T(8,128)(2,1)S(1)}, u32[]{:S(2)}, u32[]{:S(2)}) collective-permute-start(bf16[128,512]{1,0:T(8,128)(2,1)} %text_ref.1), channel_id=1, source_target_pairs={{0,1},{1,0},{2,3},{3,2},{4,5},{5,4},{6,7},{7,6},{8,9},{9,8},{10,11... | collective-permute-start | bytes 393224 | tf_op jit(solution)/shard_map/ppermute | solution.py:269
  9.3 6.4 %collective-permute-start.3 = (bf16[128,512]{1,0:T(8,128)(2,1)}, bf16[128,512]{1,0:T(8,128)(2,1)S(1)}, u32[]{:S(2)}, u32[]{:S(2)}) collective-permute-start(bf16[128,512]{1,0:T(8,128)(2,1)} %text_ref.1), channel_id=1, source_target_pairs={{0,3},{1,2},{2,1},{3,0},{4,7},{5,6},{6,5},{7,4},{8,11},{9,10},{10,... | collective-permute-start | bytes 393224 | tf_op jit(solution)/shard_map/ppermute | solution.py:269
  11.4 5.8 %collective-permute-start.5 = (bf16[128,512]{1,0:T(8,128)(2,1)S(1)}, bf16[128,512]{1,0:T(8,128)(2,1)S(1)}, u32[]{:S(2)}, u32[]{:S(2)}) collective-permute-start(bf16[128,512]{1,0:T(8,128)(2,1)S(1)} %collective-permute-done.refs_1_), channel_id=1, source_target_pairs={{0,4},{1,5},{2,6},{3,7},{4,0},{5,1},{6,2},{7,3},{8,12},{9,13},{10,... | collective-permute-start | bytes 393224 | tf_op jit(solution)/shard_map/ppermute | solution.py:269
  12.1 0.9 %copy-start = (bf16[128,512]{1,0:T(8,128)(2,1)S(1)}, bf16[128,512]{1,0:T(8,128)(2,1)}, u32[]{:S(2)}) copy-start(bf16[128,512]{1,0:T(8,128)(2,1)} %text_ref.1) | copy-start | bytes 393220
  13.1 2.9 %copy-start.2 = (bf16[128,512]{1,0:T(8,128)(2,1)S(1)}, bf16[128,512]{1,0:T(8,128)(2,1)}, u32[]{:S(2)}) copy-start(bf16[128,512]{1,0:T(8,128)(2,1)} %image_ref.1) | copy-start | bytes 393220
  15.9 2.0 %collective-permute-start.6 = (bf16[512,512]{1,0:T(8,128)(2,1)S(1)}, bf16[512,512]{1,0:T(8,128)(2,1)S(1)}, u32[]{:S(2)}, u32[]{:S(2)}) collective-permute-start(bf16[512,512]{1,0:T(8,128)(2,1)S(1)} %stack_units.1.text_ref.own_text_ref), channel_id=1, source_target_pairs={{0,16},{1,17},{2,18},{3,19},{4,20},{5,21},{6,22},{7,23},{8,24},{9,... | collective-permute-start | bytes 1572872 | tf_op jit(solution)/shard_map/ppermute | solution.py:269
  19.8 4.6 %collective-permute-start.10 = (bf16[512,512]{1,0:T(8,128)(2,1)S(1)}, bf16[512,512]{1,0:T(8,128)(2,1)S(1)}, u32[]{:S(2)}, u32[]{:S(2)}) collective-permute-start(bf16[512,512]{1,0:T(8,128)(2,1)S(1)} %get-tuple-element.27), channel_id=1, source_target_pairs={{0,16},{1,17},{2,18},{3,19},{4,20},{5,21},{6,22},{7,23},{8,24},{9,... | collective-permute-start | bytes 1572872 | tf_op jit(solution)/shard_map/ppermute | solution.py:269
  20.0 10.0 %collective-permute-start.7 = (bf16[128,512]{1,0:T(8,128)(2,1)S(1)}, bf16[128,512]{1,0:T(8,128)(2,1)S(1)}, u32[]{:S(2)}, u32[]{:S(2)}) collective-permute-start(bf16[128,512]{1,0:T(8,128)(2,1)S(1)} %get-tuple-element.23), channel_id=1, source_target_pairs={{0,8},{1,9},{2,10},{3,11},{4,12},{5,13},{6,14},{7,15},{8,0},{9,1},... | collective-permute-start | bytes 393224 | tf_op jit(solution)/shard_map/ppermute | solution.py:269
  21.2 11.2 %collective-permute-start.8 = (bf16[128,512]{1,0:T(8,128)(2,1)S(1)}, bf16[128,512]{1,0:T(8,128)(2,1)S(1)}, u32[]{:S(2)}, u32[]{:S(2)}) collective-permute-start(bf16[128,512]{1,0:T(8,128)(2,1)S(1)} %get-tuple-element.24), channel_id=1, source_target_pairs={{0,4},{1,5},{2,6},{3,7},{4,0},{5,1},{6,2},{7,3},{8,12},{9,13},{10,... | collective-permute-start | bytes 393224 | tf_op jit(solution)/shard_map/ppermute | solution.py:269
  22.9 9.4 %collective-permute-start.9 = (bf16[128,512]{1,0:T(8,128)(2,1)S(1)}, bf16[128,512]{1,0:T(8,128)(2,1)S(1)}, u32[]{:S(2)}, u32[]{:S(2)}) collective-permute-start(bf16[128,512]{1,0:T(8,128)(2,1)S(1)} %get-tuple-element.25), channel_id=1, source_target_pairs={{0,12},{1,13},{2,14},{3,15},{4,8},{5,9},{6,10},{7,11},{8,4},{9,5},... | collective-permute-start | bytes 393224 | tf_op jit(solution)/shard_map/ppermute | solution.py:269
  24.4 11.9 %copy-start.1 = (bf16[128,512]{1,0:T(8,128)(2,1)S(1)}, bf16[128,512]{1,0:T(8,128)(2,1)}, u32[]{:S(2)}) copy-start(bf16[128,512]{1,0:T(8,128)(2,1)} %text_ref.1) | copy-start | bytes 393220
  24.5 7.9 %collective-permute-start.11 = (bf16[128,512]{1,0:T(8,128)(2,1)S(1)}, bf16[128,512]{1,0:T(8,128)(2,1)S(1)}, u32[]{:S(2)}, u32[]{:S(2)}) collective-permute-start(bf16[128,512]{1,0:T(8,128)(2,1)S(1)} %get-tuple-element.29), channel_id=1, source_target_pairs={{0,1},{1,0},{2,3},{3,2},{4,5},{5,4},{6,7},{7,6},{8,9},{9,8},{10,11... | collective-permute-start | bytes 393224 | tf_op jit(solution)/shard_map/ppermute | solution.py:269
  25.5 6.9 %collective-permute-start.12 = (bf16[128,512]{1,0:T(8,128)(2,1)S(1)}, bf16[128,512]{1,0:T(8,128)(2,1)S(1)}, u32[]{:S(2)}, u32[]{:S(2)}) collective-permute-start(bf16[128,512]{1,0:T(8,128)(2,1)S(1)} %get-tuple-element.30), channel_id=1, source_target_pairs={{0,2},{1,3},{2,0},{3,1},{4,6},{5,7},{6,4},{7,5},{8,10},{9,11},{10,... | collective-permute-start | bytes 393224 | tf_op jit(solution)/shard_map/ppermute | solution.py:269
  30.0 6.2 %collective-permute-start.13 = (bf16[128,512]{1,0:T(8,128)(2,1)S(1)}, bf16[128,512]{1,0:T(8,128)(2,1)S(1)}, u32[]{:S(2)}, u32[]{:S(2)}) collective-permute-start(bf16[128,512]{1,0:T(8,128)(2,1)S(1)} %get-tuple-element.31), channel_id=1, source_target_pairs={{0,3},{1,2},{2,1},{3,0},{4,7},{5,6},{6,5},{7,4},{8,11},{9,10},{10,... | collective-permute-start | bytes 393224 | tf_op jit(solution)/shard_map/ppermute | solution.py:269

commit v9 on v8

--- a/solution.py
+++ b/solution.py
@@ -189,10 +189,14 @@
     )
 
 
-def finish_kernel(sides, image_ref, text_ref, *refs):
+def finish_kernel(sides, image_ref, text_ref, at_ref, low_ref, *refs):
     parts, outs = refs[:len(sides)], refs[len(sides):len(sides) + 2]
     staged, sems = refs[len(sides) + 2:]
     rows = image_ref.shape[0]
+    at, low_count = at_ref[0], low_ref.shape[0]
+    neighbour = [low_ref.at[lax.rem(at + w, low_count)] for w in range(1, low_count)]
+    sides = sides + [0] * len(neighbour)
+    parts = list(parts) + neighbour
     piece = math.gcd(rows, PIECE)
     copies = []
     for side, raw in enumerate((image_ref, text_ref)):
@@ -200,7 +204,7 @@
             here = pl.ds(first, piece)
             unit, factor = unit_rows(raw[here, :])
             total = sum(
-                ref[here, :].astype(jnp.float32) for at, ref in zip(sides, parts) if at == side
+                ref[here, :].astype(jnp.float32) for own, ref in zip(sides, parts) if own == side
             )
             along = jnp.sum(unit * total, axis=-1, keepdims=True)
             staged[side, here, :] = factor * (total - unit * along)
@@ -214,12 +218,12 @@
         copy.wait()
 
 
-def finish(images, texts, parts):
+def finish(images, texts, low_at, low_parts, parts):
     out = jax.ShapeDtypeStruct(images.shape, jnp.float32)
     return pl.pallas_call(
         functools.partial(finish_kernel, [side for side, _ in parts]),
         out_shape=(out, out),
-        in_specs=[VMEM] * (2 + len(parts)),
+        in_specs=[VMEM] * 2 + [pl.BlockSpec(memory_space=pltpu.SMEM)] + [VMEM] * (1 + len(parts)),
         out_specs=[pl.BlockSpec(memory_space=pl.ANY)] * 2,
         scratch_shapes=[
             pltpu.VMEM((2,) + images.shape, jnp.float32),
@@ -232,7 +236,7 @@
             transcendentals=0,
         ),
         name="finish",
-    )(images, texts, *[part for _, part in parts])
+    )(images, texts, low_at, low_parts, *[part for _, part in parts])
 
 
 def plan(grp_count, dev_count):
@@ -267,6 +271,11 @@
                         target = ((g2 * high_count + h2) * low_count + w2) * near_count + n2
                         perm.append((source, target))
         return lax.ppermute(value, AXES, perm)
+
+    low_groups = [
+        [((g * high_count + h) * low_count + w) * near_count + n for w in range(low_count)]
+        for g in range(grp_count) for h in range(high_count) for n in range(near_count)
+    ]
 
     def on_device(images, texts, logit_scale, logit_bias):
         params = jnp.concatenate(
@@ -290,15 +299,22 @@
         )
         far_parts = dict(zip([*early, *late], image_parts))
         came = [move(part, grp=-g) for g, part in enumerate(text_parts) if g]
-        far_order = [step for step in early if step[0]] + [step for step in early if step[1]] + list(late)
-        far_came = [move(far_parts[h, w], high=-h, low=-w) for h, w in far_order]
+        far_came = [move(p, high=-h, low=-w) for (h, w), p in far_parts.items() if h]
         near_parts = add_stacks([text_parts[0], *came], near_count)
         near_parts = [near_parts[0]] + [
             move(part, near=-n) for n, part in enumerate(near_parts) if n
         ]
+        low_part = far_parts[0, low_count - 1]
+        low_parts = lax.all_to_all(
+            jnp.broadcast_to(low_part, (low_count,) + low_part.shape),
+            AXES, 0, 0, axis_index_groups=low_groups, tiled=True,
+        )
+        low_at = lax.axis_index("dev") // near_count % low_count
         return finish(
             images,
             texts,
+            low_at.reshape(1),
+            low_parts,
             [(0, part) for part in [far_parts[0, 0]] + far_came]
             + [(1, part) for part in near_parts],
         )

time: 37.5 us -> 38.9 us (1.037)
  starting transfers between devices: 19.1 us -> 21.4 us
  waiting for transfers between devices: 10.6 us -> 8.33 us
  local copies, waits for them, and re-layouts: 0.91 us -> 1.63 us
  Pallas kernels: 4.59 us -> 5.16 us
    all_to_all x0 -> x1, starting transfers between devices: none -> 3.44 us  [on_device(): lax.all_to_all(jnp.broadcast_to(low_part, (low_count,) + low_part.shape),...]
    ppermute x14 -> x13, waiting for transfers between devices: 10.6 us -> 8.33 us  [move(): return lax.ppermute(value, AXES, perm)]
    ppermute x14 -> x13, starting transfers between devices: 19.1 us -> 17.9 us  [move(): return lax.ppermute(value, AXES, perm)]
    broadcast_in_dim x0 -> x1, local copies, waits for them, and re-layouts: none -> 0.72 us  [on_device(): jnp.broadcast_to(low_part, (low_count,) + low_part.shape)]
    pallas_call x6, Pallas kernels: 3.53 us -> 4.1 us  [call(): pl.pallas_call(kernel, out_shape=out_shape, in_specs=[VMEM] * len(operand...]
  transfers between devices with their start and end apart: 14 -> 14, of which waited for: 7 -> 6; matrix products, arithmetic and copies ran while one was open for 0% -> 2% of each run, Pallas kernels for 4% -> 4%
where the time goes in v9:
time: 38.9 us; the launch traced here: 38.6 us
  starting transfers between devices  21.4 us (55%)
  waiting for transfers between devices  8.33 us (21%)
  Pallas kernels  5.16 us (13%)
  between operations  2.01 us (5%)
  local copies, waits for them, and re-layouts  1.63 us (4%)
    ppermute x13, starting transfers between devices, move(): return lax.ppermute(value, AXES, perm)  17.9 us
    ppermute x13, waiting for transfers between devices, move(): return lax.ppermute(value, AXES, perm)  8.33 us
    pallas_call x6, Pallas kernels, call(): pl.pallas_call(kernel, out_shape=out_shape, in_specs=[VMEM] * len(operand...  4.1 us
    all_to_all x1, starting transfers between devices, on_device(): lax.all_to_all(jnp.broadcast_to(low_part, (low_count,) + low_part.shape),...  3.44 us
    pallas_call x1, Pallas kernels, finish(): pl.pallas_call(functools.partial(finish_kernel, [side for side, _ in part...  1.06 us
    unnamed x6, local copies, waits for them, and re-layouts  0.91 us
  transfers between devices with their start and end apart: 14, of which 6 were waited for; matrix products, arithmetic and copies ran while one was open for 2% of the time, Pallas kernels for 4%

profile of v9, /device:TPU:0, one launch (start us, length us, event | category | flops | bytes accessed | tf_op | source)
XLA Modules:
  0.0 38.6 jit_solution(10629078349062016515)
XLA Ops:
  0.6 4.1 %collective-permute-start = (bf16[128,512]{1,0:T(8,128)(2,1)}, bf16[128,512]{1,0:T(8,128)(2,1)S(1)}, u32[]{:S(2)}, u32[]{:S(2)}) collective-permute-start(bf16[128,512]{1,0:T(8,128)(2,1)} %image_ref.1), channel_id=1, source_target_pairs={{0,8},{1,9},{2,10},{3,11},{4,12},{5,13},{6,14},{7,15},{8,0},{9,1},... | collective-permute-start | bytes 393224 | tf_op jit(solution)/shard_map/ppermute | solution.py:273
  4.7 1.5 %collective-permute-start.1 = (bf16[128,512]{1,0:T(8,128)(2,1)}, bf16[128,512]{1,0:T(8,128)(2,1)S(1)}, u32[]{:S(2)}, u32[]{:S(2)}) collective-permute-start(bf16[128,512]{1,0:T(8,128)(2,1)} %text_ref.1), channel_id=1, source_target_pairs={{0,1},{1,0},{2,3},{3,2},{4,5},{5,4},{6,7},{7,6},{8,9},{9,8},{10,11... | collective-permute-start | bytes 393224 | tf_op jit(solution)/shard_map/ppermute | solution.py:273
  6.2 1.5 %collective-permute-start.2 = (bf16[128,512]{1,0:T(8,128)(2,1)}, bf16[128,512]{1,0:T(8,128)(2,1)S(1)}, u32[]{:S(2)}, u32[]{:S(2)}) collective-permute-start(bf16[128,512]{1,0:T(8,128)(2,1)} %text_ref.1), channel_id=1, source_target_pairs={{0,2},{1,3},{2,0},{3,1},{4,6},{5,7},{6,4},{7,5},{8,10},{9,11},{10,... | collective-permute-start | bytes 393224 | tf_op jit(solution)/shard_map/ppermute | solution.py:273
  7.7 0.5 %collective-permute-start.3 = (bf16[128,512]{1,0:T(8,128)(2,1)}, bf16[128,512]{1,0:T(8,128)(2,1)S(1)}, u32[]{:S(2)}, u32[]{:S(2)}) collective-permute-start(bf16[128,512]{1,0:T(8,128)(2,1)} %text_ref.1), channel_id=1, source_target_pairs={{0,3},{1,2},{2,1},{3,0},{4,7},{5,6},{6,5},{7,4},{8,11},{9,10},{10,... | collective-permute-start | bytes 393224 | tf_op jit(solution)/shard_map/ppermute | solution.py:273
  8.2 1.6 %collective-permute-start.4 = (bf16[128,512]{1,0:T(8,128)(2,1)}, bf16[128,512]{1,0:T(8,128)(2,1)S(1)}, u32[]{:S(2)}, u32[]{:S(2)}) collective-permute-start(bf16[128,512]{1,0:T(8,128)(2,1)} %image_ref.1), channel_id=1, source_target_pairs={{0,4},{1,5},{2,6},{3,7},{4,0},{5,1},{6,2},{7,3},{8,12},{9,13},{10,... | collective-permute-start | bytes 393224 | tf_op jit(solution)/shard_map/ppermute | solution.py:273
  11.2 0.2 collective-permute-done.refs_1_
  11.4 0.8 %collective-permute-start.5 = (bf16[128,512]{1,0:T(8,128)(2,1)S(1)}, bf16[128,512]{1,0:T(8,128)(2,1)S(1)}, u32[]{:S(2)}, u32[]{:S(2)}) collective-permute-start(bf16[128,512]{1,0:T(8,128)(2,1)S(1)} %collective-permute-done.refs_1_), channel_id=1, source_target_pairs={{0,4},{1,5},{2,6},{3,7},{4,0},{5,1},{6,2},{7,3},{8,12},{9,13},{10,... | collective-permute-start | bytes 393224 | tf_op jit(solution)/shard_map/ppermute | solution.py:273
  12.1 0.9 %copy-done = bf16[128,512]{1,0:T(8,128)(2,1)S(1)} copy-done((bf16[128,512]{1,0:T(8,128)(2,1)S(1)}, bf16[128,512]{1,0:T(8,128)(2,1)}, u32[]{:S(2)}) %copy-start) | copy-done | bytes 131096
  13.2 1.0 %collective-permute-done.2.refs_2_ = bf16[128,512]{1,0:T(8,128)(2,1)S(1)} collective-permute-done((bf16[128,512]{1,0:T(8,128)(2,1)}, bf16[128,512]{1,0:T(8,128)(2,1)S(1)}, u32[]{:S(2)}, u32[]{:S(2)}) %collective-permute-start.2) | collective-permute-done | bytes 131104 | tf_op jit(solution)/shard_map/ppermute | solution.py:273
  14.2 0.2 stack_units.1.text_ref.own_text_ref
  14.5 0.4 %collective-permute-done.4.refs_2_ = bf16[128,512]{1,0:T(8,128)(2,1)S(1)} collective-permute-done((bf16[128,512]{1,0:T(8,128)(2,1)}, bf16[128,512]{1,0:T(8,128)(2,1)S(1)}, u32[]{:S(2)}, u32[]{:S(2)}) %collective-permute-start.4) | collective-permute-done | bytes 131104 | tf_op jit(solution)/shard_map/ppermute | solution.py:273
  14.9 1.1 %early_pairs.1 = (f32[512,512]{1,0:T(8,128)S(1)}, bf16[384,512]{1,0:T(8,128)(2,1)S(1)}, f32[384,512]{1,0:T(8,128)S(1)}) custom-call(f32[1,3]{1,0:T(1,128)S(1)} %maximum_bitcast_fusion.params_ref, bf16[512,512]{1,0:T(8,128)(2,1)S(1)} %stack_units.1.text_ref.own_text_ref, bf16[128,512]{1,0:T(8,128)(2,1)S(1)} %copy-done.2, ...), custom_call_target="tpu_custom_call" | custom-call | flops 603979776 | bytes 3145740 | tf_op jit(solution)/shard_map/early_pairs/pallas_call | solution.py:28
  16.0 0.9 %collective-permute-done.5.refs_0_ = bf16[128,512]{1,0:T(8,128)(2,1)S(1)} collective-permute-done((bf16[128,512]{1,0:T(8,128)(2,1)S(1)}, bf16[128,512]{1,0:T(8,128)(2,1)S(1)}, u32[]{:S(2)}, u32[]{:S(2)}) %collective-permute-start.5) | collective-permute-done | bytes 131104 | tf_op jit(solution)/shard_map/ppermute | solution.py:273
  17.0 2.5 %rest_pairs.1 = (f32[512,512]{1,0:T(8,128)S(1)}, bf16[512,512]{1,0:T(8,128)(2,1)S(1)}, f32[128,512]{1,0:T(8,128)S(1)}, bf16[128,512]{1,0:T(8,128)(2,1)}, bf16[12...) custom-call(f32[1,3]{1,0:T(1,128)S(1)} %maximum_bitcast_fusion.params_ref, ...), custom_call_target="tpu_custom_call" | custom-call | flops 1006632960 | bytes 5636108 | tf_op jit(solution)/shard_map/rest_pairs/pallas_call | solution.py:28
  19.5 0.7 %broadcast_in_dim.3 = bf16[2,128,512]{2,1,0:T(8,128)(2,1)} broadcast(bf16[128,512]{1,0:T(8,128)(2,1)S(1)} %get-tuple-element.22), dimensions={1,2} | broadcast | bytes 393216 | tf_op jit(solution)/shard_map/broadcast_in_dim | solution.py:309
  20.2 3.4 %all-to-all-start = ((bf16[2,128,512]{2,1,0:T(8,128)(2,1)}), bf16[2,128,512]{2,1,0:T(8,128)(2,1)S(1)}, u32[]{:S(2)}, u32[]{:S(2)}) async-start(bf16[2,128,512]{2,1,0:T(8,128)(2,1)} %broadcast_in_dim.3), calls=%async_computation | async-start | bytes 524288 | tf_op jit(solution)/shard_map/all_to_all | solution.py:308
  23.7 2.3 %collective-permute-start.7 = (bf16[128,512]{1,0:T(8,128)(2,1)}, bf16[128,512]{1,0:T(8,128)(2,1)S(1)}, u32[]{:S(2)}, u32[]{:S(2)}) collective-permute-start(bf16[128,512]{1,0:T(8,128)(2,1)} %get-tuple-element.24), channel_id=1, source_target_pairs={{0,8},{1,9},{2,10},{3,11},{4,12},{5,13},{6,14},{7,15},{8,0},{9,1},... | collective-permute-start | bytes 393224 | tf_op jit(solution)/shard_map/ppermute | solution.py:273
  25.9 2.1 %collective-permute-start.8 = (bf16[128,512]{1,0:T(8,128)(2,1)S(1)}, bf16[128,512]{1,0:T(8,128)(2,1)S(1)}, u32[]{:S(2)}, u32[]{:S(2)}) collective-permute-start(bf16[128,512]{1,0:T(8,128)(2,1)S(1)} %get-tuple-element.25), channel_id=1, source_target_pairs={{0,12},{1,13},{2,14},{3,15},{4,8},{5,9},{6,10},{7,11},{8,4},{9,5},... | collective-permute-start | bytes 393224 | tf_op jit(solution)/shard_map/ppermute | solution.py:273
  28.1 1.6 %collective-permute-start.10 = (bf16[128,512]{1,0:T(8,128)(2,1)S(1)}, bf16[128,512]{1,0:T(8,128)(2,1)S(1)}, u32[]{:S(2)}, u32[]{:S(2)}) collective-permute-start(bf16[128,512]{1,0:T(8,128)(2,1)S(1)} %get-tuple-element.29), channel_id=1, source_target_pairs={{0,1},{1,0},{2,3},{3,2},{4,5},{5,4},{6,7},{7,6},{8,9},{9,8},{10,11... | collective-permute-start | bytes 393224 | tf_op jit(solution)/shard_map/ppermute | solution.py:273
  29.7 1.5 %collective-permute-start.11 = (bf16[128,512]{1,0:T(8,128)(2,1)S(1)}, bf16[128,512]{1,0:T(8,128)(2,1)S(1)}, u32[]{:S(2)}, u32[]{:S(2)}) collective-permute-start(bf16[128,512]{1,0:T(8,128)(2,1)S(1)} %get-tuple-element.30), channel_id=1, source_target_pairs={{0,2},{1,3},{2,0},{3,1},{4,6},{5,7},{6,4},{7,5},{8,10},{9,11},{10,... | collective-permute-start | bytes 393224 | tf_op jit(solution)/shard_map/ppermute | solution.py:273
  31.2 0.4 %collective-permute-start.12 = (bf16[128,512]{1,0:T(8,128)(2,1)S(1)}, bf16[128,512]{1,0:T(8,128)(2,1)S(1)}, u32[]{:S(2)}, u32[]{:S(2)}) collective-permute-start(bf16[128,512]{1,0:T(8,128)(2,1)S(1)} %get-tuple-element.31), channel_id=1, source_target_pairs={{0,3},{1,2},{2,1},{3,0},{4,7},{5,6},{6,5},{7,4},{8,11},{9,10},{10,... | collective-permute-start | bytes 393224 | tf_op jit(solution)/shard_map/ppermute | solution.py:273
  31.7 5.4 %collective-permute-done.8.refs_2_ = bf16[128,512]{1,0:T(8,128)(2,1)S(1)} collective-permute-done((bf16[128,512]{1,0:T(8,128)(2,1)S(1)}, bf16[128,512]{1,0:T(8,128)(2,1)S(1)}, u32[]{:S(2)}, u32[]{:S(2)}) %collective-permute-start.8) | collective-permute-done | bytes 131104 | tf_op jit(solution)/shard_map/ppermute | solution.py:273
  37.1 0.4 collective-permute-done.11.refs_5_
  37.5 1.1 %finish.1 = (f32[128,512]{1,0:T(8,128)}, f32[128,512]{1,0:T(8,128)}) custom-call(bf16[128,512]{1,0:T(8,128)(2,1)S(1)} %copy-done.2, bf16[128,512]{1,0:T(8,128)(2,1)S(1)} %copy-done.1, s32[1]{0:T(128)} %bitcast.at_ref, bf16[2,128,512]{2,1,0:T(8,128)(2,1)S(1)} %all-to-all-done.low_ref, f32[128,512]{1,0:T(8,128)S(1)} %get-tuple-element.23.refs_0_, ...), custom_call_target="tpu_custom_call" | custom-call | flops 4587520 | bytes 1376256 | tf_op jit(solution)/shard_map/finish/pallas_call | solution.py:223
  (19 shorter events, 0.5 us)
Async XLA Ops:
  0.6 10.7 %collective-permute-start = (bf16[128,512]{1,0:T(8,128)(2,1)}, bf16[128,512]{1,0:T(8,128)(2,1)S(1)}, u32[]{:S(2)}, u32[]{:S(2)}) collective-permute-start(bf16[128,512]{1,0:T(8,128)(2,1)} %image_ref.1), channel_id=1, source_target_pairs={{0,8},{1,9},{2,10},{3,11},{4,12},{5,13},{6,14},{7,15},{8,0},{9,1},... | collective-permute-start | bytes 393224 | tf_op jit(solution)/shard_map/ppermute | solution.py:273
  4.7 8.4 %collective-permute-start.1 = (bf16[128,512]{1,0:T(8,128)(2,1)}, bf16[128,512]{1,0:T(8,128)(2,1)S(1)}, u32[]{:S(2)}, u32[]{:S(2)}) collective-permute-start(bf16[128,512]{1,0:T(8,128)(2,1)} %text_ref.1), channel_id=1, source_target_pairs={{0,1},{1,0},{2,3},{3,2},{4,5},{5,4},{6,7},{7,6},{8,9},{9,8},{10,11... | collective-permute-start | bytes 393224 | tf_op jit(solution)/shard_map/ppermute | solution.py:273
  6.2 8.0 %collective-permute-start.2 = (bf16[128,512]{1,0:T(8,128)(2,1)}, bf16[128,512]{1,0:T(8,128)(2,1)S(1)}, u32[]{:S(2)}, u32[]{:S(2)}) collective-permute-start(bf16[128,512]{1,0:T(8,128)(2,1)} %text_ref.1), channel_id=1, source_target_pairs={{0,2},{1,3},{2,0},{3,1},{4,6},{5,7},{6,4},{7,5},{8,10},{9,11},{10,... | collective-permute-start | bytes 393224 | tf_op jit(solution)/shard_map/ppermute | solution.py:273
  7.7 6.5 %collective-permute-start.3 = (bf16[128,512]{1,0:T(8,128)(2,1)}, bf16[128,512]{1,0:T(8,128)(2,1)S(1)}, u32[]{:S(2)}, u32[]{:S(2)}) collective-permute-start(bf16[128,512]{1,0:T(8,128)(2,1)} %text_ref.1), channel_id=1, source_target_pairs={{0,3},{1,2},{2,1},{3,0},{4,7},{5,6},{6,5},{7,4},{8,11},{9,10},{10,... | collective-permute-start | bytes 393224 | tf_op jit(solution)/shard_map/ppermute | solution.py:273
  8.2 6.6 %collective-permute-start.4 = (bf16[128,512]{1,0:T(8,128)(2,1)}, bf16[128,512]{1,0:T(8,128)(2,1)S(1)}, u32[]{:S(2)}, u32[]{:S(2)}) collective-permute-start(bf16[128,512]{1,0:T(8,128)(2,1)} %image_ref.1), channel_id=1, source_target_pairs={{0,4},{1,5},{2,6},{3,7},{4,0},{5,1},{6,2},{7,3},{8,12},{9,13},{10,... | collective-permute-start | bytes 393224 | tf_op jit(solution)/shard_map/ppermute | solution.py:273
  11.4 5.5 %collective-permute-start.5 = (bf16[128,512]{1,0:T(8,128)(2,1)S(1)}, bf16[128,512]{1,0:T(8,128)(2,1)S(1)}, u32[]{:S(2)}, u32[]{:S(2)}) collective-permute-start(bf16[128,512]{1,0:T(8,128)(2,1)S(1)} %collective-permute-done.refs_1_), channel_id=1, source_target_pairs={{0,4},{1,5},{2,6},{3,7},{4,0},{5,1},{6,2},{7,3},{8,12},{9,13},{10,... | collective-permute-start | bytes 393224 | tf_op jit(solution)/shard_map/ppermute | solution.py:273
  12.1 0.9 %copy-start = (bf16[128,512]{1,0:T(8,128)(2,1)S(1)}, bf16[128,512]{1,0:T(8,128)(2,1)}, u32[]{:S(2)}) copy-start(bf16[128,512]{1,0:T(8,128)(2,1)} %text_ref.1) | copy-start | bytes 393220
  13.1 1.7 %copy-start.2 = (bf16[128,512]{1,0:T(8,128)(2,1)S(1)}, bf16[128,512]{1,0:T(8,128)(2,1)}, u32[]{:S(2)}) copy-start(bf16[128,512]{1,0:T(8,128)(2,1)} %image_ref.1) | copy-start | bytes 393220
  14.4 2.6 %collective-permute-start.6 = (bf16[512,512]{1,0:T(8,128)(2,1)S(1)}, bf16[512,512]{1,0:T(8,128)(2,1)S(1)}, u32[]{:S(2)}, u32[]{:S(2)}) collective-permute-start(bf16[512,512]{1,0:T(8,128)(2,1)S(1)} %stack_units.1.text_ref.own_text_ref), channel_id=1, source_target_pairs={{0,16},{1,17},{2,18},{3,19},{4,20},{5,21},{6,22},{7,23},{8,24},{9,... | collective-permute-start | bytes 1572872 | tf_op jit(solution)/shard_map/ppermute | solution.py:273
  19.5 8.5 %collective-permute-start.9 = (bf16[512,512]{1,0:T(8,128)(2,1)S(1)}, bf16[512,512]{1,0:T(8,128)(2,1)S(1)}, u32[]{:S(2)}, u32[]{:S(2)}) collective-permute-start(bf16[512,512]{1,0:T(8,128)(2,1)S(1)} %get-tuple-element.27), channel_id=1, source_target_pairs={{0,16},{1,17},{2,18},{3,19},{4,20},{5,21},{6,22},{7,23},{8,24},{9,... | collective-permute-start | bytes 1572872 | tf_op jit(solution)/shard_map/ppermute | solution.py:273
  20.2 16.9 %all-to-all-start = ((bf16[2,128,512]{2,1,0:T(8,128)(2,1)}), bf16[2,128,512]{2,1,0:T(8,128)(2,1)S(1)}, u32[]{:S(2)}, u32[]{:S(2)}) async-start(bf16[2,128,512]{2,1,0:T(8,128)(2,1)} %broadcast_in_dim.3), calls=%async_computation | async-start | bytes 524288 | tf_op jit(solution)/shard_map/all_to_all | solution.py:308
  23.7 8.0 %collective-permute-start.7 = (bf16[128,512]{1,0:T(8,128)(2,1)}, bf16[128,512]{1,0:T(8,128)(2,1)S(1)}, u32[]{:S(2)}, u32[]{:S(2)}) collective-permute-start(bf16[128,512]{1,0:T(8,128)(2,1)} %get-tuple-element.24), channel_id=1, source_target_pairs={{0,8},{1,9},{2,10},{3,11},{4,12},{5,13},{6,14},{7,15},{8,0},{9,1},... | collective-permute-start | bytes 393224 | tf_op jit(solution)/shard_map/ppermute | solution.py:273
  25.9 11.2 %collective-permute-start.8 = (bf16[128,512]{1,0:T(8,128)(2,1)S(1)}, bf16[128,512]{1,0:T(8,128)(2,1)S(1)}, u32[]{:S(2)}, u32[]{:S(2)}) collective-permute-start(bf16[128,512]{1,0:T(8,128)(2,1)S(1)} %get-tuple-element.25), channel_id=1, source_target_pairs={{0,12},{1,13},{2,14},{3,15},{4,8},{5,9},{6,10},{7,11},{8,4},{9,5},... | collective-permute-start | bytes 393224 | tf_op jit(solution)/shard_map/ppermute | solution.py:273
  28.0 9.5 %copy-start.1 = (bf16[128,512]{1,0:T(8,128)(2,1)S(1)}, bf16[128,512]{1,0:T(8,128)(2,1)}, u32[]{:S(2)}) copy-start(bf16[128,512]{1,0:T(8,128)(2,1)} %text_ref.1) | copy-start | bytes 393220
  28.1 9.0 %collective-permute-start.10 = (bf16[128,512]{1,0:T(8,128)(2,1)S(1)}, bf16[128,512]{1,0:T(8,128)(2,1)S(1)}, u32[]{:S(2)}, u32[]{:S(2)}) collective-permute-start(bf16[128,512]{1,0:T(8,128)(2,1)S(1)} %get-tuple-element.29), channel_id=1, source_target_pairs={{0,1},{1,0},{2,3},{3,2},{4,5},{5,4},{6,7},{7,6},{8,9},{9,8},{10,11... | collective-permute-start | bytes 393224 | tf_op jit(solution)/shard_map/ppermute | solution.py:273
  29.7 7.8 %collective-permute-start.11 = (bf16[128,512]{1,0:T(8,128)(2,1)S(1)}, bf16[128,512]{1,0:T(8,128)(2,1)S(1)}, u32[]{:S(2)}, u32[]{:S(2)}) collective-permute-start(bf16[128,512]{1,0:T(8,128)(2,1)S(1)} %get-tuple-element.30), channel_id=1, source_target_pairs={{0,2},{1,3},{2,0},{3,1},{4,6},{5,7},{6,4},{7,5},{8,10},{9,11},{10,... | collective-permute-start | bytes 393224 | tf_op jit(solution)/shard_map/ppermute | solution.py:273
  31.2 6.3 %collective-permute-start.12 = (bf16[128,512]{1,0:T(8,128)(2,1)S(1)}, bf16[128,512]{1,0:T(8,128)(2,1)S(1)}, u32[]{:S(2)}, u32[]{:S(2)}) collective-permute-start(bf16[128,512]{1,0:T(8,128)(2,1)S(1)} %get-tuple-element.31), channel_id=1, source_target_pairs={{0,3},{1,2},{2,1},{3,0},{4,7},{5,6},{6,5},{7,4},{8,11},{9,10},{10,... | collective-permute-start | bytes 393224 | tf_op jit(solution)/shard_map/ppermute | solution.py:273

commit v10 on v8

--- a/solution.py
+++ b/solution.py
@@ -290,12 +290,16 @@
         )
         far_parts = dict(zip([*early, *late], image_parts))
         came = [move(part, grp=-g) for g, part in enumerate(text_parts) if g]
-        far_order = [step for step in early if step[0]] + [step for step in early if step[1]] + list(late)
-        far_came = [move(far_parts[h, w], high=-h, low=-w) for h, w in far_order]
+        far_came = [move(p, high=-h, low=-w) for (h, w), p in far_parts.items() if h]
         near_parts = add_stacks([text_parts[0], *came], near_count)
         near_parts = [near_parts[0]] + [
             move(part, near=-n) for n, part in enumerate(near_parts) if n
         ]
+        low_parts = [p for (h, w), p in far_parts.items() if w and not h]
+        low_parts, far_came[:1], near_parts[:2] = lax.optimization_barrier(
+            (low_parts, far_came[:1], near_parts[:2])
+        )
+        far_came += [move(part, low=-w) for w, part in enumerate(low_parts, 1)]
         return finish(
             images,
             texts,

time: 37.5 us -> 38.9 us (1.037)
  waiting for transfers between devices: 10.6 us -> 13.8 us
  starting transfers between devices: 19.1 us -> 17.3 us
    ppermute x14, waiting for transfers between devices: 10.6 us -> 13.8 us  [move(): return lax.ppermute(value, AXES, perm)]
    ppermute x14, starting transfers between devices: 19.1 us -> 17.3 us  [move(): return lax.ppermute(value, AXES, perm)]
  transfers between devices with their start and end apart: 14 -> 14, of which waited for: 7 -> 8; matrix products, arithmetic and copies ran while one was open for 0% -> 0% of each run, Pallas kernels for 4% -> 4%
where the time goes in v10:
time: 38.9 us; the launch traced here: 38.7 us
  starting transfers between devices  17.3 us (44%)
  waiting for transfers between devices  13.8 us (35%)
  Pallas kernels  4.58 us (12%)
  between operations  2.02 us (5%)
  local copies, waits for them, and re-layouts  0.91 us (2%)
    ppermute x14, starting transfers between devices, move(): return lax.ppermute(value, AXES, perm)  17.3 us
    ppermute x14, waiting for transfers between devices, move(): return lax.ppermute(value, AXES, perm)  13.8 us
    pallas_call x6, Pallas kernels, call(): pl.pallas_call(kernel, out_shape=out_shape, in_specs=[VMEM] * len(operand...  3.52 us
    pallas_call x1, Pallas kernels, finish(): pl.pallas_call(functools.partial(finish_kernel, [side for side, _ in part...  1.07 us
    unnamed x6, local copies, waits for them, and re-layouts  0.91 us
  transfers between devices with their start and end apart: 14, of which 8 were waited for; matrix products, arithmetic and copies ran while one was open for 0% of the time, Pallas kernels for 4%

profile of v10, /device:TPU:0, one launch (start us, length us, event | category | flops | bytes accessed | tf_op | source)
XLA Modules:
  0.0 38.7 jit_solution(17208943076616618677)
XLA Ops:
  0.6 4.1 %collective-permute-start = (bf16[128,512]{1,0:T(8,128)(2,1)}, bf16[128,512]{1,0:T(8,128)(2,1)S(1)}, u32[]{:S(2)}, u32[]{:S(2)}) collective-permute-start(bf16[128,512]{1,0:T(8,128)(2,1)} %image_ref.1), channel_id=1, source_target_pairs={{0,8},{1,9},{2,10},{3,11},{4,12},{5,13},{6,14},{7,15},{8,0},{9,1},... | collective-permute-start | bytes 393224 | tf_op jit(solution)/shard_map/ppermute | solution.py:269
  4.7 1.6 %collective-permute-start.4 = (bf16[128,512]{1,0:T(8,128)(2,1)}, bf16[128,512]{1,0:T(8,128)(2,1)S(1)}, u32[]{:S(2)}, u32[]{:S(2)}) collective-permute-start(bf16[128,512]{1,0:T(8,128)(2,1)} %image_ref.1), channel_id=1, source_target_pairs={{0,4},{1,5},{2,6},{3,7},{4,0},{5,1},{6,2},{7,3},{8,12},{9,13},{10,... | collective-permute-start | bytes 393224 | tf_op jit(solution)/shard_map/ppermute | solution.py:269
  6.3 1.5 %collective-permute-start.2 = (bf16[128,512]{1,0:T(8,128)(2,1)}, bf16[128,512]{1,0:T(8,128)(2,1)S(1)}, u32[]{:S(2)}, u32[]{:S(2)}) collective-permute-start(bf16[128,512]{1,0:T(8,128)(2,1)} %text_ref.1), channel_id=1, source_target_pairs={{0,2},{1,3},{2,0},{3,1},{4,6},{5,7},{6,4},{7,5},{8,10},{9,11},{10,... | collective-permute-start | bytes 393224 | tf_op jit(solution)/shard_map/ppermute | solution.py:269
  7.8 1.5 %collective-permute-start.1 = (bf16[128,512]{1,0:T(8,128)(2,1)}, bf16[128,512]{1,0:T(8,128)(2,1)S(1)}, u32[]{:S(2)}, u32[]{:S(2)}) collective-permute-start(bf16[128,512]{1,0:T(8,128)(2,1)} %text_ref.1), channel_id=1, source_target_pairs={{0,1},{1,0},{2,3},{3,2},{4,5},{5,4},{6,7},{7,6},{8,9},{9,8},{10,11... | collective-permute-start | bytes 393224 | tf_op jit(solution)/shard_map/ppermute | solution.py:269
  9.3 0.5 %collective-permute-start.3 = (bf16[128,512]{1,0:T(8,128)(2,1)}, bf16[128,512]{1,0:T(8,128)(2,1)S(1)}, u32[]{:S(2)}, u32[]{:S(2)}) collective-permute-start(bf16[128,512]{1,0:T(8,128)(2,1)} %text_ref.1), channel_id=1, source_target_pairs={{0,3},{1,2},{2,1},{3,0},{4,7},{5,6},{6,5},{7,4},{8,11},{9,10},{10,... | collective-permute-start | bytes 393224 | tf_op jit(solution)/shard_map/ppermute | solution.py:269
  11.2 0.2 collective-permute-done.refs_1_
  11.4 0.7 %collective-permute-start.5 = (bf16[128,512]{1,0:T(8,128)(2,1)S(1)}, bf16[128,512]{1,0:T(8,128)(2,1)S(1)}, u32[]{:S(2)}, u32[]{:S(2)}) collective-permute-start(bf16[128,512]{1,0:T(8,128)(2,1)S(1)} %collective-permute-done.refs_1_), channel_id=1, source_target_pairs={{0,4},{1,5},{2,6},{3,7},{4,0},{5,1},{6,2},{7,3},{8,12},{9,13},{10,... | collective-permute-start | bytes 393224 | tf_op jit(solution)/shard_map/ppermute | solution.py:269
  12.1 0.9 %copy-done = bf16[128,512]{1,0:T(8,128)(2,1)S(1)} copy-done((bf16[128,512]{1,0:T(8,128)(2,1)S(1)}, bf16[128,512]{1,0:T(8,128)(2,1)}, u32[]{:S(2)}) %copy-start) | copy-done | bytes 131096
  13.1 0.7 %collective-permute-done.1.refs_1_ = bf16[128,512]{1,0:T(8,128)(2,1)S(1)} collective-permute-done((bf16[128,512]{1,0:T(8,128)(2,1)}, bf16[128,512]{1,0:T(8,128)(2,1)S(1)}, u32[]{:S(2)}, u32[]{:S(2)}) %collective-permute-start.1) | collective-permute-done | bytes 131104 | tf_op jit(solution)/shard_map/ppermute | solution.py:269
  13.8 1.9 %collective-permute-done.3.refs_3_ = bf16[128,512]{1,0:T(8,128)(2,1)S(1)} collective-permute-done((bf16[128,512]{1,0:T(8,128)(2,1)}, bf16[128,512]{1,0:T(8,128)(2,1)S(1)}, u32[]{:S(2)}, u32[]{:S(2)}) %collective-permute-start.3) | collective-permute-done | bytes 131104 | tf_op jit(solution)/shard_map/ppermute | solution.py:269
  16.0 1.1 %early_pairs.1 = (f32[512,512]{1,0:T(8,128)S(1)}, bf16[384,512]{1,0:T(8,128)(2,1)S(1)}, f32[384,512]{1,0:T(8,128)S(1)}) custom-call(f32[1,3]{1,0:T(1,128)S(1)} %maximum_bitcast_fusion.params_ref, bf16[512,512]{1,0:T(8,128)(2,1)S(1)} %stack_units.1.text_ref.own_text_ref, bf16[128,512]{1,0:T(8,128)(2,1)S(1)} %copy-done.2, ...), custom_call_target="tpu_custom_call" | custom-call | flops 603979776 | bytes 3145740 | tf_op jit(solution)/shard_map/early_pairs/pallas_call | solution.py:28
  17.3 0.6 %collective-permute-done.6.refs_0_ = bf16[512,512]{1,0:T(8,128)(2,1)S(1)} collective-permute-done((bf16[512,512]{1,0:T(8,128)(2,1)S(1)}, bf16[512,512]{1,0:T(8,128)(2,1)S(1)}, u32[]{:S(2)}, u32[]{:S(2)}) %collective-permute-start.6) | collective-permute-done | bytes 524320 | tf_op jit(solution)/shard_map/ppermute | solution.py:269
  17.9 1.9 %rest_pairs.1 = (f32[512,512]{1,0:T(8,128)S(1)}, bf16[512,512]{1,0:T(8,128)(2,1)S(1)}, f32[128,512]{1,0:T(8,128)S(1)}, bf16[128,512]{1,0:T(8,128)(2,1)S(1)}, bf1...) custom-call(f32[1,3]{1,0:T(1,128)S(1)} %maximum_bitcast_fusion.params_ref, ...), custom_call_target="tpu_custom_call" | custom-call | flops 1006632960 | bytes 5636108 | tf_op jit(solution)/shard_map/rest_pairs/pallas_call | solution.py:28
  19.8 0.2 collective-permute-start.8
  20.0 1.2 %collective-permute-start.7 = (bf16[128,512]{1,0:T(8,128)(2,1)S(1)}, bf16[128,512]{1,0:T(8,128)(2,1)S(1)}, u32[]{:S(2)}, u32[]{:S(2)}) collective-permute-start(bf16[128,512]{1,0:T(8,128)(2,1)S(1)} %get-tuple-element.28), channel_id=1, source_target_pairs={{0,8},{1,9},{2,10},{3,11},{4,12},{5,13},{6,14},{7,15},{8,0},{9,1},... | collective-permute-start | bytes 393224 | tf_op jit(solution)/shard_map/ppermute | solution.py:269
  21.2 0.6 %collective-permute-done.8.refs_1_ = bf16[512,512]{1,0:T(8,128)(2,1)S(1)} collective-permute-done((bf16[512,512]{1,0:T(8,128)(2,1)S(1)}, bf16[512,512]{1,0:T(8,128)(2,1)S(1)}, u32[]{:S(2)}, u32[]{:S(2)}) %collective-permute-start.8) | collective-permute-done | bytes 524320 | tf_op jit(solution)/shard_map/ppermute | solution.py:269
  21.9 1.0 %collective-permute-start.9 = (bf16[128,512]{1,0:T(8,128)(2,1)S(1)}, bf16[128,512]{1,0:T(8,128)(2,1)S(1)}, u32[]{:S(2)}, u32[]{:S(2)}) collective-permute-start(bf16[128,512]{1,0:T(8,128)(2,1)S(1)} %get-tuple-element.32), channel_id=1, source_target_pairs={{0,1},{1,0},{2,3},{3,2},{4,5},{5,4},{6,7},{7,6},{8,9},{9,8},{10,11... | collective-permute-start | bytes 393224 | tf_op jit(solution)/shard_map/ppermute | solution.py:269
  22.9 3.0 %collective-permute-start.10 = (bf16[128,512]{1,0:T(8,128)(2,1)S(1)}, bf16[128,512]{1,0:T(8,128)(2,1)S(1)}, u32[]{:S(2)}, u32[]{:S(2)}) collective-permute-start(bf16[128,512]{1,0:T(8,128)(2,1)S(1)} %get-tuple-element.34), channel_id=1, source_target_pairs={{0,12},{1,13},{2,14},{3,15},{4,8},{5,9},{6,10},{7,11},{8,4},{9,5},... | collective-permute-start | bytes 393224 | tf_op jit(solution)/shard_map/ppermute | solution.py:269
  25.9 1.5 %collective-permute-start.12 = (bf16[128,512]{1,0:T(8,128)(2,1)S(1)}, bf16[128,512]{1,0:T(8,128)(2,1)S(1)}, u32[]{:S(2)}, u32[]{:S(2)}) collective-permute-start(bf16[128,512]{1,0:T(8,128)(2,1)S(1)} %get-tuple-element.38), channel_id=1, source_target_pairs={{0,2},{1,3},{2,0},{3,1},{4,6},{5,7},{6,4},{7,5},{8,10},{9,11},{10,... | collective-permute-start | bytes 393224 | tf_op jit(solution)/shard_map/ppermute | solution.py:269
  27.4 0.5 %collective-permute-start.13 = (bf16[128,512]{1,0:T(8,128)(2,1)S(1)}, bf16[128,512]{1,0:T(8,128)(2,1)S(1)}, u32[]{:S(2)}, u32[]{:S(2)}) collective-permute-start(bf16[128,512]{1,0:T(8,128)(2,1)S(1)} %get-tuple-element.39), channel_id=1, source_target_pairs={{0,3},{1,2},{2,1},{3,0},{4,7},{5,6},{6,5},{7,4},{8,11},{9,10},{10,... | collective-permute-start | bytes 393224 | tf_op jit(solution)/shard_map/ppermute | solution.py:269
  27.9 4.4 %collective-permute-done.7.refs_1_ = bf16[128,512]{1,0:T(8,128)(2,1)S(1)} collective-permute-done((bf16[128,512]{1,0:T(8,128)(2,1)S(1)}, bf16[128,512]{1,0:T(8,128)(2,1)S(1)}, u32[]{:S(2)}, u32[]{:S(2)}) %collective-permute-start.7) | collective-permute-done | bytes 131104 | tf_op jit(solution)/shard_map/ppermute | solution.py:269
  32.2 1.4 %collective-permute-done.12.refs_6_ = bf16[128,512]{1,0:T(8,128)(2,1)S(1)} collective-permute-done((bf16[128,512]{1,0:T(8,128)(2,1)S(1)}, bf16[128,512]{1,0:T(8,128)(2,1)S(1)}, u32[]{:S(2)}, u32[]{:S(2)}) %collective-permute-start.12) | collective-permute-done | bytes 131104 | tf_op jit(solution)/shard_map/ppermute | solution.py:269
  33.7 4.0 %collective-permute-done.11.refs_3_ = bf16[128,512]{1,0:T(8,128)(2,1)S(1)} collective-permute-done((bf16[128,512]{1,0:T(8,128)(2,1)S(1)}, bf16[128,512]{1,0:T(8,128)(2,1)S(1)}, u32[]{:S(2)}, u32[]{:S(2)}) %collective-permute-start.11) | collective-permute-done | bytes 131104 | tf_op jit(solution)/shard_map/ppermute | solution.py:269
  37.6 1.1 %finish.1 = (f32[128,512]{1,0:T(8,128)}, f32[128,512]{1,0:T(8,128)}) custom-call(bf16[128,512]{1,0:T(8,128)(2,1)S(1)} %copy-done.2, bf16[128,512]{1,0:T(8,128)(2,1)S(1)} %copy-done.1, f32[128,512]{1,0:T(8,128)S(1)} %get-tuple-element.26.refs_0_, bf16[128,512]{1,0:T(8,128)(2,1)S(1)} %collective-permute-done.7.refs_1_, ...), custom_call_target="tpu_custom_call" | custom-call | flops 5242880 | bytes 1572864 | tf_op jit(solution)/shard_map/finish/pallas_call | solution.py:219
  (18 shorter events, 0.7 us)
Async XLA Ops:
  0.6 10.7 %collective-permute-start = (bf16[128,512]{1,0:T(8,128)(2,1)}, bf16[128,512]{1,0:T(8,128)(2,1)S(1)}, u32[]{:S(2)}, u32[]{:S(2)}) collective-permute-start(bf16[128,512]{1,0:T(8,128)(2,1)} %image_ref.1), channel_id=1, source_target_pairs={{0,8},{1,9},{2,10},{3,11},{4,12},{5,13},{6,14},{7,15},{8,0},{9,1},... | collective-permute-start | bytes 393224 | tf_op jit(solution)/shard_map/ppermute | solution.py:269
  4.7 11.3 %collective-permute-start.4 = (bf16[128,512]{1,0:T(8,128)(2,1)}, bf16[128,512]{1,0:T(8,128)(2,1)S(1)}, u32[]{:S(2)}, u32[]{:S(2)}) collective-permute-start(bf16[128,512]{1,0:T(8,128)(2,1)} %image_ref.1), channel_id=1, source_target_pairs={{0,4},{1,5},{2,6},{3,7},{4,0},{5,1},{6,2},{7,3},{8,12},{9,13},{10,... | collective-permute-start | bytes 393224 | tf_op jit(solution)/shard_map/ppermute | solution.py:269
  6.3 6.8 %collective-permute-start.2 = (bf16[128,512]{1,0:T(8,128)(2,1)}, bf16[128,512]{1,0:T(8,128)(2,1)S(1)}, u32[]{:S(2)}, u32[]{:S(2)}) collective-permute-start(bf16[128,512]{1,0:T(8,128)(2,1)} %text_ref.1), channel_id=1, source_target_pairs={{0,2},{1,3},{2,0},{3,1},{4,6},{5,7},{6,4},{7,5},{8,10},{9,11},{10,... | collective-permute-start | bytes 393224 | tf_op jit(solution)/shard_map/ppermute | solution.py:269
  7.8 6.0 %collective-permute-start.1 = (bf16[128,512]{1,0:T(8,128)(2,1)}, bf16[128,512]{1,0:T(8,128)(2,1)S(1)}, u32[]{:S(2)}, u32[]{:S(2)}) collective-permute-start(bf16[128,512]{1,0:T(8,128)(2,1)} %text_ref.1), channel_id=1, source_target_pairs={{0,1},{1,0},{2,3},{3,2},{4,5},{5,4},{6,7},{7,6},{8,9},{9,8},{10,11... | collective-permute-start | bytes 393224 | tf_op jit(solution)/shard_map/ppermute | solution.py:269
  9.3 6.4 %collective-permute-start.3 = (bf16[128,512]{1,0:T(8,128)(2,1)}, bf16[128,512]{1,0:T(8,128)(2,1)S(1)}, u32[]{:S(2)}, u32[]{:S(2)}) collective-permute-start(bf16[128,512]{1,0:T(8,128)(2,1)} %text_ref.1), channel_id=1, source_target_pairs={{0,3},{1,2},{2,1},{3,0},{4,7},{5,6},{6,5},{7,4},{8,11},{9,10},{10,... | collective-permute-start | bytes 393224 | tf_op jit(solution)/shard_map/ppermute | solution.py:269
  11.4 5.8 %collective-permute-start.5 = (bf16[128,512]{1,0:T(8,128)(2,1)S(1)}, bf16[128,512]{1,0:T(8,128)(2,1)S(1)}, u32[]{:S(2)}, u32[]{:S(2)}) collective-permute-start(bf16[128,512]{1,0:T(8,128)(2,1)S(1)} %collective-permute-done.refs_1_), channel_id=1, source_target_pairs={{0,4},{1,5},{2,6},{3,7},{4,0},{5,1},{6,2},{7,3},{8,12},{9,13},{10,... | collective-permute-start | bytes 393224 | tf_op jit(solution)/shard_map/ppermute | solution.py:269
  12.1 0.9 %copy-start = (bf16[128,512]{1,0:T(8,128)(2,1)S(1)}, bf16[128,512]{1,0:T(8,128)(2,1)}, u32[]{:S(2)}) copy-start(bf16[128,512]{1,0:T(8,128)(2,1)} %text_ref.1) | copy-start | bytes 393220
  13.1 2.9 %copy-start.2 = (bf16[128,512]{1,0:T(8,128)(2,1)S(1)}, bf16[128,512]{1,0:T(8,128)(2,1)}, u32[]{:S(2)}) copy-start(bf16[128,512]{1,0:T(8,128)(2,1)} %image_ref.1) | copy-start | bytes 393220
  15.9 2.0 %collective-permute-start.6 = (bf16[512,512]{1,0:T(8,128)(2,1)S(1)}, bf16[512,512]{1,0:T(8,128)(2,1)S(1)}, u32[]{:S(2)}, u32[]{:S(2)}) collective-permute-start(bf16[512,512]{1,0:T(8,128)(2,1)S(1)} %stack_units.1.text_ref.own_text_ref), channel_id=1, source_target_pairs={{0,16},{1,17},{2,18},{3,19},{4,20},{5,21},{6,22},{7,23},{8,24},{9,... | collective-permute-start | bytes 1572872 | tf_op jit(solution)/shard_map/ppermute | solution.py:269
  19.8 2.0 %collective-permute-start.8 = (bf16[512,512]{1,0:T(8,128)(2,1)S(1)}, bf16[512,512]{1,0:T(8,128)(2,1)S(1)}, u32[]{:S(2)}, u32[]{:S(2)}) collective-permute-start(bf16[512,512]{1,0:T(8,128)(2,1)S(1)} %get-tuple-element.30), channel_id=1, source_target_pairs={{0,16},{1,17},{2,18},{3,19},{4,20},{5,21},{6,22},{7,23},{8,24},{9,... | collective-permute-start | bytes 1572872 | tf_op jit(solution)/shard_map/ppermute | solution.py:269
  20.0 12.2 %collective-permute-start.7 = (bf16[128,512]{1,0:T(8,128)(2,1)S(1)}, bf16[128,512]{1,0:T(8,128)(2,1)S(1)}, u32[]{:S(2)}, u32[]{:S(2)}) collective-permute-start(bf16[128,512]{1,0:T(8,128)(2,1)S(1)} %get-tuple-element.28), channel_id=1, source_target_pairs={{0,8},{1,9},{2,10},{3,11},{4,12},{5,13},{6,14},{7,15},{8,0},{9,1},... | collective-permute-start | bytes 393224 | tf_op jit(solution)/shard_map/ppermute | solution.py:269
  21.8 15.9 %copy-start.1 = (bf16[128,512]{1,0:T(8,128)(2,1)S(1)}, bf16[128,512]{1,0:T(8,128)(2,1)}, u32[]{:S(2)}) copy-start(bf16[128,512]{1,0:T(8,128)(2,1)} %text_ref.1) | copy-start | bytes 393220
  21.9 10.3 %collective-permute-start.9 = (bf16[128,512]{1,0:T(8,128)(2,1)S(1)}, bf16[128,512]{1,0:T(8,128)(2,1)S(1)}, u32[]{:S(2)}, u32[]{:S(2)}) collective-permute-start(bf16[128,512]{1,0:T(8,128)(2,1)S(1)} %get-tuple-element.32), channel_id=1, source_target_pairs={{0,1},{1,0},{2,3},{3,2},{4,5},{5,4},{6,7},{7,6},{8,9},{9,8},{10,11... | collective-permute-start | bytes 393224 | tf_op jit(solution)/shard_map/ppermute | solution.py:269
  22.9 9.4 %collective-permute-start.10 = (bf16[128,512]{1,0:T(8,128)(2,1)S(1)}, bf16[128,512]{1,0:T(8,128)(2,1)S(1)}, u32[]{:S(2)}, u32[]{:S(2)}) collective-permute-start(bf16[128,512]{1,0:T(8,128)(2,1)S(1)} %get-tuple-element.34), channel_id=1, source_target_pairs={{0,12},{1,13},{2,14},{3,15},{4,8},{5,9},{6,10},{7,11},{8,4},{9,5},... | collective-permute-start | bytes 393224 | tf_op jit(solution)/shard_map/ppermute | solution.py:269
  25.9 7.8 %collective-permute-start.12 = (bf16[128,512]{1,0:T(8,128)(2,1)S(1)}, bf16[128,512]{1,0:T(8,128)(2,1)S(1)}, u32[]{:S(2)}, u32[]{:S(2)}) collective-permute-start(bf16[128,512]{1,0:T(8,128)(2,1)S(1)} %get-tuple-element.38), channel_id=1, source_target_pairs={{0,2},{1,3},{2,0},{3,1},{4,6},{5,7},{6,4},{7,5},{8,10},{9,11},{10,... | collective-permute-start | bytes 393224 | tf_op jit(solution)/shard_map/ppermute | solution.py:269
  27.4 6.3 %collective-permute-start.13 = (bf16[128,512]{1,0:T(8,128)(2,1)S(1)}, bf16[128,512]{1,0:T(8,128)(2,1)S(1)}, u32[]{:S(2)}, u32[]{:S(2)}) collective-permute-start(bf16[128,512]{1,0:T(8,128)(2,1)S(1)} %get-tuple-element.39), channel_id=1, source_target_pairs={{0,3},{1,2},{2,1},{3,0},{4,7},{5,6},{6,5},{7,4},{8,11},{9,10},{10,... | collective-permute-start | bytes 393224 | tf_op jit(solution)/shard_map/ppermute | solution.py:269
  32.2 5.4 %collective-permute-start.11 = (bf16[128,512]{1,0:T(8,128)(2,1)S(1)}, bf16[128,512]{1,0:T(8,128)(2,1)S(1)}, u32[]{:S(2)}, u32[]{:S(2)}) collective-permute-start(bf16[128,512]{1,0:T(8,128)(2,1)S(1)} %get-tuple-element.35), channel_id=1, source_target_pairs={{0,4},{1,5},{2,6},{3,7},{4,0},{5,1},{6,2},{7,3},{8,12},{9,13},{10,... | collective-permute-start | bytes 393224 | tf_op jit(solution)/shard_map/ppermute | solution.py:269

commit v11 on v8

--- a/solution.py
+++ b/solution.py
@@ -132,7 +132,7 @@
         ref[...] = total[a * rows:(a + 1) * rows, :].astype(ref.dtype)
 
 
-def pair_terms(params, early, late, texts):
+def pair_terms(params, early, late, texts, image_types):
     rows, width = early[0].shape
     early_rows, late_rows = rows * len(early), rows * len(late)
     own, others = texts[0], texts[1:]
@@ -157,8 +157,7 @@
         functools.partial(rest_pairs_kernel, len(others)),
         [jax.ShapeDtypeStruct(own.shape, jnp.float32)]
         + [jax.ShapeDtypeStruct(t.shape, jnp.bfloat16) for t in others]
-        + [jax.ShapeDtypeStruct((rows, width), jnp.float32)]
-        + [jax.ShapeDtypeStruct((rows, width), jnp.bfloat16)] * (len(early) + len(late) - 1),
+        + [jax.ShapeDtypeStruct((rows, width), t) for t in image_types],
         [params, early_units, total, own, own_add, late_units, *others],
         name="rest_pairs",
         **cost(late_rows * own.shape[0] + (early_rows + late_rows) * other_rows),
@@ -187,6 +186,20 @@
         flops=len(parts) * parts[0].size,
         name="add_stacks",
     )
+
+
+def add_parts_kernel(*refs):
+    total = refs[0][...].astype(jnp.float32)
+    for part in refs[1:-1]:
+        total = total + part[...].astype(jnp.float32)
+    refs[-1][...] = total.astype(refs[-1].dtype)
+
+
+def add_parts(parts):
+    out = jax.ShapeDtypeStruct(parts[0].shape, jnp.bfloat16)
+    return call(
+        add_parts_kernel, [out], parts, flops=len(parts) * out.size, name="add_parts"
+    )[0]
 
 
 def finish_kernel(sides, image_ref, text_ref, *refs):
@@ -285,22 +298,36 @@
         near_rows = [units([texts], "own_units")] + [move(texts, near=n) for n in range(1, near_count)]
         own_stack = stack_units(near_rows)
         stacks = [own_stack] + [move(own_stack, grp=g) for g in range(1, grp_count)]
+        far_steps = [*early, *late]
+        image_types = [jnp.bfloat16 if w else jnp.float32 for _, w in far_steps]
         image_parts, text_parts = pair_terms(
-            params, list(early.values()), list(late.values()), stacks
+            params, list(early.values()), list(late.values()), stacks, image_types
         )
-        far_parts = dict(zip([*early, *late], image_parts))
+        far_parts = dict(zip(far_steps, image_parts))
+        passed = {
+            h: [move(far_parts[h, w], low=-w) for w in range(1, low_count)]
+            for h in range(1, high_count)
+        }
         came = [move(part, grp=-g) for g, part in enumerate(text_parts) if g]
-        far_order = [step for step in early if step[0]] + [step for step in early if step[1]] + list(late)
-        far_came = [move(far_parts[h, w], high=-h, low=-w) for h, w in far_order]
-        near_parts = add_stacks([text_parts[0], *came], near_count)
+        near_parts = list(add_stacks([text_parts[0], *came], near_count))
+        high_parts = []
+        for h in range(1, high_count):
+            passed[h], near_parts[0] = lax.optimization_barrier((passed[h], near_parts[0]))
+            high_parts.append(move(add_parts([far_parts[h, 0], *passed[h]]), high=-h))
         near_parts = [near_parts[0]] + [
             move(part, near=-n) for n, part in enumerate(near_parts) if n
         ]
+        low_parts = [far_parts[0, w] for w in range(1, low_count)]
+        low_parts, near_parts[:2] = lax.optimization_barrier((low_parts, near_parts[:2]))
+        low_parts = [move(part, low=-w) for w, part in enumerate(low_parts, 1)]
         return finish(
             images,
             texts,
-            [(0, part) for part in [far_parts[0, 0]] + far_came]
-            + [(1, part) for part in near_parts],
+            [(0, far_parts[0, 0])]
+            + [(1, part) for part in near_parts[:3]]
+            + [(0, part) for part in high_parts]
+            + [(1, part) for part in near_parts[3:]]
+            + [(0, part) for part in low_parts],
         )
 
     in_specs = (P(AXES, None), P(AXES, None), P(), P())

time: 37.5 us -> 38.3 us (1.021)
  waiting for transfers between devices: 10.6 us -> 12.9 us
  starting transfers between devices: 19.1 us -> 17.6 us
    ppermute x14, waiting for transfers between devices: 10.6 us -> 12.9 us  [move(): return lax.ppermute(value, AXES, perm)]
    ppermute x14, starting transfers between devices: 19.1 us -> 17.6 us  [move(): return lax.ppermute(value, AXES, perm)]
    pallas_call x6 -> x7, Pallas kernels: 3.53 us -> 3.55 us  [call(): pl.pallas_call(kernel, out_shape=out_shape, in_specs=[VMEM] * len(operand...]
  transfers between devices with their start and end apart: 14 -> 14, of which waited for: 7 -> 9; matrix products, arithmetic and copies ran while one was open for 0% -> 0% of each run, Pallas kernels for 4% -> 4%
where the time goes in v11:
time: 38.3 us; the launch traced here: 38.1 us
  starting transfers between devices  17.6 us (46%)
  waiting for transfers between devices  12.9 us (34%)
  Pallas kernels  4.6 us (12%)
  between operations  2.02 us (5%)
  local copies, waits for them, and re-layouts  0.91 us (2%)
    ppermute x14, starting transfers between devices, move(): return lax.ppermute(value, AXES, perm)  17.6 us
    ppermute x14, waiting for transfers between devices, move(): return lax.ppermute(value, AXES, perm)  12.9 us
    pallas_call x7, Pallas kernels, call(): pl.pallas_call(kernel, out_shape=out_shape, in_specs=[VMEM] * len(operand...  3.55 us
    pallas_call x1, Pallas kernels, finish(): pl.pallas_call(functools.partial(finish_kernel, [side for side, _ in part...  1.06 us
    unnamed x6, local copies, waits for them, and re-layouts  0.91 us
  transfers between devices with their start and end apart: 14, of which 9 were waited for; matrix products, arithmetic and copies ran while one was open for 0% of the time, Pallas kernels for 4%

profile of v11, /device:TPU:0, one launch (start us, length us, event | category | flops | bytes accessed | tf_op | source)
XLA Modules:
  0.0 38.1 jit_solution(7701475712191633262)
XLA Ops:
  0.6 4.1 %collective-permute-start = (bf16[128,512]{1,0:T(8,128)(2,1)}, bf16[128,512]{1,0:T(8,128)(2,1)S(1)}, u32[]{:S(2)}, u32[]{:S(2)}) collective-permute-start(bf16[128,512]{1,0:T(8,128)(2,1)} %image_ref.1), channel_id=1, source_target_pairs={{0,8},{1,9},{2,10},{3,11},{4,12},{5,13},{6,14},{7,15},{8,0},{9,1},... | collective-permute-start | bytes 393224 | tf_op jit(solution)/shard_map/ppermute | solution.py:282
  4.7 1.6 %collective-permute-start.4 = (bf16[128,512]{1,0:T(8,128)(2,1)}, bf16[128,512]{1,0:T(8,128)(2,1)S(1)}, u32[]{:S(2)}, u32[]{:S(2)}) collective-permute-start(bf16[128,512]{1,0:T(8,128)(2,1)} %image_ref.1), channel_id=1, source_target_pairs={{0,4},{1,5},{2,6},{3,7},{4,0},{5,1},{6,2},{7,3},{8,12},{9,13},{10,... | collective-permute-start | bytes 393224 | tf_op jit(solution)/shard_map/ppermute | solution.py:282
  6.3 1.5 %collective-permute-start.2 = (bf16[128,512]{1,0:T(8,128)(2,1)}, bf16[128,512]{1,0:T(8,128)(2,1)S(1)}, u32[]{:S(2)}, u32[]{:S(2)}) collective-permute-start(bf16[128,512]{1,0:T(8,128)(2,1)} %text_ref.1), channel_id=1, source_target_pairs={{0,2},{1,3},{2,0},{3,1},{4,6},{5,7},{6,4},{7,5},{8,10},{9,11},{10,... | collective-permute-start | bytes 393224 | tf_op jit(solution)/shard_map/ppermute | solution.py:282
  7.8 1.5 %collective-permute-start.1 = (bf16[128,512]{1,0:T(8,128)(2,1)}, bf16[128,512]{1,0:T(8,128)(2,1)S(1)}, u32[]{:S(2)}, u32[]{:S(2)}) collective-permute-start(bf16[128,512]{1,0:T(8,128)(2,1)} %text_ref.1), channel_id=1, source_target_pairs={{0,1},{1,0},{2,3},{3,2},{4,5},{5,4},{6,7},{7,6},{8,9},{9,8},{10,11... | collective-permute-start | bytes 393224 | tf_op jit(solution)/shard_map/ppermute | solution.py:282
  9.3 0.5 %collective-permute-start.3 = (bf16[128,512]{1,0:T(8,128)(2,1)}, bf16[128,512]{1,0:T(8,128)(2,1)S(1)}, u32[]{:S(2)}, u32[]{:S(2)}) collective-permute-start(bf16[128,512]{1,0:T(8,128)(2,1)} %text_ref.1), channel_id=1, source_target_pairs={{0,3},{1,2},{2,1},{3,0},{4,7},{5,6},{6,5},{7,4},{8,11},{9,10},{10,... | collective-permute-start | bytes 393224 | tf_op jit(solution)/shard_map/ppermute | solution.py:282
  11.4 0.7 %collective-permute-start.5 = (bf16[128,512]{1,0:T(8,128)(2,1)S(1)}, bf16[128,512]{1,0:T(8,128)(2,1)S(1)}, u32[]{:S(2)}, u32[]{:S(2)}) collective-permute-start(bf16[128,512]{1,0:T(8,128)(2,1)S(1)} %collective-permute-done.refs_1_), channel_id=1, source_target_pairs={{0,4},{1,5},{2,6},{3,7},{4,0},{5,1},{6,2},{7,3},{8,12},{9,13},{10,... | collective-permute-start | bytes 393224 | tf_op jit(solution)/shard_map/ppermute | solution.py:282
  12.1 0.9 %copy-done = bf16[128,512]{1,0:T(8,128)(2,1)S(1)} copy-done((bf16[128,512]{1,0:T(8,128)(2,1)S(1)}, bf16[128,512]{1,0:T(8,128)(2,1)}, u32[]{:S(2)}) %copy-start) | copy-done | bytes 131096
  13.1 0.7 %collective-permute-done.1.refs_1_ = bf16[128,512]{1,0:T(8,128)(2,1)S(1)} collective-permute-done((bf16[128,512]{1,0:T(8,128)(2,1)}, bf16[128,512]{1,0:T(8,128)(2,1)S(1)}, u32[]{:S(2)}, u32[]{:S(2)}) %collective-permute-start.1) | collective-permute-done | bytes 131104 | tf_op jit(solution)/shard_map/ppermute | solution.py:282
  13.8 1.9 %collective-permute-done.3.refs_3_ = bf16[128,512]{1,0:T(8,128)(2,1)S(1)} collective-permute-done((bf16[128,512]{1,0:T(8,128)(2,1)}, bf16[128,512]{1,0:T(8,128)(2,1)S(1)}, u32[]{:S(2)}, u32[]{:S(2)}) %collective-permute-start.3) | collective-permute-done | bytes 131104 | tf_op jit(solution)/shard_map/ppermute | solution.py:282
  16.0 1.1 %early_pairs.1 = (f32[512,512]{1,0:T(8,128)S(1)}, bf16[384,512]{1,0:T(8,128)(2,1)S(1)}, f32[384,512]{1,0:T(8,128)S(1)}) custom-call(f32[1,3]{1,0:T(1,128)S(1)} %maximum_bitcast_fusion.params_ref, bf16[512,512]{1,0:T(8,128)(2,1)S(1)} %stack_units.1.text_ref.own_text_ref, bf16[128,512]{1,0:T(8,128)(2,1)S(1)} %copy-done.2, ...), custom_call_target="tpu_custom_call" | custom-call | flops 603979776 | bytes 3145740 | tf_op jit(solution)/shard_map/early_pairs/pallas_call | solution.py:28
  17.3 0.6 %collective-permute-done.6.refs_0_ = bf16[512,512]{1,0:T(8,128)(2,1)S(1)} collective-permute-done((bf16[512,512]{1,0:T(8,128)(2,1)S(1)}, bf16[512,512]{1,0:T(8,128)(2,1)S(1)}, u32[]{:S(2)}, u32[]{:S(2)}) %collective-permute-start.6) | collective-permute-done | bytes 524320 | tf_op jit(solution)/shard_map/ppermute | solution.py:282
  17.9 1.9 %rest_pairs.1 = (f32[512,512]{1,0:T(8,128)S(1)}, bf16[512,512]{1,0:T(8,128)(2,1)S(1)}, f32[128,512]{1,0:T(8,128)S(1)}, f32[128,512]{1,0:T(8,128)S(1)}, bf16[128,...) custom-call(f32[1,3]{1,0:T(1,128)S(1)} %maximum_bitcast_fusion.params_ref, ...), custom_call_target="tpu_custom_call" | custom-call | flops 1006632960 | bytes 5767180 | tf_op jit(solution)/shard_map/rest_pairs/pallas_call | solution.py:28
  20.0 0.5 %collective-permute-start.7 = (bf16[128,512]{1,0:T(8,128)(2,1)S(1)}, bf16[128,512]{1,0:T(8,128)(2,1)S(1)}, u32[]{:S(2)}, u32[]{:S(2)}) collective-permute-start(bf16[128,512]{1,0:T(8,128)(2,1)S(1)} %get-tuple-element.29), channel_id=1, source_target_pairs={{0,4},{1,5},{2,6},{3,7},{4,0},{5,1},{6,2},{7,3},{8,12},{9,13},{10,... | collective-permute-start | bytes 393224 | tf_op jit(solution)/shard_map/ppermute | solution.py:282
  20.4 1.3 %collective-permute-done.8.refs_1_ = bf16[512,512]{1,0:T(8,128)(2,1)S(1)} collective-permute-done((bf16[512,512]{1,0:T(8,128)(2,1)S(1)}, bf16[512,512]{1,0:T(8,128)(2,1)S(1)}, u32[]{:S(2)}, u32[]{:S(2)}) %collective-permute-start.8) | collective-permute-done | bytes 524320 | tf_op jit(solution)/shard_map/ppermute | solution.py:282
  21.9 1.0 %collective-permute-start.9 = (bf16[128,512]{1,0:T(8,128)(2,1)S(1)}, bf16[128,512]{1,0:T(8,128)(2,1)S(1)}, u32[]{:S(2)}, u32[]{:S(2)}) collective-permute-start(bf16[128,512]{1,0:T(8,128)(2,1)S(1)} %get-tuple-element.34), channel_id=1, source_target_pairs={{0,1},{1,0},{2,3},{3,2},{4,5},{5,4},{6,7},{7,6},{8,9},{9,8},{10,11... | collective-permute-start | bytes 393224 | tf_op jit(solution)/shard_map/ppermute | solution.py:282
  22.9 2.9 %collective-permute-done.7.refs_1_ = bf16[128,512]{1,0:T(8,128)(2,1)S(1)} collective-permute-done((bf16[128,512]{1,0:T(8,128)(2,1)S(1)}, bf16[128,512]{1,0:T(8,128)(2,1)S(1)}, u32[]{:S(2)}, u32[]{:S(2)}) %collective-permute-start.7) | collective-permute-done | bytes 131104 | tf_op jit(solution)/shard_map/ppermute | solution.py:282
  25.8 1.3 %collective-permute-start.11 = (bf16[128,512]{1,0:T(8,128)(2,1)S(1)}, bf16[128,512]{1,0:T(8,128)(2,1)S(1)}, u32[]{:S(2)}, u32[]{:S(2)}) collective-permute-start(bf16[128,512]{1,0:T(8,128)(2,1)S(1)} %add_parts.1), channel_id=1, source_target_pairs={{0,8},{1,9},{2,10},{3,11},{4,12},{5,13},{6,14},{7,15},{8,0},{9,1},... | collective-permute-start | bytes 393224 | tf_op jit(solution)/shard_map/ppermute | solution.py:282
  27.1 1.5 %collective-permute-start.10 = (bf16[128,512]{1,0:T(8,128)(2,1)S(1)}, bf16[128,512]{1,0:T(8,128)(2,1)S(1)}, u32[]{:S(2)}, u32[]{:S(2)}) collective-permute-start(bf16[128,512]{1,0:T(8,128)(2,1)S(1)} %get-tuple-element.37), channel_id=1, source_target_pairs={{0,2},{1,3},{2,0},{3,1},{4,6},{5,7},{6,4},{7,5},{8,10},{9,11},{10,... | collective-permute-start | bytes 393224 | tf_op jit(solution)/shard_map/ppermute | solution.py:282
  28.7 1.4 %collective-permute-start.12 = (bf16[128,512]{1,0:T(8,128)(2,1)S(1)}, bf16[128,512]{1,0:T(8,128)(2,1)S(1)}, u32[]{:S(2)}, u32[]{:S(2)}) collective-permute-start(bf16[128,512]{1,0:T(8,128)(2,1)S(1)} %get-tuple-element.40), channel_id=1, source_target_pairs={{0,3},{1,2},{2,1},{3,0},{4,7},{5,6},{6,5},{7,4},{8,11},{9,10},{10,... | collective-permute-start | bytes 393224 | tf_op jit(solution)/shard_map/ppermute | solution.py:282
  30.1 1.7 %collective-permute-start.13 = (bf16[128,512]{1,0:T(8,128)(2,1)S(1)}, bf16[128,512]{1,0:T(8,128)(2,1)S(1)}, u32[]{:S(2)}, u32[]{:S(2)}) collective-permute-start(bf16[128,512]{1,0:T(8,128)(2,1)S(1)} %get-tuple-element.41), channel_id=1, source_target_pairs={{0,4},{1,5},{2,6},{3,7},{4,0},{5,1},{6,2},{7,3},{8,12},{9,13},{10,... | collective-permute-start | bytes 393224 | tf_op jit(solution)/shard_map/ppermute | solution.py:282
  31.8 2.7 %collective-permute-done.11.refs_4_ = bf16[128,512]{1,0:T(8,128)(2,1)S(1)} collective-permute-done((bf16[128,512]{1,0:T(8,128)(2,1)S(1)}, bf16[128,512]{1,0:T(8,128)(2,1)S(1)}, u32[]{:S(2)}, u32[]{:S(2)}) %collective-permute-start.11) | collective-permute-done | bytes 131104 | tf_op jit(solution)/shard_map/ppermute | solution.py:282
  34.5 0.4 collective-permute-done.10.refs_3_
  34.9 2.1 %collective-permute-done.13.refs_6_ = bf16[128,512]{1,0:T(8,128)(2,1)S(1)} collective-permute-done((bf16[128,512]{1,0:T(8,128)(2,1)S(1)}, bf16[128,512]{1,0:T(8,128)(2,1)S(1)}, u32[]{:S(2)}, u32[]{:S(2)}) %collective-permute-start.13) | collective-permute-done | bytes 131104 | tf_op jit(solution)/shard_map/ppermute | solution.py:282
  37.0 1.1 %finish.1 = (f32[128,512]{1,0:T(8,128)}, f32[128,512]{1,0:T(8,128)}) custom-call(bf16[128,512]{1,0:T(8,128)(2,1)S(1)} %copy-done.2, bf16[128,512]{1,0:T(8,128)(2,1)S(1)} %copy-done.1, f32[128,512]{1,0:T(8,128)S(1)} %get-tuple-element.27.refs_0_, f32[128,512]{1,0:T(8,128)S(1)} %get-tuple-element.35.refs_1_, ...), custom_call_target="tpu_custom_call" | custom-call | flops 4587520 | bytes 1376256 | tf_op jit(solution)/shard_map/finish/pallas_call | solution.py:232
  (19 shorter events, 1.1 us)
Async XLA Ops:
  0.6 10.7 %collective-permute-start = (bf16[128,512]{1,0:T(8,128)(2,1)}, bf16[128,512]{1,0:T(8,128)(2,1)S(1)}, u32[]{:S(2)}, u32[]{:S(2)}) collective-permute-start(bf16[128,512]{1,0:T(8,128)(2,1)} %image_ref.1), channel_id=1, source_target_pairs={{0,8},{1,9},{2,10},{3,11},{4,12},{5,13},{6,14},{7,15},{8,0},{9,1},... | collective-permute-start | bytes 393224 | tf_op jit(solution)/shard_map/ppermute | solution.py:282
  4.7 11.3 %collective-permute-start.4 = (bf16[128,512]{1,0:T(8,128)(2,1)}, bf16[128,512]{1,0:T(8,128)(2,1)S(1)}, u32[]{:S(2)}, u32[]{:S(2)}) collective-permute-start(bf16[128,512]{1,0:T(8,128)(2,1)} %image_ref.1), channel_id=1, source_target_pairs={{0,4},{1,5},{2,6},{3,7},{4,0},{5,1},{6,2},{7,3},{8,12},{9,13},{10,... | collective-permute-start | bytes 393224 | tf_op jit(solution)/shard_map/ppermute | solution.py:282
  6.3 6.8 %collective-permute-start.2 = (bf16[128,512]{1,0:T(8,128)(2,1)}, bf16[128,512]{1,0:T(8,128)(2,1)S(1)}, u32[]{:S(2)}, u32[]{:S(2)}) collective-permute-start(bf16[128,512]{1,0:T(8,128)(2,1)} %text_ref.1), channel_id=1, source_target_pairs={{0,2},{1,3},{2,0},{3,1},{4,6},{5,7},{6,4},{7,5},{8,10},{9,11},{10,... | collective-permute-start | bytes 393224 | tf_op jit(solution)/shard_map/ppermute | solution.py:282
  7.8 6.0 %collective-permute-start.1 = (bf16[128,512]{1,0:T(8,128)(2,1)}, bf16[128,512]{1,0:T(8,128)(2,1)S(1)}, u32[]{:S(2)}, u32[]{:S(2)}) collective-permute-start(bf16[128,512]{1,0:T(8,128)(2,1)} %text_ref.1), channel_id=1, source_target_pairs={{0,1},{1,0},{2,3},{3,2},{4,5},{5,4},{6,7},{7,6},{8,9},{9,8},{10,11... | collective-permute-start | bytes 393224 | tf_op jit(solution)/shard_map/ppermute | solution.py:282
  9.3 6.4 %collective-permute-start.3 = (bf16[128,512]{1,0:T(8,128)(2,1)}, bf16[128,512]{1,0:T(8,128)(2,1)S(1)}, u32[]{:S(2)}, u32[]{:S(2)}) collective-permute-start(bf16[128,512]{1,0:T(8,128)(2,1)} %text_ref.1), channel_id=1, source_target_pairs={{0,3},{1,2},{2,1},{3,0},{4,7},{5,6},{6,5},{7,4},{8,11},{9,10},{10,... | collective-permute-start | bytes 393224 | tf_op jit(solution)/shard_map/ppermute | solution.py:282
  11.4 5.8 %collective-permute-start.5 = (bf16[128,512]{1,0:T(8,128)(2,1)S(1)}, bf16[128,512]{1,0:T(8,128)(2,1)S(1)}, u32[]{:S(2)}, u32[]{:S(2)}) collective-permute-start(bf16[128,512]{1,0:T(8,128)(2,1)S(1)} %collective-permute-done.refs_1_), channel_id=1, source_target_pairs={{0,4},{1,5},{2,6},{3,7},{4,0},{5,1},{6,2},{7,3},{8,12},{9,13},{10,... | collective-permute-start | bytes 393224 | tf_op jit(solution)/shard_map/ppermute | solution.py:282
  12.1 0.9 %copy-start = (bf16[128,512]{1,0:T(8,128)(2,1)S(1)}, bf16[128,512]{1,0:T(8,128)(2,1)}, u32[]{:S(2)}) copy-start(bf16[128,512]{1,0:T(8,128)(2,1)} %text_ref.1) | copy-start | bytes 393220
  13.1 2.9 %copy-start.2 = (bf16[128,512]{1,0:T(8,128)(2,1)S(1)}, bf16[128,512]{1,0:T(8,128)(2,1)}, u32[]{:S(2)}) copy-start(bf16[128,512]{1,0:T(8,128)(2,1)} %image_ref.1) | copy-start | bytes 393220
  15.9 2.0 %collective-permute-start.6 = (bf16[512,512]{1,0:T(8,128)(2,1)S(1)}, bf16[512,512]{1,0:T(8,128)(2,1)S(1)}, u32[]{:S(2)}, u32[]{:S(2)}) collective-permute-start(bf16[512,512]{1,0:T(8,128)(2,1)S(1)} %stack_units.1.text_ref.own_text_ref), channel_id=1, source_target_pairs={{0,16},{1,17},{2,18},{3,19},{4,20},{5,21},{6,22},{7,23},{8,24},{9,... | collective-permute-start | bytes 1572872 | tf_op jit(solution)/shard_map/ppermute | solution.py:282
  19.8 2.0 %collective-permute-start.8 = (bf16[512,512]{1,0:T(8,128)(2,1)S(1)}, bf16[512,512]{1,0:T(8,128)(2,1)S(1)}, u32[]{:S(2)}, u32[]{:S(2)}) collective-permute-start(bf16[512,512]{1,0:T(8,128)(2,1)S(1)} %get-tuple-element.31), channel_id=1, source_target_pairs={{0,16},{1,17},{2,18},{3,19},{4,20},{5,21},{6,22},{7,23},{8,24},{9,... | collective-permute-start | bytes 1572872 | tf_op jit(solution)/shard_map/ppermute | solution.py:282
  20.0 5.8 %collective-permute-start.7 = (bf16[128,512]{1,0:T(8,128)(2,1)S(1)}, bf16[128,512]{1,0:T(8,128)(2,1)S(1)}, u32[]{:S(2)}, u32[]{:S(2)}) collective-permute-start(bf16[128,512]{1,0:T(8,128)(2,1)S(1)} %get-tuple-element.29), channel_id=1, source_target_pairs={{0,4},{1,5},{2,6},{3,7},{4,0},{5,1},{6,2},{7,3},{8,12},{9,13},{10,... | collective-permute-start | bytes 393224 | tf_op jit(solution)/shard_map/ppermute | solution.py:282
  21.9 8.2 %collective-permute-start.9 = (bf16[128,512]{1,0:T(8,128)(2,1)S(1)}, bf16[128,512]{1,0:T(8,128)(2,1)S(1)}, u32[]{:S(2)}, u32[]{:S(2)}) collective-permute-start(bf16[128,512]{1,0:T(8,128)(2,1)S(1)} %get-tuple-element.34), channel_id=1, source_target_pairs={{0,1},{1,0},{2,3},{3,2},{4,5},{5,4},{6,7},{7,6},{8,9},{9,8},{10,11... | collective-permute-start | bytes 393224 | tf_op jit(solution)/shard_map/ppermute | solution.py:282
  25.8 11.3 %copy-start.1 = (bf16[128,512]{1,0:T(8,128)(2,1)S(1)}, bf16[128,512]{1,0:T(8,128)(2,1)}, u32[]{:S(2)}) copy-start(bf16[128,512]{1,0:T(8,128)(2,1)} %text_ref.1) | copy-start | bytes 393220
  25.8 8.7 %collective-permute-start.11 = (bf16[128,512]{1,0:T(8,128)(2,1)S(1)}, bf16[128,512]{1,0:T(8,128)(2,1)S(1)}, u32[]{:S(2)}, u32[]{:S(2)}) collective-permute-start(bf16[128,512]{1,0:T(8,128)(2,1)S(1)} %add_parts.1), channel_id=1, source_target_pairs={{0,8},{1,9},{2,10},{3,11},{4,12},{5,13},{6,14},{7,15},{8,0},{9,1},... | collective-permute-start | bytes 393224 | tf_op jit(solution)/shard_map/ppermute | solution.py:282
  27.1 7.8 %collective-permute-start.10 = (bf16[128,512]{1,0:T(8,128)(2,1)S(1)}, bf16[128,512]{1,0:T(8,128)(2,1)S(1)}, u32[]{:S(2)}, u32[]{:S(2)}) collective-permute-start(bf16[128,512]{1,0:T(8,128)(2,1)S(1)} %get-tuple-element.37), channel_id=1, source_target_pairs={{0,2},{1,3},{2,0},{3,1},{4,6},{5,7},{6,4},{7,5},{8,10},{9,11},{10,... | collective-permute-start | bytes 393224 | tf_op jit(solution)/shard_map/ppermute | solution.py:282
  28.7 6.3 %collective-permute-start.12 = (bf16[128,512]{1,0:T(8,128)(2,1)S(1)}, bf16[128,512]{1,0:T(8,128)(2,1)S(1)}, u32[]{:S(2)}, u32[]{:S(2)}) collective-permute-start(bf16[128,512]{1,0:T(8,128)(2,1)S(1)} %get-tuple-element.40), channel_id=1, source_target_pairs={{0,3},{1,2},{2,1},{3,0},{4,7},{5,6},{6,5},{7,4},{8,11},{9,10},{10,... | collective-permute-start | bytes 393224 | tf_op jit(solution)/shard_map/ppermute | solution.py:282
  30.1 6.9 %collective-permute-start.13 = (bf16[128,512]{1,0:T(8,128)(2,1)S(1)}, bf16[128,512]{1,0:T(8,128)(2,1)S(1)}, u32[]{:S(2)}, u32[]{:S(2)}) collective-permute-start(bf16[128,512]{1,0:T(8,128)(2,1)S(1)} %get-tuple-element.41), channel_id=1, source_target_pairs={{0,4},{1,5},{2,6},{3,7},{4,0},{5,1},{6,2},{7,3},{8,12},{9,13},{10,... | collective-permute-start | bytes 393224 | tf_op jit(solution)/shard_map/ppermute | solution.py:282

commit v12 on v8

--- a/solution.py
+++ b/solution.py
@@ -290,7 +290,7 @@
         )
         far_parts = dict(zip([*early, *late], image_parts))
         came = [move(part, grp=-g) for g, part in enumerate(text_parts) if g]
-        far_order = [step for step in early if step[0]] + [step for step in early if step[1]] + list(late)
+        far_order = sorted((step for step in far_parts if step != (0, 0)), key=lambda step: step[0])
         far_came = [move(far_parts[h, w], high=-h, low=-w) for h, w in far_order]
         near_parts = add_stacks([text_parts[0], *came], near_count)
         near_parts = [near_parts[0]] + [

time: 37.5 us -> 35.1 us (0.936)
  waiting for transfers between devices: 10.6 us -> 8.17 us
    ppermute x14, waiting for transfers between devices: 10.6 us -> 8.17 us  [move(): return lax.ppermute(value, AXES, perm)]
  transfers between devices with their start and end apart: 14 -> 14, of which waited for: 7 -> 7; matrix products, arithmetic and copies ran while one was open for 0% -> 0% of each run, Pallas kernels for 4% -> 5%
where the time goes in v12:
time: 35.1 us; the launch traced here: 34.9 us
  starting transfers between devices  19.2 us (55%)
  waiting for transfers between devices  8.17 us (23%)
  Pallas kernels  4.59 us (13%)
  between operations  2.02 us (6%)
  local copies, waits for them, and re-layouts  0.91 us (3%)
    ppermute x14, starting transfers between devices, move(): return lax.ppermute(value, AXES, perm)  19.2 us
    ppermute x14, waiting for transfers between devices, move(): return lax.ppermute(value, AXES, perm)  8.17 us
    pallas_call x6, Pallas kernels, call(): pl.pallas_call(kernel, out_shape=out_shape, in_specs=[VMEM] * len(operand...  3.53 us
    pallas_call x1, Pallas kernels, finish(): pl.pallas_call(functools.partial(finish_kernel, [side for side, _ in part...  1.07 us
    unnamed x6, local copies, waits for them, and re-layouts  0.91 us
  transfers between devices with their start and end apart: 14, of which 7 were waited for; matrix products, arithmetic and copies ran while one was open for 0% of the time, Pallas kernels for 5%

profile of v12, /device:TPU:0, one launch (start us, length us, event | category | flops | bytes accessed | tf_op | source)
XLA Modules:
  0.0 34.9 jit_solution(2684841499008869477)
XLA Ops:
  0.6 4.1 %collective-permute-start = (bf16[128,512]{1,0:T(8,128)(2,1)}, bf16[128,512]{1,0:T(8,128)(2,1)S(1)}, u32[]{:S(2)}, u32[]{:S(2)}) collective-permute-start(bf16[128,512]{1,0:T(8,128)(2,1)} %image_ref.1), channel_id=1, source_target_pairs={{0,8},{1,9},{2,10},{3,11},{4,12},{5,13},{6,14},{7,15},{8,0},{9,1},... | collective-permute-start | bytes 393224 | tf_op jit(solution)/shard_map/ppermute | solution.py:269
  4.7 1.6 %collective-permute-start.4 = (bf16[128,512]{1,0:T(8,128)(2,1)}, bf16[128,512]{1,0:T(8,128)(2,1)S(1)}, u32[]{:S(2)}, u32[]{:S(2)}) collective-permute-start(bf16[128,512]{1,0:T(8,128)(2,1)} %image_ref.1), channel_id=1, source_target_pairs={{0,4},{1,5},{2,6},{3,7},{4,0},{5,1},{6,2},{7,3},{8,12},{9,13},{10,... | collective-permute-start | bytes 393224 | tf_op jit(solution)/shard_map/ppermute | solution.py:269
  6.3 1.5 %collective-permute-start.2 = (bf16[128,512]{1,0:T(8,128)(2,1)}, bf16[128,512]{1,0:T(8,128)(2,1)S(1)}, u32[]{:S(2)}, u32[]{:S(2)}) collective-permute-start(bf16[128,512]{1,0:T(8,128)(2,1)} %text_ref.1), channel_id=1, source_target_pairs={{0,2},{1,3},{2,0},{3,1},{4,6},{5,7},{6,4},{7,5},{8,10},{9,11},{10,... | collective-permute-start | bytes 393224 | tf_op jit(solution)/shard_map/ppermute | solution.py:269
  7.8 1.5 %collective-permute-start.1 = (bf16[128,512]{1,0:T(8,128)(2,1)}, bf16[128,512]{1,0:T(8,128)(2,1)S(1)}, u32[]{:S(2)}, u32[]{:S(2)}) collective-permute-start(bf16[128,512]{1,0:T(8,128)(2,1)} %text_ref.1), channel_id=1, source_target_pairs={{0,1},{1,0},{2,3},{3,2},{4,5},{5,4},{6,7},{7,6},{8,9},{9,8},{10,11... | collective-permute-start | bytes 393224 | tf_op jit(solution)/shard_map/ppermute | solution.py:269
  9.3 0.5 %collective-permute-start.3 = (bf16[128,512]{1,0:T(8,128)(2,1)}, bf16[128,512]{1,0:T(8,128)(2,1)S(1)}, u32[]{:S(2)}, u32[]{:S(2)}) collective-permute-start(bf16[128,512]{1,0:T(8,128)(2,1)} %text_ref.1), channel_id=1, source_target_pairs={{0,3},{1,2},{2,1},{3,0},{4,7},{5,6},{6,5},{7,4},{8,11},{9,10},{10,... | collective-permute-start | bytes 393224 | tf_op jit(solution)/shard_map/ppermute | solution.py:269
  11.2 0.2 collective-permute-done.refs_1_
  11.4 0.7 %collective-permute-start.5 = (bf16[128,512]{1,0:T(8,128)(2,1)S(1)}, bf16[128,512]{1,0:T(8,128)(2,1)S(1)}, u32[]{:S(2)}, u32[]{:S(2)}) collective-permute-start(bf16[128,512]{1,0:T(8,128)(2,1)S(1)} %collective-permute-done.refs_1_), channel_id=1, source_target_pairs={{0,4},{1,5},{2,6},{3,7},{4,0},{5,1},{6,2},{7,3},{8,12},{9,13},{10,... | collective-permute-start | bytes 393224 | tf_op jit(solution)/shard_map/ppermute | solution.py:269
  12.1 0.9 %copy-done = bf16[128,512]{1,0:T(8,128)(2,1)S(1)} copy-done((bf16[128,512]{1,0:T(8,128)(2,1)S(1)}, bf16[128,512]{1,0:T(8,128)(2,1)}, u32[]{:S(2)}) %copy-start) | copy-done | bytes 131096
  13.1 0.7 %collective-permute-done.1.refs_1_ = bf16[128,512]{1,0:T(8,128)(2,1)S(1)} collective-permute-done((bf16[128,512]{1,0:T(8,128)(2,1)}, bf16[128,512]{1,0:T(8,128)(2,1)S(1)}, u32[]{:S(2)}, u32[]{:S(2)}) %collective-permute-start.1) | collective-permute-done | bytes 131104 | tf_op jit(solution)/shard_map/ppermute | solution.py:269
  13.8 1.9 %collective-permute-done.3.refs_3_ = bf16[128,512]{1,0:T(8,128)(2,1)S(1)} collective-permute-done((bf16[128,512]{1,0:T(8,128)(2,1)}, bf16[128,512]{1,0:T(8,128)(2,1)S(1)}, u32[]{:S(2)}, u32[]{:S(2)}) %collective-permute-start.3) | collective-permute-done | bytes 131104 | tf_op jit(solution)/shard_map/ppermute | solution.py:269
  16.0 1.1 %early_pairs.1 = (f32[512,512]{1,0:T(8,128)S(1)}, bf16[384,512]{1,0:T(8,128)(2,1)S(1)}, f32[384,512]{1,0:T(8,128)S(1)}) custom-call(f32[1,3]{1,0:T(1,128)S(1)} %maximum_bitcast_fusion.params_ref, bf16[512,512]{1,0:T(8,128)(2,1)S(1)} %stack_units.1.text_ref.own_text_ref, bf16[128,512]{1,0:T(8,128)(2,1)S(1)} %copy-done.2, ...), custom_call_target="tpu_custom_call" | custom-call | flops 603979776 | bytes 3145740 | tf_op jit(solution)/shard_map/early_pairs/pallas_call | solution.py:28
  17.3 0.6 %collective-permute-done.6.refs_0_ = bf16[512,512]{1,0:T(8,128)(2,1)S(1)} collective-permute-done((bf16[512,512]{1,0:T(8,128)(2,1)S(1)}, bf16[512,512]{1,0:T(8,128)(2,1)S(1)}, u32[]{:S(2)}, u32[]{:S(2)}) %collective-permute-start.6) | collective-permute-done | bytes 524320 | tf_op jit(solution)/shard_map/ppermute | solution.py:269
  17.9 1.9 %rest_pairs.1 = (f32[512,512]{1,0:T(8,128)S(1)}, bf16[512,512]{1,0:T(8,128)(2,1)S(1)}, f32[128,512]{1,0:T(8,128)S(1)}, bf16[128,512]{1,0:T(8,128)(2,1)S(1)}, bf1...) custom-call(f32[1,3]{1,0:T(1,128)S(1)} %maximum_bitcast_fusion.params_ref, ...), custom_call_target="tpu_custom_call" | custom-call | flops 1006632960 | bytes 5636108 | tf_op jit(solution)/shard_map/rest_pairs/pallas_call | solution.py:28
  19.8 0.2 collective-permute-start.10
  20.0 0.5 %collective-permute-start.7 = (bf16[128,512]{1,0:T(8,128)(2,1)S(1)}, bf16[128,512]{1,0:T(8,128)(2,1)S(1)}, u32[]{:S(2)}, u32[]{:S(2)}) collective-permute-start(bf16[128,512]{1,0:T(8,128)(2,1)S(1)} %get-tuple-element.23), channel_id=1, source_target_pairs={{0,4},{1,5},{2,6},{3,7},{4,0},{5,1},{6,2},{7,3},{8,12},{9,13},{10,... | collective-permute-start | bytes 393224 | tf_op jit(solution)/shard_map/ppermute | solution.py:269
  20.5 2.5 %collective-permute-start.8 = (bf16[128,512]{1,0:T(8,128)(2,1)S(1)}, bf16[128,512]{1,0:T(8,128)(2,1)S(1)}, u32[]{:S(2)}, u32[]{:S(2)}) collective-permute-start(bf16[128,512]{1,0:T(8,128)(2,1)S(1)} %get-tuple-element.24), channel_id=1, source_target_pairs={{0,8},{1,9},{2,10},{3,11},{4,12},{5,13},{6,14},{7,15},{8,0},{9,1},... | collective-permute-start | bytes 393224 | tf_op jit(solution)/shard_map/ppermute | solution.py:269
  22.9 1.5 %collective-permute-start.9 = (bf16[128,512]{1,0:T(8,128)(2,1)S(1)}, bf16[128,512]{1,0:T(8,128)(2,1)S(1)}, u32[]{:S(2)}, u32[]{:S(2)}) collective-permute-start(bf16[128,512]{1,0:T(8,128)(2,1)S(1)} %get-tuple-element.25), channel_id=1, source_target_pairs={{0,12},{1,13},{2,14},{3,15},{4,8},{5,9},{6,10},{7,11},{8,4},{9,5},... | collective-permute-start | bytes 393224 | tf_op jit(solution)/shard_map/ppermute | solution.py:269
  24.5 1.0 %collective-permute-start.11 = (bf16[128,512]{1,0:T(8,128)(2,1)S(1)}, bf16[128,512]{1,0:T(8,128)(2,1)S(1)}, u32[]{:S(2)}, u32[]{:S(2)}) collective-permute-start(bf16[128,512]{1,0:T(8,128)(2,1)S(1)} %get-tuple-element.29), channel_id=1, source_target_pairs={{0,1},{1,0},{2,3},{3,2},{4,5},{5,4},{6,7},{7,6},{8,9},{9,8},{10,11... | collective-permute-start | bytes 393224 | tf_op jit(solution)/shard_map/ppermute | solution.py:269
  25.5 1.5 %collective-permute-start.12 = (bf16[128,512]{1,0:T(8,128)(2,1)S(1)}, bf16[128,512]{1,0:T(8,128)(2,1)S(1)}, u32[]{:S(2)}, u32[]{:S(2)}) collective-permute-start(bf16[128,512]{1,0:T(8,128)(2,1)S(1)} %get-tuple-element.30), channel_id=1, source_target_pairs={{0,2},{1,3},{2,0},{3,1},{4,6},{5,7},{6,4},{7,5},{8,10},{9,11},{10,... | collective-permute-start | bytes 393224 | tf_op jit(solution)/shard_map/ppermute | solution.py:269
  27.0 1.0 %collective-permute-done.7.refs_1_ = bf16[128,512]{1,0:T(8,128)(2,1)S(1)} collective-permute-done((bf16[128,512]{1,0:T(8,128)(2,1)S(1)}, bf16[128,512]{1,0:T(8,128)(2,1)S(1)}, u32[]{:S(2)}, u32[]{:S(2)}) %collective-permute-start.7) | collective-permute-done | bytes 131104 | tf_op jit(solution)/shard_map/ppermute | solution.py:269
  28.0 2.1 %collective-permute-start.13 = (bf16[128,512]{1,0:T(8,128)(2,1)S(1)}, bf16[128,512]{1,0:T(8,128)(2,1)S(1)}, u32[]{:S(2)}, u32[]{:S(2)}) collective-permute-start(bf16[128,512]{1,0:T(8,128)(2,1)S(1)} %get-tuple-element.31), channel_id=1, source_target_pairs={{0,3},{1,2},{2,1},{3,0},{4,7},{5,6},{6,5},{7,4},{8,11},{9,10},{10,... | collective-permute-start | bytes 393224 | tf_op jit(solution)/shard_map/ppermute | solution.py:269
  30.1 3.3 %collective-permute-done.8.refs_2_ = bf16[128,512]{1,0:T(8,128)(2,1)S(1)} collective-permute-done((bf16[128,512]{1,0:T(8,128)(2,1)S(1)}, bf16[128,512]{1,0:T(8,128)(2,1)S(1)}, u32[]{:S(2)}, u32[]{:S(2)}) %collective-permute-start.8) | collective-permute-done | bytes 131104 | tf_op jit(solution)/shard_map/ppermute | solution.py:269
  33.4 0.5 %collective-permute-done.13.refs_7_ = bf16[128,512]{1,0:T(8,128)(2,1)S(1)} collective-permute-done((bf16[128,512]{1,0:T(8,128)(2,1)S(1)}, bf16[128,512]{1,0:T(8,128)(2,1)S(1)}, u32[]{:S(2)}, u32[]{:S(2)}) %collective-permute-start.13) | collective-permute-done | bytes 131104 | tf_op jit(solution)/shard_map/ppermute | solution.py:269
  33.9 1.1 %finish.1 = (f32[128,512]{1,0:T(8,128)}, f32[128,512]{1,0:T(8,128)}) custom-call(bf16[128,512]{1,0:T(8,128)(2,1)S(1)} %copy-done.2, bf16[128,512]{1,0:T(8,128)(2,1)S(1)} %copy-done.1, f32[128,512]{1,0:T(8,128)S(1)} %get-tuple-element.22.refs_0_, bf16[128,512]{1,0:T(8,128)(2,1)S(1)} %collective-permute-done.7.refs_1_, ...), custom_call_target="tpu_custom_call" | custom-call | flops 5242880 | bytes 1572864 | tf_op jit(solution)/shard_map/finish/pallas_call | solution.py:219
  (18 shorter events, 0.7 us)
Async XLA Ops:
  0.6 10.7 %collective-permute-start = (bf16[128,512]{1,0:T(8,128)(2,1)}, bf16[128,512]{1,0:T(8,128)(2,1)S(1)}, u32[]{:S(2)}, u32[]{:S(2)}) collective-permute-start(bf16[128,512]{1,0:T(8,128)(2,1)} %image_ref.1), channel_id=1, source_target_pairs={{0,8},{1,9},{2,10},{3,11},{4,12},{5,13},{6,14},{7,15},{8,0},{9,1},... | collective-permute-start | bytes 393224 | tf_op jit(solution)/shard_map/ppermute | solution.py:269
  4.7 11.3 %collective-permute-start.4 = (bf16[128,512]{1,0:T(8,128)(2,1)}, bf16[128,512]{1,0:T(8,128)(2,1)S(1)}, u32[]{:S(2)}, u32[]{:S(2)}) collective-permute-start(bf16[128,512]{1,0:T(8,128)(2,1)} %image_ref.1), channel_id=1, source_target_pairs={{0,4},{1,5},{2,6},{3,7},{4,0},{5,1},{6,2},{7,3},{8,12},{9,13},{10,... | collective-permute-start | bytes 393224 | tf_op jit(solution)/shard_map/ppermute | solution.py:269
  6.3 6.8 %collective-permute-start.2 = (bf16[128,512]{1,0:T(8,128)(2,1)}, bf16[128,512]{1,0:T(8,128)(2,1)S(1)}, u32[]{:S(2)}, u32[]{:S(2)}) collective-permute-start(bf16[128,512]{1,0:T(8,128)(2,1)} %text_ref.1), channel_id=1, source_target_pairs={{0,2},{1,3},{2,0},{3,1},{4,6},{5,7},{6,4},{7,5},{8,10},{9,11},{10,... | collective-permute-start | bytes 393224 | tf_op jit(solution)/shard_map/ppermute | solution.py:269
  7.8 6.0 %collective-permute-start.1 = (bf16[128,512]{1,0:T(8,128)(2,1)}, bf16[128,512]{1,0:T(8,128)(2,1)S(1)}, u32[]{:S(2)}, u32[]{:S(2)}) collective-permute-start(bf16[128,512]{1,0:T(8,128)(2,1)} %text_ref.1), channel_id=1, source_target_pairs={{0,1},{1,0},{2,3},{3,2},{4,5},{5,4},{6,7},{7,6},{8,9},{9,8},{10,11... | collective-permute-start | bytes 393224 | tf_op jit(solution)/shard_map/ppermute | solution.py:269
  9.3 6.4 %collective-permute-start.3 = (bf16[128,512]{1,0:T(8,128)(2,1)}, bf16[128,512]{1,0:T(8,128)(2,1)S(1)}, u32[]{:S(2)}, u32[]{:S(2)}) collective-permute-start(bf16[128,512]{1,0:T(8,128)(2,1)} %text_ref.1), channel_id=1, source_target_pairs={{0,3},{1,2},{2,1},{3,0},{4,7},{5,6},{6,5},{7,4},{8,11},{9,10},{10,... | collective-permute-start | bytes 393224 | tf_op jit(solution)/shard_map/ppermute | solution.py:269
  11.4 5.8 %collective-permute-start.5 = (bf16[128,512]{1,0:T(8,128)(2,1)S(1)}, bf16[128,512]{1,0:T(8,128)(2,1)S(1)}, u32[]{:S(2)}, u32[]{:S(2)}) collective-permute-start(bf16[128,512]{1,0:T(8,128)(2,1)S(1)} %collective-permute-done.refs_1_), channel_id=1, source_target_pairs={{0,4},{1,5},{2,6},{3,7},{4,0},{5,1},{6,2},{7,3},{8,12},{9,13},{10,... | collective-permute-start | bytes 393224 | tf_op jit(solution)/shard_map/ppermute | solution.py:269
  12.1 0.9 %copy-start = (bf16[128,512]{1,0:T(8,128)(2,1)S(1)}, bf16[128,512]{1,0:T(8,128)(2,1)}, u32[]{:S(2)}) copy-start(bf16[128,512]{1,0:T(8,128)(2,1)} %text_ref.1) | copy-start | bytes 393220
  13.1 2.9 %copy-start.2 = (bf16[128,512]{1,0:T(8,128)(2,1)S(1)}, bf16[128,512]{1,0:T(8,128)(2,1)}, u32[]{:S(2)}) copy-start(bf16[128,512]{1,0:T(8,128)(2,1)} %image_ref.1) | copy-start | bytes 393220
  15.9 2.0 %collective-permute-start.6 = (bf16[512,512]{1,0:T(8,128)(2,1)S(1)}, bf16[512,512]{1,0:T(8,128)(2,1)S(1)}, u32[]{:S(2)}, u32[]{:S(2)}) collective-permute-start(bf16[512,512]{1,0:T(8,128)(2,1)S(1)} %stack_units.1.text_ref.own_text_ref), channel_id=1, source_target_pairs={{0,16},{1,17},{2,18},{3,19},{4,20},{5,21},{6,22},{7,23},{8,24},{9,... | collective-permute-start | bytes 1572872 | tf_op jit(solution)/shard_map/ppermute | solution.py:269
  19.8 4.6 %collective-permute-start.10 = (bf16[512,512]{1,0:T(8,128)(2,1)S(1)}, bf16[512,512]{1,0:T(8,128)(2,1)S(1)}, u32[]{:S(2)}, u32[]{:S(2)}) collective-permute-start(bf16[512,512]{1,0:T(8,128)(2,1)S(1)} %get-tuple-element.27), channel_id=1, source_target_pairs={{0,16},{1,17},{2,18},{3,19},{4,20},{5,21},{6,22},{7,23},{8,24},{9,... | collective-permute-start | bytes 1572872 | tf_op jit(solution)/shard_map/ppermute | solution.py:269
  20.0 8.0 %collective-permute-start.7 = (bf16[128,512]{1,0:T(8,128)(2,1)S(1)}, bf16[128,512]{1,0:T(8,128)(2,1)S(1)}, u32[]{:S(2)}, u32[]{:S(2)}) collective-permute-start(bf16[128,512]{1,0:T(8,128)(2,1)S(1)} %get-tuple-element.23), channel_id=1, source_target_pairs={{0,4},{1,5},{2,6},{3,7},{4,0},{5,1},{6,2},{7,3},{8,12},{9,13},{10,... | collective-permute-start | bytes 393224 | tf_op jit(solution)/shard_map/ppermute | solution.py:269
  20.5 12.9 %collective-permute-start.8 = (bf16[128,512]{1,0:T(8,128)(2,1)S(1)}, bf16[128,512]{1,0:T(8,128)(2,1)S(1)}, u32[]{:S(2)}, u32[]{:S(2)}) collective-permute-start(bf16[128,512]{1,0:T(8,128)(2,1)S(1)} %get-tuple-element.24), channel_id=1, source_target_pairs={{0,8},{1,9},{2,10},{3,11},{4,12},{5,13},{6,14},{7,15},{8,0},{9,1},... | collective-permute-start | bytes 393224 | tf_op jit(solution)/shard_map/ppermute | solution.py:269
  22.9 10.4 %collective-permute-start.9 = (bf16[128,512]{1,0:T(8,128)(2,1)S(1)}, bf16[128,512]{1,0:T(8,128)(2,1)S(1)}, u32[]{:S(2)}, u32[]{:S(2)}) collective-permute-start(bf16[128,512]{1,0:T(8,128)(2,1)S(1)} %get-tuple-element.25), channel_id=1, source_target_pairs={{0,12},{1,13},{2,14},{3,15},{4,8},{5,9},{6,10},{7,11},{8,4},{9,5},... | collective-permute-start | bytes 393224 | tf_op jit(solution)/shard_map/ppermute | solution.py:269
  24.4 9.5 %copy-start.1 = (bf16[128,512]{1,0:T(8,128)(2,1)S(1)}, bf16[128,512]{1,0:T(8,128)(2,1)}, u32[]{:S(2)}) copy-start(bf16[128,512]{1,0:T(8,128)(2,1)} %text_ref.1) | copy-start | bytes 393220
  24.5 8.9 %collective-permute-start.11 = (bf16[128,512]{1,0:T(8,128)(2,1)S(1)}, bf16[128,512]{1,0:T(8,128)(2,1)S(1)}, u32[]{:S(2)}, u32[]{:S(2)}) collective-permute-start(bf16[128,512]{1,0:T(8,128)(2,1)S(1)} %get-tuple-element.29), channel_id=1, source_target_pairs={{0,1},{1,0},{2,3},{3,2},{4,5},{5,4},{6,7},{7,6},{8,9},{9,8},{10,11... | collective-permute-start | bytes 393224 | tf_op jit(solution)/shard_map/ppermute | solution.py:269
  25.5 7.9 %collective-permute-start.12 = (bf16[128,512]{1,0:T(8,128)(2,1)S(1)}, bf16[128,512]{1,0:T(8,128)(2,1)S(1)}, u32[]{:S(2)}, u32[]{:S(2)}) collective-permute-start(bf16[128,512]{1,0:T(8,128)(2,1)S(1)} %get-tuple-element.30), channel_id=1, source_target_pairs={{0,2},{1,3},{2,0},{3,1},{4,6},{5,7},{6,4},{7,5},{8,10},{9,11},{10,... | collective-permute-start | bytes 393224 | tf_op jit(solution)/shard_map/ppermute | solution.py:269
  28.0 5.9 %collective-permute-start.13 = (bf16[128,512]{1,0:T(8,128)(2,1)S(1)}, bf16[128,512]{1,0:T(8,128)(2,1)S(1)}, u32[]{:S(2)}, u32[]{:S(2)}) collective-permute-start(bf16[128,512]{1,0:T(8,128)(2,1)S(1)} %get-tuple-element.31), channel_id=1, source_target_pairs={{0,3},{1,2},{2,1},{3,0},{4,7},{5,6},{6,5},{7,4},{8,11},{9,10},{10,... | collective-permute-start | bytes 393224 | tf_op jit(solution)/shard_map/ppermute | solution.py:269

commit v13 on v12

--- a/solution.py
+++ b/solution.py
@@ -13,6 +13,7 @@
 SPAN = 256
 PIECE = 32
 LATE = 30000
+FAR = 60000
 LOG2_E = math.log2(math.e)
 VMEM = pl.BlockSpec(memory_space=pltpu.VMEM)
 
@@ -111,23 +112,24 @@
     total_out[...] = pairs(units_out[...], params_ref, text_ref, text_out, own=rows)
 
 
-def rest_pairs_kernel(
-    count, params_ref, early_ref, total_ref, own_text_ref, own_add_ref, late_ref, *refs
-):
-    text_refs, own_out = refs[:count], refs[count]
-    other_out, image_out = refs[count + 1:2 * count + 1], refs[2 * count + 1:]
+def early_rest_kernel(count, params_ref, units_ref, total_ref, *refs):
+    text_refs, text_out, image_out = refs[:count], refs[count:2 * count], refs[2 * count:]
     rows = image_out[0].shape[0]
-    early, late = early_ref[...], late_ref[...]
-    total = jnp.concatenate(
-        [
-            total_ref[...],
-            pairs(late, params_ref, own_text_ref, own_out, text_add=own_add_ref),
-        ],
-        axis=0,
-    )
-    vi = jnp.concatenate([early, late], axis=0)
-    for text_ref, out in zip(text_refs, other_out):
+    vi, total = units_ref[...], total_ref[...]
+    for text_ref, out in zip(text_refs, text_out):
         total = total + pairs(vi, params_ref, text_ref, out)
+    for a, ref in enumerate(image_out):
+        ref[...] = total[a * rows:(a + 1) * rows, :].astype(ref.dtype)
+
+
+def late_pairs_kernel(count, params_ref, units_ref, *refs):
+    text_refs, add_refs = refs[:count], refs[count:2 * count]
+    text_out, image_out = refs[2 * count:3 * count], refs[3 * count:]
+    rows = image_out[0].shape[0]
+    total = sum(
+        pairs(units_ref[...], params_ref, text_ref, out, text_add=add)
+        for text_ref, add, out in zip(text_refs, add_refs, text_out)
+    )
     for a, ref in enumerate(image_out):
         ref[...] = total[a * rows:(a + 1) * rows, :].astype(ref.dtype)
 
@@ -137,14 +139,18 @@
     early_rows, late_rows = rows * len(early), rows * len(late)
     own, others = texts[0], texts[1:]
     other_rows = sum(t.shape[0] for t in others)
+    part = jax.ShapeDtypeStruct((rows, width), jnp.bfloat16)
 
     def cost(pair_count):
         return dict(flops=6 * pair_count * width, transcendentals=2 * pair_count)
+
+    def text_sums(stacks, dtype):
+        return [jax.ShapeDtypeStruct(t.shape, dtype) for t in stacks]
 
     own_add, early_units, total = call(
         early_pairs_kernel,
         [
-            jax.ShapeDtypeStruct(own.shape, jnp.float32),
+            *text_sums([own], jnp.float32),
             jax.ShapeDtypeStruct((early_rows, width), jnp.bfloat16),
             jax.ShapeDtypeStruct((early_rows, width), jnp.float32),
         ],
@@ -153,18 +159,25 @@
         **cost(early_rows * own.shape[0]),
     )
     late_units = units(late, "late_units", LATE)
+    late_units, total = lax.optimization_barrier((late_units, total))
     outs = call(
-        functools.partial(rest_pairs_kernel, len(others)),
-        [jax.ShapeDtypeStruct(own.shape, jnp.float32)]
-        + [jax.ShapeDtypeStruct(t.shape, jnp.bfloat16) for t in others]
+        functools.partial(early_rest_kernel, len(others)),
+        text_sums(others, jnp.float32)
         + [jax.ShapeDtypeStruct((rows, width), jnp.float32)]
-        + [jax.ShapeDtypeStruct((rows, width), jnp.bfloat16)] * (len(early) + len(late) - 1),
-        [params, early_units, total, own, own_add, late_units, *others],
-        name="rest_pairs",
-        **cost(late_rows * own.shape[0] + (early_rows + late_rows) * other_rows),
-    )
-    count = 1 + len(others)
-    return outs[count:], outs[:count]
+        + [part] * (len(early) - 1),
+        [params, early_units, total, *others],
+        name="early_rest",
+        **cost(early_rows * other_rows),
+    )
+    other_adds, early_parts = outs[:len(others)], outs[len(others):]
+    outs = call(
+        functools.partial(late_pairs_kernel, len(texts)),
+        text_sums([own], jnp.float32) + text_sums(others, jnp.bfloat16) + [part] * len(late),
+        [params, late_units, *texts, own_add, *other_adds],
+        name="late_pairs",
+        **cost(late_rows * (own.shape[0] + other_rows)),
+    )
+    return early_parts, outs[len(texts):], outs[:len(texts)]
 
 
 def add_stacks_kernel(part_count, *refs):
@@ -187,6 +200,17 @@
         flops=len(parts) * parts[0].size,
         name="add_stacks",
     )
+
+
+def add_far_kernel(*refs):
+    refs[-1][...] = sum(ref[...].astype(jnp.float32) for ref in refs[:-1])
+
+
+def add_far(parts):
+    out = jax.ShapeDtypeStruct(parts[0].shape, jnp.float32)
+    return call(
+        add_far_kernel, [out], parts, flops=FAR * len(parts) * out.size, name="add_far"
+    )[0]
 
 
 def finish_kernel(sides, image_ref, text_ref, *refs):
@@ -285,22 +309,28 @@
         near_rows = [units([texts], "own_units")] + [move(texts, near=n) for n in range(1, near_count)]
         own_stack = stack_units(near_rows)
         stacks = [own_stack] + [move(own_stack, grp=g) for g in range(1, grp_count)]
-        image_parts, text_parts = pair_terms(
+        early_parts, late_parts, text_parts = pair_terms(
             params, list(early.values()), list(late.values()), stacks
         )
-        far_parts = dict(zip([*early, *late], image_parts))
+        far_parts = dict(zip([*early, *late], [*early_parts, *late_parts]))
+
+        def give_back(h, w):
+            return move(far_parts[h, w], high=-h, low=-w)
+
         came = [move(part, grp=-g) for g, part in enumerate(text_parts) if g]
-        far_order = sorted((step for step in far_parts if step != (0, 0)), key=lambda step: step[0])
-        far_came = [move(far_parts[h, w], high=-h, low=-w) for h, w in far_order]
-        near_parts = add_stacks([text_parts[0], *came], near_count)
+        far_sum = add_far(
+            [far_parts[0, 0]] + [give_back(h, w) for h, w in early if h]
+        )
+        far_sum, own_text = lax.optimization_barrier((far_sum, text_parts[0]))
+        far_came = [give_back(h, w) for h, w in late] + [give_back(h, w) for h, w in early if w]
+        near_parts = add_stacks([own_text, *came], near_count)
         near_parts = [near_parts[0]] + [
             move(part, near=-n) for n, part in enumerate(near_parts) if n
         ]
         return finish(
             images,
             texts,
-            [(0, part) for part in [far_parts[0, 0]] + far_came]
-            + [(1, part) for part in near_parts],
+            [(0, part) for part in [far_sum] + far_came] + [(1, part) for part in near_parts],
         )
 
     in_specs = (P(AXES, None), P(AXES, None), P(), P())

time: 35.1 us -> 40.5 us (1.15)
  waiting for transfers between devices: 8.17 us -> 14.5 us
  starting transfers between devices: 19.2 us -> 17.7 us
  Pallas kernels: 4.59 us -> 5.12 us
    ppermute x14, waiting for transfers between devices: 8.17 us -> 14.5 us  [move(): return lax.ppermute(value, AXES, perm)]
    ppermute x14, starting transfers between devices: 19.2 us -> 17.7 us  [move(): return lax.ppermute(value, AXES, perm)]
    pallas_call x6 -> x8, Pallas kernels: 3.53 us -> 4.07 us  [call(): pl.pallas_call(kernel, out_shape=out_shape, in_specs=[VMEM] * len(operand...]
  transfers between devices with their start and end apart: 14 -> 14, of which waited for: 7 -> 8; matrix products, arithmetic and copies ran while one was open for 0% -> 0% of each run, Pallas kernels for 5% -> 7%
where the time goes in v13:
time: 40.5 us; the launch traced here: 40.3 us
  starting transfers between devices  17.7 us (44%)
  waiting for transfers between devices  14.5 us (36%)
  Pallas kernels  5.12 us (13%)
  between operations  2.03 us (5%)
  local copies, waits for them, and re-layouts  0.92 us (2%)
    ppermute x14, starting transfers between devices, move(): return lax.ppermute(value, AXES, perm)  17.7 us
    ppermute x14, waiting for transfers between devices, move(): return lax.ppermute(value, AXES, perm)  14.5 us
    pallas_call x8, Pallas kernels, call(): pl.pallas_call(kernel, out_shape=out_shape, in_specs=[VMEM] * len(operand...  4.07 us
    pallas_call x1, Pallas kernels, finish(): pl.pallas_call(functools.partial(finish_kernel, [side for side, _ in part...  1.04 us
    unnamed x6, local copies, waits for them, and re-layouts  0.92 us
  transfers between devices with their start and end apart: 14, of which 8 were waited for; matrix products, arithmetic and copies ran while one was open for 0% of the time, Pallas kernels for 7%

profile of v13, /device:TPU:0, one launch (start us, length us, event | category | flops | bytes accessed | tf_op | source)
XLA Modules:
  0.0 40.3 jit_solution(7534594286367034032)
XLA Ops:
  0.6 4.1 %collective-permute-start = (bf16[128,512]{1,0:T(8,128)(2,1)}, bf16[128,512]{1,0:T(8,128)(2,1)S(1)}, u32[]{:S(2)}, u32[]{:S(2)}) collective-permute-start(bf16[128,512]{1,0:T(8,128)(2,1)} %image_ref.1), channel_id=1, source_target_pairs={{0,8},{1,9},{2,10},{3,11},{4,12},{5,13},{6,14},{7,15},{8,0},{9,1},... | collective-permute-start | bytes 393224 | tf_op jit(solution)/shard_map/ppermute | solution.py:293
  4.7 1.5 %collective-permute-start.1 = (bf16[128,512]{1,0:T(8,128)(2,1)}, bf16[128,512]{1,0:T(8,128)(2,1)S(1)}, u32[]{:S(2)}, u32[]{:S(2)}) collective-permute-start(bf16[128,512]{1,0:T(8,128)(2,1)} %text_ref.1), channel_id=1, source_target_pairs={{0,1},{1,0},{2,3},{3,2},{4,5},{5,4},{6,7},{7,6},{8,9},{9,8},{10,11... | collective-permute-start | bytes 393224 | tf_op jit(solution)/shard_map/ppermute | solution.py:293
  6.2 1.5 %collective-permute-start.2 = (bf16[128,512]{1,0:T(8,128)(2,1)}, bf16[128,512]{1,0:T(8,128)(2,1)S(1)}, u32[]{:S(2)}, u32[]{:S(2)}) collective-permute-start(bf16[128,512]{1,0:T(8,128)(2,1)} %text_ref.1), channel_id=1, source_target_pairs={{0,2},{1,3},{2,0},{3,1},{4,6},{5,7},{6,4},{7,5},{8,10},{9,11},{10,... | collective-permute-start | bytes 393224 | tf_op jit(solution)/shard_map/ppermute | solution.py:293
  7.7 0.5 %collective-permute-start.3 = (bf16[128,512]{1,0:T(8,128)(2,1)}, bf16[128,512]{1,0:T(8,128)(2,1)S(1)}, u32[]{:S(2)}, u32[]{:S(2)}) collective-permute-start(bf16[128,512]{1,0:T(8,128)(2,1)} %text_ref.1), channel_id=1, source_target_pairs={{0,3},{1,2},{2,1},{3,0},{4,7},{5,6},{6,5},{7,4},{8,11},{9,10},{10,... | collective-permute-start | bytes 393224 | tf_op jit(solution)/shard_map/ppermute | solution.py:293
  8.2 1.6 %collective-permute-start.4 = (bf16[128,512]{1,0:T(8,128)(2,1)}, bf16[128,512]{1,0:T(8,128)(2,1)S(1)}, u32[]{:S(2)}, u32[]{:S(2)}) collective-permute-start(bf16[128,512]{1,0:T(8,128)(2,1)} %image_ref.1), channel_id=1, source_target_pairs={{0,4},{1,5},{2,6},{3,7},{4,0},{5,1},{6,2},{7,3},{8,12},{9,13},{10,... | collective-permute-start | bytes 393224 | tf_op jit(solution)/shard_map/ppermute | solution.py:293
  11.4 0.8 %collective-permute-start.5 = (bf16[128,512]{1,0:T(8,128)(2,1)S(1)}, bf16[128,512]{1,0:T(8,128)(2,1)S(1)}, u32[]{:S(2)}, u32[]{:S(2)}) collective-permute-start(bf16[128,512]{1,0:T(8,128)(2,1)S(1)} %collective-permute-done.refs_1_), channel_id=1, source_target_pairs={{0,4},{1,5},{2,6},{3,7},{4,0},{5,1},{6,2},{7,3},{8,12},{9,13},{10,... | collective-permute-start | bytes 393224 | tf_op jit(solution)/shard_map/ppermute | solution.py:293
  12.1 0.9 %copy-done = bf16[128,512]{1,0:T(8,128)(2,1)S(1)} copy-done((bf16[128,512]{1,0:T(8,128)(2,1)S(1)}, bf16[128,512]{1,0:T(8,128)(2,1)}, u32[]{:S(2)}) %copy-start) | copy-done | bytes 131096
  13.2 1.0 %collective-permute-done.2.refs_2_ = bf16[128,512]{1,0:T(8,128)(2,1)S(1)} collective-permute-done((bf16[128,512]{1,0:T(8,128)(2,1)}, bf16[128,512]{1,0:T(8,128)(2,1)S(1)}, u32[]{:S(2)}, u32[]{:S(2)}) %collective-permute-start.2) | collective-permute-done | bytes 131104 | tf_op jit(solution)/shard_map/ppermute | solution.py:293
  14.5 0.4 %collective-permute-done.4.refs_2_ = bf16[128,512]{1,0:T(8,128)(2,1)S(1)} collective-permute-done((bf16[128,512]{1,0:T(8,128)(2,1)}, bf16[128,512]{1,0:T(8,128)(2,1)S(1)}, u32[]{:S(2)}, u32[]{:S(2)}) %collective-permute-start.4) | collective-permute-done | bytes 131104 | tf_op jit(solution)/shard_map/ppermute | solution.py:293
  14.9 1.1 %early_pairs.1 = (f32[512,512]{1,0:T(8,128)S(1)}, bf16[384,512]{1,0:T(8,128)(2,1)S(1)}, f32[384,512]{1,0:T(8,128)S(1)}) custom-call(f32[1,3]{1,0:T(1,128)S(1)} %maximum_bitcast_fusion.params_ref, bf16[512,512]{1,0:T(8,128)(2,1)S(1)} %stack_units.1.text_ref.refs_0_, bf16[128,512]{1,0:T(8,128)(2,1)S(1)} %copy-done.2, ...), custom_call_target="tpu_custom_call" | custom-call | flops 603979776 | bytes 3145740 | tf_op jit(solution)/shard_map/early_pairs/pallas_call | solution.py:29
  16.0 0.9 %collective-permute-done.5.refs_0_ = bf16[128,512]{1,0:T(8,128)(2,1)S(1)} collective-permute-done((bf16[128,512]{1,0:T(8,128)(2,1)S(1)}, bf16[128,512]{1,0:T(8,128)(2,1)S(1)}, u32[]{:S(2)}, u32[]{:S(2)}) %collective-permute-start.5) | collective-permute-done | bytes 131104 | tf_op jit(solution)/shard_map/ppermute | solution.py:293
  17.0 1.1 %early_rest.1 = (f32[512,512]{1,0:T(8,128)S(1)}, f32[128,512]{1,0:T(8,128)S(1)}, bf16[128,512]{1,0:T(8,128)(2,1)S(1)}, bf16[128,512]{1,0:T(8,128)(2,1)S(1)}) custom-call(f32[1,3]{1,0:T(1,128)S(1)} %maximum_bitcast_fusion.params_ref, bf16[384,512]{1,0:T(8,128)(2,1)S(1)} %get-tuple-element.23.units_ref, f32[384,512]{1,0:T(8,128)S(1)} %get-tuple-element.26.total_ref, ...), custom_call_target="tpu_custom_call" | custom-call | flops 603979776 | bytes 3276812 | tf_op jit(solution)/shard_map/early_rest/pallas_call | solution.py:29
  18.1 2.3 %collective-permute-start.7 = (bf16[128,512]{1,0:T(8,128)(2,1)S(1)}, bf16[128,512]{1,0:T(8,128)(2,1)S(1)}, u32[]{:S(2)}, u32[]{:S(2)}) collective-permute-start(bf16[128,512]{1,0:T(8,128)(2,1)S(1)} %get-tuple-element.28), channel_id=1, source_target_pairs={{0,8},{1,9},{2,10},{3,11},{4,12},{5,13},{6,14},{7,15},{8,0},{9,1},... | collective-permute-start | bytes 393224 | tf_op jit(solution)/shard_map/ppermute | solution.py:293
  20.4 1.3 %late_pairs.1 = (f32[512,512]{1,0:T(8,128)S(1)}, bf16[512,512]{1,0:T(8,128)(2,1)S(1)}, bf16[128,512]{1,0:T(8,128)(2,1)S(1)}) custom-call(f32[1,3]{1,0:T(1,128)S(1)} %maximum_bitcast_fusion.params_ref, bf16[128,512]{1,0:T(8,128)(2,1)S(1)} %late_units.1.units_ref, bf16[512,512]{1,0:T(8,128)(2,1)S(1)} %stack_units.1.text_ref.refs_0_, ...), custom_call_target="tpu_custom_call" | custom-call | flops 402653184 | bytes 4980748 | tf_op jit(solution)/shard_map/late_pairs/pallas_call | solution.py:29
  21.7 1.3 %collective-permute-start.8 = (bf16[128,512]{1,0:T(8,128)(2,1)S(1)}, bf16[128,512]{1,0:T(8,128)(2,1)S(1)}, u32[]{:S(2)}, u32[]{:S(2)}) collective-permute-start(bf16[128,512]{1,0:T(8,128)(2,1)S(1)} %get-tuple-element.34), channel_id=1, source_target_pairs={{0,12},{1,13},{2,14},{3,15},{4,8},{5,9},{6,10},{7,11},{8,4},{9,5},... | collective-permute-start | bytes 393224 | tf_op jit(solution)/shard_map/ppermute | solution.py:293
  22.9 0.6 %collective-permute-start.9 = (bf16[128,512]{1,0:T(8,128)(2,1)S(1)}, bf16[128,512]{1,0:T(8,128)(2,1)S(1)}, u32[]{:S(2)}, u32[]{:S(2)}) collective-permute-start(bf16[128,512]{1,0:T(8,128)(2,1)S(1)} %get-tuple-element.35), channel_id=1, source_target_pairs={{0,4},{1,5},{2,6},{3,7},{4,0},{5,1},{6,2},{7,3},{8,12},{9,13},{10,... | collective-permute-start | bytes 393224 | tf_op jit(solution)/shard_map/ppermute | solution.py:293
  23.6 7.2 %collective-permute-done.7.refs_1_ = bf16[128,512]{1,0:T(8,128)(2,1)S(1)} collective-permute-done((bf16[128,512]{1,0:T(8,128)(2,1)S(1)}, bf16[128,512]{1,0:T(8,128)(2,1)S(1)}, u32[]{:S(2)}, u32[]{:S(2)}) %collective-permute-start.7) | collective-permute-done | bytes 131104 | tf_op jit(solution)/shard_map/ppermute | solution.py:293
  31.0 1.0 %collective-permute-start.11 = (bf16[128,512]{1,0:T(8,128)(2,1)S(1)}, bf16[128,512]{1,0:T(8,128)(2,1)S(1)}, u32[]{:S(2)}, u32[]{:S(2)}) collective-permute-start(bf16[128,512]{1,0:T(8,128)(2,1)S(1)} %get-tuple-element.39), channel_id=1, source_target_pairs={{0,1},{1,0},{2,3},{3,2},{4,5},{5,4},{6,7},{7,6},{8,9},{9,8},{10,11... | collective-permute-start | bytes 393224 | tf_op jit(solution)/shard_map/ppermute | solution.py:293
  32.0 1.4 %collective-permute-start.12 = (bf16[128,512]{1,0:T(8,128)(2,1)S(1)}, bf16[128,512]{1,0:T(8,128)(2,1)S(1)}, u32[]{:S(2)}, u32[]{:S(2)}) collective-permute-start(bf16[128,512]{1,0:T(8,128)(2,1)S(1)} %get-tuple-element.40), channel_id=1, source_target_pairs={{0,2},{1,3},{2,0},{3,1},{4,6},{5,7},{6,4},{7,5},{8,10},{9,11},{10,... | collective-permute-start | bytes 393224 | tf_op jit(solution)/shard_map/ppermute | solution.py:293
  33.4 1.1 %collective-permute-start.13 = (bf16[128,512]{1,0:T(8,128)(2,1)S(1)}, bf16[128,512]{1,0:T(8,128)(2,1)S(1)}, u32[]{:S(2)}, u32[]{:S(2)}) collective-permute-start(bf16[128,512]{1,0:T(8,128)(2,1)S(1)} %get-tuple-element.41), channel_id=1, source_target_pairs={{0,3},{1,2},{2,1},{3,0},{4,7},{5,6},{6,5},{7,4},{8,11},{9,10},{10,... | collective-permute-start | bytes 393224 | tf_op jit(solution)/shard_map/ppermute | solution.py:293
  34.5 1.5 %collective-permute-done.11.refs_4_ = bf16[128,512]{1,0:T(8,128)(2,1)S(1)} collective-permute-done((bf16[128,512]{1,0:T(8,128)(2,1)S(1)}, bf16[128,512]{1,0:T(8,128)(2,1)S(1)}, u32[]{:S(2)}, u32[]{:S(2)}) %collective-permute-start.11) | collective-permute-done | bytes 131104 | tf_op jit(solution)/shard_map/ppermute | solution.py:293
  36.0 0.9 %collective-permute-done.12.refs_5_ = bf16[128,512]{1,0:T(8,128)(2,1)S(1)} collective-permute-done((bf16[128,512]{1,0:T(8,128)(2,1)S(1)}, bf16[128,512]{1,0:T(8,128)(2,1)S(1)}, u32[]{:S(2)}, u32[]{:S(2)}) %collective-permute-start.12) | collective-permute-done | bytes 131104 | tf_op jit(solution)/shard_map/ppermute | solution.py:293
  37.0 2.3 %collective-permute-done.13.refs_6_ = bf16[128,512]{1,0:T(8,128)(2,1)S(1)} collective-permute-done((bf16[128,512]{1,0:T(8,128)(2,1)S(1)}, bf16[128,512]{1,0:T(8,128)(2,1)S(1)}, u32[]{:S(2)}, u32[]{:S(2)}) %collective-permute-start.13) | collective-permute-done | bytes 131104 | tf_op jit(solution)/shard_map/ppermute | solution.py:293
  39.3 1.0 %finish.1 = (f32[128,512]{1,0:T(8,128)}, f32[128,512]{1,0:T(8,128)}) custom-call(bf16[128,512]{1,0:T(8,128)(2,1)S(1)} %copy-done.2, bf16[128,512]{1,0:T(8,128)(2,1)S(1)} %copy-done.1, f32[128,512]{1,0:T(8,128)S(1)} %add_far.1.refs_0_, bf16[128,512]{1,0:T(8,128)(2,1)S(1)} %collective-permute-done.8.refs_1_, ...), custom_call_target="tpu_custom_call" | custom-call | flops 4587520 | bytes 1376256 | tf_op jit(solution)/shard_map/finish/pallas_call | solution.py:243
  (20 shorter events, 0.9 us)
Async XLA Ops:
  0.6 10.7 %collective-permute-start = (bf16[128,512]{1,0:T(8,128)(2,1)}, bf16[128,512]{1,0:T(8,128)(2,1)S(1)}, u32[]{:S(2)}, u32[]{:S(2)}) collective-permute-start(bf16[128,512]{1,0:T(8,128)(2,1)} %image_ref.1), channel_id=1, source_target_pairs={{0,8},{1,9},{2,10},{3,11},{4,12},{5,13},{6,14},{7,15},{8,0},{9,1},... | collective-permute-start | bytes 393224 | tf_op jit(solution)/shard_map/ppermute | solution.py:293
  4.7 8.4 %collective-permute-start.1 = (bf16[128,512]{1,0:T(8,128)(2,1)}, bf16[128,512]{1,0:T(8,128)(2,1)S(1)}, u32[]{:S(2)}, u32[]{:S(2)}) collective-permute-start(bf16[128,512]{1,0:T(8,128)(2,1)} %text_ref.1), channel_id=1, source_target_pairs={{0,1},{1,0},{2,3},{3,2},{4,5},{5,4},{6,7},{7,6},{8,9},{9,8},{10,11... | collective-permute-start | bytes 393224 | tf_op jit(solution)/shard_map/ppermute | solution.py:293
  6.2 8.0 %collective-permute-start.2 = (bf16[128,512]{1,0:T(8,128)(2,1)}, bf16[128,512]{1,0:T(8,128)(2,1)S(1)}, u32[]{:S(2)}, u32[]{:S(2)}) collective-permute-start(bf16[128,512]{1,0:T(8,128)(2,1)} %text_ref.1), channel_id=1, source_target_pairs={{0,2},{1,3},{2,0},{3,1},{4,6},{5,7},{6,4},{7,5},{8,10},{9,11},{10,... | collective-permute-start | bytes 393224 | tf_op jit(solution)/shard_map/ppermute | solution.py:293
  7.7 6.5 %collective-permute-start.3 = (bf16[128,512]{1,0:T(8,128)(2,1)}, bf16[128,512]{1,0:T(8,128)(2,1)S(1)}, u32[]{:S(2)}, u32[]{:S(2)}) collective-permute-start(bf16[128,512]{1,0:T(8,128)(2,1)} %text_ref.1), channel_id=1, source_target_pairs={{0,3},{1,2},{2,1},{3,0},{4,7},{5,6},{6,5},{7,4},{8,11},{9,10},{10,... | collective-permute-start | bytes 393224 | tf_op jit(solution)/shard_map/ppermute | solution.py:293
  8.2 6.6 %collective-permute-start.4 = (bf16[128,512]{1,0:T(8,128)(2,1)}, bf16[128,512]{1,0:T(8,128)(2,1)S(1)}, u32[]{:S(2)}, u32[]{:S(2)}) collective-permute-start(bf16[128,512]{1,0:T(8,128)(2,1)} %image_ref.1), channel_id=1, source_target_pairs={{0,4},{1,5},{2,6},{3,7},{4,0},{5,1},{6,2},{7,3},{8,12},{9,13},{10,... | collective-permute-start | bytes 393224 | tf_op jit(solution)/shard_map/ppermute | solution.py:293
  11.4 5.5 %collective-permute-start.5 = (bf16[128,512]{1,0:T(8,128)(2,1)S(1)}, bf16[128,512]{1,0:T(8,128)(2,1)S(1)}, u32[]{:S(2)}, u32[]{:S(2)}) collective-permute-start(bf16[128,512]{1,0:T(8,128)(2,1)S(1)} %collective-permute-done.refs_1_), channel_id=1, source_target_pairs={{0,4},{1,5},{2,6},{3,7},{4,0},{5,1},{6,2},{7,3},{8,12},{9,13},{10,... | collective-permute-start | bytes 393224 | tf_op jit(solution)/shard_map/ppermute | solution.py:293
  12.1 0.9 %copy-start = (bf16[128,512]{1,0:T(8,128)(2,1)S(1)}, bf16[128,512]{1,0:T(8,128)(2,1)}, u32[]{:S(2)}) copy-start(bf16[128,512]{1,0:T(8,128)(2,1)} %text_ref.1) | copy-start | bytes 393220
  13.1 1.7 %copy-start.2 = (bf16[128,512]{1,0:T(8,128)(2,1)S(1)}, bf16[128,512]{1,0:T(8,128)(2,1)}, u32[]{:S(2)}) copy-start(bf16[128,512]{1,0:T(8,128)(2,1)} %image_ref.1) | copy-start | bytes 393220
  14.4 2.6 %collective-permute-start.6 = (bf16[512,512]{1,0:T(8,128)(2,1)S(1)}, bf16[512,512]{1,0:T(8,128)(2,1)S(1)}, u32[]{:S(2)}, u32[]{:S(2)}) collective-permute-start(bf16[512,512]{1,0:T(8,128)(2,1)S(1)} %stack_units.1.text_ref.refs_0_), channel_id=1, source_target_pairs={{0,16},{1,17},{2,18},{3,19},{4,20},{5,21},{6,22},{7,23},{8,24},{9,... | collective-permute-start | bytes 1572872 | tf_op jit(solution)/shard_map/ppermute | solution.py:293
  18.1 12.7 %collective-permute-start.7 = (bf16[128,512]{1,0:T(8,128)(2,1)S(1)}, bf16[128,512]{1,0:T(8,128)(2,1)S(1)}, u32[]{:S(2)}, u32[]{:S(2)}) collective-permute-start(bf16[128,512]{1,0:T(8,128)(2,1)S(1)} %get-tuple-element.28), channel_id=1, source_target_pairs={{0,8},{1,9},{2,10},{3,11},{4,12},{5,13},{6,14},{7,15},{8,0},{9,1},... | collective-permute-start | bytes 393224 | tf_op jit(solution)/shard_map/ppermute | solution.py:293
  21.7 12.9 %collective-permute-start.8 = (bf16[128,512]{1,0:T(8,128)(2,1)S(1)}, bf16[128,512]{1,0:T(8,128)(2,1)S(1)}, u32[]{:S(2)}, u32[]{:S(2)}) collective-permute-start(bf16[128,512]{1,0:T(8,128)(2,1)S(1)} %get-tuple-element.34), channel_id=1, source_target_pairs={{0,12},{1,13},{2,14},{3,15},{4,8},{5,9},{6,10},{7,11},{8,4},{9,5},... | collective-permute-start | bytes 393224 | tf_op jit(solution)/shard_map/ppermute | solution.py:293
  22.9 11.6 %collective-permute-start.9 = (bf16[128,512]{1,0:T(8,128)(2,1)S(1)}, bf16[128,512]{1,0:T(8,128)(2,1)S(1)}, u32[]{:S(2)}, u32[]{:S(2)}) collective-permute-start(bf16[128,512]{1,0:T(8,128)(2,1)S(1)} %get-tuple-element.35), channel_id=1, source_target_pairs={{0,4},{1,5},{2,6},{3,7},{4,0},{5,1},{6,2},{7,3},{8,12},{9,13},{10,... | collective-permute-start | bytes 393224 | tf_op jit(solution)/shard_map/ppermute | solution.py:293
  23.6 7.3 %collective-permute-start.10 = (bf16[512,512]{1,0:T(8,128)(2,1)S(1)}, bf16[512,512]{1,0:T(8,128)(2,1)S(1)}, u32[]{:S(2)}, u32[]{:S(2)}) collective-permute-start(bf16[512,512]{1,0:T(8,128)(2,1)S(1)} %get-tuple-element.37), channel_id=1, source_target_pairs={{0,16},{1,17},{2,18},{3,19},{4,20},{5,21},{6,22},{7,23},{8,24},{9,... | collective-permute-start | bytes 1572872 | tf_op jit(solution)/shard_map/ppermute | solution.py:293
  30.8 8.4 %copy-start.1 = (bf16[128,512]{1,0:T(8,128)(2,1)S(1)}, bf16[128,512]{1,0:T(8,128)(2,1)}, u32[]{:S(2)}) copy-start(bf16[128,512]{1,0:T(8,128)(2,1)} %text_ref.1) | copy-start | bytes 393220
  31.0 5.0 %collective-permute-start.11 = (bf16[128,512]{1,0:T(8,128)(2,1)S(1)}, bf16[128,512]{1,0:T(8,128)(2,1)S(1)}, u32[]{:S(2)}, u32[]{:S(2)}) collective-permute-start(bf16[128,512]{1,0:T(8,128)(2,1)S(1)} %get-tuple-element.39), channel_id=1, source_target_pairs={{0,1},{1,0},{2,3},{3,2},{4,5},{5,4},{6,7},{7,6},{8,9},{9,8},{10,11... | collective-permute-start | bytes 393224 | tf_op jit(solution)/shard_map/ppermute | solution.py:293
  32.0 5.0 %collective-permute-start.12 = (bf16[128,512]{1,0:T(8,128)(2,1)S(1)}, bf16[128,512]{1,0:T(8,128)(2,1)S(1)}, u32[]{:S(2)}, u32[]{:S(2)}) collective-permute-start(bf16[128,512]{1,0:T(8,128)(2,1)S(1)} %get-tuple-element.40), channel_id=1, source_target_pairs={{0,2},{1,3},{2,0},{3,1},{4,6},{5,7},{6,4},{7,5},{8,10},{9,11},{10,... | collective-permute-start | bytes 393224 | tf_op jit(solution)/shard_map/ppermute | solution.py:293
  33.4 5.9 %collective-permute-start.13 = (bf16[128,512]{1,0:T(8,128)(2,1)S(1)}, bf16[128,512]{1,0:T(8,128)(2,1)S(1)}, u32[]{:S(2)}, u32[]{:S(2)}) collective-permute-start(bf16[128,512]{1,0:T(8,128)(2,1)S(1)} %get-tuple-element.41), channel_id=1, source_target_pairs={{0,3},{1,2},{2,1},{3,0},{4,7},{5,6},{6,5},{7,4},{8,11},{9,10},{10,... | collective-permute-start | bytes 393224 | tf_op jit(solution)/shard_map/ppermute | solution.py:293

commit v14 on v12

--- a/solution.py
+++ b/solution.py
@@ -12,7 +12,7 @@
 VMEM_LIMIT = 32 * 1024 * 1024
 SPAN = 256
 PIECE = 32
-LATE = 30000
+LATE = 16500
 LOG2_E = math.log2(math.e)
 VMEM = pl.BlockSpec(memory_space=pltpu.VMEM)
 

time: 35.1 us -> 34.5 us (0.983)
  waiting for transfers between devices: 8.17 us -> 6.54 us
  starting transfers between devices: 19.2 us -> 20.2 us
    ppermute x14, waiting for transfers between devices: 8.17 us -> 6.54 us  [move(): return lax.ppermute(value, AXES, perm)]
    ppermute x14, starting transfers between devices: 19.2 us -> 20.2 us  [move(): return lax.ppermute(value, AXES, perm)]
where the time goes in v14:
time: 34.5 us; the launch traced here: 34.3 us
  starting transfers between devices  20.2 us (59%)
  waiting for transfers between devices  6.54 us (19%)
  Pallas kernels  4.58 us (13%)
  between operations  2.02 us (6%)
  local copies, waits for them, and re-layouts  0.91 us (3%)
    ppermute x14, starting transfers between devices, move(): return lax.ppermute(value, AXES, perm)  20.2 us
    ppermute x14, waiting for transfers between devices, move(): return lax.ppermute(value, AXES, perm)  6.54 us
    pallas_call x6, Pallas kernels, call(): pl.pallas_call(kernel, out_shape=out_shape, in_specs=[VMEM] * len(operand...  3.52 us
    pallas_call x1, Pallas kernels, finish(): pl.pallas_call(functools.partial(finish_kernel, [side for side, _ in part...  1.07 us
    unnamed x6, local copies, waits for them, and re-layouts  0.91 us
  transfers between devices with their start and end apart: 14, of which 7 were waited for; matrix products, arithmetic and copies ran while one was open for 0% of the time, Pallas kernels for 5%

profile of v14, /device:TPU:0, one launch (start us, length us, event | category | flops | bytes accessed | tf_op | source)
XLA Modules:
  0.0 34.3 jit_solution(17689585286001707233)
XLA Ops:
  0.6 4.1 %collective-permute-start = (bf16[128,512]{1,0:T(8,128)(2,1)}, bf16[128,512]{1,0:T(8,128)(2,1)S(1)}, u32[]{:S(2)}, u32[]{:S(2)}) collective-permute-start(bf16[128,512]{1,0:T(8,128)(2,1)} %image_ref.1), channel_id=1, source_target_pairs={{0,8},{1,9},{2,10},{3,11},{4,12},{5,13},{6,14},{7,15},{8,0},{9,1},... | collective-permute-start | bytes 393224 | tf_op jit(solution)/shard_map/ppermute | solution.py:269
  4.7 1.5 %collective-permute-start.2 = (bf16[128,512]{1,0:T(8,128)(2,1)}, bf16[128,512]{1,0:T(8,128)(2,1)S(1)}, u32[]{:S(2)}, u32[]{:S(2)}) collective-permute-start(bf16[128,512]{1,0:T(8,128)(2,1)} %text_ref.1), channel_id=1, source_target_pairs={{0,2},{1,3},{2,0},{3,1},{4,6},{5,7},{6,4},{7,5},{8,10},{9,11},{10,... | collective-permute-start | bytes 393224 | tf_op jit(solution)/shard_map/ppermute | solution.py:269
  6.3 1.5 %collective-permute-start.1 = (bf16[128,512]{1,0:T(8,128)(2,1)}, bf16[128,512]{1,0:T(8,128)(2,1)S(1)}, u32[]{:S(2)}, u32[]{:S(2)}) collective-permute-start(bf16[128,512]{1,0:T(8,128)(2,1)} %text_ref.1), channel_id=1, source_target_pairs={{0,1},{1,0},{2,3},{3,2},{4,5},{5,4},{6,7},{7,6},{8,9},{9,8},{10,11... | collective-permute-start | bytes 393224 | tf_op jit(solution)/shard_map/ppermute | solution.py:269
  7.7 0.5 %collective-permute-start.3 = (bf16[128,512]{1,0:T(8,128)(2,1)}, bf16[128,512]{1,0:T(8,128)(2,1)S(1)}, u32[]{:S(2)}, u32[]{:S(2)}) collective-permute-start(bf16[128,512]{1,0:T(8,128)(2,1)} %text_ref.1), channel_id=1, source_target_pairs={{0,3},{1,2},{2,1},{3,0},{4,7},{5,6},{6,5},{7,4},{8,11},{9,10},{10,... | collective-permute-start | bytes 393224 | tf_op jit(solution)/shard_map/ppermute | solution.py:269
  8.2 1.6 %collective-permute-start.4 = (bf16[128,512]{1,0:T(8,128)(2,1)}, bf16[128,512]{1,0:T(8,128)(2,1)S(1)}, u32[]{:S(2)}, u32[]{:S(2)}) collective-permute-start(bf16[128,512]{1,0:T(8,128)(2,1)} %image_ref.1), channel_id=1, source_target_pairs={{0,4},{1,5},{2,6},{3,7},{4,0},{5,1},{6,2},{7,3},{8,12},{9,13},{10,... | collective-permute-start | bytes 393224 | tf_op jit(solution)/shard_map/ppermute | solution.py:269
  11.2 0.2 collective-permute-done.refs_1_
  11.4 0.8 %collective-permute-start.5 = (bf16[128,512]{1,0:T(8,128)(2,1)S(1)}, bf16[128,512]{1,0:T(8,128)(2,1)S(1)}, u32[]{:S(2)}, u32[]{:S(2)}) collective-permute-start(bf16[128,512]{1,0:T(8,128)(2,1)S(1)} %collective-permute-done.refs_1_), channel_id=1, source_target_pairs={{0,4},{1,5},{2,6},{3,7},{4,0},{5,1},{6,2},{7,3},{8,12},{9,13},{10,... | collective-permute-start | bytes 393224 | tf_op jit(solution)/shard_map/ppermute | solution.py:269
  12.1 0.9 %copy-done = bf16[128,512]{1,0:T(8,128)(2,1)S(1)} copy-done((bf16[128,512]{1,0:T(8,128)(2,1)S(1)}, bf16[128,512]{1,0:T(8,128)(2,1)}, u32[]{:S(2)}) %copy-start) | copy-done | bytes 131096
  13.2 1.0 %collective-permute-done.3.refs_3_ = bf16[128,512]{1,0:T(8,128)(2,1)S(1)} collective-permute-done((bf16[128,512]{1,0:T(8,128)(2,1)}, bf16[128,512]{1,0:T(8,128)(2,1)S(1)}, u32[]{:S(2)}, u32[]{:S(2)}) %collective-permute-start.3) | collective-permute-done | bytes 131104 | tf_op jit(solution)/shard_map/ppermute | solution.py:269
  14.2 0.2 stack_units.1.text_ref.own_text_ref
  14.4 0.4 %collective-permute-done.4.refs_2_ = bf16[128,512]{1,0:T(8,128)(2,1)S(1)} collective-permute-done((bf16[128,512]{1,0:T(8,128)(2,1)}, bf16[128,512]{1,0:T(8,128)(2,1)S(1)}, u32[]{:S(2)}, u32[]{:S(2)}) %collective-permute-start.4) | collective-permute-done | bytes 131104 | tf_op jit(solution)/shard_map/ppermute | solution.py:269
  14.9 1.1 %early_pairs.1 = (f32[512,512]{1,0:T(8,128)S(1)}, bf16[384,512]{1,0:T(8,128)(2,1)S(1)}, f32[384,512]{1,0:T(8,128)S(1)}) custom-call(f32[1,3]{1,0:T(1,128)S(1)} %maximum_bitcast_fusion.params_ref, bf16[512,512]{1,0:T(8,128)(2,1)S(1)} %stack_units.1.text_ref.own_text_ref, bf16[128,512]{1,0:T(8,128)(2,1)S(1)} %copy-done.2, ...), custom_call_target="tpu_custom_call" | custom-call | flops 603979776 | bytes 3145740 | tf_op jit(solution)/shard_map/early_pairs/pallas_call | solution.py:28
  16.0 0.9 %collective-permute-done.5.refs_0_ = bf16[128,512]{1,0:T(8,128)(2,1)S(1)} collective-permute-done((bf16[128,512]{1,0:T(8,128)(2,1)S(1)}, bf16[128,512]{1,0:T(8,128)(2,1)S(1)}, u32[]{:S(2)}, u32[]{:S(2)}) %collective-permute-start.5) | collective-permute-done | bytes 131104 | tf_op jit(solution)/shard_map/ppermute | solution.py:269
  17.0 1.9 %rest_pairs.1 = (f32[512,512]{1,0:T(8,128)S(1)}, bf16[512,512]{1,0:T(8,128)(2,1)S(1)}, f32[128,512]{1,0:T(8,128)S(1)}, bf16[128,512]{1,0:T(8,128)(2,1)S(1)}, bf1...) custom-call(f32[1,3]{1,0:T(1,128)S(1)} %maximum_bitcast_fusion.params_ref, ...), custom_call_target="tpu_custom_call" | custom-call | flops 1006632960 | bytes 5636108 | tf_op jit(solution)/shard_map/rest_pairs/pallas_call | solution.py:28
  19.0 1.0 %collective-permute-start.7 = (bf16[128,512]{1,0:T(8,128)(2,1)S(1)}, bf16[128,512]{1,0:T(8,128)(2,1)S(1)}, u32[]{:S(2)}, u32[]{:S(2)}) collective-permute-start(bf16[128,512]{1,0:T(8,128)(2,1)S(1)} %get-tuple-element.23), channel_id=1, source_target_pairs={{0,4},{1,5},{2,6},{3,7},{4,0},{5,1},{6,2},{7,3},{8,12},{9,13},{10,... | collective-permute-start | bytes 393224 | tf_op jit(solution)/shard_map/ppermute | solution.py:269
  20.0 3.0 %collective-permute-start.8 = (bf16[128,512]{1,0:T(8,128)(2,1)S(1)}, bf16[128,512]{1,0:T(8,128)(2,1)S(1)}, u32[]{:S(2)}, u32[]{:S(2)}) collective-permute-start(bf16[128,512]{1,0:T(8,128)(2,1)S(1)} %get-tuple-element.24), channel_id=1, source_target_pairs={{0,8},{1,9},{2,10},{3,11},{4,12},{5,13},{6,14},{7,15},{8,0},{9,1},... | collective-permute-start | bytes 393224 | tf_op jit(solution)/shard_map/ppermute | solution.py:269
  23.0 0.4 %collective-permute-start.9 = (bf16[128,512]{1,0:T(8,128)(2,1)S(1)}, bf16[128,512]{1,0:T(8,128)(2,1)S(1)}, u32[]{:S(2)}, u32[]{:S(2)}) collective-permute-start(bf16[128,512]{1,0:T(8,128)(2,1)S(1)} %get-tuple-element.25), channel_id=1, source_target_pairs={{0,12},{1,13},{2,14},{3,15},{4,8},{5,9},{6,10},{7,11},{8,4},{9,5},... | collective-permute-start | bytes 393224 | tf_op jit(solution)/shard_map/ppermute | solution.py:269
  23.5 1.6 %collective-permute-start.11 = (bf16[128,512]{1,0:T(8,128)(2,1)S(1)}, bf16[128,512]{1,0:T(8,128)(2,1)S(1)}, u32[]{:S(2)}, u32[]{:S(2)}) collective-permute-start(bf16[128,512]{1,0:T(8,128)(2,1)S(1)} %get-tuple-element.29), channel_id=1, source_target_pairs={{0,1},{1,0},{2,3},{3,2},{4,5},{5,4},{6,7},{7,6},{8,9},{9,8},{10,11... | collective-permute-start | bytes 393224 | tf_op jit(solution)/shard_map/ppermute | solution.py:269
  25.1 1.5 %collective-permute-start.12 = (bf16[128,512]{1,0:T(8,128)(2,1)S(1)}, bf16[128,512]{1,0:T(8,128)(2,1)S(1)}, u32[]{:S(2)}, u32[]{:S(2)}) collective-permute-start(bf16[128,512]{1,0:T(8,128)(2,1)S(1)} %get-tuple-element.30), channel_id=1, source_target_pairs={{0,2},{1,3},{2,0},{3,1},{4,6},{5,7},{6,4},{7,5},{8,10},{9,11},{10,... | collective-permute-start | bytes 393224 | tf_op jit(solution)/shard_map/ppermute | solution.py:269
  26.7 0.7 %collective-permute-done.7.refs_1_ = bf16[128,512]{1,0:T(8,128)(2,1)S(1)} collective-permute-done((bf16[128,512]{1,0:T(8,128)(2,1)S(1)}, bf16[128,512]{1,0:T(8,128)(2,1)S(1)}, u32[]{:S(2)}, u32[]{:S(2)}) %collective-permute-start.7) | collective-permute-done | bytes 131104 | tf_op jit(solution)/shard_map/ppermute | solution.py:269
  27.3 2.5 %collective-permute-start.13 = (bf16[128,512]{1,0:T(8,128)(2,1)S(1)}, bf16[128,512]{1,0:T(8,128)(2,1)S(1)}, u32[]{:S(2)}, u32[]{:S(2)}) collective-permute-start(bf16[128,512]{1,0:T(8,128)(2,1)S(1)} %get-tuple-element.31), channel_id=1, source_target_pairs={{0,3},{1,2},{2,1},{3,0},{4,7},{5,6},{6,5},{7,4},{8,11},{9,10},{10,... | collective-permute-start | bytes 393224 | tf_op jit(solution)/shard_map/ppermute | solution.py:269
  29.8 3.1 %collective-permute-done.8.refs_2_ = bf16[128,512]{1,0:T(8,128)(2,1)S(1)} collective-permute-done((bf16[128,512]{1,0:T(8,128)(2,1)S(1)}, bf16[128,512]{1,0:T(8,128)(2,1)S(1)}, u32[]{:S(2)}, u32[]{:S(2)}) %collective-permute-start.8) | collective-permute-done | bytes 131104 | tf_op jit(solution)/shard_map/ppermute | solution.py:269
  32.9 0.3 collective-permute-done.13.refs_7_
  33.2 1.1 %finish.1 = (f32[128,512]{1,0:T(8,128)}, f32[128,512]{1,0:T(8,128)}) custom-call(bf16[128,512]{1,0:T(8,128)(2,1)S(1)} %copy-done.2, bf16[128,512]{1,0:T(8,128)(2,1)S(1)} %copy-done.1, f32[128,512]{1,0:T(8,128)S(1)} %get-tuple-element.22.refs_0_, bf16[128,512]{1,0:T(8,128)(2,1)S(1)} %collective-permute-done.7.refs_1_, ...), custom_call_target="tpu_custom_call" | custom-call | flops 5242880 | bytes 1572864 | tf_op jit(solution)/shard_map/finish/pallas_call | solution.py:219
  (18 shorter events, 0.6 us)
Async XLA Ops:
  0.6 10.7 %collective-permute-start = (bf16[128,512]{1,0:T(8,128)(2,1)}, bf16[128,512]{1,0:T(8,128)(2,1)S(1)}, u32[]{:S(2)}, u32[]{:S(2)}) collective-permute-start(bf16[128,512]{1,0:T(8,128)(2,1)} %image_ref.1), channel_id=1, source_target_pairs={{0,8},{1,9},{2,10},{3,11},{4,12},{5,13},{6,14},{7,15},{8,0},{9,1},... | collective-permute-start | bytes 393224 | tf_op jit(solution)/shard_map/ppermute | solution.py:269
  4.7 8.4 %collective-permute-start.2 = (bf16[128,512]{1,0:T(8,128)(2,1)}, bf16[128,512]{1,0:T(8,128)(2,1)S(1)}, u32[]{:S(2)}, u32[]{:S(2)}) collective-permute-start(bf16[128,512]{1,0:T(8,128)(2,1)} %text_ref.1), channel_id=1, source_target_pairs={{0,2},{1,3},{2,0},{3,1},{4,6},{5,7},{6,4},{7,5},{8,10},{9,11},{10,... | collective-permute-start | bytes 393224 | tf_op jit(solution)/shard_map/ppermute | solution.py:269
  6.3 6.9 %collective-permute-start.1 = (bf16[128,512]{1,0:T(8,128)(2,1)}, bf16[128,512]{1,0:T(8,128)(2,1)S(1)}, u32[]{:S(2)}, u32[]{:S(2)}) collective-permute-start(bf16[128,512]{1,0:T(8,128)(2,1)} %text_ref.1), channel_id=1, source_target_pairs={{0,1},{1,0},{2,3},{3,2},{4,5},{5,4},{6,7},{7,6},{8,9},{9,8},{10,11... | collective-permute-start | bytes 393224 | tf_op jit(solution)/shard_map/ppermute | solution.py:269
  7.7 6.4 %collective-permute-start.3 = (bf16[128,512]{1,0:T(8,128)(2,1)}, bf16[128,512]{1,0:T(8,128)(2,1)S(1)}, u32[]{:S(2)}, u32[]{:S(2)}) collective-permute-start(bf16[128,512]{1,0:T(8,128)(2,1)} %text_ref.1), channel_id=1, source_target_pairs={{0,3},{1,2},{2,1},{3,0},{4,7},{5,6},{6,5},{7,4},{8,11},{9,10},{10,... | collective-permute-start | bytes 393224 | tf_op jit(solution)/shard_map/ppermute | solution.py:269
  8.2 6.6 %collective-permute-start.4 = (bf16[128,512]{1,0:T(8,128)(2,1)}, bf16[128,512]{1,0:T(8,128)(2,1)S(1)}, u32[]{:S(2)}, u32[]{:S(2)}) collective-permute-start(bf16[128,512]{1,0:T(8,128)(2,1)} %image_ref.1), channel_id=1, source_target_pairs={{0,4},{1,5},{2,6},{3,7},{4,0},{5,1},{6,2},{7,3},{8,12},{9,13},{10,... | collective-permute-start | bytes 393224 | tf_op jit(solution)/shard_map/ppermute | solution.py:269
  11.4 5.5 %collective-permute-start.5 = (bf16[128,512]{1,0:T(8,128)(2,1)S(1)}, bf16[128,512]{1,0:T(8,128)(2,1)S(1)}, u32[]{:S(2)}, u32[]{:S(2)}) collective-permute-start(bf16[128,512]{1,0:T(8,128)(2,1)S(1)} %collective-permute-done.refs_1_), channel_id=1, source_target_pairs={{0,4},{1,5},{2,6},{3,7},{4,0},{5,1},{6,2},{7,3},{8,12},{9,13},{10,... | collective-permute-start | bytes 393224 | tf_op jit(solution)/shard_map/ppermute | solution.py:269
  12.1 0.9 %copy-start = (bf16[128,512]{1,0:T(8,128)(2,1)S(1)}, bf16[128,512]{1,0:T(8,128)(2,1)}, u32[]{:S(2)}) copy-start(bf16[128,512]{1,0:T(8,128)(2,1)} %text_ref.1) | copy-start | bytes 393220
  13.1 1.7 %copy-start.2 = (bf16[128,512]{1,0:T(8,128)(2,1)S(1)}, bf16[128,512]{1,0:T(8,128)(2,1)}, u32[]{:S(2)}) copy-start(bf16[128,512]{1,0:T(8,128)(2,1)} %image_ref.1) | copy-start | bytes 393220
  14.3 2.6 %collective-permute-start.6 = (bf16[512,512]{1,0:T(8,128)(2,1)S(1)}, bf16[512,512]{1,0:T(8,128)(2,1)S(1)}, u32[]{:S(2)}, u32[]{:S(2)}) collective-permute-start(bf16[512,512]{1,0:T(8,128)(2,1)S(1)} %stack_units.1.text_ref.own_text_ref), channel_id=1, source_target_pairs={{0,16},{1,17},{2,18},{3,19},{4,20},{5,21},{6,22},{7,23},{8,24},{9,... | collective-permute-start | bytes 1572872 | tf_op jit(solution)/shard_map/ppermute | solution.py:269
  18.9 4.5 %collective-permute-start.10 = (bf16[512,512]{1,0:T(8,128)(2,1)S(1)}, bf16[512,512]{1,0:T(8,128)(2,1)S(1)}, u32[]{:S(2)}, u32[]{:S(2)}) collective-permute-start(bf16[512,512]{1,0:T(8,128)(2,1)S(1)} %get-tuple-element.27), channel_id=1, source_target_pairs={{0,16},{1,17},{2,18},{3,19},{4,20},{5,21},{6,22},{7,23},{8,24},{9,... | collective-permute-start | bytes 1572872 | tf_op jit(solution)/shard_map/ppermute | solution.py:269
  19.0 8.4 %collective-permute-start.7 = (bf16[128,512]{1,0:T(8,128)(2,1)S(1)}, bf16[128,512]{1,0:T(8,128)(2,1)S(1)}, u32[]{:S(2)}, u32[]{:S(2)}) collective-permute-start(bf16[128,512]{1,0:T(8,128)(2,1)S(1)} %get-tuple-element.23), channel_id=1, source_target_pairs={{0,4},{1,5},{2,6},{3,7},{4,0},{5,1},{6,2},{7,3},{8,12},{9,13},{10,... | collective-permute-start | bytes 393224 | tf_op jit(solution)/shard_map/ppermute | solution.py:269
  20.0 12.9 %collective-permute-start.8 = (bf16[128,512]{1,0:T(8,128)(2,1)S(1)}, bf16[128,512]{1,0:T(8,128)(2,1)S(1)}, u32[]{:S(2)}, u32[]{:S(2)}) collective-permute-start(bf16[128,512]{1,0:T(8,128)(2,1)S(1)} %get-tuple-element.24), channel_id=1, source_target_pairs={{0,8},{1,9},{2,10},{3,11},{4,12},{5,13},{6,14},{7,15},{8,0},{9,1},... | collective-permute-start | bytes 393224 | tf_op jit(solution)/shard_map/ppermute | solution.py:269
  23.0 9.9 %collective-permute-start.9 = (bf16[128,512]{1,0:T(8,128)(2,1)S(1)}, bf16[128,512]{1,0:T(8,128)(2,1)S(1)}, u32[]{:S(2)}, u32[]{:S(2)}) collective-permute-start(bf16[128,512]{1,0:T(8,128)(2,1)S(1)} %get-tuple-element.25), channel_id=1, source_target_pairs={{0,12},{1,13},{2,14},{3,15},{4,8},{5,9},{6,10},{7,11},{8,4},{9,5},... | collective-permute-start | bytes 393224 | tf_op jit(solution)/shard_map/ppermute | solution.py:269
  23.4 9.8 %copy-start.1 = (bf16[128,512]{1,0:T(8,128)(2,1)S(1)}, bf16[128,512]{1,0:T(8,128)(2,1)}, u32[]{:S(2)}) copy-start(bf16[128,512]{1,0:T(8,128)(2,1)} %text_ref.1) | copy-start | bytes 393220
  23.5 9.4 %collective-permute-start.11 = (bf16[128,512]{1,0:T(8,128)(2,1)S(1)}, bf16[128,512]{1,0:T(8,128)(2,1)S(1)}, u32[]{:S(2)}, u32[]{:S(2)}) collective-permute-start(bf16[128,512]{1,0:T(8,128)(2,1)S(1)} %get-tuple-element.29), channel_id=1, source_target_pairs={{0,1},{1,0},{2,3},{3,2},{4,5},{5,4},{6,7},{7,6},{8,9},{9,8},{10,11... | collective-permute-start | bytes 393224 | tf_op jit(solution)/shard_map/ppermute | solution.py:269
  25.1 7.8 %collective-permute-start.12 = (bf16[128,512]{1,0:T(8,128)(2,1)S(1)}, bf16[128,512]{1,0:T(8,128)(2,1)S(1)}, u32[]{:S(2)}, u32[]{:S(2)}) collective-permute-start(bf16[128,512]{1,0:T(8,128)(2,1)S(1)} %get-tuple-element.30), channel_id=1, source_target_pairs={{0,2},{1,3},{2,0},{3,1},{4,6},{5,7},{6,4},{7,5},{8,10},{9,11},{10,... | collective-permute-start | bytes 393224 | tf_op jit(solution)/shard_map/ppermute | solution.py:269
  27.3 5.9 %collective-permute-start.13 = (bf16[128,512]{1,0:T(8,128)(2,1)S(1)}, bf16[128,512]{1,0:T(8,128)(2,1)S(1)}, u32[]{:S(2)}, u32[]{:S(2)}) collective-permute-start(bf16[128,512]{1,0:T(8,128)(2,1)S(1)} %get-tuple-element.31), channel_id=1, source_target_pairs={{0,3},{1,2},{2,1},{3,0},{4,7},{5,6},{6,5},{7,4},{8,11},{9,10},{10,... | collective-permute-start | bytes 393224 | tf_op jit(solution)/shard_map/ppermute | solution.py:269

commit v15 on v14

--- a/solution.py
+++ b/solution.py
@@ -13,6 +13,7 @@
 SPAN = 256
 PIECE = 32
 LATE = 16500
+FAR = 17000
 LOG2_E = math.log2(math.e)
 VMEM = pl.BlockSpec(memory_space=pltpu.VMEM)
 
@@ -187,6 +188,17 @@
         flops=len(parts) * parts[0].size,
         name="add_stacks",
     )
+
+
+def add_far_kernel(*refs):
+    refs[-1][...] = sum(ref[...].astype(jnp.float32) for ref in refs[:-1])
+
+
+def add_far(parts):
+    out = jax.ShapeDtypeStruct(parts[0].shape, jnp.float32)
+    return call(
+        add_far_kernel, [out], parts, flops=FAR * len(parts) * out.size, name="add_far"
+    )[0]
 
 
 def finish_kernel(sides, image_ref, text_ref, *refs):
@@ -252,6 +264,7 @@
     far_count, near_count = plan(grp_count, dev_count)
     low_count = 2 if far_count % 2 == 0 else 1
     high_count = far_count // low_count
+    near_low = 2 if near_count % 2 == 0 else 1
 
     def move(value, grp=0, high=0, low=0, near=0):
         perm = []
@@ -289,18 +302,21 @@
             params, list(early.values()), list(late.values()), stacks
         )
         far_parts = dict(zip([*early, *late], image_parts))
+        def give_back(h, w):
+            return move(far_parts[h, w], high=-h, low=-w)
+
         came = [move(part, grp=-g) for g, part in enumerate(text_parts) if g]
-        far_order = sorted((step for step in far_parts if step != (0, 0)), key=lambda step: step[0])
-        far_came = [move(far_parts[h, w], high=-h, low=-w) for h, w in far_order]
-        near_parts = add_stacks([text_parts[0], *came], near_count)
-        near_parts = [near_parts[0]] + [
-            move(part, near=-n) for n, part in enumerate(near_parts) if n
-        ]
+        own, *sent = add_stacks([text_parts[0], *came], near_count // near_low)
+        came = [move(part, near=-n * near_low) for n, part in enumerate(sent, 1)]
+        own, *sent = add_stacks([own, *came], near_low)
+        far_sum = add_far([far_parts[0, 0]] + [give_back(h, w) for h, w in early if h])
+        far_sum, sent = lax.optimization_barrier((far_sum, sent))
+        came = [move(part, near=-n) for n, part in enumerate(sent, 1)]
+        far_came = [give_back(h, w) for h, w in late] + [give_back(h, w) for h, w in early if w]
         return finish(
             images,
             texts,
-            [(0, part) for part in [far_parts[0, 0]] + far_came]
-            + [(1, part) for part in near_parts],
+            [(0, part) for part in [far_sum] + far_came] + [(1, part) for part in [own] + came],
         )
 
     in_specs = (P(AXES, None), P(AXES, None), P(), P())

time: 34.5 us -> 38.2 us (1.11)
  waiting for transfers between devices: 6.54 us -> 11.9 us
  starting transfers between devices: 20.2 us -> 18.5 us
    ppermute x14 -> x13, waiting for transfers between devices: 6.54 us -> 11.9 us  [move(): return lax.ppermute(value, AXES, perm)]
    ppermute x14 -> x13, starting transfers between devices: 20.2 us -> 18.5 us  [move(): return lax.ppermute(value, AXES, perm)]
    pallas_call x6 -> x8, Pallas kernels: 3.52 us -> 3.6 us  [call(): pl.pallas_call(kernel, out_shape=out_shape, in_specs=[VMEM] * len(operand...]
  transfers between devices with their start and end apart: 14 -> 13, of which waited for: 7 -> 7; matrix products, arithmetic and copies ran while one was open for 0% -> 0% of each run, Pallas kernels for 5% -> 4%
where the time goes in v15:
time: 38.2 us; the launch traced here: 38.1 us
  starting transfers between devices  18.5 us (48%)
  waiting for transfers between devices  11.9 us (31%)
  Pallas kernels  4.62 us (12%)
  between operations  2.04 us (5%)
  local copies, waits for them, and re-layouts  0.92 us (2%)
    ppermute x13, starting transfers between devices, move(): return lax.ppermute(value, AXES, perm)  18.5 us
    ppermute x13, waiting for transfers between devices, move(): return lax.ppermute(value, AXES, perm)  11.9 us
    pallas_call x8, Pallas kernels, call(): pl.pallas_call(kernel, out_shape=out_shape, in_specs=[VMEM] * len(operand...  3.6 us
    pallas_call x1, Pallas kernels, finish(): pl.pallas_call(functools.partial(finish_kernel, [side for side, _ in part...  1.03 us
    unnamed x6, local copies, waits for them, and re-layouts  0.92 us
  transfers between devices with their start and end apart: 13, of which 7 were waited for; matrix products, arithmetic and copies ran while one was open for 0% of the time, Pallas kernels for 4%

profile of v15, /device:TPU:0, one launch (start us, length us, event | category | flops | bytes accessed | tf_op | source)
XLA Modules:
  0.0 38.1 jit_solution(8892597247299277266)
XLA Ops:
  0.6 4.1 %collective-permute-start = (bf16[128,512]{1,0:T(8,128)(2,1)}, bf16[128,512]{1,0:T(8,128)(2,1)S(1)}, u32[]{:S(2)}, u32[]{:S(2)}) collective-permute-start(bf16[128,512]{1,0:T(8,128)(2,1)} %image_ref.1), channel_id=1, source_target_pairs={{0,8},{1,9},{2,10},{3,11},{4,12},{5,13},{6,14},{7,15},{8,0},{9,1},... | collective-permute-start | bytes 393224 | tf_op jit(solution)/shard_map/ppermute | solution.py:282
  4.7 1.5 %collective-permute-start.2 = (bf16[128,512]{1,0:T(8,128)(2,1)}, bf16[128,512]{1,0:T(8,128)(2,1)S(1)}, u32[]{:S(2)}, u32[]{:S(2)}) collective-permute-start(bf16[128,512]{1,0:T(8,128)(2,1)} %text_ref.1), channel_id=1, source_target_pairs={{0,2},{1,3},{2,0},{3,1},{4,6},{5,7},{6,4},{7,5},{8,10},{9,11},{10,... | collective-permute-start | bytes 393224 | tf_op jit(solution)/shard_map/ppermute | solution.py:282
  6.3 1.5 %collective-permute-start.1 = (bf16[128,512]{1,0:T(8,128)(2,1)}, bf16[128,512]{1,0:T(8,128)(2,1)S(1)}, u32[]{:S(2)}, u32[]{:S(2)}) collective-permute-start(bf16[128,512]{1,0:T(8,128)(2,1)} %text_ref.1), channel_id=1, source_target_pairs={{0,1},{1,0},{2,3},{3,2},{4,5},{5,4},{6,7},{7,6},{8,9},{9,8},{10,11... | collective-permute-start | bytes 393224 | tf_op jit(solution)/shard_map/ppermute | solution.py:282
  7.7 0.5 %collective-permute-start.3 = (bf16[128,512]{1,0:T(8,128)(2,1)}, bf16[128,512]{1,0:T(8,128)(2,1)S(1)}, u32[]{:S(2)}, u32[]{:S(2)}) collective-permute-start(bf16[128,512]{1,0:T(8,128)(2,1)} %text_ref.1), channel_id=1, source_target_pairs={{0,3},{1,2},{2,1},{3,0},{4,7},{5,6},{6,5},{7,4},{8,11},{9,10},{10,... | collective-permute-start | bytes 393224 | tf_op jit(solution)/shard_map/ppermute | solution.py:282
  8.2 1.6 %collective-permute-start.4 = (bf16[128,512]{1,0:T(8,128)(2,1)}, bf16[128,512]{1,0:T(8,128)(2,1)S(1)}, u32[]{:S(2)}, u32[]{:S(2)}) collective-permute-start(bf16[128,512]{1,0:T(8,128)(2,1)} %image_ref.1), channel_id=1, source_target_pairs={{0,4},{1,5},{2,6},{3,7},{4,0},{5,1},{6,2},{7,3},{8,12},{9,13},{10,... | collective-permute-start | bytes 393224 | tf_op jit(solution)/shard_map/ppermute | solution.py:282
  11.2 0.2 collective-permute-done.refs_1_
  11.4 0.8 %collective-permute-start.5 = (bf16[128,512]{1,0:T(8,128)(2,1)S(1)}, bf16[128,512]{1,0:T(8,128)(2,1)S(1)}, u32[]{:S(2)}, u32[]{:S(2)}) collective-permute-start(bf16[128,512]{1,0:T(8,128)(2,1)S(1)} %collective-permute-done.refs_1_), channel_id=1, source_target_pairs={{0,4},{1,5},{2,6},{3,7},{4,0},{5,1},{6,2},{7,3},{8,12},{9,13},{10,... | collective-permute-start | bytes 393224 | tf_op jit(solution)/shard_map/ppermute | solution.py:282
  12.1 0.9 %copy-done = bf16[128,512]{1,0:T(8,128)(2,1)S(1)} copy-done((bf16[128,512]{1,0:T(8,128)(2,1)S(1)}, bf16[128,512]{1,0:T(8,128)(2,1)}, u32[]{:S(2)}) %copy-start) | copy-done | bytes 131096
  13.0 0.1 own_units.1.refs_0_
  13.2 1.0 %collective-permute-done.3.refs_3_ = bf16[128,512]{1,0:T(8,128)(2,1)S(1)} collective-permute-done((bf16[128,512]{1,0:T(8,128)(2,1)}, bf16[128,512]{1,0:T(8,128)(2,1)S(1)}, u32[]{:S(2)}, u32[]{:S(2)}) %collective-permute-start.3) | collective-permute-done | bytes 131104 | tf_op jit(solution)/shard_map/ppermute | solution.py:282
  14.2 0.2 stack_units.1.text_ref.own_text_ref
  14.4 0.4 %collective-permute-done.4.refs_2_ = bf16[128,512]{1,0:T(8,128)(2,1)S(1)} collective-permute-done((bf16[128,512]{1,0:T(8,128)(2,1)}, bf16[128,512]{1,0:T(8,128)(2,1)S(1)}, u32[]{:S(2)}, u32[]{:S(2)}) %collective-permute-start.4) | collective-permute-done | bytes 131104 | tf_op jit(solution)/shard_map/ppermute | solution.py:282
  14.9 1.1 %early_pairs.1 = (f32[512,512]{1,0:T(8,128)S(1)}, bf16[384,512]{1,0:T(8,128)(2,1)S(1)}, f32[384,512]{1,0:T(8,128)S(1)}) custom-call(f32[1,3]{1,0:T(1,128)S(1)} %maximum_bitcast_fusion.params_ref, bf16[512,512]{1,0:T(8,128)(2,1)S(1)} %stack_units.1.text_ref.own_text_ref, bf16[128,512]{1,0:T(8,128)(2,1)S(1)} %copy-done.2, ...), custom_call_target="tpu_custom_call" | custom-call | flops 603979776 | bytes 3145740 | tf_op jit(solution)/shard_map/early_pairs/pallas_call | solution.py:29
  16.0 0.9 %collective-permute-done.5.refs_0_ = bf16[128,512]{1,0:T(8,128)(2,1)S(1)} collective-permute-done((bf16[128,512]{1,0:T(8,128)(2,1)S(1)}, bf16[128,512]{1,0:T(8,128)(2,1)S(1)}, u32[]{:S(2)}, u32[]{:S(2)}) %collective-permute-start.5) | collective-permute-done | bytes 131104 | tf_op jit(solution)/shard_map/ppermute | solution.py:282
  17.0 1.9 %rest_pairs.1 = (f32[512,512]{1,0:T(8,128)S(1)}, bf16[512,512]{1,0:T(8,128)(2,1)S(1)}, f32[128,512]{1,0:T(8,128)S(1)}, bf16[128,512]{1,0:T(8,128)(2,1)S(1)}, bf1...) custom-call(f32[1,3]{1,0:T(1,128)S(1)} %maximum_bitcast_fusion.params_ref, ...), custom_call_target="tpu_custom_call" | custom-call | flops 1006632960 | bytes 5636108 | tf_op jit(solution)/shard_map/rest_pairs/pallas_call | solution.py:29
  19.0 2.3 %collective-permute-start.7 = (bf16[128,512]{1,0:T(8,128)(2,1)S(1)}, bf16[128,512]{1,0:T(8,128)(2,1)S(1)}, u32[]{:S(2)}, u32[]{:S(2)}) collective-permute-start(bf16[128,512]{1,0:T(8,128)(2,1)S(1)} %get-tuple-element.25), channel_id=1, source_target_pairs={{0,8},{1,9},{2,10},{3,11},{4,12},{5,13},{6,14},{7,15},{8,0},{9,1},... | collective-permute-start | bytes 393224 | tf_op jit(solution)/shard_map/ppermute | solution.py:282
  21.2 0.1 add_stacks.2
  21.4 1.6 %collective-permute-start.9 = (bf16[256,512]{1,0:T(8,128)(2,1)S(1)}, bf16[256,512]{1,0:T(8,128)(2,1)S(1)}, u32[]{:S(2)}, u32[]{:S(2)}) collective-permute-start(bf16[256,512]{1,0:T(8,128)(2,1)S(1)} %get-tuple-element.29), channel_id=1, source_target_pairs={{0,2},{1,3},{2,0},{3,1},{4,6},{5,7},{6,4},{7,5},{8,10},{9,11},{10,... | collective-permute-start | bytes 786440 | tf_op jit(solution)/shard_map/ppermute | solution.py:282
  22.9 3.0 %collective-permute-start.10 = (bf16[128,512]{1,0:T(8,128)(2,1)S(1)}, bf16[128,512]{1,0:T(8,128)(2,1)S(1)}, u32[]{:S(2)}, u32[]{:S(2)}) collective-permute-start(bf16[128,512]{1,0:T(8,128)(2,1)S(1)} %get-tuple-element.32), channel_id=1, source_target_pairs={{0,12},{1,13},{2,14},{3,15},{4,8},{5,9},{6,10},{7,11},{8,4},{9,5},... | collective-permute-start | bytes 393224 | tf_op jit(solution)/shard_map/ppermute | solution.py:282
  26.0 5.9 %collective-permute-done.7.refs_1_ = bf16[128,512]{1,0:T(8,128)(2,1)S(1)} collective-permute-done((bf16[128,512]{1,0:T(8,128)(2,1)S(1)}, bf16[128,512]{1,0:T(8,128)(2,1)S(1)}, u32[]{:S(2)}, u32[]{:S(2)}) %collective-permute-start.7) | collective-permute-done | bytes 131104 | tf_op jit(solution)/shard_map/ppermute | solution.py:282
  32.0 1.6 %collective-permute-start.12 = (bf16[128,512]{1,0:T(8,128)(2,1)S(1)}, bf16[128,512]{1,0:T(8,128)(2,1)S(1)}, u32[]{:S(2)}, u32[]{:S(2)}) collective-permute-start(bf16[128,512]{1,0:T(8,128)(2,1)S(1)} %get-tuple-element.35), channel_id=1, source_target_pairs={{0,1},{1,0},{2,3},{3,2},{4,5},{5,4},{6,7},{7,6},{8,9},{9,8},{10,11... | collective-permute-start | bytes 393224 | tf_op jit(solution)/shard_map/ppermute | solution.py:282
  33.6 0.6 %collective-permute-done.11.refs_2_ = bf16[128,512]{1,0:T(8,128)(2,1)S(1)} collective-permute-done((bf16[128,512]{1,0:T(8,128)(2,1)S(1)}, bf16[128,512]{1,0:T(8,128)(2,1)S(1)}, u32[]{:S(2)}, u32[]{:S(2)}) %collective-permute-start.11) | collective-permute-done | bytes 131104 | tf_op jit(solution)/shard_map/ppermute | solution.py:282
  34.2 2.8 %collective-permute-done.12.refs_4_ = bf16[128,512]{1,0:T(8,128)(2,1)S(1)} collective-permute-done((bf16[128,512]{1,0:T(8,128)(2,1)S(1)}, bf16[128,512]{1,0:T(8,128)(2,1)S(1)}, u32[]{:S(2)}, u32[]{:S(2)}) %collective-permute-start.12) | collective-permute-done | bytes 131104 | tf_op jit(solution)/shard_map/ppermute | solution.py:282
  37.0 1.0 %finish.1 = (f32[128,512]{1,0:T(8,128)}, f32[128,512]{1,0:T(8,128)}) custom-call(bf16[128,512]{1,0:T(8,128)(2,1)S(1)} %copy-done.2, bf16[128,512]{1,0:T(8,128)(2,1)S(1)} %copy-done.1, f32[128,512]{1,0:T(8,128)S(1)} %add_far.1.refs_0_, bf16[128,512]{1,0:T(8,128)(2,1)S(1)} %collective-permute-done.10.refs_1_, ...), custom_call_target="tpu_custom_call" | custom-call | flops 3276800 | bytes 983040 | tf_op jit(solution)/shard_map/finish/pallas_call | solution.py:231
  (18 shorter events, 0.4 us)
Async XLA Ops:
  0.6 10.7 %collective-permute-start = (bf16[128,512]{1,0:T(8,128)(2,1)}, bf16[128,512]{1,0:T(8,128)(2,1)S(1)}, u32[]{:S(2)}, u32[]{:S(2)}) collective-permute-start(bf16[128,512]{1,0:T(8,128)(2,1)} %image_ref.1), channel_id=1, source_target_pairs={{0,8},{1,9},{2,10},{3,11},{4,12},{5,13},{6,14},{7,15},{8,0},{9,1},... | collective-permute-start | bytes 393224 | tf_op jit(solution)/shard_map/ppermute | solution.py:282
  4.7 8.4 %collective-permute-start.2 = (bf16[128,512]{1,0:T(8,128)(2,1)}, bf16[128,512]{1,0:T(8,128)(2,1)S(1)}, u32[]{:S(2)}, u32[]{:S(2)}) collective-permute-start(bf16[128,512]{1,0:T(8,128)(2,1)} %text_ref.1), channel_id=1, source_target_pairs={{0,2},{1,3},{2,0},{3,1},{4,6},{5,7},{6,4},{7,5},{8,10},{9,11},{10,... | collective-permute-start | bytes 393224 | tf_op jit(solution)/shard_map/ppermute | solution.py:282
  6.3 6.9 %collective-permute-start.1 = (bf16[128,512]{1,0:T(8,128)(2,1)}, bf16[128,512]{1,0:T(8,128)(2,1)S(1)}, u32[]{:S(2)}, u32[]{:S(2)}) collective-permute-start(bf16[128,512]{1,0:T(8,128)(2,1)} %text_ref.1), channel_id=1, source_target_pairs={{0,1},{1,0},{2,3},{3,2},{4,5},{5,4},{6,7},{7,6},{8,9},{9,8},{10,11... | collective-permute-start | bytes 393224 | tf_op jit(solution)/shard_map/ppermute | solution.py:282
  7.7 6.4 %collective-permute-start.3 = (bf16[128,512]{1,0:T(8,128)(2,1)}, bf16[128,512]{1,0:T(8,128)(2,1)S(1)}, u32[]{:S(2)}, u32[]{:S(2)}) collective-permute-start(bf16[128,512]{1,0:T(8,128)(2,1)} %text_ref.1), channel_id=1, source_target_pairs={{0,3},{1,2},{2,1},{3,0},{4,7},{5,6},{6,5},{7,4},{8,11},{9,10},{10,... | collective-permute-start | bytes 393224 | tf_op jit(solution)/shard_map/ppermute | solution.py:282
  8.2 6.6 %collective-permute-start.4 = (bf16[128,512]{1,0:T(8,128)(2,1)}, bf16[128,512]{1,0:T(8,128)(2,1)S(1)}, u32[]{:S(2)}, u32[]{:S(2)}) collective-permute-start(bf16[128,512]{1,0:T(8,128)(2,1)} %image_ref.1), channel_id=1, source_target_pairs={{0,4},{1,5},{2,6},{3,7},{4,0},{5,1},{6,2},{7,3},{8,12},{9,13},{10,... | collective-permute-start | bytes 393224 | tf_op jit(solution)/shard_map/ppermute | solution.py:282
  11.4 5.5 %collective-permute-start.5 = (bf16[128,512]{1,0:T(8,128)(2,1)S(1)}, bf16[128,512]{1,0:T(8,128)(2,1)S(1)}, u32[]{:S(2)}, u32[]{:S(2)}) collective-permute-start(bf16[128,512]{1,0:T(8,128)(2,1)S(1)} %collective-permute-done.refs_1_), channel_id=1, source_target_pairs={{0,4},{1,5},{2,6},{3,7},{4,0},{5,1},{6,2},{7,3},{8,12},{9,13},{10,... | collective-permute-start | bytes 393224 | tf_op jit(solution)/shard_map/ppermute | solution.py:282
  12.1 0.9 %copy-start = (bf16[128,512]{1,0:T(8,128)(2,1)S(1)}, bf16[128,512]{1,0:T(8,128)(2,1)}, u32[]{:S(2)}) copy-start(bf16[128,512]{1,0:T(8,128)(2,1)} %text_ref.1) | copy-start | bytes 393220
  13.1 1.7 %copy-start.2 = (bf16[128,512]{1,0:T(8,128)(2,1)S(1)}, bf16[128,512]{1,0:T(8,128)(2,1)}, u32[]{:S(2)}) copy-start(bf16[128,512]{1,0:T(8,128)(2,1)} %image_ref.1) | copy-start | bytes 393220
  14.3 2.6 %collective-permute-start.6 = (bf16[512,512]{1,0:T(8,128)(2,1)S(1)}, bf16[512,512]{1,0:T(8,128)(2,1)S(1)}, u32[]{:S(2)}, u32[]{:S(2)}) collective-permute-start(bf16[512,512]{1,0:T(8,128)(2,1)S(1)} %stack_units.1.text_ref.own_text_ref), channel_id=1, source_target_pairs={{0,16},{1,17},{2,18},{3,19},{4,20},{5,21},{6,22},{7,23},{8,24},{9,... | collective-permute-start | bytes 1572872 | tf_op jit(solution)/shard_map/ppermute | solution.py:282
  18.9 2.4 %collective-permute-start.8 = (bf16[512,512]{1,0:T(8,128)(2,1)S(1)}, bf16[512,512]{1,0:T(8,128)(2,1)S(1)}, u32[]{:S(2)}, u32[]{:S(2)}) collective-permute-start(bf16[512,512]{1,0:T(8,128)(2,1)S(1)} %get-tuple-element.27), channel_id=1, source_target_pairs={{0,16},{1,17},{2,18},{3,19},{4,20},{5,21},{6,22},{7,23},{8,24},{9,... | collective-permute-start | bytes 1572872 | tf_op jit(solution)/shard_map/ppermute | solution.py:282
  19.0 12.9 %collective-permute-start.7 = (bf16[128,512]{1,0:T(8,128)(2,1)S(1)}, bf16[128,512]{1,0:T(8,128)(2,1)S(1)}, u32[]{:S(2)}, u32[]{:S(2)}) collective-permute-start(bf16[128,512]{1,0:T(8,128)(2,1)S(1)} %get-tuple-element.25), channel_id=1, source_target_pairs={{0,8},{1,9},{2,10},{3,11},{4,12},{5,13},{6,14},{7,15},{8,0},{9,1},... | collective-permute-start | bytes 393224 | tf_op jit(solution)/shard_map/ppermute | solution.py:282
  21.4 10.6 %collective-permute-start.9 = (bf16[256,512]{1,0:T(8,128)(2,1)S(1)}, bf16[256,512]{1,0:T(8,128)(2,1)S(1)}, u32[]{:S(2)}, u32[]{:S(2)}) collective-permute-start(bf16[256,512]{1,0:T(8,128)(2,1)S(1)} %get-tuple-element.29), channel_id=1, source_target_pairs={{0,2},{1,3},{2,0},{3,1},{4,6},{5,7},{6,4},{7,5},{8,10},{9,11},{10,... | collective-permute-start | bytes 786440 | tf_op jit(solution)/shard_map/ppermute | solution.py:282
  22.9 10.7 %collective-permute-start.10 = (bf16[128,512]{1,0:T(8,128)(2,1)S(1)}, bf16[128,512]{1,0:T(8,128)(2,1)S(1)}, u32[]{:S(2)}, u32[]{:S(2)}) collective-permute-start(bf16[128,512]{1,0:T(8,128)(2,1)S(1)} %get-tuple-element.32), channel_id=1, source_target_pairs={{0,12},{1,13},{2,14},{3,15},{4,8},{5,9},{6,10},{7,11},{8,4},{9,5},... | collective-permute-start | bytes 393224 | tf_op jit(solution)/shard_map/ppermute | solution.py:282
  26.0 8.3 %collective-permute-start.11 = (bf16[128,512]{1,0:T(8,128)(2,1)S(1)}, bf16[128,512]{1,0:T(8,128)(2,1)S(1)}, u32[]{:S(2)}, u32[]{:S(2)}) collective-permute-start(bf16[128,512]{1,0:T(8,128)(2,1)S(1)} %get-tuple-element.33), channel_id=1, source_target_pairs={{0,4},{1,5},{2,6},{3,7},{4,0},{5,1},{6,2},{7,3},{8,12},{9,13},{10,... | collective-permute-start | bytes 393224 | tf_op jit(solution)/shard_map/ppermute | solution.py:282
  31.9 5.1 %copy-start.1 = (bf16[128,512]{1,0:T(8,128)(2,1)S(1)}, bf16[128,512]{1,0:T(8,128)(2,1)}, u32[]{:S(2)}) copy-start(bf16[128,512]{1,0:T(8,128)(2,1)} %text_ref.1) | copy-start | bytes 393220
  32.0 5.0 %collective-permute-start.12 = (bf16[128,512]{1,0:T(8,128)(2,1)S(1)}, bf16[128,512]{1,0:T(8,128)(2,1)S(1)}, u32[]{:S(2)}, u32[]{:S(2)}) collective-permute-start(bf16[128,512]{1,0:T(8,128)(2,1)S(1)} %get-tuple-element.35), channel_id=1, source_target_pairs={{0,1},{1,0},{2,3},{3,2},{4,5},{5,4},{6,7},{7,6},{8,9},{9,8},{10,11... | collective-permute-start | bytes 393224 | tf_op jit(solution)/shard_map/ppermute | solution.py:282

commit v16 on v15

--- a/solution.py
+++ b/solution.py
@@ -13,7 +13,6 @@
 SPAN = 256
 PIECE = 32
 LATE = 16500
-FAR = 17000
 LOG2_E = math.log2(math.e)
 VMEM = pl.BlockSpec(memory_space=pltpu.VMEM)
 
@@ -188,17 +187,6 @@
         flops=len(parts) * parts[0].size,
         name="add_stacks",
     )
-
-
-def add_far_kernel(*refs):
-    refs[-1][...] = sum(ref[...].astype(jnp.float32) for ref in refs[:-1])
-
-
-def add_far(parts):
-    out = jax.ShapeDtypeStruct(parts[0].shape, jnp.float32)
-    return call(
-        add_far_kernel, [out], parts, flops=FAR * len(parts) * out.size, name="add_far"
-    )[0]
 
 
 def finish_kernel(sides, image_ref, text_ref, *refs):
@@ -309,14 +297,13 @@
         own, *sent = add_stacks([text_parts[0], *came], near_count // near_low)
         came = [move(part, near=-n * near_low) for n, part in enumerate(sent, 1)]
         own, *sent = add_stacks([own, *came], near_low)
-        far_sum = add_far([far_parts[0, 0]] + [give_back(h, w) for h, w in early if h])
-        far_sum, sent = lax.optimization_barrier((far_sum, sent))
         came = [move(part, near=-n) for n, part in enumerate(sent, 1)]
-        far_came = [give_back(h, w) for h, w in late] + [give_back(h, w) for h, w in early if w]
+        far_order = sorted((step for step in far_parts if step != (0, 0)), key=lambda step: -step[0])
+        far_came = [give_back(h, w) for h, w in far_order]
         return finish(
             images,
             texts,
-            [(0, part) for part in [far_sum] + far_came] + [(1, part) for part in [own] + came],
+            [(0, part) for part in [far_parts[0, 0]] + far_came] + [(1, part) for part in [own] + came],
         )
 
     in_specs = (P(AXES, None), P(AXES, None), P(), P())

time: 38.2 us -> 37 us (0.969)
  starting transfers between devices: 18.5 us -> 17.2 us
    ppermute x13, starting transfers between devices: 18.5 us -> 17.2 us  [move(): return lax.ppermute(value, AXES, perm)]
    pallas_call x8 -> x7, Pallas kernels: 3.6 us -> 3.56 us  [call(): pl.pallas_call(kernel, out_shape=out_shape, in_specs=[VMEM] * len(operand...]
  transfers between devices with their start and end apart: 13 -> 13, of which waited for: 7 -> 8; matrix products, arithmetic and copies ran while one was open for 0% -> 0% of each run, Pallas kernels for 4% -> 4%
where the time goes in v16:
time: 37 us; the launch traced here: 36.8 us
  starting transfers between devices  17.2 us (46%)
  waiting for transfers between devices  12 us (32%)
  Pallas kernels  4.6 us (12%)
  between operations  2.02 us (5%)
  local copies, waits for them, and re-layouts  0.91 us (2%)
    ppermute x13, starting transfers between devices, move(): return lax.ppermute(value, AXES, perm)  17.2 us
    ppermute x13, waiting for transfers between devices, move(): return lax.ppermute(value, AXES, perm)  12 us
    pallas_call x7, Pallas kernels, call(): pl.pallas_call(kernel, out_shape=out_shape, in_specs=[VMEM] * len(operand...  3.56 us
    pallas_call x1, Pallas kernels, finish(): pl.pallas_call(functools.partial(finish_kernel, [side for side, _ in part...  1.03 us
    unnamed x6, local copies, waits for them, and re-layouts  0.91 us
  transfers between devices with their start and end apart: 13, of which 8 were waited for; matrix products, arithmetic and copies ran while one was open for 0% of the time, Pallas kernels for 4%

profile of v16, /device:TPU:0, one launch (start us, length us, event | category | flops | bytes accessed | tf_op | source)
XLA Modules:
  0.0 36.8 jit_solution(12224070707473496108)
XLA Ops:
  0.6 4.1 %collective-permute-start = (bf16[128,512]{1,0:T(8,128)(2,1)}, bf16[128,512]{1,0:T(8,128)(2,1)S(1)}, u32[]{:S(2)}, u32[]{:S(2)}) collective-permute-start(bf16[128,512]{1,0:T(8,128)(2,1)} %image_ref.1), channel_id=1, source_target_pairs={{0,8},{1,9},{2,10},{3,11},{4,12},{5,13},{6,14},{7,15},{8,0},{9,1},... | collective-permute-start | bytes 393224 | tf_op jit(solution)/shard_map/ppermute | solution.py:270
  4.7 1.5 %collective-permute-start.2 = (bf16[128,512]{1,0:T(8,128)(2,1)}, bf16[128,512]{1,0:T(8,128)(2,1)S(1)}, u32[]{:S(2)}, u32[]{:S(2)}) collective-permute-start(bf16[128,512]{1,0:T(8,128)(2,1)} %text_ref.1), channel_id=1, source_target_pairs={{0,2},{1,3},{2,0},{3,1},{4,6},{5,7},{6,4},{7,5},{8,10},{9,11},{10,... | collective-permute-start | bytes 393224 | tf_op jit(solution)/shard_map/ppermute | solution.py:270
  6.3 1.5 %collective-permute-start.1 = (bf16[128,512]{1,0:T(8,128)(2,1)}, bf16[128,512]{1,0:T(8,128)(2,1)S(1)}, u32[]{:S(2)}, u32[]{:S(2)}) collective-permute-start(bf16[128,512]{1,0:T(8,128)(2,1)} %text_ref.1), channel_id=1, source_target_pairs={{0,1},{1,0},{2,3},{3,2},{4,5},{5,4},{6,7},{7,6},{8,9},{9,8},{10,11... | collective-permute-start | bytes 393224 | tf_op jit(solution)/shard_map/ppermute | solution.py:270
  7.7 0.5 %collective-permute-start.3 = (bf16[128,512]{1,0:T(8,128)(2,1)}, bf16[128,512]{1,0:T(8,128)(2,1)S(1)}, u32[]{:S(2)}, u32[]{:S(2)}) collective-permute-start(bf16[128,512]{1,0:T(8,128)(2,1)} %text_ref.1), channel_id=1, source_target_pairs={{0,3},{1,2},{2,1},{3,0},{4,7},{5,6},{6,5},{7,4},{8,11},{9,10},{10,... | collective-permute-start | bytes 393224 | tf_op jit(solution)/shard_map/ppermute | solution.py:270
  8.2 1.6 %collective-permute-start.4 = (bf16[128,512]{1,0:T(8,128)(2,1)}, bf16[128,512]{1,0:T(8,128)(2,1)S(1)}, u32[]{:S(2)}, u32[]{:S(2)}) collective-permute-start(bf16[128,512]{1,0:T(8,128)(2,1)} %image_ref.1), channel_id=1, source_target_pairs={{0,4},{1,5},{2,6},{3,7},{4,0},{5,1},{6,2},{7,3},{8,12},{9,13},{10,... | collective-permute-start | bytes 393224 | tf_op jit(solution)/shard_map/ppermute | solution.py:270
  11.2 0.2 collective-permute-done.refs_1_
  11.4 0.8 %collective-permute-start.5 = (bf16[128,512]{1,0:T(8,128)(2,1)S(1)}, bf16[128,512]{1,0:T(8,128)(2,1)S(1)}, u32[]{:S(2)}, u32[]{:S(2)}) collective-permute-start(bf16[128,512]{1,0:T(8,128)(2,1)S(1)} %collective-permute-done.refs_1_), channel_id=1, source_target_pairs={{0,4},{1,5},{2,6},{3,7},{4,0},{5,1},{6,2},{7,3},{8,12},{9,13},{10,... | collective-permute-start | bytes 393224 | tf_op jit(solution)/shard_map/ppermute | solution.py:270
  12.1 0.9 %copy-done = bf16[128,512]{1,0:T(8,128)(2,1)S(1)} copy-done((bf16[128,512]{1,0:T(8,128)(2,1)S(1)}, bf16[128,512]{1,0:T(8,128)(2,1)}, u32[]{:S(2)}) %copy-start) | copy-done | bytes 131096
  13.2 1.0 %collective-permute-done.3.refs_3_ = bf16[128,512]{1,0:T(8,128)(2,1)S(1)} collective-permute-done((bf16[128,512]{1,0:T(8,128)(2,1)}, bf16[128,512]{1,0:T(8,128)(2,1)S(1)}, u32[]{:S(2)}, u32[]{:S(2)}) %collective-permute-start.3) | collective-permute-done | bytes 131104 | tf_op jit(solution)/shard_map/ppermute | solution.py:270
  14.2 0.2 stack_units.1.text_ref.own_text_ref
  14.4 0.4 %collective-permute-done.4.refs_2_ = bf16[128,512]{1,0:T(8,128)(2,1)S(1)} collective-permute-done((bf16[128,512]{1,0:T(8,128)(2,1)}, bf16[128,512]{1,0:T(8,128)(2,1)S(1)}, u32[]{:S(2)}, u32[]{:S(2)}) %collective-permute-start.4) | collective-permute-done | bytes 131104 | tf_op jit(solution)/shard_map/ppermute | solution.py:270
  14.9 1.1 %early_pairs.1 = (f32[512,512]{1,0:T(8,128)S(1)}, bf16[384,512]{1,0:T(8,128)(2,1)S(1)}, f32[384,512]{1,0:T(8,128)S(1)}) custom-call(f32[1,3]{1,0:T(1,128)S(1)} %maximum_bitcast_fusion.params_ref, bf16[512,512]{1,0:T(8,128)(2,1)S(1)} %stack_units.1.text_ref.own_text_ref, bf16[128,512]{1,0:T(8,128)(2,1)S(1)} %copy-done.2, ...), custom_call_target="tpu_custom_call" | custom-call | flops 603979776 | bytes 3145740 | tf_op jit(solution)/shard_map/early_pairs/pallas_call | solution.py:28
  16.0 0.9 %collective-permute-done.5.refs_0_ = bf16[128,512]{1,0:T(8,128)(2,1)S(1)} collective-permute-done((bf16[128,512]{1,0:T(8,128)(2,1)S(1)}, bf16[128,512]{1,0:T(8,128)(2,1)S(1)}, u32[]{:S(2)}, u32[]{:S(2)}) %collective-permute-start.5) | collective-permute-done | bytes 131104 | tf_op jit(solution)/shard_map/ppermute | solution.py:270
  17.0 1.9 %rest_pairs.1 = (f32[512,512]{1,0:T(8,128)S(1)}, bf16[512,512]{1,0:T(8,128)(2,1)S(1)}, f32[128,512]{1,0:T(8,128)S(1)}, bf16[128,512]{1,0:T(8,128)(2,1)S(1)}, bf1...) custom-call(f32[1,3]{1,0:T(1,128)S(1)} %maximum_bitcast_fusion.params_ref, ...), custom_call_target="tpu_custom_call" | custom-call | flops 1006632960 | bytes 5636108 | tf_op jit(solution)/shard_map/rest_pairs/pallas_call | solution.py:28
  19.0 1.9 %collective-permute-done.10.refs_1_ = bf16[512,512]{1,0:T(8,128)(2,1)S(1)} collective-permute-done((bf16[512,512]{1,0:T(8,128)(2,1)S(1)}, bf16[512,512]{1,0:T(8,128)(2,1)S(1)}, u32[]{:S(2)}, u32[]{:S(2)}) %collective-permute-start.10) | collective-permute-done | bytes 524320 | tf_op jit(solution)/shard_map/ppermute | solution.py:270
  21.0 1.6 %collective-permute-start.11 = (bf16[256,512]{1,0:T(8,128)(2,1)S(1)}, bf16[256,512]{1,0:T(8,128)(2,1)S(1)}, u32[]{:S(2)}, u32[]{:S(2)}) collective-permute-start(bf16[256,512]{1,0:T(8,128)(2,1)S(1)} %get-tuple-element.29), channel_id=1, source_target_pairs={{0,2},{1,3},{2,0},{3,1},{4,6},{5,7},{6,4},{7,5},{8,10},{9,11},{10,... | collective-permute-start | bytes 786440 | tf_op jit(solution)/shard_map/ppermute | solution.py:270
  22.6 2.2 %collective-permute-start.7 = (bf16[128,512]{1,0:T(8,128)(2,1)S(1)}, bf16[128,512]{1,0:T(8,128)(2,1)S(1)}, u32[]{:S(2)}, u32[]{:S(2)}) collective-permute-start(bf16[128,512]{1,0:T(8,128)(2,1)S(1)} %get-tuple-element.23), channel_id=1, source_target_pairs={{0,8},{1,9},{2,10},{3,11},{4,12},{5,13},{6,14},{7,15},{8,0},{9,1},... | collective-permute-start | bytes 393224 | tf_op jit(solution)/shard_map/ppermute | solution.py:270
  24.8 1.2 %collective-permute-start.8 = (bf16[128,512]{1,0:T(8,128)(2,1)S(1)}, bf16[128,512]{1,0:T(8,128)(2,1)S(1)}, u32[]{:S(2)}, u32[]{:S(2)}) collective-permute-start(bf16[128,512]{1,0:T(8,128)(2,1)S(1)} %get-tuple-element.24), channel_id=1, source_target_pairs={{0,12},{1,13},{2,14},{3,15},{4,8},{5,9},{6,10},{7,11},{8,4},{9,5},... | collective-permute-start | bytes 393224 | tf_op jit(solution)/shard_map/ppermute | solution.py:270
  26.0 0.6 %collective-permute-start.9 = (bf16[128,512]{1,0:T(8,128)(2,1)S(1)}, bf16[128,512]{1,0:T(8,128)(2,1)S(1)}, u32[]{:S(2)}, u32[]{:S(2)}) collective-permute-start(bf16[128,512]{1,0:T(8,128)(2,1)S(1)} %get-tuple-element.25), channel_id=1, source_target_pairs={{0,4},{1,5},{2,6},{3,7},{4,0},{5,1},{6,2},{7,3},{8,12},{9,13},{10,... | collective-permute-start | bytes 393224 | tf_op jit(solution)/shard_map/ppermute | solution.py:270
  26.5 2.9 %collective-permute-done.11.refs_1_ = bf16[256,512]{1,0:T(8,128)(2,1)S(1)} collective-permute-done((bf16[256,512]{1,0:T(8,128)(2,1)S(1)}, bf16[256,512]{1,0:T(8,128)(2,1)S(1)}, u32[]{:S(2)}, u32[]{:S(2)}) %collective-permute-start.11) | collective-permute-done | bytes 262176 | tf_op jit(solution)/shard_map/ppermute | solution.py:270
  29.4 1.6 %collective-permute-start.12 = (bf16[128,512]{1,0:T(8,128)(2,1)S(1)}, bf16[128,512]{1,0:T(8,128)(2,1)S(1)}, u32[]{:S(2)}, u32[]{:S(2)}) collective-permute-start(bf16[128,512]{1,0:T(8,128)(2,1)S(1)} %get-tuple-element.31), channel_id=1, source_target_pairs={{0,1},{1,0},{2,3},{3,2},{4,5},{5,4},{6,7},{7,6},{8,9},{9,8},{10,11... | collective-permute-start | bytes 393224 | tf_op jit(solution)/shard_map/ppermute | solution.py:270
  31.1 4.2 %collective-permute-done.7.refs_1_ = bf16[128,512]{1,0:T(8,128)(2,1)S(1)} collective-permute-done((bf16[128,512]{1,0:T(8,128)(2,1)S(1)}, bf16[128,512]{1,0:T(8,128)(2,1)S(1)}, u32[]{:S(2)}, u32[]{:S(2)}) %collective-permute-start.7) | collective-permute-done | bytes 131104 | tf_op jit(solution)/shard_map/ppermute | solution.py:270
  35.2 0.5 %collective-permute-done.9.refs_3_ = bf16[128,512]{1,0:T(8,128)(2,1)S(1)} collective-permute-done((bf16[128,512]{1,0:T(8,128)(2,1)S(1)}, bf16[128,512]{1,0:T(8,128)(2,1)S(1)}, u32[]{:S(2)}, u32[]{:S(2)}) %collective-permute-start.9) | collective-permute-done | bytes 131104 | tf_op jit(solution)/shard_map/ppermute | solution.py:270
  35.8 1.0 %finish.1 = (f32[128,512]{1,0:T(8,128)}, f32[128,512]{1,0:T(8,128)}) custom-call(bf16[128,512]{1,0:T(8,128)(2,1)S(1)} %copy-done.2, bf16[128,512]{1,0:T(8,128)(2,1)S(1)} %copy-done.1, f32[128,512]{1,0:T(8,128)S(1)} %get-tuple-element.22.refs_0_, bf16[128,512]{1,0:T(8,128)(2,1)S(1)} %collective-permute-done.7.refs_1_, ...), custom_call_target="tpu_custom_call" | custom-call | flops 3932160 | bytes 1179648 | tf_op jit(solution)/shard_map/finish/pallas_call | solution.py:219
  (17 shorter events, 0.6 us)
Async XLA Ops:
  0.6 10.7 %collective-permute-start = (bf16[128,512]{1,0:T(8,128)(2,1)}, bf16[128,512]{1,0:T(8,128)(2,1)S(1)}, u32[]{:S(2)}, u32[]{:S(2)}) collective-permute-start(bf16[128,512]{1,0:T(8,128)(2,1)} %image_ref.1), channel_id=1, source_target_pairs={{0,8},{1,9},{2,10},{3,11},{4,12},{5,13},{6,14},{7,15},{8,0},{9,1},... | collective-permute-start | bytes 393224 | tf_op jit(solution)/shard_map/ppermute | solution.py:270
  4.7 8.4 %collective-permute-start.2 = (bf16[128,512]{1,0:T(8,128)(2,1)}, bf16[128,512]{1,0:T(8,128)(2,1)S(1)}, u32[]{:S(2)}, u32[]{:S(2)}) collective-permute-start(bf16[128,512]{1,0:T(8,128)(2,1)} %text_ref.1), channel_id=1, source_target_pairs={{0,2},{1,3},{2,0},{3,1},{4,6},{5,7},{6,4},{7,5},{8,10},{9,11},{10,... | collective-permute-start | bytes 393224 | tf_op jit(solution)/shard_map/ppermute | solution.py:270
  6.3 6.9 %collective-permute-start.1 = (bf16[128,512]{1,0:T(8,128)(2,1)}, bf16[128,512]{1,0:T(8,128)(2,1)S(1)}, u32[]{:S(2)}, u32[]{:S(2)}) collective-permute-start(bf16[128,512]{1,0:T(8,128)(2,1)} %text_ref.1), channel_id=1, source_target_pairs={{0,1},{1,0},{2,3},{3,2},{4,5},{5,4},{6,7},{7,6},{8,9},{9,8},{10,11... | collective-permute-start | bytes 393224 | tf_op jit(solution)/shard_map/ppermute | solution.py:270
  7.7 6.4 %collective-permute-start.3 = (bf16[128,512]{1,0:T(8,128)(2,1)}, bf16[128,512]{1,0:T(8,128)(2,1)S(1)}, u32[]{:S(2)}, u32[]{:S(2)}) collective-permute-start(bf16[128,512]{1,0:T(8,128)(2,1)} %text_ref.1), channel_id=1, source_target_pairs={{0,3},{1,2},{2,1},{3,0},{4,7},{5,6},{6,5},{7,4},{8,11},{9,10},{10,... | collective-permute-start | bytes 393224 | tf_op jit(solution)/shard_map/ppermute | solution.py:270
  8.2 6.6 %collective-permute-start.4 = (bf16[128,512]{1,0:T(8,128)(2,1)}, bf16[128,512]{1,0:T(8,128)(2,1)S(1)}, u32[]{:S(2)}, u32[]{:S(2)}) collective-permute-start(bf16[128,512]{1,0:T(8,128)(2,1)} %image_ref.1), channel_id=1, source_target_pairs={{0,4},{1,5},{2,6},{3,7},{4,0},{5,1},{6,2},{7,3},{8,12},{9,13},{10,... | collective-permute-start | bytes 393224 | tf_op jit(solution)/shard_map/ppermute | solution.py:270
  11.4 5.5 %collective-permute-start.5 = (bf16[128,512]{1,0:T(8,128)(2,1)S(1)}, bf16[128,512]{1,0:T(8,128)(2,1)S(1)}, u32[]{:S(2)}, u32[]{:S(2)}) collective-permute-start(bf16[128,512]{1,0:T(8,128)(2,1)S(1)} %collective-permute-done.refs_1_), channel_id=1, source_target_pairs={{0,4},{1,5},{2,6},{3,7},{4,0},{5,1},{6,2},{7,3},{8,12},{9,13},{10,... | collective-permute-start | bytes 393224 | tf_op jit(solution)/shard_map/ppermute | solution.py:270
  12.1 0.9 %copy-start = (bf16[128,512]{1,0:T(8,128)(2,1)S(1)}, bf16[128,512]{1,0:T(8,128)(2,1)}, u32[]{:S(2)}) copy-start(bf16[128,512]{1,0:T(8,128)(2,1)} %text_ref.1) | copy-start | bytes 393220
  13.1 1.7 %copy-start.2 = (bf16[128,512]{1,0:T(8,128)(2,1)S(1)}, bf16[128,512]{1,0:T(8,128)(2,1)}, u32[]{:S(2)}) copy-start(bf16[128,512]{1,0:T(8,128)(2,1)} %image_ref.1) | copy-start | bytes 393220
  14.3 2.6 %collective-permute-start.6 = (bf16[512,512]{1,0:T(8,128)(2,1)S(1)}, bf16[512,512]{1,0:T(8,128)(2,1)S(1)}, u32[]{:S(2)}, u32[]{:S(2)}) collective-permute-start(bf16[512,512]{1,0:T(8,128)(2,1)S(1)} %stack_units.1.text_ref.own_text_ref), channel_id=1, source_target_pairs={{0,16},{1,17},{2,18},{3,19},{4,20},{5,21},{6,22},{7,23},{8,24},{9,... | collective-permute-start | bytes 1572872 | tf_op jit(solution)/shard_map/ppermute | solution.py:270
  18.9 2.0 %collective-permute-start.10 = (bf16[512,512]{1,0:T(8,128)(2,1)S(1)}, bf16[512,512]{1,0:T(8,128)(2,1)S(1)}, u32[]{:S(2)}, u32[]{:S(2)}) collective-permute-start(bf16[512,512]{1,0:T(8,128)(2,1)S(1)} %get-tuple-element.27), channel_id=1, source_target_pairs={{0,16},{1,17},{2,18},{3,19},{4,20},{5,21},{6,22},{7,23},{8,24},{9,... | collective-permute-start | bytes 1572872 | tf_op jit(solution)/shard_map/ppermute | solution.py:270
  21.0 8.4 %collective-permute-start.11 = (bf16[256,512]{1,0:T(8,128)(2,1)S(1)}, bf16[256,512]{1,0:T(8,128)(2,1)S(1)}, u32[]{:S(2)}, u32[]{:S(2)}) collective-permute-start(bf16[256,512]{1,0:T(8,128)(2,1)S(1)} %get-tuple-element.29), channel_id=1, source_target_pairs={{0,2},{1,3},{2,0},{3,1},{4,6},{5,7},{6,4},{7,5},{8,10},{9,11},{10,... | collective-permute-start | bytes 786440 | tf_op jit(solution)/shard_map/ppermute | solution.py:270
  22.6 12.6 %collective-permute-start.7 = (bf16[128,512]{1,0:T(8,128)(2,1)S(1)}, bf16[128,512]{1,0:T(8,128)(2,1)S(1)}, u32[]{:S(2)}, u32[]{:S(2)}) collective-permute-start(bf16[128,512]{1,0:T(8,128)(2,1)S(1)} %get-tuple-element.23), channel_id=1, source_target_pairs={{0,8},{1,9},{2,10},{3,11},{4,12},{5,13},{6,14},{7,15},{8,0},{9,1},... | collective-permute-start | bytes 393224 | tf_op jit(solution)/shard_map/ppermute | solution.py:270
  24.8 10.5 %collective-permute-start.8 = (bf16[128,512]{1,0:T(8,128)(2,1)S(1)}, bf16[128,512]{1,0:T(8,128)(2,1)S(1)}, u32[]{:S(2)}, u32[]{:S(2)}) collective-permute-start(bf16[128,512]{1,0:T(8,128)(2,1)S(1)} %get-tuple-element.24), channel_id=1, source_target_pairs={{0,12},{1,13},{2,14},{3,15},{4,8},{5,9},{6,10},{7,11},{8,4},{9,5},... | collective-permute-start | bytes 393224 | tf_op jit(solution)/shard_map/ppermute | solution.py:270
  26.0 9.8 %collective-permute-start.9 = (bf16[128,512]{1,0:T(8,128)(2,1)S(1)}, bf16[128,512]{1,0:T(8,128)(2,1)S(1)}, u32[]{:S(2)}, u32[]{:S(2)}) collective-permute-start(bf16[128,512]{1,0:T(8,128)(2,1)S(1)} %get-tuple-element.25), channel_id=1, source_target_pairs={{0,4},{1,5},{2,6},{3,7},{4,0},{5,1},{6,2},{7,3},{8,12},{9,13},{10,... | collective-permute-start | bytes 393224 | tf_op jit(solution)/shard_map/ppermute | solution.py:270
  29.4 6.4 %copy-start.1 = (bf16[128,512]{1,0:T(8,128)(2,1)S(1)}, bf16[128,512]{1,0:T(8,128)(2,1)}, u32[]{:S(2)}) copy-start(bf16[128,512]{1,0:T(8,128)(2,1)} %text_ref.1) | copy-start | bytes 393220
  29.4 6.3 %collective-permute-start.12 = (bf16[128,512]{1,0:T(8,128)(2,1)S(1)}, bf16[128,512]{1,0:T(8,128)(2,1)S(1)}, u32[]{:S(2)}, u32[]{:S(2)}) collective-permute-start(bf16[128,512]{1,0:T(8,128)(2,1)S(1)} %get-tuple-element.31), channel_id=1, source_target_pairs={{0,1},{1,0},{2,3},{3,2},{4,5},{5,4},{6,7},{7,6},{8,9},{9,8},{10,11... | collective-permute-start | bytes 393224 | tf_op jit(solution)/shard_map/ppermute | solution.py:270

commit v17 on v14

--- a/solution.py
+++ b/solution.py
@@ -11,7 +11,7 @@
 AXES = ("grp", "dev")
 VMEM_LIMIT = 32 * 1024 * 1024
 SPAN = 256
-PIECE = 32
+OWN = 8
 LATE = 16500
 LOG2_E = math.log2(math.e)
 VMEM = pl.BlockSpec(memory_space=pltpu.VMEM)
@@ -189,50 +189,57 @@
     )
 
 
-def finish_kernel(sides, image_ref, text_ref, *refs):
-    parts, outs = refs[:len(sides)], refs[len(sides):len(sides) + 2]
-    staged, sems = refs[len(sides) + 2:]
-    rows = image_ref.shape[0]
-    piece = math.gcd(rows, PIECE)
+def own_rows_kernel(*refs):
+    half = len(refs) // 3
+    for raw, unit_out, factor_out in zip(refs[:half], refs[half::2], refs[half + 1::2]):
+        unit, factor = unit_rows(raw[...])
+        unit_out[...] = unit
+        factor_out[...] = jnp.broadcast_to(factor, factor_out.shape)
+
+
+def own_rows(arrays):
+    out = []
+    for x in arrays:
+        out.append(jax.ShapeDtypeStruct(x.shape, jnp.float32))
+        out.append(jax.ShapeDtypeStruct((x.shape[0], 128), jnp.float32))
+    outs = call(own_rows_kernel, out, arrays, flops=OWN * arrays[0].size, name="own_rows")
+    return list(zip(outs[::2], outs[1::2]))
+
+
+def finish_kernel(sides, *refs):
+    own, parts = refs[:4], refs[4:4 + len(sides)]
+    outs, (staged, sems) = refs[4 + len(sides):6 + len(sides)], refs[6 + len(sides):]
     copies = []
-    for side, raw in enumerate((image_ref, text_ref)):
-        for first in range(0, rows, piece):
-            here = pl.ds(first, piece)
-            unit, factor = unit_rows(raw[here, :])
-            total = sum(
-                ref[here, :].astype(jnp.float32) for at, ref in zip(sides, parts) if at == side
-            )
-            along = jnp.sum(unit * total, axis=-1, keepdims=True)
-            staged[side, here, :] = factor * (total - unit * along)
-            copies.append(
-                pltpu.make_async_copy(
-                    staged.at[side, here, :], outs[side].at[here, :], sems.at[len(copies)]
-                )
-            )
-            copies[-1].start()
+    for side, (unit_ref, factor_ref, out) in enumerate(zip(own[::2], own[1::2], outs)):
+        total = sum(ref[...].astype(jnp.float32) for at, ref in zip(sides, parts) if at == side)
+        unit = unit_ref[...]
+        along = jnp.sum(unit * total, axis=-1, keepdims=True)
+        staged[side] = factor_ref[:, 0:1] * (total - unit * along)
+        copies.append(pltpu.make_async_copy(staged.at[side], out, sems.at[side]))
+        copies[-1].start()
     for copy in copies:
         copy.wait()
 
 
-def finish(images, texts, parts):
-    out = jax.ShapeDtypeStruct(images.shape, jnp.float32)
+def finish(own, parts):
+    shape = own[0][0].shape
+    out = jax.ShapeDtypeStruct(shape, jnp.float32)
+    count = len(parts)
     return pl.pallas_call(
         functools.partial(finish_kernel, [side for side, _ in parts]),
         out_shape=(out, out),
-        in_specs=[VMEM] * (2 + len(parts)),
+        in_specs=[VMEM] * (4 + count),
         out_specs=[pl.BlockSpec(memory_space=pl.ANY)] * 2,
         scratch_shapes=[
-            pltpu.VMEM((2,) + images.shape, jnp.float32),
-            pltpu.SemaphoreType.DMA((2 * (images.shape[0] // math.gcd(images.shape[0], PIECE)),)),
+            pltpu.VMEM((2,) + shape, jnp.float32),
+            pltpu.SemaphoreType.DMA((2,)),
         ],
         compiler_params=pltpu.CompilerParams(vmem_limit_bytes=VMEM_LIMIT),
         cost_estimate=pl.CostEstimate(
-            flops=10 * len(parts) * images.size,
-            bytes_accessed=3 * len(parts) * images.size,
-            transcendentals=0,
+            flops=10 * count * out.size, bytes_accessed=3 * count * out.size, transcendentals=0
         ),
         name="finish",
-    )(images, texts, *[part for _, part in parts])
+    )(*own[0], *own[1], *[part for _, part in parts])
 
 
 def plan(grp_count, dev_count):
@@ -297,8 +304,7 @@
             move(part, near=-n) for n, part in enumerate(near_parts) if n
         ]
         return finish(
-            images,
-            texts,
+            own_rows([images, texts]),
             [(0, part) for part in [far_parts[0, 0]] + far_came]
             + [(1, part) for part in near_parts],
         )

time: 34.5 us -> 34.5 us (level)
    pallas_call x6 -> x7, Pallas kernels: 3.52 us -> 3.65 us  [call(): pl.pallas_call(kernel, out_shape=out_shape, in_specs=[VMEM] * len(operand...]
where the time goes in v17:
time: 34.5 us; the launch traced here: 34.3 us
  starting transfers between devices  20.2 us (59%)
  waiting for transfers between devices  6.4 us (19%)
  Pallas kernels  4.73 us (14%)
  between operations  2.02 us (6%)
  local copies, waits for them, and re-layouts  0.91 us (3%)
    ppermute x14, starting transfers between devices, move(): return lax.ppermute(value, AXES, perm)  20.2 us
    ppermute x14, waiting for transfers between devices, move(): return lax.ppermute(value, AXES, perm)  6.4 us
    pallas_call x7, Pallas kernels, call(): pl.pallas_call(kernel, out_shape=out_shape, in_specs=[VMEM] * len(operand...  3.65 us
    pallas_call x1, Pallas kernels, finish(): pl.pallas_call(functools.partial(finish_kernel, [side for side, _ in part...  1.08 us
    unnamed x6, local copies, waits for them, and re-layouts  0.91 us
  transfers between devices with their start and end apart: 14, of which 7 were waited for; matrix products, arithmetic and copies ran while one was open for 0% of the time, Pallas kernels for 5%

profile of v17, /device:TPU:0, one launch (start us, length us, event | category | flops | bytes accessed | tf_op | source)
XLA Modules:
  0.0 34.3 jit_solution(3172375426429582294)
XLA Ops:
  0.6 4.1 %collective-permute-start = (bf16[128,512]{1,0:T(8,128)(2,1)}, bf16[128,512]{1,0:T(8,128)(2,1)S(1)}, u32[]{:S(2)}, u32[]{:S(2)}) collective-permute-start(bf16[128,512]{1,0:T(8,128)(2,1)} %refs_0_.5), channel_id=1, source_target_pairs={{0,8},{1,9},{2,10},{3,11},{4,12},{5,13},{6,14},{7,15},{8,0},{9,1},... | collective-permute-start | bytes 393224 | tf_op jit(solution)/shard_map/ppermute | solution.py:276
  4.7 1.5 %collective-permute-start.1 = (bf16[128,512]{1,0:T(8,128)(2,1)}, bf16[128,512]{1,0:T(8,128)(2,1)S(1)}, u32[]{:S(2)}, u32[]{:S(2)}) collective-permute-start(bf16[128,512]{1,0:T(8,128)(2,1)} %refs_0_.4), channel_id=1, source_target_pairs={{0,1},{1,0},{2,3},{3,2},{4,5},{5,4},{6,7},{7,6},{8,9},{9,8},{10,11... | collective-permute-start | bytes 393224 | tf_op jit(solution)/shard_map/ppermute | solution.py:276
  6.2 1.5 %collective-permute-start.2 = (bf16[128,512]{1,0:T(8,128)(2,1)}, bf16[128,512]{1,0:T(8,128)(2,1)S(1)}, u32[]{:S(2)}, u32[]{:S(2)}) collective-permute-start(bf16[128,512]{1,0:T(8,128)(2,1)} %refs_0_.4), channel_id=1, source_target_pairs={{0,2},{1,3},{2,0},{3,1},{4,6},{5,7},{6,4},{7,5},{8,10},{9,11},{10,... | collective-permute-start | bytes 393224 | tf_op jit(solution)/shard_map/ppermute | solution.py:276
  7.7 0.5 %collective-permute-start.3 = (bf16[128,512]{1,0:T(8,128)(2,1)}, bf16[128,512]{1,0:T(8,128)(2,1)S(1)}, u32[]{:S(2)}, u32[]{:S(2)}) collective-permute-start(bf16[128,512]{1,0:T(8,128)(2,1)} %refs_0_.4), channel_id=1, source_target_pairs={{0,3},{1,2},{2,1},{3,0},{4,7},{5,6},{6,5},{7,4},{8,11},{9,10},{10,... | collective-permute-start | bytes 393224 | tf_op jit(solution)/shard_map/ppermute | solution.py:276
  8.2 1.6 %collective-permute-start.4 = (bf16[128,512]{1,0:T(8,128)(2,1)}, bf16[128,512]{1,0:T(8,128)(2,1)S(1)}, u32[]{:S(2)}, u32[]{:S(2)}) collective-permute-start(bf16[128,512]{1,0:T(8,128)(2,1)} %refs_0_.5), channel_id=1, source_target_pairs={{0,4},{1,5},{2,6},{3,7},{4,0},{5,1},{6,2},{7,3},{8,12},{9,13},{10,... | collective-permute-start | bytes 393224 | tf_op jit(solution)/shard_map/ppermute | solution.py:276
  11.2 0.2 collective-permute-done.refs_1_
  11.4 0.8 %collective-permute-start.5 = (bf16[128,512]{1,0:T(8,128)(2,1)S(1)}, bf16[128,512]{1,0:T(8,128)(2,1)S(1)}, u32[]{:S(2)}, u32[]{:S(2)}) collective-permute-start(bf16[128,512]{1,0:T(8,128)(2,1)S(1)} %collective-permute-done.refs_1_), channel_id=1, source_target_pairs={{0,4},{1,5},{2,6},{3,7},{4,0},{5,1},{6,2},{7,3},{8,12},{9,13},{10,... | collective-permute-start | bytes 393224 | tf_op jit(solution)/shard_map/ppermute | solution.py:276
  12.1 0.9 %copy-done = bf16[128,512]{1,0:T(8,128)(2,1)S(1)} copy-done((bf16[128,512]{1,0:T(8,128)(2,1)S(1)}, bf16[128,512]{1,0:T(8,128)(2,1)}, u32[]{:S(2)}) %copy-start) | copy-done | bytes 131096
  13.2 1.0 %collective-permute-done.2.refs_2_ = bf16[128,512]{1,0:T(8,128)(2,1)S(1)} collective-permute-done((bf16[128,512]{1,0:T(8,128)(2,1)}, bf16[128,512]{1,0:T(8,128)(2,1)S(1)}, u32[]{:S(2)}, u32[]{:S(2)}) %collective-permute-start.2) | collective-permute-done | bytes 131104 | tf_op jit(solution)/shard_map/ppermute | solution.py:276
  14.2 0.2 stack_units.1.text_ref.own_text_ref
  14.5 0.4 %collective-permute-done.4.refs_2_ = bf16[128,512]{1,0:T(8,128)(2,1)S(1)} collective-permute-done((bf16[128,512]{1,0:T(8,128)(2,1)}, bf16[128,512]{1,0:T(8,128)(2,1)S(1)}, u32[]{:S(2)}, u32[]{:S(2)}) %collective-permute-start.4) | collective-permute-done | bytes 131104 | tf_op jit(solution)/shard_map/ppermute | solution.py:276
  14.9 1.1 %early_pairs.1 = (f32[512,512]{1,0:T(8,128)S(1)}, bf16[384,512]{1,0:T(8,128)(2,1)S(1)}, f32[384,512]{1,0:T(8,128)S(1)}) custom-call(f32[1,3]{1,0:T(1,128)S(1)} %maximum_bitcast_fusion.params_ref, bf16[512,512]{1,0:T(8,128)(2,1)S(1)} %stack_units.1.text_ref.own_text_ref, bf16[128,512]{1,0:T(8,128)(2,1)S(1)} %copy-done.2, ...), custom_call_target="tpu_custom_call" | custom-call | flops 603979776 | bytes 3145740 | tf_op jit(solution)/shard_map/early_pairs/pallas_call | solution.py:28
  16.0 0.9 %collective-permute-done.5.refs_0_ = bf16[128,512]{1,0:T(8,128)(2,1)S(1)} collective-permute-done((bf16[128,512]{1,0:T(8,128)(2,1)S(1)}, bf16[128,512]{1,0:T(8,128)(2,1)S(1)}, u32[]{:S(2)}, u32[]{:S(2)}) %collective-permute-start.5) | collective-permute-done | bytes 131104 | tf_op jit(solution)/shard_map/ppermute | solution.py:276
  17.0 1.9 %rest_pairs.1 = (f32[512,512]{1,0:T(8,128)S(1)}, bf16[512,512]{1,0:T(8,128)(2,1)S(1)}, f32[128,512]{1,0:T(8,128)S(1)}, bf16[128,512]{1,0:T(8,128)(2,1)S(1)}, bf1...) custom-call(f32[1,3]{1,0:T(1,128)S(1)} %maximum_bitcast_fusion.params_ref, ...), custom_call_target="tpu_custom_call" | custom-call | flops 1006632960 | bytes 5636108 | tf_op jit(solution)/shard_map/rest_pairs/pallas_call | solution.py:28
  19.0 1.1 %collective-permute-start.7 = (bf16[128,512]{1,0:T(8,128)(2,1)S(1)}, bf16[128,512]{1,0:T(8,128)(2,1)S(1)}, u32[]{:S(2)}, u32[]{:S(2)}) collective-permute-start(bf16[128,512]{1,0:T(8,128)(2,1)S(1)} %get-tuple-element.31), channel_id=1, source_target_pairs={{0,4},{1,5},{2,6},{3,7},{4,0},{5,1},{6,2},{7,3},{8,12},{9,13},{10,... | collective-permute-start | bytes 393224 | tf_op jit(solution)/shard_map/ppermute | solution.py:276
  20.0 3.0 %collective-permute-start.8 = (bf16[128,512]{1,0:T(8,128)(2,1)S(1)}, bf16[128,512]{1,0:T(8,128)(2,1)S(1)}, u32[]{:S(2)}, u32[]{:S(2)}) collective-permute-start(bf16[128,512]{1,0:T(8,128)(2,1)S(1)} %get-tuple-element.32), channel_id=1, source_target_pairs={{0,8},{1,9},{2,10},{3,11},{4,12},{5,13},{6,14},{7,15},{8,0},{9,1},... | collective-permute-start | bytes 393224 | tf_op jit(solution)/shard_map/ppermute | solution.py:276
  23.0 0.4 %collective-permute-start.9 = (bf16[128,512]{1,0:T(8,128)(2,1)S(1)}, bf16[128,512]{1,0:T(8,128)(2,1)S(1)}, u32[]{:S(2)}, u32[]{:S(2)}) collective-permute-start(bf16[128,512]{1,0:T(8,128)(2,1)S(1)} %get-tuple-element.33), channel_id=1, source_target_pairs={{0,12},{1,13},{2,14},{3,15},{4,8},{5,9},{6,10},{7,11},{8,4},{9,5},... | collective-permute-start | bytes 393224 | tf_op jit(solution)/shard_map/ppermute | solution.py:276
  23.5 1.6 %collective-permute-start.11 = (bf16[128,512]{1,0:T(8,128)(2,1)S(1)}, bf16[128,512]{1,0:T(8,128)(2,1)S(1)}, u32[]{:S(2)}, u32[]{:S(2)}) collective-permute-start(bf16[128,512]{1,0:T(8,128)(2,1)S(1)} %get-tuple-element.37), channel_id=1, source_target_pairs={{0,1},{1,0},{2,3},{3,2},{4,5},{5,4},{6,7},{7,6},{8,9},{9,8},{10,11... | collective-permute-start | bytes 393224 | tf_op jit(solution)/shard_map/ppermute | solution.py:276
  25.1 1.5 %collective-permute-start.12 = (bf16[128,512]{1,0:T(8,128)(2,1)S(1)}, bf16[128,512]{1,0:T(8,128)(2,1)S(1)}, u32[]{:S(2)}, u32[]{:S(2)}) collective-permute-start(bf16[128,512]{1,0:T(8,128)(2,1)S(1)} %get-tuple-element.38), channel_id=1, source_target_pairs={{0,2},{1,3},{2,0},{3,1},{4,6},{5,7},{6,4},{7,5},{8,10},{9,11},{10,... | collective-permute-start | bytes 393224 | tf_op jit(solution)/shard_map/ppermute | solution.py:276
  26.7 0.7 %collective-permute-done.7.refs_5_ = bf16[128,512]{1,0:T(8,128)(2,1)S(1)} collective-permute-done((bf16[128,512]{1,0:T(8,128)(2,1)S(1)}, bf16[128,512]{1,0:T(8,128)(2,1)S(1)}, u32[]{:S(2)}, u32[]{:S(2)}) %collective-permute-start.7) | collective-permute-done | bytes 131104 | tf_op jit(solution)/shard_map/ppermute | solution.py:276
  27.3 2.5 %collective-permute-start.13 = (bf16[128,512]{1,0:T(8,128)(2,1)S(1)}, bf16[128,512]{1,0:T(8,128)(2,1)S(1)}, u32[]{:S(2)}, u32[]{:S(2)}) collective-permute-start(bf16[128,512]{1,0:T(8,128)(2,1)S(1)} %get-tuple-element.39), channel_id=1, source_target_pairs={{0,3},{1,2},{2,1},{3,0},{4,7},{5,6},{6,5},{7,4},{8,11},{9,10},{10,... | collective-permute-start | bytes 393224 | tf_op jit(solution)/shard_map/ppermute | solution.py:276
  30.0 2.9 %collective-permute-done.8.refs_6_ = bf16[128,512]{1,0:T(8,128)(2,1)S(1)} collective-permute-done((bf16[128,512]{1,0:T(8,128)(2,1)S(1)}, bf16[128,512]{1,0:T(8,128)(2,1)S(1)}, u32[]{:S(2)}, u32[]{:S(2)}) %collective-permute-start.8) | collective-permute-done | bytes 131104 | tf_op jit(solution)/shard_map/ppermute | solution.py:276
  32.9 0.3 collective-permute-done.13.refs_11_
  33.2 1.1 %finish.1 = (f32[128,512]{1,0:T(8,128)}, f32[128,512]{1,0:T(8,128)}) custom-call(f32[128,512]{1,0:T(8,128)S(1)} %get-tuple-element.21.refs_0_, f32[128,128]{1,0:T(8,128)S(1)} %get-tuple-element.22.refs_1_, f32[128,512]{1,0:T(8,128)S(1)} %get-tuple-element.23.refs_2_, f32[128,128]{1,0:T(8,128)S(1)} %get-tuple-element.24.refs_3_, ...), custom_call_target="tpu_custom_call" | custom-call | flops 5242880 | bytes 1572864 | tf_op jit(solution)/shard_map/finish/pallas_call | solution.py:228
  (19 shorter events, 0.7 us)
Async XLA Ops:
  0.6 10.7 %collective-permute-start = (bf16[128,512]{1,0:T(8,128)(2,1)}, bf16[128,512]{1,0:T(8,128)(2,1)S(1)}, u32[]{:S(2)}, u32[]{:S(2)}) collective-permute-start(bf16[128,512]{1,0:T(8,128)(2,1)} %refs_0_.5), channel_id=1, source_target_pairs={{0,8},{1,9},{2,10},{3,11},{4,12},{5,13},{6,14},{7,15},{8,0},{9,1},... | collective-permute-start | bytes 393224 | tf_op jit(solution)/shard_map/ppermute | solution.py:276
  4.7 8.4 %collective-permute-start.1 = (bf16[128,512]{1,0:T(8,128)(2,1)}, bf16[128,512]{1,0:T(8,128)(2,1)S(1)}, u32[]{:S(2)}, u32[]{:S(2)}) collective-permute-start(bf16[128,512]{1,0:T(8,128)(2,1)} %refs_0_.4), channel_id=1, source_target_pairs={{0,1},{1,0},{2,3},{3,2},{4,5},{5,4},{6,7},{7,6},{8,9},{9,8},{10,11... | collective-permute-start | bytes 393224 | tf_op jit(solution)/shard_map/ppermute | solution.py:276
  6.2 8.0 %collective-permute-start.2 = (bf16[128,512]{1,0:T(8,128)(2,1)}, bf16[128,512]{1,0:T(8,128)(2,1)S(1)}, u32[]{:S(2)}, u32[]{:S(2)}) collective-permute-start(bf16[128,512]{1,0:T(8,128)(2,1)} %refs_0_.4), channel_id=1, source_target_pairs={{0,2},{1,3},{2,0},{3,1},{4,6},{5,7},{6,4},{7,5},{8,10},{9,11},{10,... | collective-permute-start | bytes 393224 | tf_op jit(solution)/shard_map/ppermute | solution.py:276
  7.7 6.5 %collective-permute-start.3 = (bf16[128,512]{1,0:T(8,128)(2,1)}, bf16[128,512]{1,0:T(8,128)(2,1)S(1)}, u32[]{:S(2)}, u32[]{:S(2)}) collective-permute-start(bf16[128,512]{1,0:T(8,128)(2,1)} %refs_0_.4), channel_id=1, source_target_pairs={{0,3},{1,2},{2,1},{3,0},{4,7},{5,6},{6,5},{7,4},{8,11},{9,10},{10,... | collective-permute-start | bytes 393224 | tf_op jit(solution)/shard_map/ppermute | solution.py:276
  8.2 6.6 %collective-permute-start.4 = (bf16[128,512]{1,0:T(8,128)(2,1)}, bf16[128,512]{1,0:T(8,128)(2,1)S(1)}, u32[]{:S(2)}, u32[]{:S(2)}) collective-permute-start(bf16[128,512]{1,0:T(8,128)(2,1)} %refs_0_.5), channel_id=1, source_target_pairs={{0,4},{1,5},{2,6},{3,7},{4,0},{5,1},{6,2},{7,3},{8,12},{9,13},{10,... | collective-permute-start | bytes 393224 | tf_op jit(solution)/shard_map/ppermute | solution.py:276
  11.4 5.5 %collective-permute-start.5 = (bf16[128,512]{1,0:T(8,128)(2,1)S(1)}, bf16[128,512]{1,0:T(8,128)(2,1)S(1)}, u32[]{:S(2)}, u32[]{:S(2)}) collective-permute-start(bf16[128,512]{1,0:T(8,128)(2,1)S(1)} %collective-permute-done.refs_1_), channel_id=1, source_target_pairs={{0,4},{1,5},{2,6},{3,7},{4,0},{5,1},{6,2},{7,3},{8,12},{9,13},{10,... | collective-permute-start | bytes 393224 | tf_op jit(solution)/shard_map/ppermute | solution.py:276
  12.1 0.9 %copy-start = (bf16[128,512]{1,0:T(8,128)(2,1)S(1)}, bf16[128,512]{1,0:T(8,128)(2,1)}, u32[]{:S(2)}) copy-start(bf16[128,512]{1,0:T(8,128)(2,1)} %refs_0_.4) | copy-start | bytes 393220
  13.1 1.7 %copy-start.2 = (bf16[128,512]{1,0:T(8,128)(2,1)S(1)}, bf16[128,512]{1,0:T(8,128)(2,1)}, u32[]{:S(2)}) copy-start(bf16[128,512]{1,0:T(8,128)(2,1)} %refs_0_.5) | copy-start | bytes 393220
  14.4 2.6 %collective-permute-start.6 = (bf16[512,512]{1,0:T(8,128)(2,1)S(1)}, bf16[512,512]{1,0:T(8,128)(2,1)S(1)}, u32[]{:S(2)}, u32[]{:S(2)}) collective-permute-start(bf16[512,512]{1,0:T(8,128)(2,1)S(1)} %stack_units.1.text_ref.own_text_ref), channel_id=1, source_target_pairs={{0,16},{1,17},{2,18},{3,19},{4,20},{5,21},{6,22},{7,23},{8,24},{9,... | collective-permute-start | bytes 1572872 | tf_op jit(solution)/shard_map/ppermute | solution.py:276
  18.9 4.5 %collective-permute-start.10 = (bf16[512,512]{1,0:T(8,128)(2,1)S(1)}, bf16[512,512]{1,0:T(8,128)(2,1)S(1)}, u32[]{:S(2)}, u32[]{:S(2)}) collective-permute-start(bf16[512,512]{1,0:T(8,128)(2,1)S(1)} %get-tuple-element.35), channel_id=1, source_target_pairs={{0,16},{1,17},{2,18},{3,19},{4,20},{5,21},{6,22},{7,23},{8,24},{9,... | collective-permute-start | bytes 1572872 | tf_op jit(solution)/shard_map/ppermute | solution.py:276
  19.0 8.4 %collective-permute-start.7 = (bf16[128,512]{1,0:T(8,128)(2,1)S(1)}, bf16[128,512]{1,0:T(8,128)(2,1)S(1)}, u32[]{:S(2)}, u32[]{:S(2)}) collective-permute-start(bf16[128,512]{1,0:T(8,128)(2,1)S(1)} %get-tuple-element.31), channel_id=1, source_target_pairs={{0,4},{1,5},{2,6},{3,7},{4,0},{5,1},{6,2},{7,3},{8,12},{9,13},{10,... | collective-permute-start | bytes 393224 | tf_op jit(solution)/shard_map/ppermute | solution.py:276
  20.0 12.9 %collective-permute-start.8 = (bf16[128,512]{1,0:T(8,128)(2,1)S(1)}, bf16[128,512]{1,0:T(8,128)(2,1)S(1)}, u32[]{:S(2)}, u32[]{:S(2)}) collective-permute-start(bf16[128,512]{1,0:T(8,128)(2,1)S(1)} %get-tuple-element.32), channel_id=1, source_target_pairs={{0,8},{1,9},{2,10},{3,11},{4,12},{5,13},{6,14},{7,15},{8,0},{9,1},... | collective-permute-start | bytes 393224 | tf_op jit(solution)/shard_map/ppermute | solution.py:276
  23.0 9.9 %collective-permute-start.9 = (bf16[128,512]{1,0:T(8,128)(2,1)S(1)}, bf16[128,512]{1,0:T(8,128)(2,1)S(1)}, u32[]{:S(2)}, u32[]{:S(2)}) collective-permute-start(bf16[128,512]{1,0:T(8,128)(2,1)S(1)} %get-tuple-element.33), channel_id=1, source_target_pairs={{0,12},{1,13},{2,14},{3,15},{4,8},{5,9},{6,10},{7,11},{8,4},{9,5},... | collective-permute-start | bytes 393224 | tf_op jit(solution)/shard_map/ppermute | solution.py:276
  23.4 6.4 %copy-start.1 = (bf16[128,512]{1,0:T(8,128)(2,1)S(1)}, bf16[128,512]{1,0:T(8,128)(2,1)}, u32[]{:S(2)}) copy-start(bf16[128,512]{1,0:T(8,128)(2,1)} %refs_0_.4) | copy-start | bytes 393220
  23.5 9.4 %collective-permute-start.11 = (bf16[128,512]{1,0:T(8,128)(2,1)S(1)}, bf16[128,512]{1,0:T(8,128)(2,1)S(1)}, u32[]{:S(2)}, u32[]{:S(2)}) collective-permute-start(bf16[128,512]{1,0:T(8,128)(2,1)S(1)} %get-tuple-element.37), channel_id=1, source_target_pairs={{0,1},{1,0},{2,3},{3,2},{4,5},{5,4},{6,7},{7,6},{8,9},{9,8},{10,11... | collective-permute-start | bytes 393224 | tf_op jit(solution)/shard_map/ppermute | solution.py:276
  25.1 7.8 %collective-permute-start.12 = (bf16[128,512]{1,0:T(8,128)(2,1)S(1)}, bf16[128,512]{1,0:T(8,128)(2,1)S(1)}, u32[]{:S(2)}, u32[]{:S(2)}) collective-permute-start(bf16[128,512]{1,0:T(8,128)(2,1)S(1)} %get-tuple-element.38), channel_id=1, source_target_pairs={{0,2},{1,3},{2,0},{3,1},{4,6},{5,7},{6,4},{7,5},{8,10},{9,11},{10,... | collective-permute-start | bytes 393224 | tf_op jit(solution)/shard_map/ppermute | solution.py:276
  27.3 5.9 %collective-permute-start.13 = (bf16[128,512]{1,0:T(8,128)(2,1)S(1)}, bf16[128,512]{1,0:T(8,128)(2,1)S(1)}, u32[]{:S(2)}, u32[]{:S(2)}) collective-permute-start(bf16[128,512]{1,0:T(8,128)(2,1)S(1)} %get-tuple-element.39), channel_id=1, source_target_pairs={{0,3},{1,2},{2,1},{3,0},{4,7},{5,6},{6,5},{7,4},{8,11},{9,10},{10,... | collective-permute-start | bytes 393224 | tf_op jit(solution)/shard_map/ppermute | solution.py:276

commit v18 on v14

--- a/solution.py
+++ b/solution.py
@@ -13,6 +13,7 @@
 SPAN = 256
 PIECE = 32
 LATE = 16500
+KEPT = 60000
 LOG2_E = math.log2(math.e)
 VMEM = pl.BlockSpec(memory_space=pltpu.VMEM)
 
@@ -167,25 +168,24 @@
     return outs[count:], outs[:count]
 
 
-def add_stacks_kernel(part_count, *refs):
+def add_stacks_kernel(first, part_count, *refs):
     parts, outs = refs[:part_count], refs[part_count:]
     rows = outs[0].shape[0]
-    for at, out in enumerate(outs):
-        total = parts[0][at * rows:(at + 1) * rows, :].astype(jnp.float32)
+    for at, out in enumerate(outs, first):
+        total = parts[0][at * rows:(at + 1) * rows, :]
         for part in parts[1:]:
             total = total + part[at * rows:(at + 1) * rows, :].astype(jnp.float32)
         out[...] = total.astype(out.dtype)
 
 
-def add_stacks(parts, count):
+def add_stacks(parts, count, first, last, dtype, name, weight=1):
     shape = (parts[0].shape[0] // count, parts[0].shape[1])
-    types = [jnp.float32] + [jnp.bfloat16] * (count - 1)
     return call(
-        functools.partial(add_stacks_kernel, len(parts)),
-        [jax.ShapeDtypeStruct(shape, t) for t in types],
+        functools.partial(add_stacks_kernel, first, len(parts)),
+        [jax.ShapeDtypeStruct(shape, dtype)] * (last - first),
         parts,
-        flops=len(parts) * parts[0].size,
-        name="add_stacks",
+        flops=weight * len(parts) * (last - first) * shape[0] * shape[1],
+        name=name,
     )
 
 
@@ -290,17 +290,23 @@
         )
         far_parts = dict(zip([*early, *late], image_parts))
         came = [move(part, grp=-g) for g, part in enumerate(text_parts) if g]
-        far_order = sorted((step for step in far_parts if step != (0, 0)), key=lambda step: step[0])
-        far_came = [move(far_parts[h, w], high=-h, low=-w) for h, w in far_order]
-        near_parts = add_stacks([text_parts[0], *came], near_count)
-        near_parts = [near_parts[0]] + [
-            move(part, near=-n) for n, part in enumerate(near_parts) if n
-        ]
+        def give_back(h, w):
+            return move(far_parts[h, w], high=-h, low=-w)
+
+        stacks = [text_parts[0], *came]
+        sent = add_stacks(stacks, near_count, 1, near_count, jnp.bfloat16, "add_sent")
+        (kept,) = add_stacks(stacks, near_count, 0, 1, jnp.float32, "add_kept", KEPT)
+        near_came = [move(part, near=-n) for n, part in enumerate(sent, 1)]
+        far_came = [give_back(h, w) for h, w in far_parts if h]
+        low_parts = [far_parts[0, w] for w in range(1, low_count)]
+        low_parts, near_came[:1], kept = lax.optimization_barrier((low_parts, near_came[:1], kept))
+        low_came = [move(part, low=-w) for w, part in enumerate(low_parts, 1)]
         return finish(
             images,
             texts,
             [(0, part) for part in [far_parts[0, 0]] + far_came]
-            + [(1, part) for part in near_parts],
+            + [(1, part) for part in [kept] + near_came]
+            + [(0, part) for part in low_came],
         )
 
     in_specs = (P(AXES, None), P(AXES, None), P(), P())

time: 34.5 us -> 35.4 us (1.026)
  waiting for transfers between devices: 6.54 us -> 9.94 us
  starting transfers between devices: 20.2 us -> 17.7 us
    ppermute x14, waiting for transfers between devices: 6.54 us -> 9.94 us  [move(): return lax.ppermute(value, AXES, perm)]
    ppermute x14, starting transfers between devices: 20.2 us -> 17.7 us  [move(): return lax.ppermute(value, AXES, perm)]
    pallas_call x6 -> x7, Pallas kernels: 3.52 us -> 3.51 us  [call(): pl.pallas_call(kernel, out_shape=out_shape, in_specs=[VMEM] * len(operand...]
  transfers between devices with their start and end apart: 14 -> 14, of which waited for: 7 -> 8; matrix products, arithmetic and copies ran while one was open for 0% -> 0% of each run, Pallas kernels for 5% -> 5%
where the time goes in v18:
time: 35.4 us; the launch traced here: 35.3 us
  starting transfers between devices  17.7 us (50%)
  waiting for transfers between devices  9.94 us (28%)
  Pallas kernels  4.58 us (13%)
  between operations  2.02 us (6%)
  local copies, waits for them, and re-layouts  0.91 us (3%)
    ppermute x14, starting transfers between devices, move(): return lax.ppermute(value, AXES, perm)  17.7 us
    ppermute x14, waiting for transfers between devices, move(): return lax.ppermute(value, AXES, perm)  9.94 us
    pallas_call x7, Pallas kernels, call(): pl.pallas_call(kernel, out_shape=out_shape, in_specs=[VMEM] * len(operand...  3.51 us
    pallas_call x1, Pallas kernels, finish(): pl.pallas_call(functools.partial(finish_kernel, [side for side, _ in part...  1.07 us
    unnamed x6, local copies, waits for them, and re-layouts  0.91 us
  transfers between devices with their start and end apart: 14, of which 8 were waited for; matrix products, arithmetic and copies ran while one was open for 0% of the time, Pallas kernels for 5%

profile of v18, /device:TPU:0, one launch (start us, length us, event | category | flops | bytes accessed | tf_op | source)
XLA Modules:
  0.0 35.3 jit_solution(612523824603751092)
XLA Ops:
  0.6 4.1 %collective-permute-start = (bf16[128,512]{1,0:T(8,128)(2,1)}, bf16[128,512]{1,0:T(8,128)(2,1)S(1)}, u32[]{:S(2)}, u32[]{:S(2)}) collective-permute-start(bf16[128,512]{1,0:T(8,128)(2,1)} %image_ref.1), channel_id=1, source_target_pairs={{0,8},{1,9},{2,10},{3,11},{4,12},{5,13},{6,14},{7,15},{8,0},{9,1},... | collective-permute-start | bytes 393224 | tf_op jit(solution)/shard_map/ppermute | solution.py:269
  4.7 1.5 %collective-permute-start.2 = (bf16[128,512]{1,0:T(8,128)(2,1)}, bf16[128,512]{1,0:T(8,128)(2,1)S(1)}, u32[]{:S(2)}, u32[]{:S(2)}) collective-permute-start(bf16[128,512]{1,0:T(8,128)(2,1)} %text_ref.1), channel_id=1, source_target_pairs={{0,2},{1,3},{2,0},{3,1},{4,6},{5,7},{6,4},{7,5},{8,10},{9,11},{10,... | collective-permute-start | bytes 393224 | tf_op jit(solution)/shard_map/ppermute | solution.py:269
  6.3 1.5 %collective-permute-start.1 = (bf16[128,512]{1,0:T(8,128)(2,1)}, bf16[128,512]{1,0:T(8,128)(2,1)S(1)}, u32[]{:S(2)}, u32[]{:S(2)}) collective-permute-start(bf16[128,512]{1,0:T(8,128)(2,1)} %text_ref.1), channel_id=1, source_target_pairs={{0,1},{1,0},{2,3},{3,2},{4,5},{5,4},{6,7},{7,6},{8,9},{9,8},{10,11... | collective-permute-start | bytes 393224 | tf_op jit(solution)/shard_map/ppermute | solution.py:269
  7.7 0.5 %collective-permute-start.3 = (bf16[128,512]{1,0:T(8,128)(2,1)}, bf16[128,512]{1,0:T(8,128)(2,1)S(1)}, u32[]{:S(2)}, u32[]{:S(2)}) collective-permute-start(bf16[128,512]{1,0:T(8,128)(2,1)} %text_ref.1), channel_id=1, source_target_pairs={{0,3},{1,2},{2,1},{3,0},{4,7},{5,6},{6,5},{7,4},{8,11},{9,10},{10,... | collective-permute-start | bytes 393224 | tf_op jit(solution)/shard_map/ppermute | solution.py:269
  8.2 1.6 %collective-permute-start.4 = (bf16[128,512]{1,0:T(8,128)(2,1)}, bf16[128,512]{1,0:T(8,128)(2,1)S(1)}, u32[]{:S(2)}, u32[]{:S(2)}) collective-permute-start(bf16[128,512]{1,0:T(8,128)(2,1)} %image_ref.1), channel_id=1, source_target_pairs={{0,4},{1,5},{2,6},{3,7},{4,0},{5,1},{6,2},{7,3},{8,12},{9,13},{10,... | collective-permute-start | bytes 393224 | tf_op jit(solution)/shard_map/ppermute | solution.py:269
  11.2 0.2 collective-permute-done.refs_1_
  11.4 0.8 %collective-permute-start.5 = (bf16[128,512]{1,0:T(8,128)(2,1)S(1)}, bf16[128,512]{1,0:T(8,128)(2,1)S(1)}, u32[]{:S(2)}, u32[]{:S(2)}) collective-permute-start(bf16[128,512]{1,0:T(8,128)(2,1)S(1)} %collective-permute-done.refs_1_), channel_id=1, source_target_pairs={{0,4},{1,5},{2,6},{3,7},{4,0},{5,1},{6,2},{7,3},{8,12},{9,13},{10,... | collective-permute-start | bytes 393224 | tf_op jit(solution)/shard_map/ppermute | solution.py:269
  12.1 0.9 %copy-done = bf16[128,512]{1,0:T(8,128)(2,1)S(1)} copy-done((bf16[128,512]{1,0:T(8,128)(2,1)S(1)}, bf16[128,512]{1,0:T(8,128)(2,1)}, u32[]{:S(2)}) %copy-start) | copy-done | bytes 131096
  13.2 1.0 %collective-permute-done.3.refs_3_ = bf16[128,512]{1,0:T(8,128)(2,1)S(1)} collective-permute-done((bf16[128,512]{1,0:T(8,128)(2,1)}, bf16[128,512]{1,0:T(8,128)(2,1)S(1)}, u32[]{:S(2)}, u32[]{:S(2)}) %collective-permute-start.3) | collective-permute-done | bytes 131104 | tf_op jit(solution)/shard_map/ppermute | solution.py:269
  14.4 0.4 %collective-permute-done.4.refs_2_ = bf16[128,512]{1,0:T(8,128)(2,1)S(1)} collective-permute-done((bf16[128,512]{1,0:T(8,128)(2,1)}, bf16[128,512]{1,0:T(8,128)(2,1)S(1)}, u32[]{:S(2)}, u32[]{:S(2)}) %collective-permute-start.4) | collective-permute-done | bytes 131104 | tf_op jit(solution)/shard_map/ppermute | solution.py:269
  14.9 1.1 %early_pairs.1 = (f32[512,512]{1,0:T(8,128)S(1)}, bf16[384,512]{1,0:T(8,128)(2,1)S(1)}, f32[384,512]{1,0:T(8,128)S(1)}) custom-call(f32[1,3]{1,0:T(1,128)S(1)} %maximum_bitcast_fusion.params_ref, bf16[512,512]{1,0:T(8,128)(2,1)S(1)} %stack_units.1.text_ref.own_text_ref, bf16[128,512]{1,0:T(8,128)(2,1)S(1)} %copy-done.2, ...), custom_call_target="tpu_custom_call" | custom-call | flops 603979776 | bytes 3145740 | tf_op jit(solution)/shard_map/early_pairs/pallas_call | solution.py:29
  16.0 0.9 %collective-permute-done.5.refs_0_ = bf16[128,512]{1,0:T(8,128)(2,1)S(1)} collective-permute-done((bf16[128,512]{1,0:T(8,128)(2,1)S(1)}, bf16[128,512]{1,0:T(8,128)(2,1)S(1)}, u32[]{:S(2)}, u32[]{:S(2)}) %collective-permute-start.5) | collective-permute-done | bytes 131104 | tf_op jit(solution)/shard_map/ppermute | solution.py:269
  17.0 1.9 %rest_pairs.1 = (f32[512,512]{1,0:T(8,128)S(1)}, bf16[512,512]{1,0:T(8,128)(2,1)S(1)}, f32[128,512]{1,0:T(8,128)S(1)}, bf16[128,512]{1,0:T(8,128)(2,1)S(1)}, bf1...) custom-call(f32[1,3]{1,0:T(1,128)S(1)} %maximum_bitcast_fusion.params_ref, ...), custom_call_target="tpu_custom_call" | custom-call | flops 1006632960 | bytes 5636108 | tf_op jit(solution)/shard_map/rest_pairs/pallas_call | solution.py:29
  19.0 2.3 %collective-permute-start.7 = (bf16[128,512]{1,0:T(8,128)(2,1)S(1)}, bf16[128,512]{1,0:T(8,128)(2,1)S(1)}, u32[]{:S(2)}, u32[]{:S(2)}) collective-permute-start(bf16[128,512]{1,0:T(8,128)(2,1)S(1)} %get-tuple-element.25), channel_id=1, source_target_pairs={{0,8},{1,9},{2,10},{3,11},{4,12},{5,13},{6,14},{7,15},{8,0},{9,1},... | collective-permute-start | bytes 393224 | tf_op jit(solution)/shard_map/ppermute | solution.py:269
  21.2 1.3 %collective-permute-start.8 = (bf16[128,512]{1,0:T(8,128)(2,1)S(1)}, bf16[128,512]{1,0:T(8,128)(2,1)S(1)}, u32[]{:S(2)}, u32[]{:S(2)}) collective-permute-start(bf16[128,512]{1,0:T(8,128)(2,1)S(1)} %get-tuple-element.26), channel_id=1, source_target_pairs={{0,12},{1,13},{2,14},{3,15},{4,8},{5,9},{6,10},{7,11},{8,4},{9,5},... | collective-permute-start | bytes 393224 | tf_op jit(solution)/shard_map/ppermute | solution.py:269
  22.6 1.6 %collective-permute-start.10 = (bf16[128,512]{1,0:T(8,128)(2,1)S(1)}, bf16[128,512]{1,0:T(8,128)(2,1)S(1)}, u32[]{:S(2)}, u32[]{:S(2)}) collective-permute-start(bf16[128,512]{1,0:T(8,128)(2,1)S(1)} %get-tuple-element.30), channel_id=1, source_target_pairs={{0,1},{1,0},{2,3},{3,2},{4,5},{5,4},{6,7},{7,6},{8,9},{9,8},{10,11... | collective-permute-start | bytes 393224 | tf_op jit(solution)/shard_map/ppermute | solution.py:269
  24.1 1.5 %collective-permute-start.11 = (bf16[128,512]{1,0:T(8,128)(2,1)S(1)}, bf16[128,512]{1,0:T(8,128)(2,1)S(1)}, u32[]{:S(2)}, u32[]{:S(2)}) collective-permute-start(bf16[128,512]{1,0:T(8,128)(2,1)S(1)} %get-tuple-element.33), channel_id=1, source_target_pairs={{0,2},{1,3},{2,0},{3,1},{4,6},{5,7},{6,4},{7,5},{8,10},{9,11},{10,... | collective-permute-start | bytes 393224 | tf_op jit(solution)/shard_map/ppermute | solution.py:269
  25.7 0.5 %collective-permute-start.12 = (bf16[128,512]{1,0:T(8,128)(2,1)S(1)}, bf16[128,512]{1,0:T(8,128)(2,1)S(1)}, u32[]{:S(2)}, u32[]{:S(2)}) collective-permute-start(bf16[128,512]{1,0:T(8,128)(2,1)S(1)} %get-tuple-element.34), channel_id=1, source_target_pairs={{0,3},{1,2},{2,1},{3,0},{4,7},{5,6},{6,5},{7,4},{8,11},{9,10},{10,... | collective-permute-start | bytes 393224 | tf_op jit(solution)/shard_map/ppermute | solution.py:269
  26.2 2.3 %collective-permute-done.10.refs_4_ = bf16[128,512]{1,0:T(8,128)(2,1)S(1)} collective-permute-done((bf16[128,512]{1,0:T(8,128)(2,1)S(1)}, bf16[128,512]{1,0:T(8,128)(2,1)S(1)}, u32[]{:S(2)}, u32[]{:S(2)}) %collective-permute-start.10) | collective-permute-done | bytes 131104 | tf_op jit(solution)/shard_map/ppermute | solution.py:269
  28.5 0.6 %collective-permute-start.13 = (bf16[128,512]{1,0:T(8,128)(2,1)S(1)}, bf16[128,512]{1,0:T(8,128)(2,1)S(1)}, u32[]{:S(2)}, u32[]{:S(2)}) collective-permute-start(bf16[128,512]{1,0:T(8,128)(2,1)S(1)} %get-tuple-element.35), channel_id=1, source_target_pairs={{0,4},{1,5},{2,6},{3,7},{4,0},{5,1},{6,2},{7,3},{8,12},{9,13},{10,... | collective-permute-start | bytes 393224 | tf_op jit(solution)/shard_map/ppermute | solution.py:269
  29.1 2.8 %collective-permute-done.7.refs_1_ = bf16[128,512]{1,0:T(8,128)(2,1)S(1)} collective-permute-done((bf16[128,512]{1,0:T(8,128)(2,1)S(1)}, bf16[128,512]{1,0:T(8,128)(2,1)S(1)}, u32[]{:S(2)}, u32[]{:S(2)}) %collective-permute-start.7) | collective-permute-done | bytes 131104 | tf_op jit(solution)/shard_map/ppermute | solution.py:269
  31.8 0.3 collective-permute-done.11.refs_5_
  32.1 2.1 %collective-permute-done.13.refs_7_ = bf16[128,512]{1,0:T(8,128)(2,1)S(1)} collective-permute-done((bf16[128,512]{1,0:T(8,128)(2,1)S(1)}, bf16[128,512]{1,0:T(8,128)(2,1)S(1)}, u32[]{:S(2)}, u32[]{:S(2)}) %collective-permute-start.13) | collective-permute-done | bytes 131104 | tf_op jit(solution)/shard_map/ppermute | solution.py:269
  34.2 1.1 %finish.1 = (f32[128,512]{1,0:T(8,128)}, f32[128,512]{1,0:T(8,128)}) custom-call(bf16[128,512]{1,0:T(8,128)(2,1)S(1)} %copy-done.2, bf16[128,512]{1,0:T(8,128)(2,1)S(1)} %copy-done.1, f32[128,512]{1,0:T(8,128)S(1)} %get-tuple-element.24.refs_0_, bf16[128,512]{1,0:T(8,128)(2,1)S(1)} %collective-permute-done.7.refs_1_, ...), custom_call_target="tpu_custom_call" | custom-call | flops 5242880 | bytes 1572864 | tf_op jit(solution)/shard_map/finish/pallas_call | solution.py:219
  (19 shorter events, 0.7 us)
Async XLA Ops:
  0.6 10.7 %collective-permute-start = (bf16[128,512]{1,0:T(8,128)(2,1)}, bf16[128,512]{1,0:T(8,128)(2,1)S(1)}, u32[]{:S(2)}, u32[]{:S(2)}) collective-permute-start(bf16[128,512]{1,0:T(8,128)(2,1)} %image_ref.1), channel_id=1, source_target_pairs={{0,8},{1,9},{2,10},{3,11},{4,12},{5,13},{6,14},{7,15},{8,0},{9,1},... | collective-permute-start | bytes 393224 | tf_op jit(solution)/shard_map/ppermute | solution.py:269
  4.7 8.4 %collective-permute-start.2 = (bf16[128,512]{1,0:T(8,128)(2,1)}, bf16[128,512]{1,0:T(8,128)(2,1)S(1)}, u32[]{:S(2)}, u32[]{:S(2)}) collective-permute-start(bf16[128,512]{1,0:T(8,128)(2,1)} %text_ref.1), channel_id=1, source_target_pairs={{0,2},{1,3},{2,0},{3,1},{4,6},{5,7},{6,4},{7,5},{8,10},{9,11},{10,... | collective-permute-start | bytes 393224 | tf_op jit(solution)/shard_map/ppermute | solution.py:269
  6.3 6.9 %collective-permute-start.1 = (bf16[128,512]{1,0:T(8,128)(2,1)}, bf16[128,512]{1,0:T(8,128)(2,1)S(1)}, u32[]{:S(2)}, u32[]{:S(2)}) collective-permute-start(bf16[128,512]{1,0:T(8,128)(2,1)} %text_ref.1), channel_id=1, source_target_pairs={{0,1},{1,0},{2,3},{3,2},{4,5},{5,4},{6,7},{7,6},{8,9},{9,8},{10,11... | collective-permute-start | bytes 393224 | tf_op jit(solution)/shard_map/ppermute | solution.py:269
  7.7 6.4 %collective-permute-start.3 = (bf16[128,512]{1,0:T(8,128)(2,1)}, bf16[128,512]{1,0:T(8,128)(2,1)S(1)}, u32[]{:S(2)}, u32[]{:S(2)}) collective-permute-start(bf16[128,512]{1,0:T(8,128)(2,1)} %text_ref.1), channel_id=1, source_target_pairs={{0,3},{1,2},{2,1},{3,0},{4,7},{5,6},{6,5},{7,4},{8,11},{9,10},{10,... | collective-permute-start | bytes 393224 | tf_op jit(solution)/shard_map/ppermute | solution.py:269
  8.2 6.6 %collective-permute-start.4 = (bf16[128,512]{1,0:T(8,128)(2,1)}, bf16[128,512]{1,0:T(8,128)(2,1)S(1)}, u32[]{:S(2)}, u32[]{:S(2)}) collective-permute-start(bf16[128,512]{1,0:T(8,128)(2,1)} %image_ref.1), channel_id=1, source_target_pairs={{0,4},{1,5},{2,6},{3,7},{4,0},{5,1},{6,2},{7,3},{8,12},{9,13},{10,... | collective-permute-start | bytes 393224 | tf_op jit(solution)/shard_map/ppermute | solution.py:269
  11.4 5.5 %collective-permute-start.5 = (bf16[128,512]{1,0:T(8,128)(2,1)S(1)}, bf16[128,512]{1,0:T(8,128)(2,1)S(1)}, u32[]{:S(2)}, u32[]{:S(2)}) collective-permute-start(bf16[128,512]{1,0:T(8,128)(2,1)S(1)} %collective-permute-done.refs_1_), channel_id=1, source_target_pairs={{0,4},{1,5},{2,6},{3,7},{4,0},{5,1},{6,2},{7,3},{8,12},{9,13},{10,... | collective-permute-start | bytes 393224 | tf_op jit(solution)/shard_map/ppermute | solution.py:269
  12.1 0.9 %copy-start = (bf16[128,512]{1,0:T(8,128)(2,1)S(1)}, bf16[128,512]{1,0:T(8,128)(2,1)}, u32[]{:S(2)}) copy-start(bf16[128,512]{1,0:T(8,128)(2,1)} %text_ref.1) | copy-start | bytes 393220
  13.1 1.7 %copy-start.2 = (bf16[128,512]{1,0:T(8,128)(2,1)S(1)}, bf16[128,512]{1,0:T(8,128)(2,1)}, u32[]{:S(2)}) copy-start(bf16[128,512]{1,0:T(8,128)(2,1)} %image_ref.1) | copy-start | bytes 393220
  14.3 2.6 %collective-permute-start.6 = (bf16[512,512]{1,0:T(8,128)(2,1)S(1)}, bf16[512,512]{1,0:T(8,128)(2,1)S(1)}, u32[]{:S(2)}, u32[]{:S(2)}) collective-permute-start(bf16[512,512]{1,0:T(8,128)(2,1)S(1)} %stack_units.1.text_ref.own_text_ref), channel_id=1, source_target_pairs={{0,16},{1,17},{2,18},{3,19},{4,20},{5,21},{6,22},{7,23},{8,24},{9,... | collective-permute-start | bytes 1572872 | tf_op jit(solution)/shard_map/ppermute | solution.py:269
  18.9 3.6 %collective-permute-start.9 = (bf16[512,512]{1,0:T(8,128)(2,1)S(1)}, bf16[512,512]{1,0:T(8,128)(2,1)S(1)}, u32[]{:S(2)}, u32[]{:S(2)}) collective-permute-start(bf16[512,512]{1,0:T(8,128)(2,1)S(1)} %get-tuple-element.29), channel_id=1, source_target_pairs={{0,16},{1,17},{2,18},{3,19},{4,20},{5,21},{6,22},{7,23},{8,24},{9,... | collective-permute-start | bytes 1572872 | tf_op jit(solution)/shard_map/ppermute | solution.py:269
  19.0 12.9 %collective-permute-start.7 = (bf16[128,512]{1,0:T(8,128)(2,1)S(1)}, bf16[128,512]{1,0:T(8,128)(2,1)S(1)}, u32[]{:S(2)}, u32[]{:S(2)}) collective-permute-start(bf16[128,512]{1,0:T(8,128)(2,1)S(1)} %get-tuple-element.25), channel_id=1, source_target_pairs={{0,8},{1,9},{2,10},{3,11},{4,12},{5,13},{6,14},{7,15},{8,0},{9,1},... | collective-permute-start | bytes 393224 | tf_op jit(solution)/shard_map/ppermute | solution.py:269
  21.2 10.6 %collective-permute-start.8 = (bf16[128,512]{1,0:T(8,128)(2,1)S(1)}, bf16[128,512]{1,0:T(8,128)(2,1)S(1)}, u32[]{:S(2)}, u32[]{:S(2)}) collective-permute-start(bf16[128,512]{1,0:T(8,128)(2,1)S(1)} %get-tuple-element.26), channel_id=1, source_target_pairs={{0,12},{1,13},{2,14},{3,15},{4,8},{5,9},{6,10},{7,11},{8,4},{9,5},... | collective-permute-start | bytes 393224 | tf_op jit(solution)/shard_map/ppermute | solution.py:269
  22.6 5.9 %collective-permute-start.10 = (bf16[128,512]{1,0:T(8,128)(2,1)S(1)}, bf16[128,512]{1,0:T(8,128)(2,1)S(1)}, u32[]{:S(2)}, u32[]{:S(2)}) collective-permute-start(bf16[128,512]{1,0:T(8,128)(2,1)S(1)} %get-tuple-element.30), channel_id=1, source_target_pairs={{0,1},{1,0},{2,3},{3,2},{4,5},{5,4},{6,7},{7,6},{8,9},{9,8},{10,11... | collective-permute-start | bytes 393224 | tf_op jit(solution)/shard_map/ppermute | solution.py:269
  24.1 8.0 %collective-permute-start.11 = (bf16[128,512]{1,0:T(8,128)(2,1)S(1)}, bf16[128,512]{1,0:T(8,128)(2,1)S(1)}, u32[]{:S(2)}, u32[]{:S(2)}) collective-permute-start(bf16[128,512]{1,0:T(8,128)(2,1)S(1)} %get-tuple-element.33), channel_id=1, source_target_pairs={{0,2},{1,3},{2,0},{3,1},{4,6},{5,7},{6,4},{7,5},{8,10},{9,11},{10,... | collective-permute-start | bytes 393224 | tf_op jit(solution)/shard_map/ppermute | solution.py:269
  25.7 8.5 %copy-start.1 = (bf16[128,512]{1,0:T(8,128)(2,1)S(1)}, bf16[128,512]{1,0:T(8,128)(2,1)}, u32[]{:S(2)}) copy-start(bf16[128,512]{1,0:T(8,128)(2,1)} %text_ref.1) | copy-start | bytes 393220
  25.7 6.5 %collective-permute-start.12 = (bf16[128,512]{1,0:T(8,128)(2,1)S(1)}, bf16[128,512]{1,0:T(8,128)(2,1)S(1)}, u32[]{:S(2)}, u32[]{:S(2)}) collective-permute-start(bf16[128,512]{1,0:T(8,128)(2,1)S(1)} %get-tuple-element.34), channel_id=1, source_target_pairs={{0,3},{1,2},{2,1},{3,0},{4,7},{5,6},{6,5},{7,4},{8,11},{9,10},{10,... | collective-permute-start | bytes 393224 | tf_op jit(solution)/shard_map/ppermute | solution.py:269
  28.5 5.7 %collective-permute-start.13 = (bf16[128,512]{1,0:T(8,128)(2,1)S(1)}, bf16[128,512]{1,0:T(8,128)(2,1)S(1)}, u32[]{:S(2)}, u32[]{:S(2)}) collective-permute-start(bf16[128,512]{1,0:T(8,128)(2,1)S(1)} %get-tuple-element.35), channel_id=1, source_target_pairs={{0,4},{1,5},{2,6},{3,7},{4,0},{5,1},{6,2},{7,3},{8,12},{9,13},{10,... | collective-permute-start | bytes 393224 | tf_op jit(solution)/shard_map/ppermute | solution.py:269

commit v19 on v18

--- a/solution.py
+++ b/solution.py
@@ -296,10 +296,12 @@
         stacks = [text_parts[0], *came]
         sent = add_stacks(stacks, near_count, 1, near_count, jnp.bfloat16, "add_sent")
         (kept,) = add_stacks(stacks, near_count, 0, 1, jnp.float32, "add_kept", KEPT)
-        near_came = [move(part, near=-n) for n, part in enumerate(sent, 1)]
+        low_parts = [far_parts[0, w] for w in range(1, low_count)]
+        low_parts, sent = lax.optimization_barrier((low_parts, list(sent)))
+        near_came = [move(part, near=-n) for n, part in enumerate(sent[:-1], 1)]
+        last, near_came[:1], kept = lax.optimization_barrier((sent[-1:], near_came[:1], kept))
+        near_came += [move(part, near=1 - near_count) for part in last]
         far_came = [give_back(h, w) for h, w in far_parts if h]
-        low_parts = [far_parts[0, w] for w in range(1, low_count)]
-        low_parts, near_came[:1], kept = lax.optimization_barrier((low_parts, near_came[:1], kept))
         low_came = [move(part, low=-w) for w, part in enumerate(low_parts, 1)]
         return finish(
             images,

time: 35.4 us -> 35.5 us (level)
  starting transfers between devices: 17.7 us -> 19.6 us
  waiting for transfers between devices: 9.94 us -> 8.07 us
    ppermute x14, waiting for transfers between devices: 9.94 us -> 8.07 us  [move(): return lax.ppermute(value, AXES, perm)]
    ppermute x14, starting transfers between devices: 17.7 us -> 19.6 us  [move(): return lax.ppermute(value, AXES, perm)]
  transfers between devices with their start and end apart: 14 -> 14, of which waited for: 8 -> 7; matrix products, arithmetic and copies ran while one was open for 0% -> 0% of each run, Pallas kernels for 5% -> 5%
where the time goes in v19:
time: 35.5 us; the launch traced here: 35.3 us
  starting transfers between devices  19.6 us (55%)
  waiting for transfers between devices  8.07 us (23%)
  Pallas kernels  4.58 us (13%)
  between operations  2.03 us (6%)
  local copies, waits for them, and re-layouts  0.92 us (3%)
    ppermute x14, starting transfers between devices, move(): return lax.ppermute(value, AXES, perm)  19.6 us
    ppermute x14, waiting for transfers between devices, move(): return lax.ppermute(value, AXES, perm)  8.07 us
    pallas_call x7, Pallas kernels, call(): pl.pallas_call(kernel, out_shape=out_shape, in_specs=[VMEM] * len(operand...  3.51 us
    pallas_call x1, Pallas kernels, finish(): pl.pallas_call(functools.partial(finish_kernel, [side for side, _ in part...  1.07 us
    unnamed x6, local copies, waits for them, and re-layouts  0.92 us
  transfers between devices with their start and end apart: 14, of which 7 were waited for; matrix products, arithmetic and copies ran while one was open for 0% of the time, Pallas kernels for 5%

profile of v19, /device:TPU:0, one launch (start us, length us, event | category | flops | bytes accessed | tf_op | source)
XLA Modules:
  0.0 35.3 jit_solution(1563488147416450549)
XLA Ops:
  0.6 4.1 %collective-permute-start = (bf16[128,512]{1,0:T(8,128)(2,1)}, bf16[128,512]{1,0:T(8,128)(2,1)S(1)}, u32[]{:S(2)}, u32[]{:S(2)}) collective-permute-start(bf16[128,512]{1,0:T(8,128)(2,1)} %image_ref.1), channel_id=1, source_target_pairs={{0,8},{1,9},{2,10},{3,11},{4,12},{5,13},{6,14},{7,15},{8,0},{9,1},... | collective-permute-start | bytes 393224 | tf_op jit(solution)/shard_map/ppermute | solution.py:269
  4.7 1.5 %collective-permute-start.2 = (bf16[128,512]{1,0:T(8,128)(2,1)}, bf16[128,512]{1,0:T(8,128)(2,1)S(1)}, u32[]{:S(2)}, u32[]{:S(2)}) collective-permute-start(bf16[128,512]{1,0:T(8,128)(2,1)} %text_ref.1), channel_id=1, source_target_pairs={{0,2},{1,3},{2,0},{3,1},{4,6},{5,7},{6,4},{7,5},{8,10},{9,11},{10,... | collective-permute-start | bytes 393224 | tf_op jit(solution)/shard_map/ppermute | solution.py:269
  6.3 1.5 %collective-permute-start.1 = (bf16[128,512]{1,0:T(8,128)(2,1)}, bf16[128,512]{1,0:T(8,128)(2,1)S(1)}, u32[]{:S(2)}, u32[]{:S(2)}) collective-permute-start(bf16[128,512]{1,0:T(8,128)(2,1)} %text_ref.1), channel_id=1, source_target_pairs={{0,1},{1,0},{2,3},{3,2},{4,5},{5,4},{6,7},{7,6},{8,9},{9,8},{10,11... | collective-permute-start | bytes 393224 | tf_op jit(solution)/shard_map/ppermute | solution.py:269
  7.7 0.5 %collective-permute-start.3 = (bf16[128,512]{1,0:T(8,128)(2,1)}, bf16[128,512]{1,0:T(8,128)(2,1)S(1)}, u32[]{:S(2)}, u32[]{:S(2)}) collective-permute-start(bf16[128,512]{1,0:T(8,128)(2,1)} %text_ref.1), channel_id=1, source_target_pairs={{0,3},{1,2},{2,1},{3,0},{4,7},{5,6},{6,5},{7,4},{8,11},{9,10},{10,... | collective-permute-start | bytes 393224 | tf_op jit(solution)/shard_map/ppermute | solution.py:269
  8.2 1.6 %collective-permute-start.4 = (bf16[128,512]{1,0:T(8,128)(2,1)}, bf16[128,512]{1,0:T(8,128)(2,1)S(1)}, u32[]{:S(2)}, u32[]{:S(2)}) collective-permute-start(bf16[128,512]{1,0:T(8,128)(2,1)} %image_ref.1), channel_id=1, source_target_pairs={{0,4},{1,5},{2,6},{3,7},{4,0},{5,1},{6,2},{7,3},{8,12},{9,13},{10,... | collective-permute-start | bytes 393224 | tf_op jit(solution)/shard_map/ppermute | solution.py:269
  11.2 0.2 collective-permute-done.refs_1_
  11.4 0.8 %collective-permute-start.5 = (bf16[128,512]{1,0:T(8,128)(2,1)S(1)}, bf16[128,512]{1,0:T(8,128)(2,1)S(1)}, u32[]{:S(2)}, u32[]{:S(2)}) collective-permute-start(bf16[128,512]{1,0:T(8,128)(2,1)S(1)} %collective-permute-done.refs_1_), channel_id=1, source_target_pairs={{0,4},{1,5},{2,6},{3,7},{4,0},{5,1},{6,2},{7,3},{8,12},{9,13},{10,... | collective-permute-start | bytes 393224 | tf_op jit(solution)/shard_map/ppermute | solution.py:269
  12.1 0.9 %copy-done = bf16[128,512]{1,0:T(8,128)(2,1)S(1)} copy-done((bf16[128,512]{1,0:T(8,128)(2,1)S(1)}, bf16[128,512]{1,0:T(8,128)(2,1)}, u32[]{:S(2)}) %copy-start) | copy-done | bytes 131096
  13.2 1.0 %collective-permute-done.3.refs_3_ = bf16[128,512]{1,0:T(8,128)(2,1)S(1)} collective-permute-done((bf16[128,512]{1,0:T(8,128)(2,1)}, bf16[128,512]{1,0:T(8,128)(2,1)S(1)}, u32[]{:S(2)}, u32[]{:S(2)}) %collective-permute-start.3) | collective-permute-done | bytes 131104 | tf_op jit(solution)/shard_map/ppermute | solution.py:269
  14.2 0.2 stack_units.1.text_ref.own_text_ref
  14.4 0.4 %collective-permute-done.4.refs_2_ = bf16[128,512]{1,0:T(8,128)(2,1)S(1)} collective-permute-done((bf16[128,512]{1,0:T(8,128)(2,1)}, bf16[128,512]{1,0:T(8,128)(2,1)S(1)}, u32[]{:S(2)}, u32[]{:S(2)}) %collective-permute-start.4) | collective-permute-done | bytes 131104 | tf_op jit(solution)/shard_map/ppermute | solution.py:269
  14.9 1.1 %early_pairs.1 = (f32[512,512]{1,0:T(8,128)S(1)}, bf16[384,512]{1,0:T(8,128)(2,1)S(1)}, f32[384,512]{1,0:T(8,128)S(1)}) custom-call(f32[1,3]{1,0:T(1,128)S(1)} %maximum_bitcast_fusion.params_ref, bf16[512,512]{1,0:T(8,128)(2,1)S(1)} %stack_units.1.text_ref.own_text_ref, bf16[128,512]{1,0:T(8,128)(2,1)S(1)} %copy-done.2, ...), custom_call_target="tpu_custom_call" | custom-call | flops 603979776 | bytes 3145740 | tf_op jit(solution)/shard_map/early_pairs/pallas_call | solution.py:29
  16.0 0.9 %collective-permute-done.5.refs_0_ = bf16[128,512]{1,0:T(8,128)(2,1)S(1)} collective-permute-done((bf16[128,512]{1,0:T(8,128)(2,1)S(1)}, bf16[128,512]{1,0:T(8,128)(2,1)S(1)}, u32[]{:S(2)}, u32[]{:S(2)}) %collective-permute-start.5) | collective-permute-done | bytes 131104 | tf_op jit(solution)/shard_map/ppermute | solution.py:269
  17.0 1.9 %rest_pairs.1 = (f32[512,512]{1,0:T(8,128)S(1)}, bf16[512,512]{1,0:T(8,128)(2,1)S(1)}, f32[128,512]{1,0:T(8,128)S(1)}, bf16[128,512]{1,0:T(8,128)(2,1)S(1)}, bf1...) custom-call(f32[1,3]{1,0:T(1,128)S(1)} %maximum_bitcast_fusion.params_ref, ...), custom_call_target="tpu_custom_call" | custom-call | flops 1006632960 | bytes 5636108 | tf_op jit(solution)/shard_map/rest_pairs/pallas_call | solution.py:29
  19.0 2.3 %collective-permute-start.7 = (bf16[128,512]{1,0:T(8,128)(2,1)S(1)}, bf16[128,512]{1,0:T(8,128)(2,1)S(1)}, u32[]{:S(2)}, u32[]{:S(2)}) collective-permute-start(bf16[128,512]{1,0:T(8,128)(2,1)S(1)} %get-tuple-element.29), channel_id=1, source_target_pairs={{0,8},{1,9},{2,10},{3,11},{4,12},{5,13},{6,14},{7,15},{8,0},{9,1},... | collective-permute-start | bytes 393224 | tf_op jit(solution)/shard_map/ppermute | solution.py:269
  21.2 1.3 %collective-permute-start.8 = (bf16[128,512]{1,0:T(8,128)(2,1)S(1)}, bf16[128,512]{1,0:T(8,128)(2,1)S(1)}, u32[]{:S(2)}, u32[]{:S(2)}) collective-permute-start(bf16[128,512]{1,0:T(8,128)(2,1)S(1)} %get-tuple-element.30), channel_id=1, source_target_pairs={{0,12},{1,13},{2,14},{3,15},{4,8},{5,9},{6,10},{7,11},{8,4},{9,5},... | collective-permute-start | bytes 393224 | tf_op jit(solution)/shard_map/ppermute | solution.py:269
  22.6 1.6 %collective-permute-start.10 = (bf16[128,512]{1,0:T(8,128)(2,1)S(1)}, bf16[128,512]{1,0:T(8,128)(2,1)S(1)}, u32[]{:S(2)}, u32[]{:S(2)}) collective-permute-start(bf16[128,512]{1,0:T(8,128)(2,1)S(1)} %get-tuple-element.38), channel_id=1, source_target_pairs={{0,1},{1,0},{2,3},{3,2},{4,5},{5,4},{6,7},{7,6},{8,9},{9,8},{10,11... | collective-permute-start | bytes 393224 | tf_op jit(solution)/shard_map/ppermute | solution.py:269
  24.1 1.5 %collective-permute-start.11 = (bf16[128,512]{1,0:T(8,128)(2,1)S(1)}, bf16[128,512]{1,0:T(8,128)(2,1)S(1)}, u32[]{:S(2)}, u32[]{:S(2)}) collective-permute-start(bf16[128,512]{1,0:T(8,128)(2,1)S(1)} %get-tuple-element.41), channel_id=1, source_target_pairs={{0,2},{1,3},{2,0},{3,1},{4,6},{5,7},{6,4},{7,5},{8,10},{9,11},{10,... | collective-permute-start | bytes 393224 | tf_op jit(solution)/shard_map/ppermute | solution.py:269
  25.7 0.5 %collective-permute-start.13 = (bf16[128,512]{1,0:T(8,128)(2,1)S(1)}, bf16[128,512]{1,0:T(8,128)(2,1)S(1)}, u32[]{:S(2)}, u32[]{:S(2)}) collective-permute-start(bf16[128,512]{1,0:T(8,128)(2,1)S(1)} %get-tuple-element.43), channel_id=1, source_target_pairs={{0,4},{1,5},{2,6},{3,7},{4,0},{5,1},{6,2},{7,3},{8,12},{9,13},{10,... | collective-permute-start | bytes 393224 | tf_op jit(solution)/shard_map/ppermute | solution.py:269
  26.2 2.0 %collective-permute-done.10.refs_4_ = bf16[128,512]{1,0:T(8,128)(2,1)S(1)} collective-permute-done((bf16[128,512]{1,0:T(8,128)(2,1)S(1)}, bf16[128,512]{1,0:T(8,128)(2,1)S(1)}, u32[]{:S(2)}, u32[]{:S(2)}) %collective-permute-start.10) | collective-permute-done | bytes 131104 | tf_op jit(solution)/shard_map/ppermute | solution.py:269
  28.1 2.4 %collective-permute-start.12 = (bf16[128,512]{1,0:T(8,128)(2,1)S(1)}, bf16[128,512]{1,0:T(8,128)(2,1)S(1)}, u32[]{:S(2)}, u32[]{:S(2)}) collective-permute-start(bf16[128,512]{1,0:T(8,128)(2,1)S(1)} %get-tuple-element.42), channel_id=1, source_target_pairs={{0,3},{1,2},{2,1},{3,0},{4,7},{5,6},{6,5},{7,4},{8,11},{9,10},{10,... | collective-permute-start | bytes 393224 | tf_op jit(solution)/shard_map/ppermute | solution.py:269
  30.6 1.3 %collective-permute-done.7.refs_1_ = bf16[128,512]{1,0:T(8,128)(2,1)S(1)} collective-permute-done((bf16[128,512]{1,0:T(8,128)(2,1)S(1)}, bf16[128,512]{1,0:T(8,128)(2,1)S(1)}, u32[]{:S(2)}, u32[]{:S(2)}) %collective-permute-start.7) | collective-permute-done | bytes 131104 | tf_op jit(solution)/shard_map/ppermute | solution.py:269
  31.9 2.3 %collective-permute-done.13.refs_7_ = bf16[128,512]{1,0:T(8,128)(2,1)S(1)} collective-permute-done((bf16[128,512]{1,0:T(8,128)(2,1)S(1)}, bf16[128,512]{1,0:T(8,128)(2,1)S(1)}, u32[]{:S(2)}, u32[]{:S(2)}) %collective-permute-start.13) | collective-permute-done | bytes 131104 | tf_op jit(solution)/shard_map/ppermute | solution.py:269
  34.2 1.1 %finish.1 = (f32[128,512]{1,0:T(8,128)}, f32[128,512]{1,0:T(8,128)}) custom-call(bf16[128,512]{1,0:T(8,128)(2,1)S(1)} %copy-done.2, bf16[128,512]{1,0:T(8,128)(2,1)S(1)} %copy-done.1, f32[128,512]{1,0:T(8,128)S(1)} %get-tuple-element.28.refs_0_, bf16[128,512]{1,0:T(8,128)(2,1)S(1)} %collective-permute-done.7.refs_1_, ...), custom_call_target="tpu_custom_call" | custom-call | flops 5242880 | bytes 1572864 | tf_op jit(solution)/shard_map/finish/pallas_call | solution.py:219
  (19 shorter events, 0.6 us)
Async XLA Ops:
  0.6 10.7 %collective-permute-start = (bf16[128,512]{1,0:T(8,128)(2,1)}, bf16[128,512]{1,0:T(8,128)(2,1)S(1)}, u32[]{:S(2)}, u32[]{:S(2)}) collective-permute-start(bf16[128,512]{1,0:T(8,128)(2,1)} %image_ref.1), channel_id=1, source_target_pairs={{0,8},{1,9},{2,10},{3,11},{4,12},{5,13},{6,14},{7,15},{8,0},{9,1},... | collective-permute-start | bytes 393224 | tf_op jit(solution)/shard_map/ppermute | solution.py:269
  4.7 8.4 %collective-permute-start.2 = (bf16[128,512]{1,0:T(8,128)(2,1)}, bf16[128,512]{1,0:T(8,128)(2,1)S(1)}, u32[]{:S(2)}, u32[]{:S(2)}) collective-permute-start(bf16[128,512]{1,0:T(8,128)(2,1)} %text_ref.1), channel_id=1, source_target_pairs={{0,2},{1,3},{2,0},{3,1},{4,6},{5,7},{6,4},{7,5},{8,10},{9,11},{10,... | collective-permute-start | bytes 393224 | tf_op jit(solution)/shard_map/ppermute | solution.py:269
  6.3 6.9 %collective-permute-start.1 = (bf16[128,512]{1,0:T(8,128)(2,1)}, bf16[128,512]{1,0:T(8,128)(2,1)S(1)}, u32[]{:S(2)}, u32[]{:S(2)}) collective-permute-start(bf16[128,512]{1,0:T(8,128)(2,1)} %text_ref.1), channel_id=1, source_target_pairs={{0,1},{1,0},{2,3},{3,2},{4,5},{5,4},{6,7},{7,6},{8,9},{9,8},{10,11... | collective-permute-start | bytes 393224 | tf_op jit(solution)/shard_map/ppermute | solution.py:269
  7.7 6.4 %collective-permute-start.3 = (bf16[128,512]{1,0:T(8,128)(2,1)}, bf16[128,512]{1,0:T(8,128)(2,1)S(1)}, u32[]{:S(2)}, u32[]{:S(2)}) collective-permute-start(bf16[128,512]{1,0:T(8,128)(2,1)} %text_ref.1), channel_id=1, source_target_pairs={{0,3},{1,2},{2,1},{3,0},{4,7},{5,6},{6,5},{7,4},{8,11},{9,10},{10,... | collective-permute-start | bytes 393224 | tf_op jit(solution)/shard_map/ppermute | solution.py:269
  8.2 6.6 %collective-permute-start.4 = (bf16[128,512]{1,0:T(8,128)(2,1)}, bf16[128,512]{1,0:T(8,128)(2,1)S(1)}, u32[]{:S(2)}, u32[]{:S(2)}) collective-permute-start(bf16[128,512]{1,0:T(8,128)(2,1)} %image_ref.1), channel_id=1, source_target_pairs={{0,4},{1,5},{2,6},{3,7},{4,0},{5,1},{6,2},{7,3},{8,12},{9,13},{10,... | collective-permute-start | bytes 393224 | tf_op jit(solution)/shard_map/ppermute | solution.py:269
  11.4 5.5 %collective-permute-start.5 = (bf16[128,512]{1,0:T(8,128)(2,1)S(1)}, bf16[128,512]{1,0:T(8,128)(2,1)S(1)}, u32[]{:S(2)}, u32[]{:S(2)}) collective-permute-start(bf16[128,512]{1,0:T(8,128)(2,1)S(1)} %collective-permute-done.refs_1_), channel_id=1, source_target_pairs={{0,4},{1,5},{2,6},{3,7},{4,0},{5,1},{6,2},{7,3},{8,12},{9,13},{10,... | collective-permute-start | bytes 393224 | tf_op jit(solution)/shard_map/ppermute | solution.py:269
  12.1 0.9 %copy-start = (bf16[128,512]{1,0:T(8,128)(2,1)S(1)}, bf16[128,512]{1,0:T(8,128)(2,1)}, u32[]{:S(2)}) copy-start(bf16[128,512]{1,0:T(8,128)(2,1)} %text_ref.1) | copy-start | bytes 393220
  13.1 1.7 %copy-start.2 = (bf16[128,512]{1,0:T(8,128)(2,1)S(1)}, bf16[128,512]{1,0:T(8,128)(2,1)}, u32[]{:S(2)}) copy-start(bf16[128,512]{1,0:T(8,128)(2,1)} %image_ref.1) | copy-start | bytes 393220
  14.3 2.6 %collective-permute-start.6 = (bf16[512,512]{1,0:T(8,128)(2,1)S(1)}, bf16[512,512]{1,0:T(8,128)(2,1)S(1)}, u32[]{:S(2)}, u32[]{:S(2)}) collective-permute-start(bf16[512,512]{1,0:T(8,128)(2,1)S(1)} %stack_units.1.text_ref.own_text_ref), channel_id=1, source_target_pairs={{0,16},{1,17},{2,18},{3,19},{4,20},{5,21},{6,22},{7,23},{8,24},{9,... | collective-permute-start | bytes 1572872 | tf_op jit(solution)/shard_map/ppermute | solution.py:269
  18.9 3.6 %collective-permute-start.9 = (bf16[512,512]{1,0:T(8,128)(2,1)S(1)}, bf16[512,512]{1,0:T(8,128)(2,1)S(1)}, u32[]{:S(2)}, u32[]{:S(2)}) collective-permute-start(bf16[512,512]{1,0:T(8,128)(2,1)S(1)} %get-tuple-element.33), channel_id=1, source_target_pairs={{0,16},{1,17},{2,18},{3,19},{4,20},{5,21},{6,22},{7,23},{8,24},{9,... | collective-permute-start | bytes 1572872 | tf_op jit(solution)/shard_map/ppermute | solution.py:269
  19.0 12.9 %collective-permute-start.7 = (bf16[128,512]{1,0:T(8,128)(2,1)S(1)}, bf16[128,512]{1,0:T(8,128)(2,1)S(1)}, u32[]{:S(2)}, u32[]{:S(2)}) collective-permute-start(bf16[128,512]{1,0:T(8,128)(2,1)S(1)} %get-tuple-element.29), channel_id=1, source_target_pairs={{0,8},{1,9},{2,10},{3,11},{4,12},{5,13},{6,14},{7,15},{8,0},{9,1},... | collective-permute-start | bytes 393224 | tf_op jit(solution)/shard_map/ppermute | solution.py:269
  21.2 10.7 %collective-permute-start.8 = (bf16[128,512]{1,0:T(8,128)(2,1)S(1)}, bf16[128,512]{1,0:T(8,128)(2,1)S(1)}, u32[]{:S(2)}, u32[]{:S(2)}) collective-permute-start(bf16[128,512]{1,0:T(8,128)(2,1)S(1)} %get-tuple-element.30), channel_id=1, source_target_pairs={{0,12},{1,13},{2,14},{3,15},{4,8},{5,9},{6,10},{7,11},{8,4},{9,5},... | collective-permute-start | bytes 393224 | tf_op jit(solution)/shard_map/ppermute | solution.py:269
  22.6 11.6 %copy-start.1 = (bf16[128,512]{1,0:T(8,128)(2,1)S(1)}, bf16[128,512]{1,0:T(8,128)(2,1)}, u32[]{:S(2)}) copy-start(bf16[128,512]{1,0:T(8,128)(2,1)} %text_ref.1) | copy-start | bytes 393220
  22.6 5.5 %collective-permute-start.10 = (bf16[128,512]{1,0:T(8,128)(2,1)S(1)}, bf16[128,512]{1,0:T(8,128)(2,1)S(1)}, u32[]{:S(2)}, u32[]{:S(2)}) collective-permute-start(bf16[128,512]{1,0:T(8,128)(2,1)S(1)} %get-tuple-element.38), channel_id=1, source_target_pairs={{0,1},{1,0},{2,3},{3,2},{4,5},{5,4},{6,7},{7,6},{8,9},{9,8},{10,11... | collective-permute-start | bytes 393224 | tf_op jit(solution)/shard_map/ppermute | solution.py:269
  24.1 7.7 %collective-permute-start.11 = (bf16[128,512]{1,0:T(8,128)(2,1)S(1)}, bf16[128,512]{1,0:T(8,128)(2,1)S(1)}, u32[]{:S(2)}, u32[]{:S(2)}) collective-permute-start(bf16[128,512]{1,0:T(8,128)(2,1)S(1)} %get-tuple-element.41), channel_id=1, source_target_pairs={{0,2},{1,3},{2,0},{3,1},{4,6},{5,7},{6,4},{7,5},{8,10},{9,11},{10,... | collective-permute-start | bytes 393224 | tf_op jit(solution)/shard_map/ppermute | solution.py:269
  25.7 8.5 %collective-permute-start.13 = (bf16[128,512]{1,0:T(8,128)(2,1)S(1)}, bf16[128,512]{1,0:T(8,128)(2,1)S(1)}, u32[]{:S(2)}, u32[]{:S(2)}) collective-permute-start(bf16[128,512]{1,0:T(8,128)(2,1)S(1)} %get-tuple-element.43), channel_id=1, source_target_pairs={{0,4},{1,5},{2,6},{3,7},{4,0},{5,1},{6,2},{7,3},{8,12},{9,13},{10,... | collective-permute-start | bytes 393224 | tf_op jit(solution)/shard_map/ppermute | solution.py:269
  28.1 6.1 %collective-permute-start.12 = (bf16[128,512]{1,0:T(8,128)(2,1)S(1)}, bf16[128,512]{1,0:T(8,128)(2,1)S(1)}, u32[]{:S(2)}, u32[]{:S(2)}) collective-permute-start(bf16[128,512]{1,0:T(8,128)(2,1)S(1)} %get-tuple-element.42), channel_id=1, source_target_pairs={{0,3},{1,2},{2,1},{3,0},{4,7},{5,6},{6,5},{7,4},{8,11},{9,10},{10,... | collective-permute-start | bytes 393224 | tf_op jit(solution)/shard_map/ppermute | solution.py:269

commit v20 on v14

--- a/solution.py
+++ b/solution.py
@@ -66,23 +66,25 @@
     return call(stack_units_kernel, [out], blocks, flops=4 * out.size, name="stack_units")[0]
 
 
-def pairs(vi, params_ref, text_ref, text_out, own=0, text_add=None):
+def pairs(params_ref, jobs):
     slope, shift, temper = (params_ref[0:1, at:at + 1] for at in range(3))
-    held = text_ref.shape[0]
-    total = None
-
-    def dots_of(first):
+    chunks = [
+        (at, first, min(first + SPAN, job[1].shape[0]))
+        for at, job in enumerate(jobs) for first in range(0, job[1].shape[0], SPAN)
+    ]
+
+    def dots_of(at, first, last):
+        vi, text_ref = jobs[at][:2]
         return lax.dot_general(
-            vi,
-            text_ref[first:min(first + SPAN, held), :],
-            (((1,), (1,)), ((), ())),
+            vi, text_ref[first:last, :], (((1,), (1,)), ((), ())),
             preferred_element_type=jnp.float32,
         )
 
-    coming = dots_of(0)
-    for first in range(0, held, SPAN):
-        last = min(first + SPAN, held)
-        dots, coming = coming, dots_of(last) if last < held else None
+    totals = [None] * len(jobs)
+    coming = dots_of(*chunks[0])
+    for step, (at, first, last) in enumerate(chunks):
+        vi, text_ref, text_out, own, text_add = jobs[at]
+        dots, coming = coming, dots_of(*chunks[step + 1]) if step + 1 < len(chunks) else None
         vt = text_ref[first:last, :]
         e = jnp.exp2(slope * dots + shift)
         chance = pl.reciprocal(1.0 + e, approx=True)
@@ -99,8 +101,8 @@
             text_part = text_add[first:last, :] + text_part
         text_out[first:last, :] = text_part.astype(text_out.dtype)
         part = jnp.dot(coefficient, vt, preferred_element_type=jnp.float32)
-        total = part if total is None else total + part
-    return total
+        totals[at] = part if totals[at] is None else totals[at] + part
+    return totals
 
 
 def early_pairs_kernel(params_ref, text_ref, *refs):
@@ -108,7 +110,8 @@
     rows = image_refs[0].shape[0]
     for a, ref in enumerate(image_refs):
         units_out[a * rows:(a + 1) * rows, :] = unit_rows(ref[...])[0].astype(jnp.bfloat16)
-    total_out[...] = pairs(units_out[...], params_ref, text_ref, text_out, own=rows)
+    (total,) = pairs(params_ref, [(units_out[...], text_ref, text_out, rows, None)])
+    total_out[...] = total
 
 
 def rest_pairs_kernel(
@@ -118,16 +121,13 @@
     other_out, image_out = refs[count + 1:2 * count + 1], refs[2 * count + 1:]
     rows = image_out[0].shape[0]
     early, late = early_ref[...], late_ref[...]
-    total = jnp.concatenate(
-        [
-            total_ref[...],
-            pairs(late, params_ref, own_text_ref, own_out, text_add=own_add_ref),
-        ],
-        axis=0,
-    )
     vi = jnp.concatenate([early, late], axis=0)
-    for text_ref, out in zip(text_refs, other_out):
-        total = total + pairs(vi, params_ref, text_ref, out)
+    late_total, *totals = pairs(
+        params_ref,
+        [(late, own_text_ref, own_out, 0, own_add_ref)]
+        + [(vi, text_ref, out, 0, None) for text_ref, out in zip(text_refs, other_out)],
+    )
+    total = sum(totals, jnp.concatenate([total_ref[...], late_total], axis=0))
     for a, ref in enumerate(image_out):
         ref[...] = total[a * rows:(a + 1) * rows, :].astype(ref.dtype)
 

time: 34.5 us -> 34.3 us (level)
  no operation moved by 1% of the time
where the time goes in v20:
time: 34.3 us; the launch traced here: 34.1 us
  starting transfers between devices  20.1 us (59%)
  waiting for transfers between devices  6.55 us (19%)
  Pallas kernels  4.37 us (13%)
  between operations  2.02 us (6%)
  local copies, waits for them, and re-layouts  0.91 us (3%)
    ppermute x14, starting transfers between devices, move(): return lax.ppermute(value, AXES, perm)  20.1 us
    ppermute x14, waiting for transfers between devices, move(): return lax.ppermute(value, AXES, perm)  6.55 us
    pallas_call x6, Pallas kernels, call(): pl.pallas_call(kernel, out_shape=out_shape, in_specs=[VMEM] * len(operand...  3.31 us
    pallas_call x1, Pallas kernels, finish(): pl.pallas_call(functools.partial(finish_kernel, [side for side, _ in part...  1.07 us
    unnamed x6, local copies, waits for them, and re-layouts  0.91 us
  transfers between devices with their start and end apart: 14, of which 7 were waited for; matrix products, arithmetic and copies ran while one was open for 0% of the time, Pallas kernels for 5%

profile of v20, /device:TPU:0, one launch (start us, length us, event | category | flops | bytes accessed | tf_op | source)
XLA Modules:
  0.0 34.1 jit_solution(16670637217830070609)
XLA Ops:
  0.6 4.1 %collective-permute-start = (bf16[128,512]{1,0:T(8,128)(2,1)}, bf16[128,512]{1,0:T(8,128)(2,1)S(1)}, u32[]{:S(2)}, u32[]{:S(2)}) collective-permute-start(bf16[128,512]{1,0:T(8,128)(2,1)} %image_ref.1), channel_id=1, source_target_pairs={{0,8},{1,9},{2,10},{3,11},{4,12},{5,13},{6,14},{7,15},{8,0},{9,1},... | collective-permute-start | bytes 393224 | tf_op jit(solution)/shard_map/ppermute | solution.py:269
  4.7 1.5 %collective-permute-start.2 = (bf16[128,512]{1,0:T(8,128)(2,1)}, bf16[128,512]{1,0:T(8,128)(2,1)S(1)}, u32[]{:S(2)}, u32[]{:S(2)}) collective-permute-start(bf16[128,512]{1,0:T(8,128)(2,1)} %text_ref.1), channel_id=1, source_target_pairs={{0,2},{1,3},{2,0},{3,1},{4,6},{5,7},{6,4},{7,5},{8,10},{9,11},{10,... | collective-permute-start | bytes 393224 | tf_op jit(solution)/shard_map/ppermute | solution.py:269
  6.3 1.5 %collective-permute-start.1 = (bf16[128,512]{1,0:T(8,128)(2,1)}, bf16[128,512]{1,0:T(8,128)(2,1)S(1)}, u32[]{:S(2)}, u32[]{:S(2)}) collective-permute-start(bf16[128,512]{1,0:T(8,128)(2,1)} %text_ref.1), channel_id=1, source_target_pairs={{0,1},{1,0},{2,3},{3,2},{4,5},{5,4},{6,7},{7,6},{8,9},{9,8},{10,11... | collective-permute-start | bytes 393224 | tf_op jit(solution)/shard_map/ppermute | solution.py:269
  7.7 0.5 %collective-permute-start.3 = (bf16[128,512]{1,0:T(8,128)(2,1)}, bf16[128,512]{1,0:T(8,128)(2,1)S(1)}, u32[]{:S(2)}, u32[]{:S(2)}) collective-permute-start(bf16[128,512]{1,0:T(8,128)(2,1)} %text_ref.1), channel_id=1, source_target_pairs={{0,3},{1,2},{2,1},{3,0},{4,7},{5,6},{6,5},{7,4},{8,11},{9,10},{10,... | collective-permute-start | bytes 393224 | tf_op jit(solution)/shard_map/ppermute | solution.py:269
  8.2 1.6 %collective-permute-start.4 = (bf16[128,512]{1,0:T(8,128)(2,1)}, bf16[128,512]{1,0:T(8,128)(2,1)S(1)}, u32[]{:S(2)}, u32[]{:S(2)}) collective-permute-start(bf16[128,512]{1,0:T(8,128)(2,1)} %image_ref.1), channel_id=1, source_target_pairs={{0,4},{1,5},{2,6},{3,7},{4,0},{5,1},{6,2},{7,3},{8,12},{9,13},{10,... | collective-permute-start | bytes 393224 | tf_op jit(solution)/shard_map/ppermute | solution.py:269
  11.2 0.2 collective-permute-done.refs_1_
  11.4 0.8 %collective-permute-start.5 = (bf16[128,512]{1,0:T(8,128)(2,1)S(1)}, bf16[128,512]{1,0:T(8,128)(2,1)S(1)}, u32[]{:S(2)}, u32[]{:S(2)}) collective-permute-start(bf16[128,512]{1,0:T(8,128)(2,1)S(1)} %collective-permute-done.refs_1_), channel_id=1, source_target_pairs={{0,4},{1,5},{2,6},{3,7},{4,0},{5,1},{6,2},{7,3},{8,12},{9,13},{10,... | collective-permute-start | bytes 393224 | tf_op jit(solution)/shard_map/ppermute | solution.py:269
  12.1 0.9 %copy-done = bf16[128,512]{1,0:T(8,128)(2,1)S(1)} copy-done((bf16[128,512]{1,0:T(8,128)(2,1)S(1)}, bf16[128,512]{1,0:T(8,128)(2,1)}, u32[]{:S(2)}) %copy-start) | copy-done | bytes 131096
  13.2 1.0 %collective-permute-done.3.refs_3_ = bf16[128,512]{1,0:T(8,128)(2,1)S(1)} collective-permute-done((bf16[128,512]{1,0:T(8,128)(2,1)}, bf16[128,512]{1,0:T(8,128)(2,1)S(1)}, u32[]{:S(2)}, u32[]{:S(2)}) %collective-permute-start.3) | collective-permute-done | bytes 131104 | tf_op jit(solution)/shard_map/ppermute | solution.py:269
  14.2 0.2 stack_units.1.text_ref.own_text_ref
  14.4 0.4 %collective-permute-done.4.refs_2_ = bf16[128,512]{1,0:T(8,128)(2,1)S(1)} collective-permute-done((bf16[128,512]{1,0:T(8,128)(2,1)}, bf16[128,512]{1,0:T(8,128)(2,1)S(1)}, u32[]{:S(2)}, u32[]{:S(2)}) %collective-permute-start.4) | collective-permute-done | bytes 131104 | tf_op jit(solution)/shard_map/ppermute | solution.py:269
  14.9 1.1 %early_pairs.1 = (f32[512,512]{1,0:T(8,128)S(1)}, bf16[384,512]{1,0:T(8,128)(2,1)S(1)}, f32[384,512]{1,0:T(8,128)S(1)}) custom-call(f32[1,3]{1,0:T(1,128)S(1)} %maximum_bitcast_fusion.params_ref, bf16[512,512]{1,0:T(8,128)(2,1)S(1)} %stack_units.1.text_ref.own_text_ref, bf16[128,512]{1,0:T(8,128)(2,1)S(1)} %copy-done.2, ...), custom_call_target="tpu_custom_call" | custom-call | flops 603979776 | bytes 3145740 | tf_op jit(solution)/shard_map/early_pairs/pallas_call | solution.py:28
  16.0 0.9 %collective-permute-done.5.refs_0_ = bf16[128,512]{1,0:T(8,128)(2,1)S(1)} collective-permute-done((bf16[128,512]{1,0:T(8,128)(2,1)S(1)}, bf16[128,512]{1,0:T(8,128)(2,1)S(1)}, u32[]{:S(2)}, u32[]{:S(2)}) %collective-permute-start.5) | collective-permute-done | bytes 131104 | tf_op jit(solution)/shard_map/ppermute | solution.py:269
  17.0 1.7 %rest_pairs.1 = (f32[512,512]{1,0:T(8,128)S(1)}, bf16[512,512]{1,0:T(8,128)(2,1)S(1)}, f32[128,512]{1,0:T(8,128)S(1)}, bf16[128,512]{1,0:T(8,128)(2,1)S(1)}, bf1...) custom-call(f32[1,3]{1,0:T(1,128)S(1)} %maximum_bitcast_fusion.params_ref, ...), custom_call_target="tpu_custom_call" | custom-call | flops 1006632960 | bytes 5636108 | tf_op jit(solution)/shard_map/rest_pairs/pallas_call | solution.py:28
  18.8 1.0 %collective-permute-start.7 = (bf16[128,512]{1,0:T(8,128)(2,1)S(1)}, bf16[128,512]{1,0:T(8,128)(2,1)S(1)}, u32[]{:S(2)}, u32[]{:S(2)}) collective-permute-start(bf16[128,512]{1,0:T(8,128)(2,1)S(1)} %get-tuple-element.23), channel_id=1, source_target_pairs={{0,4},{1,5},{2,6},{3,7},{4,0},{5,1},{6,2},{7,3},{8,12},{9,13},{10,... | collective-permute-start | bytes 393224 | tf_op jit(solution)/shard_map/ppermute | solution.py:269
  19.8 3.0 %collective-permute-start.8 = (bf16[128,512]{1,0:T(8,128)(2,1)S(1)}, bf16[128,512]{1,0:T(8,128)(2,1)S(1)}, u32[]{:S(2)}, u32[]{:S(2)}) collective-permute-start(bf16[128,512]{1,0:T(8,128)(2,1)S(1)} %get-tuple-element.24), channel_id=1, source_target_pairs={{0,8},{1,9},{2,10},{3,11},{4,12},{5,13},{6,14},{7,15},{8,0},{9,1},... | collective-permute-start | bytes 393224 | tf_op jit(solution)/shard_map/ppermute | solution.py:269
  22.8 0.4 %collective-permute-start.9 = (bf16[128,512]{1,0:T(8,128)(2,1)S(1)}, bf16[128,512]{1,0:T(8,128)(2,1)S(1)}, u32[]{:S(2)}, u32[]{:S(2)}) collective-permute-start(bf16[128,512]{1,0:T(8,128)(2,1)S(1)} %get-tuple-element.25), channel_id=1, source_target_pairs={{0,12},{1,13},{2,14},{3,15},{4,8},{5,9},{6,10},{7,11},{8,4},{9,5},... | collective-permute-start | bytes 393224 | tf_op jit(solution)/shard_map/ppermute | solution.py:269
  23.3 1.6 %collective-permute-start.11 = (bf16[128,512]{1,0:T(8,128)(2,1)S(1)}, bf16[128,512]{1,0:T(8,128)(2,1)S(1)}, u32[]{:S(2)}, u32[]{:S(2)}) collective-permute-start(bf16[128,512]{1,0:T(8,128)(2,1)S(1)} %get-tuple-element.29), channel_id=1, source_target_pairs={{0,1},{1,0},{2,3},{3,2},{4,5},{5,4},{6,7},{7,6},{8,9},{9,8},{10,11... | collective-permute-start | bytes 393224 | tf_op jit(solution)/shard_map/ppermute | solution.py:269
  24.9 1.5 %collective-permute-start.12 = (bf16[128,512]{1,0:T(8,128)(2,1)S(1)}, bf16[128,512]{1,0:T(8,128)(2,1)S(1)}, u32[]{:S(2)}, u32[]{:S(2)}) collective-permute-start(bf16[128,512]{1,0:T(8,128)(2,1)S(1)} %get-tuple-element.30), channel_id=1, source_target_pairs={{0,2},{1,3},{2,0},{3,1},{4,6},{5,7},{6,4},{7,5},{8,10},{9,11},{10,... | collective-permute-start | bytes 393224 | tf_op jit(solution)/shard_map/ppermute | solution.py:269
  26.5 0.7 %collective-permute-done.7.refs_1_ = bf16[128,512]{1,0:T(8,128)(2,1)S(1)} collective-permute-done((bf16[128,512]{1,0:T(8,128)(2,1)S(1)}, bf16[128,512]{1,0:T(8,128)(2,1)S(1)}, u32[]{:S(2)}, u32[]{:S(2)}) %collective-permute-start.7) | collective-permute-done | bytes 131104 | tf_op jit(solution)/shard_map/ppermute | solution.py:269
  27.1 2.5 %collective-permute-start.13 = (bf16[128,512]{1,0:T(8,128)(2,1)S(1)}, bf16[128,512]{1,0:T(8,128)(2,1)S(1)}, u32[]{:S(2)}, u32[]{:S(2)}) collective-permute-start(bf16[128,512]{1,0:T(8,128)(2,1)S(1)} %get-tuple-element.31), channel_id=1, source_target_pairs={{0,3},{1,2},{2,1},{3,0},{4,7},{5,6},{6,5},{7,4},{8,11},{9,10},{10,... | collective-permute-start | bytes 393224 | tf_op jit(solution)/shard_map/ppermute | solution.py:269
  29.6 3.1 %collective-permute-done.8.refs_2_ = bf16[128,512]{1,0:T(8,128)(2,1)S(1)} collective-permute-done((bf16[128,512]{1,0:T(8,128)(2,1)S(1)}, bf16[128,512]{1,0:T(8,128)(2,1)S(1)}, u32[]{:S(2)}, u32[]{:S(2)}) %collective-permute-start.8) | collective-permute-done | bytes 131104 | tf_op jit(solution)/shard_map/ppermute | solution.py:269
  32.7 0.3 collective-permute-done.13.refs_7_
  33.0 1.1 %finish.1 = (f32[128,512]{1,0:T(8,128)}, f32[128,512]{1,0:T(8,128)}) custom-call(bf16[128,512]{1,0:T(8,128)(2,1)S(1)} %copy-done.2, bf16[128,512]{1,0:T(8,128)(2,1)S(1)} %copy-done.1, f32[128,512]{1,0:T(8,128)S(1)} %get-tuple-element.22.refs_0_, bf16[128,512]{1,0:T(8,128)(2,1)S(1)} %collective-permute-done.7.refs_1_, ...), custom_call_target="tpu_custom_call" | custom-call | flops 5242880 | bytes 1572864 | tf_op jit(solution)/shard_map/finish/pallas_call | solution.py:219
  (18 shorter events, 0.6 us)
Async XLA Ops:
  0.6 10.7 %collective-permute-start = (bf16[128,512]{1,0:T(8,128)(2,1)}, bf16[128,512]{1,0:T(8,128)(2,1)S(1)}, u32[]{:S(2)}, u32[]{:S(2)}) collective-permute-start(bf16[128,512]{1,0:T(8,128)(2,1)} %image_ref.1), channel_id=1, source_target_pairs={{0,8},{1,9},{2,10},{3,11},{4,12},{5,13},{6,14},{7,15},{8,0},{9,1},... | collective-permute-start | bytes 393224 | tf_op jit(solution)/shard_map/ppermute | solution.py:269
  4.7 8.4 %collective-permute-start.2 = (bf16[128,512]{1,0:T(8,128)(2,1)}, bf16[128,512]{1,0:T(8,128)(2,1)S(1)}, u32[]{:S(2)}, u32[]{:S(2)}) collective-permute-start(bf16[128,512]{1,0:T(8,128)(2,1)} %text_ref.1), channel_id=1, source_target_pairs={{0,2},{1,3},{2,0},{3,1},{4,6},{5,7},{6,4},{7,5},{8,10},{9,11},{10,... | collective-permute-start | bytes 393224 | tf_op jit(solution)/shard_map/ppermute | solution.py:269
  6.3 6.9 %collective-permute-start.1 = (bf16[128,512]{1,0:T(8,128)(2,1)}, bf16[128,512]{1,0:T(8,128)(2,1)S(1)}, u32[]{:S(2)}, u32[]{:S(2)}) collective-permute-start(bf16[128,512]{1,0:T(8,128)(2,1)} %text_ref.1), channel_id=1, source_target_pairs={{0,1},{1,0},{2,3},{3,2},{4,5},{5,4},{6,7},{7,6},{8,9},{9,8},{10,11... | collective-permute-start | bytes 393224 | tf_op jit(solution)/shard_map/ppermute | solution.py:269
  7.7 6.4 %collective-permute-start.3 = (bf16[128,512]{1,0:T(8,128)(2,1)}, bf16[128,512]{1,0:T(8,128)(2,1)S(1)}, u32[]{:S(2)}, u32[]{:S(2)}) collective-permute-start(bf16[128,512]{1,0:T(8,128)(2,1)} %text_ref.1), channel_id=1, source_target_pairs={{0,3},{1,2},{2,1},{3,0},{4,7},{5,6},{6,5},{7,4},{8,11},{9,10},{10,... | collective-permute-start | bytes 393224 | tf_op jit(solution)/shard_map/ppermute | solution.py:269
  8.2 6.6 %collective-permute-start.4 = (bf16[128,512]{1,0:T(8,128)(2,1)}, bf16[128,512]{1,0:T(8,128)(2,1)S(1)}, u32[]{:S(2)}, u32[]{:S(2)}) collective-permute-start(bf16[128,512]{1,0:T(8,128)(2,1)} %image_ref.1), channel_id=1, source_target_pairs={{0,4},{1,5},{2,6},{3,7},{4,0},{5,1},{6,2},{7,3},{8,12},{9,13},{10,... | collective-permute-start | bytes 393224 | tf_op jit(solution)/shard_map/ppermute | solution.py:269
  11.4 5.5 %collective-permute-start.5 = (bf16[128,512]{1,0:T(8,128)(2,1)S(1)}, bf16[128,512]{1,0:T(8,128)(2,1)S(1)}, u32[]{:S(2)}, u32[]{:S(2)}) collective-permute-start(bf16[128,512]{1,0:T(8,128)(2,1)S(1)} %collective-permute-done.refs_1_), channel_id=1, source_target_pairs={{0,4},{1,5},{2,6},{3,7},{4,0},{5,1},{6,2},{7,3},{8,12},{9,13},{10,... | collective-permute-start | bytes 393224 | tf_op jit(solution)/shard_map/ppermute | solution.py:269
  12.1 0.9 %copy-start = (bf16[128,512]{1,0:T(8,128)(2,1)S(1)}, bf16[128,512]{1,0:T(8,128)(2,1)}, u32[]{:S(2)}) copy-start(bf16[128,512]{1,0:T(8,128)(2,1)} %text_ref.1) | copy-start | bytes 393220
  13.1 1.7 %copy-start.2 = (bf16[128,512]{1,0:T(8,128)(2,1)S(1)}, bf16[128,512]{1,0:T(8,128)(2,1)}, u32[]{:S(2)}) copy-start(bf16[128,512]{1,0:T(8,128)(2,1)} %image_ref.1) | copy-start | bytes 393220
  14.3 2.6 %collective-permute-start.6 = (bf16[512,512]{1,0:T(8,128)(2,1)S(1)}, bf16[512,512]{1,0:T(8,128)(2,1)S(1)}, u32[]{:S(2)}, u32[]{:S(2)}) collective-permute-start(bf16[512,512]{1,0:T(8,128)(2,1)S(1)} %stack_units.1.text_ref.own_text_ref), channel_id=1, source_target_pairs={{0,16},{1,17},{2,18},{3,19},{4,20},{5,21},{6,22},{7,23},{8,24},{9,... | collective-permute-start | bytes 1572872 | tf_op jit(solution)/shard_map/ppermute | solution.py:269
  18.7 4.5 %collective-permute-start.10 = (bf16[512,512]{1,0:T(8,128)(2,1)S(1)}, bf16[512,512]{1,0:T(8,128)(2,1)S(1)}, u32[]{:S(2)}, u32[]{:S(2)}) collective-permute-start(bf16[512,512]{1,0:T(8,128)(2,1)S(1)} %get-tuple-element.27), channel_id=1, source_target_pairs={{0,16},{1,17},{2,18},{3,19},{4,20},{5,21},{6,22},{7,23},{8,24},{9,... | collective-permute-start | bytes 1572872 | tf_op jit(solution)/shard_map/ppermute | solution.py:269
  18.8 8.4 %collective-permute-start.7 = (bf16[128,512]{1,0:T(8,128)(2,1)S(1)}, bf16[128,512]{1,0:T(8,128)(2,1)S(1)}, u32[]{:S(2)}, u32[]{:S(2)}) collective-permute-start(bf16[128,512]{1,0:T(8,128)(2,1)S(1)} %get-tuple-element.23), channel_id=1, source_target_pairs={{0,4},{1,5},{2,6},{3,7},{4,0},{5,1},{6,2},{7,3},{8,12},{9,13},{10,... | collective-permute-start | bytes 393224 | tf_op jit(solution)/shard_map/ppermute | solution.py:269
  19.8 12.9 %collective-permute-start.8 = (bf16[128,512]{1,0:T(8,128)(2,1)S(1)}, bf16[128,512]{1,0:T(8,128)(2,1)S(1)}, u32[]{:S(2)}, u32[]{:S(2)}) collective-permute-start(bf16[128,512]{1,0:T(8,128)(2,1)S(1)} %get-tuple-element.24), channel_id=1, source_target_pairs={{0,8},{1,9},{2,10},{3,11},{4,12},{5,13},{6,14},{7,15},{8,0},{9,1},... | collective-permute-start | bytes 393224 | tf_op jit(solution)/shard_map/ppermute | solution.py:269
  22.8 9.9 %collective-permute-start.9 = (bf16[128,512]{1,0:T(8,128)(2,1)S(1)}, bf16[128,512]{1,0:T(8,128)(2,1)S(1)}, u32[]{:S(2)}, u32[]{:S(2)}) collective-permute-start(bf16[128,512]{1,0:T(8,128)(2,1)S(1)} %get-tuple-element.25), channel_id=1, source_target_pairs={{0,12},{1,13},{2,14},{3,15},{4,8},{5,9},{6,10},{7,11},{8,4},{9,5},... | collective-permute-start | bytes 393224 | tf_op jit(solution)/shard_map/ppermute | solution.py:269
  23.2 9.8 %copy-start.1 = (bf16[128,512]{1,0:T(8,128)(2,1)S(1)}, bf16[128,512]{1,0:T(8,128)(2,1)}, u32[]{:S(2)}) copy-start(bf16[128,512]{1,0:T(8,128)(2,1)} %text_ref.1) | copy-start | bytes 393220
  23.3 9.4 %collective-permute-start.11 = (bf16[128,512]{1,0:T(8,128)(2,1)S(1)}, bf16[128,512]{1,0:T(8,128)(2,1)S(1)}, u32[]{:S(2)}, u32[]{:S(2)}) collective-permute-start(bf16[128,512]{1,0:T(8,128)(2,1)S(1)} %get-tuple-element.29), channel_id=1, source_target_pairs={{0,1},{1,0},{2,3},{3,2},{4,5},{5,4},{6,7},{7,6},{8,9},{9,8},{10,11... | collective-permute-start | bytes 393224 | tf_op jit(solution)/shard_map/ppermute | solution.py:269
  24.9 7.8 %collective-permute-start.12 = (bf16[128,512]{1,0:T(8,128)(2,1)S(1)}, bf16[128,512]{1,0:T(8,128)(2,1)S(1)}, u32[]{:S(2)}, u32[]{:S(2)}) collective-permute-start(bf16[128,512]{1,0:T(8,128)(2,1)S(1)} %get-tuple-element.30), channel_id=1, source_target_pairs={{0,2},{1,3},{2,0},{3,1},{4,6},{5,7},{6,4},{7,5},{8,10},{9,11},{10,... | collective-permute-start | bytes 393224 | tf_op jit(solution)/shard_map/ppermute | solution.py:269
  27.1 5.9 %collective-permute-start.13 = (bf16[128,512]{1,0:T(8,128)(2,1)S(1)}, bf16[128,512]{1,0:T(8,128)(2,1)S(1)}, u32[]{:S(2)}, u32[]{:S(2)}) collective-permute-start(bf16[128,512]{1,0:T(8,128)(2,1)S(1)} %get-tuple-element.31), channel_id=1, source_target_pairs={{0,3},{1,2},{2,1},{3,0},{4,7},{5,6},{6,5},{7,4},{8,11},{9,10},{10,... | collective-permute-start | bytes 393224 | tf_op jit(solution)/shard_map/ppermute | solution.py:269

commit v21 on v20

--- a/solution.py
+++ b/solution.py
@@ -80,12 +80,12 @@
             preferred_element_type=jnp.float32,
         )
 
-    totals = [None] * len(jobs)
+    coefficients = [[] for _ in jobs]
+    totals = []
     coming = dots_of(*chunks[0])
     for step, (at, first, last) in enumerate(chunks):
         vi, text_ref, text_out, own, text_add = jobs[at]
         dots, coming = coming, dots_of(*chunks[step + 1]) if step + 1 < len(chunks) else None
-        vt = text_ref[first:last, :]
         e = jnp.exp2(slope * dots + shift)
         chance = pl.reciprocal(1.0 + e, approx=True)
         if own and first == 0:
@@ -100,8 +100,10 @@
         if text_add is not None:
             text_part = text_add[first:last, :] + text_part
         text_out[first:last, :] = text_part.astype(text_out.dtype)
-        part = jnp.dot(coefficient, vt, preferred_element_type=jnp.float32)
-        totals[at] = part if totals[at] is None else totals[at] + part
+        coefficients[at].append(coefficient)
+        if last == text_ref.shape[0]:
+            whole = jnp.concatenate(coefficients[at], axis=1)
+            totals.append(jnp.dot(whole, text_ref[...], preferred_element_type=jnp.float32))
     return totals
 
 

time: 34.3 us -> 34.2 us (level)
  no operation moved by 1% of the time
where the time goes in v21:
time: 34.2 us; the launch traced here: 34.1 us
  starting transfers between devices  20.1 us (59%)
  waiting for transfers between devices  6.54 us (19%)
  Pallas kernels  4.36 us (13%)
  between operations  2.02 us (6%)
  local copies, waits for them, and re-layouts  0.91 us (3%)
    ppermute x14, starting transfers between devices, move(): return lax.ppermute(value, AXES, perm)  20.1 us
    ppermute x14, waiting for transfers between devices, move(): return lax.ppermute(value, AXES, perm)  6.54 us
    pallas_call x6, Pallas kernels, call(): pl.pallas_call(kernel, out_shape=out_shape, in_specs=[VMEM] * len(operand...  3.3 us
    pallas_call x1, Pallas kernels, finish(): pl.pallas_call(functools.partial(finish_kernel, [side for side, _ in part...  1.07 us
    unnamed x6, local copies, waits for them, and re-layouts  0.91 us
  transfers between devices with their start and end apart: 14, of which 7 were waited for; matrix products, arithmetic and copies ran while one was open for 0% of the time, Pallas kernels for 5%

profile of v21, /device:TPU:0, one launch (start us, length us, event | category | flops | bytes accessed | tf_op | source)
XLA Modules:
  0.0 34.1 jit_solution(11353727691438529763)
XLA Ops:
  0.6 4.1 %collective-permute-start = (bf16[128,512]{1,0:T(8,128)(2,1)}, bf16[128,512]{1,0:T(8,128)(2,1)S(1)}, u32[]{:S(2)}, u32[]{:S(2)}) collective-permute-start(bf16[128,512]{1,0:T(8,128)(2,1)} %image_ref.1), channel_id=1, source_target_pairs={{0,8},{1,9},{2,10},{3,11},{4,12},{5,13},{6,14},{7,15},{8,0},{9,1},... | collective-permute-start | bytes 393224 | tf_op jit(solution)/shard_map/ppermute | solution.py:271
  4.7 1.5 %collective-permute-start.2 = (bf16[128,512]{1,0:T(8,128)(2,1)}, bf16[128,512]{1,0:T(8,128)(2,1)S(1)}, u32[]{:S(2)}, u32[]{:S(2)}) collective-permute-start(bf16[128,512]{1,0:T(8,128)(2,1)} %text_ref.1), channel_id=1, source_target_pairs={{0,2},{1,3},{2,0},{3,1},{4,6},{5,7},{6,4},{7,5},{8,10},{9,11},{10,... | collective-permute-start | bytes 393224 | tf_op jit(solution)/shard_map/ppermute | solution.py:271
  6.3 1.5 %collective-permute-start.1 = (bf16[128,512]{1,0:T(8,128)(2,1)}, bf16[128,512]{1,0:T(8,128)(2,1)S(1)}, u32[]{:S(2)}, u32[]{:S(2)}) collective-permute-start(bf16[128,512]{1,0:T(8,128)(2,1)} %text_ref.1), channel_id=1, source_target_pairs={{0,1},{1,0},{2,3},{3,2},{4,5},{5,4},{6,7},{7,6},{8,9},{9,8},{10,11... | collective-permute-start | bytes 393224 | tf_op jit(solution)/shard_map/ppermute | solution.py:271
  7.7 0.5 %collective-permute-start.3 = (bf16[128,512]{1,0:T(8,128)(2,1)}, bf16[128,512]{1,0:T(8,128)(2,1)S(1)}, u32[]{:S(2)}, u32[]{:S(2)}) collective-permute-start(bf16[128,512]{1,0:T(8,128)(2,1)} %text_ref.1), channel_id=1, source_target_pairs={{0,3},{1,2},{2,1},{3,0},{4,7},{5,6},{6,5},{7,4},{8,11},{9,10},{10,... | collective-permute-start | bytes 393224 | tf_op jit(solution)/shard_map/ppermute | solution.py:271
  8.2 1.6 %collective-permute-start.4 = (bf16[128,512]{1,0:T(8,128)(2,1)}, bf16[128,512]{1,0:T(8,128)(2,1)S(1)}, u32[]{:S(2)}, u32[]{:S(2)}) collective-permute-start(bf16[128,512]{1,0:T(8,128)(2,1)} %image_ref.1), channel_id=1, source_target_pairs={{0,4},{1,5},{2,6},{3,7},{4,0},{5,1},{6,2},{7,3},{8,12},{9,13},{10,... | collective-permute-start | bytes 393224 | tf_op jit(solution)/shard_map/ppermute | solution.py:271
  11.2 0.2 collective-permute-done.refs_1_
  11.4 0.8 %collective-permute-start.5 = (bf16[128,512]{1,0:T(8,128)(2,1)S(1)}, bf16[128,512]{1,0:T(8,128)(2,1)S(1)}, u32[]{:S(2)}, u32[]{:S(2)}) collective-permute-start(bf16[128,512]{1,0:T(8,128)(2,1)S(1)} %collective-permute-done.refs_1_), channel_id=1, source_target_pairs={{0,4},{1,5},{2,6},{3,7},{4,0},{5,1},{6,2},{7,3},{8,12},{9,13},{10,... | collective-permute-start | bytes 393224 | tf_op jit(solution)/shard_map/ppermute | solution.py:271
  12.1 0.9 %copy-done = bf16[128,512]{1,0:T(8,128)(2,1)S(1)} copy-done((bf16[128,512]{1,0:T(8,128)(2,1)S(1)}, bf16[128,512]{1,0:T(8,128)(2,1)}, u32[]{:S(2)}) %copy-start) | copy-done | bytes 131096
  13.2 1.0 %collective-permute-done.3.refs_3_ = bf16[128,512]{1,0:T(8,128)(2,1)S(1)} collective-permute-done((bf16[128,512]{1,0:T(8,128)(2,1)}, bf16[128,512]{1,0:T(8,128)(2,1)S(1)}, u32[]{:S(2)}, u32[]{:S(2)}) %collective-permute-start.3) | collective-permute-done | bytes 131104 | tf_op jit(solution)/shard_map/ppermute | solution.py:271
  14.2 0.2 stack_units.1.text_ref.own_text_ref
  14.4 0.4 %collective-permute-done.4.refs_2_ = bf16[128,512]{1,0:T(8,128)(2,1)S(1)} collective-permute-done((bf16[128,512]{1,0:T(8,128)(2,1)}, bf16[128,512]{1,0:T(8,128)(2,1)S(1)}, u32[]{:S(2)}, u32[]{:S(2)}) %collective-permute-start.4) | collective-permute-done | bytes 131104 | tf_op jit(solution)/shard_map/ppermute | solution.py:271
  14.9 1.1 %early_pairs.1 = (f32[512,512]{1,0:T(8,128)S(1)}, bf16[384,512]{1,0:T(8,128)(2,1)S(1)}, f32[384,512]{1,0:T(8,128)S(1)}) custom-call(f32[1,3]{1,0:T(1,128)S(1)} %maximum_bitcast_fusion.params_ref, bf16[512,512]{1,0:T(8,128)(2,1)S(1)} %stack_units.1.text_ref.own_text_ref, bf16[128,512]{1,0:T(8,128)(2,1)S(1)} %copy-done.2, ...), custom_call_target="tpu_custom_call" | custom-call | flops 603979776 | bytes 3145740 | tf_op jit(solution)/shard_map/early_pairs/pallas_call | solution.py:28
  16.0 0.9 %collective-permute-done.5.refs_0_ = bf16[128,512]{1,0:T(8,128)(2,1)S(1)} collective-permute-done((bf16[128,512]{1,0:T(8,128)(2,1)S(1)}, bf16[128,512]{1,0:T(8,128)(2,1)S(1)}, u32[]{:S(2)}, u32[]{:S(2)}) %collective-permute-start.5) | collective-permute-done | bytes 131104 | tf_op jit(solution)/shard_map/ppermute | solution.py:271
  17.0 1.7 %rest_pairs.1 = (f32[512,512]{1,0:T(8,128)S(1)}, bf16[512,512]{1,0:T(8,128)(2,1)S(1)}, f32[128,512]{1,0:T(8,128)S(1)}, bf16[128,512]{1,0:T(8,128)(2,1)S(1)}, bf1...) custom-call(f32[1,3]{1,0:T(1,128)S(1)} %maximum_bitcast_fusion.params_ref, ...), custom_call_target="tpu_custom_call" | custom-call | flops 1006632960 | bytes 5636108 | tf_op jit(solution)/shard_map/rest_pairs/pallas_call | solution.py:28
  18.7 1.0 %collective-permute-start.7 = (bf16[128,512]{1,0:T(8,128)(2,1)S(1)}, bf16[128,512]{1,0:T(8,128)(2,1)S(1)}, u32[]{:S(2)}, u32[]{:S(2)}) collective-permute-start(bf16[128,512]{1,0:T(8,128)(2,1)S(1)} %get-tuple-element.23), channel_id=1, source_target_pairs={{0,4},{1,5},{2,6},{3,7},{4,0},{5,1},{6,2},{7,3},{8,12},{9,13},{10,... | collective-permute-start | bytes 393224 | tf_op jit(solution)/shard_map/ppermute | solution.py:271
  19.8 3.0 %collective-permute-start.8 = (bf16[128,512]{1,0:T(8,128)(2,1)S(1)}, bf16[128,512]{1,0:T(8,128)(2,1)S(1)}, u32[]{:S(2)}, u32[]{:S(2)}) collective-permute-start(bf16[128,512]{1,0:T(8,128)(2,1)S(1)} %get-tuple-element.24), channel_id=1, source_target_pairs={{0,8},{1,9},{2,10},{3,11},{4,12},{5,13},{6,14},{7,15},{8,0},{9,1},... | collective-permute-start | bytes 393224 | tf_op jit(solution)/shard_map/ppermute | solution.py:271
  22.8 0.4 %collective-permute-start.9 = (bf16[128,512]{1,0:T(8,128)(2,1)S(1)}, bf16[128,512]{1,0:T(8,128)(2,1)S(1)}, u32[]{:S(2)}, u32[]{:S(2)}) collective-permute-start(bf16[128,512]{1,0:T(8,128)(2,1)S(1)} %get-tuple-element.25), channel_id=1, source_target_pairs={{0,12},{1,13},{2,14},{3,15},{4,8},{5,9},{6,10},{7,11},{8,4},{9,5},... | collective-permute-start | bytes 393224 | tf_op jit(solution)/shard_map/ppermute | solution.py:271
  23.3 1.6 %collective-permute-start.11 = (bf16[128,512]{1,0:T(8,128)(2,1)S(1)}, bf16[128,512]{1,0:T(8,128)(2,1)S(1)}, u32[]{:S(2)}, u32[]{:S(2)}) collective-permute-start(bf16[128,512]{1,0:T(8,128)(2,1)S(1)} %get-tuple-element.29), channel_id=1, source_target_pairs={{0,1},{1,0},{2,3},{3,2},{4,5},{5,4},{6,7},{7,6},{8,9},{9,8},{10,11... | collective-permute-start | bytes 393224 | tf_op jit(solution)/shard_map/ppermute | solution.py:271
  24.9 1.5 %collective-permute-start.12 = (bf16[128,512]{1,0:T(8,128)(2,1)S(1)}, bf16[128,512]{1,0:T(8,128)(2,1)S(1)}, u32[]{:S(2)}, u32[]{:S(2)}) collective-permute-start(bf16[128,512]{1,0:T(8,128)(2,1)S(1)} %get-tuple-element.30), channel_id=1, source_target_pairs={{0,2},{1,3},{2,0},{3,1},{4,6},{5,7},{6,4},{7,5},{8,10},{9,11},{10,... | collective-permute-start | bytes 393224 | tf_op jit(solution)/shard_map/ppermute | solution.py:271
  26.4 0.7 %collective-permute-done.7.refs_1_ = bf16[128,512]{1,0:T(8,128)(2,1)S(1)} collective-permute-done((bf16[128,512]{1,0:T(8,128)(2,1)S(1)}, bf16[128,512]{1,0:T(8,128)(2,1)S(1)}, u32[]{:S(2)}, u32[]{:S(2)}) %collective-permute-start.7) | collective-permute-done | bytes 131104 | tf_op jit(solution)/shard_map/ppermute | solution.py:271
  27.1 2.5 %collective-permute-start.13 = (bf16[128,512]{1,0:T(8,128)(2,1)S(1)}, bf16[128,512]{1,0:T(8,128)(2,1)S(1)}, u32[]{:S(2)}, u32[]{:S(2)}) collective-permute-start(bf16[128,512]{1,0:T(8,128)(2,1)S(1)} %get-tuple-element.31), channel_id=1, source_target_pairs={{0,3},{1,2},{2,1},{3,0},{4,7},{5,6},{6,5},{7,4},{8,11},{9,10},{10,... | collective-permute-start | bytes 393224 | tf_op jit(solution)/shard_map/ppermute | solution.py:271
  29.6 3.1 %collective-permute-done.8.refs_2_ = bf16[128,512]{1,0:T(8,128)(2,1)S(1)} collective-permute-done((bf16[128,512]{1,0:T(8,128)(2,1)S(1)}, bf16[128,512]{1,0:T(8,128)(2,1)S(1)}, u32[]{:S(2)}, u32[]{:S(2)}) %collective-permute-start.8) | collective-permute-done | bytes 131104 | tf_op jit(solution)/shard_map/ppermute | solution.py:271
  32.7 0.3 collective-permute-done.13.refs_7_
  33.0 1.1 %finish.1 = (f32[128,512]{1,0:T(8,128)}, f32[128,512]{1,0:T(8,128)}) custom-call(bf16[128,512]{1,0:T(8,128)(2,1)S(1)} %copy-done.2, bf16[128,512]{1,0:T(8,128)(2,1)S(1)} %copy-done.1, f32[128,512]{1,0:T(8,128)S(1)} %get-tuple-element.22.refs_0_, bf16[128,512]{1,0:T(8,128)(2,1)S(1)} %collective-permute-done.7.refs_1_, ...), custom_call_target="tpu_custom_call" | custom-call | flops 5242880 | bytes 1572864 | tf_op jit(solution)/shard_map/finish/pallas_call | solution.py:221
  (18 shorter events, 0.6 us)
Async XLA Ops:
  0.6 10.7 %collective-permute-start = (bf16[128,512]{1,0:T(8,128)(2,1)}, bf16[128,512]{1,0:T(8,128)(2,1)S(1)}, u32[]{:S(2)}, u32[]{:S(2)}) collective-permute-start(bf16[128,512]{1,0:T(8,128)(2,1)} %image_ref.1), channel_id=1, source_target_pairs={{0,8},{1,9},{2,10},{3,11},{4,12},{5,13},{6,14},{7,15},{8,0},{9,1},... | collective-permute-start | bytes 393224 | tf_op jit(solution)/shard_map/ppermute | solution.py:271
  4.7 8.4 %collective-permute-start.2 = (bf16[128,512]{1,0:T(8,128)(2,1)}, bf16[128,512]{1,0:T(8,128)(2,1)S(1)}, u32[]{:S(2)}, u32[]{:S(2)}) collective-permute-start(bf16[128,512]{1,0:T(8,128)(2,1)} %text_ref.1), channel_id=1, source_target_pairs={{0,2},{1,3},{2,0},{3,1},{4,6},{5,7},{6,4},{7,5},{8,10},{9,11},{10,... | collective-permute-start | bytes 393224 | tf_op jit(solution)/shard_map/ppermute | solution.py:271
  6.3 6.9 %collective-permute-start.1 = (bf16[128,512]{1,0:T(8,128)(2,1)}, bf16[128,512]{1,0:T(8,128)(2,1)S(1)}, u32[]{:S(2)}, u32[]{:S(2)}) collective-permute-start(bf16[128,512]{1,0:T(8,128)(2,1)} %text_ref.1), channel_id=1, source_target_pairs={{0,1},{1,0},{2,3},{3,2},{4,5},{5,4},{6,7},{7,6},{8,9},{9,8},{10,11... | collective-permute-start | bytes 393224 | tf_op jit(solution)/shard_map/ppermute | solution.py:271
  7.7 6.4 %collective-permute-start.3 = (bf16[128,512]{1,0:T(8,128)(2,1)}, bf16[128,512]{1,0:T(8,128)(2,1)S(1)}, u32[]{:S(2)}, u32[]{:S(2)}) collective-permute-start(bf16[128,512]{1,0:T(8,128)(2,1)} %text_ref.1), channel_id=1, source_target_pairs={{0,3},{1,2},{2,1},{3,0},{4,7},{5,6},{6,5},{7,4},{8,11},{9,10},{10,... | collective-permute-start | bytes 393224 | tf_op jit(solution)/shard_map/ppermute | solution.py:271
  8.2 6.6 %collective-permute-start.4 = (bf16[128,512]{1,0:T(8,128)(2,1)}, bf16[128,512]{1,0:T(8,128)(2,1)S(1)}, u32[]{:S(2)}, u32[]{:S(2)}) collective-permute-start(bf16[128,512]{1,0:T(8,128)(2,1)} %image_ref.1), channel_id=1, source_target_pairs={{0,4},{1,5},{2,6},{3,7},{4,0},{5,1},{6,2},{7,3},{8,12},{9,13},{10,... | collective-permute-start | bytes 393224 | tf_op jit(solution)/shard_map/ppermute | solution.py:271
  11.4 5.5 %collective-permute-start.5 = (bf16[128,512]{1,0:T(8,128)(2,1)S(1)}, bf16[128,512]{1,0:T(8,128)(2,1)S(1)}, u32[]{:S(2)}, u32[]{:S(2)}) collective-permute-start(bf16[128,512]{1,0:T(8,128)(2,1)S(1)} %collective-permute-done.refs_1_), channel_id=1, source_target_pairs={{0,4},{1,5},{2,6},{3,7},{4,0},{5,1},{6,2},{7,3},{8,12},{9,13},{10,... | collective-permute-start | bytes 393224 | tf_op jit(solution)/shard_map/ppermute | solution.py:271
  12.1 0.9 %copy-start = (bf16[128,512]{1,0:T(8,128)(2,1)S(1)}, bf16[128,512]{1,0:T(8,128)(2,1)}, u32[]{:S(2)}) copy-start(bf16[128,512]{1,0:T(8,128)(2,1)} %text_ref.1) | copy-start | bytes 393220
  13.1 1.7 %copy-start.2 = (bf16[128,512]{1,0:T(8,128)(2,1)S(1)}, bf16[128,512]{1,0:T(8,128)(2,1)}, u32[]{:S(2)}) copy-start(bf16[128,512]{1,0:T(8,128)(2,1)} %image_ref.1) | copy-start | bytes 393220
  14.3 2.6 %collective-permute-start.6 = (bf16[512,512]{1,0:T(8,128)(2,1)S(1)}, bf16[512,512]{1,0:T(8,128)(2,1)S(1)}, u32[]{:S(2)}, u32[]{:S(2)}) collective-permute-start(bf16[512,512]{1,0:T(8,128)(2,1)S(1)} %stack_units.1.text_ref.own_text_ref), channel_id=1, source_target_pairs={{0,16},{1,17},{2,18},{3,19},{4,20},{5,21},{6,22},{7,23},{8,24},{9,... | collective-permute-start | bytes 1572872 | tf_op jit(solution)/shard_map/ppermute | solution.py:271
  18.7 4.5 %collective-permute-start.10 = (bf16[512,512]{1,0:T(8,128)(2,1)S(1)}, bf16[512,512]{1,0:T(8,128)(2,1)S(1)}, u32[]{:S(2)}, u32[]{:S(2)}) collective-permute-start(bf16[512,512]{1,0:T(8,128)(2,1)S(1)} %get-tuple-element.27), channel_id=1, source_target_pairs={{0,16},{1,17},{2,18},{3,19},{4,20},{5,21},{6,22},{7,23},{8,24},{9,... | collective-permute-start | bytes 1572872 | tf_op jit(solution)/shard_map/ppermute | solution.py:271
  18.7 8.4 %collective-permute-start.7 = (bf16[128,512]{1,0:T(8,128)(2,1)S(1)}, bf16[128,512]{1,0:T(8,128)(2,1)S(1)}, u32[]{:S(2)}, u32[]{:S(2)}) collective-permute-start(bf16[128,512]{1,0:T(8,128)(2,1)S(1)} %get-tuple-element.23), channel_id=1, source_target_pairs={{0,4},{1,5},{2,6},{3,7},{4,0},{5,1},{6,2},{7,3},{8,12},{9,13},{10,... | collective-permute-start | bytes 393224 | tf_op jit(solution)/shard_map/ppermute | solution.py:271
  19.8 12.9 %collective-permute-start.8 = (bf16[128,512]{1,0:T(8,128)(2,1)S(1)}, bf16[128,512]{1,0:T(8,128)(2,1)S(1)}, u32[]{:S(2)}, u32[]{:S(2)}) collective-permute-start(bf16[128,512]{1,0:T(8,128)(2,1)S(1)} %get-tuple-element.24), channel_id=1, source_target_pairs={{0,8},{1,9},{2,10},{3,11},{4,12},{5,13},{6,14},{7,15},{8,0},{9,1},... | collective-permute-start | bytes 393224 | tf_op jit(solution)/shard_map/ppermute | solution.py:271
  22.8 9.9 %collective-permute-start.9 = (bf16[128,512]{1,0:T(8,128)(2,1)S(1)}, bf16[128,512]{1,0:T(8,128)(2,1)S(1)}, u32[]{:S(2)}, u32[]{:S(2)}) collective-permute-start(bf16[128,512]{1,0:T(8,128)(2,1)S(1)} %get-tuple-element.25), channel_id=1, source_target_pairs={{0,12},{1,13},{2,14},{3,15},{4,8},{5,9},{6,10},{7,11},{8,4},{9,5},... | collective-permute-start | bytes 393224 | tf_op jit(solution)/shard_map/ppermute | solution.py:271
  23.2 9.8 %copy-start.1 = (bf16[128,512]{1,0:T(8,128)(2,1)S(1)}, bf16[128,512]{1,0:T(8,128)(2,1)}, u32[]{:S(2)}) copy-start(bf16[128,512]{1,0:T(8,128)(2,1)} %text_ref.1) | copy-start | bytes 393220
  23.3 9.4 %collective-permute-start.11 = (bf16[128,512]{1,0:T(8,128)(2,1)S(1)}, bf16[128,512]{1,0:T(8,128)(2,1)S(1)}, u32[]{:S(2)}, u32[]{:S(2)}) collective-permute-start(bf16[128,512]{1,0:T(8,128)(2,1)S(1)} %get-tuple-element.29), channel_id=1, source_target_pairs={{0,1},{1,0},{2,3},{3,2},{4,5},{5,4},{6,7},{7,6},{8,9},{9,8},{10,11... | collective-permute-start | bytes 393224 | tf_op jit(solution)/shard_map/ppermute | solution.py:271
  24.9 7.8 %collective-permute-start.12 = (bf16[128,512]{1,0:T(8,128)(2,1)S(1)}, bf16[128,512]{1,0:T(8,128)(2,1)S(1)}, u32[]{:S(2)}, u32[]{:S(2)}) collective-permute-start(bf16[128,512]{1,0:T(8,128)(2,1)S(1)} %get-tuple-element.30), channel_id=1, source_target_pairs={{0,2},{1,3},{2,0},{3,1},{4,6},{5,7},{6,4},{7,5},{8,10},{9,11},{10,... | collective-permute-start | bytes 393224 | tf_op jit(solution)/shard_map/ppermute | solution.py:271
  27.1 5.9 %collective-permute-start.13 = (bf16[128,512]{1,0:T(8,128)(2,1)S(1)}, bf16[128,512]{1,0:T(8,128)(2,1)S(1)}, u32[]{:S(2)}, u32[]{:S(2)}) collective-permute-start(bf16[128,512]{1,0:T(8,128)(2,1)S(1)} %get-tuple-element.31), channel_id=1, source_target_pairs={{0,3},{1,2},{2,1},{3,0},{4,7},{5,6},{6,5},{7,4},{8,11},{9,10},{10,... | collective-permute-start | bytes 393224 | tf_op jit(solution)/shard_map/ppermute | solution.py:271

commit v22 on v13

--- a/solution.py
+++ b/solution.py
@@ -12,7 +12,7 @@
 VMEM_LIMIT = 32 * 1024 * 1024
 SPAN = 256
 PIECE = 32
-LATE = 30000
+LATE = 16500
 FAR = 60000
 LOG2_E = math.log2(math.e)
 VMEM = pl.BlockSpec(memory_space=pltpu.VMEM)
@@ -67,23 +67,25 @@
     return call(stack_units_kernel, [out], blocks, flops=4 * out.size, name="stack_units")[0]
 
 
-def pairs(vi, params_ref, text_ref, text_out, own=0, text_add=None):
+def pairs(params_ref, jobs):
     slope, shift, temper = (params_ref[0:1, at:at + 1] for at in range(3))
-    held = text_ref.shape[0]
-    total = None
-
-    def dots_of(first):
+    chunks = [
+        (at, first, min(first + SPAN, job[1].shape[0]))
+        for at, job in enumerate(jobs) for first in range(0, job[1].shape[0], SPAN)
+    ]
+
+    def dots_of(at, first, last):
+        vi, text_ref = jobs[at][:2]
         return lax.dot_general(
-            vi,
-            text_ref[first:min(first + SPAN, held), :],
-            (((1,), (1,)), ((), ())),
+            vi, text_ref[first:last, :], (((1,), (1,)), ((), ())),
             preferred_element_type=jnp.float32,
         )
 
-    coming = dots_of(0)
-    for first in range(0, held, SPAN):
-        last = min(first + SPAN, held)
-        dots, coming = coming, dots_of(last) if last < held else None
+    totals = [None] * len(jobs)
+    coming = dots_of(*chunks[0])
+    for step, (at, first, last) in enumerate(chunks):
+        vi, text_ref, text_out, own, text_add = jobs[at]
+        dots, coming = coming, dots_of(*chunks[step + 1]) if step + 1 < len(chunks) else None
         vt = text_ref[first:last, :]
         e = jnp.exp2(slope * dots + shift)
         chance = pl.reciprocal(1.0 + e, approx=True)
@@ -100,8 +102,8 @@
             text_part = text_add[first:last, :] + text_part
         text_out[first:last, :] = text_part.astype(text_out.dtype)
         part = jnp.dot(coefficient, vt, preferred_element_type=jnp.float32)
-        total = part if total is None else total + part
-    return total
+        totals[at] = part if totals[at] is None else totals[at] + part
+    return totals
 
 
 def early_pairs_kernel(params_ref, text_ref, *refs):
@@ -109,15 +111,18 @@
     rows = image_refs[0].shape[0]
     for a, ref in enumerate(image_refs):
         units_out[a * rows:(a + 1) * rows, :] = unit_rows(ref[...])[0].astype(jnp.bfloat16)
-    total_out[...] = pairs(units_out[...], params_ref, text_ref, text_out, own=rows)
+    (total,) = pairs(params_ref, [(units_out[...], text_ref, text_out, rows, None)])
+    total_out[...] = total
 
 
 def early_rest_kernel(count, params_ref, units_ref, total_ref, *refs):
     text_refs, text_out, image_out = refs[:count], refs[count:2 * count], refs[2 * count:]
     rows = image_out[0].shape[0]
-    vi, total = units_ref[...], total_ref[...]
-    for text_ref, out in zip(text_refs, text_out):
-        total = total + pairs(vi, params_ref, text_ref, out)
+    vi = units_ref[...]
+    totals = pairs(
+        params_ref, [(vi, text_ref, out, 0, None) for text_ref, out in zip(text_refs, text_out)]
+    )
+    total = sum(totals, total_ref[...])
     for a, ref in enumerate(image_out):
         ref[...] = total[a * rows:(a + 1) * rows, :].astype(ref.dtype)
 
@@ -126,9 +131,15 @@
     text_refs, add_refs = refs[:count], refs[count:2 * count]
     text_out, image_out = refs[2 * count:3 * count], refs[3 * count:]
     rows = image_out[0].shape[0]
+    vi = units_ref[...]
     total = sum(
-        pairs(units_ref[...], params_ref, text_ref, out, text_add=add)
-        for text_ref, add, out in zip(text_refs, add_refs, text_out)
+        pairs(
+            params_ref,
+            [
+                (vi, text_ref, out, 0, add)
+                for text_ref, add, out in zip(text_refs, add_refs, text_out)
+            ],
+        )
     )
     for a, ref in enumerate(image_out):
         ref[...] = total[a * rows:(a + 1) * rows, :].astype(ref.dtype)
@@ -319,10 +330,10 @@
 
         came = [move(part, grp=-g) for g, part in enumerate(text_parts) if g]
         far_sum = add_far(
-            [far_parts[0, 0]] + [give_back(h, w) for h, w in early if h]
+            [far_parts[0, 0]] + [give_back(h, w) for h, w in early if w]
         )
         far_sum, own_text = lax.optimization_barrier((far_sum, text_parts[0]))
-        far_came = [give_back(h, w) for h, w in late] + [give_back(h, w) for h, w in early if w]
+        far_came = [give_back(h, w) for h, w in far_parts if h]
         near_parts = add_stacks([own_text, *came], near_count)
         near_parts = [near_parts[0]] + [
             move(part, near=-n) for n, part in enumerate(near_parts) if n

time: 40.5 us -> 36.8 us (0.909)
  waiting for transfers between devices: 14.5 us -> 10.5 us
    ppermute x14, waiting for transfers between devices: 14.5 us -> 10.5 us  [move(): return lax.ppermute(value, AXES, perm)]
  transfers between devices with their start and end apart: 14 -> 14, of which waited for: 8 -> 8; matrix products, arithmetic and copies ran while one was open for 0% -> 0% of each run, Pallas kernels for 7% -> 8%
where the time goes in v22:
time: 36.8 us; the launch traced here: 36.6 us
  starting transfers between devices  18.1 us (49%)
  waiting for transfers between devices  10.5 us (29%)
  Pallas kernels  5.04 us (14%)
  between operations  2.02 us (5%)
  local copies, waits for them, and re-layouts  0.92 us (2%)
    ppermute x14, starting transfers between devices, move(): return lax.ppermute(value, AXES, perm)  18.1 us
    ppermute x14, waiting for transfers between devices, move(): return lax.ppermute(value, AXES, perm)  10.5 us
    pallas_call x8, Pallas kernels, call(): pl.pallas_call(kernel, out_shape=out_shape, in_specs=[VMEM] * len(operand...  3.99 us
    pallas_call x1, Pallas kernels, finish(): pl.pallas_call(functools.partial(finish_kernel, [side for side, _ in part...  1.05 us
    unnamed x6, local copies, waits for them, and re-layouts  0.92 us
  transfers between devices with their start and end apart: 14, of which 8 were waited for; matrix products, arithmetic and copies ran while one was open for 0% of the time, Pallas kernels for 8%

profile of v22, /device:TPU:0, one launch (start us, length us, event | category | flops | bytes accessed | tf_op | source)
XLA Modules:
  0.0 36.6 jit_solution(8450316805590699249)
XLA Ops:
  0.6 4.1 %collective-permute-start = (bf16[128,512]{1,0:T(8,128)(2,1)}, bf16[128,512]{1,0:T(8,128)(2,1)S(1)}, u32[]{:S(2)}, u32[]{:S(2)}) collective-permute-start(bf16[128,512]{1,0:T(8,128)(2,1)} %image_ref.1), channel_id=1, source_target_pairs={{0,8},{1,9},{2,10},{3,11},{4,12},{5,13},{6,14},{7,15},{8,0},{9,1},... | collective-permute-start | bytes 393224 | tf_op jit(solution)/shard_map/ppermute | solution.py:304
  4.7 1.5 %collective-permute-start.1 = (bf16[128,512]{1,0:T(8,128)(2,1)}, bf16[128,512]{1,0:T(8,128)(2,1)S(1)}, u32[]{:S(2)}, u32[]{:S(2)}) collective-permute-start(bf16[128,512]{1,0:T(8,128)(2,1)} %text_ref.1), channel_id=1, source_target_pairs={{0,1},{1,0},{2,3},{3,2},{4,5},{5,4},{6,7},{7,6},{8,9},{9,8},{10,11... | collective-permute-start | bytes 393224 | tf_op jit(solution)/shard_map/ppermute | solution.py:304
  6.2 1.5 %collective-permute-start.2 = (bf16[128,512]{1,0:T(8,128)(2,1)}, bf16[128,512]{1,0:T(8,128)(2,1)S(1)}, u32[]{:S(2)}, u32[]{:S(2)}) collective-permute-start(bf16[128,512]{1,0:T(8,128)(2,1)} %text_ref.1), channel_id=1, source_target_pairs={{0,2},{1,3},{2,0},{3,1},{4,6},{5,7},{6,4},{7,5},{8,10},{9,11},{10,... | collective-permute-start | bytes 393224 | tf_op jit(solution)/shard_map/ppermute | solution.py:304
  7.7 0.5 %collective-permute-start.3 = (bf16[128,512]{1,0:T(8,128)(2,1)}, bf16[128,512]{1,0:T(8,128)(2,1)S(1)}, u32[]{:S(2)}, u32[]{:S(2)}) collective-permute-start(bf16[128,512]{1,0:T(8,128)(2,1)} %text_ref.1), channel_id=1, source_target_pairs={{0,3},{1,2},{2,1},{3,0},{4,7},{5,6},{6,5},{7,4},{8,11},{9,10},{10,... | collective-permute-start | bytes 393224 | tf_op jit(solution)/shard_map/ppermute | solution.py:304
  8.2 1.6 %collective-permute-start.4 = (bf16[128,512]{1,0:T(8,128)(2,1)}, bf16[128,512]{1,0:T(8,128)(2,1)S(1)}, u32[]{:S(2)}, u32[]{:S(2)}) collective-permute-start(bf16[128,512]{1,0:T(8,128)(2,1)} %image_ref.1), channel_id=1, source_target_pairs={{0,4},{1,5},{2,6},{3,7},{4,0},{5,1},{6,2},{7,3},{8,12},{9,13},{10,... | collective-permute-start | bytes 393224 | tf_op jit(solution)/shard_map/ppermute | solution.py:304
  11.4 0.8 %collective-permute-start.5 = (bf16[128,512]{1,0:T(8,128)(2,1)S(1)}, bf16[128,512]{1,0:T(8,128)(2,1)S(1)}, u32[]{:S(2)}, u32[]{:S(2)}) collective-permute-start(bf16[128,512]{1,0:T(8,128)(2,1)S(1)} %collective-permute-done.refs_1_), channel_id=1, source_target_pairs={{0,4},{1,5},{2,6},{3,7},{4,0},{5,1},{6,2},{7,3},{8,12},{9,13},{10,... | collective-permute-start | bytes 393224 | tf_op jit(solution)/shard_map/ppermute | solution.py:304
  12.1 0.9 %copy-done = bf16[128,512]{1,0:T(8,128)(2,1)S(1)} copy-done((bf16[128,512]{1,0:T(8,128)(2,1)S(1)}, bf16[128,512]{1,0:T(8,128)(2,1)}, u32[]{:S(2)}) %copy-start) | copy-done | bytes 131096
  13.2 1.0 %collective-permute-done.2.refs_2_ = bf16[128,512]{1,0:T(8,128)(2,1)S(1)} collective-permute-done((bf16[128,512]{1,0:T(8,128)(2,1)}, bf16[128,512]{1,0:T(8,128)(2,1)S(1)}, u32[]{:S(2)}, u32[]{:S(2)}) %collective-permute-start.2) | collective-permute-done | bytes 131104 | tf_op jit(solution)/shard_map/ppermute | solution.py:304
  14.5 0.4 %collective-permute-done.4.refs_2_ = bf16[128,512]{1,0:T(8,128)(2,1)S(1)} collective-permute-done((bf16[128,512]{1,0:T(8,128)(2,1)}, bf16[128,512]{1,0:T(8,128)(2,1)S(1)}, u32[]{:S(2)}, u32[]{:S(2)}) %collective-permute-start.4) | collective-permute-done | bytes 131104 | tf_op jit(solution)/shard_map/ppermute | solution.py:304
  14.9 1.1 %early_pairs.1 = (f32[512,512]{1,0:T(8,128)S(1)}, bf16[384,512]{1,0:T(8,128)(2,1)S(1)}, f32[384,512]{1,0:T(8,128)S(1)}) custom-call(f32[1,3]{1,0:T(1,128)S(1)} %maximum_bitcast_fusion.params_ref, bf16[512,512]{1,0:T(8,128)(2,1)S(1)} %stack_units.1.text_ref.refs_0_, bf16[128,512]{1,0:T(8,128)(2,1)S(1)} %copy-done.2, ...), custom_call_target="tpu_custom_call" | custom-call | flops 603979776 | bytes 3145740 | tf_op jit(solution)/shard_map/early_pairs/pallas_call | solution.py:29
  16.0 0.9 %collective-permute-done.5.refs_0_ = bf16[128,512]{1,0:T(8,128)(2,1)S(1)} collective-permute-done((bf16[128,512]{1,0:T(8,128)(2,1)S(1)}, bf16[128,512]{1,0:T(8,128)(2,1)S(1)}, u32[]{:S(2)}, u32[]{:S(2)}) %collective-permute-start.5) | collective-permute-done | bytes 131104 | tf_op jit(solution)/shard_map/ppermute | solution.py:304
  17.0 1.1 %early_rest.1 = (f32[512,512]{1,0:T(8,128)S(1)}, f32[128,512]{1,0:T(8,128)S(1)}, bf16[128,512]{1,0:T(8,128)(2,1)S(1)}, bf16[128,512]{1,0:T(8,128)(2,1)S(1)}) custom-call(f32[1,3]{1,0:T(1,128)S(1)} %maximum_bitcast_fusion.params_ref, bf16[384,512]{1,0:T(8,128)(2,1)S(1)} %get-tuple-element.23.units_ref, f32[384,512]{1,0:T(8,128)S(1)} %get-tuple-element.26.total_ref, ...), custom_call_target="tpu_custom_call" | custom-call | flops 603979776 | bytes 3276812 | tf_op jit(solution)/shard_map/early_rest/pallas_call | solution.py:29
  18.1 1.0 %collective-permute-start.7 = (bf16[128,512]{1,0:T(8,128)(2,1)S(1)}, bf16[128,512]{1,0:T(8,128)(2,1)S(1)}, u32[]{:S(2)}, u32[]{:S(2)}) collective-permute-start(bf16[128,512]{1,0:T(8,128)(2,1)S(1)} %get-tuple-element.28), channel_id=1, source_target_pairs={{0,4},{1,5},{2,6},{3,7},{4,0},{5,1},{6,2},{7,3},{8,12},{9,13},{10,... | collective-permute-start | bytes 393224 | tf_op jit(solution)/shard_map/ppermute | solution.py:304
  19.1 3.0 %collective-permute-start.8 = (bf16[128,512]{1,0:T(8,128)(2,1)S(1)}, bf16[128,512]{1,0:T(8,128)(2,1)S(1)}, u32[]{:S(2)}, u32[]{:S(2)}) collective-permute-start(bf16[128,512]{1,0:T(8,128)(2,1)S(1)} %get-tuple-element.34), channel_id=1, source_target_pairs={{0,8},{1,9},{2,10},{3,11},{4,12},{5,13},{6,14},{7,15},{8,0},{9,1},... | collective-permute-start | bytes 393224 | tf_op jit(solution)/shard_map/ppermute | solution.py:304
  22.1 1.2 %late_pairs.1 = (f32[512,512]{1,0:T(8,128)S(1)}, bf16[512,512]{1,0:T(8,128)(2,1)S(1)}, bf16[128,512]{1,0:T(8,128)(2,1)S(1)}) custom-call(f32[1,3]{1,0:T(1,128)S(1)} %maximum_bitcast_fusion.params_ref, bf16[128,512]{1,0:T(8,128)(2,1)S(1)} %late_units.1.units_ref, bf16[512,512]{1,0:T(8,128)(2,1)S(1)} %stack_units.1.text_ref.refs_0_, ...), custom_call_target="tpu_custom_call" | custom-call | flops 402653184 | bytes 4980748 | tf_op jit(solution)/shard_map/late_pairs/pallas_call | solution.py:29
  23.3 0.5 %collective-permute-start.9 = (bf16[128,512]{1,0:T(8,128)(2,1)S(1)}, bf16[128,512]{1,0:T(8,128)(2,1)S(1)}, u32[]{:S(2)}, u32[]{:S(2)}) collective-permute-start(bf16[128,512]{1,0:T(8,128)(2,1)S(1)} %get-tuple-element.35), channel_id=1, source_target_pairs={{0,12},{1,13},{2,14},{3,15},{4,8},{5,9},{6,10},{7,11},{8,4},{9,5},... | collective-permute-start | bytes 393224 | tf_op jit(solution)/shard_map/ppermute | solution.py:304
  23.9 0.9 %collective-permute-done.7.refs_1_ = bf16[128,512]{1,0:T(8,128)(2,1)S(1)} collective-permute-done((bf16[128,512]{1,0:T(8,128)(2,1)S(1)}, bf16[128,512]{1,0:T(8,128)(2,1)S(1)}, u32[]{:S(2)}, u32[]{:S(2)}) %collective-permute-start.7) | collective-permute-done | bytes 131104 | tf_op jit(solution)/shard_map/ppermute | solution.py:304
  24.8 1.0 %collective-permute-done.10.refs_1_ = bf16[512,512]{1,0:T(8,128)(2,1)S(1)} collective-permute-done((bf16[512,512]{1,0:T(8,128)(2,1)S(1)}, bf16[512,512]{1,0:T(8,128)(2,1)S(1)}, u32[]{:S(2)}, u32[]{:S(2)}) %collective-permute-start.10) | collective-permute-done | bytes 524320 | tf_op jit(solution)/shard_map/ppermute | solution.py:304
  25.9 1.6 %collective-permute-start.11 = (bf16[128,512]{1,0:T(8,128)(2,1)S(1)}, bf16[128,512]{1,0:T(8,128)(2,1)S(1)}, u32[]{:S(2)}, u32[]{:S(2)}) collective-permute-start(bf16[128,512]{1,0:T(8,128)(2,1)S(1)} %get-tuple-element.39), channel_id=1, source_target_pairs={{0,1},{1,0},{2,3},{3,2},{4,5},{5,4},{6,7},{7,6},{8,9},{9,8},{10,11... | collective-permute-start | bytes 393224 | tf_op jit(solution)/shard_map/ppermute | solution.py:304
  27.5 1.5 %collective-permute-start.12 = (bf16[128,512]{1,0:T(8,128)(2,1)S(1)}, bf16[128,512]{1,0:T(8,128)(2,1)S(1)}, u32[]{:S(2)}, u32[]{:S(2)}) collective-permute-start(bf16[128,512]{1,0:T(8,128)(2,1)S(1)} %get-tuple-element.40), channel_id=1, source_target_pairs={{0,2},{1,3},{2,0},{3,1},{4,6},{5,7},{6,4},{7,5},{8,10},{9,11},{10,... | collective-permute-start | bytes 393224 | tf_op jit(solution)/shard_map/ppermute | solution.py:304
  29.0 0.4 %collective-permute-start.13 = (bf16[128,512]{1,0:T(8,128)(2,1)S(1)}, bf16[128,512]{1,0:T(8,128)(2,1)S(1)}, u32[]{:S(2)}, u32[]{:S(2)}) collective-permute-start(bf16[128,512]{1,0:T(8,128)(2,1)S(1)} %get-tuple-element.41), channel_id=1, source_target_pairs={{0,3},{1,2},{2,1},{3,0},{4,7},{5,6},{6,5},{7,4},{8,11},{9,10},{10,... | collective-permute-start | bytes 393224 | tf_op jit(solution)/shard_map/ppermute | solution.py:304
  29.4 2.5 %collective-permute-done.8.refs_1_ = bf16[128,512]{1,0:T(8,128)(2,1)S(1)} collective-permute-done((bf16[128,512]{1,0:T(8,128)(2,1)S(1)}, bf16[128,512]{1,0:T(8,128)(2,1)S(1)}, u32[]{:S(2)}, u32[]{:S(2)}) %collective-permute-start.8) | collective-permute-done | bytes 131104 | tf_op jit(solution)/shard_map/ppermute | solution.py:304
  32.0 3.6 %collective-permute-done.12.refs_5_ = bf16[128,512]{1,0:T(8,128)(2,1)S(1)} collective-permute-done((bf16[128,512]{1,0:T(8,128)(2,1)S(1)}, bf16[128,512]{1,0:T(8,128)(2,1)S(1)}, u32[]{:S(2)}, u32[]{:S(2)}) %collective-permute-start.12) | collective-permute-done | bytes 131104 | tf_op jit(solution)/shard_map/ppermute | solution.py:304
  35.6 1.0 %finish.1 = (f32[128,512]{1,0:T(8,128)}, f32[128,512]{1,0:T(8,128)}) custom-call(bf16[128,512]{1,0:T(8,128)(2,1)S(1)} %copy-done.2, bf16[128,512]{1,0:T(8,128)(2,1)S(1)} %copy-done.1, f32[128,512]{1,0:T(8,128)S(1)} %add_far.1.refs_0_, bf16[128,512]{1,0:T(8,128)(2,1)S(1)} %collective-permute-done.8.refs_1_, ...), custom_call_target="tpu_custom_call" | custom-call | flops 4587520 | bytes 1376256 | tf_op jit(solution)/shard_map/finish/pallas_call | solution.py:254
  (20 shorter events, 0.9 us)
Async XLA Ops:
  0.6 10.7 %collective-permute-start = (bf16[128,512]{1,0:T(8,128)(2,1)}, bf16[128,512]{1,0:T(8,128)(2,1)S(1)}, u32[]{:S(2)}, u32[]{:S(2)}) collective-permute-start(bf16[128,512]{1,0:T(8,128)(2,1)} %image_ref.1), channel_id=1, source_target_pairs={{0,8},{1,9},{2,10},{3,11},{4,12},{5,13},{6,14},{7,15},{8,0},{9,1},... | collective-permute-start | bytes 393224 | tf_op jit(solution)/shard_map/ppermute | solution.py:304
  4.7 8.4 %collective-permute-start.1 = (bf16[128,512]{1,0:T(8,128)(2,1)}, bf16[128,512]{1,0:T(8,128)(2,1)S(1)}, u32[]{:S(2)}, u32[]{:S(2)}) collective-permute-start(bf16[128,512]{1,0:T(8,128)(2,1)} %text_ref.1), channel_id=1, source_target_pairs={{0,1},{1,0},{2,3},{3,2},{4,5},{5,4},{6,7},{7,6},{8,9},{9,8},{10,11... | collective-permute-start | bytes 393224 | tf_op jit(solution)/shard_map/ppermute | solution.py:304
  6.2 8.0 %collective-permute-start.2 = (bf16[128,512]{1,0:T(8,128)(2,1)}, bf16[128,512]{1,0:T(8,128)(2,1)S(1)}, u32[]{:S(2)}, u32[]{:S(2)}) collective-permute-start(bf16[128,512]{1,0:T(8,128)(2,1)} %text_ref.1), channel_id=1, source_target_pairs={{0,2},{1,3},{2,0},{3,1},{4,6},{5,7},{6,4},{7,5},{8,10},{9,11},{10,... | collective-permute-start | bytes 393224 | tf_op jit(solution)/shard_map/ppermute | solution.py:304
  7.7 6.5 %collective-permute-start.3 = (bf16[128,512]{1,0:T(8,128)(2,1)}, bf16[128,512]{1,0:T(8,128)(2,1)S(1)}, u32[]{:S(2)}, u32[]{:S(2)}) collective-permute-start(bf16[128,512]{1,0:T(8,128)(2,1)} %text_ref.1), channel_id=1, source_target_pairs={{0,3},{1,2},{2,1},{3,0},{4,7},{5,6},{6,5},{7,4},{8,11},{9,10},{10,... | collective-permute-start | bytes 393224 | tf_op jit(solution)/shard_map/ppermute | solution.py:304
  8.2 6.6 %collective-permute-start.4 = (bf16[128,512]{1,0:T(8,128)(2,1)}, bf16[128,512]{1,0:T(8,128)(2,1)S(1)}, u32[]{:S(2)}, u32[]{:S(2)}) collective-permute-start(bf16[128,512]{1,0:T(8,128)(2,1)} %image_ref.1), channel_id=1, source_target_pairs={{0,4},{1,5},{2,6},{3,7},{4,0},{5,1},{6,2},{7,3},{8,12},{9,13},{10,... | collective-permute-start | bytes 393224 | tf_op jit(solution)/shard_map/ppermute | solution.py:304
  11.4 5.5 %collective-permute-start.5 = (bf16[128,512]{1,0:T(8,128)(2,1)S(1)}, bf16[128,512]{1,0:T(8,128)(2,1)S(1)}, u32[]{:S(2)}, u32[]{:S(2)}) collective-permute-start(bf16[128,512]{1,0:T(8,128)(2,1)S(1)} %collective-permute-done.refs_1_), channel_id=1, source_target_pairs={{0,4},{1,5},{2,6},{3,7},{4,0},{5,1},{6,2},{7,3},{8,12},{9,13},{10,... | collective-permute-start | bytes 393224 | tf_op jit(solution)/shard_map/ppermute | solution.py:304
  12.1 0.9 %copy-start = (bf16[128,512]{1,0:T(8,128)(2,1)S(1)}, bf16[128,512]{1,0:T(8,128)(2,1)}, u32[]{:S(2)}) copy-start(bf16[128,512]{1,0:T(8,128)(2,1)} %text_ref.1) | copy-start | bytes 393220
  13.1 1.7 %copy-start.2 = (bf16[128,512]{1,0:T(8,128)(2,1)S(1)}, bf16[128,512]{1,0:T(8,128)(2,1)}, u32[]{:S(2)}) copy-start(bf16[128,512]{1,0:T(8,128)(2,1)} %image_ref.1) | copy-start | bytes 393220
  14.4 2.6 %collective-permute-start.6 = (bf16[512,512]{1,0:T(8,128)(2,1)S(1)}, bf16[512,512]{1,0:T(8,128)(2,1)S(1)}, u32[]{:S(2)}, u32[]{:S(2)}) collective-permute-start(bf16[512,512]{1,0:T(8,128)(2,1)S(1)} %stack_units.1.text_ref.refs_0_), channel_id=1, source_target_pairs={{0,16},{1,17},{2,18},{3,19},{4,20},{5,21},{6,22},{7,23},{8,24},{9,... | collective-permute-start | bytes 1572872 | tf_op jit(solution)/shard_map/ppermute | solution.py:304
  18.1 6.6 %collective-permute-start.7 = (bf16[128,512]{1,0:T(8,128)(2,1)S(1)}, bf16[128,512]{1,0:T(8,128)(2,1)S(1)}, u32[]{:S(2)}, u32[]{:S(2)}) collective-permute-start(bf16[128,512]{1,0:T(8,128)(2,1)S(1)} %get-tuple-element.28), channel_id=1, source_target_pairs={{0,4},{1,5},{2,6},{3,7},{4,0},{5,1},{6,2},{7,3},{8,12},{9,13},{10,... | collective-permute-start | bytes 393224 | tf_op jit(solution)/shard_map/ppermute | solution.py:304
  19.1 12.9 %collective-permute-start.8 = (bf16[128,512]{1,0:T(8,128)(2,1)S(1)}, bf16[128,512]{1,0:T(8,128)(2,1)S(1)}, u32[]{:S(2)}, u32[]{:S(2)}) collective-permute-start(bf16[128,512]{1,0:T(8,128)(2,1)S(1)} %get-tuple-element.34), channel_id=1, source_target_pairs={{0,8},{1,9},{2,10},{3,11},{4,12},{5,13},{6,14},{7,15},{8,0},{9,1},... | collective-permute-start | bytes 393224 | tf_op jit(solution)/shard_map/ppermute | solution.py:304
  23.3 8.6 %collective-permute-start.9 = (bf16[128,512]{1,0:T(8,128)(2,1)S(1)}, bf16[128,512]{1,0:T(8,128)(2,1)S(1)}, u32[]{:S(2)}, u32[]{:S(2)}) collective-permute-start(bf16[128,512]{1,0:T(8,128)(2,1)S(1)} %get-tuple-element.35), channel_id=1, source_target_pairs={{0,12},{1,13},{2,14},{3,15},{4,8},{5,9},{6,10},{7,11},{8,4},{9,5},... | collective-permute-start | bytes 393224 | tf_op jit(solution)/shard_map/ppermute | solution.py:304
  23.9 1.9 %collective-permute-start.10 = (bf16[512,512]{1,0:T(8,128)(2,1)S(1)}, bf16[512,512]{1,0:T(8,128)(2,1)S(1)}, u32[]{:S(2)}, u32[]{:S(2)}) collective-permute-start(bf16[512,512]{1,0:T(8,128)(2,1)S(1)} %get-tuple-element.37), channel_id=1, source_target_pairs={{0,16},{1,17},{2,18},{3,19},{4,20},{5,21},{6,22},{7,23},{8,24},{9,... | collective-permute-start | bytes 1572872 | tf_op jit(solution)/shard_map/ppermute | solution.py:304
  24.8 10.8 %copy-start.1 = (bf16[128,512]{1,0:T(8,128)(2,1)S(1)}, bf16[128,512]{1,0:T(8,128)(2,1)}, u32[]{:S(2)}) copy-start(bf16[128,512]{1,0:T(8,128)(2,1)} %text_ref.1) | copy-start | bytes 393220
  25.9 6.1 %collective-permute-start.11 = (bf16[128,512]{1,0:T(8,128)(2,1)S(1)}, bf16[128,512]{1,0:T(8,128)(2,1)S(1)}, u32[]{:S(2)}, u32[]{:S(2)}) collective-permute-start(bf16[128,512]{1,0:T(8,128)(2,1)S(1)} %get-tuple-element.39), channel_id=1, source_target_pairs={{0,1},{1,0},{2,3},{3,2},{4,5},{5,4},{6,7},{7,6},{8,9},{9,8},{10,11... | collective-permute-start | bytes 393224 | tf_op jit(solution)/shard_map/ppermute | solution.py:304
  27.5 8.1 %collective-permute-start.12 = (bf16[128,512]{1,0:T(8,128)(2,1)S(1)}, bf16[128,512]{1,0:T(8,128)(2,1)S(1)}, u32[]{:S(2)}, u32[]{:S(2)}) collective-permute-start(bf16[128,512]{1,0:T(8,128)(2,1)S(1)} %get-tuple-element.40), channel_id=1, source_target_pairs={{0,2},{1,3},{2,0},{3,1},{4,6},{5,7},{6,4},{7,5},{8,10},{9,11},{10,... | collective-permute-start | bytes 393224 | tf_op jit(solution)/shard_map/ppermute | solution.py:304
  29.0 6.6 %collective-permute-start.13 = (bf16[128,512]{1,0:T(8,128)(2,1)S(1)}, bf16[128,512]{1,0:T(8,128)(2,1)S(1)}, u32[]{:S(2)}, u32[]{:S(2)}) collective-permute-start(bf16[128,512]{1,0:T(8,128)(2,1)S(1)} %get-tuple-element.41), channel_id=1, source_target_pairs={{0,3},{1,2},{2,1},{3,0},{4,7},{5,6},{6,5},{7,4},{8,11},{9,10},{10,... | collective-permute-start | bytes 393224 | tf_op jit(solution)/shard_map/ppermute | solution.py:304

commit v23 on v22

--- a/solution.py
+++ b/solution.py
@@ -13,7 +13,7 @@
 SPAN = 256
 PIECE = 32
 LATE = 16500
-FAR = 60000
+FAR = 37000
 LOG2_E = math.log2(math.e)
 VMEM = pl.BlockSpec(memory_space=pltpu.VMEM)
 
@@ -325,6 +325,12 @@
         )
         far_parts = dict(zip([*early, *late], [*early_parts, *late_parts]))
 
+        held = [step for step in early if step[0]]
+        kept, text_parts = lax.optimization_barrier(
+            ([far_parts[step] for step in held], list(text_parts))
+        )
+        far_parts.update(zip(held, kept))
+
         def give_back(h, w):
             return move(far_parts[h, w], high=-h, low=-w)
 

time: 36.8 us -> 34.8 us (0.946)
  waiting for transfers between devices: 10.5 us -> 8.37 us
    ppermute x14, waiting for transfers between devices: 10.5 us -> 8.37 us  [move(): return lax.ppermute(value, AXES, perm)]
  transfers between devices with their start and end apart: 14 -> 14, of which waited for: 8 -> 6; matrix products, arithmetic and copies ran while one was open for 0% -> 0% of each run, Pallas kernels for 8% -> 8%
where the time goes in v23:
time: 34.8 us; the launch traced here: 34.6 us
  starting transfers between devices  18.1 us (52%)
  waiting for transfers between devices  8.37 us (24%)
  Pallas kernels  5.03 us (14%)
  between operations  2.04 us (6%)
  local copies, waits for them, and re-layouts  0.92 us (3%)
    ppermute x14, starting transfers between devices, move(): return lax.ppermute(value, AXES, perm)  18.1 us
    ppermute x14, waiting for transfers between devices, move(): return lax.ppermute(value, AXES, perm)  8.37 us
    pallas_call x8, Pallas kernels, call(): pl.pallas_call(kernel, out_shape=out_shape, in_specs=[VMEM] * len(operand...  3.99 us
    pallas_call x1, Pallas kernels, finish(): pl.pallas_call(functools.partial(finish_kernel, [side for side, _ in part...  1.05 us
    unnamed x6, local copies, waits for them, and re-layouts  0.92 us
  transfers between devices with their start and end apart: 14, of which 6 were waited for; matrix products, arithmetic and copies ran while one was open for 0% of the time, Pallas kernels for 8%

profile of v23, /device:TPU:0, one launch (start us, length us, event | category | flops | bytes accessed | tf_op | source)
XLA Modules:
  0.0 34.6 jit_solution(10064489230421687639)
XLA Ops:
  0.6 4.1 %collective-permute-start = (bf16[128,512]{1,0:T(8,128)(2,1)}, bf16[128,512]{1,0:T(8,128)(2,1)S(1)}, u32[]{:S(2)}, u32[]{:S(2)}) collective-permute-start(bf16[128,512]{1,0:T(8,128)(2,1)} %image_ref.1), channel_id=1, source_target_pairs={{0,8},{1,9},{2,10},{3,11},{4,12},{5,13},{6,14},{7,15},{8,0},{9,1},... | collective-permute-start | bytes 393224 | tf_op jit(solution)/shard_map/ppermute | solution.py:304
  4.7 1.5 %collective-permute-start.1 = (bf16[128,512]{1,0:T(8,128)(2,1)}, bf16[128,512]{1,0:T(8,128)(2,1)S(1)}, u32[]{:S(2)}, u32[]{:S(2)}) collective-permute-start(bf16[128,512]{1,0:T(8,128)(2,1)} %text_ref.1), channel_id=1, source_target_pairs={{0,1},{1,0},{2,3},{3,2},{4,5},{5,4},{6,7},{7,6},{8,9},{9,8},{10,11... | collective-permute-start | bytes 393224 | tf_op jit(solution)/shard_map/ppermute | solution.py:304
  6.2 1.5 %collective-permute-start.2 = (bf16[128,512]{1,0:T(8,128)(2,1)}, bf16[128,512]{1,0:T(8,128)(2,1)S(1)}, u32[]{:S(2)}, u32[]{:S(2)}) collective-permute-start(bf16[128,512]{1,0:T(8,128)(2,1)} %text_ref.1), channel_id=1, source_target_pairs={{0,2},{1,3},{2,0},{3,1},{4,6},{5,7},{6,4},{7,5},{8,10},{9,11},{10,... | collective-permute-start | bytes 393224 | tf_op jit(solution)/shard_map/ppermute | solution.py:304
  7.7 0.5 %collective-permute-start.3 = (bf16[128,512]{1,0:T(8,128)(2,1)}, bf16[128,512]{1,0:T(8,128)(2,1)S(1)}, u32[]{:S(2)}, u32[]{:S(2)}) collective-permute-start(bf16[128,512]{1,0:T(8,128)(2,1)} %text_ref.1), channel_id=1, source_target_pairs={{0,3},{1,2},{2,1},{3,0},{4,7},{5,6},{6,5},{7,4},{8,11},{9,10},{10,... | collective-permute-start | bytes 393224 | tf_op jit(solution)/shard_map/ppermute | solution.py:304
  8.2 1.6 %collective-permute-start.4 = (bf16[128,512]{1,0:T(8,128)(2,1)}, bf16[128,512]{1,0:T(8,128)(2,1)S(1)}, u32[]{:S(2)}, u32[]{:S(2)}) collective-permute-start(bf16[128,512]{1,0:T(8,128)(2,1)} %image_ref.1), channel_id=1, source_target_pairs={{0,4},{1,5},{2,6},{3,7},{4,0},{5,1},{6,2},{7,3},{8,12},{9,13},{10,... | collective-permute-start | bytes 393224 | tf_op jit(solution)/shard_map/ppermute | solution.py:304
  11.2 0.2 collective-permute-done.refs_1_
  11.4 0.8 %collective-permute-start.5 = (bf16[128,512]{1,0:T(8,128)(2,1)S(1)}, bf16[128,512]{1,0:T(8,128)(2,1)S(1)}, u32[]{:S(2)}, u32[]{:S(2)}) collective-permute-start(bf16[128,512]{1,0:T(8,128)(2,1)S(1)} %collective-permute-done.refs_1_), channel_id=1, source_target_pairs={{0,4},{1,5},{2,6},{3,7},{4,0},{5,1},{6,2},{7,3},{8,12},{9,13},{10,... | collective-permute-start | bytes 393224 | tf_op jit(solution)/shard_map/ppermute | solution.py:304
  12.1 0.9 %copy-done = bf16[128,512]{1,0:T(8,128)(2,1)S(1)} copy-done((bf16[128,512]{1,0:T(8,128)(2,1)S(1)}, bf16[128,512]{1,0:T(8,128)(2,1)}, u32[]{:S(2)}) %copy-start) | copy-done | bytes 131096
  13.2 1.0 %collective-permute-done.2.refs_2_ = bf16[128,512]{1,0:T(8,128)(2,1)S(1)} collective-permute-done((bf16[128,512]{1,0:T(8,128)(2,1)}, bf16[128,512]{1,0:T(8,128)(2,1)S(1)}, u32[]{:S(2)}, u32[]{:S(2)}) %collective-permute-start.2) | collective-permute-done | bytes 131104 | tf_op jit(solution)/shard_map/ppermute | solution.py:304
  14.2 0.2 stack_units.1.text_ref.refs_0_
  14.5 0.4 %collective-permute-done.4.refs_2_ = bf16[128,512]{1,0:T(8,128)(2,1)S(1)} collective-permute-done((bf16[128,512]{1,0:T(8,128)(2,1)}, bf16[128,512]{1,0:T(8,128)(2,1)S(1)}, u32[]{:S(2)}, u32[]{:S(2)}) %collective-permute-start.4) | collective-permute-done | bytes 131104 | tf_op jit(solution)/shard_map/ppermute | solution.py:304
  14.9 1.1 %early_pairs.1 = (f32[512,512]{1,0:T(8,128)S(1)}, bf16[384,512]{1,0:T(8,128)(2,1)S(1)}, f32[384,512]{1,0:T(8,128)S(1)}) custom-call(f32[1,3]{1,0:T(1,128)S(1)} %maximum_bitcast_fusion.params_ref, bf16[512,512]{1,0:T(8,128)(2,1)S(1)} %stack_units.1.text_ref.refs_0_, bf16[128,512]{1,0:T(8,128)(2,1)S(1)} %copy-done.2, ...), custom_call_target="tpu_custom_call" | custom-call | flops 603979776 | bytes 3145740 | tf_op jit(solution)/shard_map/early_pairs/pallas_call | solution.py:29
  16.0 0.9 %collective-permute-done.5.refs_0_ = bf16[128,512]{1,0:T(8,128)(2,1)S(1)} collective-permute-done((bf16[128,512]{1,0:T(8,128)(2,1)S(1)}, bf16[128,512]{1,0:T(8,128)(2,1)S(1)}, u32[]{:S(2)}, u32[]{:S(2)}) %collective-permute-start.5) | collective-permute-done | bytes 131104 | tf_op jit(solution)/shard_map/ppermute | solution.py:304
  17.0 1.1 %early_rest.1 = (f32[512,512]{1,0:T(8,128)S(1)}, f32[128,512]{1,0:T(8,128)S(1)}, bf16[128,512]{1,0:T(8,128)(2,1)S(1)}, bf16[128,512]{1,0:T(8,128)(2,1)S(1)}) custom-call(f32[1,3]{1,0:T(1,128)S(1)} %maximum_bitcast_fusion.params_ref, bf16[384,512]{1,0:T(8,128)(2,1)S(1)} %get-tuple-element.26.units_ref, f32[384,512]{1,0:T(8,128)S(1)} %get-tuple-element.29.total_ref, ...), custom_call_target="tpu_custom_call" | custom-call | flops 603979776 | bytes 3276812 | tf_op jit(solution)/shard_map/early_rest/pallas_call | solution.py:29
  18.1 1.0 %collective-permute-start.7 = (bf16[128,512]{1,0:T(8,128)(2,1)S(1)}, bf16[128,512]{1,0:T(8,128)(2,1)S(1)}, u32[]{:S(2)}, u32[]{:S(2)}) collective-permute-start(bf16[128,512]{1,0:T(8,128)(2,1)S(1)} %get-tuple-element.31), channel_id=1, source_target_pairs={{0,4},{1,5},{2,6},{3,7},{4,0},{5,1},{6,2},{7,3},{8,12},{9,13},{10,... | collective-permute-start | bytes 393224 | tf_op jit(solution)/shard_map/ppermute | solution.py:304
  19.1 1.2 %late_pairs.1 = (f32[512,512]{1,0:T(8,128)S(1)}, bf16[512,512]{1,0:T(8,128)(2,1)S(1)}, bf16[128,512]{1,0:T(8,128)(2,1)S(1)}) custom-call(f32[1,3]{1,0:T(1,128)S(1)} %maximum_bitcast_fusion.params_ref, bf16[128,512]{1,0:T(8,128)(2,1)S(1)} %late_units.1.units_ref, bf16[512,512]{1,0:T(8,128)(2,1)S(1)} %stack_units.1.text_ref.refs_0_, ...), custom_call_target="tpu_custom_call" | custom-call | flops 402653184 | bytes 4980748 | tf_op jit(solution)/shard_map/late_pairs/pallas_call | solution.py:29
  20.4 3.1 %collective-permute-start.8 = (bf16[128,512]{1,0:T(8,128)(2,1)S(1)}, bf16[128,512]{1,0:T(8,128)(2,1)S(1)}, u32[]{:S(2)}, u32[]{:S(2)}) collective-permute-start(bf16[128,512]{1,0:T(8,128)(2,1)S(1)} %get-tuple-element.40), channel_id=1, source_target_pairs={{0,8},{1,9},{2,10},{3,11},{4,12},{5,13},{6,14},{7,15},{8,0},{9,1},... | collective-permute-start | bytes 393224 | tf_op jit(solution)/shard_map/ppermute | solution.py:304
  23.5 0.5 %collective-permute-start.9 = (bf16[128,512]{1,0:T(8,128)(2,1)S(1)}, bf16[128,512]{1,0:T(8,128)(2,1)S(1)}, u32[]{:S(2)}, u32[]{:S(2)}) collective-permute-start(bf16[128,512]{1,0:T(8,128)(2,1)S(1)} %get-tuple-element.41), channel_id=1, source_target_pairs={{0,12},{1,13},{2,14},{3,15},{4,8},{5,9},{6,10},{7,11},{8,4},{9,5},... | collective-permute-start | bytes 393224 | tf_op jit(solution)/shard_map/ppermute | solution.py:304
  24.0 0.1 add_stacks.1
  24.1 1.6 %collective-permute-start.11 = (bf16[128,512]{1,0:T(8,128)(2,1)S(1)}, bf16[128,512]{1,0:T(8,128)(2,1)S(1)}, u32[]{:S(2)}, u32[]{:S(2)}) collective-permute-start(bf16[128,512]{1,0:T(8,128)(2,1)S(1)} %get-tuple-element.45), channel_id=1, source_target_pairs={{0,1},{1,0},{2,3},{3,2},{4,5},{5,4},{6,7},{7,6},{8,9},{9,8},{10,11... | collective-permute-start | bytes 393224 | tf_op jit(solution)/shard_map/ppermute | solution.py:304
  25.7 1.5 %collective-permute-start.12 = (bf16[128,512]{1,0:T(8,128)(2,1)S(1)}, bf16[128,512]{1,0:T(8,128)(2,1)S(1)}, u32[]{:S(2)}, u32[]{:S(2)}) collective-permute-start(bf16[128,512]{1,0:T(8,128)(2,1)S(1)} %get-tuple-element.46), channel_id=1, source_target_pairs={{0,2},{1,3},{2,0},{3,1},{4,6},{5,7},{6,4},{7,5},{8,10},{9,11},{10,... | collective-permute-start | bytes 393224 | tf_op jit(solution)/shard_map/ppermute | solution.py:304
  27.2 0.4 %collective-permute-start.13 = (bf16[128,512]{1,0:T(8,128)(2,1)S(1)}, bf16[128,512]{1,0:T(8,128)(2,1)S(1)}, u32[]{:S(2)}, u32[]{:S(2)}) collective-permute-start(bf16[128,512]{1,0:T(8,128)(2,1)S(1)} %get-tuple-element.47), channel_id=1, source_target_pairs={{0,3},{1,2},{2,1},{3,0},{4,7},{5,6},{6,5},{7,4},{8,11},{9,10},{10,... | collective-permute-start | bytes 393224 | tf_op jit(solution)/shard_map/ppermute | solution.py:304
  27.7 5.8 %collective-permute-done.8.refs_1_ = bf16[128,512]{1,0:T(8,128)(2,1)S(1)} collective-permute-done((bf16[128,512]{1,0:T(8,128)(2,1)S(1)}, bf16[128,512]{1,0:T(8,128)(2,1)S(1)}, u32[]{:S(2)}, u32[]{:S(2)}) %collective-permute-start.8) | collective-permute-done | bytes 131104 | tf_op jit(solution)/shard_map/ppermute | solution.py:304
  33.5 1.0 %finish.1 = (f32[128,512]{1,0:T(8,128)}, f32[128,512]{1,0:T(8,128)}) custom-call(bf16[128,512]{1,0:T(8,128)(2,1)S(1)} %copy-done.2, bf16[128,512]{1,0:T(8,128)(2,1)S(1)} %copy-done.1, f32[128,512]{1,0:T(8,128)S(1)} %add_far.1.refs_0_, bf16[128,512]{1,0:T(8,128)(2,1)S(1)} %collective-permute-done.8.refs_1_, ...), custom_call_target="tpu_custom_call" | custom-call | flops 4587520 | bytes 1376256 | tf_op jit(solution)/shard_map/finish/pallas_call | solution.py:254
  (20 shorter events, 0.6 us)
Async XLA Ops:
  0.6 10.7 %collective-permute-start = (bf16[128,512]{1,0:T(8,128)(2,1)}, bf16[128,512]{1,0:T(8,128)(2,1)S(1)}, u32[]{:S(2)}, u32[]{:S(2)}) collective-permute-start(bf16[128,512]{1,0:T(8,128)(2,1)} %image_ref.1), channel_id=1, source_target_pairs={{0,8},{1,9},{2,10},{3,11},{4,12},{5,13},{6,14},{7,15},{8,0},{9,1},... | collective-permute-start | bytes 393224 | tf_op jit(solution)/shard_map/ppermute | solution.py:304
  4.7 8.4 %collective-permute-start.1 = (bf16[128,512]{1,0:T(8,128)(2,1)}, bf16[128,512]{1,0:T(8,128)(2,1)S(1)}, u32[]{:S(2)}, u32[]{:S(2)}) collective-permute-start(bf16[128,512]{1,0:T(8,128)(2,1)} %text_ref.1), channel_id=1, source_target_pairs={{0,1},{1,0},{2,3},{3,2},{4,5},{5,4},{6,7},{7,6},{8,9},{9,8},{10,11... | collective-permute-start | bytes 393224 | tf_op jit(solution)/shard_map/ppermute | solution.py:304
  6.2 8.0 %collective-permute-start.2 = (bf16[128,512]{1,0:T(8,128)(2,1)}, bf16[128,512]{1,0:T(8,128)(2,1)S(1)}, u32[]{:S(2)}, u32[]{:S(2)}) collective-permute-start(bf16[128,512]{1,0:T(8,128)(2,1)} %text_ref.1), channel_id=1, source_target_pairs={{0,2},{1,3},{2,0},{3,1},{4,6},{5,7},{6,4},{7,5},{8,10},{9,11},{10,... | collective-permute-start | bytes 393224 | tf_op jit(solution)/shard_map/ppermute | solution.py:304
  7.7 6.5 %collective-permute-start.3 = (bf16[128,512]{1,0:T(8,128)(2,1)}, bf16[128,512]{1,0:T(8,128)(2,1)S(1)}, u32[]{:S(2)}, u32[]{:S(2)}) collective-permute-start(bf16[128,512]{1,0:T(8,128)(2,1)} %text_ref.1), channel_id=1, source_target_pairs={{0,3},{1,2},{2,1},{3,0},{4,7},{5,6},{6,5},{7,4},{8,11},{9,10},{10,... | collective-permute-start | bytes 393224 | tf_op jit(solution)/shard_map/ppermute | solution.py:304
  8.2 6.6 %collective-permute-start.4 = (bf16[128,512]{1,0:T(8,128)(2,1)}, bf16[128,512]{1,0:T(8,128)(2,1)S(1)}, u32[]{:S(2)}, u32[]{:S(2)}) collective-permute-start(bf16[128,512]{1,0:T(8,128)(2,1)} %image_ref.1), channel_id=1, source_target_pairs={{0,4},{1,5},{2,6},{3,7},{4,0},{5,1},{6,2},{7,3},{8,12},{9,13},{10,... | collective-permute-start | bytes 393224 | tf_op jit(solution)/shard_map/ppermute | solution.py:304
  11.4 5.5 %collective-permute-start.5 = (bf16[128,512]{1,0:T(8,128)(2,1)S(1)}, bf16[128,512]{1,0:T(8,128)(2,1)S(1)}, u32[]{:S(2)}, u32[]{:S(2)}) collective-permute-start(bf16[128,512]{1,0:T(8,128)(2,1)S(1)} %collective-permute-done.refs_1_), channel_id=1, source_target_pairs={{0,4},{1,5},{2,6},{3,7},{4,0},{5,1},{6,2},{7,3},{8,12},{9,13},{10,... | collective-permute-start | bytes 393224 | tf_op jit(solution)/shard_map/ppermute | solution.py:304
  12.1 0.9 %copy-start = (bf16[128,512]{1,0:T(8,128)(2,1)S(1)}, bf16[128,512]{1,0:T(8,128)(2,1)}, u32[]{:S(2)}) copy-start(bf16[128,512]{1,0:T(8,128)(2,1)} %text_ref.1) | copy-start | bytes 393220
  13.1 1.7 %copy-start.2 = (bf16[128,512]{1,0:T(8,128)(2,1)S(1)}, bf16[128,512]{1,0:T(8,128)(2,1)}, u32[]{:S(2)}) copy-start(bf16[128,512]{1,0:T(8,128)(2,1)} %image_ref.1) | copy-start | bytes 393220
  14.4 2.6 %collective-permute-start.6 = (bf16[512,512]{1,0:T(8,128)(2,1)S(1)}, bf16[512,512]{1,0:T(8,128)(2,1)S(1)}, u32[]{:S(2)}, u32[]{:S(2)}) collective-permute-start(bf16[512,512]{1,0:T(8,128)(2,1)S(1)} %stack_units.1.text_ref.refs_0_), channel_id=1, source_target_pairs={{0,16},{1,17},{2,18},{3,19},{4,20},{5,21},{6,22},{7,23},{8,24},{9,... | collective-permute-start | bytes 1572872 | tf_op jit(solution)/shard_map/ppermute | solution.py:304
  18.1 5.8 %collective-permute-start.7 = (bf16[128,512]{1,0:T(8,128)(2,1)S(1)}, bf16[128,512]{1,0:T(8,128)(2,1)S(1)}, u32[]{:S(2)}, u32[]{:S(2)}) collective-permute-start(bf16[128,512]{1,0:T(8,128)(2,1)S(1)} %get-tuple-element.31), channel_id=1, source_target_pairs={{0,4},{1,5},{2,6},{3,7},{4,0},{5,1},{6,2},{7,3},{8,12},{9,13},{10,... | collective-permute-start | bytes 393224 | tf_op jit(solution)/shard_map/ppermute | solution.py:304
  20.3 3.7 %collective-permute-start.10 = (bf16[512,512]{1,0:T(8,128)(2,1)S(1)}, bf16[512,512]{1,0:T(8,128)(2,1)S(1)}, u32[]{:S(2)}, u32[]{:S(2)}) collective-permute-start(bf16[512,512]{1,0:T(8,128)(2,1)S(1)} %get-tuple-element.43), channel_id=1, source_target_pairs={{0,16},{1,17},{2,18},{3,19},{4,20},{5,21},{6,22},{7,23},{8,24},{9,... | collective-permute-start | bytes 1572872 | tf_op jit(solution)/shard_map/ppermute | solution.py:304
  20.4 13.0 %collective-permute-start.8 = (bf16[128,512]{1,0:T(8,128)(2,1)S(1)}, bf16[128,512]{1,0:T(8,128)(2,1)S(1)}, u32[]{:S(2)}, u32[]{:S(2)}) collective-permute-start(bf16[128,512]{1,0:T(8,128)(2,1)S(1)} %get-tuple-element.40), channel_id=1, source_target_pairs={{0,8},{1,9},{2,10},{3,11},{4,12},{5,13},{6,14},{7,15},{8,0},{9,1},... | collective-permute-start | bytes 393224 | tf_op jit(solution)/shard_map/ppermute | solution.py:304
  23.5 10.0 %collective-permute-start.9 = (bf16[128,512]{1,0:T(8,128)(2,1)S(1)}, bf16[128,512]{1,0:T(8,128)(2,1)S(1)}, u32[]{:S(2)}, u32[]{:S(2)}) collective-permute-start(bf16[128,512]{1,0:T(8,128)(2,1)S(1)} %get-tuple-element.41), channel_id=1, source_target_pairs={{0,12},{1,13},{2,14},{3,15},{4,8},{5,9},{6,10},{7,11},{8,4},{9,5},... | collective-permute-start | bytes 393224 | tf_op jit(solution)/shard_map/ppermute | solution.py:304
  24.0 9.6 %copy-start.1 = (bf16[128,512]{1,0:T(8,128)(2,1)S(1)}, bf16[128,512]{1,0:T(8,128)(2,1)}, u32[]{:S(2)}) copy-start(bf16[128,512]{1,0:T(8,128)(2,1)} %text_ref.1) | copy-start | bytes 393220
  24.1 9.3 %collective-permute-start.11 = (bf16[128,512]{1,0:T(8,128)(2,1)S(1)}, bf16[128,512]{1,0:T(8,128)(2,1)S(1)}, u32[]{:S(2)}, u32[]{:S(2)}) collective-permute-start(bf16[128,512]{1,0:T(8,128)(2,1)S(1)} %get-tuple-element.45), channel_id=1, source_target_pairs={{0,1},{1,0},{2,3},{3,2},{4,5},{5,4},{6,7},{7,6},{8,9},{9,8},{10,11... | collective-permute-start | bytes 393224 | tf_op jit(solution)/shard_map/ppermute | solution.py:304
  25.7 7.8 %collective-permute-start.12 = (bf16[128,512]{1,0:T(8,128)(2,1)S(1)}, bf16[128,512]{1,0:T(8,128)(2,1)S(1)}, u32[]{:S(2)}, u32[]{:S(2)}) collective-permute-start(bf16[128,512]{1,0:T(8,128)(2,1)S(1)} %get-tuple-element.46), channel_id=1, source_target_pairs={{0,2},{1,3},{2,0},{3,1},{4,6},{5,7},{6,4},{7,5},{8,10},{9,11},{10,... | collective-permute-start | bytes 393224 | tf_op jit(solution)/shard_map/ppermute | solution.py:304
  27.2 6.3 %collective-permute-start.13 = (bf16[128,512]{1,0:T(8,128)(2,1)S(1)}, bf16[128,512]{1,0:T(8,128)(2,1)S(1)}, u32[]{:S(2)}, u32[]{:S(2)}) collective-permute-start(bf16[128,512]{1,0:T(8,128)(2,1)S(1)} %get-tuple-element.47), channel_id=1, source_target_pairs={{0,3},{1,2},{2,1},{3,0},{4,7},{5,6},{6,5},{7,4},{8,11},{9,10},{10,... | collective-permute-start | bytes 393224 | tf_op jit(solution)/shard_map/ppermute | solution.py:304

commit v24 on v22

--- a/solution.py
+++ b/solution.py
@@ -13,7 +13,7 @@
 SPAN = 256
 PIECE = 32
 LATE = 16500
-FAR = 60000
+PASSED = 37000
 LOG2_E = math.log2(math.e)
 VMEM = pl.BlockSpec(memory_space=pltpu.VMEM)
 
@@ -183,7 +183,9 @@
     other_adds, early_parts = outs[:len(others)], outs[len(others):]
     outs = call(
         functools.partial(late_pairs_kernel, len(texts)),
-        text_sums([own], jnp.float32) + text_sums(others, jnp.bfloat16) + [part] * len(late),
+        text_sums([own], jnp.float32)
+        + text_sums(others, jnp.bfloat16)
+        + [jax.ShapeDtypeStruct((rows, width), jnp.float32)] * len(late),
         [params, late_units, *texts, own_add, *other_adds],
         name="late_pairs",
         **cost(late_rows * (own.shape[0] + other_rows)),
@@ -213,14 +215,15 @@
     )
 
 
-def add_far_kernel(*refs):
-    refs[-1][...] = sum(ref[...].astype(jnp.float32) for ref in refs[:-1])
-
-
-def add_far(parts):
-    out = jax.ShapeDtypeStruct(parts[0].shape, jnp.float32)
+def add_parts_kernel(*refs):
+    total = sum(ref[...].astype(jnp.float32) for ref in refs[:-1])
+    refs[-1][...] = total.astype(refs[-1].dtype)
+
+
+def add_parts(parts, dtype, name, weight=1):
+    out = jax.ShapeDtypeStruct(parts[0].shape, dtype)
     return call(
-        add_far_kernel, [out], parts, flops=FAR * len(parts) * out.size, name="add_far"
+        add_parts_kernel, [out], parts, flops=weight * len(parts) * out.size, name=name
     )[0]
 
 
@@ -328,20 +331,25 @@
         def give_back(h, w):
             return move(far_parts[h, w], high=-h, low=-w)
 
+        if low_count > 1:
+            for h, w in late:
+                passed = move(far_parts[h, 0], low=w)
+                far_parts[h, w] = add_parts([far_parts[h, w], passed], jnp.bfloat16, "add_passed", PASSED)
+            far_came = [give_back(h, w) for h, w in late]
+        else:
+            far_came = [give_back(h, w) for h, w in early if h]
         came = [move(part, grp=-g) for g, part in enumerate(text_parts) if g]
-        far_sum = add_far(
-            [far_parts[0, 0]] + [give_back(h, w) for h, w in early if w]
-        )
-        far_sum, own_text = lax.optimization_barrier((far_sum, text_parts[0]))
-        far_came = [give_back(h, w) for h, w in far_parts if h]
-        near_parts = add_stacks([own_text, *came], near_count)
+        low_came = [give_back(h, w) for h, w in early if w]
+        near_parts = add_stacks([text_parts[0], *came], near_count)
         near_parts = [near_parts[0]] + [
             move(part, near=-n) for n, part in enumerate(near_parts) if n
         ]
         return finish(
             images,
             texts,
-            [(0, part) for part in [far_sum] + far_came] + [(1, part) for part in near_parts],
+            [(0, part) for part in [far_parts[0, 0]] + far_came]
+            + [(1, part) for part in near_parts]
+            + [(0, part) for part in low_came],
         )
 
     in_specs = (P(AXES, None), P(AXES, None), P(), P())

time: 36.8 us -> 37.2 us (1.011)
  starting transfers between devices: 18.1 us -> 19.5 us
  waiting for transfers between devices: 10.5 us -> 9.47 us
    ppermute x14, starting transfers between devices: 18.1 us -> 19.5 us  [move(): return lax.ppermute(value, AXES, perm)]
    ppermute x14, waiting for transfers between devices: 10.5 us -> 9.47 us  [move(): return lax.ppermute(value, AXES, perm)]
  transfers between devices with their start and end apart: 14 -> 14, of which waited for: 8 -> 9; matrix products, arithmetic and copies ran while one was open for 0% -> 0% of each run, Pallas kernels for 8% -> 8%
where the time goes in v24:
time: 37.2 us; the launch traced here: 37 us
  starting transfers between devices  19.5 us (52%)
  waiting for transfers between devices  9.47 us (25%)
  Pallas kernels  5.03 us (14%)
  between operations  2.03 us (5%)
  local copies, waits for them, and re-layouts  0.91 us (2%)
    ppermute x14, starting transfers between devices, move(): return lax.ppermute(value, AXES, perm)  19.5 us
    ppermute x14, waiting for transfers between devices, move(): return lax.ppermute(value, AXES, perm)  9.47 us
    pallas_call x8, Pallas kernels, call(): pl.pallas_call(kernel, out_shape=out_shape, in_specs=[VMEM] * len(operand...  3.99 us
    pallas_call x1, Pallas kernels, finish(): pl.pallas_call(functools.partial(finish_kernel, [side for side, _ in part...  1.04 us
    unnamed x6, local copies, waits for them, and re-layouts  0.91 us
  transfers between devices with their start and end apart: 14, of which 9 were waited for; matrix products, arithmetic and copies ran while one was open for 0% of the time, Pallas kernels for 8%

profile of v24, /device:TPU:0, one launch (start us, length us, event | category | flops | bytes accessed | tf_op | source)
XLA Modules:
  0.0 37.0 jit_solution(10020191855925544643)
XLA Ops:
  0.6 4.1 %collective-permute-start = (bf16[128,512]{1,0:T(8,128)(2,1)}, bf16[128,512]{1,0:T(8,128)(2,1)S(1)}, u32[]{:S(2)}, u32[]{:S(2)}) collective-permute-start(bf16[128,512]{1,0:T(8,128)(2,1)} %image_ref.1), channel_id=1, source_target_pairs={{0,8},{1,9},{2,10},{3,11},{4,12},{5,13},{6,14},{7,15},{8,0},{9,1},... | collective-permute-start | bytes 393224 | tf_op jit(solution)/shard_map/ppermute | solution.py:307
  4.7 1.5 %collective-permute-start.2 = (bf16[128,512]{1,0:T(8,128)(2,1)}, bf16[128,512]{1,0:T(8,128)(2,1)S(1)}, u32[]{:S(2)}, u32[]{:S(2)}) collective-permute-start(bf16[128,512]{1,0:T(8,128)(2,1)} %text_ref.1), channel_id=1, source_target_pairs={{0,2},{1,3},{2,0},{3,1},{4,6},{5,7},{6,4},{7,5},{8,10},{9,11},{10,... | collective-permute-start | bytes 393224 | tf_op jit(solution)/shard_map/ppermute | solution.py:307
  6.3 1.5 %collective-permute-start.1 = (bf16[128,512]{1,0:T(8,128)(2,1)}, bf16[128,512]{1,0:T(8,128)(2,1)S(1)}, u32[]{:S(2)}, u32[]{:S(2)}) collective-permute-start(bf16[128,512]{1,0:T(8,128)(2,1)} %text_ref.1), channel_id=1, source_target_pairs={{0,1},{1,0},{2,3},{3,2},{4,5},{5,4},{6,7},{7,6},{8,9},{9,8},{10,11... | collective-permute-start | bytes 393224 | tf_op jit(solution)/shard_map/ppermute | solution.py:307
  7.7 0.5 %collective-permute-start.3 = (bf16[128,512]{1,0:T(8,128)(2,1)}, bf16[128,512]{1,0:T(8,128)(2,1)S(1)}, u32[]{:S(2)}, u32[]{:S(2)}) collective-permute-start(bf16[128,512]{1,0:T(8,128)(2,1)} %text_ref.1), channel_id=1, source_target_pairs={{0,3},{1,2},{2,1},{3,0},{4,7},{5,6},{6,5},{7,4},{8,11},{9,10},{10,... | collective-permute-start | bytes 393224 | tf_op jit(solution)/shard_map/ppermute | solution.py:307
  8.2 1.6 %collective-permute-start.4 = (bf16[128,512]{1,0:T(8,128)(2,1)}, bf16[128,512]{1,0:T(8,128)(2,1)S(1)}, u32[]{:S(2)}, u32[]{:S(2)}) collective-permute-start(bf16[128,512]{1,0:T(8,128)(2,1)} %image_ref.1), channel_id=1, source_target_pairs={{0,4},{1,5},{2,6},{3,7},{4,0},{5,1},{6,2},{7,3},{8,12},{9,13},{10,... | collective-permute-start | bytes 393224 | tf_op jit(solution)/shard_map/ppermute | solution.py:307
  11.4 0.8 %collective-permute-start.5 = (bf16[128,512]{1,0:T(8,128)(2,1)S(1)}, bf16[128,512]{1,0:T(8,128)(2,1)S(1)}, u32[]{:S(2)}, u32[]{:S(2)}) collective-permute-start(bf16[128,512]{1,0:T(8,128)(2,1)S(1)} %collective-permute-done.refs_1_), channel_id=1, source_target_pairs={{0,4},{1,5},{2,6},{3,7},{4,0},{5,1},{6,2},{7,3},{8,12},{9,13},{10,... | collective-permute-start | bytes 393224 | tf_op jit(solution)/shard_map/ppermute | solution.py:307
  12.1 0.9 %copy-done = bf16[128,512]{1,0:T(8,128)(2,1)S(1)} copy-done((bf16[128,512]{1,0:T(8,128)(2,1)S(1)}, bf16[128,512]{1,0:T(8,128)(2,1)}, u32[]{:S(2)}) %copy-start) | copy-done | bytes 131096
  13.2 1.0 %collective-permute-done.3.refs_3_ = bf16[128,512]{1,0:T(8,128)(2,1)S(1)} collective-permute-done((bf16[128,512]{1,0:T(8,128)(2,1)}, bf16[128,512]{1,0:T(8,128)(2,1)S(1)}, u32[]{:S(2)}, u32[]{:S(2)}) %collective-permute-start.3) | collective-permute-done | bytes 131104 | tf_op jit(solution)/shard_map/ppermute | solution.py:307
  14.9 1.1 %early_pairs.1 = (f32[512,512]{1,0:T(8,128)S(1)}, bf16[384,512]{1,0:T(8,128)(2,1)S(1)}, f32[384,512]{1,0:T(8,128)S(1)}) custom-call(f32[1,3]{1,0:T(1,128)S(1)} %maximum_bitcast_fusion.params_ref, bf16[512,512]{1,0:T(8,128)(2,1)S(1)} %stack_units.1.text_ref.refs_0_, bf16[128,512]{1,0:T(8,128)(2,1)S(1)} %copy-done.2, ...), custom_call_target="tpu_custom_call" | custom-call | flops 603979776 | bytes 3145740 | tf_op jit(solution)/shard_map/early_pairs/pallas_call | solution.py:29
  16.0 0.9 %collective-permute-done.5.refs_0_ = bf16[128,512]{1,0:T(8,128)(2,1)S(1)} collective-permute-done((bf16[128,512]{1,0:T(8,128)(2,1)S(1)}, bf16[128,512]{1,0:T(8,128)(2,1)S(1)}, u32[]{:S(2)}, u32[]{:S(2)}) %collective-permute-start.5) | collective-permute-done | bytes 131104 | tf_op jit(solution)/shard_map/ppermute | solution.py:307
  17.0 1.1 %early_rest.1 = (f32[512,512]{1,0:T(8,128)S(1)}, f32[128,512]{1,0:T(8,128)S(1)}, bf16[128,512]{1,0:T(8,128)(2,1)S(1)}, bf16[128,512]{1,0:T(8,128)(2,1)S(1)}) custom-call(f32[1,3]{1,0:T(1,128)S(1)} %maximum_bitcast_fusion.params_ref, bf16[384,512]{1,0:T(8,128)(2,1)S(1)} %get-tuple-element.21.units_ref, f32[384,512]{1,0:T(8,128)S(1)} %get-tuple-element.24.total_ref, ...), custom_call_target="tpu_custom_call" | custom-call | flops 603979776 | bytes 3276812 | tf_op jit(solution)/shard_map/early_rest/pallas_call | solution.py:29
  18.1 1.0 %collective-permute-start.7 = (bf16[128,512]{1,0:T(8,128)(2,1)S(1)}, bf16[128,512]{1,0:T(8,128)(2,1)S(1)}, u32[]{:S(2)}, u32[]{:S(2)}) collective-permute-start(bf16[128,512]{1,0:T(8,128)(2,1)S(1)} %get-tuple-element.30), channel_id=1, source_target_pairs={{0,4},{1,5},{2,6},{3,7},{4,0},{5,1},{6,2},{7,3},{8,12},{9,13},{10,... | collective-permute-start | bytes 393224 | tf_op jit(solution)/shard_map/ppermute | solution.py:307
  19.1 1.2 %late_pairs.1 = (f32[512,512]{1,0:T(8,128)S(1)}, bf16[512,512]{1,0:T(8,128)(2,1)S(1)}, f32[128,512]{1,0:T(8,128)S(1)}) custom-call(f32[1,3]{1,0:T(1,128)S(1)} %maximum_bitcast_fusion.params_ref, bf16[128,512]{1,0:T(8,128)(2,1)S(1)} %late_units.1.units_ref, bf16[512,512]{1,0:T(8,128)(2,1)S(1)} %stack_units.1.text_ref.refs_0_, ...), custom_call_target="tpu_custom_call" | custom-call | flops 402653184 | bytes 5111820 | tf_op jit(solution)/shard_map/late_pairs/pallas_call | solution.py:29
  20.4 1.2 %collective-permute-start.13 = (bf16[128,512]{1,0:T(8,128)(2,1)S(1)}, bf16[128,512]{1,0:T(8,128)(2,1)S(1)}, u32[]{:S(2)}, u32[]{:S(2)}) collective-permute-start(bf16[128,512]{1,0:T(8,128)(2,1)S(1)} %get-tuple-element.37), channel_id=1, source_target_pairs={{0,4},{1,5},{2,6},{3,7},{4,0},{5,1},{6,2},{7,3},{8,12},{9,13},{10,... | collective-permute-start | bytes 393224 | tf_op jit(solution)/shard_map/ppermute | solution.py:307
  21.6 1.6 %collective-permute-done.7.refs_1_ = bf16[128,512]{1,0:T(8,128)(2,1)S(1)} collective-permute-done((bf16[128,512]{1,0:T(8,128)(2,1)S(1)}, bf16[128,512]{1,0:T(8,128)(2,1)S(1)}, u32[]{:S(2)}, u32[]{:S(2)}) %collective-permute-start.7) | collective-permute-done | bytes 131104 | tf_op jit(solution)/shard_map/ppermute | solution.py:307
  23.2 3.7 %collective-permute-start.8 = (bf16[128,512]{1,0:T(8,128)(2,1)S(1)}, bf16[128,512]{1,0:T(8,128)(2,1)S(1)}, u32[]{:S(2)}, u32[]{:S(2)}) collective-permute-start(bf16[128,512]{1,0:T(8,128)(2,1)S(1)} %add_passed.1), channel_id=1, source_target_pairs={{0,12},{1,13},{2,14},{3,15},{4,8},{5,9},{6,10},{7,11},{8,4},{9,5},... | collective-permute-start | bytes 393224 | tf_op jit(solution)/shard_map/ppermute | solution.py:307
  27.0 1.6 %collective-permute-start.10 = (bf16[128,512]{1,0:T(8,128)(2,1)S(1)}, bf16[128,512]{1,0:T(8,128)(2,1)S(1)}, u32[]{:S(2)}, u32[]{:S(2)}) collective-permute-start(bf16[128,512]{1,0:T(8,128)(2,1)S(1)} %get-tuple-element.34), channel_id=1, source_target_pairs={{0,1},{1,0},{2,3},{3,2},{4,5},{5,4},{6,7},{7,6},{8,9},{9,8},{10,11... | collective-permute-start | bytes 393224 | tf_op jit(solution)/shard_map/ppermute | solution.py:307
  28.6 1.5 %collective-permute-start.11 = (bf16[128,512]{1,0:T(8,128)(2,1)S(1)}, bf16[128,512]{1,0:T(8,128)(2,1)S(1)}, u32[]{:S(2)}, u32[]{:S(2)}) collective-permute-start(bf16[128,512]{1,0:T(8,128)(2,1)S(1)} %get-tuple-element.35), channel_id=1, source_target_pairs={{0,2},{1,3},{2,0},{3,1},{4,6},{5,7},{6,4},{7,5},{8,10},{9,11},{10,... | collective-permute-start | bytes 393224 | tf_op jit(solution)/shard_map/ppermute | solution.py:307
  30.1 0.5 %collective-permute-start.12 = (bf16[128,512]{1,0:T(8,128)(2,1)S(1)}, bf16[128,512]{1,0:T(8,128)(2,1)S(1)}, u32[]{:S(2)}, u32[]{:S(2)}) collective-permute-start(bf16[128,512]{1,0:T(8,128)(2,1)S(1)} %get-tuple-element.36), channel_id=1, source_target_pairs={{0,3},{1,2},{2,1},{3,0},{4,7},{5,6},{6,5},{7,4},{8,11},{9,10},{10,... | collective-permute-start | bytes 393224 | tf_op jit(solution)/shard_map/ppermute | solution.py:307
  30.5 1.1 %collective-permute-done.8.refs_1_ = bf16[128,512]{1,0:T(8,128)(2,1)S(1)} collective-permute-done((bf16[128,512]{1,0:T(8,128)(2,1)S(1)}, bf16[128,512]{1,0:T(8,128)(2,1)S(1)}, u32[]{:S(2)}, u32[]{:S(2)}) %collective-permute-start.8) | collective-permute-done | bytes 131104 | tf_op jit(solution)/shard_map/ppermute | solution.py:307
  31.7 1.2 %collective-permute-done.10.refs_3_ = bf16[128,512]{1,0:T(8,128)(2,1)S(1)} collective-permute-done((bf16[128,512]{1,0:T(8,128)(2,1)S(1)}, bf16[128,512]{1,0:T(8,128)(2,1)S(1)}, u32[]{:S(2)}, u32[]{:S(2)}) %collective-permute-start.10) | collective-permute-done | bytes 131104 | tf_op jit(solution)/shard_map/ppermute | solution.py:307
  32.9 1.3 %collective-permute-done.11.refs_4_ = bf16[128,512]{1,0:T(8,128)(2,1)S(1)} collective-permute-done((bf16[128,512]{1,0:T(8,128)(2,1)S(1)}, bf16[128,512]{1,0:T(8,128)(2,1)S(1)}, u32[]{:S(2)}, u32[]{:S(2)}) %collective-permute-start.11) | collective-permute-done | bytes 131104 | tf_op jit(solution)/shard_map/ppermute | solution.py:307
  34.2 1.8 %collective-permute-done.12.refs_5_ = bf16[128,512]{1,0:T(8,128)(2,1)S(1)} collective-permute-done((bf16[128,512]{1,0:T(8,128)(2,1)S(1)}, bf16[128,512]{1,0:T(8,128)(2,1)S(1)}, u32[]{:S(2)}, u32[]{:S(2)}) %collective-permute-start.12) | collective-permute-done | bytes 131104 | tf_op jit(solution)/shard_map/ppermute | solution.py:307
  36.0 1.0 %finish.1 = (f32[128,512]{1,0:T(8,128)}, f32[128,512]{1,0:T(8,128)}) custom-call(bf16[128,512]{1,0:T(8,128)(2,1)S(1)} %copy-done.2, bf16[128,512]{1,0:T(8,128)(2,1)S(1)} %copy-done.1, f32[128,512]{1,0:T(8,128)S(1)} %get-tuple-element.25.refs_0_, bf16[128,512]{1,0:T(8,128)(2,1)S(1)} %collective-permute-done.8.refs_1_, ...), custom_call_target="tpu_custom_call" | custom-call | flops 4587520 | bytes 1376256 | tf_op jit(solution)/shard_map/finish/pallas_call | solution.py:257
  (20 shorter events, 1.4 us)
Async XLA Ops:
  0.6 10.7 %collective-permute-start = (bf16[128,512]{1,0:T(8,128)(2,1)}, bf16[128,512]{1,0:T(8,128)(2,1)S(1)}, u32[]{:S(2)}, u32[]{:S(2)}) collective-permute-start(bf16[128,512]{1,0:T(8,128)(2,1)} %image_ref.1), channel_id=1, source_target_pairs={{0,8},{1,9},{2,10},{3,11},{4,12},{5,13},{6,14},{7,15},{8,0},{9,1},... | collective-permute-start | bytes 393224 | tf_op jit(solution)/shard_map/ppermute | solution.py:307
  4.7 8.4 %collective-permute-start.2 = (bf16[128,512]{1,0:T(8,128)(2,1)}, bf16[128,512]{1,0:T(8,128)(2,1)S(1)}, u32[]{:S(2)}, u32[]{:S(2)}) collective-permute-start(bf16[128,512]{1,0:T(8,128)(2,1)} %text_ref.1), channel_id=1, source_target_pairs={{0,2},{1,3},{2,0},{3,1},{4,6},{5,7},{6,4},{7,5},{8,10},{9,11},{10,... | collective-permute-start | bytes 393224 | tf_op jit(solution)/shard_map/ppermute | solution.py:307
  6.3 6.9 %collective-permute-start.1 = (bf16[128,512]{1,0:T(8,128)(2,1)}, bf16[128,512]{1,0:T(8,128)(2,1)S(1)}, u32[]{:S(2)}, u32[]{:S(2)}) collective-permute-start(bf16[128,512]{1,0:T(8,128)(2,1)} %text_ref.1), channel_id=1, source_target_pairs={{0,1},{1,0},{2,3},{3,2},{4,5},{5,4},{6,7},{7,6},{8,9},{9,8},{10,11... | collective-permute-start | bytes 393224 | tf_op jit(solution)/shard_map/ppermute | solution.py:307
  7.7 6.4 %collective-permute-start.3 = (bf16[128,512]{1,0:T(8,128)(2,1)}, bf16[128,512]{1,0:T(8,128)(2,1)S(1)}, u32[]{:S(2)}, u32[]{:S(2)}) collective-permute-start(bf16[128,512]{1,0:T(8,128)(2,1)} %text_ref.1), channel_id=1, source_target_pairs={{0,3},{1,2},{2,1},{3,0},{4,7},{5,6},{6,5},{7,4},{8,11},{9,10},{10,... | collective-permute-start | bytes 393224 | tf_op jit(solution)/shard_map/ppermute | solution.py:307
  8.2 6.6 %collective-permute-start.4 = (bf16[128,512]{1,0:T(8,128)(2,1)}, bf16[128,512]{1,0:T(8,128)(2,1)S(1)}, u32[]{:S(2)}, u32[]{:S(2)}) collective-permute-start(bf16[128,512]{1,0:T(8,128)(2,1)} %image_ref.1), channel_id=1, source_target_pairs={{0,4},{1,5},{2,6},{3,7},{4,0},{5,1},{6,2},{7,3},{8,12},{9,13},{10,... | collective-permute-start | bytes 393224 | tf_op jit(solution)/shard_map/ppermute | solution.py:307
  11.4 5.5 %collective-permute-start.5 = (bf16[128,512]{1,0:T(8,128)(2,1)S(1)}, bf16[128,512]{1,0:T(8,128)(2,1)S(1)}, u32[]{:S(2)}, u32[]{:S(2)}) collective-permute-start(bf16[128,512]{1,0:T(8,128)(2,1)S(1)} %collective-permute-done.refs_1_), channel_id=1, source_target_pairs={{0,4},{1,5},{2,6},{3,7},{4,0},{5,1},{6,2},{7,3},{8,12},{9,13},{10,... | collective-permute-start | bytes 393224 | tf_op jit(solution)/shard_map/ppermute | solution.py:307
  12.1 0.9 %copy-start = (bf16[128,512]{1,0:T(8,128)(2,1)S(1)}, bf16[128,512]{1,0:T(8,128)(2,1)}, u32[]{:S(2)}) copy-start(bf16[128,512]{1,0:T(8,128)(2,1)} %text_ref.1) | copy-start | bytes 393220
  13.1 1.7 %copy-start.2 = (bf16[128,512]{1,0:T(8,128)(2,1)S(1)}, bf16[128,512]{1,0:T(8,128)(2,1)}, u32[]{:S(2)}) copy-start(bf16[128,512]{1,0:T(8,128)(2,1)} %image_ref.1) | copy-start | bytes 393220
  14.3 2.6 %collective-permute-start.6 = (bf16[512,512]{1,0:T(8,128)(2,1)S(1)}, bf16[512,512]{1,0:T(8,128)(2,1)S(1)}, u32[]{:S(2)}, u32[]{:S(2)}) collective-permute-start(bf16[512,512]{1,0:T(8,128)(2,1)S(1)} %stack_units.1.text_ref.refs_0_), channel_id=1, source_target_pairs={{0,16},{1,17},{2,18},{3,19},{4,20},{5,21},{6,22},{7,23},{8,24},{9,... | collective-permute-start | bytes 1572872 | tf_op jit(solution)/shard_map/ppermute | solution.py:307
  18.1 5.0 %collective-permute-start.7 = (bf16[128,512]{1,0:T(8,128)(2,1)S(1)}, bf16[128,512]{1,0:T(8,128)(2,1)S(1)}, u32[]{:S(2)}, u32[]{:S(2)}) collective-permute-start(bf16[128,512]{1,0:T(8,128)(2,1)S(1)} %get-tuple-element.30), channel_id=1, source_target_pairs={{0,4},{1,5},{2,6},{3,7},{4,0},{5,1},{6,2},{7,3},{8,12},{9,13},{10,... | collective-permute-start | bytes 393224 | tf_op jit(solution)/shard_map/ppermute | solution.py:307
  20.3 6.6 %collective-permute-start.9 = (bf16[512,512]{1,0:T(8,128)(2,1)S(1)}, bf16[512,512]{1,0:T(8,128)(2,1)S(1)}, u32[]{:S(2)}, u32[]{:S(2)}) collective-permute-start(bf16[512,512]{1,0:T(8,128)(2,1)S(1)} %get-tuple-element.32), channel_id=1, source_target_pairs={{0,16},{1,17},{2,18},{3,19},{4,20},{5,21},{6,22},{7,23},{8,24},{9,... | collective-permute-start | bytes 1572872 | tf_op jit(solution)/shard_map/ppermute | solution.py:307
  20.4 10.2 %collective-permute-start.13 = (bf16[128,512]{1,0:T(8,128)(2,1)S(1)}, bf16[128,512]{1,0:T(8,128)(2,1)S(1)}, u32[]{:S(2)}, u32[]{:S(2)}) collective-permute-start(bf16[128,512]{1,0:T(8,128)(2,1)S(1)} %get-tuple-element.37), channel_id=1, source_target_pairs={{0,4},{1,5},{2,6},{3,7},{4,0},{5,1},{6,2},{7,3},{8,12},{9,13},{10,... | collective-permute-start | bytes 393224 | tf_op jit(solution)/shard_map/ppermute | solution.py:307
  23.2 8.5 %collective-permute-start.8 = (bf16[128,512]{1,0:T(8,128)(2,1)S(1)}, bf16[128,512]{1,0:T(8,128)(2,1)S(1)}, u32[]{:S(2)}, u32[]{:S(2)}) collective-permute-start(bf16[128,512]{1,0:T(8,128)(2,1)S(1)} %add_passed.1), channel_id=1, source_target_pairs={{0,12},{1,13},{2,14},{3,15},{4,8},{5,9},{6,10},{7,11},{8,4},{9,5},... | collective-permute-start | bytes 393224 | tf_op jit(solution)/shard_map/ppermute | solution.py:307
  26.9 9.1 %copy-start.1 = (bf16[128,512]{1,0:T(8,128)(2,1)S(1)}, bf16[128,512]{1,0:T(8,128)(2,1)}, u32[]{:S(2)}) copy-start(bf16[128,512]{1,0:T(8,128)(2,1)} %text_ref.1) | copy-start | bytes 393220
  27.0 5.9 %collective-permute-start.10 = (bf16[128,512]{1,0:T(8,128)(2,1)S(1)}, bf16[128,512]{1,0:T(8,128)(2,1)S(1)}, u32[]{:S(2)}, u32[]{:S(2)}) collective-permute-start(bf16[128,512]{1,0:T(8,128)(2,1)S(1)} %get-tuple-element.34), channel_id=1, source_target_pairs={{0,1},{1,0},{2,3},{3,2},{4,5},{5,4},{6,7},{7,6},{8,9},{9,8},{10,11... | collective-permute-start | bytes 393224 | tf_op jit(solution)/shard_map/ppermute | solution.py:307
  28.6 5.6 %collective-permute-start.11 = (bf16[128,512]{1,0:T(8,128)(2,1)S(1)}, bf16[128,512]{1,0:T(8,128)(2,1)S(1)}, u32[]{:S(2)}, u32[]{:S(2)}) collective-permute-start(bf16[128,512]{1,0:T(8,128)(2,1)S(1)} %get-tuple-element.35), channel_id=1, source_target_pairs={{0,2},{1,3},{2,0},{3,1},{4,6},{5,7},{6,4},{7,5},{8,10},{9,11},{10,... | collective-permute-start | bytes 393224 | tf_op jit(solution)/shard_map/ppermute | solution.py:307
  30.1 5.9 %collective-permute-start.12 = (bf16[128,512]{1,0:T(8,128)(2,1)S(1)}, bf16[128,512]{1,0:T(8,128)(2,1)S(1)}, u32[]{:S(2)}, u32[]{:S(2)}) collective-permute-start(bf16[128,512]{1,0:T(8,128)(2,1)S(1)} %get-tuple-element.36), channel_id=1, source_target_pairs={{0,3},{1,2},{2,1},{3,0},{4,7},{5,6},{6,5},{7,4},{8,11},{9,10},{10,... | collective-permute-start | bytes 393224 | tf_op jit(solution)/shard_map/ppermute | solution.py:307

commit v25 on v24

--- a/solution.py
+++ b/solution.py
@@ -13,7 +13,7 @@
 SPAN = 256
 PIECE = 32
 LATE = 16500
-PASSED = 37000
+PASSED = 45000
 LOG2_E = math.log2(math.e)
 VMEM = pl.BlockSpec(memory_space=pltpu.VMEM)
 
@@ -339,11 +339,13 @@
         else:
             far_came = [give_back(h, w) for h, w in early if h]
         came = [move(part, grp=-g) for g, part in enumerate(text_parts) if g]
-        low_came = [give_back(h, w) for h, w in early if w]
         near_parts = add_stacks([text_parts[0], *came], near_count)
+        low_parts = [far_parts[0, w] for w in range(1, low_count)]
+        low_parts, near_parts = lax.optimization_barrier((low_parts, near_parts))
         near_parts = [near_parts[0]] + [
             move(part, near=-n) for n, part in enumerate(near_parts) if n
         ]
+        low_came = [move(part, low=-w) for w, part in enumerate(low_parts, 1)]
         return finish(
             images,
             texts,

time: 37.2 us -> 36.9 us (level)
  starting transfers between devices: 19.5 us -> 18 us
  waiting for transfers between devices: 9.47 us -> 10.6 us
    ppermute x14, starting transfers between devices: 19.5 us -> 18 us  [move(): return lax.ppermute(value, AXES, perm)]
    ppermute x14, waiting for transfers between devices: 9.47 us -> 10.6 us  [move(): return lax.ppermute(value, AXES, perm)]
  transfers between devices with their start and end apart: 14 -> 14, of which waited for: 9 -> 8; matrix products, arithmetic and copies ran while one was open for 0% -> 0% of each run, Pallas kernels for 8% -> 8%
where the time goes in v25:
time: 36.9 us; the launch traced here: 36.7 us
  starting transfers between devices  18 us (49%)
  waiting for transfers between devices  10.6 us (29%)
  Pallas kernels  5.03 us (14%)
  between operations  2.03 us (6%)
  local copies, waits for them, and re-layouts  0.91 us (2%)
    ppermute x14, starting transfers between devices, move(): return lax.ppermute(value, AXES, perm)  18 us
    ppermute x14, waiting for transfers between devices, move(): return lax.ppermute(value, AXES, perm)  10.6 us
    pallas_call x8, Pallas kernels, call(): pl.pallas_call(kernel, out_shape=out_shape, in_specs=[VMEM] * len(operand...  3.99 us
    pallas_call x1, Pallas kernels, finish(): pl.pallas_call(functools.partial(finish_kernel, [side for side, _ in part...  1.05 us
    unnamed x6, local copies, waits for them, and re-layouts  0.91 us
  transfers between devices with their start and end apart: 14, of which 8 were waited for; matrix products, arithmetic and copies ran while one was open for 0% of the time, Pallas kernels for 8%

profile of v25, /device:TPU:0, one launch (start us, length us, event | category | flops | bytes accessed | tf_op | source)
XLA Modules:
  0.0 36.7 jit_solution(4837670674102338831)
XLA Ops:
  0.6 4.1 %collective-permute-start = (bf16[128,512]{1,0:T(8,128)(2,1)}, bf16[128,512]{1,0:T(8,128)(2,1)S(1)}, u32[]{:S(2)}, u32[]{:S(2)}) collective-permute-start(bf16[128,512]{1,0:T(8,128)(2,1)} %image_ref.1), channel_id=1, source_target_pairs={{0,8},{1,9},{2,10},{3,11},{4,12},{5,13},{6,14},{7,15},{8,0},{9,1},... | collective-permute-start | bytes 393224 | tf_op jit(solution)/shard_map/ppermute | solution.py:307
  4.7 1.5 %collective-permute-start.2 = (bf16[128,512]{1,0:T(8,128)(2,1)}, bf16[128,512]{1,0:T(8,128)(2,1)S(1)}, u32[]{:S(2)}, u32[]{:S(2)}) collective-permute-start(bf16[128,512]{1,0:T(8,128)(2,1)} %text_ref.1), channel_id=1, source_target_pairs={{0,2},{1,3},{2,0},{3,1},{4,6},{5,7},{6,4},{7,5},{8,10},{9,11},{10,... | collective-permute-start | bytes 393224 | tf_op jit(solution)/shard_map/ppermute | solution.py:307
  6.3 1.5 %collective-permute-start.1 = (bf16[128,512]{1,0:T(8,128)(2,1)}, bf16[128,512]{1,0:T(8,128)(2,1)S(1)}, u32[]{:S(2)}, u32[]{:S(2)}) collective-permute-start(bf16[128,512]{1,0:T(8,128)(2,1)} %text_ref.1), channel_id=1, source_target_pairs={{0,1},{1,0},{2,3},{3,2},{4,5},{5,4},{6,7},{7,6},{8,9},{9,8},{10,11... | collective-permute-start | bytes 393224 | tf_op jit(solution)/shard_map/ppermute | solution.py:307
  7.7 0.5 %collective-permute-start.3 = (bf16[128,512]{1,0:T(8,128)(2,1)}, bf16[128,512]{1,0:T(8,128)(2,1)S(1)}, u32[]{:S(2)}, u32[]{:S(2)}) collective-permute-start(bf16[128,512]{1,0:T(8,128)(2,1)} %text_ref.1), channel_id=1, source_target_pairs={{0,3},{1,2},{2,1},{3,0},{4,7},{5,6},{6,5},{7,4},{8,11},{9,10},{10,... | collective-permute-start | bytes 393224 | tf_op jit(solution)/shard_map/ppermute | solution.py:307
  8.2 1.6 %collective-permute-start.4 = (bf16[128,512]{1,0:T(8,128)(2,1)}, bf16[128,512]{1,0:T(8,128)(2,1)S(1)}, u32[]{:S(2)}, u32[]{:S(2)}) collective-permute-start(bf16[128,512]{1,0:T(8,128)(2,1)} %image_ref.1), channel_id=1, source_target_pairs={{0,4},{1,5},{2,6},{3,7},{4,0},{5,1},{6,2},{7,3},{8,12},{9,13},{10,... | collective-permute-start | bytes 393224 | tf_op jit(solution)/shard_map/ppermute | solution.py:307
  11.2 0.2 collective-permute-done.refs_1_
  11.4 0.8 %collective-permute-start.5 = (bf16[128,512]{1,0:T(8,128)(2,1)S(1)}, bf16[128,512]{1,0:T(8,128)(2,1)S(1)}, u32[]{:S(2)}, u32[]{:S(2)}) collective-permute-start(bf16[128,512]{1,0:T(8,128)(2,1)S(1)} %collective-permute-done.refs_1_), channel_id=1, source_target_pairs={{0,4},{1,5},{2,6},{3,7},{4,0},{5,1},{6,2},{7,3},{8,12},{9,13},{10,... | collective-permute-start | bytes 393224 | tf_op jit(solution)/shard_map/ppermute | solution.py:307
  12.1 0.9 %copy-done = bf16[128,512]{1,0:T(8,128)(2,1)S(1)} copy-done((bf16[128,512]{1,0:T(8,128)(2,1)S(1)}, bf16[128,512]{1,0:T(8,128)(2,1)}, u32[]{:S(2)}) %copy-start) | copy-done | bytes 131096
  13.2 1.0 %collective-permute-done.3.refs_3_ = bf16[128,512]{1,0:T(8,128)(2,1)S(1)} collective-permute-done((bf16[128,512]{1,0:T(8,128)(2,1)}, bf16[128,512]{1,0:T(8,128)(2,1)S(1)}, u32[]{:S(2)}, u32[]{:S(2)}) %collective-permute-start.3) | collective-permute-done | bytes 131104 | tf_op jit(solution)/shard_map/ppermute | solution.py:307
  14.4 0.4 %collective-permute-done.4.refs_2_ = bf16[128,512]{1,0:T(8,128)(2,1)S(1)} collective-permute-done((bf16[128,512]{1,0:T(8,128)(2,1)}, bf16[128,512]{1,0:T(8,128)(2,1)S(1)}, u32[]{:S(2)}, u32[]{:S(2)}) %collective-permute-start.4) | collective-permute-done | bytes 131104 | tf_op jit(solution)/shard_map/ppermute | solution.py:307
  14.9 1.1 %early_pairs.1 = (f32[512,512]{1,0:T(8,128)S(1)}, bf16[384,512]{1,0:T(8,128)(2,1)S(1)}, f32[384,512]{1,0:T(8,128)S(1)}) custom-call(f32[1,3]{1,0:T(1,128)S(1)} %maximum_bitcast_fusion.params_ref, bf16[512,512]{1,0:T(8,128)(2,1)S(1)} %stack_units.1.text_ref.refs_0_, bf16[128,512]{1,0:T(8,128)(2,1)S(1)} %copy-done.2, ...), custom_call_target="tpu_custom_call" | custom-call | flops 603979776 | bytes 3145740 | tf_op jit(solution)/shard_map/early_pairs/pallas_call | solution.py:29
  16.0 0.9 %collective-permute-done.5.refs_0_ = bf16[128,512]{1,0:T(8,128)(2,1)S(1)} collective-permute-done((bf16[128,512]{1,0:T(8,128)(2,1)S(1)}, bf16[128,512]{1,0:T(8,128)(2,1)S(1)}, u32[]{:S(2)}, u32[]{:S(2)}) %collective-permute-start.5) | collective-permute-done | bytes 131104 | tf_op jit(solution)/shard_map/ppermute | solution.py:307
  17.0 1.1 %early_rest.1 = (f32[512,512]{1,0:T(8,128)S(1)}, f32[128,512]{1,0:T(8,128)S(1)}, bf16[128,512]{1,0:T(8,128)(2,1)S(1)}, bf16[128,512]{1,0:T(8,128)(2,1)S(1)}) custom-call(f32[1,3]{1,0:T(1,128)S(1)} %maximum_bitcast_fusion.params_ref, bf16[384,512]{1,0:T(8,128)(2,1)S(1)} %get-tuple-element.26.units_ref, f32[384,512]{1,0:T(8,128)S(1)} %get-tuple-element.29.total_ref, ...), custom_call_target="tpu_custom_call" | custom-call | flops 603979776 | bytes 3276812 | tf_op jit(solution)/shard_map/early_rest/pallas_call | solution.py:29
  18.1 1.0 %collective-permute-start.7 = (bf16[128,512]{1,0:T(8,128)(2,1)S(1)}, bf16[128,512]{1,0:T(8,128)(2,1)S(1)}, u32[]{:S(2)}, u32[]{:S(2)}) collective-permute-start(bf16[128,512]{1,0:T(8,128)(2,1)S(1)} %get-tuple-element.35), channel_id=1, source_target_pairs={{0,4},{1,5},{2,6},{3,7},{4,0},{5,1},{6,2},{7,3},{8,12},{9,13},{10,... | collective-permute-start | bytes 393224 | tf_op jit(solution)/shard_map/ppermute | solution.py:307
  19.1 1.2 %late_pairs.1 = (f32[512,512]{1,0:T(8,128)S(1)}, bf16[512,512]{1,0:T(8,128)(2,1)S(1)}, f32[128,512]{1,0:T(8,128)S(1)}) custom-call(f32[1,3]{1,0:T(1,128)S(1)} %maximum_bitcast_fusion.params_ref, bf16[128,512]{1,0:T(8,128)(2,1)S(1)} %late_units.1.units_ref, bf16[512,512]{1,0:T(8,128)(2,1)S(1)} %stack_units.1.text_ref.refs_0_, ...), custom_call_target="tpu_custom_call" | custom-call | flops 402653184 | bytes 5111820 | tf_op jit(solution)/shard_map/late_pairs/pallas_call | solution.py:29
  20.4 2.8 %collective-permute-done.7.refs_1_ = bf16[128,512]{1,0:T(8,128)(2,1)S(1)} collective-permute-done((bf16[128,512]{1,0:T(8,128)(2,1)S(1)}, bf16[128,512]{1,0:T(8,128)(2,1)S(1)}, u32[]{:S(2)}, u32[]{:S(2)}) %collective-permute-start.7) | collective-permute-done | bytes 131104 | tf_op jit(solution)/shard_map/ppermute | solution.py:307
  23.2 3.4 %collective-permute-start.8 = (bf16[128,512]{1,0:T(8,128)(2,1)S(1)}, bf16[128,512]{1,0:T(8,128)(2,1)S(1)}, u32[]{:S(2)}, u32[]{:S(2)}) collective-permute-start(bf16[128,512]{1,0:T(8,128)(2,1)S(1)} %add_passed.1), channel_id=1, source_target_pairs={{0,12},{1,13},{2,14},{3,15},{4,8},{5,9},{6,10},{7,11},{8,4},{9,5},... | collective-permute-start | bytes 393224 | tf_op jit(solution)/shard_map/ppermute | solution.py:307
  26.7 1.6 %collective-permute-start.10 = (bf16[128,512]{1,0:T(8,128)(2,1)S(1)}, bf16[128,512]{1,0:T(8,128)(2,1)S(1)}, u32[]{:S(2)}, u32[]{:S(2)}) collective-permute-start(bf16[128,512]{1,0:T(8,128)(2,1)S(1)} %get-tuple-element.44), channel_id=1, source_target_pairs={{0,1},{1,0},{2,3},{3,2},{4,5},{5,4},{6,7},{7,6},{8,9},{9,8},{10,11... | collective-permute-start | bytes 393224 | tf_op jit(solution)/shard_map/ppermute | solution.py:307
  28.3 1.5 %collective-permute-start.11 = (bf16[128,512]{1,0:T(8,128)(2,1)S(1)}, bf16[128,512]{1,0:T(8,128)(2,1)S(1)}, u32[]{:S(2)}, u32[]{:S(2)}) collective-permute-start(bf16[128,512]{1,0:T(8,128)(2,1)S(1)} %get-tuple-element.45), channel_id=1, source_target_pairs={{0,2},{1,3},{2,0},{3,1},{4,6},{5,7},{6,4},{7,5},{8,10},{9,11},{10,... | collective-permute-start | bytes 393224 | tf_op jit(solution)/shard_map/ppermute | solution.py:307
  29.8 0.5 %collective-permute-start.12 = (bf16[128,512]{1,0:T(8,128)(2,1)S(1)}, bf16[128,512]{1,0:T(8,128)(2,1)S(1)}, u32[]{:S(2)}, u32[]{:S(2)}) collective-permute-start(bf16[128,512]{1,0:T(8,128)(2,1)S(1)} %get-tuple-element.46), channel_id=1, source_target_pairs={{0,3},{1,2},{2,1},{3,0},{4,7},{5,6},{6,5},{7,4},{8,11},{9,10},{10,... | collective-permute-start | bytes 393224 | tf_op jit(solution)/shard_map/ppermute | solution.py:307
  30.3 1.9 %collective-permute-done.10.refs_3_ = bf16[128,512]{1,0:T(8,128)(2,1)S(1)} collective-permute-done((bf16[128,512]{1,0:T(8,128)(2,1)S(1)}, bf16[128,512]{1,0:T(8,128)(2,1)S(1)}, u32[]{:S(2)}, u32[]{:S(2)}) %collective-permute-start.10) | collective-permute-done | bytes 131104 | tf_op jit(solution)/shard_map/ppermute | solution.py:307
  32.3 1.2 %collective-permute-done.11.refs_4_ = bf16[128,512]{1,0:T(8,128)(2,1)S(1)} collective-permute-done((bf16[128,512]{1,0:T(8,128)(2,1)S(1)}, bf16[128,512]{1,0:T(8,128)(2,1)S(1)}, u32[]{:S(2)}, u32[]{:S(2)}) %collective-permute-start.11) | collective-permute-done | bytes 131104 | tf_op jit(solution)/shard_map/ppermute | solution.py:307
  33.5 2.2 %collective-permute-done.12.refs_5_ = bf16[128,512]{1,0:T(8,128)(2,1)S(1)} collective-permute-done((bf16[128,512]{1,0:T(8,128)(2,1)S(1)}, bf16[128,512]{1,0:T(8,128)(2,1)S(1)}, u32[]{:S(2)}, u32[]{:S(2)}) %collective-permute-start.12) | collective-permute-done | bytes 131104 | tf_op jit(solution)/shard_map/ppermute | solution.py:307
  35.7 1.0 %finish.1 = (f32[128,512]{1,0:T(8,128)}, f32[128,512]{1,0:T(8,128)}) custom-call(bf16[128,512]{1,0:T(8,128)(2,1)S(1)} %copy-done.2, bf16[128,512]{1,0:T(8,128)(2,1)S(1)} %copy-done.1, f32[128,512]{1,0:T(8,128)S(1)} %get-tuple-element.30.refs_0_, bf16[128,512]{1,0:T(8,128)(2,1)S(1)} %collective-permute-done.8.refs_1_, ...), custom_call_target="tpu_custom_call" | custom-call | flops 4587520 | bytes 1376256 | tf_op jit(solution)/shard_map/finish/pallas_call | solution.py:257
  (20 shorter events, 0.8 us)
Async XLA Ops:
  0.6 10.7 %collective-permute-start = (bf16[128,512]{1,0:T(8,128)(2,1)}, bf16[128,512]{1,0:T(8,128)(2,1)S(1)}, u32[]{:S(2)}, u32[]{:S(2)}) collective-permute-start(bf16[128,512]{1,0:T(8,128)(2,1)} %image_ref.1), channel_id=1, source_target_pairs={{0,8},{1,9},{2,10},{3,11},{4,12},{5,13},{6,14},{7,15},{8,0},{9,1},... | collective-permute-start | bytes 393224 | tf_op jit(solution)/shard_map/ppermute | solution.py:307
  4.7 8.4 %collective-permute-start.2 = (bf16[128,512]{1,0:T(8,128)(2,1)}, bf16[128,512]{1,0:T(8,128)(2,1)S(1)}, u32[]{:S(2)}, u32[]{:S(2)}) collective-permute-start(bf16[128,512]{1,0:T(8,128)(2,1)} %text_ref.1), channel_id=1, source_target_pairs={{0,2},{1,3},{2,0},{3,1},{4,6},{5,7},{6,4},{7,5},{8,10},{9,11},{10,... | collective-permute-start | bytes 393224 | tf_op jit(solution)/shard_map/ppermute | solution.py:307
  6.3 6.9 %collective-permute-start.1 = (bf16[128,512]{1,0:T(8,128)(2,1)}, bf16[128,512]{1,0:T(8,128)(2,1)S(1)}, u32[]{:S(2)}, u32[]{:S(2)}) collective-permute-start(bf16[128,512]{1,0:T(8,128)(2,1)} %text_ref.1), channel_id=1, source_target_pairs={{0,1},{1,0},{2,3},{3,2},{4,5},{5,4},{6,7},{7,6},{8,9},{9,8},{10,11... | collective-permute-start | bytes 393224 | tf_op jit(solution)/shard_map/ppermute | solution.py:307
  7.7 6.4 %collective-permute-start.3 = (bf16[128,512]{1,0:T(8,128)(2,1)}, bf16[128,512]{1,0:T(8,128)(2,1)S(1)}, u32[]{:S(2)}, u32[]{:S(2)}) collective-permute-start(bf16[128,512]{1,0:T(8,128)(2,1)} %text_ref.1), channel_id=1, source_target_pairs={{0,3},{1,2},{2,1},{3,0},{4,7},{5,6},{6,5},{7,4},{8,11},{9,10},{10,... | collective-permute-start | bytes 393224 | tf_op jit(solution)/shard_map/ppermute | solution.py:307
  8.2 6.6 %collective-permute-start.4 = (bf16[128,512]{1,0:T(8,128)(2,1)}, bf16[128,512]{1,0:T(8,128)(2,1)S(1)}, u32[]{:S(2)}, u32[]{:S(2)}) collective-permute-start(bf16[128,512]{1,0:T(8,128)(2,1)} %image_ref.1), channel_id=1, source_target_pairs={{0,4},{1,5},{2,6},{3,7},{4,0},{5,1},{6,2},{7,3},{8,12},{9,13},{10,... | collective-permute-start | bytes 393224 | tf_op jit(solution)/shard_map/ppermute | solution.py:307
  11.4 5.5 %collective-permute-start.5 = (bf16[128,512]{1,0:T(8,128)(2,1)S(1)}, bf16[128,512]{1,0:T(8,128)(2,1)S(1)}, u32[]{:S(2)}, u32[]{:S(2)}) collective-permute-start(bf16[128,512]{1,0:T(8,128)(2,1)S(1)} %collective-permute-done.refs_1_), channel_id=1, source_target_pairs={{0,4},{1,5},{2,6},{3,7},{4,0},{5,1},{6,2},{7,3},{8,12},{9,13},{10,... | collective-permute-start | bytes 393224 | tf_op jit(solution)/shard_map/ppermute | solution.py:307
  12.1 0.9 %copy-start = (bf16[128,512]{1,0:T(8,128)(2,1)S(1)}, bf16[128,512]{1,0:T(8,128)(2,1)}, u32[]{:S(2)}) copy-start(bf16[128,512]{1,0:T(8,128)(2,1)} %text_ref.1) | copy-start | bytes 393220
  13.1 1.7 %copy-start.2 = (bf16[128,512]{1,0:T(8,128)(2,1)S(1)}, bf16[128,512]{1,0:T(8,128)(2,1)}, u32[]{:S(2)}) copy-start(bf16[128,512]{1,0:T(8,128)(2,1)} %image_ref.1) | copy-start | bytes 393220
  14.3 2.6 %collective-permute-start.6 = (bf16[512,512]{1,0:T(8,128)(2,1)S(1)}, bf16[512,512]{1,0:T(8,128)(2,1)S(1)}, u32[]{:S(2)}, u32[]{:S(2)}) collective-permute-start(bf16[512,512]{1,0:T(8,128)(2,1)S(1)} %stack_units.1.text_ref.refs_0_), channel_id=1, source_target_pairs={{0,16},{1,17},{2,18},{3,19},{4,20},{5,21},{6,22},{7,23},{8,24},{9,... | collective-permute-start | bytes 1572872 | tf_op jit(solution)/shard_map/ppermute | solution.py:307
  18.1 5.0 %collective-permute-start.7 = (bf16[128,512]{1,0:T(8,128)(2,1)S(1)}, bf16[128,512]{1,0:T(8,128)(2,1)S(1)}, u32[]{:S(2)}, u32[]{:S(2)}) collective-permute-start(bf16[128,512]{1,0:T(8,128)(2,1)S(1)} %get-tuple-element.35), channel_id=1, source_target_pairs={{0,4},{1,5},{2,6},{3,7},{4,0},{5,1},{6,2},{7,3},{8,12},{9,13},{10,... | collective-permute-start | bytes 393224 | tf_op jit(solution)/shard_map/ppermute | solution.py:307
  20.3 6.3 %collective-permute-start.9 = (bf16[512,512]{1,0:T(8,128)(2,1)S(1)}, bf16[512,512]{1,0:T(8,128)(2,1)S(1)}, u32[]{:S(2)}, u32[]{:S(2)}) collective-permute-start(bf16[512,512]{1,0:T(8,128)(2,1)S(1)} %get-tuple-element.38), channel_id=1, source_target_pairs={{0,16},{1,17},{2,18},{3,19},{4,20},{5,21},{6,22},{7,23},{8,24},{9,... | collective-permute-start | bytes 1572872 | tf_op jit(solution)/shard_map/ppermute | solution.py:307
  23.2 7.2 %collective-permute-start.8 = (bf16[128,512]{1,0:T(8,128)(2,1)S(1)}, bf16[128,512]{1,0:T(8,128)(2,1)S(1)}, u32[]{:S(2)}, u32[]{:S(2)}) collective-permute-start(bf16[128,512]{1,0:T(8,128)(2,1)S(1)} %add_passed.1), channel_id=1, source_target_pairs={{0,12},{1,13},{2,14},{3,15},{4,8},{5,9},{6,10},{7,11},{8,4},{9,5},... | collective-permute-start | bytes 393224 | tf_op jit(solution)/shard_map/ppermute | solution.py:307
  26.6 9.1 %copy-start.1 = (bf16[128,512]{1,0:T(8,128)(2,1)S(1)}, bf16[128,512]{1,0:T(8,128)(2,1)}, u32[]{:S(2)}) copy-start(bf16[128,512]{1,0:T(8,128)(2,1)} %text_ref.1) | copy-start | bytes 393220
  26.7 5.5 %collective-permute-start.10 = (bf16[128,512]{1,0:T(8,128)(2,1)S(1)}, bf16[128,512]{1,0:T(8,128)(2,1)S(1)}, u32[]{:S(2)}, u32[]{:S(2)}) collective-permute-start(bf16[128,512]{1,0:T(8,128)(2,1)S(1)} %get-tuple-element.44), channel_id=1, source_target_pairs={{0,1},{1,0},{2,3},{3,2},{4,5},{5,4},{6,7},{7,6},{8,9},{9,8},{10,11... | collective-permute-start | bytes 393224 | tf_op jit(solution)/shard_map/ppermute | solution.py:307
  28.3 5.2 %collective-permute-start.11 = (bf16[128,512]{1,0:T(8,128)(2,1)S(1)}, bf16[128,512]{1,0:T(8,128)(2,1)S(1)}, u32[]{:S(2)}, u32[]{:S(2)}) collective-permute-start(bf16[128,512]{1,0:T(8,128)(2,1)S(1)} %get-tuple-element.45), channel_id=1, source_target_pairs={{0,2},{1,3},{2,0},{3,1},{4,6},{5,7},{6,4},{7,5},{8,10},{9,11},{10,... | collective-permute-start | bytes 393224 | tf_op jit(solution)/shard_map/ppermute | solution.py:307
  29.8 5.9 %collective-permute-start.12 = (bf16[128,512]{1,0:T(8,128)(2,1)S(1)}, bf16[128,512]{1,0:T(8,128)(2,1)S(1)}, u32[]{:S(2)}, u32[]{:S(2)}) collective-permute-start(bf16[128,512]{1,0:T(8,128)(2,1)S(1)} %get-tuple-element.46), channel_id=1, source_target_pairs={{0,3},{1,2},{2,1},{3,0},{4,7},{5,6},{6,5},{7,4},{8,11},{9,10},{10,... | collective-permute-start | bytes 393224 | tf_op jit(solution)/shard_map/ppermute | solution.py:307
  30.3 5.4 %collective-permute-start.13 = (bf16[128,512]{1,0:T(8,128)(2,1)S(1)}, bf16[128,512]{1,0:T(8,128)(2,1)S(1)}, u32[]{:S(2)}, u32[]{:S(2)}) collective-permute-start(bf16[128,512]{1,0:T(8,128)(2,1)S(1)} %get-tuple-element.47), channel_id=1, source_target_pairs={{0,4},{1,5},{2,6},{3,7},{4,0},{5,1},{6,2},{7,3},{8,12},{9,13},{10,... | collective-permute-start | bytes 393224 | tf_op jit(solution)/shard_map/ppermute | solution.py:307

commit v26 on v20

--- a/solution.py
+++ b/solution.py
@@ -13,6 +13,7 @@
 SPAN = 256
 PIECE = 32
 LATE = 16500
+PASSED = 1
 LOG2_E = math.log2(math.e)
 VMEM = pl.BlockSpec(memory_space=pltpu.VMEM)
 
@@ -132,7 +133,7 @@
         ref[...] = total[a * rows:(a + 1) * rows, :].astype(ref.dtype)
 
 
-def pair_terms(params, early, late, texts):
+def pair_terms(params, early, late, texts, image_types):
     rows, width = early[0].shape
     early_rows, late_rows = rows * len(early), rows * len(late)
     own, others = texts[0], texts[1:]
@@ -157,8 +158,7 @@
         functools.partial(rest_pairs_kernel, len(others)),
         [jax.ShapeDtypeStruct(own.shape, jnp.float32)]
         + [jax.ShapeDtypeStruct(t.shape, jnp.bfloat16) for t in others]
-        + [jax.ShapeDtypeStruct((rows, width), jnp.float32)]
-        + [jax.ShapeDtypeStruct((rows, width), jnp.bfloat16)] * (len(early) + len(late) - 1),
+        + [jax.ShapeDtypeStruct((rows, width), t) for t in image_types],
         [params, early_units, total, own, own_add, late_units, *others],
         name="rest_pairs",
         **cost(late_rows * own.shape[0] + (early_rows + late_rows) * other_rows),
@@ -187,6 +187,18 @@
         flops=len(parts) * parts[0].size,
         name="add_stacks",
     )
+
+
+def add_parts_kernel(*refs):
+    total = sum(ref[...].astype(jnp.float32) for ref in refs[:-1])
+    refs[-1][...] = total.astype(refs[-1].dtype)
+
+
+def add_parts(parts, weight):
+    out = jax.ShapeDtypeStruct(parts[0].shape, jnp.bfloat16)
+    return call(
+        add_parts_kernel, [out], parts, flops=weight * len(parts) * out.size, name="add_parts"
+    )[0]
 
 
 def finish_kernel(sides, image_ref, text_ref, *refs):
@@ -285,22 +297,31 @@
         near_rows = [units([texts], "own_units")] + [move(texts, near=n) for n in range(1, near_count)]
         own_stack = stack_units(near_rows)
         stacks = [own_stack] + [move(own_stack, grp=g) for g in range(1, grp_count)]
+        far_steps = [*early, *late]
+        image_types = [jnp.bfloat16 if w else jnp.float32 for _, w in far_steps]
         image_parts, text_parts = pair_terms(
-            params, list(early.values()), list(late.values()), stacks
-        )
-        far_parts = dict(zip([*early, *late], image_parts))
+            params, list(early.values()), list(late.values()), stacks, image_types
+        )
+        far_parts = dict(zip(far_steps, image_parts))
+        passed = [move(far_parts[step], low=-step[1]) for step in late]
         came = [move(part, grp=-g) for g, part in enumerate(text_parts) if g]
-        far_order = sorted((step for step in far_parts if step != (0, 0)), key=lambda step: step[0])
-        far_came = [move(far_parts[h, w], high=-h, low=-w) for h, w in far_order]
         near_parts = add_stacks([text_parts[0], *came], near_count)
-        near_parts = [near_parts[0]] + [
-            move(part, near=-n) for n, part in enumerate(near_parts) if n
-        ]
+        low_parts = [far_parts[0, w] for w in range(1, low_count)]
+        near_came = [move(part, near=-n) for n, part in enumerate(near_parts) if n]
+        passed, low_parts, kept, near_came[:1] = lax.optimization_barrier(
+            (passed, low_parts, near_parts[0], near_came[:1])
+        )
+        high_came = []
+        for h in range(1, high_count):
+            terms = [far_parts[h, 0]] + [p for step, p in zip(late, passed) if step[0] == h]
+            high_came.append(move(add_parts(terms, PASSED), high=-h))
+        low_came = [move(part, low=-w) for w, part in enumerate(low_parts, 1)]
         return finish(
             images,
             texts,
-            [(0, part) for part in [far_parts[0, 0]] + far_came]
-            + [(1, part) for part in near_parts],
+            [(0, far_parts[0, 0])]
+            + [(1, part) for part in [kept] + near_came]
+            + [(0, part) for part in high_came + low_came],
         )
 
     in_specs = (P(AXES, None), P(AXES, None), P(), P())

time: 34.3 us -> 36.5 us (1.064)
  waiting for transfers between devices: 6.55 us -> 10.2 us
  starting transfers between devices: 20.1 us -> 18.7 us
    ppermute x14, waiting for transfers between devices: 6.55 us -> 10.2 us  [move(): return lax.ppermute(value, AXES, perm)]
    ppermute x14, starting transfers between devices: 20.1 us -> 18.7 us  [move(): return lax.ppermute(value, AXES, perm)]
    pallas_call x6 -> x7, Pallas kernels: 3.31 us -> 3.32 us  [call(): pl.pallas_call(kernel, out_shape=out_shape, in_specs=[VMEM] * len(operand...]
  transfers between devices with their start and end apart: 14 -> 14, of which waited for: 7 -> 9; matrix products, arithmetic and copies ran while one was open for 0% -> 0% of each run, Pallas kernels for 5% -> 5%
where the time goes in v26:
time: 36.5 us; the launch traced here: 36.3 us
  starting transfers between devices  18.7 us (51%)
  waiting for transfers between devices  10.2 us (28%)
  Pallas kernels  4.38 us (12%)
  between operations  2.02 us (6%)
  local copies, waits for them, and re-layouts  0.91 us (2%)
    ppermute x14, starting transfers between devices, move(): return lax.ppermute(value, AXES, perm)  18.7 us
    ppermute x14, waiting for transfers between devices, move(): return lax.ppermute(value, AXES, perm)  10.2 us
    pallas_call x7, Pallas kernels, call(): pl.pallas_call(kernel, out_shape=out_shape, in_specs=[VMEM] * len(operand...  3.32 us
    pallas_call x1, Pallas kernels, finish(): pl.pallas_call(functools.partial(finish_kernel, [side for side, _ in part...  1.06 us
    unnamed x6, local copies, waits for them, and re-layouts  0.91 us
  transfers between devices with their start and end apart: 14, of which 9 were waited for; matrix products, arithmetic and copies ran while one was open for 0% of the time, Pallas kernels for 5%

profile of v26, /device:TPU:0, one launch (start us, length us, event | category | flops | bytes accessed | tf_op | source)
XLA Modules:
  0.0 36.3 jit_solution(15002314161829834956)
XLA Ops:
  0.6 4.1 %collective-permute-start = (bf16[128,512]{1,0:T(8,128)(2,1)}, bf16[128,512]{1,0:T(8,128)(2,1)S(1)}, u32[]{:S(2)}, u32[]{:S(2)}) collective-permute-start(bf16[128,512]{1,0:T(8,128)(2,1)} %image_ref.1), channel_id=1, source_target_pairs={{0,8},{1,9},{2,10},{3,11},{4,12},{5,13},{6,14},{7,15},{8,0},{9,1},... | collective-permute-start | bytes 393224 | tf_op jit(solution)/shard_map/ppermute | solution.py:281
  4.7 1.5 %collective-permute-start.2 = (bf16[128,512]{1,0:T(8,128)(2,1)}, bf16[128,512]{1,0:T(8,128)(2,1)S(1)}, u32[]{:S(2)}, u32[]{:S(2)}) collective-permute-start(bf16[128,512]{1,0:T(8,128)(2,1)} %text_ref.1), channel_id=1, source_target_pairs={{0,2},{1,3},{2,0},{3,1},{4,6},{5,7},{6,4},{7,5},{8,10},{9,11},{10,... | collective-permute-start | bytes 393224 | tf_op jit(solution)/shard_map/ppermute | solution.py:281
  6.3 1.5 %collective-permute-start.1 = (bf16[128,512]{1,0:T(8,128)(2,1)}, bf16[128,512]{1,0:T(8,128)(2,1)S(1)}, u32[]{:S(2)}, u32[]{:S(2)}) collective-permute-start(bf16[128,512]{1,0:T(8,128)(2,1)} %text_ref.1), channel_id=1, source_target_pairs={{0,1},{1,0},{2,3},{3,2},{4,5},{5,4},{6,7},{7,6},{8,9},{9,8},{10,11... | collective-permute-start | bytes 393224 | tf_op jit(solution)/shard_map/ppermute | solution.py:281
  7.7 0.5 %collective-permute-start.3 = (bf16[128,512]{1,0:T(8,128)(2,1)}, bf16[128,512]{1,0:T(8,128)(2,1)S(1)}, u32[]{:S(2)}, u32[]{:S(2)}) collective-permute-start(bf16[128,512]{1,0:T(8,128)(2,1)} %text_ref.1), channel_id=1, source_target_pairs={{0,3},{1,2},{2,1},{3,0},{4,7},{5,6},{6,5},{7,4},{8,11},{9,10},{10,... | collective-permute-start | bytes 393224 | tf_op jit(solution)/shard_map/ppermute | solution.py:281
  8.2 1.6 %collective-permute-start.4 = (bf16[128,512]{1,0:T(8,128)(2,1)}, bf16[128,512]{1,0:T(8,128)(2,1)S(1)}, u32[]{:S(2)}, u32[]{:S(2)}) collective-permute-start(bf16[128,512]{1,0:T(8,128)(2,1)} %image_ref.1), channel_id=1, source_target_pairs={{0,4},{1,5},{2,6},{3,7},{4,0},{5,1},{6,2},{7,3},{8,12},{9,13},{10,... | collective-permute-start | bytes 393224 | tf_op jit(solution)/shard_map/ppermute | solution.py:281
  11.4 0.8 %collective-permute-start.5 = (bf16[128,512]{1,0:T(8,128)(2,1)S(1)}, bf16[128,512]{1,0:T(8,128)(2,1)S(1)}, u32[]{:S(2)}, u32[]{:S(2)}) collective-permute-start(bf16[128,512]{1,0:T(8,128)(2,1)S(1)} %collective-permute-done.refs_1_), channel_id=1, source_target_pairs={{0,4},{1,5},{2,6},{3,7},{4,0},{5,1},{6,2},{7,3},{8,12},{9,13},{10,... | collective-permute-start | bytes 393224 | tf_op jit(solution)/shard_map/ppermute | solution.py:281
  12.1 0.9 %copy-done = bf16[128,512]{1,0:T(8,128)(2,1)S(1)} copy-done((bf16[128,512]{1,0:T(8,128)(2,1)S(1)}, bf16[128,512]{1,0:T(8,128)(2,1)}, u32[]{:S(2)}) %copy-start) | copy-done | bytes 131096
  13.2 1.0 %collective-permute-done.3.refs_3_ = bf16[128,512]{1,0:T(8,128)(2,1)S(1)} collective-permute-done((bf16[128,512]{1,0:T(8,128)(2,1)}, bf16[128,512]{1,0:T(8,128)(2,1)S(1)}, u32[]{:S(2)}, u32[]{:S(2)}) %collective-permute-start.3) | collective-permute-done | bytes 131104 | tf_op jit(solution)/shard_map/ppermute | solution.py:281
  14.4 0.4 %collective-permute-done.4.refs_2_ = bf16[128,512]{1,0:T(8,128)(2,1)S(1)} collective-permute-done((bf16[128,512]{1,0:T(8,128)(2,1)}, bf16[128,512]{1,0:T(8,128)(2,1)S(1)}, u32[]{:S(2)}, u32[]{:S(2)}) %collective-permute-start.4) | collective-permute-done | bytes 131104 | tf_op jit(solution)/shard_map/ppermute | solution.py:281
  14.9 1.1 %early_pairs.1 = (f32[512,512]{1,0:T(8,128)S(1)}, bf16[384,512]{1,0:T(8,128)(2,1)S(1)}, f32[384,512]{1,0:T(8,128)S(1)}) custom-call(f32[1,3]{1,0:T(1,128)S(1)} %maximum_bitcast_fusion.params_ref, bf16[512,512]{1,0:T(8,128)(2,1)S(1)} %stack_units.1.text_ref.own_text_ref, bf16[128,512]{1,0:T(8,128)(2,1)S(1)} %copy-done.2, ...), custom_call_target="tpu_custom_call" | custom-call | flops 603979776 | bytes 3145740 | tf_op jit(solution)/shard_map/early_pairs/pallas_call | solution.py:29
  16.0 0.9 %collective-permute-done.5.refs_0_ = bf16[128,512]{1,0:T(8,128)(2,1)S(1)} collective-permute-done((bf16[128,512]{1,0:T(8,128)(2,1)S(1)}, bf16[128,512]{1,0:T(8,128)(2,1)S(1)}, u32[]{:S(2)}, u32[]{:S(2)}) %collective-permute-start.5) | collective-permute-done | bytes 131104 | tf_op jit(solution)/shard_map/ppermute | solution.py:281
  17.0 1.7 %rest_pairs.1 = (f32[512,512]{1,0:T(8,128)S(1)}, bf16[512,512]{1,0:T(8,128)(2,1)S(1)}, f32[128,512]{1,0:T(8,128)S(1)}, f32[128,512]{1,0:T(8,128)S(1)}, bf16[128,...) custom-call(f32[1,3]{1,0:T(1,128)S(1)} %maximum_bitcast_fusion.params_ref, ...), custom_call_target="tpu_custom_call" | custom-call | flops 1006632960 | bytes 5767180 | tf_op jit(solution)/shard_map/rest_pairs/pallas_call | solution.py:29
  18.7 1.0 %collective-permute-start.7 = (bf16[128,512]{1,0:T(8,128)(2,1)S(1)}, bf16[128,512]{1,0:T(8,128)(2,1)S(1)}, u32[]{:S(2)}, u32[]{:S(2)}) collective-permute-start(bf16[128,512]{1,0:T(8,128)(2,1)S(1)} %get-tuple-element.27), channel_id=1, source_target_pairs={{0,4},{1,5},{2,6},{3,7},{4,0},{5,1},{6,2},{7,3},{8,12},{9,13},{10,... | collective-permute-start | bytes 393224 | tf_op jit(solution)/shard_map/ppermute | solution.py:281
  19.8 0.9 %collective-permute-done.8.refs_1_ = bf16[512,512]{1,0:T(8,128)(2,1)S(1)} collective-permute-done((bf16[512,512]{1,0:T(8,128)(2,1)S(1)}, bf16[512,512]{1,0:T(8,128)(2,1)S(1)}, u32[]{:S(2)}, u32[]{:S(2)}) %collective-permute-start.8) | collective-permute-done | bytes 524320 | tf_op jit(solution)/shard_map/ppermute | solution.py:281
  20.8 1.6 %collective-permute-start.9 = (bf16[128,512]{1,0:T(8,128)(2,1)S(1)}, bf16[128,512]{1,0:T(8,128)(2,1)S(1)}, u32[]{:S(2)}, u32[]{:S(2)}) collective-permute-start(bf16[128,512]{1,0:T(8,128)(2,1)S(1)} %get-tuple-element.32), channel_id=1, source_target_pairs={{0,1},{1,0},{2,3},{3,2},{4,5},{5,4},{6,7},{7,6},{8,9},{9,8},{10,11... | collective-permute-start | bytes 393224 | tf_op jit(solution)/shard_map/ppermute | solution.py:281
  22.4 1.5 %collective-permute-start.10 = (bf16[128,512]{1,0:T(8,128)(2,1)S(1)}, bf16[128,512]{1,0:T(8,128)(2,1)S(1)}, u32[]{:S(2)}, u32[]{:S(2)}) collective-permute-start(bf16[128,512]{1,0:T(8,128)(2,1)S(1)} %get-tuple-element.35), channel_id=1, source_target_pairs={{0,2},{1,3},{2,0},{3,1},{4,6},{5,7},{6,4},{7,5},{8,10},{9,11},{10,... | collective-permute-start | bytes 393224 | tf_op jit(solution)/shard_map/ppermute | solution.py:281
  23.9 0.4 %collective-permute-start.11 = (bf16[128,512]{1,0:T(8,128)(2,1)S(1)}, bf16[128,512]{1,0:T(8,128)(2,1)S(1)}, u32[]{:S(2)}, u32[]{:S(2)}) collective-permute-start(bf16[128,512]{1,0:T(8,128)(2,1)S(1)} %get-tuple-element.36), channel_id=1, source_target_pairs={{0,3},{1,2},{2,1},{3,0},{4,7},{5,6},{6,5},{7,4},{8,11},{9,10},{10,... | collective-permute-start | bytes 393224 | tf_op jit(solution)/shard_map/ppermute | solution.py:281
  24.3 0.3 collective-permute-done.7.refs_1_
  24.7 2.0 %collective-permute-done.9.refs_2_ = bf16[128,512]{1,0:T(8,128)(2,1)S(1)} collective-permute-done((bf16[128,512]{1,0:T(8,128)(2,1)S(1)}, bf16[128,512]{1,0:T(8,128)(2,1)S(1)}, u32[]{:S(2)}, u32[]{:S(2)}) %collective-permute-start.9) | collective-permute-done | bytes 131104 | tf_op jit(solution)/shard_map/ppermute | solution.py:281
  26.7 2.3 %collective-permute-start.12 = (bf16[128,512]{1,0:T(8,128)(2,1)S(1)}, bf16[128,512]{1,0:T(8,128)(2,1)S(1)}, u32[]{:S(2)}, u32[]{:S(2)}) collective-permute-start(bf16[128,512]{1,0:T(8,128)(2,1)S(1)} %add_parts.1), channel_id=1, source_target_pairs={{0,8},{1,9},{2,10},{3,11},{4,12},{5,13},{6,14},{7,15},{8,0},{9,1},... | collective-permute-start | bytes 393224 | tf_op jit(solution)/shard_map/ppermute | solution.py:281
  29.0 1.8 %collective-permute-start.13 = (bf16[128,512]{1,0:T(8,128)(2,1)S(1)}, bf16[128,512]{1,0:T(8,128)(2,1)S(1)}, u32[]{:S(2)}, u32[]{:S(2)}) collective-permute-start(bf16[128,512]{1,0:T(8,128)(2,1)S(1)} %get-tuple-element.39), channel_id=1, source_target_pairs={{0,4},{1,5},{2,6},{3,7},{4,0},{5,1},{6,2},{7,3},{8,12},{9,13},{10,... | collective-permute-start | bytes 393224 | tf_op jit(solution)/shard_map/ppermute | solution.py:281
  30.8 4.2 %collective-permute-done.12.refs_5_ = bf16[128,512]{1,0:T(8,128)(2,1)S(1)} collective-permute-done((bf16[128,512]{1,0:T(8,128)(2,1)S(1)}, bf16[128,512]{1,0:T(8,128)(2,1)S(1)}, u32[]{:S(2)}, u32[]{:S(2)}) %collective-permute-start.12) | collective-permute-done | bytes 131104 | tf_op jit(solution)/shard_map/ppermute | solution.py:281
  34.9 0.3 collective-permute-done.13.refs_6_
  35.3 1.1 %finish.1 = (f32[128,512]{1,0:T(8,128)}, f32[128,512]{1,0:T(8,128)}) custom-call(bf16[128,512]{1,0:T(8,128)(2,1)S(1)} %copy-done.2, bf16[128,512]{1,0:T(8,128)(2,1)S(1)} %copy-done.1, f32[128,512]{1,0:T(8,128)S(1)} %get-tuple-element.26.refs_0_, f32[128,512]{1,0:T(8,128)S(1)} %get-tuple-element.33.refs_1_, ...), custom_call_target="tpu_custom_call" | custom-call | flops 4587520 | bytes 1376256 | tf_op jit(solution)/shard_map/finish/pallas_call | solution.py:231
  (19 shorter events, 1.0 us)
Async XLA Ops:
  0.6 10.7 %collective-permute-start = (bf16[128,512]{1,0:T(8,128)(2,1)}, bf16[128,512]{1,0:T(8,128)(2,1)S(1)}, u32[]{:S(2)}, u32[]{:S(2)}) collective-permute-start(bf16[128,512]{1,0:T(8,128)(2,1)} %image_ref.1), channel_id=1, source_target_pairs={{0,8},{1,9},{2,10},{3,11},{4,12},{5,13},{6,14},{7,15},{8,0},{9,1},... | collective-permute-start | bytes 393224 | tf_op jit(solution)/shard_map/ppermute | solution.py:281
  4.7 8.4 %collective-permute-start.2 = (bf16[128,512]{1,0:T(8,128)(2,1)}, bf16[128,512]{1,0:T(8,128)(2,1)S(1)}, u32[]{:S(2)}, u32[]{:S(2)}) collective-permute-start(bf16[128,512]{1,0:T(8,128)(2,1)} %text_ref.1), channel_id=1, source_target_pairs={{0,2},{1,3},{2,0},{3,1},{4,6},{5,7},{6,4},{7,5},{8,10},{9,11},{10,... | collective-permute-start | bytes 393224 | tf_op jit(solution)/shard_map/ppermute | solution.py:281
  6.3 6.9 %collective-permute-start.1 = (bf16[128,512]{1,0:T(8,128)(2,1)}, bf16[128,512]{1,0:T(8,128)(2,1)S(1)}, u32[]{:S(2)}, u32[]{:S(2)}) collective-permute-start(bf16[128,512]{1,0:T(8,128)(2,1)} %text_ref.1), channel_id=1, source_target_pairs={{0,1},{1,0},{2,3},{3,2},{4,5},{5,4},{6,7},{7,6},{8,9},{9,8},{10,11... | collective-permute-start | bytes 393224 | tf_op jit(solution)/shard_map/ppermute | solution.py:281
  7.7 6.4 %collective-permute-start.3 = (bf16[128,512]{1,0:T(8,128)(2,1)}, bf16[128,512]{1,0:T(8,128)(2,1)S(1)}, u32[]{:S(2)}, u32[]{:S(2)}) collective-permute-start(bf16[128,512]{1,0:T(8,128)(2,1)} %text_ref.1), channel_id=1, source_target_pairs={{0,3},{1,2},{2,1},{3,0},{4,7},{5,6},{6,5},{7,4},{8,11},{9,10},{10,... | collective-permute-start | bytes 393224 | tf_op jit(solution)/shard_map/ppermute | solution.py:281
  8.2 6.6 %collective-permute-start.4 = (bf16[128,512]{1,0:T(8,128)(2,1)}, bf16[128,512]{1,0:T(8,128)(2,1)S(1)}, u32[]{:S(2)}, u32[]{:S(2)}) collective-permute-start(bf16[128,512]{1,0:T(8,128)(2,1)} %image_ref.1), channel_id=1, source_target_pairs={{0,4},{1,5},{2,6},{3,7},{4,0},{5,1},{6,2},{7,3},{8,12},{9,13},{10,... | collective-permute-start | bytes 393224 | tf_op jit(solution)/shard_map/ppermute | solution.py:281
  11.4 5.5 %collective-permute-start.5 = (bf16[128,512]{1,0:T(8,128)(2,1)S(1)}, bf16[128,512]{1,0:T(8,128)(2,1)S(1)}, u32[]{:S(2)}, u32[]{:S(2)}) collective-permute-start(bf16[128,512]{1,0:T(8,128)(2,1)S(1)} %collective-permute-done.refs_1_), channel_id=1, source_target_pairs={{0,4},{1,5},{2,6},{3,7},{4,0},{5,1},{6,2},{7,3},{8,12},{9,13},{10,... | collective-permute-start | bytes 393224 | tf_op jit(solution)/shard_map/ppermute | solution.py:281
  12.1 0.9 %copy-start = (bf16[128,512]{1,0:T(8,128)(2,1)S(1)}, bf16[128,512]{1,0:T(8,128)(2,1)}, u32[]{:S(2)}) copy-start(bf16[128,512]{1,0:T(8,128)(2,1)} %text_ref.1) | copy-start | bytes 393220
  13.1 1.7 %copy-start.2 = (bf16[128,512]{1,0:T(8,128)(2,1)S(1)}, bf16[128,512]{1,0:T(8,128)(2,1)}, u32[]{:S(2)}) copy-start(bf16[128,512]{1,0:T(8,128)(2,1)} %image_ref.1) | copy-start | bytes 393220
  14.3 2.6 %collective-permute-start.6 = (bf16[512,512]{1,0:T(8,128)(2,1)S(1)}, bf16[512,512]{1,0:T(8,128)(2,1)S(1)}, u32[]{:S(2)}, u32[]{:S(2)}) collective-permute-start(bf16[512,512]{1,0:T(8,128)(2,1)S(1)} %stack_units.1.text_ref.own_text_ref), channel_id=1, source_target_pairs={{0,16},{1,17},{2,18},{3,19},{4,20},{5,21},{6,22},{7,23},{8,24},{9,... | collective-permute-start | bytes 1572872 | tf_op jit(solution)/shard_map/ppermute | solution.py:281
  18.7 2.0 %collective-permute-start.8 = (bf16[512,512]{1,0:T(8,128)(2,1)S(1)}, bf16[512,512]{1,0:T(8,128)(2,1)S(1)}, u32[]{:S(2)}, u32[]{:S(2)}) collective-permute-start(bf16[512,512]{1,0:T(8,128)(2,1)S(1)} %get-tuple-element.30), channel_id=1, source_target_pairs={{0,16},{1,17},{2,18},{3,19},{4,20},{5,21},{6,22},{7,23},{8,24},{9,... | collective-permute-start | bytes 1572872 | tf_op jit(solution)/shard_map/ppermute | solution.py:281
  18.7 5.9 %collective-permute-start.7 = (bf16[128,512]{1,0:T(8,128)(2,1)S(1)}, bf16[128,512]{1,0:T(8,128)(2,1)S(1)}, u32[]{:S(2)}, u32[]{:S(2)}) collective-permute-start(bf16[128,512]{1,0:T(8,128)(2,1)S(1)} %get-tuple-element.27), channel_id=1, source_target_pairs={{0,4},{1,5},{2,6},{3,7},{4,0},{5,1},{6,2},{7,3},{8,12},{9,13},{10,... | collective-permute-start | bytes 393224 | tf_op jit(solution)/shard_map/ppermute | solution.py:281
  20.8 5.9 %collective-permute-start.9 = (bf16[128,512]{1,0:T(8,128)(2,1)S(1)}, bf16[128,512]{1,0:T(8,128)(2,1)S(1)}, u32[]{:S(2)}, u32[]{:S(2)}) collective-permute-start(bf16[128,512]{1,0:T(8,128)(2,1)S(1)} %get-tuple-element.32), channel_id=1, source_target_pairs={{0,1},{1,0},{2,3},{3,2},{4,5},{5,4},{6,7},{7,6},{8,9},{9,8},{10,11... | collective-permute-start | bytes 393224 | tf_op jit(solution)/shard_map/ppermute | solution.py:281
  22.4 8.4 %collective-permute-start.10 = (bf16[128,512]{1,0:T(8,128)(2,1)S(1)}, bf16[128,512]{1,0:T(8,128)(2,1)S(1)}, u32[]{:S(2)}, u32[]{:S(2)}) collective-permute-start(bf16[128,512]{1,0:T(8,128)(2,1)S(1)} %get-tuple-element.35), channel_id=1, source_target_pairs={{0,2},{1,3},{2,0},{3,1},{4,6},{5,7},{6,4},{7,5},{8,10},{9,11},{10,... | collective-permute-start | bytes 393224 | tf_op jit(solution)/shard_map/ppermute | solution.py:281
  23.9 6.9 %collective-permute-start.11 = (bf16[128,512]{1,0:T(8,128)(2,1)S(1)}, bf16[128,512]{1,0:T(8,128)(2,1)S(1)}, u32[]{:S(2)}, u32[]{:S(2)}) collective-permute-start(bf16[128,512]{1,0:T(8,128)(2,1)S(1)} %get-tuple-element.36), channel_id=1, source_target_pairs={{0,3},{1,2},{2,1},{3,0},{4,7},{5,6},{6,5},{7,4},{8,11},{9,10},{10,... | collective-permute-start | bytes 393224 | tf_op jit(solution)/shard_map/ppermute | solution.py:281
  26.7 8.6 %copy-start.1 = (bf16[128,512]{1,0:T(8,128)(2,1)S(1)}, bf16[128,512]{1,0:T(8,128)(2,1)}, u32[]{:S(2)}) copy-start(bf16[128,512]{1,0:T(8,128)(2,1)} %text_ref.1) | copy-start | bytes 393220
  26.7 8.2 %collective-permute-start.12 = (bf16[128,512]{1,0:T(8,128)(2,1)S(1)}, bf16[128,512]{1,0:T(8,128)(2,1)S(1)}, u32[]{:S(2)}, u32[]{:S(2)}) collective-permute-start(bf16[128,512]{1,0:T(8,128)(2,1)S(1)} %add_parts.1), channel_id=1, source_target_pairs={{0,8},{1,9},{2,10},{3,11},{4,12},{5,13},{6,14},{7,15},{8,0},{9,1},... | collective-permute-start | bytes 393224 | tf_op jit(solution)/shard_map/ppermute | solution.py:281
  29.0 6.3 %collective-permute-start.13 = (bf16[128,512]{1,0:T(8,128)(2,1)S(1)}, bf16[128,512]{1,0:T(8,128)(2,1)S(1)}, u32[]{:S(2)}, u32[]{:S(2)}) collective-permute-start(bf16[128,512]{1,0:T(8,128)(2,1)S(1)} %get-tuple-element.39), channel_id=1, source_target_pairs={{0,4},{1,5},{2,6},{3,7},{4,0},{5,1},{6,2},{7,3},{8,12},{9,13},{10,... | collective-permute-start | bytes 393224 | tf_op jit(solution)/shard_map/ppermute | solution.py:281

commit v27 on v26

--- a/solution.py
+++ b/solution.py
@@ -13,7 +13,7 @@
 SPAN = 256
 PIECE = 32
 LATE = 16500
-PASSED = 1
+NEAR = 30000
 LOG2_E = math.log2(math.e)
 VMEM = pl.BlockSpec(memory_space=pltpu.VMEM)
 
@@ -194,10 +194,10 @@
     refs[-1][...] = total.astype(refs[-1].dtype)
 
 
-def add_parts(parts, weight):
-    out = jax.ShapeDtypeStruct(parts[0].shape, jnp.bfloat16)
+def add_parts(parts, dtype, weight, name):
+    out = jax.ShapeDtypeStruct(parts[0].shape, dtype)
     return call(
-        add_parts_kernel, [out], parts, flops=weight * len(parts) * out.size, name="add_parts"
+        add_parts_kernel, [out], parts, flops=weight * len(parts) * out.size, name=name
     )[0]
 
 
@@ -308,20 +308,18 @@
         near_parts = add_stacks([text_parts[0], *came], near_count)
         low_parts = [far_parts[0, w] for w in range(1, low_count)]
         near_came = [move(part, near=-n) for n, part in enumerate(near_parts) if n]
-        passed, low_parts, kept, near_came[:1] = lax.optimization_barrier(
-            (passed, low_parts, near_parts[0], near_came[:1])
-        )
         high_came = []
         for h in range(1, high_count):
             terms = [far_parts[h, 0]] + [p for step, p in zip(late, passed) if step[0] == h]
-            high_came.append(move(add_parts(terms, PASSED), high=-h))
+            both = add_parts(terms, jnp.bfloat16, 1, "add_passed")
+            both, low_parts = lax.optimization_barrier((both, low_parts))
+            high_came.append(move(both, high=-h))
         low_came = [move(part, low=-w) for w, part in enumerate(low_parts, 1)]
         return finish(
             images,
             texts,
-            [(0, far_parts[0, 0])]
-            + [(1, part) for part in [kept] + near_came]
-            + [(0, part) for part in high_came + low_came],
+            [(1, add_parts([near_parts[0], *near_came], jnp.float32, NEAR, "add_near"))]
+            + [(0, part) for part in [far_parts[0, 0]] + high_came + low_came],
         )
 
     in_specs = (P(AXES, None), P(AXES, None), P(), P())

time: 36.5 us -> 35.1 us (0.962)
  waiting for transfers between devices: 10.2 us -> 8.83 us
    ppermute x14, waiting for transfers between devices: 10.2 us -> 8.83 us  [move(): return lax.ppermute(value, AXES, perm)]
    pallas_call x7 -> x8, Pallas kernels: 3.32 us -> 3.37 us  [call(): pl.pallas_call(kernel, out_shape=out_shape, in_specs=[VMEM] * len(operand...]
where the time goes in v27:
time: 35.1 us; the launch traced here: 34.9 us
  starting transfers between devices  18.7 us (53%)
  waiting for transfers between devices  8.83 us (25%)
  Pallas kernels  4.4 us (13%)
  between operations  2.02 us (6%)
  local copies, waits for them, and re-layouts  0.91 us (3%)
    ppermute x14, starting transfers between devices, move(): return lax.ppermute(value, AXES, perm)  18.7 us
    ppermute x14, waiting for transfers between devices, move(): return lax.ppermute(value, AXES, perm)  8.83 us
    pallas_call x8, Pallas kernels, call(): pl.pallas_call(kernel, out_shape=out_shape, in_specs=[VMEM] * len(operand...  3.37 us
    pallas_call x1, Pallas kernels, finish(): pl.pallas_call(functools.partial(finish_kernel, [side for side, _ in part...  1.03 us
    unnamed x6, local copies, waits for them, and re-layouts  0.91 us
  transfers between devices with their start and end apart: 14, of which 9 were waited for; matrix products, arithmetic and copies ran while one was open for 0% of the time, Pallas kernels for 5%

profile of v27, /device:TPU:0, one launch (start us, length us, event | category | flops | bytes accessed | tf_op | source)
XLA Modules:
  0.0 34.9 jit_solution(8700345504588925109)
XLA Ops:
  0.6 4.1 %collective-permute-start = (bf16[128,512]{1,0:T(8,128)(2,1)}, bf16[128,512]{1,0:T(8,128)(2,1)S(1)}, u32[]{:S(2)}, u32[]{:S(2)}) collective-permute-start(bf16[128,512]{1,0:T(8,128)(2,1)} %image_ref.1), channel_id=1, source_target_pairs={{0,8},{1,9},{2,10},{3,11},{4,12},{5,13},{6,14},{7,15},{8,0},{9,1},... | collective-permute-start | bytes 393224 | tf_op jit(solution)/shard_map/ppermute | solution.py:281
  4.7 1.5 %collective-permute-start.2 = (bf16[128,512]{1,0:T(8,128)(2,1)}, bf16[128,512]{1,0:T(8,128)(2,1)S(1)}, u32[]{:S(2)}, u32[]{:S(2)}) collective-permute-start(bf16[128,512]{1,0:T(8,128)(2,1)} %text_ref.1), channel_id=1, source_target_pairs={{0,2},{1,3},{2,0},{3,1},{4,6},{5,7},{6,4},{7,5},{8,10},{9,11},{10,... | collective-permute-start | bytes 393224 | tf_op jit(solution)/shard_map/ppermute | solution.py:281
  6.3 1.5 %collective-permute-start.1 = (bf16[128,512]{1,0:T(8,128)(2,1)}, bf16[128,512]{1,0:T(8,128)(2,1)S(1)}, u32[]{:S(2)}, u32[]{:S(2)}) collective-permute-start(bf16[128,512]{1,0:T(8,128)(2,1)} %text_ref.1), channel_id=1, source_target_pairs={{0,1},{1,0},{2,3},{3,2},{4,5},{5,4},{6,7},{7,6},{8,9},{9,8},{10,11... | collective-permute-start | bytes 393224 | tf_op jit(solution)/shard_map/ppermute | solution.py:281
  7.7 0.5 %collective-permute-start.3 = (bf16[128,512]{1,0:T(8,128)(2,1)}, bf16[128,512]{1,0:T(8,128)(2,1)S(1)}, u32[]{:S(2)}, u32[]{:S(2)}) collective-permute-start(bf16[128,512]{1,0:T(8,128)(2,1)} %text_ref.1), channel_id=1, source_target_pairs={{0,3},{1,2},{2,1},{3,0},{4,7},{5,6},{6,5},{7,4},{8,11},{9,10},{10,... | collective-permute-start | bytes 393224 | tf_op jit(solution)/shard_map/ppermute | solution.py:281
  8.2 1.6 %collective-permute-start.4 = (bf16[128,512]{1,0:T(8,128)(2,1)}, bf16[128,512]{1,0:T(8,128)(2,1)S(1)}, u32[]{:S(2)}, u32[]{:S(2)}) collective-permute-start(bf16[128,512]{1,0:T(8,128)(2,1)} %image_ref.1), channel_id=1, source_target_pairs={{0,4},{1,5},{2,6},{3,7},{4,0},{5,1},{6,2},{7,3},{8,12},{9,13},{10,... | collective-permute-start | bytes 393224 | tf_op jit(solution)/shard_map/ppermute | solution.py:281
  11.4 0.8 %collective-permute-start.5 = (bf16[128,512]{1,0:T(8,128)(2,1)S(1)}, bf16[128,512]{1,0:T(8,128)(2,1)S(1)}, u32[]{:S(2)}, u32[]{:S(2)}) collective-permute-start(bf16[128,512]{1,0:T(8,128)(2,1)S(1)} %collective-permute-done.refs_1_), channel_id=1, source_target_pairs={{0,4},{1,5},{2,6},{3,7},{4,0},{5,1},{6,2},{7,3},{8,12},{9,13},{10,... | collective-permute-start | bytes 393224 | tf_op jit(solution)/shard_map/ppermute | solution.py:281
  12.1 0.9 %copy-done = bf16[128,512]{1,0:T(8,128)(2,1)S(1)} copy-done((bf16[128,512]{1,0:T(8,128)(2,1)S(1)}, bf16[128,512]{1,0:T(8,128)(2,1)}, u32[]{:S(2)}) %copy-start) | copy-done | bytes 131096
  13.2 1.0 %collective-permute-done.3.refs_3_ = bf16[128,512]{1,0:T(8,128)(2,1)S(1)} collective-permute-done((bf16[128,512]{1,0:T(8,128)(2,1)}, bf16[128,512]{1,0:T(8,128)(2,1)S(1)}, u32[]{:S(2)}, u32[]{:S(2)}) %collective-permute-start.3) | collective-permute-done | bytes 131104 | tf_op jit(solution)/shard_map/ppermute | solution.py:281
  14.4 0.4 %collective-permute-done.4.refs_2_ = bf16[128,512]{1,0:T(8,128)(2,1)S(1)} collective-permute-done((bf16[128,512]{1,0:T(8,128)(2,1)}, bf16[128,512]{1,0:T(8,128)(2,1)S(1)}, u32[]{:S(2)}, u32[]{:S(2)}) %collective-permute-start.4) | collective-permute-done | bytes 131104 | tf_op jit(solution)/shard_map/ppermute | solution.py:281
  14.9 1.1 %early_pairs.1 = (f32[512,512]{1,0:T(8,128)S(1)}, bf16[384,512]{1,0:T(8,128)(2,1)S(1)}, f32[384,512]{1,0:T(8,128)S(1)}) custom-call(f32[1,3]{1,0:T(1,128)S(1)} %maximum_bitcast_fusion.params_ref, bf16[512,512]{1,0:T(8,128)(2,1)S(1)} %stack_units.1.text_ref.own_text_ref, bf16[128,512]{1,0:T(8,128)(2,1)S(1)} %copy-done.2, ...), custom_call_target="tpu_custom_call" | custom-call | flops 603979776 | bytes 3145740 | tf_op jit(solution)/shard_map/early_pairs/pallas_call | solution.py:29
  16.0 0.9 %collective-permute-done.5.refs_0_ = bf16[128,512]{1,0:T(8,128)(2,1)S(1)} collective-permute-done((bf16[128,512]{1,0:T(8,128)(2,1)S(1)}, bf16[128,512]{1,0:T(8,128)(2,1)S(1)}, u32[]{:S(2)}, u32[]{:S(2)}) %collective-permute-start.5) | collective-permute-done | bytes 131104 | tf_op jit(solution)/shard_map/ppermute | solution.py:281
  17.0 1.7 %rest_pairs.1 = (f32[512,512]{1,0:T(8,128)S(1)}, bf16[512,512]{1,0:T(8,128)(2,1)S(1)}, f32[128,512]{1,0:T(8,128)S(1)}, f32[128,512]{1,0:T(8,128)S(1)}, bf16[128,...) custom-call(f32[1,3]{1,0:T(1,128)S(1)} %maximum_bitcast_fusion.params_ref, ...), custom_call_target="tpu_custom_call" | custom-call | flops 1006632960 | bytes 5767180 | tf_op jit(solution)/shard_map/rest_pairs/pallas_call | solution.py:29
  18.7 1.0 %collective-permute-start.11 = (bf16[128,512]{1,0:T(8,128)(2,1)S(1)}, bf16[128,512]{1,0:T(8,128)(2,1)S(1)}, u32[]{:S(2)}, u32[]{:S(2)}) collective-permute-start(bf16[128,512]{1,0:T(8,128)(2,1)S(1)} %get-tuple-element.32), channel_id=1, source_target_pairs={{0,4},{1,5},{2,6},{3,7},{4,0},{5,1},{6,2},{7,3},{8,12},{9,13},{10,... | collective-permute-start | bytes 393224 | tf_op jit(solution)/shard_map/ppermute | solution.py:281
  19.8 0.9 %collective-permute-done.7.refs_1_ = bf16[512,512]{1,0:T(8,128)(2,1)S(1)} collective-permute-done((bf16[512,512]{1,0:T(8,128)(2,1)S(1)}, bf16[512,512]{1,0:T(8,128)(2,1)S(1)}, u32[]{:S(2)}, u32[]{:S(2)}) %collective-permute-start.7) | collective-permute-done | bytes 524320 | tf_op jit(solution)/shard_map/ppermute | solution.py:281
  20.8 1.6 %collective-permute-start.8 = (bf16[128,512]{1,0:T(8,128)(2,1)S(1)}, bf16[128,512]{1,0:T(8,128)(2,1)S(1)}, u32[]{:S(2)}, u32[]{:S(2)}) collective-permute-start(bf16[128,512]{1,0:T(8,128)(2,1)S(1)} %get-tuple-element.27), channel_id=1, source_target_pairs={{0,1},{1,0},{2,3},{3,2},{4,5},{5,4},{6,7},{7,6},{8,9},{9,8},{10,11... | collective-permute-start | bytes 393224 | tf_op jit(solution)/shard_map/ppermute | solution.py:281
  22.4 1.5 %collective-permute-start.9 = (bf16[128,512]{1,0:T(8,128)(2,1)S(1)}, bf16[128,512]{1,0:T(8,128)(2,1)S(1)}, u32[]{:S(2)}, u32[]{:S(2)}) collective-permute-start(bf16[128,512]{1,0:T(8,128)(2,1)S(1)} %get-tuple-element.28), channel_id=1, source_target_pairs={{0,2},{1,3},{2,0},{3,1},{4,6},{5,7},{6,4},{7,5},{8,10},{9,11},{10,... | collective-permute-start | bytes 393224 | tf_op jit(solution)/shard_map/ppermute | solution.py:281
  23.9 0.4 %collective-permute-start.10 = (bf16[128,512]{1,0:T(8,128)(2,1)S(1)}, bf16[128,512]{1,0:T(8,128)(2,1)S(1)}, u32[]{:S(2)}, u32[]{:S(2)}) collective-permute-start(bf16[128,512]{1,0:T(8,128)(2,1)S(1)} %get-tuple-element.29), channel_id=1, source_target_pairs={{0,3},{1,2},{2,1},{3,0},{4,7},{5,6},{6,5},{7,4},{8,11},{9,10},{10,... | collective-permute-start | bytes 393224 | tf_op jit(solution)/shard_map/ppermute | solution.py:281
  24.3 0.3 collective-permute-done.11.refs_1_
  24.7 2.3 %collective-permute-start.12 = (bf16[128,512]{1,0:T(8,128)(2,1)S(1)}, bf16[128,512]{1,0:T(8,128)(2,1)S(1)}, u32[]{:S(2)}, u32[]{:S(2)}) collective-permute-start(bf16[128,512]{1,0:T(8,128)(2,1)S(1)} %add_passed.1), channel_id=1, source_target_pairs={{0,8},{1,9},{2,10},{3,11},{4,12},{5,13},{6,14},{7,15},{8,0},{9,1},... | collective-permute-start | bytes 393224 | tf_op jit(solution)/shard_map/ppermute | solution.py:281
  27.0 1.7 %collective-permute-start.13 = (bf16[128,512]{1,0:T(8,128)(2,1)S(1)}, bf16[128,512]{1,0:T(8,128)(2,1)S(1)}, u32[]{:S(2)}, u32[]{:S(2)}) collective-permute-start(bf16[128,512]{1,0:T(8,128)(2,1)S(1)} %get-tuple-element.35), channel_id=1, source_target_pairs={{0,4},{1,5},{2,6},{3,7},{4,0},{5,1},{6,2},{7,3},{8,12},{9,13},{10,... | collective-permute-start | bytes 393224 | tf_op jit(solution)/shard_map/ppermute | solution.py:281
  28.7 1.7 %collective-permute-done.9.refs_2_ = bf16[128,512]{1,0:T(8,128)(2,1)S(1)} collective-permute-done((bf16[128,512]{1,0:T(8,128)(2,1)S(1)}, bf16[128,512]{1,0:T(8,128)(2,1)S(1)}, u32[]{:S(2)}, u32[]{:S(2)}) %collective-permute-start.9) | collective-permute-done | bytes 131104 | tf_op jit(solution)/shard_map/ppermute | solution.py:281
  30.5 3.1 %collective-permute-done.12.refs_2_ = bf16[128,512]{1,0:T(8,128)(2,1)S(1)} collective-permute-done((bf16[128,512]{1,0:T(8,128)(2,1)S(1)}, bf16[128,512]{1,0:T(8,128)(2,1)S(1)}, u32[]{:S(2)}, u32[]{:S(2)}) %collective-permute-start.12) | collective-permute-done | bytes 131104 | tf_op jit(solution)/shard_map/ppermute | solution.py:281
  33.6 0.3 collective-permute-done.13.refs_3_
  33.9 1.0 %finish.1 = (f32[128,512]{1,0:T(8,128)}, f32[128,512]{1,0:T(8,128)}) custom-call(bf16[128,512]{1,0:T(8,128)(2,1)S(1)} %copy-done.2, bf16[128,512]{1,0:T(8,128)(2,1)S(1)} %copy-done.1, f32[128,512]{1,0:T(8,128)S(1)} %add_near.1.refs_0_, f32[128,512]{1,0:T(8,128)S(1)} %get-tuple-element.30.refs_1_, bf16[128,512]{1,0:T(8,128)(2,1)S(1)} %collective-permute-done.12.refs_2_, ...), custom_call_target="tpu_custom_call" | custom-call | flops 2621440 | bytes 786432 | tf_op jit(solution)/shard_map/finish/pallas_call | solution.py:231
  (20 shorter events, 1.0 us)
Async XLA Ops:
  0.6 10.7 %collective-permute-start = (bf16[128,512]{1,0:T(8,128)(2,1)}, bf16[128,512]{1,0:T(8,128)(2,1)S(1)}, u32[]{:S(2)}, u32[]{:S(2)}) collective-permute-start(bf16[128,512]{1,0:T(8,128)(2,1)} %image_ref.1), channel_id=1, source_target_pairs={{0,8},{1,9},{2,10},{3,11},{4,12},{5,13},{6,14},{7,15},{8,0},{9,1},... | collective-permute-start | bytes 393224 | tf_op jit(solution)/shard_map/ppermute | solution.py:281
  4.7 8.4 %collective-permute-start.2 = (bf16[128,512]{1,0:T(8,128)(2,1)}, bf16[128,512]{1,0:T(8,128)(2,1)S(1)}, u32[]{:S(2)}, u32[]{:S(2)}) collective-permute-start(bf16[128,512]{1,0:T(8,128)(2,1)} %text_ref.1), channel_id=1, source_target_pairs={{0,2},{1,3},{2,0},{3,1},{4,6},{5,7},{6,4},{7,5},{8,10},{9,11},{10,... | collective-permute-start | bytes 393224 | tf_op jit(solution)/shard_map/ppermute | solution.py:281
  6.3 6.9 %collective-permute-start.1 = (bf16[128,512]{1,0:T(8,128)(2,1)}, bf16[128,512]{1,0:T(8,128)(2,1)S(1)}, u32[]{:S(2)}, u32[]{:S(2)}) collective-permute-start(bf16[128,512]{1,0:T(8,128)(2,1)} %text_ref.1), channel_id=1, source_target_pairs={{0,1},{1,0},{2,3},{3,2},{4,5},{5,4},{6,7},{7,6},{8,9},{9,8},{10,11... | collective-permute-start | bytes 393224 | tf_op jit(solution)/shard_map/ppermute | solution.py:281
  7.7 6.4 %collective-permute-start.3 = (bf16[128,512]{1,0:T(8,128)(2,1)}, bf16[128,512]{1,0:T(8,128)(2,1)S(1)}, u32[]{:S(2)}, u32[]{:S(2)}) collective-permute-start(bf16[128,512]{1,0:T(8,128)(2,1)} %text_ref.1), channel_id=1, source_target_pairs={{0,3},{1,2},{2,1},{3,0},{4,7},{5,6},{6,5},{7,4},{8,11},{9,10},{10,... | collective-permute-start | bytes 393224 | tf_op jit(solution)/shard_map/ppermute | solution.py:281
  8.2 6.6 %collective-permute-start.4 = (bf16[128,512]{1,0:T(8,128)(2,1)}, bf16[128,512]{1,0:T(8,128)(2,1)S(1)}, u32[]{:S(2)}, u32[]{:S(2)}) collective-permute-start(bf16[128,512]{1,0:T(8,128)(2,1)} %image_ref.1), channel_id=1, source_target_pairs={{0,4},{1,5},{2,6},{3,7},{4,0},{5,1},{6,2},{7,3},{8,12},{9,13},{10,... | collective-permute-start | bytes 393224 | tf_op jit(solution)/shard_map/ppermute | solution.py:281
  11.4 5.5 %collective-permute-start.5 = (bf16[128,512]{1,0:T(8,128)(2,1)S(1)}, bf16[128,512]{1,0:T(8,128)(2,1)S(1)}, u32[]{:S(2)}, u32[]{:S(2)}) collective-permute-start(bf16[128,512]{1,0:T(8,128)(2,1)S(1)} %collective-permute-done.refs_1_), channel_id=1, source_target_pairs={{0,4},{1,5},{2,6},{3,7},{4,0},{5,1},{6,2},{7,3},{8,12},{9,13},{10,... | collective-permute-start | bytes 393224 | tf_op jit(solution)/shard_map/ppermute | solution.py:281
  12.1 0.9 %copy-start = (bf16[128,512]{1,0:T(8,128)(2,1)S(1)}, bf16[128,512]{1,0:T(8,128)(2,1)}, u32[]{:S(2)}) copy-start(bf16[128,512]{1,0:T(8,128)(2,1)} %text_ref.1) | copy-start | bytes 393220
  13.1 1.7 %copy-start.2 = (bf16[128,512]{1,0:T(8,128)(2,1)S(1)}, bf16[128,512]{1,0:T(8,128)(2,1)}, u32[]{:S(2)}) copy-start(bf16[128,512]{1,0:T(8,128)(2,1)} %image_ref.1) | copy-start | bytes 393220
  14.3 2.6 %collective-permute-start.6 = (bf16[512,512]{1,0:T(8,128)(2,1)S(1)}, bf16[512,512]{1,0:T(8,128)(2,1)S(1)}, u32[]{:S(2)}, u32[]{:S(2)}) collective-permute-start(bf16[512,512]{1,0:T(8,128)(2,1)S(1)} %stack_units.1.text_ref.own_text_ref), channel_id=1, source_target_pairs={{0,16},{1,17},{2,18},{3,19},{4,20},{5,21},{6,22},{7,23},{8,24},{9,... | collective-permute-start | bytes 1572872 | tf_op jit(solution)/shard_map/ppermute | solution.py:281
  18.7 2.0 %collective-permute-start.7 = (bf16[512,512]{1,0:T(8,128)(2,1)S(1)}, bf16[512,512]{1,0:T(8,128)(2,1)S(1)}, u32[]{:S(2)}, u32[]{:S(2)}) collective-permute-start(bf16[512,512]{1,0:T(8,128)(2,1)S(1)} %get-tuple-element.25), channel_id=1, source_target_pairs={{0,16},{1,17},{2,18},{3,19},{4,20},{5,21},{6,22},{7,23},{8,24},{9,... | collective-permute-start | bytes 1572872 | tf_op jit(solution)/shard_map/ppermute | solution.py:281
  18.7 5.9 %collective-permute-start.11 = (bf16[128,512]{1,0:T(8,128)(2,1)S(1)}, bf16[128,512]{1,0:T(8,128)(2,1)S(1)}, u32[]{:S(2)}, u32[]{:S(2)}) collective-permute-start(bf16[128,512]{1,0:T(8,128)(2,1)S(1)} %get-tuple-element.32), channel_id=1, source_target_pairs={{0,4},{1,5},{2,6},{3,7},{4,0},{5,1},{6,2},{7,3},{8,12},{9,13},{10,... | collective-permute-start | bytes 393224 | tf_op jit(solution)/shard_map/ppermute | solution.py:281
  20.8 8.0 %collective-permute-start.8 = (bf16[128,512]{1,0:T(8,128)(2,1)S(1)}, bf16[128,512]{1,0:T(8,128)(2,1)S(1)}, u32[]{:S(2)}, u32[]{:S(2)}) collective-permute-start(bf16[128,512]{1,0:T(8,128)(2,1)S(1)} %get-tuple-element.27), channel_id=1, source_target_pairs={{0,1},{1,0},{2,3},{3,2},{4,5},{5,4},{6,7},{7,6},{8,9},{9,8},{10,11... | collective-permute-start | bytes 393224 | tf_op jit(solution)/shard_map/ppermute | solution.py:281
  22.4 8.1 %collective-permute-start.9 = (bf16[128,512]{1,0:T(8,128)(2,1)S(1)}, bf16[128,512]{1,0:T(8,128)(2,1)S(1)}, u32[]{:S(2)}, u32[]{:S(2)}) collective-permute-start(bf16[128,512]{1,0:T(8,128)(2,1)S(1)} %get-tuple-element.28), channel_id=1, source_target_pairs={{0,2},{1,3},{2,0},{3,1},{4,6},{5,7},{6,4},{7,5},{8,10},{9,11},{10,... | collective-permute-start | bytes 393224 | tf_op jit(solution)/shard_map/ppermute | solution.py:281
  23.9 6.6 %collective-permute-start.10 = (bf16[128,512]{1,0:T(8,128)(2,1)S(1)}, bf16[128,512]{1,0:T(8,128)(2,1)S(1)}, u32[]{:S(2)}, u32[]{:S(2)}) collective-permute-start(bf16[128,512]{1,0:T(8,128)(2,1)S(1)} %get-tuple-element.29), channel_id=1, source_target_pairs={{0,3},{1,2},{2,1},{3,0},{4,7},{5,6},{6,5},{7,4},{8,11},{9,10},{10,... | collective-permute-start | bytes 393224 | tf_op jit(solution)/shard_map/ppermute | solution.py:281
  24.7 8.9 %collective-permute-start.12 = (bf16[128,512]{1,0:T(8,128)(2,1)S(1)}, bf16[128,512]{1,0:T(8,128)(2,1)S(1)}, u32[]{:S(2)}, u32[]{:S(2)}) collective-permute-start(bf16[128,512]{1,0:T(8,128)(2,1)S(1)} %add_passed.1), channel_id=1, source_target_pairs={{0,8},{1,9},{2,10},{3,11},{4,12},{5,13},{6,14},{7,15},{8,0},{9,1},... | collective-permute-start | bytes 393224 | tf_op jit(solution)/shard_map/ppermute | solution.py:281
  27.0 6.9 %collective-permute-start.13 = (bf16[128,512]{1,0:T(8,128)(2,1)S(1)}, bf16[128,512]{1,0:T(8,128)(2,1)S(1)}, u32[]{:S(2)}, u32[]{:S(2)}) collective-permute-start(bf16[128,512]{1,0:T(8,128)(2,1)S(1)} %get-tuple-element.35), channel_id=1, source_target_pairs={{0,4},{1,5},{2,6},{3,7},{4,0},{5,1},{6,2},{7,3},{8,12},{9,13},{10,... | collective-permute-start | bytes 393224 | tf_op jit(solution)/shard_map/ppermute | solution.py:281
  30.4 3.5 %copy-start.1 = (bf16[128,512]{1,0:T(8,128)(2,1)S(1)}, bf16[128,512]{1,0:T(8,128)(2,1)}, u32[]{:S(2)}) copy-start(bf16[128,512]{1,0:T(8,128)(2,1)} %text_ref.1) | copy-start | bytes 393220

commit v28 on v27

--- a/solution.py
+++ b/solution.py
@@ -14,6 +14,7 @@
 PIECE = 32
 LATE = 16500
 NEAR = 30000
+LOW = 3000
 LOG2_E = math.log2(math.e)
 VMEM = pl.BlockSpec(memory_space=pltpu.VMEM)
 
@@ -305,22 +306,18 @@
         far_parts = dict(zip(far_steps, image_parts))
         passed = [move(far_parts[step], low=-step[1]) for step in late]
         came = [move(part, grp=-g) for g, part in enumerate(text_parts) if g]
-        near_parts = add_stacks([text_parts[0], *came], near_count)
-        low_parts = [far_parts[0, w] for w in range(1, low_count)]
+        near_parts = list(add_stacks([text_parts[0], *came], near_count))
         near_came = [move(part, near=-n) for n, part in enumerate(near_parts) if n]
         high_came = []
         for h in range(1, high_count):
             terms = [far_parts[h, 0]] + [p for step, p in zip(late, passed) if step[0] == h]
             both = add_parts(terms, jnp.bfloat16, 1, "add_passed")
-            both, low_parts = lax.optimization_barrier((both, low_parts))
             high_came.append(move(both, high=-h))
-        low_came = [move(part, low=-w) for w, part in enumerate(low_parts, 1)]
-        return finish(
-            images,
-            texts,
-            [(1, add_parts([near_parts[0], *near_came], jnp.float32, NEAR, "add_near"))]
-            + [(0, part) for part in [far_parts[0, 0]] + high_came + low_came],
-        )
+        low_came = [move(far_parts[0, w], low=-w) for w in range(1, low_count)]
+        low_sum = add_parts([far_parts[0, 0], *low_came], jnp.float32, LOW, "add_low")
+        low_sum, near_parts[0] = lax.optimization_barrier((low_sum, near_parts[0]))
+        near_sum = add_parts([near_parts[0], *near_came], jnp.float32, NEAR, "add_near")
+        return finish(images, texts, [(1, near_sum)] + [(0, part) for part in [low_sum] + high_came])
 
     in_specs = (P(AXES, None), P(AXES, None), P(), P())
     out_specs = (P(AXES, None), P(AXES, None))

time: 35.1 us -> 34.7 us (0.989)
  starting transfers between devices: 18.7 us -> 18 us
    ppermute x14, starting transfers between devices: 18.7 us -> 18 us  [move(): return lax.ppermute(value, AXES, perm)]
    pallas_call x8 -> x9, Pallas kernels: 3.37 us -> 3.41 us  [call(): pl.pallas_call(kernel, out_shape=out_shape, in_specs=[VMEM] * len(operand...]
  transfers between devices with their start and end apart: 14 -> 14, of which waited for: 9 -> 8; matrix products, arithmetic and copies ran while one was open for 0% -> 0% of each run, Pallas kernels for 5% -> 5%
where the time goes in v28:
time: 34.7 us; the launch traced here: 34.5 us
  starting transfers between devices  18 us (52%)
  waiting for transfers between devices  9.09 us (26%)
  Pallas kernels  4.44 us (13%)
  between operations  2.04 us (6%)
  local copies, waits for them, and re-layouts  0.92 us (3%)
    ppermute x14, starting transfers between devices, move(): return lax.ppermute(value, AXES, perm)  18 us
    ppermute x14, waiting for transfers between devices, move(): return lax.ppermute(value, AXES, perm)  9.09 us
    pallas_call x9, Pallas kernels, call(): pl.pallas_call(kernel, out_shape=out_shape, in_specs=[VMEM] * len(operand...  3.41 us
    pallas_call x1, Pallas kernels, finish(): pl.pallas_call(functools.partial(finish_kernel, [side for side, _ in part...  1.03 us
    unnamed x6, local copies, waits for them, and re-layouts  0.92 us
  transfers between devices with their start and end apart: 14, of which 8 were waited for; matrix products, arithmetic and copies ran while one was open for 0% of the time, Pallas kernels for 5%

profile of v28, /device:TPU:0, one launch (start us, length us, event | category | flops | bytes accessed | tf_op | source)
XLA Modules:
  0.0 34.5 jit_solution(8814415945273416617)
XLA Ops:
  0.6 4.1 %collective-permute-start = (bf16[128,512]{1,0:T(8,128)(2,1)}, bf16[128,512]{1,0:T(8,128)(2,1)S(1)}, u32[]{:S(2)}, u32[]{:S(2)}) collective-permute-start(bf16[128,512]{1,0:T(8,128)(2,1)} %image_ref.1), channel_id=1, source_target_pairs={{0,8},{1,9},{2,10},{3,11},{4,12},{5,13},{6,14},{7,15},{8,0},{9,1},... | collective-permute-start | bytes 393224 | tf_op jit(solution)/shard_map/ppermute | solution.py:282
  4.7 1.5 %collective-permute-start.2 = (bf16[128,512]{1,0:T(8,128)(2,1)}, bf16[128,512]{1,0:T(8,128)(2,1)S(1)}, u32[]{:S(2)}, u32[]{:S(2)}) collective-permute-start(bf16[128,512]{1,0:T(8,128)(2,1)} %text_ref.1), channel_id=1, source_target_pairs={{0,2},{1,3},{2,0},{3,1},{4,6},{5,7},{6,4},{7,5},{8,10},{9,11},{10,... | collective-permute-start | bytes 393224 | tf_op jit(solution)/shard_map/ppermute | solution.py:282
  6.3 1.5 %collective-permute-start.1 = (bf16[128,512]{1,0:T(8,128)(2,1)}, bf16[128,512]{1,0:T(8,128)(2,1)S(1)}, u32[]{:S(2)}, u32[]{:S(2)}) collective-permute-start(bf16[128,512]{1,0:T(8,128)(2,1)} %text_ref.1), channel_id=1, source_target_pairs={{0,1},{1,0},{2,3},{3,2},{4,5},{5,4},{6,7},{7,6},{8,9},{9,8},{10,11... | collective-permute-start | bytes 393224 | tf_op jit(solution)/shard_map/ppermute | solution.py:282
  7.7 0.5 %collective-permute-start.3 = (bf16[128,512]{1,0:T(8,128)(2,1)}, bf16[128,512]{1,0:T(8,128)(2,1)S(1)}, u32[]{:S(2)}, u32[]{:S(2)}) collective-permute-start(bf16[128,512]{1,0:T(8,128)(2,1)} %text_ref.1), channel_id=1, source_target_pairs={{0,3},{1,2},{2,1},{3,0},{4,7},{5,6},{6,5},{7,4},{8,11},{9,10},{10,... | collective-permute-start | bytes 393224 | tf_op jit(solution)/shard_map/ppermute | solution.py:282
  8.2 1.6 %collective-permute-start.4 = (bf16[128,512]{1,0:T(8,128)(2,1)}, bf16[128,512]{1,0:T(8,128)(2,1)S(1)}, u32[]{:S(2)}, u32[]{:S(2)}) collective-permute-start(bf16[128,512]{1,0:T(8,128)(2,1)} %image_ref.1), channel_id=1, source_target_pairs={{0,4},{1,5},{2,6},{3,7},{4,0},{5,1},{6,2},{7,3},{8,12},{9,13},{10,... | collective-permute-start | bytes 393224 | tf_op jit(solution)/shard_map/ppermute | solution.py:282
  11.2 0.2 collective-permute-done.refs_1_
  11.4 0.8 %collective-permute-start.5 = (bf16[128,512]{1,0:T(8,128)(2,1)S(1)}, bf16[128,512]{1,0:T(8,128)(2,1)S(1)}, u32[]{:S(2)}, u32[]{:S(2)}) collective-permute-start(bf16[128,512]{1,0:T(8,128)(2,1)S(1)} %collective-permute-done.refs_1_), channel_id=1, source_target_pairs={{0,4},{1,5},{2,6},{3,7},{4,0},{5,1},{6,2},{7,3},{8,12},{9,13},{10,... | collective-permute-start | bytes 393224 | tf_op jit(solution)/shard_map/ppermute | solution.py:282
  12.1 0.9 %copy-done = bf16[128,512]{1,0:T(8,128)(2,1)S(1)} copy-done((bf16[128,512]{1,0:T(8,128)(2,1)S(1)}, bf16[128,512]{1,0:T(8,128)(2,1)}, u32[]{:S(2)}) %copy-start) | copy-done | bytes 131096
  13.2 1.0 %collective-permute-done.3.refs_3_ = bf16[128,512]{1,0:T(8,128)(2,1)S(1)} collective-permute-done((bf16[128,512]{1,0:T(8,128)(2,1)}, bf16[128,512]{1,0:T(8,128)(2,1)S(1)}, u32[]{:S(2)}, u32[]{:S(2)}) %collective-permute-start.3) | collective-permute-done | bytes 131104 | tf_op jit(solution)/shard_map/ppermute | solution.py:282
  14.2 0.2 stack_units.1.text_ref.own_text_ref
  14.4 0.4 %collective-permute-done.4.refs_2_ = bf16[128,512]{1,0:T(8,128)(2,1)S(1)} collective-permute-done((bf16[128,512]{1,0:T(8,128)(2,1)}, bf16[128,512]{1,0:T(8,128)(2,1)S(1)}, u32[]{:S(2)}, u32[]{:S(2)}) %collective-permute-start.4) | collective-permute-done | bytes 131104 | tf_op jit(solution)/shard_map/ppermute | solution.py:282
  14.9 1.1 %early_pairs.1 = (f32[512,512]{1,0:T(8,128)S(1)}, bf16[384,512]{1,0:T(8,128)(2,1)S(1)}, f32[384,512]{1,0:T(8,128)S(1)}) custom-call(f32[1,3]{1,0:T(1,128)S(1)} %maximum_bitcast_fusion.params_ref, bf16[512,512]{1,0:T(8,128)(2,1)S(1)} %stack_units.1.text_ref.own_text_ref, bf16[128,512]{1,0:T(8,128)(2,1)S(1)} %copy-done.2, ...), custom_call_target="tpu_custom_call" | custom-call | flops 603979776 | bytes 3145740 | tf_op jit(solution)/shard_map/early_pairs/pallas_call | solution.py:30
  16.0 0.9 %collective-permute-done.5.refs_0_ = bf16[128,512]{1,0:T(8,128)(2,1)S(1)} collective-permute-done((bf16[128,512]{1,0:T(8,128)(2,1)S(1)}, bf16[128,512]{1,0:T(8,128)(2,1)S(1)}, u32[]{:S(2)}, u32[]{:S(2)}) %collective-permute-start.5) | collective-permute-done | bytes 131104 | tf_op jit(solution)/shard_map/ppermute | solution.py:282
  17.0 1.7 %rest_pairs.1 = (f32[512,512]{1,0:T(8,128)S(1)}, bf16[512,512]{1,0:T(8,128)(2,1)S(1)}, f32[128,512]{1,0:T(8,128)S(1)}, f32[128,512]{1,0:T(8,128)S(1)}, bf16[128,...) custom-call(f32[1,3]{1,0:T(1,128)S(1)} %maximum_bitcast_fusion.params_ref, ...), custom_call_target="tpu_custom_call" | custom-call | flops 1006632960 | bytes 5767180 | tf_op jit(solution)/shard_map/rest_pairs/pallas_call | solution.py:30
  18.7 1.0 %collective-permute-start.12 = (bf16[128,512]{1,0:T(8,128)(2,1)S(1)}, bf16[128,512]{1,0:T(8,128)(2,1)S(1)}, u32[]{:S(2)}, u32[]{:S(2)}) collective-permute-start(bf16[128,512]{1,0:T(8,128)(2,1)S(1)} %get-tuple-element.35), channel_id=1, source_target_pairs={{0,4},{1,5},{2,6},{3,7},{4,0},{5,1},{6,2},{7,3},{8,12},{9,13},{10,... | collective-permute-start | bytes 393224 | tf_op jit(solution)/shard_map/ppermute | solution.py:282
  19.8 1.1 %collective-permute-start.7 = (bf16[128,512]{1,0:T(8,128)(2,1)S(1)}, bf16[128,512]{1,0:T(8,128)(2,1)S(1)}, u32[]{:S(2)}, u32[]{:S(2)}) collective-permute-start(bf16[128,512]{1,0:T(8,128)(2,1)S(1)} %get-tuple-element.25), channel_id=1, source_target_pairs={{0,4},{1,5},{2,6},{3,7},{4,0},{5,1},{6,2},{7,3},{8,12},{9,13},{10,... | collective-permute-start | bytes 393224 | tf_op jit(solution)/shard_map/ppermute | solution.py:282
  21.0 1.6 %collective-permute-start.9 = (bf16[128,512]{1,0:T(8,128)(2,1)S(1)}, bf16[128,512]{1,0:T(8,128)(2,1)S(1)}, u32[]{:S(2)}, u32[]{:S(2)}) collective-permute-start(bf16[128,512]{1,0:T(8,128)(2,1)S(1)} %get-tuple-element.30), channel_id=1, source_target_pairs={{0,1},{1,0},{2,3},{3,2},{4,5},{5,4},{6,7},{7,6},{8,9},{9,8},{10,11... | collective-permute-start | bytes 393224 | tf_op jit(solution)/shard_map/ppermute | solution.py:282
  22.6 1.5 %collective-permute-start.10 = (bf16[128,512]{1,0:T(8,128)(2,1)S(1)}, bf16[128,512]{1,0:T(8,128)(2,1)S(1)}, u32[]{:S(2)}, u32[]{:S(2)}) collective-permute-start(bf16[128,512]{1,0:T(8,128)(2,1)S(1)} %get-tuple-element.31), channel_id=1, source_target_pairs={{0,2},{1,3},{2,0},{3,1},{4,6},{5,7},{6,4},{7,5},{8,10},{9,11},{10,... | collective-permute-start | bytes 393224 | tf_op jit(solution)/shard_map/ppermute | solution.py:282
  24.1 0.4 %collective-permute-start.11 = (bf16[128,512]{1,0:T(8,128)(2,1)S(1)}, bf16[128,512]{1,0:T(8,128)(2,1)S(1)}, u32[]{:S(2)}, u32[]{:S(2)}) collective-permute-start(bf16[128,512]{1,0:T(8,128)(2,1)S(1)} %get-tuple-element.32), channel_id=1, source_target_pairs={{0,3},{1,2},{2,1},{3,0},{4,7},{5,6},{6,5},{7,4},{8,11},{9,10},{10,... | collective-permute-start | bytes 393224 | tf_op jit(solution)/shard_map/ppermute | solution.py:282
  24.5 0.6 %collective-permute-done.12.refs_1_ = bf16[128,512]{1,0:T(8,128)(2,1)S(1)} collective-permute-done((bf16[128,512]{1,0:T(8,128)(2,1)S(1)}, bf16[128,512]{1,0:T(8,128)(2,1)S(1)}, u32[]{:S(2)}, u32[]{:S(2)}) %collective-permute-start.12) | collective-permute-done | bytes 131104 | tf_op jit(solution)/shard_map/ppermute | solution.py:282
  25.1 2.3 %collective-permute-start.13 = (bf16[128,512]{1,0:T(8,128)(2,1)S(1)}, bf16[128,512]{1,0:T(8,128)(2,1)S(1)}, u32[]{:S(2)}, u32[]{:S(2)}) collective-permute-start(bf16[128,512]{1,0:T(8,128)(2,1)S(1)} %add_passed.1), channel_id=1, source_target_pairs={{0,8},{1,9},{2,10},{3,11},{4,12},{5,13},{6,14},{7,15},{8,0},{9,1},... | collective-permute-start | bytes 393224 | tf_op jit(solution)/shard_map/ppermute | solution.py:282
  27.5 2.9 %collective-permute-done.10.refs_2_ = bf16[128,512]{1,0:T(8,128)(2,1)S(1)} collective-permute-done((bf16[128,512]{1,0:T(8,128)(2,1)S(1)}, bf16[128,512]{1,0:T(8,128)(2,1)S(1)}, u32[]{:S(2)}, u32[]{:S(2)}) %collective-permute-start.10) | collective-permute-done | bytes 131104 | tf_op jit(solution)/shard_map/ppermute | solution.py:282
  30.5 3.0 %collective-permute-done.13.refs_2_ = bf16[128,512]{1,0:T(8,128)(2,1)S(1)} collective-permute-done((bf16[128,512]{1,0:T(8,128)(2,1)S(1)}, bf16[128,512]{1,0:T(8,128)(2,1)S(1)}, u32[]{:S(2)}, u32[]{:S(2)}) %collective-permute-start.13) | collective-permute-done | bytes 131104 | tf_op jit(solution)/shard_map/ppermute | solution.py:282
  33.5 1.0 %finish.1 = (f32[128,512]{1,0:T(8,128)}, f32[128,512]{1,0:T(8,128)}) custom-call(bf16[128,512]{1,0:T(8,128)(2,1)S(1)} %copy-done.2, bf16[128,512]{1,0:T(8,128)(2,1)S(1)} %copy-done.1, f32[128,512]{1,0:T(8,128)S(1)} %add_near.1.refs_0_, f32[128,512]{1,0:T(8,128)S(1)} %add_low.1.refs_1_, bf16[128,512]{1,0:T(8,128)(2,1)S(1)} %collective-permute-done.13.refs_2_), custom_call_target="tpu_custom_call" | custom-call | flops 1966080 | bytes 589824 | tf_op jit(solution)/shard_map/finish/pallas_call | solution.py:232
  (21 shorter events, 0.8 us)
Async XLA Ops:
  0.6 10.7 %collective-permute-start = (bf16[128,512]{1,0:T(8,128)(2,1)}, bf16[128,512]{1,0:T(8,128)(2,1)S(1)}, u32[]{:S(2)}, u32[]{:S(2)}) collective-permute-start(bf16[128,512]{1,0:T(8,128)(2,1)} %image_ref.1), channel_id=1, source_target_pairs={{0,8},{1,9},{2,10},{3,11},{4,12},{5,13},{6,14},{7,15},{8,0},{9,1},... | collective-permute-start | bytes 393224 | tf_op jit(solution)/shard_map/ppermute | solution.py:282
  4.7 8.4 %collective-permute-start.2 = (bf16[128,512]{1,0:T(8,128)(2,1)}, bf16[128,512]{1,0:T(8,128)(2,1)S(1)}, u32[]{:S(2)}, u32[]{:S(2)}) collective-permute-start(bf16[128,512]{1,0:T(8,128)(2,1)} %text_ref.1), channel_id=1, source_target_pairs={{0,2},{1,3},{2,0},{3,1},{4,6},{5,7},{6,4},{7,5},{8,10},{9,11},{10,... | collective-permute-start | bytes 393224 | tf_op jit(solution)/shard_map/ppermute | solution.py:282
  6.3 6.9 %collective-permute-start.1 = (bf16[128,512]{1,0:T(8,128)(2,1)}, bf16[128,512]{1,0:T(8,128)(2,1)S(1)}, u32[]{:S(2)}, u32[]{:S(2)}) collective-permute-start(bf16[128,512]{1,0:T(8,128)(2,1)} %text_ref.1), channel_id=1, source_target_pairs={{0,1},{1,0},{2,3},{3,2},{4,5},{5,4},{6,7},{7,6},{8,9},{9,8},{10,11... | collective-permute-start | bytes 393224 | tf_op jit(solution)/shard_map/ppermute | solution.py:282
  7.7 6.4 %collective-permute-start.3 = (bf16[128,512]{1,0:T(8,128)(2,1)}, bf16[128,512]{1,0:T(8,128)(2,1)S(1)}, u32[]{:S(2)}, u32[]{:S(2)}) collective-permute-start(bf16[128,512]{1,0:T(8,128)(2,1)} %text_ref.1), channel_id=1, source_target_pairs={{0,3},{1,2},{2,1},{3,0},{4,7},{5,6},{6,5},{7,4},{8,11},{9,10},{10,... | collective-permute-start | bytes 393224 | tf_op jit(solution)/shard_map/ppermute | solution.py:282
  8.2 6.6 %collective-permute-start.4 = (bf16[128,512]{1,0:T(8,128)(2,1)}, bf16[128,512]{1,0:T(8,128)(2,1)S(1)}, u32[]{:S(2)}, u32[]{:S(2)}) collective-permute-start(bf16[128,512]{1,0:T(8,128)(2,1)} %image_ref.1), channel_id=1, source_target_pairs={{0,4},{1,5},{2,6},{3,7},{4,0},{5,1},{6,2},{7,3},{8,12},{9,13},{10,... | collective-permute-start | bytes 393224 | tf_op jit(solution)/shard_map/ppermute | solution.py:282
  11.4 5.5 %collective-permute-start.5 = (bf16[128,512]{1,0:T(8,128)(2,1)S(1)}, bf16[128,512]{1,0:T(8,128)(2,1)S(1)}, u32[]{:S(2)}, u32[]{:S(2)}) collective-permute-start(bf16[128,512]{1,0:T(8,128)(2,1)S(1)} %collective-permute-done.refs_1_), channel_id=1, source_target_pairs={{0,4},{1,5},{2,6},{3,7},{4,0},{5,1},{6,2},{7,3},{8,12},{9,13},{10,... | collective-permute-start | bytes 393224 | tf_op jit(solution)/shard_map/ppermute | solution.py:282
  12.1 0.9 %copy-start = (bf16[128,512]{1,0:T(8,128)(2,1)S(1)}, bf16[128,512]{1,0:T(8,128)(2,1)}, u32[]{:S(2)}) copy-start(bf16[128,512]{1,0:T(8,128)(2,1)} %text_ref.1) | copy-start | bytes 393220
  13.1 1.7 %copy-start.2 = (bf16[128,512]{1,0:T(8,128)(2,1)S(1)}, bf16[128,512]{1,0:T(8,128)(2,1)}, u32[]{:S(2)}) copy-start(bf16[128,512]{1,0:T(8,128)(2,1)} %image_ref.1) | copy-start | bytes 393220
  14.3 2.6 %collective-permute-start.6 = (bf16[512,512]{1,0:T(8,128)(2,1)S(1)}, bf16[512,512]{1,0:T(8,128)(2,1)S(1)}, u32[]{:S(2)}, u32[]{:S(2)}) collective-permute-start(bf16[512,512]{1,0:T(8,128)(2,1)S(1)} %stack_units.1.text_ref.own_text_ref), channel_id=1, source_target_pairs={{0,16},{1,17},{2,18},{3,19},{4,20},{5,21},{6,22},{7,23},{8,24},{9,... | collective-permute-start | bytes 1572872 | tf_op jit(solution)/shard_map/ppermute | solution.py:282
  18.7 2.2 %collective-permute-start.8 = (bf16[512,512]{1,0:T(8,128)(2,1)S(1)}, bf16[512,512]{1,0:T(8,128)(2,1)S(1)}, u32[]{:S(2)}, u32[]{:S(2)}) collective-permute-start(bf16[512,512]{1,0:T(8,128)(2,1)S(1)} %get-tuple-element.27), channel_id=1, source_target_pairs={{0,16},{1,17},{2,18},{3,19},{4,20},{5,21},{6,22},{7,23},{8,24},{9,... | collective-permute-start | bytes 1572872 | tf_op jit(solution)/shard_map/ppermute | solution.py:282
  18.7 6.4 %collective-permute-start.12 = (bf16[128,512]{1,0:T(8,128)(2,1)S(1)}, bf16[128,512]{1,0:T(8,128)(2,1)S(1)}, u32[]{:S(2)}, u32[]{:S(2)}) collective-permute-start(bf16[128,512]{1,0:T(8,128)(2,1)S(1)} %get-tuple-element.35), channel_id=1, source_target_pairs={{0,4},{1,5},{2,6},{3,7},{4,0},{5,1},{6,2},{7,3},{8,12},{9,13},{10,... | collective-permute-start | bytes 393224 | tf_op jit(solution)/shard_map/ppermute | solution.py:282
  19.8 7.7 %collective-permute-start.7 = (bf16[128,512]{1,0:T(8,128)(2,1)S(1)}, bf16[128,512]{1,0:T(8,128)(2,1)S(1)}, u32[]{:S(2)}, u32[]{:S(2)}) collective-permute-start(bf16[128,512]{1,0:T(8,128)(2,1)S(1)} %get-tuple-element.25), channel_id=1, source_target_pairs={{0,4},{1,5},{2,6},{3,7},{4,0},{5,1},{6,2},{7,3},{8,12},{9,13},{10,... | collective-permute-start | bytes 393224 | tf_op jit(solution)/shard_map/ppermute | solution.py:282
  21.0 6.6 %collective-permute-start.9 = (bf16[128,512]{1,0:T(8,128)(2,1)S(1)}, bf16[128,512]{1,0:T(8,128)(2,1)S(1)}, u32[]{:S(2)}, u32[]{:S(2)}) collective-permute-start(bf16[128,512]{1,0:T(8,128)(2,1)S(1)} %get-tuple-element.30), channel_id=1, source_target_pairs={{0,1},{1,0},{2,3},{3,2},{4,5},{5,4},{6,7},{7,6},{8,9},{9,8},{10,11... | collective-permute-start | bytes 393224 | tf_op jit(solution)/shard_map/ppermute | solution.py:282
  22.6 7.9 %collective-permute-start.10 = (bf16[128,512]{1,0:T(8,128)(2,1)S(1)}, bf16[128,512]{1,0:T(8,128)(2,1)S(1)}, u32[]{:S(2)}, u32[]{:S(2)}) collective-permute-start(bf16[128,512]{1,0:T(8,128)(2,1)S(1)} %get-tuple-element.31), channel_id=1, source_target_pairs={{0,2},{1,3},{2,0},{3,1},{4,6},{5,7},{6,4},{7,5},{8,10},{9,11},{10,... | collective-permute-start | bytes 393224 | tf_op jit(solution)/shard_map/ppermute | solution.py:282
  24.1 6.4 %collective-permute-start.11 = (bf16[128,512]{1,0:T(8,128)(2,1)S(1)}, bf16[128,512]{1,0:T(8,128)(2,1)S(1)}, u32[]{:S(2)}, u32[]{:S(2)}) collective-permute-start(bf16[128,512]{1,0:T(8,128)(2,1)S(1)} %get-tuple-element.32), channel_id=1, source_target_pairs={{0,3},{1,2},{2,1},{3,0},{4,7},{5,6},{6,5},{7,4},{8,11},{9,10},{10,... | collective-permute-start | bytes 393224 | tf_op jit(solution)/shard_map/ppermute | solution.py:282
  25.1 8.4 %collective-permute-start.13 = (bf16[128,512]{1,0:T(8,128)(2,1)S(1)}, bf16[128,512]{1,0:T(8,128)(2,1)S(1)}, u32[]{:S(2)}, u32[]{:S(2)}) collective-permute-start(bf16[128,512]{1,0:T(8,128)(2,1)S(1)} %add_passed.1), channel_id=1, source_target_pairs={{0,8},{1,9},{2,10},{3,11},{4,12},{5,13},{6,14},{7,15},{8,0},{9,1},... | collective-permute-start | bytes 393224 | tf_op jit(solution)/shard_map/ppermute | solution.py:282
  27.5 6.0 %copy-start.1 = (bf16[128,512]{1,0:T(8,128)(2,1)S(1)}, bf16[128,512]{1,0:T(8,128)(2,1)}, u32[]{:S(2)}) copy-start(bf16[128,512]{1,0:T(8,128)(2,1)} %text_ref.1) | copy-start | bytes 393220

commit v29 on v20

--- a/solution.py
+++ b/solution.py
@@ -290,7 +290,7 @@
         )
         far_parts = dict(zip([*early, *late], image_parts))
         came = [move(part, grp=-g) for g, part in enumerate(text_parts) if g]
-        far_order = sorted((step for step in far_parts if step != (0, 0)), key=lambda step: step[0])
+        far_order = sorted((step for step in far_parts if step != (0, 0)), key=lambda step: (step[0], -step[1]) if step[0] else step)
         far_came = [move(far_parts[h, w], high=-h, low=-w) for h, w in far_order]
         near_parts = add_stacks([text_parts[0], *came], near_count)
         near_parts = [near_parts[0]] + [

time: 34.3 us -> 36.3 us (1.058)
  waiting for transfers between devices: 6.55 us -> 10.4 us
  starting transfers between devices: 20.1 us -> 18.4 us
    ppermute x14, waiting for transfers between devices: 6.55 us -> 10.4 us  [move(): return lax.ppermute(value, AXES, perm)]
    ppermute x14, starting transfers between devices: 20.1 us -> 18.4 us  [move(): return lax.ppermute(value, AXES, perm)]
  transfers between devices with their start and end apart: 14 -> 14, of which waited for: 7 -> 6; matrix products, arithmetic and copies ran while one was open for 0% -> 0% of each run, Pallas kernels for 5% -> 5%
where the time goes in v29:
time: 36.3 us; the launch traced here: 36.1 us
  starting transfers between devices  18.4 us (51%)
  waiting for transfers between devices  10.4 us (29%)
  Pallas kernels  4.38 us (12%)
  between operations  2.03 us (6%)
  local copies, waits for them, and re-layouts  0.91 us (3%)
    ppermute x14, starting transfers between devices, move(): return lax.ppermute(value, AXES, perm)  18.4 us
    ppermute x14, waiting for transfers between devices, move(): return lax.ppermute(value, AXES, perm)  10.4 us
    pallas_call x6, Pallas kernels, call(): pl.pallas_call(kernel, out_shape=out_shape, in_specs=[VMEM] * len(operand...  3.31 us
    pallas_call x1, Pallas kernels, finish(): pl.pallas_call(functools.partial(finish_kernel, [side for side, _ in part...  1.07 us
    unnamed x6, local copies, waits for them, and re-layouts  0.91 us
  transfers between devices with their start and end apart: 14, of which 6 were waited for; matrix products, arithmetic and copies ran while one was open for 0% of the time, Pallas kernels for 5%

profile of v29, /device:TPU:0, one launch (start us, length us, event | category | flops | bytes accessed | tf_op | source)
XLA Modules:
  0.0 36.1 jit_solution(5782231534328403496)
XLA Ops:
  0.6 4.1 %collective-permute-start = (bf16[128,512]{1,0:T(8,128)(2,1)}, bf16[128,512]{1,0:T(8,128)(2,1)S(1)}, u32[]{:S(2)}, u32[]{:S(2)}) collective-permute-start(bf16[128,512]{1,0:T(8,128)(2,1)} %image_ref.1), channel_id=1, source_target_pairs={{0,8},{1,9},{2,10},{3,11},{4,12},{5,13},{6,14},{7,15},{8,0},{9,1},... | collective-permute-start | bytes 393224 | tf_op jit(solution)/shard_map/ppermute | solution.py:269
  4.7 1.5 %collective-permute-start.2 = (bf16[128,512]{1,0:T(8,128)(2,1)}, bf16[128,512]{1,0:T(8,128)(2,1)S(1)}, u32[]{:S(2)}, u32[]{:S(2)}) collective-permute-start(bf16[128,512]{1,0:T(8,128)(2,1)} %text_ref.1), channel_id=1, source_target_pairs={{0,2},{1,3},{2,0},{3,1},{4,6},{5,7},{6,4},{7,5},{8,10},{9,11},{10,... | collective-permute-start | bytes 393224 | tf_op jit(solution)/shard_map/ppermute | solution.py:269
  6.3 1.5 %collective-permute-start.1 = (bf16[128,512]{1,0:T(8,128)(2,1)}, bf16[128,512]{1,0:T(8,128)(2,1)S(1)}, u32[]{:S(2)}, u32[]{:S(2)}) collective-permute-start(bf16[128,512]{1,0:T(8,128)(2,1)} %text_ref.1), channel_id=1, source_target_pairs={{0,1},{1,0},{2,3},{3,2},{4,5},{5,4},{6,7},{7,6},{8,9},{9,8},{10,11... | collective-permute-start | bytes 393224 | tf_op jit(solution)/shard_map/ppermute | solution.py:269
  7.7 0.5 %collective-permute-start.3 = (bf16[128,512]{1,0:T(8,128)(2,1)}, bf16[128,512]{1,0:T(8,128)(2,1)S(1)}, u32[]{:S(2)}, u32[]{:S(2)}) collective-permute-start(bf16[128,512]{1,0:T(8,128)(2,1)} %text_ref.1), channel_id=1, source_target_pairs={{0,3},{1,2},{2,1},{3,0},{4,7},{5,6},{6,5},{7,4},{8,11},{9,10},{10,... | collective-permute-start | bytes 393224 | tf_op jit(solution)/shard_map/ppermute | solution.py:269
  8.2 1.6 %collective-permute-start.4 = (bf16[128,512]{1,0:T(8,128)(2,1)}, bf16[128,512]{1,0:T(8,128)(2,1)S(1)}, u32[]{:S(2)}, u32[]{:S(2)}) collective-permute-start(bf16[128,512]{1,0:T(8,128)(2,1)} %image_ref.1), channel_id=1, source_target_pairs={{0,4},{1,5},{2,6},{3,7},{4,0},{5,1},{6,2},{7,3},{8,12},{9,13},{10,... | collective-permute-start | bytes 393224 | tf_op jit(solution)/shard_map/ppermute | solution.py:269
  11.2 0.2 collective-permute-done.refs_1_
  11.4 0.8 %collective-permute-start.5 = (bf16[128,512]{1,0:T(8,128)(2,1)S(1)}, bf16[128,512]{1,0:T(8,128)(2,1)S(1)}, u32[]{:S(2)}, u32[]{:S(2)}) collective-permute-start(bf16[128,512]{1,0:T(8,128)(2,1)S(1)} %collective-permute-done.refs_1_), channel_id=1, source_target_pairs={{0,4},{1,5},{2,6},{3,7},{4,0},{5,1},{6,2},{7,3},{8,12},{9,13},{10,... | collective-permute-start | bytes 393224 | tf_op jit(solution)/shard_map/ppermute | solution.py:269
  12.1 0.9 %copy-done = bf16[128,512]{1,0:T(8,128)(2,1)S(1)} copy-done((bf16[128,512]{1,0:T(8,128)(2,1)S(1)}, bf16[128,512]{1,0:T(8,128)(2,1)}, u32[]{:S(2)}) %copy-start) | copy-done | bytes 131096
  13.2 1.0 %collective-permute-done.3.refs_3_ = bf16[128,512]{1,0:T(8,128)(2,1)S(1)} collective-permute-done((bf16[128,512]{1,0:T(8,128)(2,1)}, bf16[128,512]{1,0:T(8,128)(2,1)S(1)}, u32[]{:S(2)}, u32[]{:S(2)}) %collective-permute-start.3) | collective-permute-done | bytes 131104 | tf_op jit(solution)/shard_map/ppermute | solution.py:269
  14.2 0.2 stack_units.1.text_ref.own_text_ref
  14.4 0.4 %collective-permute-done.4.refs_2_ = bf16[128,512]{1,0:T(8,128)(2,1)S(1)} collective-permute-done((bf16[128,512]{1,0:T(8,128)(2,1)}, bf16[128,512]{1,0:T(8,128)(2,1)S(1)}, u32[]{:S(2)}, u32[]{:S(2)}) %collective-permute-start.4) | collective-permute-done | bytes 131104 | tf_op jit(solution)/shard_map/ppermute | solution.py:269
  14.9 1.1 %early_pairs.1 = (f32[512,512]{1,0:T(8,128)S(1)}, bf16[384,512]{1,0:T(8,128)(2,1)S(1)}, f32[384,512]{1,0:T(8,128)S(1)}) custom-call(f32[1,3]{1,0:T(1,128)S(1)} %maximum_bitcast_fusion.params_ref, bf16[512,512]{1,0:T(8,128)(2,1)S(1)} %stack_units.1.text_ref.own_text_ref, bf16[128,512]{1,0:T(8,128)(2,1)S(1)} %copy-done.2, ...), custom_call_target="tpu_custom_call" | custom-call | flops 603979776 | bytes 3145740 | tf_op jit(solution)/shard_map/early_pairs/pallas_call | solution.py:28
  16.0 0.9 %collective-permute-done.5.refs_0_ = bf16[128,512]{1,0:T(8,128)(2,1)S(1)} collective-permute-done((bf16[128,512]{1,0:T(8,128)(2,1)S(1)}, bf16[128,512]{1,0:T(8,128)(2,1)S(1)}, u32[]{:S(2)}, u32[]{:S(2)}) %collective-permute-start.5) | collective-permute-done | bytes 131104 | tf_op jit(solution)/shard_map/ppermute | solution.py:269
  17.0 1.7 %rest_pairs.1 = (f32[512,512]{1,0:T(8,128)S(1)}, bf16[512,512]{1,0:T(8,128)(2,1)S(1)}, f32[128,512]{1,0:T(8,128)S(1)}, bf16[128,512]{1,0:T(8,128)(2,1)S(1)}, bf1...) custom-call(f32[1,3]{1,0:T(1,128)S(1)} %maximum_bitcast_fusion.params_ref, ...), custom_call_target="tpu_custom_call" | custom-call | flops 1006632960 | bytes 5636108 | tf_op jit(solution)/shard_map/rest_pairs/pallas_call | solution.py:28
  18.8 1.0 %collective-permute-start.7 = (bf16[128,512]{1,0:T(8,128)(2,1)S(1)}, bf16[128,512]{1,0:T(8,128)(2,1)S(1)}, u32[]{:S(2)}, u32[]{:S(2)}) collective-permute-start(bf16[128,512]{1,0:T(8,128)(2,1)S(1)} %get-tuple-element.23), channel_id=1, source_target_pairs={{0,4},{1,5},{2,6},{3,7},{4,0},{5,1},{6,2},{7,3},{8,12},{9,13},{10,... | collective-permute-start | bytes 393224 | tf_op jit(solution)/shard_map/ppermute | solution.py:269
  19.8 2.7 %collective-permute-start.8 = (bf16[128,512]{1,0:T(8,128)(2,1)S(1)}, bf16[128,512]{1,0:T(8,128)(2,1)S(1)}, u32[]{:S(2)}, u32[]{:S(2)}) collective-permute-start(bf16[128,512]{1,0:T(8,128)(2,1)S(1)} %get-tuple-element.24), channel_id=1, source_target_pairs={{0,12},{1,13},{2,14},{3,15},{4,8},{5,9},{6,10},{7,11},{8,4},{9,5},... | collective-permute-start | bytes 393224 | tf_op jit(solution)/shard_map/ppermute | solution.py:269
  22.5 0.3 collective-permute-start.9
  22.8 0.1 add_stacks.1
  22.9 1.5 %collective-permute-start.11 = (bf16[128,512]{1,0:T(8,128)(2,1)S(1)}, bf16[128,512]{1,0:T(8,128)(2,1)S(1)}, u32[]{:S(2)}, u32[]{:S(2)}) collective-permute-start(bf16[128,512]{1,0:T(8,128)(2,1)S(1)} %get-tuple-element.29), channel_id=1, source_target_pairs={{0,1},{1,0},{2,3},{3,2},{4,5},{5,4},{6,7},{7,6},{8,9},{9,8},{10,11... | collective-permute-start | bytes 393224 | tf_op jit(solution)/shard_map/ppermute | solution.py:269
  24.4 1.5 %collective-permute-start.12 = (bf16[128,512]{1,0:T(8,128)(2,1)S(1)}, bf16[128,512]{1,0:T(8,128)(2,1)S(1)}, u32[]{:S(2)}, u32[]{:S(2)}) collective-permute-start(bf16[128,512]{1,0:T(8,128)(2,1)S(1)} %get-tuple-element.30), channel_id=1, source_target_pairs={{0,2},{1,3},{2,0},{3,1},{4,6},{5,7},{6,4},{7,5},{8,10},{9,11},{10,... | collective-permute-start | bytes 393224 | tf_op jit(solution)/shard_map/ppermute | solution.py:269
  26.0 1.2 %collective-permute-start.13 = (bf16[128,512]{1,0:T(8,128)(2,1)S(1)}, bf16[128,512]{1,0:T(8,128)(2,1)S(1)}, u32[]{:S(2)}, u32[]{:S(2)}) collective-permute-start(bf16[128,512]{1,0:T(8,128)(2,1)S(1)} %get-tuple-element.31), channel_id=1, source_target_pairs={{0,3},{1,2},{2,1},{3,0},{4,7},{5,6},{6,5},{7,4},{8,11},{9,10},{10,... | collective-permute-start | bytes 393224 | tf_op jit(solution)/shard_map/ppermute | solution.py:269
  27.2 2.5 %collective-permute-done.8.refs_2_ = bf16[128,512]{1,0:T(8,128)(2,1)S(1)} collective-permute-done((bf16[128,512]{1,0:T(8,128)(2,1)S(1)}, bf16[128,512]{1,0:T(8,128)(2,1)S(1)}, u32[]{:S(2)}, u32[]{:S(2)}) %collective-permute-start.8) | collective-permute-done | bytes 131104 | tf_op jit(solution)/shard_map/ppermute | solution.py:269
  29.7 5.4 %collective-permute-done.9.refs_3_ = bf16[128,512]{1,0:T(8,128)(2,1)S(1)} collective-permute-done((bf16[128,512]{1,0:T(8,128)(2,1)S(1)}, bf16[128,512]{1,0:T(8,128)(2,1)S(1)}, u32[]{:S(2)}, u32[]{:S(2)}) %collective-permute-start.9) | collective-permute-done | bytes 131104 | tf_op jit(solution)/shard_map/ppermute | solution.py:269
  35.0 1.1 %finish.1 = (f32[128,512]{1,0:T(8,128)}, f32[128,512]{1,0:T(8,128)}) custom-call(bf16[128,512]{1,0:T(8,128)(2,1)S(1)} %copy-done.2, bf16[128,512]{1,0:T(8,128)(2,1)S(1)} %copy-done.1, f32[128,512]{1,0:T(8,128)S(1)} %get-tuple-element.22.refs_0_, bf16[128,512]{1,0:T(8,128)(2,1)S(1)} %collective-permute-done.7.refs_1_, ...), custom_call_target="tpu_custom_call" | custom-call | flops 5242880 | bytes 1572864 | tf_op jit(solution)/shard_map/finish/pallas_call | solution.py:219
  (18 shorter events, 0.5 us)
Async XLA Ops:
  0.6 10.7 %collective-permute-start = (bf16[128,512]{1,0:T(8,128)(2,1)}, bf16[128,512]{1,0:T(8,128)(2,1)S(1)}, u32[]{:S(2)}, u32[]{:S(2)}) collective-permute-start(bf16[128,512]{1,0:T(8,128)(2,1)} %image_ref.1), channel_id=1, source_target_pairs={{0,8},{1,9},{2,10},{3,11},{4,12},{5,13},{6,14},{7,15},{8,0},{9,1},... | collective-permute-start | bytes 393224 | tf_op jit(solution)/shard_map/ppermute | solution.py:269
  4.7 8.4 %collective-permute-start.2 = (bf16[128,512]{1,0:T(8,128)(2,1)}, bf16[128,512]{1,0:T(8,128)(2,1)S(1)}, u32[]{:S(2)}, u32[]{:S(2)}) collective-permute-start(bf16[128,512]{1,0:T(8,128)(2,1)} %text_ref.1), channel_id=1, source_target_pairs={{0,2},{1,3},{2,0},{3,1},{4,6},{5,7},{6,4},{7,5},{8,10},{9,11},{10,... | collective-permute-start | bytes 393224 | tf_op jit(solution)/shard_map/ppermute | solution.py:269
  6.3 6.9 %collective-permute-start.1 = (bf16[128,512]{1,0:T(8,128)(2,1)}, bf16[128,512]{1,0:T(8,128)(2,1)S(1)}, u32[]{:S(2)}, u32[]{:S(2)}) collective-permute-start(bf16[128,512]{1,0:T(8,128)(2,1)} %text_ref.1), channel_id=1, source_target_pairs={{0,1},{1,0},{2,3},{3,2},{4,5},{5,4},{6,7},{7,6},{8,9},{9,8},{10,11... | collective-permute-start | bytes 393224 | tf_op jit(solution)/shard_map/ppermute | solution.py:269
  7.7 6.4 %collective-permute-start.3 = (bf16[128,512]{1,0:T(8,128)(2,1)}, bf16[128,512]{1,0:T(8,128)(2,1)S(1)}, u32[]{:S(2)}, u32[]{:S(2)}) collective-permute-start(bf16[128,512]{1,0:T(8,128)(2,1)} %text_ref.1), channel_id=1, source_target_pairs={{0,3},{1,2},{2,1},{3,0},{4,7},{5,6},{6,5},{7,4},{8,11},{9,10},{10,... | collective-permute-start | bytes 393224 | tf_op jit(solution)/shard_map/ppermute | solution.py:269
  8.2 6.6 %collective-permute-start.4 = (bf16[128,512]{1,0:T(8,128)(2,1)}, bf16[128,512]{1,0:T(8,128)(2,1)S(1)}, u32[]{:S(2)}, u32[]{:S(2)}) collective-permute-start(bf16[128,512]{1,0:T(8,128)(2,1)} %image_ref.1), channel_id=1, source_target_pairs={{0,4},{1,5},{2,6},{3,7},{4,0},{5,1},{6,2},{7,3},{8,12},{9,13},{10,... | collective-permute-start | bytes 393224 | tf_op jit(solution)/shard_map/ppermute | solution.py:269
  11.4 5.5 %collective-permute-start.5 = (bf16[128,512]{1,0:T(8,128)(2,1)S(1)}, bf16[128,512]{1,0:T(8,128)(2,1)S(1)}, u32[]{:S(2)}, u32[]{:S(2)}) collective-permute-start(bf16[128,512]{1,0:T(8,128)(2,1)S(1)} %collective-permute-done.refs_1_), channel_id=1, source_target_pairs={{0,4},{1,5},{2,6},{3,7},{4,0},{5,1},{6,2},{7,3},{8,12},{9,13},{10,... | collective-permute-start | bytes 393224 | tf_op jit(solution)/shard_map/ppermute | solution.py:269
  12.1 0.9 %copy-start = (bf16[128,512]{1,0:T(8,128)(2,1)S(1)}, bf16[128,512]{1,0:T(8,128)(2,1)}, u32[]{:S(2)}) copy-start(bf16[128,512]{1,0:T(8,128)(2,1)} %text_ref.1) | copy-start | bytes 393220
  13.1 1.7 %copy-start.2 = (bf16[128,512]{1,0:T(8,128)(2,1)S(1)}, bf16[128,512]{1,0:T(8,128)(2,1)}, u32[]{:S(2)}) copy-start(bf16[128,512]{1,0:T(8,128)(2,1)} %image_ref.1) | copy-start | bytes 393220
  14.3 2.6 %collective-permute-start.6 = (bf16[512,512]{1,0:T(8,128)(2,1)S(1)}, bf16[512,512]{1,0:T(8,128)(2,1)S(1)}, u32[]{:S(2)}, u32[]{:S(2)}) collective-permute-start(bf16[512,512]{1,0:T(8,128)(2,1)S(1)} %stack_units.1.text_ref.own_text_ref), channel_id=1, source_target_pairs={{0,16},{1,17},{2,18},{3,19},{4,20},{5,21},{6,22},{7,23},{8,24},{9,... | collective-permute-start | bytes 1572872 | tf_op jit(solution)/shard_map/ppermute | solution.py:269
  18.7 4.1 %collective-permute-start.10 = (bf16[512,512]{1,0:T(8,128)(2,1)S(1)}, bf16[512,512]{1,0:T(8,128)(2,1)S(1)}, u32[]{:S(2)}, u32[]{:S(2)}) collective-permute-start(bf16[512,512]{1,0:T(8,128)(2,1)S(1)} %get-tuple-element.27), channel_id=1, source_target_pairs={{0,16},{1,17},{2,18},{3,19},{4,20},{5,21},{6,22},{7,23},{8,24},{9,... | collective-permute-start | bytes 1572872 | tf_op jit(solution)/shard_map/ppermute | solution.py:269
  18.8 7.2 %collective-permute-start.7 = (bf16[128,512]{1,0:T(8,128)(2,1)S(1)}, bf16[128,512]{1,0:T(8,128)(2,1)S(1)}, u32[]{:S(2)}, u32[]{:S(2)}) collective-permute-start(bf16[128,512]{1,0:T(8,128)(2,1)S(1)} %get-tuple-element.23), channel_id=1, source_target_pairs={{0,4},{1,5},{2,6},{3,7},{4,0},{5,1},{6,2},{7,3},{8,12},{9,13},{10,... | collective-permute-start | bytes 393224 | tf_op jit(solution)/shard_map/ppermute | solution.py:269
  19.8 9.9 %collective-permute-start.8 = (bf16[128,512]{1,0:T(8,128)(2,1)S(1)}, bf16[128,512]{1,0:T(8,128)(2,1)S(1)}, u32[]{:S(2)}, u32[]{:S(2)}) collective-permute-start(bf16[128,512]{1,0:T(8,128)(2,1)S(1)} %get-tuple-element.24), channel_id=1, source_target_pairs={{0,12},{1,13},{2,14},{3,15},{4,8},{5,9},{6,10},{7,11},{8,4},{9,5},... | collective-permute-start | bytes 393224 | tf_op jit(solution)/shard_map/ppermute | solution.py:269
  22.5 12.5 %collective-permute-start.9 = (bf16[128,512]{1,0:T(8,128)(2,1)S(1)}, bf16[128,512]{1,0:T(8,128)(2,1)S(1)}, u32[]{:S(2)}, u32[]{:S(2)}) collective-permute-start(bf16[128,512]{1,0:T(8,128)(2,1)S(1)} %get-tuple-element.25), channel_id=1, source_target_pairs={{0,8},{1,9},{2,10},{3,11},{4,12},{5,13},{6,14},{7,15},{8,0},{9,1},... | collective-permute-start | bytes 393224 | tf_op jit(solution)/shard_map/ppermute | solution.py:269
  22.8 12.3 %copy-start.1 = (bf16[128,512]{1,0:T(8,128)(2,1)S(1)}, bf16[128,512]{1,0:T(8,128)(2,1)}, u32[]{:S(2)}) copy-start(bf16[128,512]{1,0:T(8,128)(2,1)} %text_ref.1) | copy-start | bytes 393220
  22.9 12.1 %collective-permute-start.11 = (bf16[128,512]{1,0:T(8,128)(2,1)S(1)}, bf16[128,512]{1,0:T(8,128)(2,1)S(1)}, u32[]{:S(2)}, u32[]{:S(2)}) collective-permute-start(bf16[128,512]{1,0:T(8,128)(2,1)S(1)} %get-tuple-element.29), channel_id=1, source_target_pairs={{0,1},{1,0},{2,3},{3,2},{4,5},{5,4},{6,7},{7,6},{8,9},{9,8},{10,11... | collective-permute-start | bytes 393224 | tf_op jit(solution)/shard_map/ppermute | solution.py:269
  24.4 10.6 %collective-permute-start.12 = (bf16[128,512]{1,0:T(8,128)(2,1)S(1)}, bf16[128,512]{1,0:T(8,128)(2,1)S(1)}, u32[]{:S(2)}, u32[]{:S(2)}) collective-permute-start(bf16[128,512]{1,0:T(8,128)(2,1)S(1)} %get-tuple-element.30), channel_id=1, source_target_pairs={{0,2},{1,3},{2,0},{3,1},{4,6},{5,7},{6,4},{7,5},{8,10},{9,11},{10,... | collective-permute-start | bytes 393224 | tf_op jit(solution)/shard_map/ppermute | solution.py:269
  26.0 9.1 %collective-permute-start.13 = (bf16[128,512]{1,0:T(8,128)(2,1)S(1)}, bf16[128,512]{1,0:T(8,128)(2,1)S(1)}, u32[]{:S(2)}, u32[]{:S(2)}) collective-permute-start(bf16[128,512]{1,0:T(8,128)(2,1)S(1)} %get-tuple-element.31), channel_id=1, source_target_pairs={{0,3},{1,2},{2,1},{3,0},{4,7},{5,6},{6,5},{7,4},{8,11},{9,10},{10,... | collective-permute-start | bytes 393224 | tf_op jit(solution)/shard_map/ppermute | solution.py:269

commit v30 on v28

--- a/solution.py
+++ b/solution.py
@@ -313,7 +313,9 @@
             terms = [far_parts[h, 0]] + [p for step, p in zip(late, passed) if step[0] == h]
             both = add_parts(terms, jnp.bfloat16, 1, "add_passed")
             high_came.append(move(both, high=-h))
-        low_came = [move(far_parts[0, w], low=-w) for w in range(1, low_count)]
+        low_parts = [far_parts[0, w] for w in range(1, low_count)]
+        low_parts, near_parts[0] = lax.optimization_barrier((low_parts, near_parts[0]))
+        low_came = [move(part, low=-w) for w, part in enumerate(low_parts, 1)]
         low_sum = add_parts([far_parts[0, 0], *low_came], jnp.float32, LOW, "add_low")
         low_sum, near_parts[0] = lax.optimization_barrier((low_sum, near_parts[0]))
         near_sum = add_parts([near_parts[0], *near_came], jnp.float32, NEAR, "add_near")

time: 34.7 us -> 35.1 us (1.012)
  starting transfers between devices: 18 us -> 18.7 us
    ppermute x14, starting transfers between devices: 18 us -> 18.7 us  [move(): return lax.ppermute(value, AXES, perm)]
    ppermute x14, waiting for transfers between devices: 9.09 us -> 8.74 us  [move(): return lax.ppermute(value, AXES, perm)]
  transfers between devices with their start and end apart: 14 -> 14, of which waited for: 8 -> 7; matrix products, arithmetic and copies ran while one was open for 0% -> 0% of each run, Pallas kernels for 5% -> 5%
where the time goes in v30:
time: 35.1 us; the launch traced here: 34.9 us
  starting transfers between devices  18.7 us (53%)
  waiting for transfers between devices  8.74 us (25%)
  Pallas kernels  4.44 us (13%)
  between operations  2.04 us (6%)
  local copies, waits for them, and re-layouts  0.92 us (3%)
    ppermute x14, starting transfers between devices, move(): return lax.ppermute(value, AXES, perm)  18.7 us
    ppermute x14, waiting for transfers between devices, move(): return lax.ppermute(value, AXES, perm)  8.74 us
    pallas_call x9, Pallas kernels, call(): pl.pallas_call(kernel, out_shape=out_shape, in_specs=[VMEM] * len(operand...  3.41 us
    pallas_call x1, Pallas kernels, finish(): pl.pallas_call(functools.partial(finish_kernel, [side for side, _ in part...  1.03 us
    unnamed x6, local copies, waits for them, and re-layouts  0.92 us
  transfers between devices with their start and end apart: 14, of which 7 were waited for; matrix products, arithmetic and copies ran while one was open for 0% of the time, Pallas kernels for 5%

profile of v30, /device:TPU:0, one launch (start us, length us, event | category | flops | bytes accessed | tf_op | source)
XLA Modules:
  0.0 34.9 jit_solution(5789723577192280423)
XLA Ops:
  0.6 4.1 %collective-permute-start = (bf16[128,512]{1,0:T(8,128)(2,1)}, bf16[128,512]{1,0:T(8,128)(2,1)S(1)}, u32[]{:S(2)}, u32[]{:S(2)}) collective-permute-start(bf16[128,512]{1,0:T(8,128)(2,1)} %image_ref.1), channel_id=1, source_target_pairs={{0,8},{1,9},{2,10},{3,11},{4,12},{5,13},{6,14},{7,15},{8,0},{9,1},... | collective-permute-start | bytes 393224 | tf_op jit(solution)/shard_map/ppermute | solution.py:282
  4.7 1.5 %collective-permute-start.2 = (bf16[128,512]{1,0:T(8,128)(2,1)}, bf16[128,512]{1,0:T(8,128)(2,1)S(1)}, u32[]{:S(2)}, u32[]{:S(2)}) collective-permute-start(bf16[128,512]{1,0:T(8,128)(2,1)} %text_ref.1), channel_id=1, source_target_pairs={{0,2},{1,3},{2,0},{3,1},{4,6},{5,7},{6,4},{7,5},{8,10},{9,11},{10,... | collective-permute-start | bytes 393224 | tf_op jit(solution)/shard_map/ppermute | solution.py:282
  6.3 1.5 %collective-permute-start.1 = (bf16[128,512]{1,0:T(8,128)(2,1)}, bf16[128,512]{1,0:T(8,128)(2,1)S(1)}, u32[]{:S(2)}, u32[]{:S(2)}) collective-permute-start(bf16[128,512]{1,0:T(8,128)(2,1)} %text_ref.1), channel_id=1, source_target_pairs={{0,1},{1,0},{2,3},{3,2},{4,5},{5,4},{6,7},{7,6},{8,9},{9,8},{10,11... | collective-permute-start | bytes 393224 | tf_op jit(solution)/shard_map/ppermute | solution.py:282
  7.7 0.5 %collective-permute-start.3 = (bf16[128,512]{1,0:T(8,128)(2,1)}, bf16[128,512]{1,0:T(8,128)(2,1)S(1)}, u32[]{:S(2)}, u32[]{:S(2)}) collective-permute-start(bf16[128,512]{1,0:T(8,128)(2,1)} %text_ref.1), channel_id=1, source_target_pairs={{0,3},{1,2},{2,1},{3,0},{4,7},{5,6},{6,5},{7,4},{8,11},{9,10},{10,... | collective-permute-start | bytes 393224 | tf_op jit(solution)/shard_map/ppermute | solution.py:282
  8.2 1.6 %collective-permute-start.4 = (bf16[128,512]{1,0:T(8,128)(2,1)}, bf16[128,512]{1,0:T(8,128)(2,1)S(1)}, u32[]{:S(2)}, u32[]{:S(2)}) collective-permute-start(bf16[128,512]{1,0:T(8,128)(2,1)} %image_ref.1), channel_id=1, source_target_pairs={{0,4},{1,5},{2,6},{3,7},{4,0},{5,1},{6,2},{7,3},{8,12},{9,13},{10,... | collective-permute-start | bytes 393224 | tf_op jit(solution)/shard_map/ppermute | solution.py:282
  11.2 0.2 collective-permute-done.refs_1_
  11.4 0.8 %collective-permute-start.5 = (bf16[128,512]{1,0:T(8,128)(2,1)S(1)}, bf16[128,512]{1,0:T(8,128)(2,1)S(1)}, u32[]{:S(2)}, u32[]{:S(2)}) collective-permute-start(bf16[128,512]{1,0:T(8,128)(2,1)S(1)} %collective-permute-done.refs_1_), channel_id=1, source_target_pairs={{0,4},{1,5},{2,6},{3,7},{4,0},{5,1},{6,2},{7,3},{8,12},{9,13},{10,... | collective-permute-start | bytes 393224 | tf_op jit(solution)/shard_map/ppermute | solution.py:282
  12.1 0.9 %copy-done = bf16[128,512]{1,0:T(8,128)(2,1)S(1)} copy-done((bf16[128,512]{1,0:T(8,128)(2,1)S(1)}, bf16[128,512]{1,0:T(8,128)(2,1)}, u32[]{:S(2)}) %copy-start) | copy-done | bytes 131096
  13.2 1.0 %collective-permute-done.3.refs_3_ = bf16[128,512]{1,0:T(8,128)(2,1)S(1)} collective-permute-done((bf16[128,512]{1,0:T(8,128)(2,1)}, bf16[128,512]{1,0:T(8,128)(2,1)S(1)}, u32[]{:S(2)}, u32[]{:S(2)}) %collective-permute-start.3) | collective-permute-done | bytes 131104 | tf_op jit(solution)/shard_map/ppermute | solution.py:282
  14.2 0.2 stack_units.1.text_ref.own_text_ref
  14.4 0.4 %collective-permute-done.4.refs_2_ = bf16[128,512]{1,0:T(8,128)(2,1)S(1)} collective-permute-done((bf16[128,512]{1,0:T(8,128)(2,1)}, bf16[128,512]{1,0:T(8,128)(2,1)S(1)}, u32[]{:S(2)}, u32[]{:S(2)}) %collective-permute-start.4) | collective-permute-done | bytes 131104 | tf_op jit(solution)/shard_map/ppermute | solution.py:282
  14.9 1.1 %early_pairs.1 = (f32[512,512]{1,0:T(8,128)S(1)}, bf16[384,512]{1,0:T(8,128)(2,1)S(1)}, f32[384,512]{1,0:T(8,128)S(1)}) custom-call(f32[1,3]{1,0:T(1,128)S(1)} %maximum_bitcast_fusion.params_ref, bf16[512,512]{1,0:T(8,128)(2,1)S(1)} %stack_units.1.text_ref.own_text_ref, bf16[128,512]{1,0:T(8,128)(2,1)S(1)} %copy-done.2, ...), custom_call_target="tpu_custom_call" | custom-call | flops 603979776 | bytes 3145740 | tf_op jit(solution)/shard_map/early_pairs/pallas_call | solution.py:30
  16.0 0.9 %collective-permute-done.5.refs_0_ = bf16[128,512]{1,0:T(8,128)(2,1)S(1)} collective-permute-done((bf16[128,512]{1,0:T(8,128)(2,1)S(1)}, bf16[128,512]{1,0:T(8,128)(2,1)S(1)}, u32[]{:S(2)}, u32[]{:S(2)}) %collective-permute-start.5) | collective-permute-done | bytes 131104 | tf_op jit(solution)/shard_map/ppermute | solution.py:282
  17.0 1.7 %rest_pairs.1 = (f32[512,512]{1,0:T(8,128)S(1)}, bf16[512,512]{1,0:T(8,128)(2,1)S(1)}, f32[128,512]{1,0:T(8,128)S(1)}, f32[128,512]{1,0:T(8,128)S(1)}, bf16[128,...) custom-call(f32[1,3]{1,0:T(1,128)S(1)} %maximum_bitcast_fusion.params_ref, ...), custom_call_target="tpu_custom_call" | custom-call | flops 1006632960 | bytes 5767180 | tf_op jit(solution)/shard_map/rest_pairs/pallas_call | solution.py:30
  18.7 1.0 %collective-permute-start.12 = (bf16[128,512]{1,0:T(8,128)(2,1)S(1)}, bf16[128,512]{1,0:T(8,128)(2,1)S(1)}, u32[]{:S(2)}, u32[]{:S(2)}) collective-permute-start(bf16[128,512]{1,0:T(8,128)(2,1)S(1)} %get-tuple-element.39), channel_id=1, source_target_pairs={{0,4},{1,5},{2,6},{3,7},{4,0},{5,1},{6,2},{7,3},{8,12},{9,13},{10,... | collective-permute-start | bytes 393224 | tf_op jit(solution)/shard_map/ppermute | solution.py:282
  19.8 0.9 %collective-permute-done.7.refs_1_ = bf16[512,512]{1,0:T(8,128)(2,1)S(1)} collective-permute-done((bf16[512,512]{1,0:T(8,128)(2,1)S(1)}, bf16[512,512]{1,0:T(8,128)(2,1)S(1)}, u32[]{:S(2)}, u32[]{:S(2)}) %collective-permute-start.7) | collective-permute-done | bytes 524320 | tf_op jit(solution)/shard_map/ppermute | solution.py:282
  20.8 1.0 %collective-permute-start.8 = (bf16[128,512]{1,0:T(8,128)(2,1)S(1)}, bf16[128,512]{1,0:T(8,128)(2,1)S(1)}, u32[]{:S(2)}, u32[]{:S(2)}) collective-permute-start(bf16[128,512]{1,0:T(8,128)(2,1)S(1)} %get-tuple-element.31), channel_id=1, source_target_pairs={{0,4},{1,5},{2,6},{3,7},{4,0},{5,1},{6,2},{7,3},{8,12},{9,13},{10,... | collective-permute-start | bytes 393224 | tf_op jit(solution)/shard_map/ppermute | solution.py:282
  21.7 1.5 %collective-permute-start.9 = (bf16[128,512]{1,0:T(8,128)(2,1)S(1)}, bf16[128,512]{1,0:T(8,128)(2,1)S(1)}, u32[]{:S(2)}, u32[]{:S(2)}) collective-permute-start(bf16[128,512]{1,0:T(8,128)(2,1)S(1)} %get-tuple-element.34), channel_id=1, source_target_pairs={{0,1},{1,0},{2,3},{3,2},{4,5},{5,4},{6,7},{7,6},{8,9},{9,8},{10,11... | collective-permute-start | bytes 393224 | tf_op jit(solution)/shard_map/ppermute | solution.py:282
  23.2 1.5 %collective-permute-start.10 = (bf16[128,512]{1,0:T(8,128)(2,1)S(1)}, bf16[128,512]{1,0:T(8,128)(2,1)S(1)}, u32[]{:S(2)}, u32[]{:S(2)}) collective-permute-start(bf16[128,512]{1,0:T(8,128)(2,1)S(1)} %get-tuple-element.35), channel_id=1, source_target_pairs={{0,2},{1,3},{2,0},{3,1},{4,6},{5,7},{6,4},{7,5},{8,10},{9,11},{10,... | collective-permute-start | bytes 393224 | tf_op jit(solution)/shard_map/ppermute | solution.py:282
  24.7 0.5 %collective-permute-start.11 = (bf16[128,512]{1,0:T(8,128)(2,1)S(1)}, bf16[128,512]{1,0:T(8,128)(2,1)S(1)}, u32[]{:S(2)}, u32[]{:S(2)}) collective-permute-start(bf16[128,512]{1,0:T(8,128)(2,1)S(1)} %get-tuple-element.36), channel_id=1, source_target_pairs={{0,3},{1,2},{2,1},{3,0},{4,7},{5,6},{6,5},{7,4},{8,11},{9,10},{10,... | collective-permute-start | bytes 393224 | tf_op jit(solution)/shard_map/ppermute | solution.py:282
  25.3 3.1 %collective-permute-start.13 = (bf16[128,512]{1,0:T(8,128)(2,1)S(1)}, bf16[128,512]{1,0:T(8,128)(2,1)S(1)}, u32[]{:S(2)}, u32[]{:S(2)}) collective-permute-start(bf16[128,512]{1,0:T(8,128)(2,1)S(1)} %add_passed.1), channel_id=1, source_target_pairs={{0,8},{1,9},{2,10},{3,11},{4,12},{5,13},{6,14},{7,15},{8,0},{9,1},... | collective-permute-start | bytes 393224 | tf_op jit(solution)/shard_map/ppermute | solution.py:282
  28.4 2.6 %collective-permute-done.10.refs_2_ = bf16[128,512]{1,0:T(8,128)(2,1)S(1)} collective-permute-done((bf16[128,512]{1,0:T(8,128)(2,1)S(1)}, bf16[128,512]{1,0:T(8,128)(2,1)S(1)}, u32[]{:S(2)}, u32[]{:S(2)}) %collective-permute-start.10) | collective-permute-done | bytes 131104 | tf_op jit(solution)/shard_map/ppermute | solution.py:282
  31.1 2.8 %collective-permute-done.13.refs_2_ = bf16[128,512]{1,0:T(8,128)(2,1)S(1)} collective-permute-done((bf16[128,512]{1,0:T(8,128)(2,1)S(1)}, bf16[128,512]{1,0:T(8,128)(2,1)S(1)}, u32[]{:S(2)}, u32[]{:S(2)}) %collective-permute-start.13) | collective-permute-done | bytes 131104 | tf_op jit(solution)/shard_map/ppermute | solution.py:282
  33.8 1.0 %finish.1 = (f32[128,512]{1,0:T(8,128)}, f32[128,512]{1,0:T(8,128)}) custom-call(bf16[128,512]{1,0:T(8,128)(2,1)S(1)} %copy-done.2, bf16[128,512]{1,0:T(8,128)(2,1)S(1)} %copy-done.1, f32[128,512]{1,0:T(8,128)S(1)} %add_near.1.refs_0_, f32[128,512]{1,0:T(8,128)S(1)} %add_low.1.refs_1_, bf16[128,512]{1,0:T(8,128)(2,1)S(1)} %collective-permute-done.13.refs_2_), custom_call_target="tpu_custom_call" | custom-call | flops 1966080 | bytes 589824 | tf_op jit(solution)/shard_map/finish/pallas_call | solution.py:232
  (21 shorter events, 0.7 us)
Async XLA Ops:
  0.6 10.7 %collective-permute-start = (bf16[128,512]{1,0:T(8,128)(2,1)}, bf16[128,512]{1,0:T(8,128)(2,1)S(1)}, u32[]{:S(2)}, u32[]{:S(2)}) collective-permute-start(bf16[128,512]{1,0:T(8,128)(2,1)} %image_ref.1), channel_id=1, source_target_pairs={{0,8},{1,9},{2,10},{3,11},{4,12},{5,13},{6,14},{7,15},{8,0},{9,1},... | collective-permute-start | bytes 393224 | tf_op jit(solution)/shard_map/ppermute | solution.py:282
  4.7 8.4 %collective-permute-start.2 = (bf16[128,512]{1,0:T(8,128)(2,1)}, bf16[128,512]{1,0:T(8,128)(2,1)S(1)}, u32[]{:S(2)}, u32[]{:S(2)}) collective-permute-start(bf16[128,512]{1,0:T(8,128)(2,1)} %text_ref.1), channel_id=1, source_target_pairs={{0,2},{1,3},{2,0},{3,1},{4,6},{5,7},{6,4},{7,5},{8,10},{9,11},{10,... | collective-permute-start | bytes 393224 | tf_op jit(solution)/shard_map/ppermute | solution.py:282
  6.3 6.9 %collective-permute-start.1 = (bf16[128,512]{1,0:T(8,128)(2,1)}, bf16[128,512]{1,0:T(8,128)(2,1)S(1)}, u32[]{:S(2)}, u32[]{:S(2)}) collective-permute-start(bf16[128,512]{1,0:T(8,128)(2,1)} %text_ref.1), channel_id=1, source_target_pairs={{0,1},{1,0},{2,3},{3,2},{4,5},{5,4},{6,7},{7,6},{8,9},{9,8},{10,11... | collective-permute-start | bytes 393224 | tf_op jit(solution)/shard_map/ppermute | solution.py:282
  7.7 6.4 %collective-permute-start.3 = (bf16[128,512]{1,0:T(8,128)(2,1)}, bf16[128,512]{1,0:T(8,128)(2,1)S(1)}, u32[]{:S(2)}, u32[]{:S(2)}) collective-permute-start(bf16[128,512]{1,0:T(8,128)(2,1)} %text_ref.1), channel_id=1, source_target_pairs={{0,3},{1,2},{2,1},{3,0},{4,7},{5,6},{6,5},{7,4},{8,11},{9,10},{10,... | collective-permute-start | bytes 393224 | tf_op jit(solution)/shard_map/ppermute | solution.py:282
  8.2 6.6 %collective-permute-start.4 = (bf16[128,512]{1,0:T(8,128)(2,1)}, bf16[128,512]{1,0:T(8,128)(2,1)S(1)}, u32[]{:S(2)}, u32[]{:S(2)}) collective-permute-start(bf16[128,512]{1,0:T(8,128)(2,1)} %image_ref.1), channel_id=1, source_target_pairs={{0,4},{1,5},{2,6},{3,7},{4,0},{5,1},{6,2},{7,3},{8,12},{9,13},{10,... | collective-permute-start | bytes 393224 | tf_op jit(solution)/shard_map/ppermute | solution.py:282
  11.4 5.5 %collective-permute-start.5 = (bf16[128,512]{1,0:T(8,128)(2,1)S(1)}, bf16[128,512]{1,0:T(8,128)(2,1)S(1)}, u32[]{:S(2)}, u32[]{:S(2)}) collective-permute-start(bf16[128,512]{1,0:T(8,128)(2,1)S(1)} %collective-permute-done.refs_1_), channel_id=1, source_target_pairs={{0,4},{1,5},{2,6},{3,7},{4,0},{5,1},{6,2},{7,3},{8,12},{9,13},{10,... | collective-permute-start | bytes 393224 | tf_op jit(solution)/shard_map/ppermute | solution.py:282
  12.1 0.9 %copy-start = (bf16[128,512]{1,0:T(8,128)(2,1)S(1)}, bf16[128,512]{1,0:T(8,128)(2,1)}, u32[]{:S(2)}) copy-start(bf16[128,512]{1,0:T(8,128)(2,1)} %text_ref.1) | copy-start | bytes 393220
  13.1 1.7 %copy-start.2 = (bf16[128,512]{1,0:T(8,128)(2,1)S(1)}, bf16[128,512]{1,0:T(8,128)(2,1)}, u32[]{:S(2)}) copy-start(bf16[128,512]{1,0:T(8,128)(2,1)} %image_ref.1) | copy-start | bytes 393220
  14.3 2.6 %collective-permute-start.6 = (bf16[512,512]{1,0:T(8,128)(2,1)S(1)}, bf16[512,512]{1,0:T(8,128)(2,1)S(1)}, u32[]{:S(2)}, u32[]{:S(2)}) collective-permute-start(bf16[512,512]{1,0:T(8,128)(2,1)S(1)} %stack_units.1.text_ref.own_text_ref), channel_id=1, source_target_pairs={{0,16},{1,17},{2,18},{3,19},{4,20},{5,21},{6,22},{7,23},{8,24},{9,... | collective-permute-start | bytes 1572872 | tf_op jit(solution)/shard_map/ppermute | solution.py:282
  18.7 2.0 %collective-permute-start.7 = (bf16[512,512]{1,0:T(8,128)(2,1)S(1)}, bf16[512,512]{1,0:T(8,128)(2,1)S(1)}, u32[]{:S(2)}, u32[]{:S(2)}) collective-permute-start(bf16[512,512]{1,0:T(8,128)(2,1)S(1)} %get-tuple-element.29), channel_id=1, source_target_pairs={{0,16},{1,17},{2,18},{3,19},{4,20},{5,21},{6,22},{7,23},{8,24},{9,... | collective-permute-start | bytes 1572872 | tf_op jit(solution)/shard_map/ppermute | solution.py:282
  18.7 6.5 %collective-permute-start.12 = (bf16[128,512]{1,0:T(8,128)(2,1)S(1)}, bf16[128,512]{1,0:T(8,128)(2,1)S(1)}, u32[]{:S(2)}, u32[]{:S(2)}) collective-permute-start(bf16[128,512]{1,0:T(8,128)(2,1)S(1)} %get-tuple-element.39), channel_id=1, source_target_pairs={{0,4},{1,5},{2,6},{3,7},{4,0},{5,1},{6,2},{7,3},{8,12},{9,13},{10,... | collective-permute-start | bytes 393224 | tf_op jit(solution)/shard_map/ppermute | solution.py:282
  20.8 7.6 %collective-permute-start.8 = (bf16[128,512]{1,0:T(8,128)(2,1)S(1)}, bf16[128,512]{1,0:T(8,128)(2,1)S(1)}, u32[]{:S(2)}, u32[]{:S(2)}) collective-permute-start(bf16[128,512]{1,0:T(8,128)(2,1)S(1)} %get-tuple-element.31), channel_id=1, source_target_pairs={{0,4},{1,5},{2,6},{3,7},{4,0},{5,1},{6,2},{7,3},{8,12},{9,13},{10,... | collective-permute-start | bytes 393224 | tf_op jit(solution)/shard_map/ppermute | solution.py:282
  21.7 6.7 %collective-permute-start.9 = (bf16[128,512]{1,0:T(8,128)(2,1)S(1)}, bf16[128,512]{1,0:T(8,128)(2,1)S(1)}, u32[]{:S(2)}, u32[]{:S(2)}) collective-permute-start(bf16[128,512]{1,0:T(8,128)(2,1)S(1)} %get-tuple-element.34), channel_id=1, source_target_pairs={{0,1},{1,0},{2,3},{3,2},{4,5},{5,4},{6,7},{7,6},{8,9},{9,8},{10,11... | collective-permute-start | bytes 393224 | tf_op jit(solution)/shard_map/ppermute | solution.py:282
  23.2 7.8 %collective-permute-start.10 = (bf16[128,512]{1,0:T(8,128)(2,1)S(1)}, bf16[128,512]{1,0:T(8,128)(2,1)S(1)}, u32[]{:S(2)}, u32[]{:S(2)}) collective-permute-start(bf16[128,512]{1,0:T(8,128)(2,1)S(1)} %get-tuple-element.35), channel_id=1, source_target_pairs={{0,2},{1,3},{2,0},{3,1},{4,6},{5,7},{6,4},{7,5},{8,10},{9,11},{10,... | collective-permute-start | bytes 393224 | tf_op jit(solution)/shard_map/ppermute | solution.py:282
  24.7 6.3 %collective-permute-start.11 = (bf16[128,512]{1,0:T(8,128)(2,1)S(1)}, bf16[128,512]{1,0:T(8,128)(2,1)S(1)}, u32[]{:S(2)}, u32[]{:S(2)}) collective-permute-start(bf16[128,512]{1,0:T(8,128)(2,1)S(1)} %get-tuple-element.36), channel_id=1, source_target_pairs={{0,3},{1,2},{2,1},{3,0},{4,7},{5,6},{6,5},{7,4},{8,11},{9,10},{10,... | collective-permute-start | bytes 393224 | tf_op jit(solution)/shard_map/ppermute | solution.py:282
  25.3 8.6 %collective-permute-start.13 = (bf16[128,512]{1,0:T(8,128)(2,1)S(1)}, bf16[128,512]{1,0:T(8,128)(2,1)S(1)}, u32[]{:S(2)}, u32[]{:S(2)}) collective-permute-start(bf16[128,512]{1,0:T(8,128)(2,1)S(1)} %add_passed.1), channel_id=1, source_target_pairs={{0,8},{1,9},{2,10},{3,11},{4,12},{5,13},{6,14},{7,15},{8,0},{9,1},... | collective-permute-start | bytes 393224 | tf_op jit(solution)/shard_map/ppermute | solution.py:282
  28.4 5.5 %copy-start.1 = (bf16[128,512]{1,0:T(8,128)(2,1)S(1)}, bf16[128,512]{1,0:T(8,128)(2,1)}, u32[]{:S(2)}) copy-start(bf16[128,512]{1,0:T(8,128)(2,1)} %text_ref.1) | copy-start | bytes 393220

commit v31 on v20

--- a/solution.py
+++ b/solution.py
@@ -294,7 +294,8 @@
         far_came = [move(far_parts[h, w], high=-h, low=-w) for h, w in far_order]
         near_parts = add_stacks([text_parts[0], *came], near_count)
         near_parts = [near_parts[0]] + [
-            move(part, near=-n) for n, part in enumerate(near_parts) if n
+            move(near_parts[n], near=-n)
+            for n in sorted(range(1, near_count), key=lambda n: (2 * n != near_count, n))
         ]
         return finish(
             images,

time: 34.3 us -> 34.3 us (level)
  no operation moved by 1% of the time
where the time goes in v31:
time: 34.3 us; the launch traced here: 34.1 us
  starting transfers between devices  20.1 us (59%)
  waiting for transfers between devices  6.55 us (19%)
  Pallas kernels  4.37 us (13%)
  between operations  2.02 us (6%)
  local copies, waits for them, and re-layouts  0.91 us (3%)
    ppermute x14, starting transfers between devices, move(): return lax.ppermute(value, AXES, perm)  20.1 us
    ppermute x14, waiting for transfers between devices, move(): return lax.ppermute(value, AXES, perm)  6.55 us
    pallas_call x6, Pallas kernels, call(): pl.pallas_call(kernel, out_shape=out_shape, in_specs=[VMEM] * len(operand...  3.31 us
    pallas_call x1, Pallas kernels, finish(): pl.pallas_call(functools.partial(finish_kernel, [side for side, _ in part...  1.07 us
    unnamed x6, local copies, waits for them, and re-layouts  0.91 us
  transfers between devices with their start and end apart: 14, of which 7 were waited for; matrix products, arithmetic and copies ran while one was open for 0% of the time, Pallas kernels for 5%

profile of v31, /device:TPU:0, one launch (start us, length us, event | category | flops | bytes accessed | tf_op | source)
XLA Modules:
  0.0 34.1 jit_solution(255718736100900672)
XLA Ops:
  0.6 4.1 %collective-permute-start = (bf16[128,512]{1,0:T(8,128)(2,1)}, bf16[128,512]{1,0:T(8,128)(2,1)S(1)}, u32[]{:S(2)}, u32[]{:S(2)}) collective-permute-start(bf16[128,512]{1,0:T(8,128)(2,1)} %image_ref.1), channel_id=1, source_target_pairs={{0,8},{1,9},{2,10},{3,11},{4,12},{5,13},{6,14},{7,15},{8,0},{9,1},... | collective-permute-start | bytes 393224 | tf_op jit(solution)/shard_map/ppermute | solution.py:269
  4.7 1.5 %collective-permute-start.2 = (bf16[128,512]{1,0:T(8,128)(2,1)}, bf16[128,512]{1,0:T(8,128)(2,1)S(1)}, u32[]{:S(2)}, u32[]{:S(2)}) collective-permute-start(bf16[128,512]{1,0:T(8,128)(2,1)} %text_ref.1), channel_id=1, source_target_pairs={{0,2},{1,3},{2,0},{3,1},{4,6},{5,7},{6,4},{7,5},{8,10},{9,11},{10,... | collective-permute-start | bytes 393224 | tf_op jit(solution)/shard_map/ppermute | solution.py:269
  6.3 1.5 %collective-permute-start.1 = (bf16[128,512]{1,0:T(8,128)(2,1)}, bf16[128,512]{1,0:T(8,128)(2,1)S(1)}, u32[]{:S(2)}, u32[]{:S(2)}) collective-permute-start(bf16[128,512]{1,0:T(8,128)(2,1)} %text_ref.1), channel_id=1, source_target_pairs={{0,1},{1,0},{2,3},{3,2},{4,5},{5,4},{6,7},{7,6},{8,9},{9,8},{10,11... | collective-permute-start | bytes 393224 | tf_op jit(solution)/shard_map/ppermute | solution.py:269
  7.7 0.5 %collective-permute-start.3 = (bf16[128,512]{1,0:T(8,128)(2,1)}, bf16[128,512]{1,0:T(8,128)(2,1)S(1)}, u32[]{:S(2)}, u32[]{:S(2)}) collective-permute-start(bf16[128,512]{1,0:T(8,128)(2,1)} %text_ref.1), channel_id=1, source_target_pairs={{0,3},{1,2},{2,1},{3,0},{4,7},{5,6},{6,5},{7,4},{8,11},{9,10},{10,... | collective-permute-start | bytes 393224 | tf_op jit(solution)/shard_map/ppermute | solution.py:269
  8.2 1.6 %collective-permute-start.4 = (bf16[128,512]{1,0:T(8,128)(2,1)}, bf16[128,512]{1,0:T(8,128)(2,1)S(1)}, u32[]{:S(2)}, u32[]{:S(2)}) collective-permute-start(bf16[128,512]{1,0:T(8,128)(2,1)} %image_ref.1), channel_id=1, source_target_pairs={{0,4},{1,5},{2,6},{3,7},{4,0},{5,1},{6,2},{7,3},{8,12},{9,13},{10,... | collective-permute-start | bytes 393224 | tf_op jit(solution)/shard_map/ppermute | solution.py:269
  11.2 0.2 collective-permute-done.refs_1_
  11.4 0.8 %collective-permute-start.5 = (bf16[128,512]{1,0:T(8,128)(2,1)S(1)}, bf16[128,512]{1,0:T(8,128)(2,1)S(1)}, u32[]{:S(2)}, u32[]{:S(2)}) collective-permute-start(bf16[128,512]{1,0:T(8,128)(2,1)S(1)} %collective-permute-done.refs_1_), channel_id=1, source_target_pairs={{0,4},{1,5},{2,6},{3,7},{4,0},{5,1},{6,2},{7,3},{8,12},{9,13},{10,... | collective-permute-start | bytes 393224 | tf_op jit(solution)/shard_map/ppermute | solution.py:269
  12.1 0.9 %copy-done = bf16[128,512]{1,0:T(8,128)(2,1)S(1)} copy-done((bf16[128,512]{1,0:T(8,128)(2,1)S(1)}, bf16[128,512]{1,0:T(8,128)(2,1)}, u32[]{:S(2)}) %copy-start) | copy-done | bytes 131096
  13.2 1.0 %collective-permute-done.3.refs_3_ = bf16[128,512]{1,0:T(8,128)(2,1)S(1)} collective-permute-done((bf16[128,512]{1,0:T(8,128)(2,1)}, bf16[128,512]{1,0:T(8,128)(2,1)S(1)}, u32[]{:S(2)}, u32[]{:S(2)}) %collective-permute-start.3) | collective-permute-done | bytes 131104 | tf_op jit(solution)/shard_map/ppermute | solution.py:269
  14.2 0.2 stack_units.1.text_ref.own_text_ref
  14.4 0.4 %collective-permute-done.4.refs_2_ = bf16[128,512]{1,0:T(8,128)(2,1)S(1)} collective-permute-done((bf16[128,512]{1,0:T(8,128)(2,1)}, bf16[128,512]{1,0:T(8,128)(2,1)S(1)}, u32[]{:S(2)}, u32[]{:S(2)}) %collective-permute-start.4) | collective-permute-done | bytes 131104 | tf_op jit(solution)/shard_map/ppermute | solution.py:269
  14.9 1.1 %early_pairs.1 = (f32[512,512]{1,0:T(8,128)S(1)}, bf16[384,512]{1,0:T(8,128)(2,1)S(1)}, f32[384,512]{1,0:T(8,128)S(1)}) custom-call(f32[1,3]{1,0:T(1,128)S(1)} %maximum_bitcast_fusion.params_ref, bf16[512,512]{1,0:T(8,128)(2,1)S(1)} %stack_units.1.text_ref.own_text_ref, bf16[128,512]{1,0:T(8,128)(2,1)S(1)} %copy-done.2, ...), custom_call_target="tpu_custom_call" | custom-call | flops 603979776 | bytes 3145740 | tf_op jit(solution)/shard_map/early_pairs/pallas_call | solution.py:28
  16.0 0.9 %collective-permute-done.5.refs_0_ = bf16[128,512]{1,0:T(8,128)(2,1)S(1)} collective-permute-done((bf16[128,512]{1,0:T(8,128)(2,1)S(1)}, bf16[128,512]{1,0:T(8,128)(2,1)S(1)}, u32[]{:S(2)}, u32[]{:S(2)}) %collective-permute-start.5) | collective-permute-done | bytes 131104 | tf_op jit(solution)/shard_map/ppermute | solution.py:269
  17.0 1.7 %rest_pairs.1 = (f32[512,512]{1,0:T(8,128)S(1)}, bf16[512,512]{1,0:T(8,128)(2,1)S(1)}, f32[128,512]{1,0:T(8,128)S(1)}, bf16[128,512]{1,0:T(8,128)(2,1)S(1)}, bf1...) custom-call(f32[1,3]{1,0:T(1,128)S(1)} %maximum_bitcast_fusion.params_ref, ...), custom_call_target="tpu_custom_call" | custom-call | flops 1006632960 | bytes 5636108 | tf_op jit(solution)/shard_map/rest_pairs/pallas_call | solution.py:28
  18.8 1.0 %collective-permute-start.7 = (bf16[128,512]{1,0:T(8,128)(2,1)S(1)}, bf16[128,512]{1,0:T(8,128)(2,1)S(1)}, u32[]{:S(2)}, u32[]{:S(2)}) collective-permute-start(bf16[128,512]{1,0:T(8,128)(2,1)S(1)} %get-tuple-element.23), channel_id=1, source_target_pairs={{0,4},{1,5},{2,6},{3,7},{4,0},{5,1},{6,2},{7,3},{8,12},{9,13},{10,... | collective-permute-start | bytes 393224 | tf_op jit(solution)/shard_map/ppermute | solution.py:269
  19.8 3.0 %collective-permute-start.8 = (bf16[128,512]{1,0:T(8,128)(2,1)S(1)}, bf16[128,512]{1,0:T(8,128)(2,1)S(1)}, u32[]{:S(2)}, u32[]{:S(2)}) collective-permute-start(bf16[128,512]{1,0:T(8,128)(2,1)S(1)} %get-tuple-element.24), channel_id=1, source_target_pairs={{0,8},{1,9},{2,10},{3,11},{4,12},{5,13},{6,14},{7,15},{8,0},{9,1},... | collective-permute-start | bytes 393224 | tf_op jit(solution)/shard_map/ppermute | solution.py:269
  22.8 0.4 %collective-permute-start.9 = (bf16[128,512]{1,0:T(8,128)(2,1)S(1)}, bf16[128,512]{1,0:T(8,128)(2,1)S(1)}, u32[]{:S(2)}, u32[]{:S(2)}) collective-permute-start(bf16[128,512]{1,0:T(8,128)(2,1)S(1)} %get-tuple-element.25), channel_id=1, source_target_pairs={{0,12},{1,13},{2,14},{3,15},{4,8},{5,9},{6,10},{7,11},{8,4},{9,5},... | collective-permute-start | bytes 393224 | tf_op jit(solution)/shard_map/ppermute | solution.py:269
  23.3 1.6 %collective-permute-start.11 = (bf16[128,512]{1,0:T(8,128)(2,1)S(1)}, bf16[128,512]{1,0:T(8,128)(2,1)S(1)}, u32[]{:S(2)}, u32[]{:S(2)}) collective-permute-start(bf16[128,512]{1,0:T(8,128)(2,1)S(1)} %get-tuple-element.29), channel_id=1, source_target_pairs={{0,2},{1,3},{2,0},{3,1},{4,6},{5,7},{6,4},{7,5},{8,10},{9,11},{10,... | collective-permute-start | bytes 393224 | tf_op jit(solution)/shard_map/ppermute | solution.py:269
  25.0 1.5 %collective-permute-start.12 = (bf16[128,512]{1,0:T(8,128)(2,1)S(1)}, bf16[128,512]{1,0:T(8,128)(2,1)S(1)}, u32[]{:S(2)}, u32[]{:S(2)}) collective-permute-start(bf16[128,512]{1,0:T(8,128)(2,1)S(1)} %get-tuple-element.30), channel_id=1, source_target_pairs={{0,1},{1,0},{2,3},{3,2},{4,5},{5,4},{6,7},{7,6},{8,9},{9,8},{10,11... | collective-permute-start | bytes 393224 | tf_op jit(solution)/shard_map/ppermute | solution.py:269
  26.5 0.7 %collective-permute-done.7.refs_1_ = bf16[128,512]{1,0:T(8,128)(2,1)S(1)} collective-permute-done((bf16[128,512]{1,0:T(8,128)(2,1)S(1)}, bf16[128,512]{1,0:T(8,128)(2,1)S(1)}, u32[]{:S(2)}, u32[]{:S(2)}) %collective-permute-start.7) | collective-permute-done | bytes 131104 | tf_op jit(solution)/shard_map/ppermute | solution.py:269
  27.1 2.5 %collective-permute-start.13 = (bf16[128,512]{1,0:T(8,128)(2,1)S(1)}, bf16[128,512]{1,0:T(8,128)(2,1)S(1)}, u32[]{:S(2)}, u32[]{:S(2)}) collective-permute-start(bf16[128,512]{1,0:T(8,128)(2,1)S(1)} %get-tuple-element.31), channel_id=1, source_target_pairs={{0,3},{1,2},{2,1},{3,0},{4,7},{5,6},{6,5},{7,4},{8,11},{9,10},{10,... | collective-permute-start | bytes 393224 | tf_op jit(solution)/shard_map/ppermute | solution.py:269
  29.6 3.1 %collective-permute-done.8.refs_2_ = bf16[128,512]{1,0:T(8,128)(2,1)S(1)} collective-permute-done((bf16[128,512]{1,0:T(8,128)(2,1)S(1)}, bf16[128,512]{1,0:T(8,128)(2,1)S(1)}, u32[]{:S(2)}, u32[]{:S(2)}) %collective-permute-start.8) | collective-permute-done | bytes 131104 | tf_op jit(solution)/shard_map/ppermute | solution.py:269
  32.7 0.3 collective-permute-done.13.refs_7_
  33.0 1.1 %finish.1 = (f32[128,512]{1,0:T(8,128)}, f32[128,512]{1,0:T(8,128)}) custom-call(bf16[128,512]{1,0:T(8,128)(2,1)S(1)} %copy-done.2, bf16[128,512]{1,0:T(8,128)(2,1)S(1)} %copy-done.1, f32[128,512]{1,0:T(8,128)S(1)} %get-tuple-element.22.refs_0_, bf16[128,512]{1,0:T(8,128)(2,1)S(1)} %collective-permute-done.7.refs_1_, ...), custom_call_target="tpu_custom_call" | custom-call | flops 5242880 | bytes 1572864 | tf_op jit(solution)/shard_map/finish/pallas_call | solution.py:219
  (18 shorter events, 0.6 us)
Async XLA Ops:
  0.6 10.7 %collective-permute-start = (bf16[128,512]{1,0:T(8,128)(2,1)}, bf16[128,512]{1,0:T(8,128)(2,1)S(1)}, u32[]{:S(2)}, u32[]{:S(2)}) collective-permute-start(bf16[128,512]{1,0:T(8,128)(2,1)} %image_ref.1), channel_id=1, source_target_pairs={{0,8},{1,9},{2,10},{3,11},{4,12},{5,13},{6,14},{7,15},{8,0},{9,1},... | collective-permute-start | bytes 393224 | tf_op jit(solution)/shard_map/ppermute | solution.py:269
  4.7 8.4 %collective-permute-start.2 = (bf16[128,512]{1,0:T(8,128)(2,1)}, bf16[128,512]{1,0:T(8,128)(2,1)S(1)}, u32[]{:S(2)}, u32[]{:S(2)}) collective-permute-start(bf16[128,512]{1,0:T(8,128)(2,1)} %text_ref.1), channel_id=1, source_target_pairs={{0,2},{1,3},{2,0},{3,1},{4,6},{5,7},{6,4},{7,5},{8,10},{9,11},{10,... | collective-permute-start | bytes 393224 | tf_op jit(solution)/shard_map/ppermute | solution.py:269
  6.3 6.9 %collective-permute-start.1 = (bf16[128,512]{1,0:T(8,128)(2,1)}, bf16[128,512]{1,0:T(8,128)(2,1)S(1)}, u32[]{:S(2)}, u32[]{:S(2)}) collective-permute-start(bf16[128,512]{1,0:T(8,128)(2,1)} %text_ref.1), channel_id=1, source_target_pairs={{0,1},{1,0},{2,3},{3,2},{4,5},{5,4},{6,7},{7,6},{8,9},{9,8},{10,11... | collective-permute-start | bytes 393224 | tf_op jit(solution)/shard_map/ppermute | solution.py:269
  7.7 6.4 %collective-permute-start.3 = (bf16[128,512]{1,0:T(8,128)(2,1)}, bf16[128,512]{1,0:T(8,128)(2,1)S(1)}, u32[]{:S(2)}, u32[]{:S(2)}) collective-permute-start(bf16[128,512]{1,0:T(8,128)(2,1)} %text_ref.1), channel_id=1, source_target_pairs={{0,3},{1,2},{2,1},{3,0},{4,7},{5,6},{6,5},{7,4},{8,11},{9,10},{10,... | collective-permute-start | bytes 393224 | tf_op jit(solution)/shard_map/ppermute | solution.py:269
  8.2 6.6 %collective-permute-start.4 = (bf16[128,512]{1,0:T(8,128)(2,1)}, bf16[128,512]{1,0:T(8,128)(2,1)S(1)}, u32[]{:S(2)}, u32[]{:S(2)}) collective-permute-start(bf16[128,512]{1,0:T(8,128)(2,1)} %image_ref.1), channel_id=1, source_target_pairs={{0,4},{1,5},{2,6},{3,7},{4,0},{5,1},{6,2},{7,3},{8,12},{9,13},{10,... | collective-permute-start | bytes 393224 | tf_op jit(solution)/shard_map/ppermute | solution.py:269
  11.4 5.5 %collective-permute-start.5 = (bf16[128,512]{1,0:T(8,128)(2,1)S(1)}, bf16[128,512]{1,0:T(8,128)(2,1)S(1)}, u32[]{:S(2)}, u32[]{:S(2)}) collective-permute-start(bf16[128,512]{1,0:T(8,128)(2,1)S(1)} %collective-permute-done.refs_1_), channel_id=1, source_target_pairs={{0,4},{1,5},{2,6},{3,7},{4,0},{5,1},{6,2},{7,3},{8,12},{9,13},{10,... | collective-permute-start | bytes 393224 | tf_op jit(solution)/shard_map/ppermute | solution.py:269
  12.1 0.9 %copy-start = (bf16[128,512]{1,0:T(8,128)(2,1)S(1)}, bf16[128,512]{1,0:T(8,128)(2,1)}, u32[]{:S(2)}) copy-start(bf16[128,512]{1,0:T(8,128)(2,1)} %text_ref.1) | copy-start | bytes 393220
  13.1 1.7 %copy-start.2 = (bf16[128,512]{1,0:T(8,128)(2,1)S(1)}, bf16[128,512]{1,0:T(8,128)(2,1)}, u32[]{:S(2)}) copy-start(bf16[128,512]{1,0:T(8,128)(2,1)} %image_ref.1) | copy-start | bytes 393220
  14.3 2.6 %collective-permute-start.6 = (bf16[512,512]{1,0:T(8,128)(2,1)S(1)}, bf16[512,512]{1,0:T(8,128)(2,1)S(1)}, u32[]{:S(2)}, u32[]{:S(2)}) collective-permute-start(bf16[512,512]{1,0:T(8,128)(2,1)S(1)} %stack_units.1.text_ref.own_text_ref), channel_id=1, source_target_pairs={{0,16},{1,17},{2,18},{3,19},{4,20},{5,21},{6,22},{7,23},{8,24},{9,... | collective-permute-start | bytes 1572872 | tf_op jit(solution)/shard_map/ppermute | solution.py:269
  18.7 4.5 %collective-permute-start.10 = (bf16[512,512]{1,0:T(8,128)(2,1)S(1)}, bf16[512,512]{1,0:T(8,128)(2,1)S(1)}, u32[]{:S(2)}, u32[]{:S(2)}) collective-permute-start(bf16[512,512]{1,0:T(8,128)(2,1)S(1)} %get-tuple-element.27), channel_id=1, source_target_pairs={{0,16},{1,17},{2,18},{3,19},{4,20},{5,21},{6,22},{7,23},{8,24},{9,... | collective-permute-start | bytes 1572872 | tf_op jit(solution)/shard_map/ppermute | solution.py:269
  18.8 8.4 %collective-permute-start.7 = (bf16[128,512]{1,0:T(8,128)(2,1)S(1)}, bf16[128,512]{1,0:T(8,128)(2,1)S(1)}, u32[]{:S(2)}, u32[]{:S(2)}) collective-permute-start(bf16[128,512]{1,0:T(8,128)(2,1)S(1)} %get-tuple-element.23), channel_id=1, source_target_pairs={{0,4},{1,5},{2,6},{3,7},{4,0},{5,1},{6,2},{7,3},{8,12},{9,13},{10,... | collective-permute-start | bytes 393224 | tf_op jit(solution)/shard_map/ppermute | solution.py:269
  19.8 12.9 %collective-permute-start.8 = (bf16[128,512]{1,0:T(8,128)(2,1)S(1)}, bf16[128,512]{1,0:T(8,128)(2,1)S(1)}, u32[]{:S(2)}, u32[]{:S(2)}) collective-permute-start(bf16[128,512]{1,0:T(8,128)(2,1)S(1)} %get-tuple-element.24), channel_id=1, source_target_pairs={{0,8},{1,9},{2,10},{3,11},{4,12},{5,13},{6,14},{7,15},{8,0},{9,1},... | collective-permute-start | bytes 393224 | tf_op jit(solution)/shard_map/ppermute | solution.py:269
  22.8 9.9 %collective-permute-start.9 = (bf16[128,512]{1,0:T(8,128)(2,1)S(1)}, bf16[128,512]{1,0:T(8,128)(2,1)S(1)}, u32[]{:S(2)}, u32[]{:S(2)}) collective-permute-start(bf16[128,512]{1,0:T(8,128)(2,1)S(1)} %get-tuple-element.25), channel_id=1, source_target_pairs={{0,12},{1,13},{2,14},{3,15},{4,8},{5,9},{6,10},{7,11},{8,4},{9,5},... | collective-permute-start | bytes 393224 | tf_op jit(solution)/shard_map/ppermute | solution.py:269
  23.2 9.8 %copy-start.1 = (bf16[128,512]{1,0:T(8,128)(2,1)S(1)}, bf16[128,512]{1,0:T(8,128)(2,1)}, u32[]{:S(2)}) copy-start(bf16[128,512]{1,0:T(8,128)(2,1)} %text_ref.1) | copy-start | bytes 393220
  23.3 9.4 %collective-permute-start.11 = (bf16[128,512]{1,0:T(8,128)(2,1)S(1)}, bf16[128,512]{1,0:T(8,128)(2,1)S(1)}, u32[]{:S(2)}, u32[]{:S(2)}) collective-permute-start(bf16[128,512]{1,0:T(8,128)(2,1)S(1)} %get-tuple-element.29), channel_id=1, source_target_pairs={{0,2},{1,3},{2,0},{3,1},{4,6},{5,7},{6,4},{7,5},{8,10},{9,11},{10,... | collective-permute-start | bytes 393224 | tf_op jit(solution)/shard_map/ppermute | solution.py:269
  25.0 7.8 %collective-permute-start.12 = (bf16[128,512]{1,0:T(8,128)(2,1)S(1)}, bf16[128,512]{1,0:T(8,128)(2,1)S(1)}, u32[]{:S(2)}, u32[]{:S(2)}) collective-permute-start(bf16[128,512]{1,0:T(8,128)(2,1)S(1)} %get-tuple-element.30), channel_id=1, source_target_pairs={{0,1},{1,0},{2,3},{3,2},{4,5},{5,4},{6,7},{7,6},{8,9},{9,8},{10,11... | collective-permute-start | bytes 393224 | tf_op jit(solution)/shard_map/ppermute | solution.py:269
  27.1 5.9 %collective-permute-start.13 = (bf16[128,512]{1,0:T(8,128)(2,1)S(1)}, bf16[128,512]{1,0:T(8,128)(2,1)S(1)}, u32[]{:S(2)}, u32[]{:S(2)}) collective-permute-start(bf16[128,512]{1,0:T(8,128)(2,1)S(1)} %get-tuple-element.31), channel_id=1, source_target_pairs={{0,3},{1,2},{2,1},{3,0},{4,7},{5,6},{6,5},{7,4},{8,11},{9,10},{10,... | collective-permute-start | bytes 393224 | tf_op jit(solution)/shard_map/ppermute | solution.py:269
